TPU v7x, 32 devices: a whole 2x2x4 slice. The times are simulated.
32 devices in a mesh: rows: 8 (over z, x), sub: 4 (over y, core).
Axes of the slice: x: 2, y: 2, z: 4, core: 2. Of those that a mesh axis runs over, the one named last changes fastest.
Arguments:
- rhs_solved: float32 [32768, 128], P(('rows', 'sub')), may hold values from -41 to 41
- generators: float32 [3, 32768, 256], P(None, ('rows', 'sub')), may hold values from -0.047111148 to 0.047111148
- solved_gens: float32 [3, 32768, 256], P(None, ('rows', 'sub')), may hold values from -0.18844459 to 0.18844459
Outputs:
- solution: float32 [32768, 128], P(('rows', 'sub'))
All inputs are finite; a program needn't handle non-finite values.
Results may differ from a plain program's by a relative error of at most 0.0001.
Values sent between devices are 32-bit elements; how exact they have to be, the bound alone decides.
No kernel may reach another device: no remote copies, remote signals or barrier semaphores. Data moves between devices by JAX's collectives and lax.ppermute only.
A program may use at most 64 MiB of HBM per device.

v0:
```python
import jax
import jax.numpy as jnp
from jax import lax
from jax.sharding import PartitionSpec as P

RANK = 256
RHS = 128


highest = lax.Precision.HIGHEST


def from_partner(value, axis, apart):
    mask = 2**apart
    pairs = [(source, source ^ mask) for source in range(lax.axis_size(axis))]
    return lax.ppermute(value, axis, pairs)


def lower_solve(factor, values):
    return lax.linalg.triangular_solve(factor, values, left_side=True, lower=True)


def factor_solve(factor, values):
    middle = lax.linalg.triangular_solve(factor, values, left_side=True, lower=True)
    return lax.linalg.triangular_solve(factor, middle, left_side=True, lower=True, transpose_a=True)


def pair_solve(p_first, p_second, r_first, r_second):
    identity_matrix = jnp.eye(p_first.shape[0], dtype=p_first.dtype)
    lower_factor = jnp.linalg.cholesky(p_first)
    inner_matrix = identity_matrix - jnp.dot(
        lower_factor.T, jnp.dot(p_second, lower_factor, precision=highest), precision=highest
    )
    inner_factor = jnp.linalg.cholesky(inner_matrix)
    shifted = r_first - jnp.dot(p_first, r_second, precision=highest)
    partial_solve = lower_solve(lower_factor, shifted)
    partial_solve = factor_solve(inner_factor, partial_solve)
    z_second = jnp.dot(lower_factor, partial_solve, precision=highest)
    z_first = r_second - jnp.dot(p_second, z_second, precision=highest)
    return (z_first, z_second)


def on_device(rhs_solved, generators, solved_gens):
    row_index = lax.axis_index("rows")
    sub_index = lax.axis_index("sub")
    groups = lax.axis_size("rows")
    sub_count = lax.axis_size("sub")
    current = rhs_solved
    solved_list = [solved_gens[0], solved_gens[1], solved_gens[2]]
    for level_index in range(3):
        child_count = 2 ** (3 - level_index)
        group_span = groups // child_count
        span_bits = group_span.bit_length() - 1
        child_index = row_index // group_span
        position = child_index % 2
        stacked = jnp.concatenate([current] + solved_list[level_index + 1 :], axis=1)
        col_count = stacked.shape[1]
        own_solved = solved_list[level_index]
        gen_level = generators[level_index]
        full_cols = jnp.concatenate([stacked, own_solved], axis=1)
        local_term = lax.dot_general(
            gen_level, full_cols, (((0,), (0,)), ((), ())), precision=highest
        )
        child_total = lax.psum(local_term, "sub")
        for bit_number in range(span_bits):
            child_total = child_total + from_partner(child_total, "rows", bit_number)
        sibling_sum = from_partner(child_total, "rows", span_bits)
        first_half = jnp.where(position == 0, child_total, sibling_sum)
        second_half = jnp.where(position == 0, sibling_sum, child_total)
        block_width = col_count // sub_count
        block_start = sub_index * block_width
        first_cols = lax.dynamic_slice_in_dim(
            first_half[:, :col_count], block_start, block_width, 1
        )
        second_cols = lax.dynamic_slice_in_dim(
            second_half[:, :col_count], block_start, block_width, 1
        )
        z_first, z_second = pair_solve(
            first_half[:, col_count:], second_half[:, col_count:], first_cols, second_cols
        )
        z_block = jnp.where(position == 0, z_first, z_second)
        z_own = lax.all_gather(z_block, "sub", axis=1, tiled=True)
        stacked = stacked - jnp.dot(own_solved, z_own, precision=highest)
        current = stacked[:, :RHS]
        for offset in range(2 - level_index):
            solved_list[level_index + 1 + offset] = stacked[
                :, RHS + offset * RANK : RHS + (offset + 1) * RANK
            ]
    return current


def solution(mesh):
    placed = (
        P(("rows", "sub"), None),
        P(None, ("rows", "sub"), None),
        P(None, ("rows", "sub"), None),
    )
    return jax.shard_map(
        on_device, mesh=mesh, in_specs=placed, out_specs=P(("rows", "sub"), None), check_vma=False
    )
```

profile of v0, /device:TPU:0, one launch (start us, length us, event | category | flops | bytes accessed | tf_op | source)
XLA Modules:
  0.0 704.3 jit_solution(10158698694177861485)
XLA Ops:
  6.5 3.2 fusion.161
  10.1 1.9 copy.27
  14.6 5.5 fusion.14
  20.4 37.8 %all-reduce.5.cloned.1.call-done = f32[256,896]{0,1:T(8,128)} async-done(((f32[256,896]{0,1:T(8,128)}), f32[256,896]{0,1:T(8,128)}) %all-reduce.5.cloned.1.call-update) | async-done | bytes 917520 | tf_op jit(solution)/shard_map/psum | solution.py:64
  59.7 20.0 %collective-permute-done = f32[256,896]{0,1:T(8,128)} collective-permute-done((f32[256,896]{0,1:T(8,128)}, f32[256,896]{0,1:T(8,128)}, u32[]{:S(2)}, u32[]{:S(2)}) %collective-permute-start) | collective-permute-done | bytes 917536 | tf_op jit(solution)/shard_map/ppermute | solution.py:16
  79.7 1.6 broadcast_select_fusion.1
  81.5 11.7 %cholesky.298 = f32[128,128]{1,0:T(8,128)S(1)} custom-call(f32[128,128]{1,0:T(8,128)S(1)} %cholesky.498), custom_call_target="Cholesky" | custom-call | tf_op jit(solution)/shard_map/jit(cholesky)/cholesky | solution.py:30
  93.3 9.8 %custom-call.37 = f32[1,128,128]{1,2,0:T(8,128)S(1)} custom-call(f32[1,128,128]{2,1,0:T(8,128)S(1)} %get-tuple-element.175), custom_call_target="InvertDiagBlocksLowerTriangular" | custom-call | tf_op jit(solution)/shard_map/jit(cholesky)/cholesky | solution.py:30
  103.6 11.7 %cholesky.315 = f32[128,128]{1,0:T(8,128)S(1)} custom-call(f32[128,128]{1,0:T(8,128)S(1)} %convolution_subtract_fusion.13), custom_call_target="Cholesky" | custom-call | tf_op jit(solution)/shard_map/jit(cholesky)/cholesky | solution.py:30
  121.1 12.1 %cholesky.332 = f32[128,128]{1,0:T(8,128)S(1)} custom-call(f32[128,128]{1,0:T(8,128)S(1)} %cholesky.501), custom_call_target="Cholesky" | custom-call | tf_op jit(solution)/shard_map/jit(cholesky)/cholesky | solution.py:34
  133.3 9.8 %custom-call.38 = f32[1,128,128]{1,2,0:T(8,128)S(1)} custom-call(f32[1,128,128]{2,1,0:T(8,128)S(1)} %get-tuple-element.171), custom_call_target="InvertDiagBlocksLowerTriangular" | custom-call | tf_op jit(solution)/shard_map/jit(cholesky)/cholesky | solution.py:34
  145.3 11.7 %cholesky.349 = f32[128,128]{1,0:T(8,128)S(1)} custom-call(f32[128,128]{1,0:T(8,128)S(1)} %convolution_subtract_fusion.12), custom_call_target="Cholesky" | custom-call | tf_op jit(solution)/shard_map/jit(cholesky)/cholesky | solution.py:34
  159.6 4.0 while.15
  163.6 19.7 %custom-call.26 = f32[2,128,128]{1,2,0:T(8,128)S(1)} custom-call(f32[2,128,128]{2,1,0:T(8,128)S(1)} %get-tuple-element.40), custom_call_target="InvertDiagBlocksLowerTriangular" | custom-call | tf_op jit(solution)/shard_map/triangular_solve | solution.py:25
  183.3 3.8 while.18
  187.2 19.7 %custom-call.39 = f32[2,128,128]{1,2,0:T(8,128)S(1)} custom-call(f32[2,128,128]{2,1,0:T(8,128)S(1)} %get-tuple-element.75), custom_call_target="InvertDiagBlocksLowerTriangular" | custom-call | tf_op jit(solution)/shard_map/triangular_solve/custom-call.0 | solution.py:20
  212.1 7.9 %all_gather.9 = f32[256,640]{0,1:T(8,128)S(1)} all-gather(f32[256,160]{0,1:T(8,128)S(1)} %fusion.20), channel_id=1, replica_groups=mesh['rows'=8,'sub'=4] {'sub'}, dimensions={1}, use_global_device_ids=true | all-gather | bytes 819200 | tf_op jit(solution)/shard_map/all_gather | solution.py:82
  220.0 4.1 maximum_subtract_fusion
  225.4 4.3 fusion.17
  230.2 33.7 %all-reduce.7.cloned.1.call-done = f32[256,640]{0,1:T(8,128)} async-done(((f32[256,640]{0,1:T(8,128)}), f32[256,640]{0,1:T(8,128)}) %all-reduce.7.cloned.1.call-update) | async-done | bytes 655376 | tf_op jit(solution)/shard_map/psum | solution.py:64
  265.4 14.0 %collective-permute-done.1 = f32[256,640]{0,1:T(8,128)S(1)} collective-permute-done((f32[256,640]{0,1:T(8,128)}, f32[256,640]{0,1:T(8,128)S(1)}, u32[]{:S(2)}, u32[]{:S(2)}) %collective-permute-start.1) | collective-permute-done | bytes 655392 | tf_op jit(solution)/shard_map/ppermute | solution.py:16
  280.6 1.8 collective-permute-start.2
  282.4 13.0 %collective-permute-done.2 = f32[256,640]{0,1:T(8,128)} collective-permute-done((f32[256,640]{0,1:T(8,128)S(1)}, f32[256,640]{0,1:T(8,128)}, u32[]{:S(2)}, u32[]{:S(2)}) %collective-permute-start.2) | collective-permute-done | bytes 655392 | tf_op jit(solution)/shard_map/ppermute | solution.py:16
  295.4 2.2 broadcast_select_fusion.3
  301.0 11.7 %cholesky.366 = f32[128,128]{1,0:T(8,128)S(1)} custom-call(f32[128,128]{1,0:T(8,128)S(1)} %cholesky.504), custom_call_target="Cholesky" | custom-call | tf_op jit(solution)/shard_map/jit(cholesky)/cholesky | solution.py:30
  314.8 11.3 %custom-call.41 = f32[1,128,128]{1,2,0:T(8,128)} custom-call(f32[1,128,128]{2,1,0:T(8,128)} %get-tuple-element.167), custom_call_target="InvertDiagBlocksLowerTriangular" | custom-call | tf_op jit(solution)/shard_map/jit(cholesky)/cholesky | solution.py:30
  327.2 1.7 convolution_subtract_fusion.11
  328.9 13.2 %cholesky.383 = f32[128,128]{1,0:T(8,128)} custom-call(f32[128,128]{1,0:T(8,128)} %convolution_subtract_fusion.11), custom_call_target="Cholesky" | custom-call | tf_op jit(solution)/shard_map/jit(cholesky)/cholesky | solution.py:30
  344.4 1.8 slice.320
  351.1 2.0 copy.14
  355.4 13.2 %cholesky.400 = f32[128,128]{1,0:T(8,128)} custom-call(f32[128,128]{1,0:T(8,128)} %cholesky.507), custom_call_target="Cholesky" | custom-call | tf_op jit(solution)/shard_map/jit(cholesky)/cholesky | solution.py:34
  370.1 1.6 cholesky.425
  371.7 11.3 %custom-call.42 = f32[1,128,128]{1,2,0:T(8,128)} custom-call(f32[1,128,128]{2,1,0:T(8,128)} %get-tuple-element.163), custom_call_target="InvertDiagBlocksLowerTriangular" | custom-call | tf_op jit(solution)/shard_map/jit(cholesky)/cholesky | solution.py:34
  382.9 1.7 constant_dynamic-update-slice_fusion.3
  384.6 1.7 convolution_subtract_fusion.10
  386.4 13.2 %cholesky.417 = f32[128,128]{1,0:T(8,128)} custom-call(f32[128,128]{1,0:T(8,128)} %convolution_subtract_fusion.10), custom_call_target="Cholesky" | custom-call | tf_op jit(solution)/shard_map/jit(cholesky)/cholesky | solution.py:34
  403.5 1.7 select_select_fusion.1
  405.8 7.0 while.16
  406.5 2.9 bitcast_dynamic-update-slice_fusion.13
  410.0 2.8 bitcast_dynamic-update-slice_fusion.13
  412.8 21.1 %custom-call.27 = f32[2,128,128]{1,2,0:T(8,128)} custom-call(f32[2,128,128]{2,1,0:T(8,128)} %get-tuple-element.48), custom_call_target="InvertDiagBlocksLowerTriangular" | custom-call | tf_op jit(solution)/shard_map/triangular_solve | solution.py:25
  434.5 6.8 while.19
  435.1 2.8 bitcast_dynamic-update-slice_fusion.16
  438.6 2.8 bitcast_dynamic-update-slice_fusion.16
  441.3 21.1 %custom-call.43 = f32[2,128,128]{1,2,0:T(8,128)} custom-call(f32[2,128,128]{2,1,0:T(8,128)} %get-tuple-element.77), custom_call_target="InvertDiagBlocksLowerTriangular" | custom-call | tf_op jit(solution)/shard_map/triangular_solve/custom-call.5 | solution.py:20
  475.0 7.5 %all_gather.10 = f32[256,384]{0,1:T(8,128)S(1)} all-gather(f32[256,96]{0,1:T(8,128)S(1)} %fusion.21), channel_id=1, replica_groups=mesh['rows'=8,'sub'=4] {'sub'}, dimensions={1}, use_global_device_ids=true | all-gather | bytes 491520 | tf_op jit(solution)/shard_map/all_gather | solution.py:82
  485.3 3.4 convolution_bitcast_fusion
  488.7 33.0 %all-reduce.9.cloned.1.call-done = f32[256,384]{0,1:T(8,128)} async-done(((f32[256,384]{0,1:T(8,128)}), f32[256,384]{0,1:T(8,128)}) %all-reduce.9.cloned.1.call-update) | async-done | bytes 393232 | tf_op jit(solution)/shard_map/psum | solution.py:64
  523.1 8.2 %collective-permute-done.3 = f32[256,384]{0,1:T(8,128)S(1)} collective-permute-done((f32[256,384]{0,1:T(8,128)}, f32[256,384]{0,1:T(8,128)S(1)}, u32[]{:S(2)}, u32[]{:S(2)}) %collective-permute-start.3) | collective-permute-done | bytes 393248 | tf_op jit(solution)/shard_map/ppermute | solution.py:16
  532.4 1.8 collective-permute-start.4
  534.2 7.1 %collective-permute-done.4 = f32[256,384]{0,1:T(8,128)S(1)} collective-permute-done((f32[256,384]{0,1:T(8,128)S(1)}, f32[256,384]{0,1:T(8,128)S(1)}, u32[]{:S(2)}, u32[]{:S(2)}) %collective-permute-start.4) | collective-permute-done | bytes 393248 | tf_op jit(solution)/shard_map/ppermute | solution.py:16
  541.4 3.1 collective-permute-start.5
  544.5 14.3 %collective-permute-done.5 = f32[256,384]{0,1:T(8,128)S(1)} collective-permute-done((f32[256,384]{0,1:T(8,128)S(1)}, f32[256,384]{0,1:T(8,128)S(1)}, u32[]{:S(2)}, u32[]{:S(2)}) %collective-permute-start.5) | collective-permute-done | bytes 393248 | tf_op jit(solution)/shard_map/ppermute | solution.py:16
  559.7 11.7 %cholesky.434 = f32[128,128]{1,0:T(8,128)S(1)} custom-call(f32[128,128]{1,0:T(8,128)S(1)} %cholesky.510), custom_call_target="Cholesky" | custom-call | tf_op jit(solution)/shard_map/jit(cholesky)/cholesky | solution.py:30
  571.4 9.8 %custom-call.45 = f32[1,128,128]{1,2,0:T(8,128)S(1)} custom-call(f32[1,128,128]{2,1,0:T(8,128)S(1)} %get-tuple-element.159), custom_call_target="InvertDiagBlocksLowerTriangular" | custom-call | tf_op jit(solution)/shard_map/jit(cholesky)/cholesky | solution.py:30
  581.7 11.9 %cholesky.451 = f32[128,128]{1,0:T(8,128)S(1)} custom-call(f32[128,128]{1,0:T(8,128)S(1)} %convolution_subtract_fusion.9), custom_call_target="Cholesky" | custom-call | tf_op jit(solution)/shard_map/jit(cholesky)/cholesky | solution.py:30
  597.8 11.7 %cholesky.468 = f32[128,128]{1,0:T(8,128)S(1)} custom-call(f32[128,128]{1,0:T(8,128)S(1)} %cholesky.513), custom_call_target="Cholesky" | custom-call | tf_op jit(solution)/shard_map/jit(cholesky)/cholesky | solution.py:34
  609.5 9.8 %custom-call.46 = f32[1,128,128]{1,2,0:T(8,128)S(1)} custom-call(f32[1,128,128]{2,1,0:T(8,128)S(1)} %get-tuple-element.155), custom_call_target="InvertDiagBlocksLowerTriangular" | custom-call | tf_op jit(solution)/shard_map/jit(cholesky)/cholesky | solution.py:34
  621.6 11.9 %cholesky.485 = f32[128,128]{1,0:T(8,128)S(1)} custom-call(f32[128,128]{1,0:T(8,128)S(1)} %convolution_subtract_fusion.8), custom_call_target="Cholesky" | custom-call | tf_op jit(solution)/shard_map/jit(cholesky)/cholesky | solution.py:34
  636.3 4.1 while.17
  640.4 19.7 %custom-call.28 = f32[2,128,128]{1,2,0:T(8,128)S(1)} custom-call(f32[2,128,128]{2,1,0:T(8,128)S(1)} %get-tuple-element.56), custom_call_target="InvertDiagBlocksLowerTriangular" | custom-call | tf_op jit(solution)/shard_map/triangular_solve | solution.py:25
  660.1 4.0 while.20
  664.1 20.3 %custom-call.47 = f32[2,128,128]{1,2,0:T(8,128)} custom-call(f32[2,128,128]{2,1,0:T(8,128)S(1)} %get-tuple-element.79), custom_call_target="InvertDiagBlocksLowerTriangular" | custom-call | tf_op jit(solution)/shard_map/triangular_solve/custom-call.7 | solution.py:20
  689.5 6.4 all_gather.11
  (198 shorter events, 93.9 us)
Async XLA Ops:
  6.5 51.7 %all-reduce.5.cloned.1.call-start = ((), (), s32[]{:S(2)}) async-start(), calls=%async_computation | async-start | bytes 1835008 | tf_op jit(solution)/shard_map/psum | solution.py:64
  10.1 4.6 copy-start.2
  12.0 8.1 %copy-start.3 = (f32[1,1024,256]{1,2,0:T(8,128)}, f32[1,1024,256]{1,2,0:T(8,128)S(1)}, u32[]{:S(2)}) copy-start(f32[1,1024,256]{1,2,0:T(8,128)S(1)} %copy.27) | copy-start | bytes 3145732
  20.1 243.8 %all-reduce.7.cloned.1.call-start = ((), (), s32[]{:S(2)}) async-start(), calls=%async_computation.1 | async-start | bytes 1310720 | tf_op jit(solution)/shard_map/psum | solution.py:64
  58.2 21.5 %collective-permute-start = (f32[256,896]{0,1:T(8,128)}, f32[256,896]{0,1:T(8,128)}, u32[]{:S(2)}, u32[]{:S(2)}) collective-permute-start(f32[256,896]{0,1:T(8,128)} %all-reduce.5.cloned.1.call-done), channel_id=1, source_target_pairs={{0,4},{4,0},{8,12},{12,8},{16,20},{20,16},{24,28},{28,24},{1,5},{5... | collective-permute-start | bytes 2752520 | tf_op jit(solution)/shard_map/ppermute | solution.py:16
  120.4 0.7 copy-start.9
  224.3 1.0 copy-start.4
  224.3 1.1 copy-start.7
  229.7 292.0 %all-reduce.9.cloned.1.call-start = ((), (), s32[]{:S(2)}) async-start(), calls=%async_computation.2 | async-start | bytes 786432 | tf_op jit(solution)/shard_map/psum | solution.py:64
  263.9 15.5 %collective-permute-start.1 = (f32[256,640]{0,1:T(8,128)}, f32[256,640]{0,1:T(8,128)S(1)}, u32[]{:S(2)}, u32[]{:S(2)}) collective-permute-start(f32[256,640]{0,1:T(8,128)} %all-reduce.7.cloned.1.call-done), channel_id=1, source_target_pairs={{0,4},{4,0},{8,12},{12,8},{16,20},{20,16},{24,28},{28,24},{1,5},{5... | collective-permute-start | bytes 1966088 | tf_op jit(solution)/shard_map/ppermute | solution.py:16
  280.6 1.8 copy-start.6
  280.6 14.8 %collective-permute-start.2 = (f32[256,640]{0,1:T(8,128)S(1)}, f32[256,640]{0,1:T(8,128)}, u32[]{:S(2)}, u32[]{:S(2)}) collective-permute-start(f32[256,640]{0,1:T(8,128)S(1)} %add.68), channel_id=1, source_target_pairs={{0,8},{4,12},{8,0},{12,4},{16,24},{20,28},{24,16},{28,20},{1,9},{5... | collective-permute-start | bytes 1966088 | tf_op jit(solution)/shard_map/ppermute | solution.py:16
  300.3 0.7 copy-start.12
  312.7 0.6 copy-start.13
  354.1 0.7 copy-start.10
  462.4 20.2 %copy-start.5 = (f32[1024,256]{0,1:T(8,128)S(1)}, f32[1024,256]{0,1:T(8,128)}, u32[]{:S(2)}) copy-start(f32[1024,256]{0,1:T(8,128)} %copy-done.4) | copy-start | bytes 3145732
  462.4 20.2 %copy-start.8 = (f32[1024,128]{0,1:T(8,128)S(1)}, f32[1024,128]{0,1:T(8,128)}, u32[]{:S(2)}) copy-start(f32[1024,128]{0,1:T(8,128)} %copy-done.7) | copy-start | bytes 1572868
  484.1 1.2 copy-start
  521.7 9.7 %collective-permute-start.3 = (f32[256,384]{0,1:T(8,128)}, f32[256,384]{0,1:T(8,128)S(1)}, u32[]{:S(2)}, u32[]{:S(2)}) collective-permute-start(f32[256,384]{0,1:T(8,128)} %all-reduce.9.cloned.1.call-done), channel_id=1, source_target_pairs={{0,4},{4,0},{8,12},{12,8},{16,20},{20,16},{24,28},{28,24},{1,5},{5... | collective-permute-start | bytes 1179656 | tf_op jit(solution)/shard_map/ppermute | solution.py:16
  532.4 8.9 %collective-permute-start.4 = (f32[256,384]{0,1:T(8,128)S(1)}, f32[256,384]{0,1:T(8,128)S(1)}, u32[]{:S(2)}, u32[]{:S(2)}) collective-permute-start(f32[256,384]{0,1:T(8,128)S(1)} %add.71), channel_id=1, source_target_pairs={{0,8},{4,12},{8,0},{12,4},{16,24},{20,28},{24,16},{28,20},{1,9},{5... | collective-permute-start | bytes 1179656 | tf_op jit(solution)/shard_map/ppermute | solution.py:16
  541.4 17.3 %collective-permute-start.5 = (f32[256,384]{0,1:T(8,128)S(1)}, f32[256,384]{0,1:T(8,128)S(1)}, u32[]{:S(2)}, u32[]{:S(2)}) collective-permute-start(f32[256,384]{0,1:T(8,128)S(1)} %add.72), channel_id=1, source_target_pairs={{0,16},{4,20},{8,24},{12,28},{16,0},{20,4},{24,8},{28,12},{1,17},{... | collective-permute-start | bytes 1179656 | tf_op jit(solution)/shard_map/ppermute | solution.py:16
  597.7 11.8 %copy-start.11 = (f32[256,256]{1,0:T(8,128)}, f32[256,256]{1,0:T(8,128)S(1)}, u32[]{:S(2)}) copy-start(f32[256,256]{1,0:T(8,128)S(1)} %fusion.31) | copy-start | bytes 786436
  619.4 76.5 %copy-start.1 = (f32[1024,384]{0,1:T(8,128)S(1)}, f32[1024,384]{0,1:T(8,128)}, u32[]{:S(2)}) copy-start(f32[1024,384]{0,1:T(8,128)} %copy-done) | copy-start | bytes 4718596
Sparse Core Ops, SparseCore 0:
  20.2 37.9 all-reduce.4
  229.8 34.0 all-reduce.6
  488.8 32.8 all-reduce.8
where the time goes:
time: 711 us; the launch traced here: 704 us
  other arithmetic  351 us (49%)
  waiting for transfers between devices  181 us (25%)
  matrix products  59 us (8%)
  local copies, waits for them, and re-layouts  57.3 us (8%)
  between operations  21.9 us (3%)
  blocking collectives  21.8 us (3%)
  starting transfers between devices  11.8 us (2%)
    another operation x21, other arithmetic, pair_solve(): inner_factor = jnp.linalg.cholesky(inner_matrix)  112 us
    another operation x20, other arithmetic, pair_solve(): lower_factor = jnp.linalg.cholesky(p_first)  108 us
    psum x3, waiting for transfers between devices, on_device(): child_total = lax.psum(local_term, 'sub')  105 us
    ppermute x6, waiting for transfers between devices, from_partner(): return lax.ppermute(value, axis, pairs)  76.6 us
    another operation x7, other arithmetic, factor_solve(): lax.linalg.triangular_solve(factor, middle, left_side=True, lower=True, t...  62.2 us
    another operation x6, other arithmetic, lower_solve(): lax.linalg.triangular_solve(factor, values, left_side=True, lower=True)  61.9 us
    all_gather x3, blocking collectives, on_device(): z_own = lax.all_gather(z_block, 'sub', axis=1, tiled=True)  21.8 us
    another operation x18, local copies, waits for them, and re-layouts  14.7 us
  transfers between devices with their start and end apart: 9, of which 9 were waited for; matrix products, arithmetic and copies ran while one was open for 0% of the time, Pallas kernels for 0%

commit v1 on v0

v1 whole, which is shorter than its diff:
```python
import jax
import jax.numpy as jnp
from jax import lax
from jax.experimental import pallas as pl
from jax.experimental.pallas import tpu as pltpu
from jax.sharding import PartitionSpec as P

RANK = 256
RHS = 128
HALF = RANK // 2
TOLERANCE = 1e-7
DIVERGED = 1e4
VMEM_LIMIT = 40 * 2**20

SMEM = pl.BlockSpec(memory_space=pltpu.SMEM)
VMEM = pl.BlockSpec(memory_space=pltpu.VMEM)


def swap(value, axis, bit):
    mask = 2**bit
    pairs = [(source, source ^ mask) for source in range(lax.axis_size(axis))]
    return lax.ppermute(value, axis, pairs)


def split(value):
    high = value.astype(jnp.bfloat16)
    low = (value - high.astype(jnp.float32)).astype(jnp.bfloat16)
    return high, low


def dot(left, right, contract=((1,), (0,))):
    def part(first, second):
        return lax.dot_general(first, second, (contract, ((), ())), preferred_element_type=jnp.float32)

    left_high, left_low = split(left)
    right_high, right_low = split(right)
    return part(left_high, right_high) + (part(left_high, right_low) + part(left_low, right_high))


def in_order(core, own, other):
    first = core == 0
    return jnp.concatenate([jnp.where(first, own, other), jnp.where(first, other, own)], axis=1)


def product_kernel(core_ref, *refs):
    *gens_refs, solved_ref, rhs_ref, keep_ref, send_ref, total = refs
    step = pl.program_id(0)
    for place, gens_ref in enumerate(gens_refs):
        rows = slice(place * RANK, (place + 1) * RANK)
        left = gens_ref[0].T
        for index in range(4):
            right = rhs_ref[...] if index == 3 else solved_ref[index]
            value = dot(left, right)
            cols = slice(index * RANK, index * RANK + value.shape[1])

            @pl.when(step == 0)
            def _():
                total[rows, cols] = value

            @pl.when(step > 0)
            def _():
                total[rows, cols] += value

    @pl.when(step == pl.num_programs(0) - 1)
    def _():
        first = core_ref[0] == 0
        for index in range(3):
            low = total[:, index * RANK : index * RANK + HALF]
            high = total[:, index * RANK + HALF : (index + 1) * RANK]
            cols = slice(index * HALF, (index + 1) * HALF)
            keep_ref[:, cols] = jnp.where(first, low, high)
            send_ref[:, cols] = jnp.where(first, high, low)
        keep_ref[:, 3 * HALF :] = total[:, 3 * RANK :]
        send_ref[:, 3 * HALF :] = total[:, 3 * RANK :]


def products(core, generators, solved_gens, rhs, wanted):
    rows = rhs.shape[0]
    block = 256
    levels = len(wanted)
    out = jax.ShapeDtypeStruct((levels * RANK, 3 * HALF + RHS), jnp.float32)

    def level_block(level):
        return pl.BlockSpec((1, block, RANK), lambda i: (level, i, 0))

    return pl.pallas_call(
        product_kernel,
        grid=(rows // block,),
        in_specs=[
            SMEM,
            *[level_block(level) for level in wanted],
            pl.BlockSpec((3, block, RANK), lambda i: (0, i, 0)),
            pl.BlockSpec((block, RHS), lambda i: (i, 0)),
        ],
        out_specs=[pl.BlockSpec(out.shape, lambda i: (0, 0))] * 2,
        out_shape=[out, out],
        scratch_shapes=[pltpu.VMEM((levels * RANK, 3 * RANK + RHS), jnp.float32)],
        compiler_params=pltpu.CompilerParams(vmem_limit_bytes=VMEM_LIMIT),
        cost_estimate=pl.CostEstimate(
            flops=6 * rows * levels * RANK * (3 * RANK + RHS),
            bytes_accessed=4 * rows * ((levels + 3) * RANK + RHS),
            transcendentals=0,
        ),
    )(core, *[generators] * levels, solved_gens, rhs)


def square_norm(value):
    return jnp.sum(value * value)


def series(power_ref, sum_ref):
    def proceed(state):
        count, norm, _ = state
        return (count < 60) & (norm > TOLERANCE) & (norm < DIVERGED * DIVERGED)

    def body(state):
        count, _, _ = state
        power = power_ref[...]
        norm = square_norm(power)
        values = sum_ref[...]
        both = dot(power, jnp.concatenate([power, values], axis=1))
        power_ref[...] = both[:, :RANK]
        sum_ref[...] = values + both[:, RANK:]
        return count + 1, norm, norm

    return lax.while_loop(proceed, body, (jnp.int32(0), jnp.float32(1.0), jnp.float32(1.0)))


def pair_solve(p_own, p_sibling, r_own, r_sibling, power_ref, sum_ref):
    both = dot(p_sibling, jnp.concatenate([p_own, r_own], axis=1))
    product = both[:, :RANK]
    shifted = r_sibling - both[:, RANK:]
    power_ref[...] = product
    sum_ref[...] = shifted
    _, norm, _ = series(power_ref, sum_ref)

    @pl.when(jnp.logical_not(norm <= TOLERANCE))
    def _():
        scale = 1.0 / (1.0 + jnp.sqrt(square_norm(product)))
        row = lax.broadcasted_iota(jnp.int32, (RANK, RANK), 0)
        col = lax.broadcasted_iota(jnp.int32, (RANK, RANK), 1)
        power_ref[...] = jnp.where(row == col, 1.0 - scale, 0.0) + scale * product
        sum_ref[...] = scale * shifted
        series(power_ref, sum_ref)

    return sum_ref[...]


def solve_kernel(core_ref, own_ref, sib_ref, other_ref, mixed_ref, mixed_other_ref, z_ref, next_ref, power, total):
    core = core_ref[0]
    p_own = in_order(core, own_ref[:, :HALF], other_ref[:, :HALF])
    p_sib = in_order(core, sib_ref[:, :HALF], other_ref[:, HALF:])
    z = pair_solve(p_own, p_sib, own_ref[:, HALF:], sib_ref[:, HALF:], power, total)
    z_ref[...] = z
    mixed = in_order(core, mixed_ref[:, :HALF], mixed_other_ref[...])
    next_ref[...] = mixed_ref[:, HALF:] - dot(mixed, z)


def solve(core, own, sib, other, mixed, mixed_other):
    width = own.shape[1] - HALF
    out = jax.ShapeDtypeStruct((RANK, width), jnp.float32)
    return pl.pallas_call(
        solve_kernel,
        in_specs=[SMEM] + [VMEM] * 5,
        out_specs=[VMEM] * 2,
        out_shape=[out, out],
        scratch_shapes=[pltpu.VMEM((RANK, RANK), jnp.float32), pltpu.VMEM((RANK, width), jnp.float32)],
        compiler_params=pltpu.CompilerParams(vmem_limit_bytes=VMEM_LIMIT),
        cost_estimate=pl.CostEstimate(flops=6 * 7 * RANK * RANK * 640, bytes_accessed=4 * RANK * 2560, transcendentals=0),
    )(core, own, sib, other, mixed, mixed_other)


def mix_kernel(core_ref, mixed_ref, other_ref, z_ref, next_ref):
    mixed = in_order(core_ref[0], mixed_ref[:, :HALF], other_ref[...])
    next_ref[...] = mixed_ref[:, HALF:] - dot(mixed, z_ref[...])


def mix(core, mixed, other, z):
    out = jax.ShapeDtypeStruct(z.shape, jnp.float32)
    return pl.pallas_call(
        mix_kernel,
        in_specs=[SMEM] + [VMEM] * 3,
        out_specs=VMEM,
        out_shape=out,
        compiler_params=pltpu.CompilerParams(vmem_limit_bytes=VMEM_LIMIT),
        cost_estimate=pl.CostEstimate(flops=6 * RANK * RANK * 384, bytes_accessed=4 * RANK * 1400, transcendentals=0),
    )(core, mixed, other, z)


def final_kernel(core_ref, own_ref, sib_ref, other_ref, z1_ref, z1_other_ref, z0_ref, z0_other_ref, solved_ref, rhs_ref, out_ref, power, total, coef):
    core = core_ref[0]

    @pl.when(pl.program_id(0) == 0)
    def _():
        p_own = in_order(core, own_ref[:, :HALF], other_ref[:, :HALF])
        p_sib = in_order(core, sib_ref[:, :HALF], other_ref[:, HALF:])
        last = pair_solve(p_own, p_sib, own_ref[:, HALF:], sib_ref[:, HALF:], power, total)
        middle = z1_ref[:, HALF:] - dot(in_order(core, z1_ref[:, :HALF], z1_other_ref[...]), last)
        z01 = in_order(core, z0_ref[:, :HALF], z0_other_ref[:, :HALF])
        z02 = in_order(core, z0_ref[:, HALF:RANK], z0_other_ref[:, HALF:])
        first = z0_ref[:, RANK:] - dot(z01, middle) - dot(z02, last)
        coef[0] = first
        coef[1] = middle
        coef[2] = last

    value = rhs_ref[...]
    for level in range(3):
        value = value - dot(solved_ref[level], coef[level])
    out_ref[...] = value


def final(core, own, sib, other, z1, z1_other, z0, z0_other, solved_gens, rhs):
    rows = rhs.shape[0]
    block = 256

    def whole(value):
        return pl.BlockSpec(value.shape, lambda i: (0, 0))

    small = (own, sib, other, z1, z1_other, z0, z0_other)
    return pl.pallas_call(
        final_kernel,
        grid=(rows // block,),
        in_specs=[SMEM]
        + [whole(value) for value in small]
        + [pl.BlockSpec((3, block, RANK), lambda i: (0, i, 0)), pl.BlockSpec((block, RHS), lambda i: (i, 0))],
        out_specs=pl.BlockSpec((block, RHS), lambda i: (i, 0)),
        out_shape=jax.ShapeDtypeStruct(rhs.shape, jnp.float32),
        scratch_shapes=[
            pltpu.VMEM((RANK, RANK), jnp.float32),
            pltpu.VMEM((RANK, RHS), jnp.float32),
            pltpu.VMEM((3, RANK, RHS), jnp.float32),
        ],
        compiler_params=pltpu.CompilerParams(vmem_limit_bytes=VMEM_LIMIT),
        cost_estimate=pl.CostEstimate(
            flops=6 * rows * 3 * RANK * RHS, bytes_accessed=4 * rows * 4 * RANK, transcendentals=0
        ),
    )(core, *small, solved_gens, rhs)


def on_device(rhs, generators, solved_gens):
    groups = lax.axis_size("rows")
    sub_bits = lax.axis_size("sub").bit_length() - 1
    span_bits = (groups // 8).bit_length() - 1
    core = (lax.axis_index("sub") % 2).astype(jnp.int32).reshape(1)

    keep, send = products(core, generators, solved_gens, rhs, (0,))
    low = keep + swap(send, "sub", 0)
    keep, send = products(core, generators, solved_gens, rhs, (1, 2))
    high = keep + swap(send, "sub", 0)
    for bit in range(1, sub_bits):
        low = low + swap(low, "sub", bit)
    for bit in range(span_bits):
        low = low + swap(low, "rows", bit)
    sibling = swap(low, "rows", span_bits)
    other = swap(jnp.concatenate([low[:, :HALF], sibling[:, :HALF]], axis=1), "sub", 0)
    for bit in range(1, sub_bits):
        high = high + swap(high, "sub", bit)
    for bit in range(span_bits):
        high = high + swap(high, "rows", bit)
    high_other = swap(high[:, :HALF], "sub", 0)

    z0, own = solve(core, low, sibling, other, high[:RANK], high_other[:RANK])
    own = own + swap(own, "rows", span_bits)
    sibling = swap(own, "rows", span_bits + 1)
    other = swap(jnp.concatenate([own[:, :HALF], sibling[:, :HALF]], axis=1), "sub", 0)
    third = mix(core, high[RANK:], high_other[RANK:], z0)
    third = third + swap(third, "rows", span_bits)
    third_other = swap(third[:, :HALF], "sub", 0)
    z0_other = swap(z0[:, :RANK], "sub", 0)

    z1, own = solve(core, own, sibling, other, third, third_other)
    own = own + swap(own, "rows", span_bits + 1)
    sibling = swap(own, "rows", span_bits + 2)
    other = swap(jnp.concatenate([own[:, :HALF], sibling[:, :HALF]], axis=1), "sub", 0)
    z1_other = swap(z1[:, :HALF], "sub", 0)
    return final(core, own, sibling, other, z1, z1_other, z0, z0_other, solved_gens, rhs)


def solution(mesh):
    placed = (
        P(("rows", "sub"), None),
        P(None, ("rows", "sub"), None),
        P(None, ("rows", "sub"), None),
    )
    return jax.shard_map(
        on_device, mesh=mesh, in_specs=placed, out_specs=P(("rows", "sub"), None), check_vma=False
    )
```

time: 711 us -> 127 us (0.18)
  other arithmetic: 351 us -> 0.75 us
  waiting for transfers between devices: 181 us -> 75.2 us
  matrix products: 59 us -> 0 us
  local copies, waits for them, and re-layouts: 57.3 us -> 5.07 us
  Pallas kernels: 0 us -> 31 us
  blocking collectives: 21.8 us -> 0 us
  between operations: 21.9 us -> 0.23 us
    another operation x54 -> x0, other arithmetic: 344 us -> none  [the longest x21 112 us: pair_solve(): inner_factor = jnp.linalg.cholesky(inner_matrix)]
    psum x3 -> x0, waiting for transfers between devices: 105 us -> none  [on_device(): child_total = lax.psum(local_term, 'sub')]
    another operation x49 -> x0, local copies, waits for them, and re-layouts: 32.4 us -> none
    dot_general x21 -> x0, matrix products: 32.3 us -> none  [the longest x3 13.1 us: on_device(): lax.dot_general(gen_level, full_cols, (((0,), (0,)), ((), ())), precision...]
    pallas_call x0 -> x6, Pallas kernels: none -> 31 us  [the longest x2 18.9 us: products(): pl.pallas_call(product_kernel, grid=(rows // block,), in_specs=[SMEM, *[l...]
    another operation x39 -> x0, matrix products: 26.7 us -> none  [the longest x6 7.85 us: pair_solve(): inner_factor = jnp.linalg.cholesky(inner_matrix)]
    all_gather x3 -> x0, blocking collectives: 21.8 us -> none  [on_device(): z_own = lax.all_gather(z_block, 'sub', axis=1, tiled=True)]
    slice x15 -> x12, local copies, waits for them, and re-layouts: 10.5 us -> 0.24 us  [the longest x2 0.09 us: on_device(): third = mix(core, high[RANK:], high_other[RANK:], z0)]
  transfers between devices with their start and end apart: 9 -> 17, of which waited for: 9 -> 12; matrix products, arithmetic and copies ran while one was open for 0% -> 1% of each run, Pallas kernels for 0% -> 5%
where the time goes in v1:
time: 127 us
  waiting for transfers between devices  75.2 us (59%)
  Pallas kernels  31 us (24%)
  starting transfers between devices  14.7 us (12%)
  local copies, waits for them, and re-layouts  5.07 us (4%)
    ppermute x17, waiting for transfers between devices, swap(): return lax.ppermute(value, axis, pairs)  75.2 us
    pallas_call x2, Pallas kernels, products(): pl.pallas_call(product_kernel, grid=(rows // block,), in_specs=[SMEM, *[l...  18.9 us
    ppermute x17, starting transfers between devices, swap(): return lax.ppermute(value, axis, pairs)  14.7 us
    pallas_call x2, Pallas kernels, solve(): pl.pallas_call(solve_kernel, in_specs=[SMEM] + [VMEM] * 5, out_specs=[VME...  5.91 us
    pallas_call x1, Pallas kernels, final(): pl.pallas_call(final_kernel, grid=(rows // block,), in_specs=[SMEM] + [wh...  5.77 us
    unnamed x10, local copies, waits for them, and re-layouts  4.83 us
  transfers between devices with their start and end apart: 17, of which 12 were waited for; matrix products, arithmetic and copies ran while one was open for 1% of the time, Pallas kernels for 5%

profile of v1, /device:TPU:0, one launch (start us, length us, event | category | flops | bytes accessed | tf_op | source)
XLA Modules:
  0.0 126.9 jit_solution(13793407312009159304)
XLA Ops:
  0.0 0.0 copy-start
  0.0 1.9 %copy-done = f32[3,1024,256]{2,1,0:T(8,128)S(1)} copy-done((f32[3,1024,256]{2,1,0:T(8,128)S(1)}, f32[3,1024,256]{2,1,0:T(8,128)}, u32[]{:S(2)}) %copy-start) | copy-done | bytes 3145752
  1.9 0.0 copy-start.2
  1.9 1.9 %copy-done.2 = f32[3,1024,256]{2,1,0:T(8,128)S(1)} copy-done((f32[3,1024,256]{2,1,0:T(8,128)S(1)}, f32[3,1024,256]{2,1,0:T(8,128)}, u32[]{:S(2)}) %copy-start.2) | copy-done | bytes 3145752
  3.8 0.0 copy-start.3
  3.8 1.0 copy-done.3
  4.8 12.5 %shard_map.38 = (f32[512,512]{1,0:T(8,128)S(1)}, f32[512,512]{1,0:T(8,128)S(1)}) custom-call(s32[1]{0:T(128)} %bitcast.core_ref, f32[3,1024,256]{2,1,0:T(8,128)S(1)} %copy-done.2, f32[3,1024,256]{2,1,0:T(8,128)S(1)} %copy-done.2, f32[3,1024,256]{2,1,0:T(8,128)S(1)} %copy-done, f32[1024,128]{1,0:T(8,128)S(1)} %copy-done.3), custom_call_target="tpu_custom_call" | custom-call | flops 2818572288 | bytes 5767168 | tf_op jit(solution)/shard_map/pallas_call | solution.py:86
  17.4 0.5 collective-permute-start.4
  17.9 6.4 %shard_map.37 = (f32[256,512]{1,0:T(8,128)S(1)}, f32[256,512]{1,0:T(8,128)S(1)}) custom-call(s32[1]{0:T(128)} %bitcast.core_ref, f32[3,1024,256]{2,1,0:T(8,128)S(1)} %copy-done.2, f32[3,1024,256]{2,1,0:T(8,128)S(1)} %copy-done, f32[1024,128]{1,0:T(8,128)S(1)} %copy-done.3), custom_call_target="tpu_custom_call" | custom-call | flops 1409286144 | bytes 4718592 | tf_op jit(solution)/shard_map/pallas_call | solution.py:86
  24.3 0.1 collective-permute-start
  24.4 1.9 %collective-permute-done = f32[256,512]{1,0:T(8,128)S(1)} collective-permute-done((f32[256,512]{1,0:T(8,128)S(1)}, f32[256,512]{1,0:T(8,128)S(1)}, u32[]{:S(2)}, u32[]{:S(2)}) %collective-permute-start) | collective-permute-done | bytes 524320 | tf_op jit(solution)/shard_map/ppermute | solution.py:22
  26.3 0.1 add.26
  26.3 2.7 %collective-permute-start.1 = (f32[256,512]{1,0:T(8,128)S(1)}, f32[256,512]{1,0:T(8,128)S(1)}, u32[]{:S(2)}, u32[]{:S(2)}) collective-permute-start(f32[256,512]{1,0:T(8,128)S(1)} %add.26), channel_id=1, source_target_pairs={{0,2},{1,3},{2,0},{3,1},{4,6},{5,7},{6,4},{7,5},{8,10},{9,11},{10,... | collective-permute-start | bytes 1572872 | tf_op jit(solution)/shard_map/ppermute | solution.py:22
  29.1 0.0 collective-permute-done.4
  29.1 0.2 add.28
  29.3 0.1 collective-permute-start.5
  29.4 12.5 %collective-permute-done.1 = f32[256,512]{1,0:T(8,128)S(1)} collective-permute-done((f32[256,512]{1,0:T(8,128)S(1)}, f32[256,512]{1,0:T(8,128)S(1)}, u32[]{:S(2)}, u32[]{:S(2)}) %collective-permute-start.1) | collective-permute-done | bytes 524320 | tf_op jit(solution)/shard_map/ppermute | solution.py:22
  41.8 0.1 add.27.own_ref
  41.9 2.0 %collective-permute-start.2 = (f32[256,512]{1,0:T(8,128)S(1)}, f32[256,512]{1,0:T(8,128)S(1)}, u32[]{:S(2)}, u32[]{:S(2)}) collective-permute-start(f32[256,512]{1,0:T(8,128)S(1)} %add.27.own_ref), channel_id=1, source_target_pairs={{0,4},{4,0},{8,12},{12,8},{16,20},{20,16},{24,28},{28,24},{1,5},{5... | collective-permute-start | bytes 1572872 | tf_op jit(solution)/shard_map/ppermute | solution.py:22
  44.0 11.3 %collective-permute-done.2.sib_ref = f32[256,512]{1,0:T(8,128)S(1)} collective-permute-done((f32[256,512]{1,0:T(8,128)S(1)}, f32[256,512]{1,0:T(8,128)S(1)}, u32[]{:S(2)}, u32[]{:S(2)}) %collective-permute-start.2) | collective-permute-done | bytes 524320 | tf_op jit(solution)/shard_map/ppermute | solution.py:22
  55.3 0.1 collective-permute-start.3
  55.4 8.6 %collective-permute-done.5 = f32[512,512]{1,0:T(8,128)S(1)} collective-permute-done((f32[512,512]{1,0:T(8,128)S(1)}, f32[512,512]{1,0:T(8,128)S(1)}, u32[]{:S(2)}, u32[]{:S(2)}) %collective-permute-start.5) | collective-permute-done | bytes 1048608 | tf_op jit(solution)/shard_map/ppermute | solution.py:22
  64.0 0.2 add.29
  64.2 0.1 collective-permute-start.6
  64.3 0.1 fusion
  64.4 1.4 %collective-permute-done.6 = f32[512,128]{1,0:T(8,128)S(1)} collective-permute-done((f32[512,128]{1,0:T(8,128)S(1)}, f32[512,128]{1,0:T(8,128)S(1)}, u32[]{:S(2)}, u32[]{:S(2)}) %collective-permute-start.6) | collective-permute-done | bytes 262176 | tf_op jit(solution)/shard_map/ppermute | solution.py:22
  65.9 0.0 collective-permute-done.3.other_ref
  65.9 3.3 %shard_map.39 = (f32[256,384]{1,0:T(8,128)S(1)}, f32[256,384]{1,0:T(8,128)S(1)}) custom-call(s32[1]{0:T(128)} %bitcast.core_ref, f32[256,512]{1,0:T(8,128)S(1)} %add.27.own_ref, f32[256,512]{1,0:T(8,128)S(1)} %collective-permute-done.2.sib_ref, f32[256,256]{1,0:T(8,128)S(1)} %collective-permute-done.3.other_ref, f32[256,512]{1,0:T(8,128)S(1)} %get-tuple-element.22.mixed_ref, ...), custom_call_target="tpu_custom_call" | custom-call | flops 1761607680 | bytes 2621440 | tf_op jit(solution)/shard_map/pallas_call | solution.py:162
  69.2 1.8 %collective-permute-start.7 = (f32[256,384]{1,0:T(8,128)S(1)}, f32[256,384]{1,0:T(8,128)S(1)}, u32[]{:S(2)}, u32[]{:S(2)}) collective-permute-start(f32[256,384]{1,0:T(8,128)S(1)} %get-tuple-element.17), channel_id=1, source_target_pairs={{0,4},{4,0},{8,12},{12,8},{16,20},{20,16},{24,28},{28,24},{1,5},{5... | collective-permute-start | bytes 1179656 | tf_op jit(solution)/shard_map/ppermute | solution.py:22
  71.0 9.4 %collective-permute-done.7 = f32[256,384]{1,0:T(8,128)S(1)} collective-permute-done((f32[256,384]{1,0:T(8,128)S(1)}, f32[256,384]{1,0:T(8,128)S(1)}, u32[]{:S(2)}, u32[]{:S(2)}) %collective-permute-start.7) | collective-permute-done | bytes 393248 | tf_op jit(solution)/shard_map/ppermute | solution.py:22
  80.5 1.9 %collective-permute-start.8 = (f32[256,384]{1,0:T(8,128)S(1)}, f32[256,384]{1,0:T(8,128)S(1)}, u32[]{:S(2)}, u32[]{:S(2)}) collective-permute-start(f32[256,384]{1,0:T(8,128)S(1)} %add.30.own_ref), channel_id=1, source_target_pairs={{0,8},{4,12},{8,0},{12,4},{16,24},{20,28},{24,16},{28,20},{1,9},{5... | collective-permute-start | bytes 1179656 | tf_op jit(solution)/shard_map/ppermute | solution.py:22
  82.4 0.4 shard_map.40
  82.7 1.6 %collective-permute-start.10 = (f32[256,384]{1,0:T(8,128)S(1)}, f32[256,384]{1,0:T(8,128)S(1)}, u32[]{:S(2)}, u32[]{:S(2)}) collective-permute-start(f32[256,384]{1,0:T(8,128)S(1)} %shard_map.40), channel_id=1, source_target_pairs={{0,4},{4,0},{8,12},{12,8},{16,20},{20,16},{24,28},{28,24},{1,5},{5... | collective-permute-start | bytes 1179656 | tf_op jit(solution)/shard_map/ppermute | solution.py:22
  84.3 6.6 %collective-permute-done.8.sib_ref = f32[256,384]{1,0:T(8,128)S(1)} collective-permute-done((f32[256,384]{1,0:T(8,128)S(1)}, f32[256,384]{1,0:T(8,128)S(1)}, u32[]{:S(2)}, u32[]{:S(2)}) %collective-permute-start.8) | collective-permute-done | bytes 393248 | tf_op jit(solution)/shard_map/ppermute | solution.py:22
  91.0 0.1 collective-permute-start.9
  91.1 1.8 %collective-permute-done.10 = f32[256,384]{1,0:T(8,128)S(1)} collective-permute-done((f32[256,384]{1,0:T(8,128)S(1)}, f32[256,384]{1,0:T(8,128)S(1)}, u32[]{:S(2)}, u32[]{:S(2)}) %collective-permute-start.10) | collective-permute-done | bytes 393248 | tf_op jit(solution)/shard_map/ppermute | solution.py:22
  92.9 0.0 copy-start.1
  92.9 0.0 copy-start.4
  92.9 0.1 collective-permute-start.11
  93.0 1.3 %collective-permute-done.11.mixed_other_ref = f32[256,128]{1,0:T(8,128)S(1)} collective-permute-done((f32[256,128]{1,0:T(8,128)S(1)}, f32[256,128]{1,0:T(8,128)S(1)}, u32[]{:S(2)}, u32[]{:S(2)}) %collective-permute-start.11) | collective-permute-done | bytes 131104 | tf_op jit(solution)/shard_map/ppermute | solution.py:22
  94.3 0.0 collective-permute-done.9.other_ref
  94.3 2.6 %shard_map.41 = (f32[256,256]{1,0:T(8,128)S(1)}, f32[256,256]{1,0:T(8,128)S(1)}) custom-call(s32[1]{0:T(128)} %bitcast.core_ref, f32[256,384]{1,0:T(8,128)S(1)} %add.30.own_ref, f32[256,384]{1,0:T(8,128)S(1)} %collective-permute-done.8.sib_ref, f32[256,256]{1,0:T(8,128)S(1)} %collective-permute-done.9.other_ref, f32[256,384]{1,0:T(8,128)S(1)} %add.31.mixed_ref, ...), custom_call_target="tpu_custom_call" | custom-call | flops 1761607680 | bytes 2621440 | tf_op jit(solution)/shard_map/pallas_call | solution.py:162
  96.9 0.4 collective-permute-start.12
  97.3 8.1 %collective-permute-done.12 = f32[256,256]{1,0:T(8,128)S(1)} collective-permute-done((f32[256,256]{1,0:T(8,128)S(1)}, f32[256,256]{1,0:T(8,128)S(1)}, u32[]{:S(2)}, u32[]{:S(2)}) %collective-permute-start.12) | collective-permute-done | bytes 262176 | tf_op jit(solution)/shard_map/ppermute | solution.py:22
  105.4 2.7 %collective-permute-start.13 = (f32[256,256]{1,0:T(8,128)S(1)}, f32[256,256]{1,0:T(8,128)S(1)}, u32[]{:S(2)}, u32[]{:S(2)}) collective-permute-start(f32[256,256]{1,0:T(8,128)S(1)} %add.32.own_ref), channel_id=1, source_target_pairs={{0,16},{4,20},{8,24},{12,28},{16,0},{20,4},{24,8},{28,12},{1,17},{... | collective-permute-start | bytes 786440 | tf_op jit(solution)/shard_map/ppermute | solution.py:22
  108.1 0.1 collective-permute-start.16
  108.2 11.2 %collective-permute-done.13.sib_ref = f32[256,256]{1,0:T(8,128)S(1)} collective-permute-done((f32[256,256]{1,0:T(8,128)S(1)}, f32[256,256]{1,0:T(8,128)S(1)}, u32[]{:S(2)}, u32[]{:S(2)}) %collective-permute-start.13) | collective-permute-done | bytes 262176 | tf_op jit(solution)/shard_map/ppermute | solution.py:22
  119.4 0.1 collective-permute-start.14
  119.5 0.6 collective-permute-start.15
  120.0 0.0 collective-permute-done.16.z0_other_ref
  120.0 1.1 collective-permute-done.15.z1_other_ref
  121.2 0.0 collective-permute-done.14.other_ref
  121.2 0.0 copy-done.1
  121.2 0.0 copy-done.4
  121.2 5.8 %shard_map.42 = f32[1024,128]{1,0:T(8,128)} custom-call(s32[1]{0:T(128)} %bitcast.core_ref, f32[256,256]{1,0:T(8,128)S(1)} %add.32.own_ref, f32[256,256]{1,0:T(8,128)S(1)} %collective-permute-done.13.sib_ref, f32[256,256]{1,0:T(8,128)S(1)} %collective-permute-done.14.other_ref, f32[256,256]{1,0:T(8,128)S(1)} %get-tuple-element.20.z1_ref, ...), custom_call_target="tpu_custom_call" | custom-call | flops 603979776 | bytes 4194304 | tf_op jit(solution)/shard_map/pallas_call | solution.py:220
  (17 shorter events, 0.3 us)
Async XLA Ops:
  0.0 1.9 %copy-start = (f32[3,1024,256]{2,1,0:T(8,128)S(1)}, f32[3,1024,256]{2,1,0:T(8,128)}, u32[]{:S(2)}) copy-start(f32[3,1024,256]{2,1,0:T(8,128)} %solved_ref.1) | copy-start | bytes 9437188
  1.9 1.9 %copy-start.2 = (f32[3,1024,256]{2,1,0:T(8,128)S(1)}, f32[3,1024,256]{2,1,0:T(8,128)}, u32[]{:S(2)}) copy-start(f32[3,1024,256]{2,1,0:T(8,128)} %refs_1_.3) | copy-start | bytes 9437188
  3.8 1.0 copy-start.3
  17.4 11.7 %collective-permute-start.4 = (f32[512,512]{1,0:T(8,128)S(1)}, f32[512,512]{1,0:T(8,128)S(1)}, u32[]{:S(2)}, u32[]{:S(2)}) collective-permute-start(f32[512,512]{1,0:T(8,128)S(1)} %get-tuple-element.16), channel_id=1, source_target_pairs={{0,1},{1,0},{2,3},{3,2},{4,5},{5,4},{6,7},{7,6},{8,9},{9,8},{10,11... | collective-permute-start | bytes 3145736 | tf_op jit(solution)/shard_map/ppermute | solution.py:22
  24.3 2.0 %collective-permute-start = (f32[256,512]{1,0:T(8,128)S(1)}, f32[256,512]{1,0:T(8,128)S(1)}, u32[]{:S(2)}, u32[]{:S(2)}) collective-permute-start(f32[256,512]{1,0:T(8,128)S(1)} %get-tuple-element.14), channel_id=1, source_target_pairs={{0,1},{1,0},{2,3},{3,2},{4,5},{5,4},{6,7},{7,6},{8,9},{9,8},{10,11... | collective-permute-start | bytes 1572872 | tf_op jit(solution)/shard_map/ppermute | solution.py:22
  26.3 15.5 %collective-permute-start.1 = (f32[256,512]{1,0:T(8,128)S(1)}, f32[256,512]{1,0:T(8,128)S(1)}, u32[]{:S(2)}, u32[]{:S(2)}) collective-permute-start(f32[256,512]{1,0:T(8,128)S(1)} %add.26), channel_id=1, source_target_pairs={{0,2},{1,3},{2,0},{3,1},{4,6},{5,7},{6,4},{7,5},{8,10},{9,11},{10,... | collective-permute-start | bytes 1572872 | tf_op jit(solution)/shard_map/ppermute | solution.py:22
  29.3 34.7 %collective-permute-start.5 = (f32[512,512]{1,0:T(8,128)S(1)}, f32[512,512]{1,0:T(8,128)S(1)}, u32[]{:S(2)}, u32[]{:S(2)}) collective-permute-start(f32[512,512]{1,0:T(8,128)S(1)} %add.28), channel_id=1, source_target_pairs={{0,2},{1,3},{2,0},{3,1},{4,6},{5,7},{6,4},{7,5},{8,10},{9,11},{10,... | collective-permute-start | bytes 3145736 | tf_op jit(solution)/shard_map/ppermute | solution.py:22
  41.9 13.4 %collective-permute-start.2 = (f32[256,512]{1,0:T(8,128)S(1)}, f32[256,512]{1,0:T(8,128)S(1)}, u32[]{:S(2)}, u32[]{:S(2)}) collective-permute-start(f32[256,512]{1,0:T(8,128)S(1)} %add.27.own_ref), channel_id=1, source_target_pairs={{0,4},{4,0},{8,12},{12,8},{16,20},{20,16},{24,28},{28,24},{1,5},{5... | collective-permute-start | bytes 1572872 | tf_op jit(solution)/shard_map/ppermute | solution.py:22
  55.3 10.5 %collective-permute-start.3 = (f32[256,256]{1,0:T(8,128)S(1)}, f32[256,256]{1,0:T(8,128)S(1)}, u32[]{:S(2)}, u32[]{:S(2)}) collective-permute-start(f32[256,256]{1,0:T(8,128)S(1)} %pad_maximum_fusion), channel_id=1, source_target_pairs={{0,1},{1,0},{2,3},{3,2},{4,5},{5,4},{6,7},{7,6},{8,9},{9,8},{10,11... | collective-permute-start | bytes 786440 | tf_op jit(solution)/shard_map/ppermute | solution.py:22
  64.2 1.6 %collective-permute-start.6 = (f32[512,128]{1,0:T(8,128)S(1)}, f32[512,128]{1,0:T(8,128)S(1)}, u32[]{:S(2)}, u32[]{:S(2)}) collective-permute-start(f32[512,128]{1,0:T(8,128)S(1)} %slice.59), channel_id=1, source_target_pairs={{0,1},{1,0},{2,3},{3,2},{4,5},{5,4},{6,7},{7,6},{8,9},{9,8},{10,11... | collective-permute-start | bytes 786440 | tf_op jit(solution)/shard_map/ppermute | solution.py:22
  69.2 11.2 %collective-permute-start.7 = (f32[256,384]{1,0:T(8,128)S(1)}, f32[256,384]{1,0:T(8,128)S(1)}, u32[]{:S(2)}, u32[]{:S(2)}) collective-permute-start(f32[256,384]{1,0:T(8,128)S(1)} %get-tuple-element.17), channel_id=1, source_target_pairs={{0,4},{4,0},{8,12},{12,8},{16,20},{20,16},{24,28},{28,24},{1,5},{5... | collective-permute-start | bytes 1179656 | tf_op jit(solution)/shard_map/ppermute | solution.py:22
  80.5 10.4 %collective-permute-start.8 = (f32[256,384]{1,0:T(8,128)S(1)}, f32[256,384]{1,0:T(8,128)S(1)}, u32[]{:S(2)}, u32[]{:S(2)}) collective-permute-start(f32[256,384]{1,0:T(8,128)S(1)} %add.30.own_ref), channel_id=1, source_target_pairs={{0,8},{4,12},{8,0},{12,4},{16,24},{20,28},{24,16},{28,20},{1,9},{5... | collective-permute-start | bytes 1179656 | tf_op jit(solution)/shard_map/ppermute | solution.py:22
  82.7 10.1 %collective-permute-start.10 = (f32[256,384]{1,0:T(8,128)S(1)}, f32[256,384]{1,0:T(8,128)S(1)}, u32[]{:S(2)}, u32[]{:S(2)}) collective-permute-start(f32[256,384]{1,0:T(8,128)S(1)} %shard_map.40), channel_id=1, source_target_pairs={{0,4},{4,0},{8,12},{12,8},{16,20},{20,16},{24,28},{28,24},{1,5},{5... | collective-permute-start | bytes 1179656 | tf_op jit(solution)/shard_map/ppermute | solution.py:22
  91.0 3.4 %collective-permute-start.9 = (f32[256,256]{1,0:T(8,128)S(1)}, f32[256,256]{1,0:T(8,128)S(1)}, u32[]{:S(2)}, u32[]{:S(2)}) collective-permute-start(f32[256,256]{1,0:T(8,128)S(1)} %pad_maximum_fusion.1), channel_id=1, source_target_pairs={{0,1},{1,0},{2,3},{3,2},{4,5},{5,4},{6,7},{7,6},{8,9},{9,8},{10,11... | collective-permute-start | bytes 786440 | tf_op jit(solution)/shard_map/ppermute | solution.py:22
  92.9 28.3 %copy-start.1 = (f32[3,1024,256]{2,1,0:T(8,128)S(1)}, f32[3,1024,256]{2,1,0:T(8,128)}, u32[]{:S(2)}) copy-start(f32[3,1024,256]{2,1,0:T(8,128)} %solved_ref.1) | copy-start | bytes 9437188
  92.9 28.3 %copy-start.4 = (f32[1024,128]{1,0:T(8,128)S(1)}, f32[1024,128]{1,0:T(8,128)}, u32[]{:S(2)}) copy-start(f32[1024,128]{1,0:T(8,128)} %rhs_ref.1) | copy-start | bytes 1572868
  92.9 1.4 %collective-permute-start.11 = (f32[256,128]{1,0:T(8,128)S(1)}, f32[256,128]{1,0:T(8,128)S(1)}, u32[]{:S(2)}, u32[]{:S(2)}) collective-permute-start(f32[256,128]{1,0:T(8,128)S(1)} %slice.65), channel_id=1, source_target_pairs={{0,1},{1,0},{2,3},{3,2},{4,5},{5,4},{6,7},{7,6},{8,9},{9,8},{10,11... | collective-permute-start | bytes 393224 | tf_op jit(solution)/shard_map/ppermute | solution.py:22
  96.9 8.4 %collective-permute-start.12 = (f32[256,256]{1,0:T(8,128)S(1)}, f32[256,256]{1,0:T(8,128)S(1)}, u32[]{:S(2)}, u32[]{:S(2)}) collective-permute-start(f32[256,256]{1,0:T(8,128)S(1)} %get-tuple-element.19), channel_id=1, source_target_pairs={{0,8},{4,12},{8,0},{12,4},{16,24},{20,28},{24,16},{28,20},{1,9},{5... | collective-permute-start | bytes 786440 | tf_op jit(solution)/shard_map/ppermute | solution.py:22
  105.4 14.0 %collective-permute-start.13 = (f32[256,256]{1,0:T(8,128)S(1)}, f32[256,256]{1,0:T(8,128)S(1)}, u32[]{:S(2)}, u32[]{:S(2)}) collective-permute-start(f32[256,256]{1,0:T(8,128)S(1)} %add.32.own_ref), channel_id=1, source_target_pairs={{0,16},{4,20},{8,24},{12,28},{16,0},{20,4},{24,8},{28,12},{1,17},{... | collective-permute-start | bytes 786440 | tf_op jit(solution)/shard_map/ppermute | solution.py:22
  108.1 12.0 %collective-permute-start.16 = (f32[256,256]{1,0:T(8,128)S(1)}, f32[256,256]{1,0:T(8,128)S(1)}, u32[]{:S(2)}, u32[]{:S(2)}) collective-permute-start(f32[256,256]{1,0:T(8,128)S(1)} %slice.55), channel_id=1, source_target_pairs={{0,1},{1,0},{2,3},{3,2},{4,5},{5,4},{6,7},{7,6},{8,9},{9,8},{10,11... | collective-permute-start | bytes 786440 | tf_op jit(solution)/shard_map/ppermute | solution.py:22
  119.4 1.8 %collective-permute-start.14 = (f32[256,256]{1,0:T(8,128)S(1)}, f32[256,256]{1,0:T(8,128)S(1)}, u32[]{:S(2)}, u32[]{:S(2)}) collective-permute-start(f32[256,256]{1,0:T(8,128)S(1)} %pad_maximum_fusion.2), channel_id=1, source_target_pairs={{0,1},{1,0},{2,3},{3,2},{4,5},{5,4},{6,7},{7,6},{8,9},{9,8},{10,11... | collective-permute-start | bytes 786440 | tf_op jit(solution)/shard_map/ppermute | solution.py:22
  119.5 1.7 %collective-permute-start.15 = (f32[256,128]{1,0:T(8,128)S(1)}, f32[256,128]{1,0:T(8,128)S(1)}, u32[]{:S(2)}, u32[]{:S(2)}) collective-permute-start(f32[256,128]{1,0:T(8,128)S(1)} %slice.54), channel_id=1, source_target_pairs={{0,1},{1,0},{2,3},{3,2},{4,5},{5,4},{6,7},{7,6},{8,9},{9,8},{10,11... | collective-permute-start | bytes 393224 | tf_op jit(solution)/shard_map/ppermute | solution.py:22

commit v2 on v0

v2 whole, which is shorter than its diff:
```python
import functools

import jax
import jax.numpy as jnp
from jax import lax
from jax.experimental import pallas as pl
from jax.experimental.pallas import tpu as pltpu
from jax.sharding import PartitionSpec as P

RANK = 256
RHS = 128
HALF = RANK // 2
QUARTER = HALF // 2
TOLERANCE = 1e-7
DIVERGED = 1e4
VMEM_LIMIT = 40 * 2**20
STREAM_LIMIT = 52 * 2**20

SMEM = pl.BlockSpec(memory_space=pltpu.SMEM)
VMEM = pl.BlockSpec(memory_space=pltpu.VMEM)
HBM = pl.BlockSpec(memory_space=pltpu.HBM)
ANY = pl.BlockSpec(memory_space=pl.ANY)


def swap(value, axis, bit):
    mask = 2**bit
    pairs = [(source, source ^ mask) for source in range(lax.axis_size(axis))]
    return lax.ppermute(value, axis, pairs)


def struct(rows, cols=HALF):
    return jax.ShapeDtypeStruct((rows, cols), jnp.float32)


def cost(flops, floats):
    return pl.CostEstimate(flops=int(flops), bytes_accessed=int(4 * floats), transcendentals=0)


def split(value):
    high = value.astype(jnp.bfloat16)
    low = (value - high.astype(jnp.float32)).astype(jnp.bfloat16)
    return high, low


def dot_parts(left, right):
    def part(first, second):
        return lax.dot_general(first, second, (((1,), (0,)), ((), ())), preferred_element_type=jnp.float32)

    return part(left[0], right[0]) + (part(left[0], right[1]) + part(left[1], right[0]))


def dot(left, right):
    return dot_parts(split(left), split(right))


def in_order(core, own, other):
    first = core == 0
    return jnp.concatenate([jnp.where(first, own, other), jnp.where(first, other, own)], axis=1)


def pack(value):
    whole = value.shape[1] // HALF
    units = [value[:, index * HALF : (index + 1) * HALF] for index in range(whole)]
    if value.shape[1] % HALF:
        tail = value[:, whole * HALF :]
        units.append(jnp.concatenate([tail[:HALF], tail[HALF:]], axis=1))
    return units


def unpack(ref):
    whole = ref.shape[0] // RANK
    parts = [ref[index * RANK : (index + 1) * RANK, :] for index in range(whole)]
    if ref.shape[0] % RANK:
        tail = ref[whole * RANK :, :]
        parts.append(jnp.concatenate([tail[:, :QUARTER], tail[:, QUARTER:]], axis=0))
    return jnp.concatenate(parts, axis=1) if len(parts) > 1 else parts[0]


def store(ref, value):
    start = 0
    for unit in pack(value):
        ref[start : start + unit.shape[0], :] = unit
        start += unit.shape[0]


def product_kernel(lefts, rights, core_ref, gens_ref, solved_ref, rhs_ref, *refs):
    keep_ref, send_ref, gens, solved, rhs, total, sems = refs[-7:]
    chunks = sems.shape[1]
    block = gens.shape[1] // chunks
    copies = []
    for chunk in range(chunks):
        rows = pl.ds(chunk * block, block)
        row = []
        for place, level in enumerate(lefts):
            row.append((gens_ref.at[level, rows], gens.at[place, rows]))
        for place, level in enumerate(rights):
            if level < 3:
                row.append((solved_ref.at[level, rows], solved.at[place, rows]))
            else:
                row.append((rhs_ref.at[rows], rhs.at[rows]))
        row = [pltpu.make_async_copy(*ends, sems.at[index, chunk]) for index, ends in enumerate(row)]
        for copy in row:
            copy.start()
        copies.append(row)
    for chunk in range(chunks):
        rows = pl.ds(chunk * block, block)
        for copy in copies[chunk]:
            copy.wait()
        right = [rhs[rows, :] if level == 3 else solved[place, rows, :] for place, level in enumerate(rights)]
        right = split(jnp.concatenate(right, axis=1) if len(right) > 1 else right[0])
        for place in range(len(lefts)):
            left = [part.T for part in split(gens[place, rows, :])]
            value = dot_parts(left, right)
            if chunk == 0:
                total[place] = value
            else:
                total[place] += value
    first = core_ref[0] == 0
    start = 0
    for place in range(len(lefts)):
        for index, level in enumerate(rights):
            at = index * RANK
            if level < 3:
                low = total[place, :, at : at + HALF]
                high = total[place, :, at + HALF : at + RANK]
            else:
                value = total[place, :, at : at + RHS]
                low = jnp.concatenate([value[:HALF, :QUARTER], value[HALF:, :QUARTER]], axis=1)
                high = jnp.concatenate([value[:HALF, QUARTER:], value[HALF:, QUARTER:]], axis=1)
            rows = slice(start, start + low.shape[0])
            keep_ref[rows, :] = jnp.where(first, low, high)
            send_ref[rows, :] = jnp.where(first, high, low)
            start += low.shape[0]


def products(core, generators, solved_gens, rhs, lefts, rights, after):
    rows = rhs.shape[0]
    chunks = 2
    width = sum(RHS if level == 3 else RANK for level in rights)
    out = struct(len(lefts) * sum(HALF if level == 3 else RANK for level in rights))
    held = sum(level < 3 for level in rights)
    return pl.pallas_call(
        functools.partial(product_kernel, lefts, rights),
        in_specs=[SMEM, HBM, HBM, HBM] + [ANY] * len(after),
        out_specs=[VMEM] * 2,
        out_shape=[out, out],
        scratch_shapes=[
            pltpu.VMEM((len(lefts), rows, RANK), jnp.float32),
            pltpu.VMEM((held, rows, RANK), jnp.float32),
            pltpu.VMEM((rows, RHS), jnp.float32),
            pltpu.VMEM((len(lefts), RANK, width), jnp.float32),
            pltpu.SemaphoreType.DMA((len(lefts) + len(rights), chunks)),
        ],
        compiler_params=pltpu.CompilerParams(vmem_limit_bytes=STREAM_LIMIT),
        cost_estimate=cost(6 * rows * len(lefts) * RANK * width, rows * (len(lefts) * RANK + width)),
    )(core, generators, solved_gens, rhs, *after)


def square_norm(value):
    return jnp.sum(value * value)


def identity():
    row = lax.broadcasted_iota(jnp.int32, (RANK, RANK), 0)
    col = lax.broadcasted_iota(jnp.int32, (RANK, RANK), 1)
    return jnp.where(row == col, 1.0, 0.0)


def series(start, scale, power_ref, sum_ref):
    norm = square_norm(start)
    power_ref[...] = dot(start, start)
    sum_ref[...] = scale * (identity() + start)

    def proceed(state):
        count, bound = state
        return (count < 60) & (bound > TOLERANCE) & (bound < DIVERGED * DIVERGED)

    def body(state):
        count, _ = state
        power = power_ref[...]
        bound = square_norm(power)
        values = sum_ref[...]
        both = dot(power, jnp.concatenate([power, values], axis=1))
        power_ref[...] = both[:, :RANK]
        sum_ref[...] = values + both[:, RANK:]
        return count + 1, bound

    return lax.while_loop(proceed, body, (jnp.int32(0), norm))[1]


def invert(p_own, p_sib, power_ref, sum_ref):
    product = dot(p_sib, p_own)
    bound = series(product, 1.0, power_ref, sum_ref)

    @pl.when(jnp.logical_not(bound <= TOLERANCE))
    def _():
        scale = 1.0 / (1.0 + jnp.sqrt(square_norm(product)))
        series((1.0 - scale) * identity() + scale * product, scale, power_ref, sum_ref)


def invert_kernel(core_ref, own_ref, sib_ref, own_other_ref, sib_other_ref, inverse_ref, p_sib_ref, power):
    core = core_ref[0]
    p_own = in_order(core, own_ref[...], own_other_ref[...])
    p_sib = in_order(core, sib_ref[...], sib_other_ref[...])
    p_sib_ref[...] = p_sib
    invert(p_own, p_sib, power, inverse_ref)


def inverse(core, own, sib, own_other, sib_other):
    return pl.pallas_call(
        invert_kernel,
        in_specs=[SMEM] + [VMEM] * 4,
        out_specs=[VMEM] * 2,
        out_shape=[struct(RANK, RANK)] * 2,
        scratch_shapes=[pltpu.VMEM((RANK, RANK), jnp.float32)],
        compiler_params=pltpu.CompilerParams(vmem_limit_bytes=VMEM_LIMIT),
        cost_estimate=cost(6 * 9 * RANK**3, 4 * RANK * RANK),
    )(core, own, sib, own_other, sib_other)


def apply_kernel(core_ref, inverse_ref, p_sib_ref, own_ref, sib_ref, mixed_ref, mixed_other_ref, next_ref, *refs):
    z_ref, out_ref = refs[-2:]
    shifted = unpack(sib_ref) - dot(p_sib_ref[...], unpack(own_ref))
    z = dot(inverse_ref[...], shifted)
    store(z_ref, z)
    mixed = in_order(core_ref[0], mixed_ref[...], mixed_other_ref[...])
    store(out_ref, unpack(next_ref) - dot(mixed, z))


def apply(core, inverted, p_sib, own, sib, mixed, mixed_other, following, *after):
    return pl.pallas_call(
        apply_kernel,
        in_specs=[SMEM] + [VMEM] * 7 + [ANY] * len(after),
        out_specs=[VMEM] * 2,
        out_shape=[struct(own.shape[0])] * 2,
        compiler_params=pltpu.CompilerParams(vmem_limit_bytes=VMEM_LIMIT),
        cost_estimate=cost(6 * 3 * RANK * RANK * HALF, 12 * RANK * HALF),
    )(core, inverted, p_sib, own, sib, mixed, mixed_other, following, *after)


def mix_kernel(core_ref, mixed_ref, mixed_other_ref, next_ref, first_ref, second_ref, out_ref):
    mixed = in_order(core_ref[0], mixed_ref[...], mixed_other_ref[...])
    z = jnp.concatenate([unpack(first_ref), unpack(second_ref)], axis=1)
    store(out_ref, unpack(next_ref) - dot(mixed, z))


def mix(core, mixed, mixed_other, following, first, second):
    return pl.pallas_call(
        mix_kernel,
        in_specs=[SMEM] + [VMEM] * 5,
        out_specs=VMEM,
        out_shape=struct(following.shape[0]),
        compiler_params=pltpu.CompilerParams(vmem_limit_bytes=VMEM_LIMIT),
        cost_estimate=cost(6 * RANK * RANK * 320, 12 * RANK * HALF),
    )(core, mixed, mixed_other, following, first, second)


def rhs_in_order(core, own, other):
    first = core == 0
    low = jnp.where(first, own, other)
    high = jnp.where(first, other, own)
    top = jnp.concatenate([low[:, :QUARTER], high[:, :QUARTER]], axis=1)
    bottom = jnp.concatenate([low[:, QUARTER:], high[:, QUARTER:]], axis=1)
    return jnp.concatenate([top, bottom], axis=0)


def final_kernel(
    core_ref, own_ref, sib_ref, own_other_ref, sib_other_ref, z1_ref, z1_other_ref, z0_ref, z0_other_ref,
    z01_ref, z01_other_ref, solved_ref, rhs_ref, out_ref, power, inverted, solved, rhs, sems,
):
    core = core_ref[0]
    copies = [
        pltpu.make_async_copy(solved_ref, solved, sems.at[0]),
        pltpu.make_async_copy(rhs_ref, rhs, sems.at[1]),
    ]
    for copy in copies:
        copy.start()

    def matrix(own, other):
        return in_order(core, own[:RANK, :], other[:RANK, :])

    def columns(own, other):
        return rhs_in_order(core, own[RANK:, :], other[RANK:, :])

    p_sib = matrix(sib_ref, sib_other_ref)
    invert(matrix(own_ref, own_other_ref), p_sib, power, inverted)
    shifted = columns(sib_ref, sib_other_ref) - dot(p_sib, columns(own_ref, own_other_ref))
    last = dot(inverted[...], shifted)
    middle = columns(z1_ref, z1_other_ref) - dot(matrix(z1_ref, z1_other_ref), last)
    both = jnp.concatenate([matrix(z01_ref, z01_other_ref), matrix(z0_ref, z0_other_ref)], axis=1)
    first = columns(z0_ref, z0_other_ref) - dot(both, jnp.concatenate([middle, last], axis=0))
    for copy in copies:
        copy.wait()
    value = rhs[...]
    for level, coefs in enumerate((first, middle, last)):
        value = value - dot(solved[level], coefs)
    out_ref[...] = value


def final(core, small, solved_gens, rhs):
    rows = rhs.shape[0]
    return pl.pallas_call(
        final_kernel,
        in_specs=[SMEM] + [VMEM] * len(small) + [HBM, HBM],
        out_specs=VMEM,
        out_shape=struct(rows, RHS),
        scratch_shapes=[
            pltpu.VMEM((RANK, RANK), jnp.float32),
            pltpu.VMEM((RANK, RANK), jnp.float32),
            pltpu.VMEM((3, rows, RANK), jnp.float32),
            pltpu.VMEM((rows, RHS), jnp.float32),
            pltpu.SemaphoreType.DMA((2,)),
        ],
        compiler_params=pltpu.CompilerParams(vmem_limit_bytes=STREAM_LIMIT),
        cost_estimate=cost(6 * rows * 3 * RANK * RHS, rows * 4 * RANK),
    )(core, *small, solved_gens, rhs)


def on_device(rhs, generators, solved_gens):
    groups = lax.axis_size("rows")
    sub_bits = lax.axis_size("sub").bit_length() - 1
    span_bits = (groups // 8).bit_length() - 1
    core = (lax.axis_index("sub") % 2).astype(jnp.int32).reshape(1)

    def partial_products(lefts, rights, *after):
        keep, send = products(core, generators, solved_gens, rhs, lefts, rights, after)
        return keep + swap(send, "sub", 0), send

    def over_child(value):
        for bit in range(1, sub_bits):
            value = value + swap(value, "sub", bit)
        for bit in range(span_bits):
            value = value + swap(value, "rows", bit)
        return value

    head, _ = partial_products((0,), (0, 1))
    tail, sent = partial_products((0,), (2, 3), head)
    second, sent = partial_products((1,), (0, 1, 2, 3), sent)
    p_own = over_child(head[:RANK])
    third, _ = partial_products((2,), (0, 1, 2, 3), sent, p_own)

    p_own_other = swap(p_own, "sub", 0)
    r_own = over_child(head[RANK:])
    p_sib = swap(p_own, "rows", span_bits)
    p_sib_other = swap(p_sib, "sub", 0)
    r_sib = swap(r_own, "rows", span_bits)
    tail = over_child(tail)
    tail_sib = swap(tail, "rows", span_bits)
    near = over_child(second[: 2 * RANK])
    near_other = swap(near[:RANK], "sub", 0)
    far = over_child(second[2 * RANK :])
    third = over_child(third)
    third_other = swap(third[:RANK], "sub", 0)

    inverted, p_sib = inverse(core, p_own, p_sib, p_own_other, p_sib_other)
    z01, p_own = apply(core, inverted, p_sib, r_own, r_sib, near[:RANK], near_other, near[RANK:])
    z0, r_own = apply(core, inverted, p_sib, tail, tail_sib, near[:RANK], near_other, far, p_own)
    third = mix(core, third[:RANK], third_other, third[RANK:], z01, z0)

    p_own = p_own + swap(p_own, "rows", span_bits)
    p_own_other = swap(p_own, "sub", 0)
    p_sib = swap(p_own, "rows", span_bits + 1)
    p_sib_other = swap(p_sib, "sub", 0)
    r_own = r_own + swap(r_own, "rows", span_bits)
    r_sib = swap(r_own, "rows", span_bits + 1)
    third = third + swap(third, "rows", span_bits)
    third_other = swap(third[:RANK], "sub", 0)
    z01_other = swap(z01, "sub", 0)
    z0_other = swap(z0, "sub", 0)
    inverted, p_sib = inverse(core, p_own, p_sib, p_own_other, p_sib_other)
    z1, own = apply(core, inverted, p_sib, r_own, r_sib, third[:RANK], third_other, third[RANK:])

    own = own + swap(own, "rows", span_bits + 1)
    own_other = swap(own, "sub", 0)
    sib = swap(own, "rows", span_bits + 2)
    sib_other = swap(sib, "sub", 0)
    z1_other = swap(z1, "sub", 0)
    small = (own, sib, own_other, sib_other, z1, z1_other, z0, z0_other, z01, z01_other)
    return final(core, small, solved_gens, rhs)


def solution(mesh):
    placed = (
        P(("rows", "sub"), None),
        P(None, ("rows", "sub"), None),
        P(None, ("rows", "sub"), None),
    )
    return jax.shard_map(
        on_device, mesh=mesh, in_specs=placed, out_specs=P(("rows", "sub"), None), check_vma=False
    )
```

time: 711 us -> 99.1 us (0.14)
  other arithmetic: 351 us -> 0.39 us
  waiting for transfers between devices: 181 us -> 46.8 us
  matrix products: 59 us -> 0 us
  local copies, waits for them, and re-layouts: 57.3 us -> 1.17 us
  Pallas kernels: 0 us -> 26.3 us
  blocking collectives: 21.8 us -> 0 us
  between operations: 21.9 us -> 0.47 us
  starting transfers between devices: 11.8 us -> 23.7 us
    another operation x54 -> x0, other arithmetic: 344 us -> none  [the longest x21 112 us: pair_solve(): inner_factor = jnp.linalg.cholesky(inner_matrix)]
    psum x3 -> x0, waiting for transfers between devices: 105 us -> none  [on_device(): child_total = lax.psum(local_term, 'sub')]
    another operation x49 -> x0, local copies, waits for them, and re-layouts: 32.4 us -> none
    dot_general x21 -> x0, matrix products: 32.3 us -> none  [the longest x3 13.1 us: on_device(): lax.dot_general(gen_level, full_cols, (((0,), (0,)), ((), ())), precision...]
    ppermute x6 -> x32, waiting for transfers between devices: 76.6 us -> 46.8 us  [swap(): return lax.ppermute(value, axis, pairs)]
    another operation x39 -> x0, matrix products: 26.7 us -> none  [the longest x6 7.85 us: pair_solve(): inner_factor = jnp.linalg.cholesky(inner_matrix)]
    pallas_call x0 -> x11, Pallas kernels: none -> 26.3 us  [the longest x4 12.6 us: products(): pl.pallas_call(functools.partial(product_kernel, lefts, rights), in_specs...]
    all_gather x3 -> x0, blocking collectives: 21.8 us -> none  [on_device(): z_own = lax.all_gather(z_block, 'sub', axis=1, tiled=True)]
  transfers between devices with their start and end apart: 9 -> 32, of which waited for: 9 -> 12; matrix products, arithmetic and copies ran while one was open for 0% -> 0% of each run, Pallas kernels for 0% -> 15%
where the time goes in v2:
time: 99.1 us; the launch traced here: 98.9 us
  waiting for transfers between devices  46.8 us (47%)
  Pallas kernels  26.3 us (27%)
  starting transfers between devices  23.7 us (24%)
  local copies, waits for them, and re-layouts  1.17 us (1%)
    ppermute x32, waiting for transfers between devices, swap(): return lax.ppermute(value, axis, pairs)  46.8 us
    ppermute x32, starting transfers between devices, swap(): return lax.ppermute(value, axis, pairs)  23.7 us
    pallas_call x4, Pallas kernels, products(): pl.pallas_call(functools.partial(product_kernel, lefts, rights), in_specs...  12.6 us
    pallas_call x1, Pallas kernels, final(): pl.pallas_call(final_kernel, in_specs=[SMEM] + [VMEM] * len(small) + [HBM...  5.68 us
    pallas_call x2, Pallas kernels, inverse(): pl.pallas_call(invert_kernel, in_specs=[SMEM] + [VMEM] * 4, out_specs=[VM...  4.68 us
    pallas_call x3, Pallas kernels, apply(): pl.pallas_call(apply_kernel, in_specs=[SMEM] + [VMEM] * 7 + [ANY] * len(a...  2.89 us
  transfers between devices with their start and end apart: 32, of which 12 were waited for; matrix products, arithmetic and copies ran while one was open for 0% of the time, Pallas kernels for 15%

profile of v2, /device:TPU:0, one launch (start us, length us, event | category | flops | bytes accessed | tf_op | source)
XLA Modules:
  0.0 98.9 jit_solution(17898712570013916362)
XLA Ops:
  0.0 1.0 %copy-done = f32[1024,128]{1,0:T(8,128)S(1)} copy-done((f32[1024,128]{1,0:T(8,128)S(1)}, f32[1024,128]{1,0:T(8,128)}, u32[]{:S(2)}) %copy-start) | copy-done | bytes 524312
  1.0 2.5 %shard_map.37 = (f32[512,128]{1,0:T(8,128)S(1)}, f32[512,128]{1,0:T(8,128)S(1)}) custom-call(s32[1]{0:T(128)} %bitcast.core_ref, f32[3,1024,256]{2,1,0:T(8,128)} %gens_ref.7, f32[3,1024,256]{2,1,0:T(8,128)} %solved_ref.9, f32[1024,128]{1,0:T(8,128)S(1)} %copy-done), custom_call_target="tpu_custom_call" | custom-call | flops 805306368 | bytes 3145728 | tf_op jit(solution)/shard_map/pallas_call | solution.py:142
  3.6 0.5 collective-permute-start
  4.1 1.2 %collective-permute-done = f32[512,128]{1,0:T(8,128)S(1)} collective-permute-done((f32[512,128]{1,0:T(8,128)S(1)}, f32[512,128]{1,0:T(8,128)S(1)}, u32[]{:S(2)}, u32[]{:S(2)}) %collective-permute-start) | collective-permute-done | bytes 262176 | tf_op jit(solution)/shard_map/ppermute | solution.py:28
  5.3 2.6 %shard_map.39 = (f32[384,128]{1,0:T(8,128)S(1)}, f32[384,128]{1,0:T(8,128)S(1)}) custom-call(s32[1]{0:T(128)} %bitcast.core_ref, f32[3,1024,256]{2,1,0:T(8,128)} %gens_ref.7, f32[3,1024,256]{2,1,0:T(8,128)} %solved_ref.9, f32[1024,128]{1,0:T(8,128)S(1)} %copy-done, f32[512,128]{1,0:T(8,128)S(1)} %add.47.refs_0_), custom_call_target="tpu_custom_call" | custom-call | flops 603979776 | bytes 2621440 | tf_op jit(solution)/shard_map/pallas_call | solution.py:142
  7.9 3.0 %collective-permute-start.1 = (f32[256,128]{1,0:T(8,128)S(1)}, f32[256,128]{1,0:T(8,128)S(1)}, u32[]{:S(2)}, u32[]{:S(2)}) collective-permute-start(f32[256,128]{1,0:T(8,128)S(1)} %get-tuple-element.46), channel_id=1, source_target_pairs={{0,2},{1,3},{2,0},{3,1},{4,6},{5,7},{6,4},{7,5},{8,10},{9,11},{10,... | collective-permute-start | bytes 393224 | tf_op jit(solution)/shard_map/ppermute | solution.py:28
  10.8 0.1 collective-permute-start.5
  10.9 0.0 collective-permute-start.14
  10.9 3.7 %shard_map.40 = (f32[896,128]{1,0:T(8,128)S(1)}, f32[896,128]{1,0:T(8,128)S(1)}) custom-call(s32[1]{0:T(128)} %bitcast.core_ref, f32[3,1024,256]{2,1,0:T(8,128)} %gens_ref.7, f32[3,1024,256]{2,1,0:T(8,128)} %solved_ref.9, f32[1024,128]{1,0:T(8,128)S(1)} %copy-done, f32[384,128]{1,0:T(8,128)S(1)} %get-tuple-element.27.refs_0_), custom_call_target="tpu_custom_call" | custom-call | flops 1409286144 | bytes 4718592 | tf_op jit(solution)/shard_map/pallas_call | solution.py:142
  14.6 0.6 collective-permute-start.7
  15.2 0.0 collective-permute-done.1
  15.2 2.2 %collective-permute-done.5 = f32[256,128]{1,0:T(8,128)S(1)} collective-permute-done((f32[256,128]{1,0:T(8,128)S(1)}, f32[256,128]{1,0:T(8,128)S(1)}, u32[]{:S(2)}, u32[]{:S(2)}) %collective-permute-start.5) | collective-permute-done | bytes 131104 | tf_op jit(solution)/shard_map/ppermute | solution.py:28
  17.5 3.8 %shard_map.44 = (f32[896,128]{1,0:T(8,128)S(1)}, f32[896,128]{1,0:T(8,128)S(1)}) custom-call(s32[1]{0:T(128)} %bitcast.core_ref, f32[3,1024,256]{2,1,0:T(8,128)} %gens_ref.7, f32[3,1024,256]{2,1,0:T(8,128)} %solved_ref.9, f32[1024,128]{1,0:T(8,128)} %rhs_ref.9, f32[896,128]{1,0:T(8,128)S(1)} %get-tuple-element.29.refs_0_, ...), custom_call_target="tpu_custom_call" | custom-call | flops 1409286144 | bytes 4718592 | tf_op jit(solution)/shard_map/pallas_call | solution.py:142
  21.3 0.1 collective-permute-start.20
  21.3 1.8 %collective-permute-start.2 = (f32[256,128]{1,0:T(8,128)S(1)}, f32[256,128]{1,0:T(8,128)S(1)}, u32[]{:S(2)}, u32[]{:S(2)}) collective-permute-start(f32[256,128]{1,0:T(8,128)S(1)} %get-tuple-element.44.own_ref.refs_1_), channel_id=1, source_target_pairs={{0,4},{4,0},{8,12},{12,8},{16,20},{20,16},{24,28},{28,24},{1,5},{5... | collective-permute-start | bytes 393224 | tf_op jit(solution)/shard_map/ppermute | solution.py:28
  23.2 1.6 %collective-permute-start.15 = (f32[384,128]{1,0:T(8,128)S(1)}, f32[384,128]{1,0:T(8,128)S(1)}, u32[]{:S(2)}, u32[]{:S(2)}) collective-permute-start(f32[384,128]{1,0:T(8,128)S(1)} %add.53), channel_id=1, source_target_pairs={{0,2},{1,3},{2,0},{3,1},{4,6},{5,7},{6,4},{7,5},{8,10},{9,11},{10,... | collective-permute-start | bytes 589832 | tf_op jit(solution)/shard_map/ppermute | solution.py:28
  24.7 0.0 collective-permute-done.7
  24.8 0.6 collective-permute-start.8
  25.4 1.9 %collective-permute-done.2.sib_ref = f32[256,128]{1,0:T(8,128)S(1)} collective-permute-done((f32[256,128]{1,0:T(8,128)S(1)}, f32[256,128]{1,0:T(8,128)S(1)}, u32[]{:S(2)}, u32[]{:S(2)}) %collective-permute-start.2) | collective-permute-done | bytes 131104 | tf_op jit(solution)/shard_map/ppermute | solution.py:28
  27.3 0.0 collective-permute-start.4
  27.3 3.7 %collective-permute-done.15 = f32[384,128]{1,0:T(8,128)S(1)} collective-permute-done((f32[384,128]{1,0:T(8,128)S(1)}, f32[384,128]{1,0:T(8,128)S(1)}, u32[]{:S(2)}, u32[]{:S(2)}) %collective-permute-start.15) | collective-permute-done | bytes 196640 | tf_op jit(solution)/shard_map/ppermute | solution.py:28
  31.0 0.3 collective-permute-start.6
  31.3 0.0 collective-permute-done.3.own_other_ref
  31.3 1.8 %collective-permute-start.16 = (f32[384,128]{1,0:T(8,128)S(1)}, f32[384,128]{1,0:T(8,128)S(1)}, u32[]{:S(2)}, u32[]{:S(2)}) collective-permute-start(f32[384,128]{1,0:T(8,128)S(1)} %add.54.own_ref), channel_id=1, source_target_pairs={{0,4},{4,0},{8,12},{12,8},{16,20},{20,16},{24,28},{28,24},{1,5},{5... | collective-permute-start | bytes 589832 | tf_op jit(solution)/shard_map/ppermute | solution.py:28
  33.1 0.0 collective-permute-done.4.sib_other_ref
  33.1 2.2 %shard_map.38 = (f32[256,256]{1,0:T(8,128)S(1)}, f32[256,256]{1,0:T(8,128)S(1)}) custom-call(s32[1]{0:T(128)} %bitcast.core_ref, f32[256,128]{1,0:T(8,128)S(1)} %get-tuple-element.44.own_ref.refs_1_, f32[256,128]{1,0:T(8,128)S(1)} %collective-permute-done.2.sib_ref, f32[256,128]{1,0:T(8,128)S(1)} %collective-permute-done.3.own_other_ref, ...), custom_call_target="tpu_custom_call" | custom-call | flops 905969664 | bytes 1048576 | tf_op jit(solution)/shard_map/pallas_call | solution.py:210
  35.4 1.6 %collective-permute-start.17 = (f32[384,128]{1,0:T(8,128)S(1)}, f32[384,128]{1,0:T(8,128)S(1)}, u32[]{:S(2)}, u32[]{:S(2)}) collective-permute-start(f32[384,128]{1,0:T(8,128)S(1)} %slice.49), channel_id=1, source_target_pairs={{0,2},{1,3},{2,0},{3,1},{4,6},{5,7},{6,4},{7,5},{8,10},{9,11},{10,... | collective-permute-start | bytes 589832 | tf_op jit(solution)/shard_map/ppermute | solution.py:28
  37.0 0.0 collective-permute-done.20
  37.0 0.6 collective-permute-start.21
  37.6 0.0 collective-permute-done.8
  37.7 0.1 collective-permute-start.9
  37.7 12.3 %collective-permute-done.21 = f32[896,128]{1,0:T(8,128)S(1)} collective-permute-done((f32[896,128]{1,0:T(8,128)S(1)}, f32[896,128]{1,0:T(8,128)S(1)}, u32[]{:S(2)}, u32[]{:S(2)}) %collective-permute-start.21) | collective-permute-done | bytes 458784 | tf_op jit(solution)/shard_map/ppermute | solution.py:28
  50.2 0.1 collective-permute-start.22
  50.2 0.0 collective-permute-done.17
  50.3 0.0 collective-permute-done.6.sib_ref
  50.3 0.8 shard_map.41
  51.1 0.4 collective-permute-start.10
  51.5 0.0 collective-permute-done.16.sib_ref
  51.5 1.0 %shard_map.43 = (f32[384,128]{1,0:T(8,128)S(1)}, f32[384,128]{1,0:T(8,128)S(1)}) custom-call(s32[1]{0:T(128)} %bitcast.core_ref, f32[256,256]{1,0:T(8,128)S(1)} %get-tuple-element.25.inverse_ref, f32[256,256]{1,0:T(8,128)S(1)} %get-tuple-element.26.p_sib_ref, f32[384,128]{1,0:T(8,128)S(1)} %add.54.own_ref, f32[384,128]{1,0:T(8,128)S(1)} %collective-permute-done.16.sib_ref, ...), custom_call_target="tpu_custom_call" | custom-call | flops 150994944 | bytes 1572864 | tf_op jit(solution)/shard_map/pallas_call | solution.py:231
  52.6 0.0 collective-permute-done.22.mixed_other_ref
  52.6 0.5 shard_map.45
  53.1 1.8 %collective-permute-start.23 = (f32[640,128]{1,0:T(8,128)S(1)}, f32[640,128]{1,0:T(8,128)S(1)}, u32[]{:S(2)}, u32[]{:S(2)}) collective-permute-start(f32[640,128]{1,0:T(8,128)S(1)} %shard_map.45), channel_id=1, source_target_pairs={{0,4},{4,0},{8,12},{12,8},{16,20},{20,16},{24,28},{28,24},{1,5},{5... | collective-permute-start | bytes 983048 | tf_op jit(solution)/shard_map/ppermute | solution.py:28
  54.8 0.3 collective-permute-start.18
  55.2 2.3 %collective-permute-done.10 = f32[256,128]{1,0:T(8,128)S(1)} collective-permute-done((f32[256,128]{1,0:T(8,128)S(1)}, f32[256,128]{1,0:T(8,128)S(1)}, u32[]{:S(2)}, u32[]{:S(2)}) %collective-permute-start.10) | collective-permute-done | bytes 131104 | tf_op jit(solution)/shard_map/ppermute | solution.py:28
  57.5 1.7 %collective-permute-start.11 = (f32[256,128]{1,0:T(8,128)S(1)}, f32[256,128]{1,0:T(8,128)S(1)}, u32[]{:S(2)}, u32[]{:S(2)}) collective-permute-start(f32[256,128]{1,0:T(8,128)S(1)} %add.52.own_ref), channel_id=1, source_target_pairs={{0,8},{4,12},{8,0},{12,4},{16,24},{20,28},{24,16},{28,20},{1,9},{5... | collective-permute-start | bytes 393224 | tf_op jit(solution)/shard_map/ppermute | solution.py:28
  59.1 3.4 %collective-permute-done.11.sib_ref = f32[256,128]{1,0:T(8,128)S(1)} collective-permute-done((f32[256,128]{1,0:T(8,128)S(1)}, f32[256,128]{1,0:T(8,128)S(1)}, u32[]{:S(2)}, u32[]{:S(2)}) %collective-permute-start.11) | collective-permute-done | bytes 131104 | tf_op jit(solution)/shard_map/ppermute | solution.py:28
  62.5 0.0 collective-permute-start.13
  62.5 5.8 %collective-permute-done.18 = f32[384,128]{1,0:T(8,128)S(1)} collective-permute-done((f32[384,128]{1,0:T(8,128)S(1)}, f32[384,128]{1,0:T(8,128)S(1)}, u32[]{:S(2)}, u32[]{:S(2)}) %collective-permute-start.18) | collective-permute-done | bytes 196640 | tf_op jit(solution)/shard_map/ppermute | solution.py:28
  68.3 1.7 %collective-permute-start.19 = (f32[384,128]{1,0:T(8,128)S(1)}, f32[384,128]{1,0:T(8,128)S(1)}, u32[]{:S(2)}, u32[]{:S(2)}) collective-permute-start(f32[384,128]{1,0:T(8,128)S(1)} %add.56.own_ref), channel_id=1, source_target_pairs={{0,8},{4,12},{8,0},{12,4},{16,24},{20,28},{24,16},{28,20},{1,9},{5... | collective-permute-start | bytes 589832 | tf_op jit(solution)/shard_map/ppermute | solution.py:28
  70.0 0.1 collective-permute-start.24
  70.1 0.0 collective-permute-done.12.own_other_ref
  70.1 2.4 %shard_map.42 = (f32[256,256]{1,0:T(8,128)S(1)}, f32[256,256]{1,0:T(8,128)S(1)}) custom-call(s32[1]{0:T(128)} %bitcast.core_ref, f32[256,128]{1,0:T(8,128)S(1)} %add.52.own_ref, f32[256,128]{1,0:T(8,128)S(1)} %collective-permute-done.11.sib_ref, f32[256,128]{1,0:T(8,128)S(1)} %collective-permute-done.12.own_other_ref, ...), custom_call_target="tpu_custom_call" | custom-call | flops 905969664 | bytes 1048576 | tf_op jit(solution)/shard_map/pallas_call | solution.py:210
  72.6 2.3 %collective-permute-done.19.sib_ref = f32[384,128]{1,0:T(8,128)S(1)} collective-permute-done((f32[384,128]{1,0:T(8,128)S(1)}, f32[384,128]{1,0:T(8,128)S(1)}, u32[]{:S(2)}, u32[]{:S(2)}) %collective-permute-start.19) | collective-permute-done | bytes 196640 | tf_op jit(solution)/shard_map/ppermute | solution.py:28
  74.9 0.0 collective-permute-done.24.mixed_other_ref
  74.9 1.0 %shard_map.46 = (f32[384,128]{1,0:T(8,128)S(1)}, f32[384,128]{1,0:T(8,128)S(1)}) custom-call(s32[1]{0:T(128)} %bitcast.core_ref, f32[256,256]{1,0:T(8,128)S(1)} %get-tuple-element.31.inverse_ref, f32[256,256]{1,0:T(8,128)S(1)} %get-tuple-element.32.p_sib_ref, f32[384,128]{1,0:T(8,128)S(1)} %add.56.own_ref, f32[384,128]{1,0:T(8,128)S(1)} %collective-permute-done.19.sib_ref, ...), custom_call_target="tpu_custom_call" | custom-call | flops 150994944 | bytes 1572864 | tf_op jit(solution)/shard_map/pallas_call | solution.py:231
  75.9 1.7 %collective-permute-start.25 = (f32[384,128]{1,0:T(8,128)S(1)}, f32[384,128]{1,0:T(8,128)S(1)}, u32[]{:S(2)}, u32[]{:S(2)}) collective-permute-start(f32[384,128]{1,0:T(8,128)S(1)} %get-tuple-element.39), channel_id=1, source_target_pairs={{0,8},{4,12},{8,0},{12,4},{16,24},{20,28},{24,16},{28,20},{1,9},{5... | collective-permute-start | bytes 589832 | tf_op jit(solution)/shard_map/ppermute | solution.py:28
  77.6 4.1 %collective-permute-done.25 = f32[384,128]{1,0:T(8,128)S(1)} collective-permute-done((f32[384,128]{1,0:T(8,128)S(1)}, f32[384,128]{1,0:T(8,128)S(1)}, u32[]{:S(2)}, u32[]{:S(2)}) %collective-permute-start.25) | collective-permute-done | bytes 196640 | tf_op jit(solution)/shard_map/ppermute | solution.py:28
  81.7 2.7 %collective-permute-start.26 = (f32[384,128]{1,0:T(8,128)S(1)}, f32[384,128]{1,0:T(8,128)S(1)}, u32[]{:S(2)}, u32[]{:S(2)}) collective-permute-start(f32[384,128]{1,0:T(8,128)S(1)} %add.60.own_ref), channel_id=1, source_target_pairs={{0,16},{4,20},{8,24},{12,28},{16,0},{20,4},{24,8},{28,12},{1,17},{... | collective-permute-start | bytes 589832 | tf_op jit(solution)/shard_map/ppermute | solution.py:28
  84.4 0.0 collective-permute-start.30
  84.4 0.5 collective-permute-start.29
  84.9 6.5 %collective-permute-done.26.sib_ref = f32[384,128]{1,0:T(8,128)S(1)} collective-permute-done((f32[384,128]{1,0:T(8,128)S(1)}, f32[384,128]{1,0:T(8,128)S(1)}, u32[]{:S(2)}, u32[]{:S(2)}) %collective-permute-start.26) | collective-permute-done | bytes 196640 | tf_op jit(solution)/shard_map/ppermute | solution.py:28
  91.4 0.5 collective-permute-start.31
  91.9 1.1 %collective-permute-done.31.z01_other_ref = f32[256,128]{1,0:T(8,128)S(1)} collective-permute-done((f32[256,128]{1,0:T(8,128)S(1)}, f32[256,128]{1,0:T(8,128)S(1)}, u32[]{:S(2)}, u32[]{:S(2)}) %collective-permute-start.31) | collective-permute-done | bytes 131104 | tf_op jit(solution)/shard_map/ppermute | solution.py:28
  93.0 5.7 %shard_map.47 = f32[1024,128]{1,0:T(8,128)} custom-call(s32[1]{0:T(128)} %bitcast.core_ref, f32[384,128]{1,0:T(8,128)S(1)} %add.60.own_ref, f32[384,128]{1,0:T(8,128)S(1)} %collective-permute-done.26.sib_ref, f32[384,128]{1,0:T(8,128)S(1)} %collective-permute-done.27.own_other_ref, f32[384,128]{1,0:T(8,128)S(1)} %collective-permute-done.28.sib_other_ref, ...), custom_call_target="tpu_custom_call" | custom-call | flops 603979776 | bytes 4194304 | tf_op jit(solution)/shard_map/pallas_call | solution.py:302
  (34 shorter events, 0.6 us)
Async XLA Ops:
  0.0 1.0 %copy-start = (f32[1024,128]{1,0:T(8,128)S(1)}, f32[1024,128]{1,0:T(8,128)}, u32[]{:S(2)}) copy-start(f32[1024,128]{1,0:T(8,128)} %rhs_ref.9) | copy-start | bytes 1572868
  3.6 1.7 %collective-permute-start = (f32[512,128]{1,0:T(8,128)S(1)}, f32[512,128]{1,0:T(8,128)S(1)}, u32[]{:S(2)}, u32[]{:S(2)}) collective-permute-start(f32[512,128]{1,0:T(8,128)S(1)} %get-tuple-element.24), channel_id=1, source_target_pairs={{0,1},{1,0},{2,3},{3,2},{4,5},{5,4},{6,7},{7,6},{8,9},{9,8},{10,11... | collective-permute-start | bytes 786440 | tf_op jit(solution)/shard_map/ppermute | solution.py:28
  7.9 7.3 %collective-permute-start.1 = (f32[256,128]{1,0:T(8,128)S(1)}, f32[256,128]{1,0:T(8,128)S(1)}, u32[]{:S(2)}, u32[]{:S(2)}) collective-permute-start(f32[256,128]{1,0:T(8,128)S(1)} %get-tuple-element.46), channel_id=1, source_target_pairs={{0,2},{1,3},{2,0},{3,1},{4,6},{5,7},{6,4},{7,5},{8,10},{9,11},{10,... | collective-permute-start | bytes 393224 | tf_op jit(solution)/shard_map/ppermute | solution.py:28
  10.8 6.6 %collective-permute-start.5 = (f32[256,128]{1,0:T(8,128)S(1)}, f32[256,128]{1,0:T(8,128)S(1)}, u32[]{:S(2)}, u32[]{:S(2)}) collective-permute-start(f32[256,128]{1,0:T(8,128)S(1)} %get-tuple-element.45), channel_id=1, source_target_pairs={{0,2},{1,3},{2,0},{3,1},{4,6},{5,7},{6,4},{7,5},{8,10},{9,11},{10,... | collective-permute-start | bytes 393224 | tf_op jit(solution)/shard_map/ppermute | solution.py:28
  10.9 12.2 %collective-permute-start.14 = (f32[384,128]{1,0:T(8,128)S(1)}, f32[384,128]{1,0:T(8,128)S(1)}, u32[]{:S(2)}, u32[]{:S(2)}) collective-permute-start(f32[384,128]{1,0:T(8,128)S(1)} %get-tuple-element.27.refs_0_), channel_id=1, source_target_pairs={{0,1},{1,0},{2,3},{3,2},{4,5},{5,4},{6,7},{7,6},{8,9},{9,8},{10,11... | collective-permute-start | bytes 589832 | tf_op jit(solution)/shard_map/ppermute | solution.py:28
  14.6 10.1 %collective-permute-start.7 = (f32[896,128]{1,0:T(8,128)S(1)}, f32[896,128]{1,0:T(8,128)S(1)}, u32[]{:S(2)}, u32[]{:S(2)}) collective-permute-start(f32[896,128]{1,0:T(8,128)S(1)} %get-tuple-element.29.refs_0_), channel_id=1, source_target_pairs={{0,1},{1,0},{2,3},{3,2},{4,5},{5,4},{6,7},{7,6},{8,9},{9,8},{10,11... | collective-permute-start | bytes 1376264 | tf_op jit(solution)/shard_map/ppermute | solution.py:28
  21.3 15.7 %collective-permute-start.20 = (f32[896,128]{1,0:T(8,128)S(1)}, f32[896,128]{1,0:T(8,128)S(1)}, u32[]{:S(2)}, u32[]{:S(2)}) collective-permute-start(f32[896,128]{1,0:T(8,128)S(1)} %get-tuple-element.36), channel_id=1, source_target_pairs={{0,1},{1,0},{2,3},{3,2},{4,5},{5,4},{6,7},{7,6},{8,9},{9,8},{10,11... | collective-permute-start | bytes 1376264 | tf_op jit(solution)/shard_map/ppermute | solution.py:28
  21.3 5.9 %collective-permute-start.2 = (f32[256,128]{1,0:T(8,128)S(1)}, f32[256,128]{1,0:T(8,128)S(1)}, u32[]{:S(2)}, u32[]{:S(2)}) collective-permute-start(f32[256,128]{1,0:T(8,128)S(1)} %get-tuple-element.44.own_ref.refs_1_), channel_id=1, source_target_pairs={{0,4},{4,0},{8,12},{12,8},{16,20},{20,16},{24,28},{28,24},{1,5},{5... | collective-permute-start | bytes 393224 | tf_op jit(solution)/shard_map/ppermute | solution.py:28
  23.2 7.8 %collective-permute-start.15 = (f32[384,128]{1,0:T(8,128)S(1)}, f32[384,128]{1,0:T(8,128)S(1)}, u32[]{:S(2)}, u32[]{:S(2)}) collective-permute-start(f32[384,128]{1,0:T(8,128)S(1)} %add.53), channel_id=1, source_target_pairs={{0,2},{1,3},{2,0},{3,1},{4,6},{5,7},{6,4},{7,5},{8,10},{9,11},{10,... | collective-permute-start | bytes 589832 | tf_op jit(solution)/shard_map/ppermute | solution.py:28
  24.8 12.8 %collective-permute-start.8 = (f32[512,128]{1,0:T(8,128)S(1)}, f32[512,128]{1,0:T(8,128)S(1)}, u32[]{:S(2)}, u32[]{:S(2)}) collective-permute-start(f32[512,128]{1,0:T(8,128)S(1)} %slice.46), channel_id=1, source_target_pairs={{0,2},{1,3},{2,0},{3,1},{4,6},{5,7},{6,4},{7,5},{8,10},{9,11},{10,... | collective-permute-start | bytes 786440 | tf_op jit(solution)/shard_map/ppermute | solution.py:28
  25.4 5.9 %collective-permute-start.3 = (f32[256,128]{1,0:T(8,128)S(1)}, f32[256,128]{1,0:T(8,128)S(1)}, u32[]{:S(2)}, u32[]{:S(2)}) collective-permute-start(f32[256,128]{1,0:T(8,128)S(1)} %get-tuple-element.44.own_ref.refs_1_), channel_id=1, source_target_pairs={{0,1},{1,0},{2,3},{3,2},{4,5},{5,4},{6,7},{7,6},{8,9},{9,8},{10,11... | collective-permute-start | bytes 393224 | tf_op jit(solution)/shard_map/ppermute | solution.py:28
  27.3 5.8 %collective-permute-start.4 = (f32[256,128]{1,0:T(8,128)S(1)}, f32[256,128]{1,0:T(8,128)S(1)}, u32[]{:S(2)}, u32[]{:S(2)}) collective-permute-start(f32[256,128]{1,0:T(8,128)S(1)} %collective-permute-done.2.sib_ref), channel_id=1, source_target_pairs={{0,1},{1,0},{2,3},{3,2},{4,5},{5,4},{6,7},{7,6},{8,9},{9,8},{10,11... | collective-permute-start | bytes 393224 | tf_op jit(solution)/shard_map/ppermute | solution.py:28
  31.0 19.3 %collective-permute-start.6 = (f32[256,128]{1,0:T(8,128)S(1)}, f32[256,128]{1,0:T(8,128)S(1)}, u32[]{:S(2)}, u32[]{:S(2)}) collective-permute-start(f32[256,128]{1,0:T(8,128)S(1)} %get-tuple-element.43.own_ref), channel_id=1, source_target_pairs={{0,4},{4,0},{8,12},{12,8},{16,20},{20,16},{24,28},{28,24},{1,5},{5... | collective-permute-start | bytes 393224 | tf_op jit(solution)/shard_map/ppermute | solution.py:28
  31.3 20.2 %collective-permute-start.16 = (f32[384,128]{1,0:T(8,128)S(1)}, f32[384,128]{1,0:T(8,128)S(1)}, u32[]{:S(2)}, u32[]{:S(2)}) collective-permute-start(f32[384,128]{1,0:T(8,128)S(1)} %add.54.own_ref), channel_id=1, source_target_pairs={{0,4},{4,0},{8,12},{12,8},{16,20},{20,16},{24,28},{28,24},{1,5},{5... | collective-permute-start | bytes 589832 | tf_op jit(solution)/shard_map/ppermute | solution.py:28
  35.4 14.9 %collective-permute-start.17 = (f32[384,128]{1,0:T(8,128)S(1)}, f32[384,128]{1,0:T(8,128)S(1)}, u32[]{:S(2)}, u32[]{:S(2)}) collective-permute-start(f32[384,128]{1,0:T(8,128)S(1)} %slice.49), channel_id=1, source_target_pairs={{0,2},{1,3},{2,0},{3,1},{4,6},{5,7},{6,4},{7,5},{8,10},{9,11},{10,... | collective-permute-start | bytes 589832 | tf_op jit(solution)/shard_map/ppermute | solution.py:28
  37.0 13.1 %collective-permute-start.21 = (f32[896,128]{1,0:T(8,128)S(1)}, f32[896,128]{1,0:T(8,128)S(1)}, u32[]{:S(2)}, u32[]{:S(2)}) collective-permute-start(f32[896,128]{1,0:T(8,128)S(1)} %add.57), channel_id=1, source_target_pairs={{0,2},{1,3},{2,0},{3,1},{4,6},{5,7},{6,4},{7,5},{8,10},{9,11},{10,... | collective-permute-start | bytes 1376264 | tf_op jit(solution)/shard_map/ppermute | solution.py:28
  37.7 12.6 %collective-permute-start.9 = (f32[256,128]{1,0:T(8,128)S(1)}, f32[256,128]{1,0:T(8,128)S(1)}, u32[]{:S(2)}, u32[]{:S(2)}) collective-permute-start(f32[256,128]{1,0:T(8,128)S(1)} %get-tuple-element.42.mixed_ref), channel_id=1, source_target_pairs={{0,1},{1,0},{2,3},{3,2},{4,5},{5,4},{6,7},{7,6},{8,9},{9,8},{10,11... | collective-permute-start | bytes 393224 | tf_op jit(solution)/shard_map/ppermute | solution.py:28
  50.2 2.4 %collective-permute-start.22 = (f32[256,128]{1,0:T(8,128)S(1)}, f32[256,128]{1,0:T(8,128)S(1)}, u32[]{:S(2)}, u32[]{:S(2)}) collective-permute-start(f32[256,128]{1,0:T(8,128)S(1)} %slice.50.mixed_ref), channel_id=1, source_target_pairs={{0,1},{1,0},{2,3},{3,2},{4,5},{5,4},{6,7},{7,6},{8,9},{9,8},{10,11... | collective-permute-start | bytes 393224 | tf_op jit(solution)/shard_map/ppermute | solution.py:28
  51.1 6.4 %collective-permute-start.10 = (f32[256,128]{1,0:T(8,128)S(1)}, f32[256,128]{1,0:T(8,128)S(1)}, u32[]{:S(2)}, u32[]{:S(2)}) collective-permute-start(f32[256,128]{1,0:T(8,128)S(1)} %get-tuple-element.30.refs_0_), channel_id=1, source_target_pairs={{0,4},{4,0},{8,12},{12,8},{16,20},{20,16},{24,28},{28,24},{1,5},{5... | collective-permute-start | bytes 393224 | tf_op jit(solution)/shard_map/ppermute | solution.py:28
  53.1 16.9 %collective-permute-start.23 = (f32[640,128]{1,0:T(8,128)S(1)}, f32[640,128]{1,0:T(8,128)S(1)}, u32[]{:S(2)}, u32[]{:S(2)}) collective-permute-start(f32[640,128]{1,0:T(8,128)S(1)} %shard_map.45), channel_id=1, source_target_pairs={{0,4},{4,0},{8,12},{12,8},{16,20},{20,16},{24,28},{28,24},{1,5},{5... | collective-permute-start | bytes 983048 | tf_op jit(solution)/shard_map/ppermute | solution.py:28
  54.8 13.4 %collective-permute-start.18 = (f32[384,128]{1,0:T(8,128)S(1)}, f32[384,128]{1,0:T(8,128)S(1)}, u32[]{:S(2)}, u32[]{:S(2)}) collective-permute-start(f32[384,128]{1,0:T(8,128)S(1)} %get-tuple-element.34), channel_id=1, source_target_pairs={{0,4},{4,0},{8,12},{12,8},{16,20},{20,16},{24,28},{28,24},{1,5},{5... | collective-permute-start | bytes 589832 | tf_op jit(solution)/shard_map/ppermute | solution.py:28
  57.5 5.0 %collective-permute-start.11 = (f32[256,128]{1,0:T(8,128)S(1)}, f32[256,128]{1,0:T(8,128)S(1)}, u32[]{:S(2)}, u32[]{:S(2)}) collective-permute-start(f32[256,128]{1,0:T(8,128)S(1)} %add.52.own_ref), channel_id=1, source_target_pairs={{0,8},{4,12},{8,0},{12,4},{16,24},{20,28},{24,16},{28,20},{1,9},{5... | collective-permute-start | bytes 393224 | tf_op jit(solution)/shard_map/ppermute | solution.py:28
  59.1 11.0 %collective-permute-start.12 = (f32[256,128]{1,0:T(8,128)S(1)}, f32[256,128]{1,0:T(8,128)S(1)}, u32[]{:S(2)}, u32[]{:S(2)}) collective-permute-start(f32[256,128]{1,0:T(8,128)S(1)} %add.52.own_ref), channel_id=1, source_target_pairs={{0,1},{1,0},{2,3},{3,2},{4,5},{5,4},{6,7},{7,6},{8,9},{9,8},{10,11... | collective-permute-start | bytes 393224 | tf_op jit(solution)/shard_map/ppermute | solution.py:28
  62.5 7.6 %collective-permute-start.13 = (f32[256,128]{1,0:T(8,128)S(1)}, f32[256,128]{1,0:T(8,128)S(1)}, u32[]{:S(2)}, u32[]{:S(2)}) collective-permute-start(f32[256,128]{1,0:T(8,128)S(1)} %collective-permute-done.11.sib_ref), channel_id=1, source_target_pairs={{0,1},{1,0},{2,3},{3,2},{4,5},{5,4},{6,7},{7,6},{8,9},{9,8},{10,11... | collective-permute-start | bytes 393224 | tf_op jit(solution)/shard_map/ppermute | solution.py:28
  68.3 6.6 %collective-permute-start.19 = (f32[384,128]{1,0:T(8,128)S(1)}, f32[384,128]{1,0:T(8,128)S(1)}, u32[]{:S(2)}, u32[]{:S(2)}) collective-permute-start(f32[384,128]{1,0:T(8,128)S(1)} %add.56.own_ref), channel_id=1, source_target_pairs={{0,8},{4,12},{8,0},{12,4},{16,24},{20,28},{24,16},{28,20},{1,9},{5... | collective-permute-start | bytes 589832 | tf_op jit(solution)/shard_map/ppermute | solution.py:28
  70.0 4.9 %collective-permute-start.24 = (f32[256,128]{1,0:T(8,128)S(1)}, f32[256,128]{1,0:T(8,128)S(1)}, u32[]{:S(2)}, u32[]{:S(2)}) collective-permute-start(f32[256,128]{1,0:T(8,128)S(1)} %slice.52.mixed_ref), channel_id=1, source_target_pairs={{0,1},{1,0},{2,3},{3,2},{4,5},{5,4},{6,7},{7,6},{8,9},{9,8},{10,11... | collective-permute-start | bytes 393224 | tf_op jit(solution)/shard_map/ppermute | solution.py:28
  75.9 5.7 %collective-permute-start.25 = (f32[384,128]{1,0:T(8,128)S(1)}, f32[384,128]{1,0:T(8,128)S(1)}, u32[]{:S(2)}, u32[]{:S(2)}) collective-permute-start(f32[384,128]{1,0:T(8,128)S(1)} %get-tuple-element.39), channel_id=1, source_target_pairs={{0,8},{4,12},{8,0},{12,4},{16,24},{20,28},{24,16},{28,20},{1,9},{5... | collective-permute-start | bytes 589832 | tf_op jit(solution)/shard_map/ppermute | solution.py:28
  81.7 9.7 %collective-permute-start.26 = (f32[384,128]{1,0:T(8,128)S(1)}, f32[384,128]{1,0:T(8,128)S(1)}, u32[]{:S(2)}, u32[]{:S(2)}) collective-permute-start(f32[384,128]{1,0:T(8,128)S(1)} %add.60.own_ref), channel_id=1, source_target_pairs={{0,16},{4,20},{8,24},{12,28},{16,0},{20,4},{24,8},{28,12},{1,17},{... | collective-permute-start | bytes 589832 | tf_op jit(solution)/shard_map/ppermute | solution.py:28
  84.4 8.6 %collective-permute-start.30 = (f32[384,128]{1,0:T(8,128)S(1)}, f32[384,128]{1,0:T(8,128)S(1)}, u32[]{:S(2)}, u32[]{:S(2)}) collective-permute-start(f32[384,128]{1,0:T(8,128)S(1)} %get-tuple-element.38.second_ref.z0_ref), channel_id=1, source_target_pairs={{0,1},{1,0},{2,3},{3,2},{4,5},{5,4},{6,7},{7,6},{8,9},{9,8},{10,11... | collective-permute-start | bytes 589832 | tf_op jit(solution)/shard_map/ppermute | solution.py:28
  84.4 8.6 %collective-permute-start.29 = (f32[384,128]{1,0:T(8,128)S(1)}, f32[384,128]{1,0:T(8,128)S(1)}, u32[]{:S(2)}, u32[]{:S(2)}) collective-permute-start(f32[384,128]{1,0:T(8,128)S(1)} %get-tuple-element.40.z1_ref), channel_id=1, source_target_pairs={{0,1},{1,0},{2,3},{3,2},{4,5},{5,4},{6,7},{7,6},{8,9},{9,8},{10,11... | collective-permute-start | bytes 589832 | tf_op jit(solution)/shard_map/ppermute | solution.py:28
  84.9 8.1 %collective-permute-start.27 = (f32[384,128]{1,0:T(8,128)S(1)}, f32[384,128]{1,0:T(8,128)S(1)}, u32[]{:S(2)}, u32[]{:S(2)}) collective-permute-start(f32[384,128]{1,0:T(8,128)S(1)} %add.60.own_ref), channel_id=1, source_target_pairs={{0,1},{1,0},{2,3},{3,2},{4,5},{5,4},{6,7},{7,6},{8,9},{9,8},{10,11... | collective-permute-start | bytes 589832 | tf_op jit(solution)/shard_map/ppermute | solution.py:28
  91.4 1.6 %collective-permute-start.28 = (f32[384,128]{1,0:T(8,128)S(1)}, f32[384,128]{1,0:T(8,128)S(1)}, u32[]{:S(2)}, u32[]{:S(2)}) collective-permute-start(f32[384,128]{1,0:T(8,128)S(1)} %collective-permute-done.26.sib_ref), channel_id=1, source_target_pairs={{0,1},{1,0},{2,3},{3,2},{4,5},{5,4},{6,7},{7,6},{8,9},{9,8},{10,11... | collective-permute-start | bytes 589832 | tf_op jit(solution)/shard_map/ppermute | solution.py:28
  91.4 1.6 %collective-permute-start.31 = (f32[256,128]{1,0:T(8,128)S(1)}, f32[256,128]{1,0:T(8,128)S(1)}, u32[]{:S(2)}, u32[]{:S(2)}) collective-permute-start(f32[256,128]{1,0:T(8,128)S(1)} %get-tuple-element.37.first_ref.z01_ref), channel_id=1, source_target_pairs={{0,1},{1,0},{2,3},{3,2},{4,5},{5,4},{6,7},{7,6},{8,9},{9,8},{10,11... | collective-permute-start | bytes 393224 | tf_op jit(solution)/shard_map/ppermute | solution.py:28

commit v3 on v2

v3 whole, which is shorter than its diff:
```python
import functools

import jax
import jax.numpy as jnp
from jax import lax
from jax.experimental import pallas as pl
from jax.experimental.pallas import tpu as pltpu
from jax.sharding import PartitionSpec as P

RANK = 256
RHS = 128
HALF = RANK // 2
QUARTER = HALF // 2
TOLERANCE = 1e-7
DIVERGED = 1e4
VMEM_LIMIT = 40 * 2**20
STREAM_LIMIT = 52 * 2**20

SMEM = pl.BlockSpec(memory_space=pltpu.SMEM)
VMEM = pl.BlockSpec(memory_space=pltpu.VMEM)
HBM = pl.BlockSpec(memory_space=pltpu.HBM)
ANY = pl.BlockSpec(memory_space=pl.ANY)


def swap(value, axis, bit):
    mask = 2**bit
    pairs = [(source, source ^ mask) for source in range(lax.axis_size(axis))]
    return lax.ppermute(value, axis, pairs)


def struct(rows, cols=HALF):
    return jax.ShapeDtypeStruct((rows, cols), jnp.float32)


def cost(flops, floats):
    return pl.CostEstimate(flops=int(flops), bytes_accessed=int(4 * floats), transcendentals=0)


def split(value):
    high = value.astype(jnp.bfloat16)
    low = (value - high.astype(jnp.float32)).astype(jnp.bfloat16)
    return high, low


def dot_parts(left, right):
    def part(first, second):
        return lax.dot_general(first, second, (((1,), (0,)), ((), ())), preferred_element_type=jnp.float32)

    return part(left[0], right[0]) + (part(left[0], right[1]) + part(left[1], right[0]))


def dot(left, right):
    return dot_parts(split(left), split(right))


def dot_turned(left, right):
    return dot_parts([part.T for part in split(left)], split(right))


def in_order(core, own, other):
    first = core == 0
    return jnp.concatenate([jnp.where(first, own, other), jnp.where(first, other, own)], axis=1)


def pack(value):
    whole = value.shape[1] // HALF
    units = [value[:, index * HALF : (index + 1) * HALF] for index in range(whole)]
    if value.shape[1] % HALF:
        tail = value[:, whole * HALF :]
        units.append(jnp.concatenate([tail[:HALF], tail[HALF:]], axis=1))
    return units


def unpack(ref):
    whole = ref.shape[0] // RANK
    parts = [ref[index * RANK : (index + 1) * RANK, :] for index in range(whole)]
    if ref.shape[0] % RANK:
        tail = ref[whole * RANK :, :]
        parts.append(jnp.concatenate([tail[:, :QUARTER], tail[:, QUARTER:]], axis=0))
    return jnp.concatenate(parts, axis=1) if len(parts) > 1 else parts[0]


def store(ref, value):
    start = 0
    for unit in pack(value):
        ref[start : start + unit.shape[0], :] = unit
        start += unit.shape[0]


def product_kernel(groups, core_ref, gens_ref, solved_ref, rhs_ref, *refs):
    gens, solved, rhs, total, sems = refs[-5:]
    outs = refs[-5 - 2 * len(groups) : -5]
    pairs, lefts, rights = needed(groups)
    chunks = sems.shape[1]
    block = gens.shape[1] // chunks
    copies = []
    for chunk in range(chunks):
        rows = pl.ds(chunk * block, block)
        row = []
        for place, level in enumerate(lefts):
            row.append((gens_ref.at[level, rows], gens.at[place, rows]))
        for place, level in enumerate(rights):
            if level < 3:
                row.append((solved_ref.at[level, rows], solved.at[place, rows]))
            else:
                row.append((rhs_ref.at[rows], rhs.at[rows]))
        row = [pltpu.make_async_copy(*ends, sems.at[index, chunk]) for index, ends in enumerate(row)]
        for copy in row:
            copy.start()
        copies.append(row)
    places = {}
    for chunk in range(chunks):
        rows = pl.ds(chunk * block, block)
        for copy in copies[chunk]:
            copy.wait()
        right = {}
        for place, level in enumerate(rights):
            right[level] = split(rhs[rows, :] if level == 3 else solved[place, rows, :])
        start = 0
        for place, level in enumerate(lefts):
            left = [part.T for part in split(gens[place, rows, :])]
            wanted = [second for first, second in pairs if first == level]
            value = dot_parts(left, [jnp.concatenate([right[second][half] for second in wanted], axis=1) for half in (0, 1)])
            for second in wanted:
                places[level, second] = start
                start += width_of(second)
            cols = slice(start - value.shape[1], start)
            if chunk == 0:
                total[:, cols] = value
            else:
                total[:, cols] += value
    first = core_ref[0] == 0
    for index, group in enumerate(groups):
        keep_ref, send_ref = outs[2 * index : 2 * index + 2]
        start = 0
        for pair in group:
            at = places[pair]
            if pair[1] < 3:
                low = total[:, at : at + HALF]
                high = total[:, at + HALF : at + RANK]
            else:
                value = total[:, at : at + RHS]
                low = jnp.concatenate([value[:HALF, :QUARTER], value[HALF:, :QUARTER]], axis=1)
                high = jnp.concatenate([value[:HALF, QUARTER:], value[HALF:, QUARTER:]], axis=1)
            rows = slice(start, start + low.shape[0])
            keep_ref[rows, :] = jnp.where(first, low, high)
            send_ref[rows, :] = jnp.where(first, high, low)
            start += low.shape[0]


def width_of(level):
    return RHS if level == 3 else RANK


def needed(groups):
    pairs = sorted(pair for group in groups for pair in group)
    return pairs, sorted({left for left, _ in pairs}), sorted({right for _, right in pairs})


def products(core, generators, solved_gens, rhs, groups, after):
    rows = rhs.shape[0]
    chunks = 4
    pairs, lefts, rights = needed(groups)
    width = sum(width_of(right) for _, right in pairs)
    outs = [struct(sum(HALF if right == 3 else RANK for _, right in group)) for group in groups for _ in range(2)]
    return pl.pallas_call(
        functools.partial(product_kernel, groups),
        in_specs=[SMEM, HBM, HBM, HBM] + [ANY] * len(after),
        out_specs=[VMEM] * len(outs),
        out_shape=outs,
        scratch_shapes=[
            pltpu.VMEM((len(lefts), rows, RANK), jnp.float32),
            pltpu.VMEM((sum(level < 3 for level in rights), rows, RANK), jnp.float32),
            pltpu.VMEM((rows, RHS), jnp.float32),
            pltpu.VMEM((RANK, width), jnp.float32),
            pltpu.SemaphoreType.DMA((len(lefts) + len(rights), chunks)),
        ],
        compiler_params=pltpu.CompilerParams(vmem_limit_bytes=STREAM_LIMIT),
        cost_estimate=cost(6 * rows * RANK * width, rows * (len(lefts) + len(rights)) * RANK),
    )(core, generators, solved_gens, rhs, *after)


def square_norm(value):
    return jnp.sum(value * value)


def identity():
    row = lax.broadcasted_iota(jnp.int32, (RANK, RANK), 0)
    col = lax.broadcasted_iota(jnp.int32, (RANK, RANK), 1)
    return jnp.where(row == col, 1.0, 0.0)


def series(start, scale, power_ref, sum_ref):
    norm = square_norm(start)
    power_ref[...] = dot(start, start)
    sum_ref[...] = scale * (identity() + start)

    def proceed(state):
        count, bound = state
        return (count < 60) & (bound > TOLERANCE) & (bound < DIVERGED * DIVERGED)

    def body(state):
        count, _ = state
        power = power_ref[...]
        bound = square_norm(power)
        values = sum_ref[...]
        both = dot(power, jnp.concatenate([power, values], axis=1))
        power_ref[...] = both[:, :RANK]
        sum_ref[...] = values + both[:, RANK:]
        return count + 1, bound

    return lax.while_loop(proceed, body, (jnp.int32(0), norm))[1]


def invert_kernel(core_ref, own_ref, sib_ref, own_other_ref, sib_other_ref, inverse_ref, p_sib_ref, power):
    core = core_ref[0]
    p_own = in_order(core, own_ref[...], own_other_ref[...])
    p_sib = in_order(core, sib_ref[...], sib_other_ref[...])
    p_sib_ref[...] = p_sib
    product = dot(p_sib, p_own)
    bound = series(product, 1.0, power, inverse_ref)

    @pl.when(jnp.logical_not(bound <= TOLERANCE))
    def _():
        scale = 1.0 / (1.0 + jnp.sqrt(square_norm(product)))
        series((1.0 - scale) * identity() + scale * product, scale, power, inverse_ref)


def call(kernel, out_shape, flops, *values, after=()):
    many = isinstance(out_shape, (list, tuple))
    floats = sum(value.size for value in values) + sum(out.size for out in (out_shape if many else [out_shape]))
    return pl.pallas_call(
        kernel,
        in_specs=[SMEM] + [VMEM] * (len(values) - 1) + [ANY] * len(after),
        out_specs=[VMEM] * len(out_shape) if many else VMEM,
        out_shape=out_shape,
        compiler_params=pltpu.CompilerParams(vmem_limit_bytes=VMEM_LIMIT),
        cost_estimate=cost(flops, floats),
    )(*values, *after)


def inverse(core, own, sib, own_other, sib_other):
    return pl.pallas_call(
        invert_kernel,
        in_specs=[SMEM] + [VMEM] * 4,
        out_specs=[VMEM] * 2,
        out_shape=[struct(RANK, RANK)] * 2,
        scratch_shapes=[pltpu.VMEM((RANK, RANK), jnp.float32)],
        compiler_params=pltpu.CompilerParams(vmem_limit_bytes=VMEM_LIMIT),
        cost_estimate=cost(6 * 9 * RANK**3, 4 * RANK * RANK),
    )(core, own, sib, own_other, sib_other)


def head_kernel(core_ref, inverse_ref, p_sib_ref, own_ref, sib_ref, own_other_ref, next_ref, z_ref, out_ref):
    own = own_ref[...]
    z = dot(inverse_ref[...], sib_ref[...] - dot(p_sib_ref[...], own))
    z_ref[...] = z
    out_ref[...] = next_ref[...] - dot_turned(in_order(core_ref[0], own, own_other_ref[...]), z)


def tail_kernel(core_ref, inverse_ref, p_sib_ref, own_ref, sib_ref, head_ref, head_other_ref, next_ref, *refs):
    z_ref, out_ref = refs[-2:]
    z = dot(inverse_ref[...], unpack(sib_ref) - dot(p_sib_ref[...], unpack(own_ref)))
    store(z_ref, z)
    crossed = in_order(core_ref[0], head_ref[...], head_other_ref[...])
    store(out_ref, unpack(next_ref) - dot_turned(crossed, z))


def third_kernel(core_ref, own_ref, own_other_ref, z_ref, next_ref, *refs):
    crossed = in_order(core_ref[0], own_ref[:RANK, :], own_other_ref[...])
    store(refs[-1], unpack(next_ref) - dot_turned(crossed, unpack(z_ref)))


def middle_kernel(core_ref, inverse_ref, p_sib_ref, own_ref, sib_ref, own_other_ref, next_ref, z_ref, out_ref):
    z = dot(inverse_ref[...], unpack(sib_ref) - dot(p_sib_ref[...], unpack(own_ref)))
    store(z_ref, z)
    crossed = in_order(core_ref[0], own_ref[:RANK, :], own_other_ref[...])
    store(out_ref, unpack(next_ref) - dot_turned(crossed, z))


def rhs_in_order(core, own, other):
    first = core == 0
    low = jnp.where(first, own, other)
    high = jnp.where(first, other, own)
    top = jnp.concatenate([low[:, :QUARTER], high[:, :QUARTER]], axis=1)
    bottom = jnp.concatenate([low[:, QUARTER:], high[:, QUARTER:]], axis=1)
    return jnp.concatenate([top, bottom], axis=0)


def reduced_kernel(
    core_ref, z1_ref, z1_other_ref, z0_ref, z0_other_ref, z01_ref, z01_other_ref, solved_ref, rhs_ref,
    high_ref, low_ref, out_ref, solved, rhs, sems,
):
    core = core_ref[0]
    copies = [
        pltpu.make_async_copy(solved_ref, solved, sems.at[0]),
        pltpu.make_async_copy(rhs_ref, rhs, sems.at[1]),
    ]
    for copy in copies:
        copy.start()
    z12 = in_order(core, z1_ref[:RANK, :], z1_other_ref[:RANK, :])
    z1x = rhs_in_order(core, z1_ref[RANK:, :], z1_other_ref[RANK:, :])
    z02 = in_order(core, z0_ref[:RANK, :], z0_other_ref[:RANK, :])
    z0x = rhs_in_order(core, z0_ref[RANK:, :], z0_other_ref[RANK:, :])
    z01 = in_order(core, z01_ref[...], z01_other_ref[...])
    middle = jnp.concatenate([z12, z1x], axis=1)
    first = jnp.concatenate([z02, z0x], axis=1) - dot(z01, middle)
    coefs = split(jnp.concatenate([first, middle], axis=0))
    for copy in copies:
        copy.wait()
    blocks = 4
    block = rhs.shape[0] // blocks
    for index in range(blocks):
        rows = slice(index * block, (index + 1) * block)
        left = split(jnp.concatenate([solved[0, rows, :], solved[1, rows, :]], axis=1))
        value = dot_parts(left, coefs)
        high, low = split(solved[2, rows, :] - value[:, :RANK])
        high_ref[rows, :] = high
        low_ref[rows, :] = low
        out_ref[rows, :] = rhs[rows, :] - value[:, RANK:]


def reduced(core, small, solved_gens, rhs):
    rows = rhs.shape[0]
    part = jax.ShapeDtypeStruct((rows, RANK), jnp.bfloat16)
    return pl.pallas_call(
        reduced_kernel,
        in_specs=[SMEM] + [VMEM] * len(small) + [HBM, HBM],
        out_specs=[VMEM] * 3,
        out_shape=[part, part, struct(rows, RHS)],
        scratch_shapes=[
            pltpu.VMEM((3, rows, RANK), jnp.float32),
            pltpu.VMEM((rows, RHS), jnp.float32),
            pltpu.SemaphoreType.DMA((2,)),
        ],
        compiler_params=pltpu.CompilerParams(vmem_limit_bytes=STREAM_LIMIT),
        cost_estimate=cost(6 * rows * 2 * RANK * (RANK + RHS), rows * 5 * RANK),
    )(core, *small, solved_gens, rhs)


def final_kernel(
    core_ref, inverse_ref, p_sib_ref, own_ref, own_other_ref, sib_ref, sib_other_ref, high_ref, low_ref, rhs_ref, out_ref
):
    core = core_ref[0]
    own = rhs_in_order(core, own_ref[...], own_other_ref[...])
    sib = rhs_in_order(core, sib_ref[...], sib_other_ref[...])
    z = dot(inverse_ref[...], sib - dot(p_sib_ref[...], own))
    out_ref[...] = rhs_ref[...] - dot_parts((high_ref[...], low_ref[...]), split(z))


def on_device(rhs, generators, solved_gens):
    groups = lax.axis_size("rows")
    sub_bits = lax.axis_size("sub").bit_length() - 1
    span_bits = (groups // 8).bit_length() - 1
    core = (lax.axis_index("sub") % 2).astype(jnp.int32).reshape(1)
    flops = 6 * RANK * RANK * HALF

    def partial_products(groups, *after):
        values = products(core, generators, solved_gens, rhs, groups, after)
        return [keep + swap(send, "sub", 0) for keep, send in zip(values[::2], values[1::2])], values[-1]

    def over_child(value):
        for bit in range(1, sub_bits):
            value = value + swap(value, "sub", bit)
        for bit in range(span_bits):
            value = value + swap(value, "rows", bit)
        return value

    (p_own, r_own), sent = partial_products((((0, 0),), ((0, 1),)))
    (tail,), _ = partial_products((((0, 2), (0, 3)),), sent)
    (near, far, third), _ = partial_products((((1, 1),), ((1, 2), (1, 3)), ((2, 2), (2, 3))), tail)
    p_own, r_own, tail, near, far, third = map(over_child, (p_own, r_own, tail, near, far, third))

    p_sib = swap(p_own, "rows", span_bits)
    r_sib = swap(r_own, "rows", span_bits)
    tail_sib = swap(tail, "rows", span_bits)
    p_own_other = swap(p_own, "sub", 0)
    r_own_other = swap(r_own, "sub", 0)
    tail_other = swap(tail[:RANK], "sub", 0)
    p_sib_other = swap(p_sib, "sub", 0)
    inverted, p_sib = inverse(core, p_own, p_sib, p_own_other, p_sib_other)
    z01, p_own = call(
        head_kernel, [struct(RANK)] * 2, 3 * flops, core, inverted, p_sib, r_own, r_sib, r_own_other, near
    )
    z0, r_own = call(
        tail_kernel, [struct(RANK + HALF)] * 2, 5 * flops,
        core, inverted, p_sib, tail, tail_sib, r_own, r_own_other, far, after=(p_own,),
    )
    third = call(third_kernel, struct(RANK + HALF), 2 * flops, core, tail, tail_other, z0, third, after=(r_own,))

    p_own = p_own + swap(p_own, "rows", span_bits)
    r_own = r_own + swap(r_own, "rows", span_bits)
    third = third + swap(third, "rows", span_bits)
    p_sib = swap(p_own, "rows", span_bits + 1)
    r_sib = swap(r_own, "rows", span_bits + 1)
    p_own_other = swap(p_own, "sub", 0)
    r_own_other = swap(r_own[:RANK], "sub", 0)
    p_sib_other = swap(p_sib, "sub", 0)
    inverted, p_sib = inverse(core, p_own, p_sib, p_own_other, p_sib_other)
    z1, own = call(
        middle_kernel, [struct(RANK + HALF)] * 2, 5 * flops,
        core, inverted, p_sib, r_own, r_sib, r_own_other, third,
    )

    p_own, r_own = own[:RANK], own[RANK:]
    p_own = p_own + swap(p_own, "rows", span_bits + 1)
    r_own = r_own + swap(r_own, "rows", span_bits + 1)
    p_sib = swap(p_own, "rows", span_bits + 2)
    r_sib = swap(r_own, "rows", span_bits + 2)
    p_own_other = swap(p_own, "sub", 0)
    r_own_other = swap(r_own, "sub", 0)
    small = (z1, swap(z1, "sub", 0), z0, swap(z0, "sub", 0), z01, swap(z01, "sub", 0))
    high, low, current = reduced(core, small, solved_gens, rhs)
    p_sib_other = swap(p_sib, "sub", 0)
    r_sib_other = swap(r_sib, "sub", 0)
    inverted, p_sib = inverse(core, p_own, p_sib, p_own_other, p_sib_other)
    return call(
        final_kernel, struct(rhs.shape[0], RHS), 6 * rhs.shape[0] * RANK * RHS,
        core, inverted, p_sib, r_own, r_own_other, r_sib, r_sib_other, high, low, current,
    )


def solution(mesh):
    placed = (
        P(("rows", "sub"), None),
        P(None, ("rows", "sub"), None),
        P(None, ("rows", "sub"), None),
    )
    return jax.shard_map(
        on_device, mesh=mesh, in_specs=placed, out_specs=P(("rows", "sub"), None), check_vma=False
    )
```

time: 99.1 us -> 79.1 us (0.80)
  waiting for transfers between devices: 46.8 us -> 20.6 us
  starting transfers between devices: 23.7 us -> 29.4 us
    ppermute x32 -> x38, waiting for transfers between devices: 46.8 us -> 20.6 us  [swap(): return lax.ppermute(value, axis, pairs)]
    ppermute x32 -> x38, starting transfers between devices: 23.7 us -> 29.4 us  [swap(): return lax.ppermute(value, axis, pairs)]
    pallas_call x2 -> x3, Pallas kernels: 4.68 us -> 6.93 us  [inverse(): pl.pallas_call(invert_kernel, in_specs=[SMEM] + [VMEM] * 4, out_specs=[VM...]
    pallas_call x9, Pallas kernels: 21.6 us -> 20.1 us  [the longest x3 9.63 us: products(): pl.pallas_call(functools.partial(product_kernel, groups), in_specs=[SMEM,...]
  transfers between devices with their start and end apart: 32 -> 38, of which waited for: 12 -> 15; matrix products, arithmetic and copies ran while one was open for 0% -> 0% of each run, Pallas kernels for 15% -> 24%
where the time goes in v3:
time: 79.1 us; the launch traced here: 78.8 us
  starting transfers between devices  29.4 us (37%)
  Pallas kernels  27 us (34%)
  waiting for transfers between devices  20.6 us (26%)
  local copies, waits for them, and re-layouts  1.09 us (1%)
    ppermute x38, starting transfers between devices, swap(): return lax.ppermute(value, axis, pairs)  29.4 us
    ppermute x38, waiting for transfers between devices, swap(): return lax.ppermute(value, axis, pairs)  20.6 us
    pallas_call x3, Pallas kernels, products(): pl.pallas_call(functools.partial(product_kernel, groups), in_specs=[SMEM,...  9.63 us
    pallas_call x3, Pallas kernels, inverse(): pl.pallas_call(invert_kernel, in_specs=[SMEM] + [VMEM] * 4, out_specs=[VM...  6.93 us
    pallas_call x5, Pallas kernels, call(): pl.pallas_call(kernel, in_specs=[SMEM] + [VMEM] * (len(values) - 1) + [AN...  5.3 us
    pallas_call x1, Pallas kernels, reduced(): pl.pallas_call(reduced_kernel, in_specs=[SMEM] + [VMEM] * len(small) + [H...  5.15 us
  transfers between devices with their start and end apart: 38, of which 15 were waited for; matrix products, arithmetic and copies ran while one was open for 0% of the time, Pallas kernels for 24%

profile of v3, /device:TPU:0, one launch (start us, length us, event | category | flops | bytes accessed | tf_op | source)
XLA Modules:
  0.0 78.8 jit_solution(4970061577692496954)
XLA Ops:
  0.0 1.0 %copy-done = f32[1024,128]{1,0:T(8,128)S(1)} copy-done((f32[1024,128]{1,0:T(8,128)S(1)}, f32[1024,128]{1,0:T(8,128)}, u32[]{:S(2)}) %copy-start) | copy-done | bytes 524312
  1.0 2.5 %shard_map.37 = (f32[256,128]{1,0:T(8,128)S(1)}, f32[256,128]{1,0:T(8,128)S(1)}, f32[256,128]{1,0:T(8,128)S(1)}, f32[256,128]{1,0:T(8,128)S(1)}) custom-call(s32[1]{0:T(128)} %bitcast.core_ref, f32[3,1024,256]{2,1,0:T(8,128)} %gens_ref.5, f32[3,1024,256]{2,1,0:T(8,128)} %solved_ref.7, f32[1024,128]{1,0:T(8,128)S(1)} %copy-done), custom_call_target="tpu_custom_call" | custom-call | flops 805306368 | bytes 3145728 | tf_op jit(solution)/shard_map/pallas_call | solution.py:166
  3.5 2.8 %shard_map.39 = (f32[384,128]{1,0:T(8,128)S(1)}, f32[384,128]{1,0:T(8,128)S(1)}) custom-call(s32[1]{0:T(128)} %bitcast.core_ref, f32[3,1024,256]{2,1,0:T(8,128)} %gens_ref.5, f32[3,1024,256]{2,1,0:T(8,128)} %solved_ref.7, f32[1024,128]{1,0:T(8,128)S(1)} %copy-done, f32[256,128]{1,0:T(8,128)S(1)} %get-tuple-element.37.refs_0_), custom_call_target="tpu_custom_call" | custom-call | flops 603979776 | bytes 3145728 | tf_op jit(solution)/shard_map/pallas_call | solution.py:166
  6.4 0.5 collective-permute-start.9
  6.9 0.1 collective-permute-start.5
  7.0 0.4 collective-permute-start
  7.4 0.8 %collective-permute-done.5 = f32[256,128]{1,0:T(8,128)S(1)} collective-permute-done((f32[256,128]{1,0:T(8,128)S(1)}, f32[256,128]{1,0:T(8,128)S(1)}, u32[]{:S(2)}, u32[]{:S(2)}) %collective-permute-start.5) | collective-permute-done | bytes 131104 | tf_op jit(solution)/shard_map/ppermute | solution.py:28
  8.3 2.9 %collective-permute-start.6 = (f32[256,128]{1,0:T(8,128)S(1)}, f32[256,128]{1,0:T(8,128)S(1)}, u32[]{:S(2)}, u32[]{:S(2)}) collective-permute-start(f32[256,128]{1,0:T(8,128)S(1)} %add.58), channel_id=1, source_target_pairs={{0,2},{1,3},{2,0},{3,1},{4,6},{5,7},{6,4},{7,5},{8,10},{9,11},{10,... | collective-permute-start | bytes 393224 | tf_op jit(solution)/shard_map/ppermute | solution.py:28
  11.1 0.0 collective-permute-done
  11.1 0.2 collective-permute-start.1
  11.3 0.0 collective-permute-done.9
  11.4 4.3 %shard_map.40 = (f32[256,128]{1,0:T(8,128)S(1)}, f32[256,128]{1,0:T(8,128)S(1)}, f32[384,128]{1,0:T(8,128)S(1)}, f32[384,128]{1,0:T(8,128)S(1)}, f32[384,128]{1,0:T(8,128)S(1)}, /*index=5*/f32[384,128]{1,0:T(8,128)S(1)}) custom-call(s32[1]{0:T(128)} %bitcast.core_ref, f32[3,1024,256]{2,1,0:T(8,128)} %gens_ref.5, f32[3,1024,256]{2,1,0:T(8,128)} %solved_ref.7, ...), custom_call_target="tpu_custom_call" | custom-call | flops 1610612736 | bytes 5242880 | tf_op jit(solution)/shard_map/pallas_call | solution.py:166
  15.7 0.1 collective-permute-start.10
  15.8 2.0 %collective-permute-done.1 = f32[256,128]{1,0:T(8,128)S(1)} collective-permute-done((f32[256,128]{1,0:T(8,128)S(1)}, f32[256,128]{1,0:T(8,128)S(1)}, u32[]{:S(2)}, u32[]{:S(2)}) %collective-permute-start.1) | collective-permute-done | bytes 131104 | tf_op jit(solution)/shard_map/ppermute | solution.py:28
  17.8 1.8 %collective-permute-start.2 = (f32[256,128]{1,0:T(8,128)S(1)}, f32[256,128]{1,0:T(8,128)S(1)}, u32[]{:S(2)}, u32[]{:S(2)}) collective-permute-start(f32[256,128]{1,0:T(8,128)S(1)} %add.57.own_ref), channel_id=1, source_target_pairs={{0,4},{4,0},{8,12},{12,8},{16,20},{20,16},{24,28},{28,24},{1,5},{5... | collective-permute-start | bytes 393224 | tf_op jit(solution)/shard_map/ppermute | solution.py:28
  19.6 0.5 collective-permute-start.18
  20.1 0.0 collective-permute-done.6
  20.1 1.5 %collective-permute-start.16 = (f32[384,128]{1,0:T(8,128)S(1)}, f32[384,128]{1,0:T(8,128)S(1)}, u32[]{:S(2)}, u32[]{:S(2)}) collective-permute-start(f32[384,128]{1,0:T(8,128)S(1)} %add.60.refs_0_), channel_id=1, source_target_pairs={{0,2},{1,3},{2,0},{3,1},{4,6},{5,7},{6,4},{7,5},{8,10},{9,11},{10,... | collective-permute-start | bytes 589832 | tf_op jit(solution)/shard_map/ppermute | solution.py:28
  21.7 0.0 collective-permute-done.10
  21.7 0.0 collective-permute-start.24
  21.7 1.4 %collective-permute-done.2.sib_ref = f32[256,128]{1,0:T(8,128)S(1)} collective-permute-done((f32[256,128]{1,0:T(8,128)S(1)}, f32[256,128]{1,0:T(8,128)S(1)}, u32[]{:S(2)}, u32[]{:S(2)}) %collective-permute-start.2) | collective-permute-done | bytes 131104 | tf_op jit(solution)/shard_map/ppermute | solution.py:28
  23.0 1.6 %collective-permute-start.11 = (f32[256,128]{1,0:T(8,128)S(1)}, f32[256,128]{1,0:T(8,128)S(1)}, u32[]{:S(2)}, u32[]{:S(2)}) collective-permute-start(f32[256,128]{1,0:T(8,128)S(1)} %add.61), channel_id=1, source_target_pairs={{0,2},{1,3},{2,0},{3,1},{4,6},{5,7},{6,4},{7,5},{8,10},{9,11},{10,... | collective-permute-start | bytes 393224 | tf_op jit(solution)/shard_map/ppermute | solution.py:28
  24.6 0.0 collective-permute-done.18
  24.6 1.6 %collective-permute-start.7 = (f32[256,128]{1,0:T(8,128)S(1)}, f32[256,128]{1,0:T(8,128)S(1)}, u32[]{:S(2)}, u32[]{:S(2)}) collective-permute-start(f32[256,128]{1,0:T(8,128)S(1)} %add.59.own_ref.head_ref), channel_id=1, source_target_pairs={{0,4},{4,0},{8,12},{12,8},{16,20},{20,16},{24,28},{28,24},{1,5},{5... | collective-permute-start | bytes 393224 | tf_op jit(solution)/shard_map/ppermute | solution.py:28
  26.2 1.7 %collective-permute-done.16 = f32[384,128]{1,0:T(8,128)S(1)} collective-permute-done((f32[384,128]{1,0:T(8,128)S(1)}, f32[384,128]{1,0:T(8,128)S(1)}, u32[]{:S(2)}, u32[]{:S(2)}) %collective-permute-start.16) | collective-permute-done | bytes 196640 | tf_op jit(solution)/shard_map/ppermute | solution.py:28
  28.0 1.6 %collective-permute-start.19 = (f32[384,128]{1,0:T(8,128)S(1)}, f32[384,128]{1,0:T(8,128)S(1)}, u32[]{:S(2)}, u32[]{:S(2)}) collective-permute-start(f32[384,128]{1,0:T(8,128)S(1)} %add.65), channel_id=1, source_target_pairs={{0,2},{1,3},{2,0},{3,1},{4,6},{5,7},{6,4},{7,5},{8,10},{9,11},{10,... | collective-permute-start | bytes 589832 | tf_op jit(solution)/shard_map/ppermute | solution.py:28
  29.6 0.2 collective-permute-done.11
  29.7 0.3 collective-permute-start.17
  30.1 0.0 collective-permute-done.4.sib_other_ref
  30.2 1.8 %collective-permute-start.25 = (f32[384,128]{1,0:T(8,128)S(1)}, f32[384,128]{1,0:T(8,128)S(1)}, u32[]{:S(2)}, u32[]{:S(2)}) collective-permute-start(f32[384,128]{1,0:T(8,128)S(1)} %add.68), channel_id=1, source_target_pairs={{0,2},{1,3},{2,0},{3,1},{4,6},{5,7},{6,4},{7,5},{8,10},{9,11},{10,... | collective-permute-start | bytes 589832 | tf_op jit(solution)/shard_map/ppermute | solution.py:28
  31.9 2.2 %shard_map.38 = (f32[256,256]{1,0:T(8,128)S(1)}, f32[256,256]{1,0:T(8,128)S(1)}) custom-call(s32[1]{0:T(128)} %bitcast.core_ref, f32[256,128]{1,0:T(8,128)S(1)} %add.57.own_ref, f32[256,128]{1,0:T(8,128)S(1)} %collective-permute-done.2.sib_ref, f32[256,128]{1,0:T(8,128)S(1)} %collective-permute-done.3.own_other_ref, ...), custom_call_target="tpu_custom_call" | custom-call | flops 905969664 | bytes 1048576 | tf_op jit(solution)/shard_map/pallas_call | solution.py:243
  34.2 0.8 %shard_map.41 = (f32[256,128]{1,0:T(8,128)S(1)}, f32[256,128]{1,0:T(8,128)S(1)}) custom-call(s32[1]{0:T(128)} %bitcast.core_ref, f32[256,256]{1,0:T(8,128)S(1)} %get-tuple-element.34.inverse_ref, f32[256,256]{1,0:T(8,128)S(1)} %get-tuple-element.35.p_sib_ref, f32[256,128]{1,0:T(8,128)S(1)} %add.59.own_ref.head_ref, ...), custom_call_target="tpu_custom_call" | custom-call | flops 150994944 | bytes 1310724 | tf_op jit(solution)/shard_map/pallas_call | solution.py:232
  35.0 1.6 %collective-permute-start.12 = (f32[256,128]{1,0:T(8,128)S(1)}, f32[256,128]{1,0:T(8,128)S(1)}, u32[]{:S(2)}, u32[]{:S(2)}) collective-permute-start(f32[256,128]{1,0:T(8,128)S(1)} %get-tuple-element.42.refs_0_), channel_id=1, source_target_pairs={{0,4},{4,0},{8,12},{12,8},{16,20},{20,16},{24,28},{28,24},{1,5},{5... | collective-permute-start | bytes 393224 | tf_op jit(solution)/shard_map/ppermute | solution.py:28
  36.6 0.1 collective-permute-start.23
  36.7 0.2 collective-permute-done.17.sib_ref
  36.9 1.0 %shard_map.43 = (f32[384,128]{1,0:T(8,128)S(1)}, f32[384,128]{1,0:T(8,128)S(1)}) custom-call(s32[1]{0:T(128)} %bitcast.core_ref, f32[256,256]{1,0:T(8,128)S(1)} %get-tuple-element.34.inverse_ref, f32[256,256]{1,0:T(8,128)S(1)} %get-tuple-element.35.p_sib_ref, f32[384,128]{1,0:T(8,128)S(1)} %add.64.own_ref, f32[384,128]{1,0:T(8,128)S(1)} %collective-permute-done.17.sib_ref, ...), custom_call_target="tpu_custom_call" | custom-call | flops 251658240 | bytes 1769476 | tf_op jit(solution)/shard_map/pallas_call | solution.py:232
  37.9 0.5 collective-permute-start.20
  38.4 1.7 %collective-permute-done.12 = f32[256,128]{1,0:T(8,128)S(1)} collective-permute-done((f32[256,128]{1,0:T(8,128)S(1)}, f32[256,128]{1,0:T(8,128)S(1)}, u32[]{:S(2)}, u32[]{:S(2)}) %collective-permute-start.12) | collective-permute-done | bytes 131104 | tf_op jit(solution)/shard_map/ppermute | solution.py:28
  40.1 1.7 %collective-permute-start.13 = (f32[256,128]{1,0:T(8,128)S(1)}, f32[256,128]{1,0:T(8,128)S(1)}, u32[]{:S(2)}, u32[]{:S(2)}) collective-permute-start(f32[256,128]{1,0:T(8,128)S(1)} %add.63.own_ref), channel_id=1, source_target_pairs={{0,8},{4,12},{8,0},{12,4},{16,24},{20,28},{24,16},{28,20},{1,9},{5... | collective-permute-start | bytes 393224 | tf_op jit(solution)/shard_map/ppermute | solution.py:28
  41.8 0.4 shard_map.44
  42.2 1.6 %collective-permute-start.26 = (f32[384,128]{1,0:T(8,128)S(1)}, f32[384,128]{1,0:T(8,128)S(1)}, u32[]{:S(2)}, u32[]{:S(2)}) collective-permute-start(f32[384,128]{1,0:T(8,128)S(1)} %shard_map.44), channel_id=1, source_target_pairs={{0,4},{4,0},{8,12},{12,8},{16,20},{20,16},{24,28},{28,24},{1,5},{5... | collective-permute-start | bytes 589832 | tf_op jit(solution)/shard_map/ppermute | solution.py:28
  43.7 1.3 %collective-permute-done.13.sib_ref = f32[256,128]{1,0:T(8,128)S(1)} collective-permute-done((f32[256,128]{1,0:T(8,128)S(1)}, f32[256,128]{1,0:T(8,128)S(1)}, u32[]{:S(2)}, u32[]{:S(2)}) %collective-permute-start.13) | collective-permute-done | bytes 131104 | tf_op jit(solution)/shard_map/ppermute | solution.py:28
  45.1 0.6 collective-permute-done.20
  45.7 1.6 %collective-permute-start.21 = (f32[384,128]{1,0:T(8,128)S(1)}, f32[384,128]{1,0:T(8,128)S(1)}, u32[]{:S(2)}, u32[]{:S(2)}) collective-permute-start(f32[384,128]{1,0:T(8,128)S(1)} %add.67.own_ref), channel_id=1, source_target_pairs={{0,8},{4,12},{8,0},{12,4},{16,24},{20,28},{24,16},{28,20},{1,9},{5... | collective-permute-start | bytes 589832 | tf_op jit(solution)/shard_map/ppermute | solution.py:28
  47.4 0.1 collective-permute-start.22
  47.4 1.9 %collective-permute-done.26 = f32[384,128]{1,0:T(8,128)S(1)} collective-permute-done((f32[384,128]{1,0:T(8,128)S(1)}, f32[384,128]{1,0:T(8,128)S(1)}, u32[]{:S(2)}, u32[]{:S(2)}) %collective-permute-start.26) | collective-permute-done | bytes 196640 | tf_op jit(solution)/shard_map/ppermute | solution.py:28
  49.4 2.4 %shard_map.42 = (f32[256,256]{1,0:T(8,128)S(1)}, f32[256,256]{1,0:T(8,128)S(1)}) custom-call(s32[1]{0:T(128)} %bitcast.core_ref, f32[256,128]{1,0:T(8,128)S(1)} %add.63.own_ref, f32[256,128]{1,0:T(8,128)S(1)} %collective-permute-done.13.sib_ref, f32[256,128]{1,0:T(8,128)S(1)} %collective-permute-done.14.own_other_ref, ...), custom_call_target="tpu_custom_call" | custom-call | flops 905969664 | bytes 1048576 | tf_op jit(solution)/shard_map/pallas_call | solution.py:243
  51.8 0.7 collective-permute-done.21.sib_ref
  52.5 1.0 %shard_map.45 = (f32[384,128]{1,0:T(8,128)S(1)}, f32[384,128]{1,0:T(8,128)S(1)}) custom-call(s32[1]{0:T(128)} %bitcast.core_ref, f32[256,256]{1,0:T(8,128)S(1)} %get-tuple-element.43.inverse_ref, f32[256,256]{1,0:T(8,128)S(1)} %get-tuple-element.44.p_sib_ref, f32[384,128]{1,0:T(8,128)S(1)} %add.67.own_ref, f32[384,128]{1,0:T(8,128)S(1)} %collective-permute-done.21.sib_ref, ...), custom_call_target="tpu_custom_call" | custom-call | flops 251658240 | bytes 1638404 | tf_op jit(solution)/shard_map/pallas_call | solution.py:232
  53.6 1.7 %collective-permute-start.27 = (f32[256,128]{1,0:T(8,128)S(1)}, f32[256,128]{1,0:T(8,128)S(1)}, u32[]{:S(2)}, u32[]{:S(2)}) collective-permute-start(f32[256,128]{1,0:T(8,128)S(1)} %slice.14), channel_id=1, source_target_pairs={{0,8},{4,12},{8,0},{12,4},{16,24},{20,28},{24,16},{28,20},{1,9},{5... | collective-permute-start | bytes 393224 | tf_op jit(solution)/shard_map/ppermute | solution.py:28
  55.2 0.5 collective-permute-start.36
  55.7 0.1 collective-permute-start.35
  55.8 0.4 collective-permute-start.31
  56.2 2.4 %collective-permute-done.27 = f32[256,128]{1,0:T(8,128)S(1)} collective-permute-done((f32[256,128]{1,0:T(8,128)S(1)}, f32[256,128]{1,0:T(8,128)S(1)}, u32[]{:S(2)}, u32[]{:S(2)}) %collective-permute-start.27) | collective-permute-done | bytes 131104 | tf_op jit(solution)/shard_map/ppermute | solution.py:28
  58.6 2.7 %collective-permute-start.28 = (f32[256,128]{1,0:T(8,128)S(1)}, f32[256,128]{1,0:T(8,128)S(1)}, u32[]{:S(2)}, u32[]{:S(2)}) collective-permute-start(f32[256,128]{1,0:T(8,128)S(1)} %slice_add_fusion.1.own_ref), channel_id=1, source_target_pairs={{0,16},{4,20},{8,24},{12,28},{16,0},{20,4},{24,8},{28,12},{1,17},{... | collective-permute-start | bytes 393224 | tf_op jit(solution)/shard_map/ppermute | solution.py:28
  61.3 0.4 collective-permute-done.31
  61.7 1.7 %collective-permute-start.33 = (f32[128,128]{1,0:T(8,128)S(1)}, f32[128,128]{1,0:T(8,128)S(1)}, u32[]{:S(2)}, u32[]{:S(2)}) collective-permute-start(f32[128,128]{1,0:T(8,128)S(1)} %slice_add_fusion.own_ref), channel_id=1, source_target_pairs={{0,16},{4,20},{8,24},{12,28},{16,0},{20,4},{24,8},{28,12},{1,17},{... | collective-permute-start | bytes 196616 | tf_op jit(solution)/shard_map/ppermute | solution.py:28
  63.4 5.2 %collective-permute-done.28.sib_ref = f32[256,128]{1,0:T(8,128)S(1)} collective-permute-done((f32[256,128]{1,0:T(8,128)S(1)}, f32[256,128]{1,0:T(8,128)S(1)}, u32[]{:S(2)}, u32[]{:S(2)}) %collective-permute-start.28) | collective-permute-done | bytes 131104 | tf_op jit(solution)/shard_map/ppermute | solution.py:28
  68.6 0.5 collective-permute-start.32
  69.1 0.2 collective-permute-done.33.sib_ref
  69.3 5.1 %shard_map.47 = (bf16[1024,256]{1,0:T(8,128)(2,1)S(1)}, bf16[1024,256]{1,0:T(8,128)(2,1)}, f32[1024,128]{1,0:T(8,128)}) custom-call(s32[1]{0:T(128)} %bitcast.core_ref, f32[384,128]{1,0:T(8,128)S(1)} %get-tuple-element.54.z1_ref, f32[384,128]{1,0:T(8,128)S(1)} %collective-permute-done.35.z1_other_ref, f32[384,128]{1,0:T(8,128)S(1)} %get-tuple-element.48.z_ref.z0_ref, ...), custom_call_target="tpu_custom_call" | custom-call | flops 1207959552 | bytes 5242880 | tf_op jit(solution)/shard_map/pallas_call | solution.py:326
  74.5 0.0 copy-start.1
  74.5 2.3 %shard_map.46 = (f32[256,256]{1,0:T(8,128)S(1)}, f32[256,256]{1,0:T(8,128)S(1)}) custom-call(s32[1]{0:T(128)} %bitcast.core_ref, f32[256,128]{1,0:T(8,128)S(1)} %slice_add_fusion.1.own_ref, f32[256,128]{1,0:T(8,128)S(1)} %collective-permute-done.28.sib_ref, f32[256,128]{1,0:T(8,128)S(1)} %collective-permute-done.29.own_other_ref, ...), custom_call_target="tpu_custom_call" | custom-call | flops 905969664 | bytes 1048576 | tf_op jit(solution)/shard_map/pallas_call | solution.py:243
  76.8 2.0 %shard_map.48 = f32[1024,128]{1,0:T(8,128)} custom-call(s32[1]{0:T(128)} %bitcast.core_ref, f32[256,256]{1,0:T(8,128)S(1)} %get-tuple-element.52.inverse_ref, f32[256,256]{1,0:T(8,128)S(1)} %get-tuple-element.53.p_sib_ref, f32[128,128]{1,0:T(8,128)S(1)} %slice_add_fusion.own_ref, f32[128,128]{1,0:T(8,128)S(1)} %collective-permute-done.32.own_other_ref, ...), custom_call_target="tpu_custom_call" | custom-call | flops 201326592 | bytes 3932164 | tf_op jit(solution)/shard_map/pallas_call | solution.py:232
  (51 shorter events, 0.4 us)
Async XLA Ops:
  0.0 1.0 %copy-start = (f32[1024,128]{1,0:T(8,128)S(1)}, f32[1024,128]{1,0:T(8,128)}, u32[]{:S(2)}) copy-start(f32[1024,128]{1,0:T(8,128)} %rhs_ref.7) | copy-start | bytes 1572868
  6.4 5.0 %collective-permute-start.9 = (f32[384,128]{1,0:T(8,128)S(1)}, f32[384,128]{1,0:T(8,128)S(1)}, u32[]{:S(2)}, u32[]{:S(2)}) collective-permute-start(f32[384,128]{1,0:T(8,128)S(1)} %get-tuple-element.39), channel_id=1, source_target_pairs={{0,1},{1,0},{2,3},{3,2},{4,5},{5,4},{6,7},{7,6},{8,9},{9,8},{10,11... | collective-permute-start | bytes 589832 | tf_op jit(solution)/shard_map/ppermute | solution.py:28
  6.9 1.3 %collective-permute-start.5 = (f32[256,128]{1,0:T(8,128)S(1)}, f32[256,128]{1,0:T(8,128)S(1)}, u32[]{:S(2)}, u32[]{:S(2)}) collective-permute-start(f32[256,128]{1,0:T(8,128)S(1)} %get-tuple-element.37.refs_0_), channel_id=1, source_target_pairs={{0,1},{1,0},{2,3},{3,2},{4,5},{5,4},{6,7},{7,6},{8,9},{9,8},{10,11... | collective-permute-start | bytes 393224 | tf_op jit(solution)/shard_map/ppermute | solution.py:28
  7.0 4.1 %collective-permute-start = (f32[256,128]{1,0:T(8,128)S(1)}, f32[256,128]{1,0:T(8,128)S(1)}, u32[]{:S(2)}, u32[]{:S(2)}) collective-permute-start(f32[256,128]{1,0:T(8,128)S(1)} %get-tuple-element.33), channel_id=1, source_target_pairs={{0,1},{1,0},{2,3},{3,2},{4,5},{5,4},{6,7},{7,6},{8,9},{9,8},{10,11... | collective-permute-start | bytes 393224 | tf_op jit(solution)/shard_map/ppermute | solution.py:28
  8.3 11.9 %collective-permute-start.6 = (f32[256,128]{1,0:T(8,128)S(1)}, f32[256,128]{1,0:T(8,128)S(1)}, u32[]{:S(2)}, u32[]{:S(2)}) collective-permute-start(f32[256,128]{1,0:T(8,128)S(1)} %add.58), channel_id=1, source_target_pairs={{0,2},{1,3},{2,0},{3,1},{4,6},{5,7},{6,4},{7,5},{8,10},{9,11},{10,... | collective-permute-start | bytes 393224 | tf_op jit(solution)/shard_map/ppermute | solution.py:28
  11.1 6.7 %collective-permute-start.1 = (f32[256,128]{1,0:T(8,128)S(1)}, f32[256,128]{1,0:T(8,128)S(1)}, u32[]{:S(2)}, u32[]{:S(2)}) collective-permute-start(f32[256,128]{1,0:T(8,128)S(1)} %add.56), channel_id=1, source_target_pairs={{0,2},{1,3},{2,0},{3,1},{4,6},{5,7},{6,4},{7,5},{8,10},{9,11},{10,... | collective-permute-start | bytes 393224 | tf_op jit(solution)/shard_map/ppermute | solution.py:28
  15.7 6.0 %collective-permute-start.10 = (f32[256,128]{1,0:T(8,128)S(1)}, f32[256,128]{1,0:T(8,128)S(1)}, u32[]{:S(2)}, u32[]{:S(2)}) collective-permute-start(f32[256,128]{1,0:T(8,128)S(1)} %get-tuple-element.41), channel_id=1, source_target_pairs={{0,1},{1,0},{2,3},{3,2},{4,5},{5,4},{6,7},{7,6},{8,9},{9,8},{10,11... | collective-permute-start | bytes 393224 | tf_op jit(solution)/shard_map/ppermute | solution.py:28
  17.8 5.2 %collective-permute-start.2 = (f32[256,128]{1,0:T(8,128)S(1)}, f32[256,128]{1,0:T(8,128)S(1)}, u32[]{:S(2)}, u32[]{:S(2)}) collective-permute-start(f32[256,128]{1,0:T(8,128)S(1)} %add.57.own_ref), channel_id=1, source_target_pairs={{0,4},{4,0},{8,12},{12,8},{16,20},{20,16},{24,28},{28,24},{1,5},{5... | collective-permute-start | bytes 393224 | tf_op jit(solution)/shard_map/ppermute | solution.py:28
  19.6 5.0 %collective-permute-start.3 = (f32[256,128]{1,0:T(8,128)S(1)}, f32[256,128]{1,0:T(8,128)S(1)}, u32[]{:S(2)}, u32[]{:S(2)}) collective-permute-start(f32[256,128]{1,0:T(8,128)S(1)} %add.57.own_ref), channel_id=1, source_target_pairs={{0,1},{1,0},{2,3},{3,2},{4,5},{5,4},{6,7},{7,6},{8,9},{9,8},{10,11... | collective-permute-start | bytes 393224 | tf_op jit(solution)/shard_map/ppermute | solution.py:28
  19.6 5.0 %collective-permute-start.18 = (f32[384,128]{1,0:T(8,128)S(1)}, f32[384,128]{1,0:T(8,128)S(1)}, u32[]{:S(2)}, u32[]{:S(2)}) collective-permute-start(f32[384,128]{1,0:T(8,128)S(1)} %get-tuple-element.46), channel_id=1, source_target_pairs={{0,1},{1,0},{2,3},{3,2},{4,5},{5,4},{6,7},{7,6},{8,9},{9,8},{10,11... | collective-permute-start | bytes 589832 | tf_op jit(solution)/shard_map/ppermute | solution.py:28
  20.1 7.8 %collective-permute-start.16 = (f32[384,128]{1,0:T(8,128)S(1)}, f32[384,128]{1,0:T(8,128)S(1)}, u32[]{:S(2)}, u32[]{:S(2)}) collective-permute-start(f32[384,128]{1,0:T(8,128)S(1)} %add.60.refs_0_), channel_id=1, source_target_pairs={{0,2},{1,3},{2,0},{3,1},{4,6},{5,7},{6,4},{7,5},{8,10},{9,11},{10,... | collective-permute-start | bytes 589832 | tf_op jit(solution)/shard_map/ppermute | solution.py:28
  21.7 6.3 %collective-permute-start.24 = (f32[384,128]{1,0:T(8,128)S(1)}, f32[384,128]{1,0:T(8,128)S(1)}, u32[]{:S(2)}, u32[]{:S(2)}) collective-permute-start(f32[384,128]{1,0:T(8,128)S(1)} %get-tuple-element.50), channel_id=1, source_target_pairs={{0,1},{1,0},{2,3},{3,2},{4,5},{5,4},{6,7},{7,6},{8,9},{9,8},{10,11... | collective-permute-start | bytes 589832 | tf_op jit(solution)/shard_map/ppermute | solution.py:28
  23.0 6.7 %collective-permute-start.11 = (f32[256,128]{1,0:T(8,128)S(1)}, f32[256,128]{1,0:T(8,128)S(1)}, u32[]{:S(2)}, u32[]{:S(2)}) collective-permute-start(f32[256,128]{1,0:T(8,128)S(1)} %add.61), channel_id=1, source_target_pairs={{0,2},{1,3},{2,0},{3,1},{4,6},{5,7},{6,4},{7,5},{8,10},{9,11},{10,... | collective-permute-start | bytes 393224 | tf_op jit(solution)/shard_map/ppermute | solution.py:28
  24.6 5.5 %collective-permute-start.4 = (f32[256,128]{1,0:T(8,128)S(1)}, f32[256,128]{1,0:T(8,128)S(1)}, u32[]{:S(2)}, u32[]{:S(2)}) collective-permute-start(f32[256,128]{1,0:T(8,128)S(1)} %collective-permute-done.2.sib_ref), channel_id=1, source_target_pairs={{0,1},{1,0},{2,3},{3,2},{4,5},{5,4},{6,7},{7,6},{8,9},{9,8},{10,11... | collective-permute-start | bytes 393224 | tf_op jit(solution)/shard_map/ppermute | solution.py:28
  24.6 9.5 %collective-permute-start.7 = (f32[256,128]{1,0:T(8,128)S(1)}, f32[256,128]{1,0:T(8,128)S(1)}, u32[]{:S(2)}, u32[]{:S(2)}) collective-permute-start(f32[256,128]{1,0:T(8,128)S(1)} %add.59.own_ref.head_ref), channel_id=1, source_target_pairs={{0,4},{4,0},{8,12},{12,8},{16,20},{20,16},{24,28},{28,24},{1,5},{5... | collective-permute-start | bytes 393224 | tf_op jit(solution)/shard_map/ppermute | solution.py:28
  27.9 6.3 %collective-permute-start.8 = (f32[256,128]{1,0:T(8,128)S(1)}, f32[256,128]{1,0:T(8,128)S(1)}, u32[]{:S(2)}, u32[]{:S(2)}) collective-permute-start(f32[256,128]{1,0:T(8,128)S(1)} %add.59.own_ref.head_ref), channel_id=1, source_target_pairs={{0,1},{1,0},{2,3},{3,2},{4,5},{5,4},{6,7},{7,6},{8,9},{9,8},{10,11... | collective-permute-start | bytes 393224 | tf_op jit(solution)/shard_map/ppermute | solution.py:28
  28.0 8.7 %collective-permute-start.19 = (f32[384,128]{1,0:T(8,128)S(1)}, f32[384,128]{1,0:T(8,128)S(1)}, u32[]{:S(2)}, u32[]{:S(2)}) collective-permute-start(f32[384,128]{1,0:T(8,128)S(1)} %add.65), channel_id=1, source_target_pairs={{0,2},{1,3},{2,0},{3,1},{4,6},{5,7},{6,4},{7,5},{8,10},{9,11},{10,... | collective-permute-start | bytes 589832 | tf_op jit(solution)/shard_map/ppermute | solution.py:28
  29.7 7.1 %collective-permute-start.17 = (f32[384,128]{1,0:T(8,128)S(1)}, f32[384,128]{1,0:T(8,128)S(1)}, u32[]{:S(2)}, u32[]{:S(2)}) collective-permute-start(f32[384,128]{1,0:T(8,128)S(1)} %add.64.own_ref), channel_id=1, source_target_pairs={{0,4},{4,0},{8,12},{12,8},{16,20},{20,16},{24,28},{28,24},{1,5},{5... | collective-permute-start | bytes 589832 | tf_op jit(solution)/shard_map/ppermute | solution.py:28
  30.2 11.6 %collective-permute-start.25 = (f32[384,128]{1,0:T(8,128)S(1)}, f32[384,128]{1,0:T(8,128)S(1)}, u32[]{:S(2)}, u32[]{:S(2)}) collective-permute-start(f32[384,128]{1,0:T(8,128)S(1)} %add.68), channel_id=1, source_target_pairs={{0,2},{1,3},{2,0},{3,1},{4,6},{5,7},{6,4},{7,5},{8,10},{9,11},{10,... | collective-permute-start | bytes 589832 | tf_op jit(solution)/shard_map/ppermute | solution.py:28
  35.0 5.0 %collective-permute-start.12 = (f32[256,128]{1,0:T(8,128)S(1)}, f32[256,128]{1,0:T(8,128)S(1)}, u32[]{:S(2)}, u32[]{:S(2)}) collective-permute-start(f32[256,128]{1,0:T(8,128)S(1)} %get-tuple-element.42.refs_0_), channel_id=1, source_target_pairs={{0,4},{4,0},{8,12},{12,8},{16,20},{20,16},{24,28},{28,24},{1,5},{5... | collective-permute-start | bytes 393224 | tf_op jit(solution)/shard_map/ppermute | solution.py:28
  36.6 5.2 %collective-permute-start.23 = (f32[256,128]{1,0:T(8,128)S(1)}, f32[256,128]{1,0:T(8,128)S(1)}, u32[]{:S(2)}, u32[]{:S(2)}) collective-permute-start(f32[256,128]{1,0:T(8,128)S(1)} %slice.17), channel_id=1, source_target_pairs={{0,1},{1,0},{2,3},{3,2},{4,5},{5,4},{6,7},{7,6},{8,9},{9,8},{10,11... | collective-permute-start | bytes 393224 | tf_op jit(solution)/shard_map/ppermute | solution.py:28
  37.9 7.8 %collective-permute-start.20 = (f32[384,128]{1,0:T(8,128)S(1)}, f32[384,128]{1,0:T(8,128)S(1)}, u32[]{:S(2)}, u32[]{:S(2)}) collective-permute-start(f32[384,128]{1,0:T(8,128)S(1)} %get-tuple-element.47.refs_0_), channel_id=1, source_target_pairs={{0,4},{4,0},{8,12},{12,8},{16,20},{20,16},{24,28},{28,24},{1,5},{5... | collective-permute-start | bytes 589832 | tf_op jit(solution)/shard_map/ppermute | solution.py:28
  40.1 5.0 %collective-permute-start.13 = (f32[256,128]{1,0:T(8,128)S(1)}, f32[256,128]{1,0:T(8,128)S(1)}, u32[]{:S(2)}, u32[]{:S(2)}) collective-permute-start(f32[256,128]{1,0:T(8,128)S(1)} %add.63.own_ref), channel_id=1, source_target_pairs={{0,8},{4,12},{8,0},{12,4},{16,24},{20,28},{24,16},{28,20},{1,9},{5... | collective-permute-start | bytes 393224 | tf_op jit(solution)/shard_map/ppermute | solution.py:28
  42.2 7.2 %collective-permute-start.26 = (f32[384,128]{1,0:T(8,128)S(1)}, f32[384,128]{1,0:T(8,128)S(1)}, u32[]{:S(2)}, u32[]{:S(2)}) collective-permute-start(f32[384,128]{1,0:T(8,128)S(1)} %shard_map.44), channel_id=1, source_target_pairs={{0,4},{4,0},{8,12},{12,8},{16,20},{20,16},{24,28},{28,24},{1,5},{5... | collective-permute-start | bytes 589832 | tf_op jit(solution)/shard_map/ppermute | solution.py:28
  43.7 5.6 %collective-permute-start.14 = (f32[256,128]{1,0:T(8,128)S(1)}, f32[256,128]{1,0:T(8,128)S(1)}, u32[]{:S(2)}, u32[]{:S(2)}) collective-permute-start(f32[256,128]{1,0:T(8,128)S(1)} %add.63.own_ref), channel_id=1, source_target_pairs={{0,1},{1,0},{2,3},{3,2},{4,5},{5,4},{6,7},{7,6},{8,9},{9,8},{10,11... | collective-permute-start | bytes 393224 | tf_op jit(solution)/shard_map/ppermute | solution.py:28
  45.1 4.3 %collective-permute-start.15 = (f32[256,128]{1,0:T(8,128)S(1)}, f32[256,128]{1,0:T(8,128)S(1)}, u32[]{:S(2)}, u32[]{:S(2)}) collective-permute-start(f32[256,128]{1,0:T(8,128)S(1)} %collective-permute-done.13.sib_ref), channel_id=1, source_target_pairs={{0,1},{1,0},{2,3},{3,2},{4,5},{5,4},{6,7},{7,6},{8,9},{9,8},{10,11... | collective-permute-start | bytes 393224 | tf_op jit(solution)/shard_map/ppermute | solution.py:28
  45.7 6.8 %collective-permute-start.21 = (f32[384,128]{1,0:T(8,128)S(1)}, f32[384,128]{1,0:T(8,128)S(1)}, u32[]{:S(2)}, u32[]{:S(2)}) collective-permute-start(f32[384,128]{1,0:T(8,128)S(1)} %add.67.own_ref), channel_id=1, source_target_pairs={{0,8},{4,12},{8,0},{12,4},{16,24},{20,28},{24,16},{28,20},{1,9},{5... | collective-permute-start | bytes 589832 | tf_op jit(solution)/shard_map/ppermute | solution.py:28
  47.4 4.5 %collective-permute-start.22 = (f32[256,128]{1,0:T(8,128)S(1)}, f32[256,128]{1,0:T(8,128)S(1)}, u32[]{:S(2)}, u32[]{:S(2)}) collective-permute-start(f32[256,128]{1,0:T(8,128)S(1)} %slice.16), channel_id=1, source_target_pairs={{0,1},{1,0},{2,3},{3,2},{4,5},{5,4},{6,7},{7,6},{8,9},{9,8},{10,11... | collective-permute-start | bytes 393224 | tf_op jit(solution)/shard_map/ppermute | solution.py:28
  53.6 5.0 %collective-permute-start.27 = (f32[256,128]{1,0:T(8,128)S(1)}, f32[256,128]{1,0:T(8,128)S(1)}, u32[]{:S(2)}, u32[]{:S(2)}) collective-permute-start(f32[256,128]{1,0:T(8,128)S(1)} %slice.14), channel_id=1, source_target_pairs={{0,8},{4,12},{8,0},{12,4},{16,24},{20,28},{24,16},{28,20},{1,9},{5... | collective-permute-start | bytes 393224 | tf_op jit(solution)/shard_map/ppermute | solution.py:28
  55.2 8.1 %collective-permute-start.37 = (f32[256,128]{1,0:T(8,128)S(1)}, f32[256,128]{1,0:T(8,128)S(1)}, u32[]{:S(2)}, u32[]{:S(2)}) collective-permute-start(f32[256,128]{1,0:T(8,128)S(1)} %get-tuple-element.55.z01_ref), channel_id=1, source_target_pairs={{0,1},{1,0},{2,3},{3,2},{4,5},{5,4},{6,7},{7,6},{8,9},{9,8},{10,11... | collective-permute-start | bytes 393224 | tf_op jit(solution)/shard_map/ppermute | solution.py:28
  55.2 13.4 %collective-permute-start.36 = (f32[384,128]{1,0:T(8,128)S(1)}, f32[384,128]{1,0:T(8,128)S(1)}, u32[]{:S(2)}, u32[]{:S(2)}) collective-permute-start(f32[384,128]{1,0:T(8,128)S(1)} %get-tuple-element.48.z_ref.z0_ref), channel_id=1, source_target_pairs={{0,1},{1,0},{2,3},{3,2},{4,5},{5,4},{6,7},{7,6},{8,9},{9,8},{10,11... | collective-permute-start | bytes 589832 | tf_op jit(solution)/shard_map/ppermute | solution.py:28
  55.7 13.5 %collective-permute-start.35 = (f32[384,128]{1,0:T(8,128)S(1)}, f32[384,128]{1,0:T(8,128)S(1)}, u32[]{:S(2)}, u32[]{:S(2)}) collective-permute-start(f32[384,128]{1,0:T(8,128)S(1)} %get-tuple-element.54.z1_ref), channel_id=1, source_target_pairs={{0,1},{1,0},{2,3},{3,2},{4,5},{5,4},{6,7},{7,6},{8,9},{9,8},{10,11... | collective-permute-start | bytes 589832 | tf_op jit(solution)/shard_map/ppermute | solution.py:28
  55.8 5.8 %collective-permute-start.31 = (f32[128,128]{1,0:T(8,128)S(1)}, f32[128,128]{1,0:T(8,128)S(1)}, u32[]{:S(2)}, u32[]{:S(2)}) collective-permute-start(f32[128,128]{1,0:T(8,128)S(1)} %slice.15), channel_id=1, source_target_pairs={{0,8},{4,12},{8,0},{12,4},{16,24},{20,28},{24,16},{28,20},{1,9},{5... | collective-permute-start | bytes 196616 | tf_op jit(solution)/shard_map/ppermute | solution.py:28
  58.6 10.0 %collective-permute-start.28 = (f32[256,128]{1,0:T(8,128)S(1)}, f32[256,128]{1,0:T(8,128)S(1)}, u32[]{:S(2)}, u32[]{:S(2)}) collective-permute-start(f32[256,128]{1,0:T(8,128)S(1)} %slice_add_fusion.1.own_ref), channel_id=1, source_target_pairs={{0,16},{4,20},{8,24},{12,28},{16,0},{20,4},{24,8},{28,12},{1,17},{... | collective-permute-start | bytes 393224 | tf_op jit(solution)/shard_map/ppermute | solution.py:28
  61.7 7.6 %collective-permute-start.33 = (f32[128,128]{1,0:T(8,128)S(1)}, f32[128,128]{1,0:T(8,128)S(1)}, u32[]{:S(2)}, u32[]{:S(2)}) collective-permute-start(f32[128,128]{1,0:T(8,128)S(1)} %slice_add_fusion.own_ref), channel_id=1, source_target_pairs={{0,16},{4,20},{8,24},{12,28},{16,0},{20,4},{24,8},{28,12},{1,17},{... | collective-permute-start | bytes 196616 | tf_op jit(solution)/shard_map/ppermute | solution.py:28
  63.4 11.1 %collective-permute-start.29 = (f32[256,128]{1,0:T(8,128)S(1)}, f32[256,128]{1,0:T(8,128)S(1)}, u32[]{:S(2)}, u32[]{:S(2)}) collective-permute-start(f32[256,128]{1,0:T(8,128)S(1)} %slice_add_fusion.1.own_ref), channel_id=1, source_target_pairs={{0,1},{1,0},{2,3},{3,2},{4,5},{5,4},{6,7},{7,6},{8,9},{9,8},{10,11... | collective-permute-start | bytes 393224 | tf_op jit(solution)/shard_map/ppermute | solution.py:28
  68.6 5.9 %collective-permute-start.30 = (f32[256,128]{1,0:T(8,128)S(1)}, f32[256,128]{1,0:T(8,128)S(1)}, u32[]{:S(2)}, u32[]{:S(2)}) collective-permute-start(f32[256,128]{1,0:T(8,128)S(1)} %collective-permute-done.28.sib_ref), channel_id=1, source_target_pairs={{0,1},{1,0},{2,3},{3,2},{4,5},{5,4},{6,7},{7,6},{8,9},{9,8},{10,11... | collective-permute-start | bytes 393224 | tf_op jit(solution)/shard_map/ppermute | solution.py:28
  68.6 8.2 %collective-permute-start.32 = (f32[128,128]{1,0:T(8,128)S(1)}, f32[128,128]{1,0:T(8,128)S(1)}, u32[]{:S(2)}, u32[]{:S(2)}) collective-permute-start(f32[128,128]{1,0:T(8,128)S(1)} %slice_add_fusion.own_ref), channel_id=1, source_target_pairs={{0,1},{1,0},{2,3},{3,2},{4,5},{5,4},{6,7},{7,6},{8,9},{9,8},{10,11... | collective-permute-start | bytes 196616 | tf_op jit(solution)/shard_map/ppermute | solution.py:28
  69.3 7.5 %collective-permute-start.34 = (f32[128,128]{1,0:T(8,128)S(1)}, f32[128,128]{1,0:T(8,128)S(1)}, u32[]{:S(2)}, u32[]{:S(2)}) collective-permute-start(f32[128,128]{1,0:T(8,128)S(1)} %collective-permute-done.33.sib_ref), channel_id=1, source_target_pairs={{0,1},{1,0},{2,3},{3,2},{4,5},{5,4},{6,7},{7,6},{8,9},{9,8},{10,11... | collective-permute-start | bytes 196616 | tf_op jit(solution)/shard_map/ppermute | solution.py:28
  74.5 2.3 %copy-start.1 = (bf16[1024,256]{1,0:T(8,128)(2,1)S(1)}, bf16[1024,256]{1,0:T(8,128)(2,1)}, u32[]{:S(2)}) copy-start(bf16[1024,256]{1,0:T(8,128)(2,1)} %get-tuple-element.57.low_ref) | copy-start | bytes 1572868
  74.5 2.3 %copy-start.2 = (f32[1024,128]{1,0:T(8,128)S(1)}, f32[1024,128]{1,0:T(8,128)}, u32[]{:S(2)}) copy-start(f32[1024,128]{1,0:T(8,128)} %get-tuple-element.58.rhs_ref) | copy-start | bytes 1572868

commit v4 on v3

--- a/solution.py
+++ b/solution.py
@@ -43,10 +43,9 @@
 
 
 def dot_parts(left, right):
-    def part(first, second):
-        return lax.dot_general(first, second, (((1,), (0,)), ((), ())), preferred_element_type=jnp.float32)
-
-    return part(left[0], right[0]) + (part(left[0], right[1]) + part(left[1], right[0]))
+    first = jnp.concatenate([left[0], left[0], left[1]], axis=1)
+    second = jnp.concatenate([right[0], right[1], right[0]], axis=0)
+    return lax.dot_general(first, second, (((1,), (0,)), ((), ())), preferred_element_type=jnp.float32)
 
 
 def dot(left, right):
@@ -87,10 +86,11 @@
         start += unit.shape[0]
 
 
-def product_kernel(groups, core_ref, gens_ref, solved_ref, rhs_ref, *refs):
+def product_kernel(groups, core_ref, gens_ref, solved_ref, *refs):
     gens, solved, rhs, total, sems = refs[-5:]
     outs = refs[-5 - 2 * len(groups) : -5]
     pairs, lefts, rights = needed(groups)
+    rhs_ref = refs[0] if 3 in rights else None
     chunks = sems.shape[1]
     block = gens.shape[1] // chunks
     copies = []
@@ -163,9 +163,10 @@
     pairs, lefts, rights = needed(groups)
     width = sum(width_of(right) for _, right in pairs)
     outs = [struct(sum(HALF if right == 3 else RANK for _, right in group)) for group in groups for _ in range(2)]
+    given = (generators, solved_gens, rhs) if 3 in rights else (generators, solved_gens)
     return pl.pallas_call(
         functools.partial(product_kernel, groups),
-        in_specs=[SMEM, HBM, HBM, HBM] + [ANY] * len(after),
+        in_specs=[SMEM] + [HBM] * len(given) + [ANY] * len(after),
         out_specs=[VMEM] * len(outs),
         out_shape=outs,
         scratch_shapes=[
@@ -177,7 +178,7 @@
         ],
         compiler_params=pltpu.CompilerParams(vmem_limit_bytes=STREAM_LIMIT),
         cost_estimate=cost(6 * rows * RANK * width, rows * (len(lefts) + len(rights)) * RANK),
-    )(core, generators, solved_gens, rhs, *after)
+    )(core, *given, *after)
 
 
 def square_norm(value):
@@ -214,8 +215,8 @@
 
 def invert_kernel(core_ref, own_ref, sib_ref, own_other_ref, sib_other_ref, inverse_ref, p_sib_ref, power):
     core = core_ref[0]
-    p_own = in_order(core, own_ref[...], own_other_ref[...])
-    p_sib = in_order(core, sib_ref[...], sib_other_ref[...])
+    p_own = in_order(core, own_ref[:RANK, :], own_other_ref[:RANK, :])
+    p_sib = in_order(core, sib_ref[:RANK, :], sib_other_ref[:RANK, :])
     p_sib_ref[...] = p_sib
     product = dot(p_sib, p_own)
     bound = series(product, 1.0, power, inverse_ref)
@@ -252,18 +253,18 @@
 
 
 def head_kernel(core_ref, inverse_ref, p_sib_ref, own_ref, sib_ref, own_other_ref, next_ref, z_ref, out_ref):
-    own = own_ref[...]
-    z = dot(inverse_ref[...], sib_ref[...] - dot(p_sib_ref[...], own))
+    own = own_ref[RANK:, :]
+    z = dot(inverse_ref[...], sib_ref[RANK:, :] - dot(p_sib_ref[...], own))
     z_ref[...] = z
-    out_ref[...] = next_ref[...] - dot_turned(in_order(core_ref[0], own, own_other_ref[...]), z)
+    out_ref[...] = next_ref[:RANK, :] - dot_turned(in_order(core_ref[0], own, own_other_ref[RANK:, :]), z)
 
 
 def tail_kernel(core_ref, inverse_ref, p_sib_ref, own_ref, sib_ref, head_ref, head_other_ref, next_ref, *refs):
     z_ref, out_ref = refs[-2:]
     z = dot(inverse_ref[...], unpack(sib_ref) - dot(p_sib_ref[...], unpack(own_ref)))
     store(z_ref, z)
-    crossed = in_order(core_ref[0], head_ref[...], head_other_ref[...])
-    store(out_ref, unpack(next_ref) - dot_turned(crossed, z))
+    crossed = in_order(core_ref[0], head_ref[RANK:, :], head_other_ref[RANK:, :])
+    store(out_ref, unpack(next_ref.at[RANK:]) - dot_turned(crossed, z))
 
 
 def third_kernel(core_ref, own_ref, own_other_ref, z_ref, next_ref, *refs):
@@ -288,9 +289,9 @@
 
 
 def reduced_kernel(
-    core_ref, z1_ref, z1_other_ref, z0_ref, z0_other_ref, z01_ref, z01_other_ref, solved_ref, rhs_ref,
-    high_ref, low_ref, out_ref, solved, rhs, sems,
+    core_ref, z1_ref, z1_other_ref, z0_ref, z0_other_ref, z01_ref, z01_other_ref, solved_ref, rhs_ref, *refs
 ):
+    high_ref, low_ref, out_ref, solved, rhs, sems = refs[-6:]
     core = core_ref[0]
     copies = [
         pltpu.make_async_copy(solved_ref, solved, sems.at[0]),
@@ -320,12 +321,12 @@
         out_ref[rows, :] = rhs[rows, :] - value[:, RANK:]
 
 
-def reduced(core, small, solved_gens, rhs):
+def reduced(core, small, solved_gens, rhs, *after):
     rows = rhs.shape[0]
     part = jax.ShapeDtypeStruct((rows, RANK), jnp.bfloat16)
     return pl.pallas_call(
         reduced_kernel,
-        in_specs=[SMEM] + [VMEM] * len(small) + [HBM, HBM],
+        in_specs=[SMEM] + [VMEM] * len(small) + [HBM, HBM] + [ANY] * len(after),
         out_specs=[VMEM] * 3,
         out_shape=[part, part, struct(rows, RHS)],
         scratch_shapes=[
@@ -335,7 +336,11 @@
         ],
         compiler_params=pltpu.CompilerParams(vmem_limit_bytes=STREAM_LIMIT),
         cost_estimate=cost(6 * rows * 2 * RANK * (RANK + RHS), rows * 5 * RANK),
-    )(core, *small, solved_gens, rhs)
+    )(core, *small, solved_gens, rhs, *after)
+
+
+def keep_kernel(core_ref, value_ref, *refs):
+    refs[-1][...] = value_ref[...]
 
 
 def final_kernel(
@@ -357,7 +362,7 @@
 
     def partial_products(groups, *after):
         values = products(core, generators, solved_gens, rhs, groups, after)
-        return [keep + swap(send, "sub", 0) for keep, send in zip(values[::2], values[1::2])], values[-1]
+        return [keep + swap(send, "sub", 0) for keep, send in zip(values[::2], values[1::2])]
 
     def over_child(value):
         for bit in range(1, sub_bits):
@@ -366,25 +371,25 @@
             value = value + swap(value, "rows", bit)
         return value
 
-    (p_own, r_own), sent = partial_products((((0, 0),), ((0, 1),)))
-    (tail,), _ = partial_products((((0, 2), (0, 3)),), sent)
-    (near, far, third), _ = partial_products((((1, 1),), ((1, 2), (1, 3)), ((2, 2), (2, 3))), tail)
-    p_own, r_own, tail, near, far, third = map(over_child, (p_own, r_own, tail, near, far, third))
-
-    p_sib = swap(p_own, "rows", span_bits)
-    r_sib = swap(r_own, "rows", span_bits)
+    (head,) = partial_products((((0, 0), (0, 1)),))
+    (tail,) = partial_products((((0, 2), (0, 3)),), head)
+    (near,) = partial_products((((1, 1), (1, 2), (1, 3)),), tail)
+    head, tail = over_child(head), over_child(tail)
+    (third,) = partial_products((((2, 2), (2, 3)),), tail)
+    near, third = over_child(near), over_child(third)
+
+    head_sib = swap(head, "rows", span_bits)
     tail_sib = swap(tail, "rows", span_bits)
-    p_own_other = swap(p_own, "sub", 0)
-    r_own_other = swap(r_own, "sub", 0)
+    head_other = swap(head, "sub", 0)
     tail_other = swap(tail[:RANK], "sub", 0)
-    p_sib_other = swap(p_sib, "sub", 0)
-    inverted, p_sib = inverse(core, p_own, p_sib, p_own_other, p_sib_other)
+    p_sib_other = swap(head_sib[:RANK], "sub", 0)
+    inverted, p_sib = inverse(core, head, head_sib, head_other, p_sib_other)
     z01, p_own = call(
-        head_kernel, [struct(RANK)] * 2, 3 * flops, core, inverted, p_sib, r_own, r_sib, r_own_other, near
+        head_kernel, [struct(RANK)] * 2, 3 * flops, core, inverted, p_sib, head, head_sib, head_other, near
     )
     z0, r_own = call(
         tail_kernel, [struct(RANK + HALF)] * 2, 5 * flops,
-        core, inverted, p_sib, tail, tail_sib, r_own, r_own_other, far, after=(p_own,),
+        core, inverted, p_sib, tail, tail_sib, head, head_other, near, after=(p_own,),
     )
     third = call(third_kernel, struct(RANK + HALF), 2 * flops, core, tail, tail_other, z0, third, after=(r_own,))
 
@@ -404,13 +409,14 @@
 
     p_own, r_own = own[:RANK], own[RANK:]
     p_own = p_own + swap(p_own, "rows", span_bits + 1)
+    p_sib = swap(p_own, "rows", span_bits + 2)
     r_own = r_own + swap(r_own, "rows", span_bits + 1)
-    p_sib = swap(p_own, "rows", span_bits + 2)
     r_sib = swap(r_own, "rows", span_bits + 2)
+    small = (z1, swap(z1, "sub", 0), z0, swap(z0, "sub", 0), z01, swap(z01, "sub", 0))
+    high, low, current = reduced(core, small, solved_gens, rhs, r_own)
+    p_sib = call(keep_kernel, struct(RANK), 0, core, p_sib, after=(high,))
     p_own_other = swap(p_own, "sub", 0)
     r_own_other = swap(r_own, "sub", 0)
-    small = (z1, swap(z1, "sub", 0), z0, swap(z0, "sub", 0), z01, swap(z01, "sub", 0))
-    high, low, current = reduced(core, small, solved_gens, rhs)
     p_sib_other = swap(p_sib, "sub", 0)
     r_sib_other = swap(r_sib, "sub", 0)
     inverted, p_sib = inverse(core, p_own, p_sib, p_own_other, p_sib_other)

time: 79.1 us -> 76.2 us (0.963)
  the two profiles are of different devices: /device:TPU:0 before, /device:TPU:7 now
where the time goes in v4:
time: 76.2 us; the launch traced here: 76 us
  starting transfers between devices  33.3 us (44%)
  Pallas kernels  29 us (38%)
  waiting for transfers between devices  13.1 us (17%)
    ppermute x32, starting transfers between devices, swap(): return lax.ppermute(value, axis, pairs)  33.3 us
    ppermute x32, waiting for transfers between devices, swap(): return lax.ppermute(value, axis, pairs)  13.1 us
    pallas_call x4, Pallas kernels, products(): pl.pallas_call(functools.partial(product_kernel, groups), in_specs=[SMEM]...  11.7 us
    pallas_call x3, Pallas kernels, inverse(): pl.pallas_call(invert_kernel, in_specs=[SMEM] + [VMEM] * 4, out_specs=[VM...  6.83 us
    pallas_call x6, Pallas kernels, call(): pl.pallas_call(kernel, in_specs=[SMEM] + [VMEM] * (len(values) - 1) + [AN...  5.29 us
    pallas_call x1, Pallas kernels, reduced(): pl.pallas_call(reduced_kernel, in_specs=[SMEM] + [VMEM] * len(small) + [H...  5.14 us
  transfers between devices with their start and end apart: 32, of which 8 were waited for; matrix products, arithmetic and copies ran while one was open for 0% of the time, Pallas kernels for 27%

profile of v4, /device:TPU:7, one launch (start us, length us, event | category | flops | bytes accessed | tf_op | source)
XLA Modules:
  0.0 76.0 jit_solution(10956263075187922145)
XLA Ops:
  0.0 2.6 %shard_map.37 = (f32[512,128]{1,0:T(8,128)S(1)}, f32[512,128]{1,0:T(8,128)S(1)}) custom-call(s32[1]{0:T(128)} %bitcast.core_ref, f32[3,1024,256]{2,1,0:T(8,128)} %gens_ref.7, f32[3,1024,256]{2,1,0:T(8,128)} %solved_ref.9), custom_call_target="tpu_custom_call" | custom-call | flops 805306368 | bytes 3145728 | tf_op jit(solution)/shard_map/pallas_call | solution.py:167
  2.6 0.7 collective-permute-start
  3.3 1.2 %collective-permute-done = f32[512,128]{1,0:T(8,128)S(1)} collective-permute-done((f32[512,128]{1,0:T(8,128)S(1)}, f32[512,128]{1,0:T(8,128)S(1)}, u32[]{:S(2)}, u32[]{:S(2)}) %collective-permute-start) | collective-permute-done | bytes 262176 | tf_op jit(solution)/shard_map/ppermute | solution.py:28
  4.5 2.8 %shard_map.39 = (f32[384,128]{1,0:T(8,128)S(1)}, f32[384,128]{1,0:T(8,128)S(1)}) custom-call(s32[1]{0:T(128)} %bitcast.core_ref, f32[3,1024,256]{2,1,0:T(8,128)} %gens_ref.7, f32[3,1024,256]{2,1,0:T(8,128)} %solved_ref.9, f32[1024,128]{1,0:T(8,128)S(1)} %copy-done, f32[512,128]{1,0:T(8,128)S(1)} %add.44.refs_1_), custom_call_target="tpu_custom_call" | custom-call | flops 603979776 | bytes 3145728 | tf_op jit(solution)/shard_map/pallas_call | solution.py:167
  7.3 0.4 collective-permute-start.5
  7.8 0.2 collective-permute-start.1
  8.0 0.9 %collective-permute-done.5 = f32[384,128]{1,0:T(8,128)S(1)} collective-permute-done((f32[384,128]{1,0:T(8,128)S(1)}, f32[384,128]{1,0:T(8,128)S(1)}, u32[]{:S(2)}, u32[]{:S(2)}) %collective-permute-start.5) | collective-permute-done | bytes 196640 | tf_op jit(solution)/shard_map/ppermute | solution.py:28
  8.9 3.5 %shard_map.40 = (f32[640,128]{1,0:T(8,128)S(1)}, f32[640,128]{1,0:T(8,128)S(1)}) custom-call(s32[1]{0:T(128)} %bitcast.core_ref, f32[3,1024,256]{2,1,0:T(8,128)} %gens_ref.7, f32[3,1024,256]{2,1,0:T(8,128)} %solved_ref.9, f32[1024,128]{1,0:T(8,128)S(1)} %copy-done, f32[384,128]{1,0:T(8,128)S(1)} %add.46.refs_1_), custom_call_target="tpu_custom_call" | custom-call | flops 1006632960 | bytes 4194304 | tf_op jit(solution)/shard_map/pallas_call | solution.py:167
  12.4 0.4 collective-permute-start.6
  12.9 0.5 collective-permute-start.12
  13.3 2.2 %collective-permute-done.1 = f32[512,128]{1,0:T(8,128)S(1)} collective-permute-done((f32[512,128]{1,0:T(8,128)S(1)}, f32[512,128]{1,0:T(8,128)S(1)}, u32[]{:S(2)}, u32[]{:S(2)}) %collective-permute-start.1) | collective-permute-done | bytes 262176 | tf_op jit(solution)/shard_map/ppermute | solution.py:28
  15.6 0.3 collective-permute-start.2
  15.9 1.7 %collective-permute-start.3 = (f32[512,128]{1,0:T(8,128)S(1)}, f32[512,128]{1,0:T(8,128)S(1)}, u32[]{:S(2)}, u32[]{:S(2)}) collective-permute-start(f32[512,128]{1,0:T(8,128)S(1)} %add.45.own_ref.head_ref), channel_id=1, source_target_pairs={{0,1},{1,0},{2,3},{3,2},{4,5},{5,4},{6,7},{7,6},{8,9},{9,8},{10,11... | collective-permute-start | bytes 786440 | tf_op jit(solution)/shard_map/ppermute | solution.py:28
  17.6 2.3 %collective-permute-done.12 = f32[384,128]{1,0:T(8,128)S(1)} collective-permute-done((f32[384,128]{1,0:T(8,128)S(1)}, f32[384,128]{1,0:T(8,128)S(1)}, u32[]{:S(2)}, u32[]{:S(2)}) %collective-permute-start.12) | collective-permute-done | bytes 196640 | tf_op jit(solution)/shard_map/ppermute | solution.py:28
  19.9 0.5 collective-permute-start.7
  20.4 2.8 %shard_map.44 = (f32[384,128]{1,0:T(8,128)S(1)}, f32[384,128]{1,0:T(8,128)S(1)}) custom-call(s32[1]{0:T(128)} %bitcast.core_ref, f32[3,1024,256]{2,1,0:T(8,128)} %gens_ref.7, f32[3,1024,256]{2,1,0:T(8,128)} %solved_ref.9, f32[1024,128]{1,0:T(8,128)S(1)} %copy-done, f32[384,128]{1,0:T(8,128)S(1)} %add.50.own_ref.refs_1_), custom_call_target="tpu_custom_call" | custom-call | flops 603979776 | bytes 3145728 | tf_op jit(solution)/shard_map/pallas_call | solution.py:167
  23.2 1.0 %collective-permute-start.18 = (f32[384,128]{1,0:T(8,128)S(1)}, f32[384,128]{1,0:T(8,128)S(1)}, u32[]{:S(2)}, u32[]{:S(2)}) collective-permute-start(f32[384,128]{1,0:T(8,128)S(1)} %get-tuple-element.42), channel_id=1, source_target_pairs={{0,1},{1,0},{2,3},{3,2},{4,5},{5,4},{6,7},{7,6},{8,9},{9,8},{10,11... | collective-permute-start | bytes 589832 | tf_op jit(solution)/shard_map/ppermute | solution.py:28
  24.2 0.2 collective-permute-start.4
  24.4 0.2 collective-permute-start.13
  24.7 0.6 collective-permute-done.18
  25.3 1.3 %collective-permute-start.19 = (f32[384,128]{1,0:T(8,128)S(1)}, f32[384,128]{1,0:T(8,128)S(1)}, u32[]{:S(2)}, u32[]{:S(2)}) collective-permute-start(f32[384,128]{1,0:T(8,128)S(1)} %add.52), channel_id=1, source_target_pairs={{0,2},{1,3},{2,0},{3,1},{4,6},{5,7},{6,4},{7,5},{8,10},{9,11},{10,... | collective-permute-start | bytes 589832 | tf_op jit(solution)/shard_map/ppermute | solution.py:28
  26.6 0.0 collective-permute-done.4.sib_other_ref
  26.6 2.2 %shard_map.38 = (f32[256,256]{1,0:T(8,128)S(1)}, f32[256,256]{1,0:T(8,128)S(1)}) custom-call(s32[1]{0:T(128)} %bitcast.core_ref, f32[512,128]{1,0:T(8,128)S(1)} %add.45.own_ref.head_ref, f32[512,128]{1,0:T(8,128)S(1)} %collective-permute-done.2.sib_ref, f32[512,128]{1,0:T(8,128)S(1)} %collective-permute-done.3.own_other_ref.head_other_ref, ...), custom_call_target="tpu_custom_call" | custom-call | flops 905969664 | bytes 1048576 | tf_op jit(solution)/shard_map/pallas_call | solution.py:244
  28.9 0.0 collective-permute-done.7
  28.9 0.8 %shard_map.41 = (f32[256,128]{1,0:T(8,128)S(1)}, f32[256,128]{1,0:T(8,128)S(1)}) custom-call(s32[1]{0:T(128)} %bitcast.core_ref, f32[256,256]{1,0:T(8,128)S(1)} %get-tuple-element.30.inverse_ref, f32[256,256]{1,0:T(8,128)S(1)} %get-tuple-element.31.p_sib_ref, f32[512,128]{1,0:T(8,128)S(1)} %add.45.own_ref.head_ref, ...), custom_call_target="tpu_custom_call" | custom-call | flops 150994944 | bytes 1900548 | tf_op jit(solution)/shard_map/pallas_call | solution.py:233
  29.7 0.6 collective-permute-start.8
  30.4 2.5 %collective-permute-start.17 = (f32[256,128]{1,0:T(8,128)S(1)}, f32[256,128]{1,0:T(8,128)S(1)}, u32[]{:S(2)}, u32[]{:S(2)}) collective-permute-start(f32[256,128]{1,0:T(8,128)S(1)} %slice.22), channel_id=1, source_target_pairs={{0,1},{1,0},{2,3},{3,2},{4,5},{5,4},{6,7},{7,6},{8,9},{9,8},{10,11... | collective-permute-start | bytes 393224 | tf_op jit(solution)/shard_map/ppermute | solution.py:28
  32.8 1.0 %shard_map.43 = (f32[384,128]{1,0:T(8,128)S(1)}, f32[384,128]{1,0:T(8,128)S(1)}) custom-call(s32[1]{0:T(128)} %bitcast.core_ref, f32[256,256]{1,0:T(8,128)S(1)} %get-tuple-element.30.inverse_ref, f32[256,256]{1,0:T(8,128)S(1)} %get-tuple-element.31.p_sib_ref, f32[384,128]{1,0:T(8,128)S(1)} %add.50.own_ref.refs_1_, ...), custom_call_target="tpu_custom_call" | custom-call | flops 251658240 | bytes 2162692 | tf_op jit(solution)/shard_map/pallas_call | solution.py:233
  33.9 1.5 %collective-permute-start.14 = (f32[384,128]{1,0:T(8,128)S(1)}, f32[384,128]{1,0:T(8,128)S(1)}, u32[]{:S(2)}, u32[]{:S(2)}) collective-permute-start(f32[384,128]{1,0:T(8,128)S(1)} %get-tuple-element.39.refs_0_), channel_id=1, source_target_pairs={{0,4},{4,0},{8,12},{12,8},{16,20},{20,16},{24,28},{28,24},{1,5},{5... | collective-permute-start | bytes 589832 | tf_op jit(solution)/shard_map/ppermute | solution.py:28
  35.3 0.0 collective-permute-done.8
  35.4 1.4 %collective-permute-start.9 = (f32[256,128]{1,0:T(8,128)S(1)}, f32[256,128]{1,0:T(8,128)S(1)}, u32[]{:S(2)}, u32[]{:S(2)}) collective-permute-start(f32[256,128]{1,0:T(8,128)S(1)} %add.49.own_ref), channel_id=1, source_target_pairs={{0,8},{4,12},{8,0},{12,4},{16,24},{20,28},{24,16},{28,20},{1,9},{5... | collective-permute-start | bytes 393224 | tf_op jit(solution)/shard_map/ppermute | solution.py:28
  36.7 0.0 collective-permute-done.19
  36.8 0.4 shard_map.45
  37.2 0.2 collective-permute-start.20
  37.3 2.6 %collective-permute-start.10 = (f32[256,128]{1,0:T(8,128)S(1)}, f32[256,128]{1,0:T(8,128)S(1)}, u32[]{:S(2)}, u32[]{:S(2)}) collective-permute-start(f32[256,128]{1,0:T(8,128)S(1)} %add.49.own_ref), channel_id=1, source_target_pairs={{0,1},{1,0},{2,3},{3,2},{4,5},{5,4},{6,7},{7,6},{8,9},{9,8},{10,11... | collective-permute-start | bytes 393224 | tf_op jit(solution)/shard_map/ppermute | solution.py:28
  39.9 2.8 %collective-permute-start.11 = (f32[256,128]{1,0:T(8,128)S(1)}, f32[256,128]{1,0:T(8,128)S(1)}, u32[]{:S(2)}, u32[]{:S(2)}) collective-permute-start(f32[256,128]{1,0:T(8,128)S(1)} %collective-permute-done.9.sib_ref), channel_id=1, source_target_pairs={{0,1},{1,0},{2,3},{3,2},{4,5},{5,4},{6,7},{7,6},{8,9},{9,8},{10,11... | collective-permute-start | bytes 393224 | tf_op jit(solution)/shard_map/ppermute | solution.py:28
  42.7 0.0 collective-permute-done.14
  42.7 1.3 %collective-permute-start.15 = (f32[384,128]{1,0:T(8,128)S(1)}, f32[384,128]{1,0:T(8,128)S(1)}, u32[]{:S(2)}, u32[]{:S(2)}) collective-permute-start(f32[384,128]{1,0:T(8,128)S(1)} %add.51.own_ref), channel_id=1, source_target_pairs={{0,8},{4,12},{8,0},{12,4},{16,24},{20,28},{24,16},{28,20},{1,9},{5... | collective-permute-start | bytes 589832 | tf_op jit(solution)/shard_map/ppermute | solution.py:28
  44.1 0.3 collective-permute-start.16
  44.4 0.0 collective-permute-done.20
  44.5 0.0 collective-permute-done.11.sib_other_ref
  44.5 2.4 %shard_map.42 = (f32[256,256]{1,0:T(8,128)S(1)}, f32[256,256]{1,0:T(8,128)S(1)}) custom-call(s32[1]{0:T(128)} %bitcast.core_ref, f32[256,128]{1,0:T(8,128)S(1)} %add.49.own_ref, f32[256,128]{1,0:T(8,128)S(1)} %collective-permute-done.9.sib_ref, f32[256,128]{1,0:T(8,128)S(1)} %collective-permute-done.10.own_other_ref, ...), custom_call_target="tpu_custom_call" | custom-call | flops 905969664 | bytes 1048576 | tf_op jit(solution)/shard_map/pallas_call | solution.py:244
  46.9 0.0 collective-permute-done.16.own_other_ref
  46.9 2.4 %collective-permute-done.15.sib_ref = f32[384,128]{1,0:T(8,128)S(1)} collective-permute-done((f32[384,128]{1,0:T(8,128)S(1)}, f32[384,128]{1,0:T(8,128)S(1)}, u32[]{:S(2)}, u32[]{:S(2)}) %collective-permute-start.15) | collective-permute-done | bytes 196640 | tf_op jit(solution)/shard_map/ppermute | solution.py:28
  49.3 1.0 %shard_map.46 = (f32[384,128]{1,0:T(8,128)S(1)}, f32[384,128]{1,0:T(8,128)S(1)}) custom-call(s32[1]{0:T(128)} %bitcast.core_ref, f32[256,256]{1,0:T(8,128)S(1)} %get-tuple-element.37.inverse_ref, f32[256,256]{1,0:T(8,128)S(1)} %get-tuple-element.38.p_sib_ref, f32[384,128]{1,0:T(8,128)S(1)} %add.51.own_ref, f32[384,128]{1,0:T(8,128)S(1)} %collective-permute-done.15.sib_ref, ...), custom_call_target="tpu_custom_call" | custom-call | flops 251658240 | bytes 1638404 | tf_op jit(solution)/shard_map/pallas_call | solution.py:233
  50.4 1.3 %collective-permute-start.21 = (f32[256,128]{1,0:T(8,128)S(1)}, f32[256,128]{1,0:T(8,128)S(1)}, u32[]{:S(2)}, u32[]{:S(2)}) collective-permute-start(f32[256,128]{1,0:T(8,128)S(1)} %slice.18), channel_id=1, source_target_pairs={{0,8},{4,12},{8,0},{12,4},{16,24},{20,28},{24,16},{28,20},{1,9},{5... | collective-permute-start | bytes 393224 | tf_op jit(solution)/shard_map/ppermute | solution.py:28
  51.7 1.1 %collective-permute-start.24 = (f32[384,128]{1,0:T(8,128)S(1)}, f32[384,128]{1,0:T(8,128)S(1)}, u32[]{:S(2)}, u32[]{:S(2)}) collective-permute-start(f32[384,128]{1,0:T(8,128)S(1)} %get-tuple-element.40.z_ref.z0_ref), channel_id=1, source_target_pairs={{0,1},{1,0},{2,3},{3,2},{4,5},{5,4},{6,7},{7,6},{8,9},{9,8},{10,11... | collective-permute-start | bytes 589832 | tf_op jit(solution)/shard_map/ppermute | solution.py:28
  52.8 0.3 collective-permute-start.26
  53.1 0.7 collective-permute-start.23
  53.8 0.9 %collective-permute-done.21 = f32[256,128]{1,0:T(8,128)S(1)} collective-permute-done((f32[256,128]{1,0:T(8,128)S(1)}, f32[256,128]{1,0:T(8,128)S(1)}, u32[]{:S(2)}, u32[]{:S(2)}) %collective-permute-start.21) | collective-permute-done | bytes 131104 | tf_op jit(solution)/shard_map/ppermute | solution.py:28
  54.7 2.3 %collective-permute-start.22 = (f32[256,128]{1,0:T(8,128)S(1)}, f32[256,128]{1,0:T(8,128)S(1)}, u32[]{:S(2)}, u32[]{:S(2)}) collective-permute-start(f32[256,128]{1,0:T(8,128)S(1)} %slice_add_fusion.1.own_ref), channel_id=1, source_target_pairs={{0,16},{4,20},{8,24},{12,28},{16,0},{20,4},{24,8},{28,12},{1,17},{... | collective-permute-start | bytes 393224 | tf_op jit(solution)/shard_map/ppermute | solution.py:28
  57.1 0.0 collective-permute-done.26
  57.1 2.3 %collective-permute-start.27 = (f32[256,128]{1,0:T(8,128)S(1)}, f32[256,128]{1,0:T(8,128)S(1)}, u32[]{:S(2)}, u32[]{:S(2)}) collective-permute-start(f32[256,128]{1,0:T(8,128)S(1)} %slice_add_fusion.1.own_ref), channel_id=1, source_target_pairs={{0,1},{1,0},{2,3},{3,2},{4,5},{5,4},{6,7},{7,6},{8,9},{9,8},{10,11... | collective-permute-start | bytes 393224 | tf_op jit(solution)/shard_map/ppermute | solution.py:28
  59.4 0.0 collective-permute-done.25.z01_other_ref
  59.4 5.1 %shard_map.47 = (bf16[1024,256]{1,0:T(8,128)(2,1)S(1)}, bf16[1024,256]{1,0:T(8,128)(2,1)}, f32[1024,128]{1,0:T(8,128)}) custom-call(s32[1]{0:T(128)} %bitcast.core_ref, f32[384,128]{1,0:T(8,128)S(1)} %get-tuple-element.44.z1_ref, f32[384,128]{1,0:T(8,128)S(1)} %collective-permute-done.23.z1_other_ref, f32[384,128]{1,0:T(8,128)S(1)} %get-tuple-element.40.z_ref.z0_ref, ...), custom_call_target="tpu_custom_call" | custom-call | flops 1207959552 | bytes 5242880 | tf_op jit(solution)/shard_map/pallas_call | solution.py:327
  64.6 0.0 copy-start.1
  64.6 0.0 collective-permute-done.22.value_ref
  64.6 0.1 collective-permute-start.28
  64.7 0.8 collective-permute-start.30
  65.5 0.7 collective-permute-start.29
  66.2 2.6 %collective-permute-done.30.sib_ref = f32[128,128]{1,0:T(8,128)S(1)} collective-permute-done((f32[128,128]{1,0:T(8,128)S(1)}, f32[128,128]{1,0:T(8,128)S(1)}, u32[]{:S(2)}, u32[]{:S(2)}) %collective-permute-start.30) | collective-permute-done | bytes 65568 | tf_op jit(solution)/shard_map/ppermute | solution.py:28
  68.8 3.0 %collective-permute-start.31 = (f32[128,128]{1,0:T(8,128)S(1)}, f32[128,128]{1,0:T(8,128)S(1)}, u32[]{:S(2)}, u32[]{:S(2)}) collective-permute-start(f32[128,128]{1,0:T(8,128)S(1)} %collective-permute-done.30.sib_ref), channel_id=1, source_target_pairs={{0,1},{1,0},{2,3},{3,2},{4,5},{5,4},{6,7},{7,6},{8,9},{9,8},{10,11... | collective-permute-start | bytes 196616 | tf_op jit(solution)/shard_map/ppermute | solution.py:28
  71.8 2.2 %shard_map.49 = (f32[256,256]{1,0:T(8,128)S(1)}, f32[256,256]{1,0:T(8,128)S(1)}) custom-call(s32[1]{0:T(128)} %bitcast.core_ref, f32[256,128]{1,0:T(8,128)S(1)} %slice_add_fusion.1.own_ref, f32[256,128]{1,0:T(8,128)S(1)} %shard_map.48.sib_ref, f32[256,128]{1,0:T(8,128)S(1)} %collective-permute-done.27.own_other_ref, ...), custom_call_target="tpu_custom_call" | custom-call | flops 905969664 | bytes 1048576 | tf_op jit(solution)/shard_map/pallas_call | solution.py:244
  74.0 2.0 %shard_map.50 = f32[1024,128]{1,0:T(8,128)} custom-call(s32[1]{0:T(128)} %bitcast.core_ref, f32[256,256]{1,0:T(8,128)S(1)} %get-tuple-element.47.inverse_ref, f32[256,256]{1,0:T(8,128)S(1)} %get-tuple-element.48.p_sib_ref, f32[128,128]{1,0:T(8,128)S(1)} %slice_add_fusion.refs_0_.own_ref, f32[128,128]{1,0:T(8,128)S(1)} %collective-permute-done.29.own_other_ref, ...), custom_call_target="tpu_custom_call" | custom-call | flops 201326592 | bytes 3932164 | tf_op jit(solution)/shard_map/pallas_call | solution.py:233
  (38 shorter events, 0.4 us)
Async XLA Ops:
  0.0 4.5 %copy-start = (f32[1024,128]{1,0:T(8,128)S(1)}, f32[1024,128]{1,0:T(8,128)}, u32[]{:S(2)}) copy-start(f32[1024,128]{1,0:T(8,128)} %rhs_ref.1) | copy-start | bytes 1572868
  2.6 1.9 %collective-permute-start = (f32[512,128]{1,0:T(8,128)S(1)}, f32[512,128]{1,0:T(8,128)S(1)}, u32[]{:S(2)}, u32[]{:S(2)}) collective-permute-start(f32[512,128]{1,0:T(8,128)S(1)} %get-tuple-element.29), channel_id=1, source_target_pairs={{0,1},{1,0},{2,3},{3,2},{4,5},{5,4},{6,7},{7,6},{8,9},{9,8},{10,11... | collective-permute-start | bytes 786440 | tf_op jit(solution)/shard_map/ppermute | solution.py:28
  7.3 1.5 %collective-permute-start.5 = (f32[384,128]{1,0:T(8,128)S(1)}, f32[384,128]{1,0:T(8,128)S(1)}, u32[]{:S(2)}, u32[]{:S(2)}) collective-permute-start(f32[384,128]{1,0:T(8,128)S(1)} %get-tuple-element.33), channel_id=1, source_target_pairs={{0,1},{1,0},{2,3},{3,2},{4,5},{5,4},{6,7},{7,6},{8,9},{9,8},{10,11... | collective-permute-start | bytes 589832 | tf_op jit(solution)/shard_map/ppermute | solution.py:28
  7.8 7.8 %collective-permute-start.1 = (f32[512,128]{1,0:T(8,128)S(1)}, f32[512,128]{1,0:T(8,128)S(1)}, u32[]{:S(2)}, u32[]{:S(2)}) collective-permute-start(f32[512,128]{1,0:T(8,128)S(1)} %add.44.refs_1_), channel_id=1, source_target_pairs={{0,2},{1,3},{2,0},{3,1},{4,6},{5,7},{6,4},{7,5},{8,10},{9,11},{10,... | collective-permute-start | bytes 786440 | tf_op jit(solution)/shard_map/ppermute | solution.py:28
  12.4 7.5 %collective-permute-start.6 = (f32[640,128]{1,0:T(8,128)S(1)}, f32[640,128]{1,0:T(8,128)S(1)}, u32[]{:S(2)}, u32[]{:S(2)}) collective-permute-start(f32[640,128]{1,0:T(8,128)S(1)} %get-tuple-element.35), channel_id=1, source_target_pairs={{0,1},{1,0},{2,3},{3,2},{4,5},{5,4},{6,7},{7,6},{8,9},{9,8},{10,11... | collective-permute-start | bytes 983048 | tf_op jit(solution)/shard_map/ppermute | solution.py:28
  12.9 7.0 %collective-permute-start.12 = (f32[384,128]{1,0:T(8,128)S(1)}, f32[384,128]{1,0:T(8,128)S(1)}, u32[]{:S(2)}, u32[]{:S(2)}) collective-permute-start(f32[384,128]{1,0:T(8,128)S(1)} %add.46.refs_1_), channel_id=1, source_target_pairs={{0,2},{1,3},{2,0},{3,1},{4,6},{5,7},{6,4},{7,5},{8,10},{9,11},{10,... | collective-permute-start | bytes 589832 | tf_op jit(solution)/shard_map/ppermute | solution.py:28
  15.6 8.7 %collective-permute-start.2 = (f32[512,128]{1,0:T(8,128)S(1)}, f32[512,128]{1,0:T(8,128)S(1)}, u32[]{:S(2)}, u32[]{:S(2)}) collective-permute-start(f32[512,128]{1,0:T(8,128)S(1)} %add.45.own_ref.head_ref), channel_id=1, source_target_pairs={{0,4},{4,0},{8,12},{12,8},{16,20},{20,16},{24,28},{28,24},{1,5},{5... | collective-permute-start | bytes 786440 | tf_op jit(solution)/shard_map/ppermute | solution.py:28
  15.9 10.8 %collective-permute-start.3 = (f32[512,128]{1,0:T(8,128)S(1)}, f32[512,128]{1,0:T(8,128)S(1)}, u32[]{:S(2)}, u32[]{:S(2)}) collective-permute-start(f32[512,128]{1,0:T(8,128)S(1)} %add.45.own_ref.head_ref), channel_id=1, source_target_pairs={{0,1},{1,0},{2,3},{3,2},{4,5},{5,4},{6,7},{7,6},{8,9},{9,8},{10,11... | collective-permute-start | bytes 786440 | tf_op jit(solution)/shard_map/ppermute | solution.py:28
  19.9 8.9 %collective-permute-start.7 = (f32[640,128]{1,0:T(8,128)S(1)}, f32[640,128]{1,0:T(8,128)S(1)}, u32[]{:S(2)}, u32[]{:S(2)}) collective-permute-start(f32[640,128]{1,0:T(8,128)S(1)} %add.47), channel_id=1, source_target_pairs={{0,2},{1,3},{2,0},{3,1},{4,6},{5,7},{6,4},{7,5},{8,10},{9,11},{10,... | collective-permute-start | bytes 983048 | tf_op jit(solution)/shard_map/ppermute | solution.py:28
  23.2 2.1 %collective-permute-start.18 = (f32[384,128]{1,0:T(8,128)S(1)}, f32[384,128]{1,0:T(8,128)S(1)}, u32[]{:S(2)}, u32[]{:S(2)}) collective-permute-start(f32[384,128]{1,0:T(8,128)S(1)} %get-tuple-element.42), channel_id=1, source_target_pairs={{0,1},{1,0},{2,3},{3,2},{4,5},{5,4},{6,7},{7,6},{8,9},{9,8},{10,11... | collective-permute-start | bytes 589832 | tf_op jit(solution)/shard_map/ppermute | solution.py:28
  24.2 2.4 %collective-permute-start.4 = (f32[256,128]{1,0:T(8,128)S(1)}, f32[256,128]{1,0:T(8,128)S(1)}, u32[]{:S(2)}, u32[]{:S(2)}) collective-permute-start(f32[256,128]{1,0:T(8,128)S(1)} %slice.20), channel_id=1, source_target_pairs={{0,1},{1,0},{2,3},{3,2},{4,5},{5,4},{6,7},{7,6},{8,9},{9,8},{10,11... | collective-permute-start | bytes 393224 | tf_op jit(solution)/shard_map/ppermute | solution.py:28
  24.4 8.4 %collective-permute-start.13 = (f32[384,128]{1,0:T(8,128)S(1)}, f32[384,128]{1,0:T(8,128)S(1)}, u32[]{:S(2)}, u32[]{:S(2)}) collective-permute-start(f32[384,128]{1,0:T(8,128)S(1)} %add.50.own_ref.refs_1_), channel_id=1, source_target_pairs={{0,4},{4,0},{8,12},{12,8},{16,20},{20,16},{24,28},{28,24},{1,5},{5... | collective-permute-start | bytes 589832 | tf_op jit(solution)/shard_map/ppermute | solution.py:28
  25.3 11.4 %collective-permute-start.19 = (f32[384,128]{1,0:T(8,128)S(1)}, f32[384,128]{1,0:T(8,128)S(1)}, u32[]{:S(2)}, u32[]{:S(2)}) collective-permute-start(f32[384,128]{1,0:T(8,128)S(1)} %add.52), channel_id=1, source_target_pairs={{0,2},{1,3},{2,0},{3,1},{4,6},{5,7},{6,4},{7,5},{8,10},{9,11},{10,... | collective-permute-start | bytes 589832 | tf_op jit(solution)/shard_map/ppermute | solution.py:28
  29.7 5.6 %collective-permute-start.8 = (f32[256,128]{1,0:T(8,128)S(1)}, f32[256,128]{1,0:T(8,128)S(1)}, u32[]{:S(2)}, u32[]{:S(2)}) collective-permute-start(f32[256,128]{1,0:T(8,128)S(1)} %get-tuple-element.36.refs_0_), channel_id=1, source_target_pairs={{0,4},{4,0},{8,12},{12,8},{16,20},{20,16},{24,28},{28,24},{1,5},{5... | collective-permute-start | bytes 393224 | tf_op jit(solution)/shard_map/ppermute | solution.py:28
  30.4 6.4 %collective-permute-start.17 = (f32[256,128]{1,0:T(8,128)S(1)}, f32[256,128]{1,0:T(8,128)S(1)}, u32[]{:S(2)}, u32[]{:S(2)}) collective-permute-start(f32[256,128]{1,0:T(8,128)S(1)} %slice.22), channel_id=1, source_target_pairs={{0,1},{1,0},{2,3},{3,2},{4,5},{5,4},{6,7},{7,6},{8,9},{9,8},{10,11... | collective-permute-start | bytes 393224 | tf_op jit(solution)/shard_map/ppermute | solution.py:28
  33.9 8.9 %collective-permute-start.14 = (f32[384,128]{1,0:T(8,128)S(1)}, f32[384,128]{1,0:T(8,128)S(1)}, u32[]{:S(2)}, u32[]{:S(2)}) collective-permute-start(f32[384,128]{1,0:T(8,128)S(1)} %get-tuple-element.39.refs_0_), channel_id=1, source_target_pairs={{0,4},{4,0},{8,12},{12,8},{16,20},{20,16},{24,28},{28,24},{1,5},{5... | collective-permute-start | bytes 589832 | tf_op jit(solution)/shard_map/ppermute | solution.py:28
  35.4 4.5 %collective-permute-start.9 = (f32[256,128]{1,0:T(8,128)S(1)}, f32[256,128]{1,0:T(8,128)S(1)}, u32[]{:S(2)}, u32[]{:S(2)}) collective-permute-start(f32[256,128]{1,0:T(8,128)S(1)} %add.49.own_ref), channel_id=1, source_target_pairs={{0,8},{4,12},{8,0},{12,4},{16,24},{20,28},{24,16},{28,20},{1,9},{5... | collective-permute-start | bytes 393224 | tf_op jit(solution)/shard_map/ppermute | solution.py:28
  37.2 7.3 %collective-permute-start.20 = (f32[384,128]{1,0:T(8,128)S(1)}, f32[384,128]{1,0:T(8,128)S(1)}, u32[]{:S(2)}, u32[]{:S(2)}) collective-permute-start(f32[384,128]{1,0:T(8,128)S(1)} %shard_map.45), channel_id=1, source_target_pairs={{0,4},{4,0},{8,12},{12,8},{16,20},{20,16},{24,28},{28,24},{1,5},{5... | collective-permute-start | bytes 589832 | tf_op jit(solution)/shard_map/ppermute | solution.py:28
  37.3 7.2 %collective-permute-start.10 = (f32[256,128]{1,0:T(8,128)S(1)}, f32[256,128]{1,0:T(8,128)S(1)}, u32[]{:S(2)}, u32[]{:S(2)}) collective-permute-start(f32[256,128]{1,0:T(8,128)S(1)} %add.49.own_ref), channel_id=1, source_target_pairs={{0,1},{1,0},{2,3},{3,2},{4,5},{5,4},{6,7},{7,6},{8,9},{9,8},{10,11... | collective-permute-start | bytes 393224 | tf_op jit(solution)/shard_map/ppermute | solution.py:28
  39.9 4.6 %collective-permute-start.11 = (f32[256,128]{1,0:T(8,128)S(1)}, f32[256,128]{1,0:T(8,128)S(1)}, u32[]{:S(2)}, u32[]{:S(2)}) collective-permute-start(f32[256,128]{1,0:T(8,128)S(1)} %collective-permute-done.9.sib_ref), channel_id=1, source_target_pairs={{0,1},{1,0},{2,3},{3,2},{4,5},{5,4},{6,7},{7,6},{8,9},{9,8},{10,11... | collective-permute-start | bytes 393224 | tf_op jit(solution)/shard_map/ppermute | solution.py:28
  42.7 6.6 %collective-permute-start.15 = (f32[384,128]{1,0:T(8,128)S(1)}, f32[384,128]{1,0:T(8,128)S(1)}, u32[]{:S(2)}, u32[]{:S(2)}) collective-permute-start(f32[384,128]{1,0:T(8,128)S(1)} %add.51.own_ref), channel_id=1, source_target_pairs={{0,8},{4,12},{8,0},{12,4},{16,24},{20,28},{24,16},{28,20},{1,9},{5... | collective-permute-start | bytes 589832 | tf_op jit(solution)/shard_map/ppermute | solution.py:28
  44.1 2.8 %collective-permute-start.16 = (f32[256,128]{1,0:T(8,128)S(1)}, f32[256,128]{1,0:T(8,128)S(1)}, u32[]{:S(2)}, u32[]{:S(2)}) collective-permute-start(f32[256,128]{1,0:T(8,128)S(1)} %slice.21), channel_id=1, source_target_pairs={{0,1},{1,0},{2,3},{3,2},{4,5},{5,4},{6,7},{7,6},{8,9},{9,8},{10,11... | collective-permute-start | bytes 393224 | tf_op jit(solution)/shard_map/ppermute | solution.py:28
  50.4 4.3 %collective-permute-start.21 = (f32[256,128]{1,0:T(8,128)S(1)}, f32[256,128]{1,0:T(8,128)S(1)}, u32[]{:S(2)}, u32[]{:S(2)}) collective-permute-start(f32[256,128]{1,0:T(8,128)S(1)} %slice.18), channel_id=1, source_target_pairs={{0,8},{4,12},{8,0},{12,4},{16,24},{20,28},{24,16},{28,20},{1,9},{5... | collective-permute-start | bytes 393224 | tf_op jit(solution)/shard_map/ppermute | solution.py:28
  51.7 7.7 %collective-permute-start.24 = (f32[384,128]{1,0:T(8,128)S(1)}, f32[384,128]{1,0:T(8,128)S(1)}, u32[]{:S(2)}, u32[]{:S(2)}) collective-permute-start(f32[384,128]{1,0:T(8,128)S(1)} %get-tuple-element.40.z_ref.z0_ref), channel_id=1, source_target_pairs={{0,1},{1,0},{2,3},{3,2},{4,5},{5,4},{6,7},{7,6},{8,9},{9,8},{10,11... | collective-permute-start | bytes 589832 | tf_op jit(solution)/shard_map/ppermute | solution.py:28
  52.8 6.6 %collective-permute-start.25 = (f32[256,128]{1,0:T(8,128)S(1)}, f32[256,128]{1,0:T(8,128)S(1)}, u32[]{:S(2)}, u32[]{:S(2)}) collective-permute-start(f32[256,128]{1,0:T(8,128)S(1)} %get-tuple-element.45.z01_ref), channel_id=1, source_target_pairs={{0,1},{1,0},{2,3},{3,2},{4,5},{5,4},{6,7},{7,6},{8,9},{9,8},{10,11... | collective-permute-start | bytes 393224 | tf_op jit(solution)/shard_map/ppermute | solution.py:28
  52.8 4.2 %collective-permute-start.26 = (f32[128,128]{1,0:T(8,128)S(1)}, f32[128,128]{1,0:T(8,128)S(1)}, u32[]{:S(2)}, u32[]{:S(2)}) collective-permute-start(f32[128,128]{1,0:T(8,128)S(1)} %slice.19), channel_id=1, source_target_pairs={{0,8},{4,12},{8,0},{12,4},{16,24},{20,28},{24,16},{28,20},{1,9},{5... | collective-permute-start | bytes 196616 | tf_op jit(solution)/shard_map/ppermute | solution.py:28
  53.1 6.3 %collective-permute-start.23 = (f32[384,128]{1,0:T(8,128)S(1)}, f32[384,128]{1,0:T(8,128)S(1)}, u32[]{:S(2)}, u32[]{:S(2)}) collective-permute-start(f32[384,128]{1,0:T(8,128)S(1)} %get-tuple-element.44.z1_ref), channel_id=1, source_target_pairs={{0,1},{1,0},{2,3},{3,2},{4,5},{5,4},{6,7},{7,6},{8,9},{9,8},{10,11... | collective-permute-start | bytes 589832 | tf_op jit(solution)/shard_map/ppermute | solution.py:28
  54.7 9.9 %collective-permute-start.22 = (f32[256,128]{1,0:T(8,128)S(1)}, f32[256,128]{1,0:T(8,128)S(1)}, u32[]{:S(2)}, u32[]{:S(2)}) collective-permute-start(f32[256,128]{1,0:T(8,128)S(1)} %slice_add_fusion.1.own_ref), channel_id=1, source_target_pairs={{0,16},{4,20},{8,24},{12,28},{16,0},{20,4},{24,8},{28,12},{1,17},{... | collective-permute-start | bytes 393224 | tf_op jit(solution)/shard_map/ppermute | solution.py:28
  57.1 14.7 %collective-permute-start.27 = (f32[256,128]{1,0:T(8,128)S(1)}, f32[256,128]{1,0:T(8,128)S(1)}, u32[]{:S(2)}, u32[]{:S(2)}) collective-permute-start(f32[256,128]{1,0:T(8,128)S(1)} %slice_add_fusion.1.own_ref), channel_id=1, source_target_pairs={{0,1},{1,0},{2,3},{3,2},{4,5},{5,4},{6,7},{7,6},{8,9},{9,8},{10,11... | collective-permute-start | bytes 393224 | tf_op jit(solution)/shard_map/ppermute | solution.py:28
  64.6 9.4 %copy-start.1 = (bf16[1024,256]{1,0:T(8,128)(2,1)S(1)}, bf16[1024,256]{1,0:T(8,128)(2,1)}, u32[]{:S(2)}) copy-start(bf16[1024,256]{1,0:T(8,128)(2,1)} %get-tuple-element.49.low_ref) | copy-start | bytes 1572868
  64.6 9.4 %copy-start.2 = (f32[1024,128]{1,0:T(8,128)S(1)}, f32[1024,128]{1,0:T(8,128)}, u32[]{:S(2)}) copy-start(f32[1024,128]{1,0:T(8,128)} %get-tuple-element.50.rhs_ref) | copy-start | bytes 1572868
  64.6 7.2 %collective-permute-start.28 = (f32[256,128]{1,0:T(8,128)S(1)}, f32[256,128]{1,0:T(8,128)S(1)}, u32[]{:S(2)}, u32[]{:S(2)}) collective-permute-start(f32[256,128]{1,0:T(8,128)S(1)} %shard_map.48.sib_ref), channel_id=1, source_target_pairs={{0,1},{1,0},{2,3},{3,2},{4,5},{5,4},{6,7},{7,6},{8,9},{9,8},{10,11... | collective-permute-start | bytes 393224 | tf_op jit(solution)/shard_map/ppermute | solution.py:28
  64.7 4.1 %collective-permute-start.30 = (f32[128,128]{1,0:T(8,128)S(1)}, f32[128,128]{1,0:T(8,128)S(1)}, u32[]{:S(2)}, u32[]{:S(2)}) collective-permute-start(f32[128,128]{1,0:T(8,128)S(1)} %slice_add_fusion.refs_0_.own_ref), channel_id=1, source_target_pairs={{0,16},{4,20},{8,24},{12,28},{16,0},{20,4},{24,8},{28,12},{1,17},{... | collective-permute-start | bytes 196616 | tf_op jit(solution)/shard_map/ppermute | solution.py:28
  65.5 8.5 %collective-permute-start.29 = (f32[128,128]{1,0:T(8,128)S(1)}, f32[128,128]{1,0:T(8,128)S(1)}, u32[]{:S(2)}, u32[]{:S(2)}) collective-permute-start(f32[128,128]{1,0:T(8,128)S(1)} %slice_add_fusion.refs_0_.own_ref), channel_id=1, source_target_pairs={{0,1},{1,0},{2,3},{3,2},{4,5},{5,4},{6,7},{7,6},{8,9},{9,8},{10,11... | collective-permute-start | bytes 196616 | tf_op jit(solution)/shard_map/ppermute | solution.py:28
  68.8 5.2 %collective-permute-start.31 = (f32[128,128]{1,0:T(8,128)S(1)}, f32[128,128]{1,0:T(8,128)S(1)}, u32[]{:S(2)}, u32[]{:S(2)}) collective-permute-start(f32[128,128]{1,0:T(8,128)S(1)} %collective-permute-done.30.sib_ref), channel_id=1, source_target_pairs={{0,1},{1,0},{2,3},{3,2},{4,5},{5,4},{6,7},{7,6},{8,9},{9,8},{10,11... | collective-permute-start | bytes 196616 | tf_op jit(solution)/shard_map/ppermute | solution.py:28

commit v5 on v4

--- a/solution.py
+++ b/solution.py
@@ -13,8 +13,10 @@
 QUARTER = HALF // 2
 TOLERANCE = 1e-7
 DIVERGED = 1e4
+SHIFT_FLOPS = 6e9
 VMEM_LIMIT = 40 * 2**20
 STREAM_LIMIT = 52 * 2**20
+FIRST_LIMIT = 52 * 2**20
 
 SMEM = pl.BlockSpec(memory_space=pltpu.SMEM)
 VMEM = pl.BlockSpec(memory_space=pltpu.VMEM)
@@ -157,7 +159,7 @@
     return pairs, sorted({left for left, _ in pairs}), sorted({right for _, right in pairs})
 
 
-def products(core, generators, solved_gens, rhs, groups, after):
+def products(core, generators, solved_gens, rhs, groups, after, limit):
     rows = rhs.shape[0]
     chunks = 4
     pairs, lefts, rights = needed(groups)
@@ -176,7 +178,7 @@
             pltpu.VMEM((RANK, width), jnp.float32),
             pltpu.SemaphoreType.DMA((len(lefts) + len(rights), chunks)),
         ],
-        compiler_params=pltpu.CompilerParams(vmem_limit_bytes=STREAM_LIMIT),
+        compiler_params=pltpu.CompilerParams(vmem_limit_bytes=limit),
         cost_estimate=cost(6 * rows * RANK * width, rows * (len(lefts) + len(rights)) * RANK),
     )(core, *given, *after)
 
@@ -259,9 +261,9 @@
     out_ref[...] = next_ref[:RANK, :] - dot_turned(in_order(core_ref[0], own, own_other_ref[RANK:, :]), z)
 
 
-def tail_kernel(core_ref, inverse_ref, p_sib_ref, own_ref, sib_ref, head_ref, head_other_ref, next_ref, *refs):
+def tail_kernel(core_ref, inverse_ref, shifted_ref, head_ref, head_other_ref, next_ref, *refs):
     z_ref, out_ref = refs[-2:]
-    z = dot(inverse_ref[...], unpack(sib_ref) - dot(p_sib_ref[...], unpack(own_ref)))
+    z = dot(inverse_ref[...], unpack(shifted_ref))
     store(z_ref, z)
     crossed = in_order(core_ref[0], head_ref[RANK:, :], head_other_ref[RANK:, :])
     store(out_ref, unpack(next_ref.at[RANK:]) - dot_turned(crossed, z))
@@ -288,17 +290,8 @@
     return jnp.concatenate([top, bottom], axis=0)
 
 
-def reduced_kernel(
-    core_ref, z1_ref, z1_other_ref, z0_ref, z0_other_ref, z01_ref, z01_other_ref, solved_ref, rhs_ref, *refs
-):
-    high_ref, low_ref, out_ref, solved, rhs, sems = refs[-6:]
+def combine_kernel(core_ref, z1_ref, z1_other_ref, z0_ref, z0_other_ref, z01_ref, z01_other_ref, factor_ref, base_ref):
     core = core_ref[0]
-    copies = [
-        pltpu.make_async_copy(solved_ref, solved, sems.at[0]),
-        pltpu.make_async_copy(rhs_ref, rhs, sems.at[1]),
-    ]
-    for copy in copies:
-        copy.start()
     z12 = in_order(core, z1_ref[:RANK, :], z1_other_ref[:RANK, :])
     z1x = rhs_in_order(core, z1_ref[RANK:, :], z1_other_ref[RANK:, :])
     z02 = in_order(core, z0_ref[:RANK, :], z0_other_ref[:RANK, :])
@@ -306,51 +299,31 @@
     z01 = in_order(core, z01_ref[...], z01_other_ref[...])
     middle = jnp.concatenate([z12, z1x], axis=1)
     first = jnp.concatenate([z02, z0x], axis=1) - dot(z01, middle)
-    coefs = split(jnp.concatenate([first, middle], axis=0))
-    for copy in copies:
-        copy.wait()
-    blocks = 4
-    block = rhs.shape[0] // blocks
-    for index in range(blocks):
-        rows = slice(index * block, (index + 1) * block)
-        left = split(jnp.concatenate([solved[0, rows, :], solved[1, rows, :]], axis=1))
-        value = dot_parts(left, coefs)
-        high, low = split(solved[2, rows, :] - value[:, :RANK])
-        high_ref[rows, :] = high
-        low_ref[rows, :] = low
-        out_ref[rows, :] = rhs[rows, :] - value[:, RANK:]
-
-
-def reduced(core, small, solved_gens, rhs, *after):
-    rows = rhs.shape[0]
-    part = jax.ShapeDtypeStruct((rows, RANK), jnp.bfloat16)
-    return pl.pallas_call(
-        reduced_kernel,
-        in_specs=[SMEM] + [VMEM] * len(small) + [HBM, HBM] + [ANY] * len(after),
-        out_specs=[VMEM] * 3,
-        out_shape=[part, part, struct(rows, RHS)],
-        scratch_shapes=[
-            pltpu.VMEM((3, rows, RANK), jnp.float32),
-            pltpu.VMEM((rows, RHS), jnp.float32),
-            pltpu.SemaphoreType.DMA((2,)),
-        ],
-        compiler_params=pltpu.CompilerParams(vmem_limit_bytes=STREAM_LIMIT),
-        cost_estimate=cost(6 * rows * 2 * RANK * (RANK + RHS), rows * 5 * RANK),
-    )(core, *small, solved_gens, rhs, *after)
+    factor_ref[:RANK, :] = first[:, :RANK]
+    factor_ref[RANK:, :] = z12
+    base_ref[:RANK, :] = first[:, RANK:]
+    base_ref[RANK:, :] = z1x
 
 
 def keep_kernel(core_ref, value_ref, *refs):
     refs[-1][...] = value_ref[...]
 
 
+def shift_kernel(core_ref, p_sib_ref, own_ref, sib_ref, out_ref):
+    store(out_ref, unpack(sib_ref) - dot(p_sib_ref[...], unpack(own_ref)))
+
+
 def final_kernel(
-    core_ref, inverse_ref, p_sib_ref, own_ref, own_other_ref, sib_ref, sib_other_ref, high_ref, low_ref, rhs_ref, out_ref
+    core_ref, inverse_ref, p_sib_ref, own_ref, own_other_ref, sib_ref, sib_other_ref, factor_ref, base_ref,
+    solved_ref, rhs_ref, out_ref,
 ):
     core = core_ref[0]
-    own = rhs_in_order(core, own_ref[...], own_other_ref[...])
-    sib = rhs_in_order(core, sib_ref[...], sib_other_ref[...])
+    own = rhs_in_order(core, own_ref[RANK:, :], own_other_ref[RANK:, :])
+    sib = rhs_in_order(core, sib_ref[RANK:, :], sib_other_ref[RANK:, :])
     z = dot(inverse_ref[...], sib - dot(p_sib_ref[...], own))
-    out_ref[...] = rhs_ref[...] - dot_parts((high_ref[...], low_ref[...]), split(z))
+    coefs = jnp.concatenate([base_ref[...] - dot(factor_ref[...], z), z], axis=0)
+    solved = jnp.concatenate([solved_ref[level] for level in range(3)], axis=1)
+    out_ref[...] = rhs_ref[...] - dot(solved, coefs)
 
 
 def on_device(rhs, generators, solved_gens):
@@ -360,9 +333,8 @@
     core = (lax.axis_index("sub") % 2).astype(jnp.int32).reshape(1)
     flops = 6 * RANK * RANK * HALF
 
-    def partial_products(groups, *after):
-        values = products(core, generators, solved_gens, rhs, groups, after)
-        return [keep + swap(send, "sub", 0) for keep, send in zip(values[::2], values[1::2])]
+    def met(keep, send):
+        return keep + swap(send, "sub", 0)
 
     def over_child(value):
         for bit in range(1, sub_bits):
@@ -371,12 +343,16 @@
             value = value + swap(value, "rows", bit)
         return value
 
-    (head,) = partial_products((((0, 0), (0, 1)),))
-    (tail,) = partial_products((((0, 2), (0, 3)),), head)
-    (near,) = partial_products((((1, 1), (1, 2), (1, 3)),), tail)
-    head, tail = over_child(head), over_child(tail)
-    (third,) = partial_products((((2, 2), (2, 3)),), tail)
-    near, third = over_child(near), over_child(third)
+    keep, send, tail_keep, tail_send = products(
+        core, generators, solved_gens, rhs, (((0, 0), (0, 1)), ((0, 2), (0, 3))), (), FIRST_LIMIT
+    )
+    head = met(keep, send)
+    tail = met(tail_keep, call(keep_kernel, struct(RANK + HALF), 0, core, tail_send, after=(head,)))
+    keep, send, third_keep, third_send = products(
+        core, generators, solved_gens, rhs, (((1, 1), (1, 2), (1, 3)), ((2, 2), (2, 3))), (tail,), STREAM_LIMIT
+    )
+    near, third = met(keep, send), met(third_keep, third_send)
+    head, tail, near, third = map(over_child, (head, tail, near, third))
 
     head_sib = swap(head, "rows", span_bits)
     tail_sib = swap(tail, "rows", span_bits)
@@ -387,9 +363,9 @@
     z01, p_own = call(
         head_kernel, [struct(RANK)] * 2, 3 * flops, core, inverted, p_sib, head, head_sib, head_other, near
     )
+    shifted = call(shift_kernel, struct(RANK + HALF), SHIFT_FLOPS, core, p_sib, tail, tail_sib)
     z0, r_own = call(
-        tail_kernel, [struct(RANK + HALF)] * 2, 5 * flops,
-        core, inverted, p_sib, tail, tail_sib, head, head_other, near, after=(p_own,),
+        tail_kernel, [struct(RANK + HALF)] * 2, 4 * flops, core, inverted, shifted, head, head_other, near, after=(p_own,)
     )
     third = call(third_kernel, struct(RANK + HALF), 2 * flops, core, tail, tail_other, z0, third, after=(r_own,))
 
@@ -409,20 +385,18 @@
 
     p_own, r_own = own[:RANK], own[RANK:]
     p_own = p_own + swap(p_own, "rows", span_bits + 1)
-    p_sib = swap(p_own, "rows", span_bits + 2)
     r_own = r_own + swap(r_own, "rows", span_bits + 1)
-    r_sib = swap(r_own, "rows", span_bits + 2)
-    small = (z1, swap(z1, "sub", 0), z0, swap(z0, "sub", 0), z01, swap(z01, "sub", 0))
-    high, low, current = reduced(core, small, solved_gens, rhs, r_own)
-    p_sib = call(keep_kernel, struct(RANK), 0, core, p_sib, after=(high,))
-    p_own_other = swap(p_own, "sub", 0)
-    r_own_other = swap(r_own, "sub", 0)
-    p_sib_other = swap(p_sib, "sub", 0)
-    r_sib_other = swap(r_sib, "sub", 0)
-    inverted, p_sib = inverse(core, p_own, p_sib, p_own_other, p_sib_other)
+    sib = jnp.concatenate([swap(p_own, "rows", span_bits + 2), swap(r_own, "rows", span_bits + 2)])
+    own = jnp.concatenate([p_own, r_own])
+    own_other, sib_other = swap(own, "sub", 0), swap(sib, "sub", 0)
+    factor, base = call(
+        combine_kernel, [struct(2 * RANK, RANK), struct(2 * RANK, RHS)], 3 * flops,
+        core, z1, swap(z1, "sub", 0), z0, swap(z0, "sub", 0), z01, swap(z01, "sub", 0),
+    )
+    inverted, p_sib = inverse(core, own, sib, own_other, sib_other)
     return call(
-        final_kernel, struct(rhs.shape[0], RHS), 6 * rhs.shape[0] * RANK * RHS,
-        core, inverted, p_sib, r_own, r_own_other, r_sib, r_sib_other, high, low, current,
+        final_kernel, struct(rhs.shape[0], RHS), 6 * rhs.shape[0] * 3 * RANK * RHS,
+        core, inverted, p_sib, own, own_other, sib, sib_other, factor, base, solved_gens, rhs,
     )
 
 

time: 76.2 us -> 77.8 us (1.021)
  the two profiles are of different devices: /device:TPU:7 before, /device:TPU:0 now
where the time goes in v5:
time: 77.8 us; the launch traced here: 77.6 us
  waiting for transfers between devices  29.6 us (38%)
  starting transfers between devices  23.8 us (31%)
  Pallas kernels  22.5 us (29%)
  local copies, waits for them, and re-layouts  1.11 us (1%)
    ppermute x30, waiting for transfers between devices, swap(): return lax.ppermute(value, axis, pairs)  29.6 us
    ppermute x30, starting transfers between devices, swap(): return lax.ppermute(value, axis, pairs)  23.8 us
    pallas_call x2, Pallas kernels, products(): pl.pallas_call(functools.partial(product_kernel, groups), in_specs=[SMEM]...  8.25 us
    pallas_call x8, Pallas kernels, call(): pl.pallas_call(kernel, in_specs=[SMEM] + [VMEM] * (len(values) - 1) + [AN...  7.4 us
    pallas_call x3, Pallas kernels, inverse(): pl.pallas_call(invert_kernel, in_specs=[SMEM] + [VMEM] * 4, out_specs=[VM...  6.84 us
  transfers between devices with their start and end apart: 30, of which 13 were waited for; matrix products, arithmetic and copies ran while one was open for 0% of the time, Pallas kernels for 15%

profile of v5, /device:TPU:0, one launch (start us, length us, event | category | flops | bytes accessed | tf_op | source)
XLA Modules:
  0.0 77.6 jit_solution(1070283720039440320)
XLA Ops:
  0.0 1.0 %copy-done.1 = f32[1024,128]{1,0:T(8,128)S(1)} copy-done((f32[1024,128]{1,0:T(8,128)S(1)}, f32[1024,128]{1,0:T(8,128)}, u32[]{:S(2)}) %copy-start.1) | copy-done | bytes 524312
  1.0 3.9 %shard_map.37 = (f32[512,128]{1,0:T(8,128)S(1)}, f32[512,128]{1,0:T(8,128)S(1)}, f32[384,128]{1,0:T(8,128)S(1)}, f32[384,128]{1,0:T(8,128)S(1)}) custom-call(s32[1]{0:T(128)} %bitcast.core_ref, f32[3,1024,256]{2,1,0:T(8,128)} %gens_ref.3, f32[3,1024,256]{2,1,0:T(8,128)} %solved_ref.5, f32[1024,128]{1,0:T(8,128)S(1)} %copy-done.1), custom_call_target="tpu_custom_call" | custom-call | flops 1409286144 | bytes 5242880 | tf_op jit(solution)/shard_map/pallas_call | solution.py:169
  5.0 0.5 collective-permute-start
  5.5 1.2 %collective-permute-done = f32[512,128]{1,0:T(8,128)S(1)} collective-permute-done((f32[512,128]{1,0:T(8,128)S(1)}, f32[512,128]{1,0:T(8,128)S(1)}, u32[]{:S(2)}, u32[]{:S(2)}) %collective-permute-start) | collective-permute-done | bytes 262176 | tf_op jit(solution)/shard_map/ppermute | solution.py:30
  6.7 0.4 collective-permute-start.5
  7.2 2.7 %collective-permute-start.1 = (f32[512,128]{1,0:T(8,128)S(1)}, f32[512,128]{1,0:T(8,128)S(1)}, u32[]{:S(2)}, u32[]{:S(2)}) collective-permute-start(f32[512,128]{1,0:T(8,128)S(1)} %add.44.refs_0_), channel_id=1, source_target_pairs={{0,2},{1,3},{2,0},{3,1},{4,6},{5,7},{6,4},{7,5},{8,10},{9,11},{10,... | collective-permute-start | bytes 786440 | tf_op jit(solution)/shard_map/ppermute | solution.py:30
  9.8 0.0 collective-permute-done.5
  9.9 4.3 %shard_map.40 = (f32[640,128]{1,0:T(8,128)S(1)}, f32[640,128]{1,0:T(8,128)S(1)}, f32[384,128]{1,0:T(8,128)S(1)}, f32[384,128]{1,0:T(8,128)S(1)}) custom-call(s32[1]{0:T(128)} %bitcast.core_ref, f32[3,1024,256]{2,1,0:T(8,128)} %gens_ref.3, f32[3,1024,256]{2,1,0:T(8,128)} %solved_ref.5, f32[1024,128]{1,0:T(8,128)S(1)} %copy-done.1, f32[384,128]{1,0:T(8,128)S(1)} %add.46.refs_1_), custom_call_target="tpu_custom_call" | custom-call | flops 1610612736 | bytes 5242880 | tf_op jit(solution)/shard_map/pallas_call | solution.py:169
  14.2 0.1 collective-permute-start.6
  14.3 2.3 %collective-permute-done.1 = f32[512,128]{1,0:T(8,128)S(1)} collective-permute-done((f32[512,128]{1,0:T(8,128)S(1)}, f32[512,128]{1,0:T(8,128)S(1)}, u32[]{:S(2)}, u32[]{:S(2)}) %collective-permute-start.1) | collective-permute-done | bytes 262176 | tf_op jit(solution)/shard_map/ppermute | solution.py:30
  16.7 1.8 %collective-permute-start.2 = (f32[512,128]{1,0:T(8,128)S(1)}, f32[512,128]{1,0:T(8,128)S(1)}, u32[]{:S(2)}, u32[]{:S(2)}) collective-permute-start(f32[512,128]{1,0:T(8,128)S(1)} %add.45.own_ref.head_ref), channel_id=1, source_target_pairs={{0,4},{4,0},{8,12},{12,8},{16,20},{20,16},{24,28},{28,24},{1,5},{5... | collective-permute-start | bytes 786440 | tf_op jit(solution)/shard_map/ppermute | solution.py:30
  18.5 1.5 %collective-permute-start.12 = (f32[384,128]{1,0:T(8,128)S(1)}, f32[384,128]{1,0:T(8,128)S(1)}, u32[]{:S(2)}, u32[]{:S(2)}) collective-permute-start(f32[384,128]{1,0:T(8,128)S(1)} %add.46.refs_1_), channel_id=1, source_target_pairs={{0,2},{1,3},{2,0},{3,1},{4,6},{5,7},{6,4},{7,5},{8,10},{9,11},{10,... | collective-permute-start | bytes 589832 | tf_op jit(solution)/shard_map/ppermute | solution.py:30
  20.0 0.0 collective-permute-start.3
  20.0 0.0 collective-permute-done.6
  20.0 0.6 collective-permute-start.7
  20.6 0.2 collective-permute-start.18
  20.8 3.9 %collective-permute-done.2.sib_ref = f32[512,128]{1,0:T(8,128)S(1)} collective-permute-done((f32[512,128]{1,0:T(8,128)S(1)}, f32[512,128]{1,0:T(8,128)S(1)}, u32[]{:S(2)}, u32[]{:S(2)}) %collective-permute-start.2) | collective-permute-done | bytes 262176 | tf_op jit(solution)/shard_map/ppermute | solution.py:30
  24.8 0.1 collective-permute-start.4
  24.8 1.0 %collective-permute-done.12 = f32[384,128]{1,0:T(8,128)S(1)} collective-permute-done((f32[384,128]{1,0:T(8,128)S(1)}, f32[384,128]{1,0:T(8,128)S(1)}, u32[]{:S(2)}, u32[]{:S(2)}) %collective-permute-start.12) | collective-permute-done | bytes 196640 | tf_op jit(solution)/shard_map/ppermute | solution.py:30
  25.9 0.6 collective-permute-start.13
  26.6 2.0 %collective-permute-start.19 = (f32[384,128]{1,0:T(8,128)S(1)}, f32[384,128]{1,0:T(8,128)S(1)}, u32[]{:S(2)}, u32[]{:S(2)}) collective-permute-start(f32[384,128]{1,0:T(8,128)S(1)} %add.52), channel_id=1, source_target_pairs={{0,2},{1,3},{2,0},{3,1},{4,6},{5,7},{6,4},{7,5},{8,10},{9,11},{10,... | collective-permute-start | bytes 589832 | tf_op jit(solution)/shard_map/ppermute | solution.py:30
  28.6 0.0 collective-permute-done.3.own_other_ref.head_other_ref
  28.6 0.0 collective-permute-start.17
  28.6 0.0 collective-permute-done.4.sib_other_ref
  28.6 2.2 %shard_map.38 = (f32[256,256]{1,0:T(8,128)S(1)}, f32[256,256]{1,0:T(8,128)S(1)}) custom-call(s32[1]{0:T(128)} %bitcast.core_ref, f32[512,128]{1,0:T(8,128)S(1)} %add.45.own_ref.head_ref, f32[512,128]{1,0:T(8,128)S(1)} %collective-permute-done.2.sib_ref, f32[512,128]{1,0:T(8,128)S(1)} %collective-permute-done.3.own_other_ref.head_other_ref, ...), custom_call_target="tpu_custom_call" | custom-call | flops 905969664 | bytes 1048576 | tf_op jit(solution)/shard_map/pallas_call | solution.py:246
  30.8 2.1 %collective-permute-done.7 = f32[640,128]{1,0:T(8,128)S(1)} collective-permute-done((f32[640,128]{1,0:T(8,128)S(1)}, f32[640,128]{1,0:T(8,128)S(1)}, u32[]{:S(2)}, u32[]{:S(2)}) %collective-permute-start.7) | collective-permute-done | bytes 327712 | tf_op jit(solution)/shard_map/ppermute | solution.py:30
  32.9 0.8 %shard_map.41 = (f32[256,128]{1,0:T(8,128)S(1)}, f32[256,128]{1,0:T(8,128)S(1)}) custom-call(s32[1]{0:T(128)} %bitcast.core_ref, f32[256,256]{1,0:T(8,128)S(1)} %get-tuple-element.29.inverse_ref, f32[256,256]{1,0:T(8,128)S(1)} %get-tuple-element.30.p_sib_ref, f32[512,128]{1,0:T(8,128)S(1)} %add.45.own_ref.head_ref, ...), custom_call_target="tpu_custom_call" | custom-call | flops 150994944 | bytes 1900548 | tf_op jit(solution)/shard_map/pallas_call | solution.py:235
  33.7 0.6 collective-permute-start.8
  34.4 0.0 collective-permute-done.13.sib_ref
  34.4 0.4 shard_map.43.shifted_ref
  34.8 0.8 %shard_map.44 = (f32[384,128]{1,0:T(8,128)S(1)}, f32[384,128]{1,0:T(8,128)S(1)}) custom-call(s32[1]{0:T(128)} %bitcast.core_ref, f32[256,256]{1,0:T(8,128)S(1)} %get-tuple-element.29.inverse_ref, f32[384,128]{1,0:T(8,128)S(1)} %shard_map.43.shifted_ref, f32[512,128]{1,0:T(8,128)S(1)} %add.45.own_ref.head_ref, ...), custom_call_target="tpu_custom_call" | custom-call | flops 201326592 | bytes 1703940 | tf_op jit(solution)/shard_map/pallas_call | solution.py:235
  35.6 1.5 %collective-permute-start.14 = (f32[384,128]{1,0:T(8,128)S(1)}, f32[384,128]{1,0:T(8,128)S(1)}, u32[]{:S(2)}, u32[]{:S(2)}) collective-permute-start(f32[384,128]{1,0:T(8,128)S(1)} %get-tuple-element.38.refs_0_), channel_id=1, source_target_pairs={{0,4},{4,0},{8,12},{12,8},{16,20},{20,16},{24,28},{28,24},{1,5},{5... | collective-permute-start | bytes 589832 | tf_op jit(solution)/shard_map/ppermute | solution.py:30
  37.1 3.1 %collective-permute-done.8 = f32[256,128]{1,0:T(8,128)S(1)} collective-permute-done((f32[256,128]{1,0:T(8,128)S(1)}, f32[256,128]{1,0:T(8,128)S(1)}, u32[]{:S(2)}, u32[]{:S(2)}) %collective-permute-start.8) | collective-permute-done | bytes 131104 | tf_op jit(solution)/shard_map/ppermute | solution.py:30
  40.2 1.6 %collective-permute-start.9 = (f32[256,128]{1,0:T(8,128)S(1)}, f32[256,128]{1,0:T(8,128)S(1)}, u32[]{:S(2)}, u32[]{:S(2)}) collective-permute-start(f32[256,128]{1,0:T(8,128)S(1)} %add.49.own_ref), channel_id=1, source_target_pairs={{0,8},{4,12},{8,0},{12,4},{16,24},{20,28},{24,16},{28,20},{1,9},{5... | collective-permute-start | bytes 393224 | tf_op jit(solution)/shard_map/ppermute | solution.py:30
  41.8 0.0 collective-permute-done.19
  41.9 0.4 shard_map.45
  42.3 0.6 collective-permute-start.20
  42.9 0.0 collective-permute-start.10
  42.9 2.4 %collective-permute-done.9.sib_ref = f32[256,128]{1,0:T(8,128)S(1)} collective-permute-done((f32[256,128]{1,0:T(8,128)S(1)}, f32[256,128]{1,0:T(8,128)S(1)}, u32[]{:S(2)}, u32[]{:S(2)}) %collective-permute-start.9) | collective-permute-done | bytes 131104 | tf_op jit(solution)/shard_map/ppermute | solution.py:30
  45.2 0.0 collective-permute-start.11
  45.2 0.0 collective-permute-done.14
  45.3 1.6 %collective-permute-start.15 = (f32[384,128]{1,0:T(8,128)S(1)}, f32[384,128]{1,0:T(8,128)S(1)}, u32[]{:S(2)}, u32[]{:S(2)}) collective-permute-start(f32[384,128]{1,0:T(8,128)S(1)} %add.51.own_ref), channel_id=1, source_target_pairs={{0,8},{4,12},{8,0},{12,4},{16,24},{20,28},{24,16},{28,20},{1,9},{5... | collective-permute-start | bytes 589832 | tf_op jit(solution)/shard_map/ppermute | solution.py:30
  46.9 0.3 collective-permute-start.16
  47.2 0.8 %collective-permute-done.20 = f32[384,128]{1,0:T(8,128)S(1)} collective-permute-done((f32[384,128]{1,0:T(8,128)S(1)}, f32[384,128]{1,0:T(8,128)S(1)}, u32[]{:S(2)}, u32[]{:S(2)}) %collective-permute-start.20) | collective-permute-done | bytes 196640 | tf_op jit(solution)/shard_map/ppermute | solution.py:30
  48.0 0.0 collective-permute-done.10.own_other_ref
  48.0 0.0 collective-permute-done.11.sib_other_ref
  48.1 2.4 %shard_map.42 = (f32[256,256]{1,0:T(8,128)S(1)}, f32[256,256]{1,0:T(8,128)S(1)}) custom-call(s32[1]{0:T(128)} %bitcast.core_ref, f32[256,128]{1,0:T(8,128)S(1)} %add.49.own_ref, f32[256,128]{1,0:T(8,128)S(1)} %collective-permute-done.9.sib_ref, f32[256,128]{1,0:T(8,128)S(1)} %collective-permute-done.10.own_other_ref, ...), custom_call_target="tpu_custom_call" | custom-call | flops 905969664 | bytes 1048576 | tf_op jit(solution)/shard_map/pallas_call | solution.py:246
  50.5 2.2 %collective-permute-done.15.sib_ref = f32[384,128]{1,0:T(8,128)S(1)} collective-permute-done((f32[384,128]{1,0:T(8,128)S(1)}, f32[384,128]{1,0:T(8,128)S(1)}, u32[]{:S(2)}, u32[]{:S(2)}) %collective-permute-start.15) | collective-permute-done | bytes 196640 | tf_op jit(solution)/shard_map/ppermute | solution.py:30
  52.6 1.0 %shard_map.46 = (f32[384,128]{1,0:T(8,128)S(1)}, f32[384,128]{1,0:T(8,128)S(1)}) custom-call(s32[1]{0:T(128)} %bitcast.core_ref, f32[256,256]{1,0:T(8,128)S(1)} %get-tuple-element.36.inverse_ref, f32[256,256]{1,0:T(8,128)S(1)} %get-tuple-element.37.p_sib_ref, f32[384,128]{1,0:T(8,128)S(1)} %add.51.own_ref, f32[384,128]{1,0:T(8,128)S(1)} %collective-permute-done.15.sib_ref, ...), custom_call_target="tpu_custom_call" | custom-call | flops 251658240 | bytes 1638404 | tf_op jit(solution)/shard_map/pallas_call | solution.py:235
  53.7 0.0 copy-start
  53.7 1.6 %collective-permute-start.21 = (f32[256,128]{1,0:T(8,128)S(1)}, f32[256,128]{1,0:T(8,128)S(1)}, u32[]{:S(2)}, u32[]{:S(2)}) collective-permute-start(f32[256,128]{1,0:T(8,128)S(1)} %slice.18), channel_id=1, source_target_pairs={{0,8},{4,12},{8,0},{12,4},{16,24},{20,28},{24,16},{28,20},{1,9},{5... | collective-permute-start | bytes 393224 | tf_op jit(solution)/shard_map/ppermute | solution.py:30
  55.4 0.5 collective-permute-start.27
  55.9 0.5 collective-permute-start.22
  56.3 2.9 %collective-permute-done.21 = f32[256,128]{1,0:T(8,128)S(1)} collective-permute-done((f32[256,128]{1,0:T(8,128)S(1)}, f32[256,128]{1,0:T(8,128)S(1)}, u32[]{:S(2)}, u32[]{:S(2)}) %collective-permute-start.21) | collective-permute-done | bytes 131104 | tf_op jit(solution)/shard_map/ppermute | solution.py:30
  59.3 2.7 %collective-permute-start.23 = (f32[256,128]{1,0:T(8,128)S(1)}, f32[256,128]{1,0:T(8,128)S(1)}, u32[]{:S(2)}, u32[]{:S(2)}) collective-permute-start(f32[256,128]{1,0:T(8,128)S(1)} %slice_add_fusion.1), channel_id=1, source_target_pairs={{0,16},{4,20},{8,24},{12,28},{16,0},{20,4},{24,8},{28,12},{1,17},{... | collective-permute-start | bytes 393224 | tf_op jit(solution)/shard_map/ppermute | solution.py:30
  62.0 1.1 %collective-permute-start.24 = (f32[128,128]{1,0:T(8,128)S(1)}, f32[128,128]{1,0:T(8,128)S(1)}, u32[]{:S(2)}, u32[]{:S(2)}) collective-permute-start(f32[128,128]{1,0:T(8,128)S(1)} %slice_add_fusion), channel_id=1, source_target_pairs={{0,16},{4,20},{8,24},{12,28},{16,0},{20,4},{24,8},{28,12},{1,17},{... | collective-permute-start | bytes 196616 | tf_op jit(solution)/shard_map/ppermute | solution.py:30
  63.1 0.1 collective-permute-start.25
  63.2 5.9 %collective-permute-done.23 = f32[256,128]{1,0:T(8,128)S(1)} collective-permute-done((f32[256,128]{1,0:T(8,128)S(1)}, f32[256,128]{1,0:T(8,128)S(1)}, u32[]{:S(2)}, u32[]{:S(2)}) %collective-permute-start.23) | collective-permute-done | bytes 131104 | tf_op jit(solution)/shard_map/ppermute | solution.py:30
  69.1 0.7 collective-permute-done.24
  69.8 0.5 collective-permute-start.29
  70.3 1.1 %collective-permute-done.29.z01_other_ref = f32[256,128]{1,0:T(8,128)S(1)} collective-permute-done((f32[256,128]{1,0:T(8,128)S(1)}, f32[256,128]{1,0:T(8,128)S(1)}, u32[]{:S(2)}, u32[]{:S(2)}) %collective-permute-start.29) | collective-permute-done | bytes 131104 | tf_op jit(solution)/shard_map/ppermute | solution.py:30
  71.4 0.5 shard_map.48
  71.9 2.2 %shard_map.47 = (f32[256,256]{1,0:T(8,128)S(1)}, f32[256,256]{1,0:T(8,128)S(1)}) custom-call(s32[1]{0:T(128)} %bitcast.core_ref, f32[384,128]{1,0:T(8,128)S(1)} %pad_maximum_fusion.own_ref, f32[384,128]{1,0:T(8,128)S(1)} %constant_dynamic-update-slice_fusion.sib_ref, f32[384,128]{1,0:T(8,128)S(1)} %collective-permute-done.25.own_other_ref, ...), custom_call_target="tpu_custom_call" | custom-call | flops 905969664 | bytes 1048576 | tf_op jit(solution)/shard_map/pallas_call | solution.py:246
  74.1 3.5 %shard_map.49 = f32[1024,128]{1,0:T(8,128)} custom-call(s32[1]{0:T(128)} %bitcast.core_ref, f32[256,256]{1,0:T(8,128)S(1)} %get-tuple-element.43.inverse_ref, f32[256,256]{1,0:T(8,128)S(1)} %get-tuple-element.44.p_sib_ref, f32[384,128]{1,0:T(8,128)S(1)} %pad_maximum_fusion.own_ref, f32[384,128]{1,0:T(8,128)S(1)} %collective-permute-done.25.own_other_ref, ...), custom_call_target="tpu_custom_call" | custom-call | flops 603979776 | bytes 6291460 | tf_op jit(solution)/shard_map/pallas_call | solution.py:235
  (34 shorter events, 0.4 us)
Async XLA Ops:
  0.0 1.0 %copy-start.1 = (f32[1024,128]{1,0:T(8,128)S(1)}, f32[1024,128]{1,0:T(8,128)}, u32[]{:S(2)}) copy-start(f32[1024,128]{1,0:T(8,128)} %rhs_ref.1) | copy-start | bytes 1572868
  5.0 1.7 %collective-permute-start = (f32[512,128]{1,0:T(8,128)S(1)}, f32[512,128]{1,0:T(8,128)S(1)}, u32[]{:S(2)}, u32[]{:S(2)}) collective-permute-start(f32[512,128]{1,0:T(8,128)S(1)} %get-tuple-element.28), channel_id=1, source_target_pairs={{0,1},{1,0},{2,3},{3,2},{4,5},{5,4},{6,7},{7,6},{8,9},{9,8},{10,11... | collective-permute-start | bytes 786440 | tf_op jit(solution)/shard_map/ppermute | solution.py:30
  6.7 3.1 %collective-permute-start.5 = (f32[384,128]{1,0:T(8,128)S(1)}, f32[384,128]{1,0:T(8,128)S(1)}, u32[]{:S(2)}, u32[]{:S(2)}) collective-permute-start(f32[384,128]{1,0:T(8,128)S(1)} %shard_map.39), channel_id=1, source_target_pairs={{0,1},{1,0},{2,3},{3,2},{4,5},{5,4},{6,7},{7,6},{8,9},{9,8},{10,11... | collective-permute-start | bytes 589832 | tf_op jit(solution)/shard_map/ppermute | solution.py:30
  7.2 9.5 %collective-permute-start.1 = (f32[512,128]{1,0:T(8,128)S(1)}, f32[512,128]{1,0:T(8,128)S(1)}, u32[]{:S(2)}, u32[]{:S(2)}) collective-permute-start(f32[512,128]{1,0:T(8,128)S(1)} %add.44.refs_0_), channel_id=1, source_target_pairs={{0,2},{1,3},{2,0},{3,1},{4,6},{5,7},{6,4},{7,5},{8,10},{9,11},{10,... | collective-permute-start | bytes 786440 | tf_op jit(solution)/shard_map/ppermute | solution.py:30
  14.2 5.8 %collective-permute-start.6 = (f32[640,128]{1,0:T(8,128)S(1)}, f32[640,128]{1,0:T(8,128)S(1)}, u32[]{:S(2)}, u32[]{:S(2)}) collective-permute-start(f32[640,128]{1,0:T(8,128)S(1)} %get-tuple-element.34), channel_id=1, source_target_pairs={{0,1},{1,0},{2,3},{3,2},{4,5},{5,4},{6,7},{7,6},{8,9},{9,8},{10,11... | collective-permute-start | bytes 983048 | tf_op jit(solution)/shard_map/ppermute | solution.py:30
  16.7 8.1 %collective-permute-start.2 = (f32[512,128]{1,0:T(8,128)S(1)}, f32[512,128]{1,0:T(8,128)S(1)}, u32[]{:S(2)}, u32[]{:S(2)}) collective-permute-start(f32[512,128]{1,0:T(8,128)S(1)} %add.45.own_ref.head_ref), channel_id=1, source_target_pairs={{0,4},{4,0},{8,12},{12,8},{16,20},{20,16},{24,28},{28,24},{1,5},{5... | collective-permute-start | bytes 786440 | tf_op jit(solution)/shard_map/ppermute | solution.py:30
  18.5 7.4 %collective-permute-start.12 = (f32[384,128]{1,0:T(8,128)S(1)}, f32[384,128]{1,0:T(8,128)S(1)}, u32[]{:S(2)}, u32[]{:S(2)}) collective-permute-start(f32[384,128]{1,0:T(8,128)S(1)} %add.46.refs_1_), channel_id=1, source_target_pairs={{0,2},{1,3},{2,0},{3,1},{4,6},{5,7},{6,4},{7,5},{8,10},{9,11},{10,... | collective-permute-start | bytes 589832 | tf_op jit(solution)/shard_map/ppermute | solution.py:30
  20.0 8.6 %collective-permute-start.3 = (f32[512,128]{1,0:T(8,128)S(1)}, f32[512,128]{1,0:T(8,128)S(1)}, u32[]{:S(2)}, u32[]{:S(2)}) collective-permute-start(f32[512,128]{1,0:T(8,128)S(1)} %add.45.own_ref.head_ref), channel_id=1, source_target_pairs={{0,1},{1,0},{2,3},{3,2},{4,5},{5,4},{6,7},{7,6},{8,9},{9,8},{10,11... | collective-permute-start | bytes 786440 | tf_op jit(solution)/shard_map/ppermute | solution.py:30
  20.0 12.9 %collective-permute-start.7 = (f32[640,128]{1,0:T(8,128)S(1)}, f32[640,128]{1,0:T(8,128)S(1)}, u32[]{:S(2)}, u32[]{:S(2)}) collective-permute-start(f32[640,128]{1,0:T(8,128)S(1)} %add.47), channel_id=1, source_target_pairs={{0,2},{1,3},{2,0},{3,1},{4,6},{5,7},{6,4},{7,5},{8,10},{9,11},{10,... | collective-permute-start | bytes 983048 | tf_op jit(solution)/shard_map/ppermute | solution.py:30
  20.6 5.9 %collective-permute-start.18 = (f32[384,128]{1,0:T(8,128)S(1)}, f32[384,128]{1,0:T(8,128)S(1)}, u32[]{:S(2)}, u32[]{:S(2)}) collective-permute-start(f32[384,128]{1,0:T(8,128)S(1)} %get-tuple-element.41), channel_id=1, source_target_pairs={{0,1},{1,0},{2,3},{3,2},{4,5},{5,4},{6,7},{7,6},{8,9},{9,8},{10,11... | collective-permute-start | bytes 589832 | tf_op jit(solution)/shard_map/ppermute | solution.py:30
  24.8 3.8 %collective-permute-start.4 = (f32[256,128]{1,0:T(8,128)S(1)}, f32[256,128]{1,0:T(8,128)S(1)}, u32[]{:S(2)}, u32[]{:S(2)}) collective-permute-start(f32[256,128]{1,0:T(8,128)S(1)} %slice.20), channel_id=1, source_target_pairs={{0,1},{1,0},{2,3},{3,2},{4,5},{5,4},{6,7},{7,6},{8,9},{9,8},{10,11... | collective-permute-start | bytes 393224 | tf_op jit(solution)/shard_map/ppermute | solution.py:30
  25.9 8.4 %collective-permute-start.13 = (f32[384,128]{1,0:T(8,128)S(1)}, f32[384,128]{1,0:T(8,128)S(1)}, u32[]{:S(2)}, u32[]{:S(2)}) collective-permute-start(f32[384,128]{1,0:T(8,128)S(1)} %add.50.own_ref), channel_id=1, source_target_pairs={{0,4},{4,0},{8,12},{12,8},{16,20},{20,16},{24,28},{28,24},{1,5},{5... | collective-permute-start | bytes 589832 | tf_op jit(solution)/shard_map/ppermute | solution.py:30
  26.6 15.3 %collective-permute-start.19 = (f32[384,128]{1,0:T(8,128)S(1)}, f32[384,128]{1,0:T(8,128)S(1)}, u32[]{:S(2)}, u32[]{:S(2)}) collective-permute-start(f32[384,128]{1,0:T(8,128)S(1)} %add.52), channel_id=1, source_target_pairs={{0,2},{1,3},{2,0},{3,1},{4,6},{5,7},{6,4},{7,5},{8,10},{9,11},{10,... | collective-permute-start | bytes 589832 | tf_op jit(solution)/shard_map/ppermute | solution.py:30
  28.6 13.3 %collective-permute-start.17 = (f32[256,128]{1,0:T(8,128)S(1)}, f32[256,128]{1,0:T(8,128)S(1)}, u32[]{:S(2)}, u32[]{:S(2)}) collective-permute-start(f32[256,128]{1,0:T(8,128)S(1)} %slice.22), channel_id=1, source_target_pairs={{0,1},{1,0},{2,3},{3,2},{4,5},{5,4},{6,7},{7,6},{8,9},{9,8},{10,11... | collective-permute-start | bytes 393224 | tf_op jit(solution)/shard_map/ppermute | solution.py:30
  33.7 6.4 %collective-permute-start.8 = (f32[256,128]{1,0:T(8,128)S(1)}, f32[256,128]{1,0:T(8,128)S(1)}, u32[]{:S(2)}, u32[]{:S(2)}) collective-permute-start(f32[256,128]{1,0:T(8,128)S(1)} %get-tuple-element.35.refs_0_), channel_id=1, source_target_pairs={{0,4},{4,0},{8,12},{12,8},{16,20},{20,16},{24,28},{28,24},{1,5},{5... | collective-permute-start | bytes 393224 | tf_op jit(solution)/shard_map/ppermute | solution.py:30
  35.6 9.7 %collective-permute-start.14 = (f32[384,128]{1,0:T(8,128)S(1)}, f32[384,128]{1,0:T(8,128)S(1)}, u32[]{:S(2)}, u32[]{:S(2)}) collective-permute-start(f32[384,128]{1,0:T(8,128)S(1)} %get-tuple-element.38.refs_0_), channel_id=1, source_target_pairs={{0,4},{4,0},{8,12},{12,8},{16,20},{20,16},{24,28},{28,24},{1,5},{5... | collective-permute-start | bytes 589832 | tf_op jit(solution)/shard_map/ppermute | solution.py:30
  40.2 5.0 %collective-permute-start.9 = (f32[256,128]{1,0:T(8,128)S(1)}, f32[256,128]{1,0:T(8,128)S(1)}, u32[]{:S(2)}, u32[]{:S(2)}) collective-permute-start(f32[256,128]{1,0:T(8,128)S(1)} %add.49.own_ref), channel_id=1, source_target_pairs={{0,8},{4,12},{8,0},{12,4},{16,24},{20,28},{24,16},{28,20},{1,9},{5... | collective-permute-start | bytes 393224 | tf_op jit(solution)/shard_map/ppermute | solution.py:30
  42.3 5.7 %collective-permute-start.20 = (f32[384,128]{1,0:T(8,128)S(1)}, f32[384,128]{1,0:T(8,128)S(1)}, u32[]{:S(2)}, u32[]{:S(2)}) collective-permute-start(f32[384,128]{1,0:T(8,128)S(1)} %shard_map.45), channel_id=1, source_target_pairs={{0,4},{4,0},{8,12},{12,8},{16,20},{20,16},{24,28},{28,24},{1,5},{5... | collective-permute-start | bytes 589832 | tf_op jit(solution)/shard_map/ppermute | solution.py:30
  42.9 5.2 %collective-permute-start.10 = (f32[256,128]{1,0:T(8,128)S(1)}, f32[256,128]{1,0:T(8,128)S(1)}, u32[]{:S(2)}, u32[]{:S(2)}) collective-permute-start(f32[256,128]{1,0:T(8,128)S(1)} %add.49.own_ref), channel_id=1, source_target_pairs={{0,1},{1,0},{2,3},{3,2},{4,5},{5,4},{6,7},{7,6},{8,9},{9,8},{10,11... | collective-permute-start | bytes 393224 | tf_op jit(solution)/shard_map/ppermute | solution.py:30
  45.2 2.8 %collective-permute-start.11 = (f32[256,128]{1,0:T(8,128)S(1)}, f32[256,128]{1,0:T(8,128)S(1)}, u32[]{:S(2)}, u32[]{:S(2)}) collective-permute-start(f32[256,128]{1,0:T(8,128)S(1)} %collective-permute-done.9.sib_ref), channel_id=1, source_target_pairs={{0,1},{1,0},{2,3},{3,2},{4,5},{5,4},{6,7},{7,6},{8,9},{9,8},{10,11... | collective-permute-start | bytes 393224 | tf_op jit(solution)/shard_map/ppermute | solution.py:30
  45.3 7.4 %collective-permute-start.15 = (f32[384,128]{1,0:T(8,128)S(1)}, f32[384,128]{1,0:T(8,128)S(1)}, u32[]{:S(2)}, u32[]{:S(2)}) collective-permute-start(f32[384,128]{1,0:T(8,128)S(1)} %add.51.own_ref), channel_id=1, source_target_pairs={{0,8},{4,12},{8,0},{12,4},{16,24},{20,28},{24,16},{28,20},{1,9},{5... | collective-permute-start | bytes 589832 | tf_op jit(solution)/shard_map/ppermute | solution.py:30
  46.9 3.6 %collective-permute-start.16 = (f32[256,128]{1,0:T(8,128)S(1)}, f32[256,128]{1,0:T(8,128)S(1)}, u32[]{:S(2)}, u32[]{:S(2)}) collective-permute-start(f32[256,128]{1,0:T(8,128)S(1)} %slice.21), channel_id=1, source_target_pairs={{0,1},{1,0},{2,3},{3,2},{4,5},{5,4},{6,7},{7,6},{8,9},{9,8},{10,11... | collective-permute-start | bytes 393224 | tf_op jit(solution)/shard_map/ppermute | solution.py:30
  53.7 20.4 %copy-start = (f32[3,1024,256]{2,1,0:T(8,128)S(1)}, f32[3,1024,256]{2,1,0:T(8,128)}, u32[]{:S(2)}) copy-start(f32[3,1024,256]{2,1,0:T(8,128)} %solved_ref.5) | copy-start | bytes 9437188
  53.7 5.6 %collective-permute-start.21 = (f32[256,128]{1,0:T(8,128)S(1)}, f32[256,128]{1,0:T(8,128)S(1)}, u32[]{:S(2)}, u32[]{:S(2)}) collective-permute-start(f32[256,128]{1,0:T(8,128)S(1)} %slice.18), channel_id=1, source_target_pairs={{0,8},{4,12},{8,0},{12,4},{16,24},{20,28},{24,16},{28,20},{1,9},{5... | collective-permute-start | bytes 393224 | tf_op jit(solution)/shard_map/ppermute | solution.py:30
  55.4 16.0 %collective-permute-start.28 = (f32[384,128]{1,0:T(8,128)S(1)}, f32[384,128]{1,0:T(8,128)S(1)}, u32[]{:S(2)}, u32[]{:S(2)}) collective-permute-start(f32[384,128]{1,0:T(8,128)S(1)} %get-tuple-element.39.z_ref.z0_ref), channel_id=1, source_target_pairs={{0,1},{1,0},{2,3},{3,2},{4,5},{5,4},{6,7},{7,6},{8,9},{9,8},{10,11... | collective-permute-start | bytes 589832 | tf_op jit(solution)/shard_map/ppermute | solution.py:30
  55.4 16.0 %collective-permute-start.27 = (f32[384,128]{1,0:T(8,128)S(1)}, f32[384,128]{1,0:T(8,128)S(1)}, u32[]{:S(2)}, u32[]{:S(2)}) collective-permute-start(f32[384,128]{1,0:T(8,128)S(1)} %get-tuple-element.45.z1_ref), channel_id=1, source_target_pairs={{0,1},{1,0},{2,3},{3,2},{4,5},{5,4},{6,7},{7,6},{8,9},{9,8},{10,11... | collective-permute-start | bytes 589832 | tf_op jit(solution)/shard_map/ppermute | solution.py:30
  55.9 6.1 %collective-permute-start.22 = (f32[128,128]{1,0:T(8,128)S(1)}, f32[128,128]{1,0:T(8,128)S(1)}, u32[]{:S(2)}, u32[]{:S(2)}) collective-permute-start(f32[128,128]{1,0:T(8,128)S(1)} %slice.19), channel_id=1, source_target_pairs={{0,8},{4,12},{8,0},{12,4},{16,24},{20,28},{24,16},{28,20},{1,9},{5... | collective-permute-start | bytes 196616 | tf_op jit(solution)/shard_map/ppermute | solution.py:30
  59.3 9.8 %collective-permute-start.23 = (f32[256,128]{1,0:T(8,128)S(1)}, f32[256,128]{1,0:T(8,128)S(1)}, u32[]{:S(2)}, u32[]{:S(2)}) collective-permute-start(f32[256,128]{1,0:T(8,128)S(1)} %slice_add_fusion.1), channel_id=1, source_target_pairs={{0,16},{4,20},{8,24},{12,28},{16,0},{20,4},{24,8},{28,12},{1,17},{... | collective-permute-start | bytes 393224 | tf_op jit(solution)/shard_map/ppermute | solution.py:30
  62.0 7.8 %collective-permute-start.24 = (f32[128,128]{1,0:T(8,128)S(1)}, f32[128,128]{1,0:T(8,128)S(1)}, u32[]{:S(2)}, u32[]{:S(2)}) collective-permute-start(f32[128,128]{1,0:T(8,128)S(1)} %slice_add_fusion), channel_id=1, source_target_pairs={{0,16},{4,20},{8,24},{12,28},{16,0},{20,4},{24,8},{28,12},{1,17},{... | collective-permute-start | bytes 196616 | tf_op jit(solution)/shard_map/ppermute | solution.py:30
  63.1 8.8 %collective-permute-start.25 = (f32[384,128]{1,0:T(8,128)S(1)}, f32[384,128]{1,0:T(8,128)S(1)}, u32[]{:S(2)}, u32[]{:S(2)}) collective-permute-start(f32[384,128]{1,0:T(8,128)S(1)} %pad_maximum_fusion.own_ref), channel_id=1, source_target_pairs={{0,1},{1,0},{2,3},{3,2},{4,5},{5,4},{6,7},{7,6},{8,9},{9,8},{10,11... | collective-permute-start | bytes 589832 | tf_op jit(solution)/shard_map/ppermute | solution.py:30
  69.8 2.1 %collective-permute-start.26 = (f32[384,128]{1,0:T(8,128)S(1)}, f32[384,128]{1,0:T(8,128)S(1)}, u32[]{:S(2)}, u32[]{:S(2)}) collective-permute-start(f32[384,128]{1,0:T(8,128)S(1)} %constant_dynamic-update-slice_fusion.sib_ref), channel_id=1, source_target_pairs={{0,1},{1,0},{2,3},{3,2},{4,5},{5,4},{6,7},{7,6},{8,9},{9,8},{10,11... | collective-permute-start | bytes 589832 | tf_op jit(solution)/shard_map/ppermute | solution.py:30
  69.8 1.6 %collective-permute-start.29 = (f32[256,128]{1,0:T(8,128)S(1)}, f32[256,128]{1,0:T(8,128)S(1)}, u32[]{:S(2)}, u32[]{:S(2)}) collective-permute-start(f32[256,128]{1,0:T(8,128)S(1)} %get-tuple-element.46.z01_ref), channel_id=1, source_target_pairs={{0,1},{1,0},{2,3},{3,2},{4,5},{5,4},{6,7},{7,6},{8,9},{9,8},{10,11... | collective-permute-start | bytes 393224 | tf_op jit(solution)/shard_map/ppermute | solution.py:30

commit v6 on v4

--- a/solution.py
+++ b/solution.py
@@ -11,8 +11,11 @@
 RHS = 128
 HALF = RANK // 2
 QUARTER = HALF // 2
+SYM = HALF + QUARTER
 TOLERANCE = 1e-7
 DIVERGED = 1e4
+SCALE = 1
+FIRST_FLOPS = 6e9
 VMEM_LIMIT = 40 * 2**20
 STREAM_LIMIT = 52 * 2**20
 
@@ -33,7 +36,7 @@
 
 
 def cost(flops, floats):
-    return pl.CostEstimate(flops=int(flops), bytes_accessed=int(4 * floats), transcendentals=0)
+    return pl.CostEstimate(flops=int(flops / SCALE), bytes_accessed=int(4 * floats / SCALE), transcendentals=0)
 
 
 def split(value):
@@ -59,6 +62,27 @@
 def in_order(core, own, other):
     first = core == 0
     return jnp.concatenate([jnp.where(first, own, other), jnp.where(first, other, own)], axis=1)
+
+
+def symmetric(core, own, other):
+    first = core == 0
+    low = jnp.where(first, own, other)
+    high = jnp.where(first, other, own)
+    upper = jnp.concatenate([low[HALF:], high[HALF:]], axis=0)
+    return jnp.concatenate(
+        [jnp.concatenate([low[:HALF], upper], axis=1), jnp.concatenate([upper.T, high[:HALF]], axis=1)], axis=0
+    )
+
+
+def symmetric_half(core, value):
+    first = core == 0
+    return jnp.concatenate(
+        [
+            jnp.where(first, value[:HALF], value[HALF:]),
+            jnp.where(first, value[HALF:].T[:QUARTER], value[QUARTER:HALF]),
+        ],
+        axis=0,
+    )
 
 
 def pack(value):
@@ -135,7 +159,11 @@
         start = 0
         for pair in group:
             at = places[pair]
-            if pair[1] < 3:
+            if pair[0] == pair[1]:
+                value = total[:, at : at + RANK]
+                low = jnp.concatenate([value[:HALF, :HALF], value[:QUARTER, HALF:]], axis=0)
+                high = jnp.concatenate([value[HALF:, HALF:], value[QUARTER:HALF, HALF:]], axis=0)
+            elif pair[1] < 3:
                 low = total[:, at : at + HALF]
                 high = total[:, at + HALF : at + RANK]
             else:
@@ -148,6 +176,10 @@
             start += low.shape[0]
 
 
+def rows_of(pair):
+    return SYM if pair[0] == pair[1] else HALF if pair[1] == 3 else RANK
+
+
 def width_of(level):
     return RHS if level == 3 else RANK
 
@@ -157,12 +189,12 @@
     return pairs, sorted({left for left, _ in pairs}), sorted({right for _, right in pairs})
 
 
-def products(core, generators, solved_gens, rhs, groups, after):
+def products(core, generators, solved_gens, rhs, groups, *after):
     rows = rhs.shape[0]
     chunks = 4
     pairs, lefts, rights = needed(groups)
     width = sum(width_of(right) for _, right in pairs)
-    outs = [struct(sum(HALF if right == 3 else RANK for _, right in group)) for group in groups for _ in range(2)]
+    outs = [struct(sum(rows_of(pair) for pair in group)) for group in groups for _ in range(2)]
     given = (generators, solved_gens, rhs) if 3 in rights else (generators, solved_gens)
     return pl.pallas_call(
         functools.partial(product_kernel, groups),
@@ -215,8 +247,8 @@
 
 def invert_kernel(core_ref, own_ref, sib_ref, own_other_ref, sib_other_ref, inverse_ref, p_sib_ref, power):
     core = core_ref[0]
-    p_own = in_order(core, own_ref[:RANK, :], own_other_ref[:RANK, :])
-    p_sib = in_order(core, sib_ref[:RANK, :], sib_other_ref[:RANK, :])
+    p_own = symmetric(core, own_ref[:SYM, :], own_other_ref[:SYM, :])
+    p_sib = symmetric(core, sib_ref[:SYM, :], sib_other_ref[:SYM, :])
     p_sib_ref[...] = p_sib
     product = dot(p_sib, p_own)
     bound = series(product, 1.0, power, inverse_ref)
@@ -252,31 +284,33 @@
     )(core, own, sib, own_other, sib_other)
 
 
-def head_kernel(core_ref, inverse_ref, p_sib_ref, own_ref, sib_ref, own_other_ref, next_ref, z_ref, out_ref):
-    own = own_ref[RANK:, :]
-    z = dot(inverse_ref[...], sib_ref[RANK:, :] - dot(p_sib_ref[...], own))
-    z_ref[...] = z
-    out_ref[...] = next_ref[:RANK, :] - dot_turned(in_order(core_ref[0], own, own_other_ref[RANK:, :]), z)
-
-
-def tail_kernel(core_ref, inverse_ref, p_sib_ref, own_ref, sib_ref, head_ref, head_other_ref, next_ref, *refs):
-    z_ref, out_ref = refs[-2:]
+def first_kernel(core_ref, inverse_ref, p_sib_ref, head_ref, head_sib_ref, head_other_ref, tail_ref, tail_sib_ref, z_ref, out_ref):
+    core = core_ref[0]
+    own = jnp.concatenate([head_ref[SYM:, :], unpack(tail_ref)], axis=1)
+    sib = jnp.concatenate([head_sib_ref[SYM:, :], unpack(tail_sib_ref)], axis=1)
+    z = dot(inverse_ref[...], sib - dot(p_sib_ref[...], own))
+    store(z_ref, z)
+    value = dot_turned(in_order(core, head_ref[SYM:, :], head_other_ref[SYM:, :]), z)
+    out_ref[:SYM, :] = symmetric_half(core, value[:, :HALF])
+    store(out_ref.at[SYM:], value[:, HALF:])
+
+
+def last_parts(core, crossed, z, next_ref, out_ref):
+    value = dot_turned(crossed, z)
+    out_ref[:SYM, :] = next_ref[:SYM, :] - symmetric_half(core, value[:, :HALF])
+    store(out_ref.at[SYM:], unpack(next_ref.at[SYM:]) - value[:, HALF:])
+
+
+def third_kernel(core_ref, own_ref, own_other_ref, z_ref, next_ref, *refs):
+    core = core_ref[0]
+    last_parts(core, in_order(core, own_ref[:RANK, :], own_other_ref[...]), unpack(z_ref.at[RANK:]), next_ref, refs[-1])
+
+
+def middle_kernel(core_ref, inverse_ref, p_sib_ref, own_ref, sib_ref, own_other_ref, next_ref, z_ref, out_ref):
+    core = core_ref[0]
     z = dot(inverse_ref[...], unpack(sib_ref) - dot(p_sib_ref[...], unpack(own_ref)))
     store(z_ref, z)
-    crossed = in_order(core_ref[0], head_ref[RANK:, :], head_other_ref[RANK:, :])
-    store(out_ref, unpack(next_ref.at[RANK:]) - dot_turned(crossed, z))
-
-
-def third_kernel(core_ref, own_ref, own_other_ref, z_ref, next_ref, *refs):
-    crossed = in_order(core_ref[0], own_ref[:RANK, :], own_other_ref[...])
-    store(refs[-1], unpack(next_ref) - dot_turned(crossed, unpack(z_ref)))
-
-
-def middle_kernel(core_ref, inverse_ref, p_sib_ref, own_ref, sib_ref, own_other_ref, next_ref, z_ref, out_ref):
-    z = dot(inverse_ref[...], unpack(sib_ref) - dot(p_sib_ref[...], unpack(own_ref)))
-    store(z_ref, z)
-    crossed = in_order(core_ref[0], own_ref[:RANK, :], own_other_ref[...])
-    store(out_ref, unpack(next_ref) - dot_turned(crossed, z))
+    last_parts(core, in_order(core, own_ref[:RANK, :], own_other_ref[...]), z, next_ref, out_ref)
 
 
 def rhs_in_order(core, own, other):
@@ -289,36 +323,33 @@
 
 
 def reduced_kernel(
-    core_ref, z1_ref, z1_other_ref, z0_ref, z0_other_ref, z01_ref, z01_other_ref, solved_ref, rhs_ref, *refs
+    core_ref, z1_ref, z1_other_ref, z0_ref, z0_other_ref, solved_ref, rhs_ref, *refs
 ):
     high_ref, low_ref, out_ref, solved, rhs, sems = refs[-6:]
     core = core_ref[0]
     copies = [
-        pltpu.make_async_copy(solved_ref, solved, sems.at[0]),
-        pltpu.make_async_copy(rhs_ref, rhs, sems.at[1]),
+        pltpu.make_async_copy(solved_ref.at[0], solved.at[0], sems.at[0]),
+        pltpu.make_async_copy(solved_ref.at[1], solved.at[1], sems.at[1]),
+        pltpu.make_async_copy(solved_ref.at[2], solved.at[2], sems.at[2]),
+        pltpu.make_async_copy(rhs_ref, rhs, sems.at[3]),
     ]
     for copy in copies:
         copy.start()
     z12 = in_order(core, z1_ref[:RANK, :], z1_other_ref[:RANK, :])
     z1x = rhs_in_order(core, z1_ref[RANK:, :], z1_other_ref[RANK:, :])
-    z02 = in_order(core, z0_ref[:RANK, :], z0_other_ref[:RANK, :])
-    z0x = rhs_in_order(core, z0_ref[RANK:, :], z0_other_ref[RANK:, :])
-    z01 = in_order(core, z01_ref[...], z01_other_ref[...])
+    z01 = in_order(core, z0_ref[:RANK, :], z0_other_ref[:RANK, :])
+    z02 = in_order(core, z0_ref[RANK : 2 * RANK, :], z0_other_ref[RANK : 2 * RANK, :])
+    z0x = rhs_in_order(core, z0_ref[2 * RANK :, :], z0_other_ref[2 * RANK :, :])
     middle = jnp.concatenate([z12, z1x], axis=1)
     first = jnp.concatenate([z02, z0x], axis=1) - dot(z01, middle)
-    coefs = split(jnp.concatenate([first, middle], axis=0))
+    coefs = jnp.concatenate([first, middle], axis=0)
     for copy in copies:
         copy.wait()
-    blocks = 4
-    block = rhs.shape[0] // blocks
-    for index in range(blocks):
-        rows = slice(index * block, (index + 1) * block)
-        left = split(jnp.concatenate([solved[0, rows, :], solved[1, rows, :]], axis=1))
-        value = dot_parts(left, coefs)
-        high, low = split(solved[2, rows, :] - value[:, :RANK])
-        high_ref[rows, :] = high
-        low_ref[rows, :] = low
-        out_ref[rows, :] = rhs[rows, :] - value[:, RANK:]
+    value = dot(jnp.concatenate([solved[0], solved[1]], axis=1), coefs)
+    high, low = split(solved[2] - value[:, :RANK])
+    high_ref[...] = high
+    low_ref[...] = low
+    out_ref[...] = rhs[...] - value[:, RANK:]
 
 
 def reduced(core, small, solved_gens, rhs, *after):
@@ -332,7 +363,7 @@
         scratch_shapes=[
             pltpu.VMEM((3, rows, RANK), jnp.float32),
             pltpu.VMEM((rows, RHS), jnp.float32),
-            pltpu.SemaphoreType.DMA((2,)),
+            pltpu.SemaphoreType.DMA((4,)),
         ],
         compiler_params=pltpu.CompilerParams(vmem_limit_bytes=STREAM_LIMIT),
         cost_estimate=cost(6 * rows * 2 * RANK * (RANK + RHS), rows * 5 * RANK),
@@ -343,12 +374,16 @@
     refs[-1][...] = value_ref[...]
 
 
+def add_kernel(core_ref, first_ref, second_ref, *refs):
+    refs[-1][...] = first_ref[...] + second_ref[...]
+
+
 def final_kernel(
     core_ref, inverse_ref, p_sib_ref, own_ref, own_other_ref, sib_ref, sib_other_ref, high_ref, low_ref, rhs_ref, out_ref
 ):
     core = core_ref[0]
-    own = rhs_in_order(core, own_ref[...], own_other_ref[...])
-    sib = rhs_in_order(core, sib_ref[...], sib_other_ref[...])
+    own = rhs_in_order(core, own_ref[SYM:, :], own_other_ref[SYM:, :])
+    sib = rhs_in_order(core, sib_ref[SYM:, :], sib_other_ref[SYM:, :])
     z = dot(inverse_ref[...], sib - dot(p_sib_ref[...], own))
     out_ref[...] = rhs_ref[...] - dot_parts((high_ref[...], low_ref[...]), split(z))
 
@@ -359,10 +394,7 @@
     span_bits = (groups // 8).bit_length() - 1
     core = (lax.axis_index("sub") % 2).astype(jnp.int32).reshape(1)
     flops = 6 * RANK * RANK * HALF
-
-    def partial_products(groups, *after):
-        values = products(core, generators, solved_gens, rhs, groups, after)
-        return [keep + swap(send, "sub", 0) for keep, send in zip(values[::2], values[1::2])]
+    last = SYM + HALF
 
     def over_child(value):
         for bit in range(1, sub_bits):
@@ -371,30 +403,32 @@
             value = value + swap(value, "rows", bit)
         return value
 
-    (head,) = partial_products((((0, 0), (0, 1)),))
-    (tail,) = partial_products((((0, 2), (0, 3)),), head)
-    (near,) = partial_products((((1, 1), (1, 2), (1, 3)),), tail)
-    head, tail = over_child(head), over_child(tail)
-    (third,) = partial_products((((2, 2), (2, 3)),), tail)
-    near, third = over_child(near), over_child(third)
+    keep, send = products(core, generators, solved_gens, rhs, (((0, 0), (0, 1)),))
+    head = keep + swap(send, "sub", 0)
+    token = swap(call(keep_kernel, struct(8), 0, core, send[:8], after=(head,)), "sub", 0)
+    groups = (((0, 2), (0, 3)), ((1, 1), (1, 2), (1, 3)), ((2, 2), (2, 3)))
+    parts = products(core, generators, solved_gens, rhs, groups, token)
+    parts = [(keep, swap(send, "sub", 0)) for keep, send in zip(parts[::2], parts[1::2])]
+    head = over_child(head)
+    tail = over_child(parts[0][0] + parts[0][1])
+    near = over_child(call(add_kernel, struct(SYM + RANK + HALF), 0, core, *parts[1], after=(tail,)))
+    third = over_child(call(add_kernel, struct(last), 0, core, *parts[2], after=(near,)))
 
     head_sib = swap(head, "rows", span_bits)
     tail_sib = swap(tail, "rows", span_bits)
     head_other = swap(head, "sub", 0)
     tail_other = swap(tail[:RANK], "sub", 0)
-    p_sib_other = swap(head_sib[:RANK], "sub", 0)
+    p_sib_other = swap(head_sib[:SYM], "sub", 0)
     inverted, p_sib = inverse(core, head, head_sib, head_other, p_sib_other)
-    z01, p_own = call(
-        head_kernel, [struct(RANK)] * 2, 3 * flops, core, inverted, p_sib, head, head_sib, head_other, near
-    )
-    z0, r_own = call(
-        tail_kernel, [struct(RANK + HALF)] * 2, 5 * flops,
-        core, inverted, p_sib, tail, tail_sib, head, head_other, near, after=(p_own,),
-    )
-    third = call(third_kernel, struct(RANK + HALF), 2 * flops, core, tail, tail_other, z0, third, after=(r_own,))
-
-    p_own = p_own + swap(p_own, "rows", span_bits)
-    r_own = r_own + swap(r_own, "rows", span_bits)
+    z0, crossed = call(
+        first_kernel, [struct(2 * RANK + HALF), struct(SYM + RANK + HALF)], FIRST_FLOPS,
+        core, inverted, p_sib, head, head_sib, head_other, tail, tail_sib,
+    )
+    near = near - crossed
+    third = call(third_kernel, struct(last), 2 * flops, core, tail, tail_other, z0, third, after=(near,))
+
+    near = near + swap(near, "rows", span_bits)
+    p_own, r_own = near[:SYM], near[SYM:]
     third = third + swap(third, "rows", span_bits)
     p_sib = swap(p_own, "rows", span_bits + 1)
     r_sib = swap(r_own, "rows", span_bits + 1)
@@ -403,26 +437,20 @@
     p_sib_other = swap(p_sib, "sub", 0)
     inverted, p_sib = inverse(core, p_own, p_sib, p_own_other, p_sib_other)
     z1, own = call(
-        middle_kernel, [struct(RANK + HALF)] * 2, 5 * flops,
+        middle_kernel, [struct(RANK + HALF), struct(last)], 5 * flops,
         core, inverted, p_sib, r_own, r_sib, r_own_other, third,
     )
 
-    p_own, r_own = own[:RANK], own[RANK:]
-    p_own = p_own + swap(p_own, "rows", span_bits + 1)
-    p_sib = swap(p_own, "rows", span_bits + 2)
-    r_own = r_own + swap(r_own, "rows", span_bits + 1)
-    r_sib = swap(r_own, "rows", span_bits + 2)
-    small = (z1, swap(z1, "sub", 0), z0, swap(z0, "sub", 0), z01, swap(z01, "sub", 0))
-    high, low, current = reduced(core, small, solved_gens, rhs, r_own)
-    p_sib = call(keep_kernel, struct(RANK), 0, core, p_sib, after=(high,))
-    p_own_other = swap(p_own, "sub", 0)
-    r_own_other = swap(r_own, "sub", 0)
-    p_sib_other = swap(p_sib, "sub", 0)
-    r_sib_other = swap(r_sib, "sub", 0)
-    inverted, p_sib = inverse(core, p_own, p_sib, p_own_other, p_sib_other)
+    own = own + swap(own, "rows", span_bits + 1)
+    sib = swap(own, "rows", span_bits + 2)
+    small = (z1, swap(z1, "sub", 0), z0, swap(z0, "sub", 0))
+    high, low, current = reduced(core, small, solved_gens, rhs, own)
+    sib = call(keep_kernel, struct(last), 0, core, sib, after=(high,))
+    own_other, sib_other = swap(own, "sub", 0), swap(sib, "sub", 0)
+    inverted, p_sib = inverse(core, own, sib, own_other, sib_other)
     return call(
         final_kernel, struct(rhs.shape[0], RHS), 6 * rhs.shape[0] * RANK * RHS,
-        core, inverted, p_sib, r_own, r_own_other, r_sib, r_sib_other, high, low, current,
+        core, inverted, p_sib, own, own_other, sib, sib_other, high, low, current,
     )
 
 

time: 76.2 us -> 74.2 us (0.974)
  the two profiles are of different devices: /device:TPU:7 before, /device:TPU:0 now
where the time goes in v6:
time: 74.2 us; the launch traced here: 74.1 us
  waiting for transfers between devices  28.5 us (38%)
  Pallas kernels  24.6 us (33%)
  starting transfers between devices  20.4 us (27%)
    ppermute x27, waiting for transfers between devices, swap(): return lax.ppermute(value, axis, pairs)  28.5 us
    ppermute x27, starting transfers between devices, swap(): return lax.ppermute(value, axis, pairs)  20.4 us
    pallas_call x2, Pallas kernels, products(): pl.pallas_call(functools.partial(product_kernel, groups), in_specs=[SMEM]...  7.78 us
    pallas_call x3, Pallas kernels, inverse(): pl.pallas_call(invert_kernel, in_specs=[SMEM] + [VMEM] * 4, out_specs=[VM...  7.01 us
    pallas_call x1, Pallas kernels, reduced(): pl.pallas_call(reduced_kernel, in_specs=[SMEM] + [VMEM] * len(small) + [H...  5.15 us
    pallas_call x8, Pallas kernels, call(): pl.pallas_call(kernel, in_specs=[SMEM] + [VMEM] * (len(values) - 1) + [AN...  4.65 us
  transfers between devices with their start and end apart: 27, of which 11 were waited for; matrix products, arithmetic and copies ran while one was open for 0% of the time, Pallas kernels for 24%

profile of v6, /device:TPU:0, one launch (start us, length us, event | category | flops | bytes accessed | tf_op | source)
XLA Modules:
  0.0 74.1 jit_solution(13317543932162775591)
XLA Ops:
  0.0 2.6 %shard_map.37 = (f32[448,128]{1,0:T(8,128)S(1)}, f32[448,128]{1,0:T(8,128)S(1)}) custom-call(s32[1]{0:T(128)} %bitcast.core_ref, f32[3,1024,256]{2,1,0:T(8,128)} %gens_ref.3, f32[3,1024,256]{2,1,0:T(8,128)} %solved_ref.5), custom_call_target="tpu_custom_call" | custom-call | flops 805306368 | bytes 3145728 | tf_op jit(solution)/shard_map/pallas_call | solution.py:199
  2.6 0.5 collective-permute-start
  3.1 1.1 %collective-permute-done = f32[448,128]{1,0:T(8,128)S(1)} collective-permute-done((f32[448,128]{1,0:T(8,128)S(1)}, f32[448,128]{1,0:T(8,128)S(1)}, u32[]{:S(2)}, u32[]{:S(2)}) %collective-permute-start) | collective-permute-done | bytes 229408 | tf_op jit(solution)/shard_map/ppermute | solution.py:31
  4.2 0.4 collective-permute-start.1
  4.7 2.7 %collective-permute-start.6 = (f32[448,128]{1,0:T(8,128)S(1)}, f32[448,128]{1,0:T(8,128)S(1)}, u32[]{:S(2)}, u32[]{:S(2)}) collective-permute-start(f32[448,128]{1,0:T(8,128)S(1)} %add.32.refs_0_), channel_id=1, source_target_pairs={{0,2},{1,3},{2,0},{3,1},{4,6},{5,7},{6,4},{7,5},{8,10},{9,11},{10,... | collective-permute-start | bytes 688136 | tf_op jit(solution)/shard_map/ppermute | solution.py:31
  7.3 0.0 collective-permute-done.1.refs_1_
  7.4 5.2 %shard_map.39 = (f32[384,128]{1,0:T(8,128)S(1)}, f32[384,128]{1,0:T(8,128)S(1)}, f32[576,128]{1,0:T(8,128)S(1)}, f32[576,128]{1,0:T(8,128)S(1)}, f32[320,128]{1,0:T(8,128)S(1)}, /*index=5*/f32[320,128]{1,0:T(8,128)S(1)}) custom-call(s32[1]{0:T(128)} %bitcast.core_ref, f32[3,1024,256]{2,1,0:T(8,128)} %gens_ref.3, f32[3,1024,256]{2,1,0:T(8,128)} %solved_ref.5, ...), custom_call_target="tpu_custom_call" | custom-call | flops 2214592512 | bytes 6291456 | tf_op jit(solution)/shard_map/pallas_call | solution.py:199
  12.6 0.1 collective-permute-start.3
  12.7 0.7 collective-permute-done.6
  13.5 1.8 %collective-permute-start.7 = (f32[448,128]{1,0:T(8,128)S(1)}, f32[448,128]{1,0:T(8,128)S(1)}, u32[]{:S(2)}, u32[]{:S(2)}) collective-permute-start(f32[448,128]{1,0:T(8,128)S(1)} %add.36.own_ref.head_ref), channel_id=1, source_target_pairs={{0,4},{4,0},{8,12},{12,8},{16,20},{20,16},{24,28},{28,24},{1,5},{5... | collective-permute-start | bytes 688136 | tf_op jit(solution)/shard_map/ppermute | solution.py:31
  15.3 0.0 collective-permute-done.3
  15.3 1.6 %collective-permute-start.4 = (f32[384,128]{1,0:T(8,128)S(1)}, f32[384,128]{1,0:T(8,128)S(1)}, u32[]{:S(2)}, u32[]{:S(2)}) collective-permute-start(f32[384,128]{1,0:T(8,128)S(1)} %add.33), channel_id=1, source_target_pairs={{0,2},{1,3},{2,0},{3,1},{4,6},{5,7},{6,4},{7,5},{8,10},{9,11},{10,... | collective-permute-start | bytes 589832 | tf_op jit(solution)/shard_map/ppermute | solution.py:31
  16.9 0.0 collective-permute-start.2
  16.9 0.5 collective-permute-start.8
  17.4 4.0 %collective-permute-done.4 = f32[384,128]{1,0:T(8,128)S(1)} collective-permute-done((f32[384,128]{1,0:T(8,128)S(1)}, f32[384,128]{1,0:T(8,128)S(1)}, u32[]{:S(2)}, u32[]{:S(2)}) %collective-permute-start.4) | collective-permute-done | bytes 196640 | tf_op jit(solution)/shard_map/ppermute | solution.py:31
  21.5 1.2 %collective-permute-start.10 = (f32[384,128]{1,0:T(8,128)S(1)}, f32[384,128]{1,0:T(8,128)S(1)}, u32[]{:S(2)}, u32[]{:S(2)}) collective-permute-start(f32[384,128]{1,0:T(8,128)S(1)} %add.34.refs_0_.tail_ref.own_ref), channel_id=1, source_target_pairs={{0,4},{4,0},{8,12},{12,8},{16,20},{20,16},{24,28},{28,24},{1,5},{5... | collective-permute-start | bytes 589832 | tf_op jit(solution)/shard_map/ppermute | solution.py:31
  22.7 0.0 collective-permute-done.7.sib_ref.head_sib_ref
  22.7 0.1 collective-permute-start.9
  22.8 0.5 collective-permute-start.18
  23.3 0.0 collective-permute-done.2.second_ref
  23.4 1.1 %collective-permute-start.5 = (f32[576,128]{1,0:T(8,128)S(1)}, f32[576,128]{1,0:T(8,128)S(1)}, u32[]{:S(2)}, u32[]{:S(2)}) collective-permute-start(f32[576,128]{1,0:T(8,128)S(1)} %shard_map.40), channel_id=1, source_target_pairs={{0,2},{1,3},{2,0},{3,1},{4,6},{5,7},{6,4},{7,5},{8,10},{9,11},{10,... | collective-permute-start | bytes 884744 | tf_op jit(solution)/shard_map/ppermute | solution.py:31
  24.5 0.0 collective-permute-done.8.own_other_ref.head_other_ref
  24.5 0.0 collective-permute-done.9.sib_other_ref
  24.5 2.3 %shard_map.41 = (f32[256,256]{1,0:T(8,128)S(1)}, f32[256,256]{1,0:T(8,128)S(1)}) custom-call(s32[1]{0:T(128)} %bitcast.core_ref, f32[448,128]{1,0:T(8,128)S(1)} %add.36.own_ref.head_ref, f32[448,128]{1,0:T(8,128)S(1)} %collective-permute-done.7.sib_ref.head_sib_ref, f32[448,128]{1,0:T(8,128)S(1)} %collective-permute-done.8.own_other_ref.head_other_ref, ...), custom_call_target="tpu_custom_call" | custom-call | flops 905969664 | bytes 1048576 | tf_op jit(solution)/shard_map/pallas_call | solution.py:276
  26.8 0.5 collective-permute-done.10.tail_sib_ref
  27.2 1.1 %shard_map.42 = (f32[640,128]{1,0:T(8,128)S(1)}, f32[576,128]{1,0:T(8,128)S(1)}) custom-call(s32[1]{0:T(128)} %bitcast.core_ref, f32[256,256]{1,0:T(8,128)S(1)} %get-tuple-element.32.inverse_ref, f32[256,256]{1,0:T(8,128)S(1)} %get-tuple-element.33.p_sib_ref, f32[448,128]{1,0:T(8,128)S(1)} %add.36.own_ref.head_ref, ...), custom_call_target="tpu_custom_call" | custom-call | flops 6000000000 | bytes 2228228 | tf_op jit(solution)/shard_map/pallas_call | solution.py:265
  28.4 4.1 %collective-permute-done.5 = f32[576,128]{1,0:T(8,128)S(1)} collective-permute-done((f32[576,128]{1,0:T(8,128)S(1)}, f32[576,128]{1,0:T(8,128)S(1)}, u32[]{:S(2)}, u32[]{:S(2)}) %collective-permute-start.5) | collective-permute-done | bytes 294944 | tf_op jit(solution)/shard_map/ppermute | solution.py:31
  32.4 0.1 fusion
  32.5 0.9 %collective-permute-start.11 = (f32[576,128]{1,0:T(8,128)S(1)}, f32[576,128]{1,0:T(8,128)S(1)}, u32[]{:S(2)}, u32[]{:S(2)}) collective-permute-start(f32[576,128]{1,0:T(8,128)S(1)} %get-tuple-element.47.refs_0_), channel_id=1, source_target_pairs={{0,4},{4,0},{8,12},{12,8},{16,20},{20,16},{24,28},{28,24},{1,5},{5... | collective-permute-start | bytes 884744 | tf_op jit(solution)/shard_map/ppermute | solution.py:31
  33.4 0.0 collective-permute-done.18.second_ref
  33.4 1.6 %collective-permute-start.19 = (f32[320,128]{1,0:T(8,128)S(1)}, f32[320,128]{1,0:T(8,128)S(1)}, u32[]{:S(2)}, u32[]{:S(2)}) collective-permute-start(f32[320,128]{1,0:T(8,128)S(1)} %shard_map.44), channel_id=1, source_target_pairs={{0,2},{1,3},{2,0},{3,1},{4,6},{5,7},{6,4},{7,5},{8,10},{9,11},{10,... | collective-permute-start | bytes 491528 | tf_op jit(solution)/shard_map/ppermute | solution.py:31
  35.0 0.1 collective-permute-start.17
  35.1 5.6 %collective-permute-done.11 = f32[576,128]{1,0:T(8,128)S(1)} collective-permute-done((f32[576,128]{1,0:T(8,128)S(1)}, f32[576,128]{1,0:T(8,128)S(1)}, u32[]{:S(2)}, u32[]{:S(2)}) %collective-permute-start.11) | collective-permute-done | bytes 294944 | tf_op jit(solution)/shard_map/ppermute | solution.py:31
  40.7 1.6 %collective-permute-start.12 = (f32[192,128]{1,0:T(8,128)S(1)}, f32[192,128]{1,0:T(8,128)S(1)}, u32[]{:S(2)}, u32[]{:S(2)}) collective-permute-start(f32[192,128]{1,0:T(8,128)S(1)} %slice.26.own_ref), channel_id=1, source_target_pairs={{0,8},{4,12},{8,0},{12,4},{16,24},{20,28},{24,16},{28,20},{1,9},{5... | collective-permute-start | bytes 294920 | tf_op jit(solution)/shard_map/ppermute | solution.py:31
  42.4 0.0 collective-permute-done.19
  42.4 0.0 collective-permute-done.17.own_other_ref
  42.4 0.4 shard_map.45
  42.8 0.9 %collective-permute-start.20 = (f32[320,128]{1,0:T(8,128)S(1)}, f32[320,128]{1,0:T(8,128)S(1)}, u32[]{:S(2)}, u32[]{:S(2)}) collective-permute-start(f32[320,128]{1,0:T(8,128)S(1)} %shard_map.45), channel_id=1, source_target_pairs={{0,4},{4,0},{8,12},{12,8},{16,20},{20,16},{24,28},{28,24},{1,5},{5... | collective-permute-start | bytes 491528 | tf_op jit(solution)/shard_map/ppermute | solution.py:31
  43.8 0.5 collective-permute-start.15
  44.3 0.0 collective-permute-start.13
  44.3 2.2 %collective-permute-done.12.sib_ref = f32[192,128]{1,0:T(8,128)S(1)} collective-permute-done((f32[192,128]{1,0:T(8,128)S(1)}, f32[192,128]{1,0:T(8,128)S(1)}, u32[]{:S(2)}, u32[]{:S(2)}) %collective-permute-start.12) | collective-permute-done | bytes 98336 | tf_op jit(solution)/shard_map/ppermute | solution.py:31
  46.5 0.0 collective-permute-start.14
  46.5 0.6 collective-permute-start.16
  47.1 1.1 %collective-permute-done.20 = f32[320,128]{1,0:T(8,128)S(1)} collective-permute-done((f32[320,128]{1,0:T(8,128)S(1)}, f32[320,128]{1,0:T(8,128)S(1)}, u32[]{:S(2)}, u32[]{:S(2)}) %collective-permute-start.20) | collective-permute-done | bytes 163872 | tf_op jit(solution)/shard_map/ppermute | solution.py:31
  48.2 0.0 collective-permute-start.24
  48.2 0.0 collective-permute-done.13.own_other_ref
  48.2 0.0 collective-permute-done.14.sib_other_ref
  48.2 2.5 %shard_map.43 = (f32[256,256]{1,0:T(8,128)S(1)}, f32[256,256]{1,0:T(8,128)S(1)}) custom-call(s32[1]{0:T(128)} %bitcast.core_ref, f32[192,128]{1,0:T(8,128)S(1)} %slice.26.own_ref, f32[192,128]{1,0:T(8,128)S(1)} %collective-permute-done.12.sib_ref, f32[192,128]{1,0:T(8,128)S(1)} %collective-permute-done.13.own_other_ref, ...), custom_call_target="tpu_custom_call" | custom-call | flops 905969664 | bytes 1048576 | tf_op jit(solution)/shard_map/pallas_call | solution.py:276
  50.7 0.0 collective-permute-done.16.own_other_ref
  50.7 0.0 collective-permute-done.15.sib_ref
  50.7 1.1 %shard_map.46 = (f32[384,128]{1,0:T(8,128)S(1)}, f32[320,128]{1,0:T(8,128)S(1)}) custom-call(s32[1]{0:T(128)} %bitcast.core_ref, f32[256,256]{1,0:T(8,128)S(1)} %get-tuple-element.35.inverse_ref, f32[256,256]{1,0:T(8,128)S(1)} %get-tuple-element.36.p_sib_ref, f32[384,128]{1,0:T(8,128)S(1)} %slice.27.own_ref, f32[384,128]{1,0:T(8,128)S(1)} %collective-permute-done.15.sib_ref, ...), custom_call_target="tpu_custom_call" | custom-call | flops 251658240 | bytes 1572868 | tf_op jit(solution)/shard_map/pallas_call | solution.py:265
  51.8 0.9 %collective-permute-start.21 = (f32[320,128]{1,0:T(8,128)S(1)}, f32[320,128]{1,0:T(8,128)S(1)}, u32[]{:S(2)}, u32[]{:S(2)}) collective-permute-start(f32[320,128]{1,0:T(8,128)S(1)} %get-tuple-element.40), channel_id=1, source_target_pairs={{0,8},{4,12},{8,0},{12,4},{16,24},{20,28},{24,16},{28,20},{1,9},{5... | collective-permute-start | bytes 491528 | tf_op jit(solution)/shard_map/ppermute | solution.py:31
  52.7 0.0 collective-permute-start.23
  52.7 5.8 %collective-permute-done.21 = f32[320,128]{1,0:T(8,128)S(1)} collective-permute-done((f32[320,128]{1,0:T(8,128)S(1)}, f32[320,128]{1,0:T(8,128)S(1)}, u32[]{:S(2)}, u32[]{:S(2)}) %collective-permute-start.21) | collective-permute-done | bytes 163872 | tf_op jit(solution)/shard_map/ppermute | solution.py:31
  58.5 2.7 %collective-permute-start.22 = (f32[320,128]{1,0:T(8,128)S(1)}, f32[320,128]{1,0:T(8,128)S(1)}, u32[]{:S(2)}, u32[]{:S(2)}) collective-permute-start(f32[320,128]{1,0:T(8,128)S(1)} %add.40.refs_0_.own_ref), channel_id=1, source_target_pairs={{0,16},{4,20},{8,24},{12,28},{16,0},{20,4},{24,8},{28,12},{1,17},{... | collective-permute-start | bytes 491528 | tf_op jit(solution)/shard_map/ppermute | solution.py:31
  61.2 0.0 collective-permute-start.25
  61.2 5.1 %shard_map.47 = (bf16[1024,256]{1,0:T(8,128)(2,1)S(1)}, bf16[1024,256]{1,0:T(8,128)(2,1)}, f32[1024,128]{1,0:T(8,128)}) custom-call(s32[1]{0:T(128)} %bitcast.core_ref, f32[384,128]{1,0:T(8,128)S(1)} %get-tuple-element.41.z1_ref, f32[384,128]{1,0:T(8,128)S(1)} %collective-permute-done.23.z1_other_ref, f32[640,128]{1,0:T(8,128)S(1)} %get-tuple-element.37.z_ref.z0_ref, ...), custom_call_target="tpu_custom_call" | custom-call | flops 1207959552 | bytes 5242880 | tf_op jit(solution)/shard_map/pallas_call | solution.py:358
  66.3 0.0 copy-start.1
  66.3 2.0 %collective-permute-done.22.value_ref = f32[320,128]{1,0:T(8,128)S(1)} collective-permute-done((f32[320,128]{1,0:T(8,128)S(1)}, f32[320,128]{1,0:T(8,128)S(1)}, u32[]{:S(2)}, u32[]{:S(2)}) %collective-permute-start.22) | collective-permute-done | bytes 163872 | tf_op jit(solution)/shard_map/ppermute | solution.py:31
  68.3 0.1 collective-permute-start.26
  68.4 0.0 collective-permute-done.25.own_other_ref
  68.4 1.4 %collective-permute-done.26.sib_other_ref = f32[320,128]{1,0:T(8,128)S(1)} collective-permute-done((f32[320,128]{1,0:T(8,128)S(1)}, f32[320,128]{1,0:T(8,128)S(1)}, u32[]{:S(2)}, u32[]{:S(2)}) %collective-permute-start.26) | collective-permute-done | bytes 163872 | tf_op jit(solution)/shard_map/ppermute | solution.py:31
  69.8 2.3 %shard_map.49 = (f32[256,256]{1,0:T(8,128)S(1)}, f32[256,256]{1,0:T(8,128)S(1)}) custom-call(s32[1]{0:T(128)} %bitcast.core_ref, f32[320,128]{1,0:T(8,128)S(1)} %add.40.refs_0_.own_ref, f32[320,128]{1,0:T(8,128)S(1)} %shard_map.48.sib_ref, f32[320,128]{1,0:T(8,128)S(1)} %collective-permute-done.25.own_other_ref, ...), custom_call_target="tpu_custom_call" | custom-call | flops 905969664 | bytes 1048576 | tf_op jit(solution)/shard_map/pallas_call | solution.py:276
  72.1 2.0 %shard_map.50 = f32[1024,128]{1,0:T(8,128)} custom-call(s32[1]{0:T(128)} %bitcast.core_ref, f32[256,256]{1,0:T(8,128)S(1)} %get-tuple-element.43.inverse_ref, f32[256,256]{1,0:T(8,128)S(1)} %get-tuple-element.44.p_sib_ref, f32[320,128]{1,0:T(8,128)S(1)} %add.40.refs_0_.own_ref, f32[320,128]{1,0:T(8,128)S(1)} %collective-permute-done.25.own_other_ref, ...), custom_call_target="tpu_custom_call" | custom-call | flops 201326592 | bytes 4325380 | tf_op jit(solution)/shard_map/pallas_call | solution.py:265
  (25 shorter events, 0.3 us)
Async XLA Ops:
  0.0 7.3 %copy-start = (f32[1024,128]{1,0:T(8,128)S(1)}, f32[1024,128]{1,0:T(8,128)}, u32[]{:S(2)}) copy-start(f32[1024,128]{1,0:T(8,128)} %rhs_ref.1) | copy-start | bytes 1572868
  2.6 1.6 %collective-permute-start = (f32[448,128]{1,0:T(8,128)S(1)}, f32[448,128]{1,0:T(8,128)S(1)}, u32[]{:S(2)}, u32[]{:S(2)}) collective-permute-start(f32[448,128]{1,0:T(8,128)S(1)} %get-tuple-element.26), channel_id=1, source_target_pairs={{0,1},{1,0},{2,3},{3,2},{4,5},{5,4},{6,7},{7,6},{8,9},{9,8},{10,11... | collective-permute-start | bytes 688136 | tf_op jit(solution)/shard_map/ppermute | solution.py:31
  4.2 3.1 %collective-permute-start.1 = (f32[8,128]{1,0:T(8,128)S(1)}, f32[8,128]{1,0:T(8,128)S(1)}, u32[]{:S(2)}, u32[]{:S(2)}) collective-permute-start(f32[8,128]{1,0:T(8,128)S(1)} %shard_map.38), channel_id=1, source_target_pairs={{0,1},{1,0},{2,3},{3,2},{4,5},{5,4},{6,7},{7,6},{8,9},{9,8},{10,11... | collective-permute-start | bytes 12296 | tf_op jit(solution)/shard_map/ppermute | solution.py:31
  4.7 8.8 %collective-permute-start.6 = (f32[448,128]{1,0:T(8,128)S(1)}, f32[448,128]{1,0:T(8,128)S(1)}, u32[]{:S(2)}, u32[]{:S(2)}) collective-permute-start(f32[448,128]{1,0:T(8,128)S(1)} %add.32.refs_0_), channel_id=1, source_target_pairs={{0,2},{1,3},{2,0},{3,1},{4,6},{5,7},{6,4},{7,5},{8,10},{9,11},{10,... | collective-permute-start | bytes 688136 | tf_op jit(solution)/shard_map/ppermute | solution.py:31
  12.6 2.7 %collective-permute-start.3 = (f32[384,128]{1,0:T(8,128)S(1)}, f32[384,128]{1,0:T(8,128)S(1)}, u32[]{:S(2)}, u32[]{:S(2)}) collective-permute-start(f32[384,128]{1,0:T(8,128)S(1)} %get-tuple-element.31), channel_id=1, source_target_pairs={{0,1},{1,0},{2,3},{3,2},{4,5},{5,4},{6,7},{7,6},{8,9},{9,8},{10,11... | collective-permute-start | bytes 589832 | tf_op jit(solution)/shard_map/ppermute | solution.py:31
  13.5 9.2 %collective-permute-start.7 = (f32[448,128]{1,0:T(8,128)S(1)}, f32[448,128]{1,0:T(8,128)S(1)}, u32[]{:S(2)}, u32[]{:S(2)}) collective-permute-start(f32[448,128]{1,0:T(8,128)S(1)} %add.36.own_ref.head_ref), channel_id=1, source_target_pairs={{0,4},{4,0},{8,12},{12,8},{16,20},{20,16},{24,28},{28,24},{1,5},{5... | collective-permute-start | bytes 688136 | tf_op jit(solution)/shard_map/ppermute | solution.py:31
  15.3 6.1 %collective-permute-start.4 = (f32[384,128]{1,0:T(8,128)S(1)}, f32[384,128]{1,0:T(8,128)S(1)}, u32[]{:S(2)}, u32[]{:S(2)}) collective-permute-start(f32[384,128]{1,0:T(8,128)S(1)} %add.33), channel_id=1, source_target_pairs={{0,2},{1,3},{2,0},{3,1},{4,6},{5,7},{6,4},{7,5},{8,10},{9,11},{10,... | collective-permute-start | bytes 589832 | tf_op jit(solution)/shard_map/ppermute | solution.py:31
  16.9 6.4 %collective-permute-start.2 = (f32[576,128]{1,0:T(8,128)S(1)}, f32[576,128]{1,0:T(8,128)S(1)}, u32[]{:S(2)}, u32[]{:S(2)}) collective-permute-start(f32[576,128]{1,0:T(8,128)S(1)} %get-tuple-element.29), channel_id=1, source_target_pairs={{0,1},{1,0},{2,3},{3,2},{4,5},{5,4},{6,7},{7,6},{8,9},{9,8},{10,11... | collective-permute-start | bytes 884744 | tf_op jit(solution)/shard_map/ppermute | solution.py:31
  16.9 7.6 %collective-permute-start.8 = (f32[448,128]{1,0:T(8,128)S(1)}, f32[448,128]{1,0:T(8,128)S(1)}, u32[]{:S(2)}, u32[]{:S(2)}) collective-permute-start(f32[448,128]{1,0:T(8,128)S(1)} %add.36.own_ref.head_ref), channel_id=1, source_target_pairs={{0,1},{1,0},{2,3},{3,2},{4,5},{5,4},{6,7},{7,6},{8,9},{9,8},{10,11... | collective-permute-start | bytes 688136 | tf_op jit(solution)/shard_map/ppermute | solution.py:31
  21.5 5.7 %collective-permute-start.10 = (f32[384,128]{1,0:T(8,128)S(1)}, f32[384,128]{1,0:T(8,128)S(1)}, u32[]{:S(2)}, u32[]{:S(2)}) collective-permute-start(f32[384,128]{1,0:T(8,128)S(1)} %add.34.refs_0_.tail_ref.own_ref), channel_id=1, source_target_pairs={{0,4},{4,0},{8,12},{12,8},{16,20},{20,16},{24,28},{28,24},{1,5},{5... | collective-permute-start | bytes 589832 | tf_op jit(solution)/shard_map/ppermute | solution.py:31
  22.7 1.7 %collective-permute-start.9 = (f32[192,128]{1,0:T(8,128)S(1)}, f32[192,128]{1,0:T(8,128)S(1)}, u32[]{:S(2)}, u32[]{:S(2)}) collective-permute-start(f32[192,128]{1,0:T(8,128)S(1)} %slice.25), channel_id=1, source_target_pairs={{0,1},{1,0},{2,3},{3,2},{4,5},{5,4},{6,7},{7,6},{8,9},{9,8},{10,11... | collective-permute-start | bytes 294920 | tf_op jit(solution)/shard_map/ppermute | solution.py:31
  22.8 10.6 %collective-permute-start.18 = (f32[320,128]{1,0:T(8,128)S(1)}, f32[320,128]{1,0:T(8,128)S(1)}, u32[]{:S(2)}, u32[]{:S(2)}) collective-permute-start(f32[320,128]{1,0:T(8,128)S(1)} %get-tuple-element.39), channel_id=1, source_target_pairs={{0,1},{1,0},{2,3},{3,2},{4,5},{5,4},{6,7},{7,6},{8,9},{9,8},{10,11... | collective-permute-start | bytes 491528 | tf_op jit(solution)/shard_map/ppermute | solution.py:31
  23.4 9.1 %collective-permute-start.5 = (f32[576,128]{1,0:T(8,128)S(1)}, f32[576,128]{1,0:T(8,128)S(1)}, u32[]{:S(2)}, u32[]{:S(2)}) collective-permute-start(f32[576,128]{1,0:T(8,128)S(1)} %shard_map.40), channel_id=1, source_target_pairs={{0,2},{1,3},{2,0},{3,1},{4,6},{5,7},{6,4},{7,5},{8,10},{9,11},{10,... | collective-permute-start | bytes 884744 | tf_op jit(solution)/shard_map/ppermute | solution.py:31
  32.5 8.2 %collective-permute-start.11 = (f32[576,128]{1,0:T(8,128)S(1)}, f32[576,128]{1,0:T(8,128)S(1)}, u32[]{:S(2)}, u32[]{:S(2)}) collective-permute-start(f32[576,128]{1,0:T(8,128)S(1)} %get-tuple-element.47.refs_0_), channel_id=1, source_target_pairs={{0,4},{4,0},{8,12},{12,8},{16,20},{20,16},{24,28},{28,24},{1,5},{5... | collective-permute-start | bytes 884744 | tf_op jit(solution)/shard_map/ppermute | solution.py:31
  33.4 9.0 %collective-permute-start.19 = (f32[320,128]{1,0:T(8,128)S(1)}, f32[320,128]{1,0:T(8,128)S(1)}, u32[]{:S(2)}, u32[]{:S(2)}) collective-permute-start(f32[320,128]{1,0:T(8,128)S(1)} %shard_map.44), channel_id=1, source_target_pairs={{0,2},{1,3},{2,0},{3,1},{4,6},{5,7},{6,4},{7,5},{8,10},{9,11},{10,... | collective-permute-start | bytes 491528 | tf_op jit(solution)/shard_map/ppermute | solution.py:31
  35.0 7.4 %collective-permute-start.17 = (f32[256,128]{1,0:T(8,128)S(1)}, f32[256,128]{1,0:T(8,128)S(1)}, u32[]{:S(2)}, u32[]{:S(2)}) collective-permute-start(f32[256,128]{1,0:T(8,128)S(1)} %slice.29), channel_id=1, source_target_pairs={{0,1},{1,0},{2,3},{3,2},{4,5},{5,4},{6,7},{7,6},{8,9},{9,8},{10,11... | collective-permute-start | bytes 393224 | tf_op jit(solution)/shard_map/ppermute | solution.py:31
  40.7 5.7 %collective-permute-start.12 = (f32[192,128]{1,0:T(8,128)S(1)}, f32[192,128]{1,0:T(8,128)S(1)}, u32[]{:S(2)}, u32[]{:S(2)}) collective-permute-start(f32[192,128]{1,0:T(8,128)S(1)} %slice.26.own_ref), channel_id=1, source_target_pairs={{0,8},{4,12},{8,0},{12,4},{16,24},{20,28},{24,16},{28,20},{1,9},{5... | collective-permute-start | bytes 294920 | tf_op jit(solution)/shard_map/ppermute | solution.py:31
  42.8 5.4 %collective-permute-start.20 = (f32[320,128]{1,0:T(8,128)S(1)}, f32[320,128]{1,0:T(8,128)S(1)}, u32[]{:S(2)}, u32[]{:S(2)}) collective-permute-start(f32[320,128]{1,0:T(8,128)S(1)} %shard_map.45), channel_id=1, source_target_pairs={{0,4},{4,0},{8,12},{12,8},{16,20},{20,16},{24,28},{28,24},{1,5},{5... | collective-permute-start | bytes 491528 | tf_op jit(solution)/shard_map/ppermute | solution.py:31
  43.8 7.0 %collective-permute-start.15 = (f32[384,128]{1,0:T(8,128)S(1)}, f32[384,128]{1,0:T(8,128)S(1)}, u32[]{:S(2)}, u32[]{:S(2)}) collective-permute-start(f32[384,128]{1,0:T(8,128)S(1)} %slice.27.own_ref), channel_id=1, source_target_pairs={{0,8},{4,12},{8,0},{12,4},{16,24},{20,28},{24,16},{28,20},{1,9},{5... | collective-permute-start | bytes 589832 | tf_op jit(solution)/shard_map/ppermute | solution.py:31
  44.3 4.0 %collective-permute-start.13 = (f32[192,128]{1,0:T(8,128)S(1)}, f32[192,128]{1,0:T(8,128)S(1)}, u32[]{:S(2)}, u32[]{:S(2)}) collective-permute-start(f32[192,128]{1,0:T(8,128)S(1)} %slice.26.own_ref), channel_id=1, source_target_pairs={{0,1},{1,0},{2,3},{3,2},{4,5},{5,4},{6,7},{7,6},{8,9},{9,8},{10,11... | collective-permute-start | bytes 294920 | tf_op jit(solution)/shard_map/ppermute | solution.py:31
  46.5 1.8 %collective-permute-start.14 = (f32[192,128]{1,0:T(8,128)S(1)}, f32[192,128]{1,0:T(8,128)S(1)}, u32[]{:S(2)}, u32[]{:S(2)}) collective-permute-start(f32[192,128]{1,0:T(8,128)S(1)} %collective-permute-done.12.sib_ref), channel_id=1, source_target_pairs={{0,1},{1,0},{2,3},{3,2},{4,5},{5,4},{6,7},{7,6},{8,9},{9,8},{10,11... | collective-permute-start | bytes 294920 | tf_op jit(solution)/shard_map/ppermute | solution.py:31
  46.5 4.2 %collective-permute-start.16 = (f32[256,128]{1,0:T(8,128)S(1)}, f32[256,128]{1,0:T(8,128)S(1)}, u32[]{:S(2)}, u32[]{:S(2)}) collective-permute-start(f32[256,128]{1,0:T(8,128)S(1)} %slice.28), channel_id=1, source_target_pairs={{0,1},{1,0},{2,3},{3,2},{4,5},{5,4},{6,7},{7,6},{8,9},{9,8},{10,11... | collective-permute-start | bytes 393224 | tf_op jit(solution)/shard_map/ppermute | solution.py:31
  48.2 13.0 %collective-permute-start.24 = (f32[640,128]{1,0:T(8,128)S(1)}, f32[640,128]{1,0:T(8,128)S(1)}, u32[]{:S(2)}, u32[]{:S(2)}) collective-permute-start(f32[640,128]{1,0:T(8,128)S(1)} %get-tuple-element.37.z_ref.z0_ref), channel_id=1, source_target_pairs={{0,1},{1,0},{2,3},{3,2},{4,5},{5,4},{6,7},{7,6},{8,9},{9,8},{10,11... | collective-permute-start | bytes 983048 | tf_op jit(solution)/shard_map/ppermute | solution.py:31
  51.8 6.7 %collective-permute-start.21 = (f32[320,128]{1,0:T(8,128)S(1)}, f32[320,128]{1,0:T(8,128)S(1)}, u32[]{:S(2)}, u32[]{:S(2)}) collective-permute-start(f32[320,128]{1,0:T(8,128)S(1)} %get-tuple-element.40), channel_id=1, source_target_pairs={{0,8},{4,12},{8,0},{12,4},{16,24},{20,28},{24,16},{28,20},{1,9},{5... | collective-permute-start | bytes 491528 | tf_op jit(solution)/shard_map/ppermute | solution.py:31
  52.7 8.5 %collective-permute-start.23 = (f32[384,128]{1,0:T(8,128)S(1)}, f32[384,128]{1,0:T(8,128)S(1)}, u32[]{:S(2)}, u32[]{:S(2)}) collective-permute-start(f32[384,128]{1,0:T(8,128)S(1)} %get-tuple-element.41.z1_ref), channel_id=1, source_target_pairs={{0,1},{1,0},{2,3},{3,2},{4,5},{5,4},{6,7},{7,6},{8,9},{9,8},{10,11... | collective-permute-start | bytes 589832 | tf_op jit(solution)/shard_map/ppermute | solution.py:31
  58.5 9.8 %collective-permute-start.22 = (f32[320,128]{1,0:T(8,128)S(1)}, f32[320,128]{1,0:T(8,128)S(1)}, u32[]{:S(2)}, u32[]{:S(2)}) collective-permute-start(f32[320,128]{1,0:T(8,128)S(1)} %add.40.refs_0_.own_ref), channel_id=1, source_target_pairs={{0,16},{4,20},{8,24},{12,28},{16,0},{20,4},{24,8},{28,12},{1,17},{... | collective-permute-start | bytes 491528 | tf_op jit(solution)/shard_map/ppermute | solution.py:31
  61.2 7.3 %collective-permute-start.25 = (f32[320,128]{1,0:T(8,128)S(1)}, f32[320,128]{1,0:T(8,128)S(1)}, u32[]{:S(2)}, u32[]{:S(2)}) collective-permute-start(f32[320,128]{1,0:T(8,128)S(1)} %add.40.refs_0_.own_ref), channel_id=1, source_target_pairs={{0,1},{1,0},{2,3},{3,2},{4,5},{5,4},{6,7},{7,6},{8,9},{9,8},{10,11... | collective-permute-start | bytes 491528 | tf_op jit(solution)/shard_map/ppermute | solution.py:31
  66.3 5.8 %copy-start.1 = (bf16[1024,256]{1,0:T(8,128)(2,1)S(1)}, bf16[1024,256]{1,0:T(8,128)(2,1)}, u32[]{:S(2)}) copy-start(bf16[1024,256]{1,0:T(8,128)(2,1)} %get-tuple-element.45.low_ref) | copy-start | bytes 1572868
  66.3 5.7 %copy-start.2 = (f32[1024,128]{1,0:T(8,128)S(1)}, f32[1024,128]{1,0:T(8,128)}, u32[]{:S(2)}) copy-start(f32[1024,128]{1,0:T(8,128)} %get-tuple-element.46.rhs_ref) | copy-start | bytes 1572868
  68.3 1.5 %collective-permute-start.26 = (f32[320,128]{1,0:T(8,128)S(1)}, f32[320,128]{1,0:T(8,128)S(1)}, u32[]{:S(2)}, u32[]{:S(2)}) collective-permute-start(f32[320,128]{1,0:T(8,128)S(1)} %shard_map.48.sib_ref), channel_id=1, source_target_pairs={{0,1},{1,0},{2,3},{3,2},{4,5},{5,4},{6,7},{7,6},{8,9},{9,8},{10,11... | collective-permute-start | bytes 491528 | tf_op jit(solution)/shard_map/ppermute | solution.py:31

commit v7 on v6

--- a/solution.py
+++ b/solution.py
@@ -14,8 +14,8 @@
 SYM = HALF + QUARTER
 TOLERANCE = 1e-7
 DIVERGED = 1e4
-SCALE = 1
-FIRST_FLOPS = 6e9
+FIRST_FLOPS = 6.5e8
+THIRD_FLOPS = 3e9
 VMEM_LIMIT = 40 * 2**20
 STREAM_LIMIT = 52 * 2**20
 
@@ -36,7 +36,7 @@
 
 
 def cost(flops, floats):
-    return pl.CostEstimate(flops=int(flops / SCALE), bytes_accessed=int(4 * floats / SCALE), transcendentals=0)
+    return pl.CostEstimate(flops=int(flops), bytes_accessed=int(4 * floats), transcendentals=0)
 
 
 def split(value):
@@ -111,23 +111,17 @@
 
 
 def product_kernel(groups, core_ref, gens_ref, solved_ref, *refs):
-    gens, solved, rhs, total, sems = refs[-5:]
-    outs = refs[-5 - 2 * len(groups) : -5]
-    pairs, lefts, rights = needed(groups)
+    gens, solved, total, sems = refs[-4:]
+    outs = refs[-4 - 2 * len(groups) : -4]
+    blocks, lefts, rights = needed(groups)
     rhs_ref = refs[0] if 3 in rights else None
     chunks = sems.shape[1]
     block = gens.shape[1] // chunks
     copies = []
     for chunk in range(chunks):
         rows = pl.ds(chunk * block, block)
-        row = []
-        for place, level in enumerate(lefts):
-            row.append((gens_ref.at[level, rows], gens.at[place, rows]))
-        for place, level in enumerate(rights):
-            if level < 3:
-                row.append((solved_ref.at[level, rows], solved.at[place, rows]))
-            else:
-                row.append((rhs_ref.at[rows], rhs.at[rows]))
+        row = [(gens_ref.at[level, rows], gens.at[place, rows]) for place, level in enumerate(lefts)]
+        row += [(solved_ref.at[level, rows], solved.at[place, rows]) for place, level in enumerate(rights) if level < 3]
         row = [pltpu.make_async_copy(*ends, sems.at[index, chunk]) for index, ends in enumerate(row)]
         for copy in row:
             copy.start()
@@ -139,35 +133,37 @@
             copy.wait()
         right = {}
         for place, level in enumerate(rights):
-            right[level] = split(rhs[rows, :] if level == 3 else solved[place, rows, :])
+            right[level] = split(rhs_ref[rows, :] if level == 3 else solved[place, rows, :])
+        left = [[part.T for part in split(gens[place, rows, :])] for place in range(len(lefts))]
         start = 0
-        for place, level in enumerate(lefts):
-            left = [part.T for part in split(gens[place, rows, :])]
-            wanted = [second for first, second in pairs if first == level]
-            value = dot_parts(left, [jnp.concatenate([right[second][half] for second in wanted], axis=1) for half in (0, 1)])
-            for second in wanted:
-                places[level, second] = start
-                start += width_of(second)
-            cols = slice(start - value.shape[1], start)
+        for firsts, seconds in blocks:
+            value = dot_parts(
+                [jnp.concatenate([left[lefts.index(level)][half] for level in firsts], axis=0) for half in (0, 1)],
+                [jnp.concatenate([right[level][half] for level in seconds], axis=1) for half in (0, 1)],
+            )
+            cols = slice(start, start + value.shape[1])
             if chunk == 0:
-                total[:, cols] = value
+                total[: value.shape[0], cols] = value
             else:
-                total[:, cols] += value
+                total[: value.shape[0], cols] += value
+            for level in seconds:
+                for place, first in enumerate(firsts):
+                    places[first, level] = (place * RANK, start)
+                start += width_of(level)
     first = core_ref[0] == 0
     for index, group in enumerate(groups):
         keep_ref, send_ref = outs[2 * index : 2 * index + 2]
         start = 0
         for pair in group:
-            at = places[pair]
+            row, at = places[pair]
+            value = total[row : row + RANK, at : at + width_of(pair[1])]
             if pair[0] == pair[1]:
-                value = total[:, at : at + RANK]
                 low = jnp.concatenate([value[:HALF, :HALF], value[:QUARTER, HALF:]], axis=0)
                 high = jnp.concatenate([value[HALF:, HALF:], value[QUARTER:HALF, HALF:]], axis=0)
             elif pair[1] < 3:
-                low = total[:, at : at + HALF]
-                high = total[:, at + HALF : at + RANK]
+                low = value[:, :HALF]
+                high = value[:, HALF:]
             else:
-                value = total[:, at : at + RHS]
                 low = jnp.concatenate([value[:HALF, :QUARTER], value[HALF:, :QUARTER]], axis=1)
                 high = jnp.concatenate([value[:HALF, QUARTER:], value[HALF:, QUARTER:]], axis=1)
             rows = slice(start, start + low.shape[0])
@@ -186,30 +182,38 @@
 
 def needed(groups):
     pairs = sorted(pair for group in groups for pair in group)
-    return pairs, sorted({left for left, _ in pairs}), sorted({right for _, right in pairs})
+    rights = sorted({right for _, right in pairs})
+    blocks = {}
+    for right in rights:
+        blocks.setdefault(tuple(left for left, other in pairs if other == right), []).append(right)
+    return list(blocks.items()), sorted({left for left, _ in pairs}), rights
 
 
 def products(core, generators, solved_gens, rhs, groups, *after):
     rows = rhs.shape[0]
     chunks = 4
-    pairs, lefts, rights = needed(groups)
-    width = sum(width_of(right) for _, right in pairs)
+    blocks, lefts, rights = needed(groups)
+    width = sum(width_of(right) for right in rights)
+    height = max(len(firsts) for firsts, _ in blocks) * RANK
+    flops = sum(len(firsts) * width_of(right) for firsts, seconds in blocks for right in seconds) * 6 * rows * RANK
     outs = [struct(sum(rows_of(pair) for pair in group)) for group in groups for _ in range(2)]
-    given = (generators, solved_gens, rhs) if 3 in rights else (generators, solved_gens)
+    held = sum(level < 3 for level in rights)
+    given, specs = [generators, solved_gens], [HBM, HBM]
+    if 3 in rights:
+        given, specs = given + [rhs], specs + [VMEM]
     return pl.pallas_call(
         functools.partial(product_kernel, groups),
-        in_specs=[SMEM] + [HBM] * len(given) + [ANY] * len(after),
+        in_specs=[SMEM] + specs + [ANY] * len(after),
         out_specs=[VMEM] * len(outs),
         out_shape=outs,
         scratch_shapes=[
             pltpu.VMEM((len(lefts), rows, RANK), jnp.float32),
-            pltpu.VMEM((sum(level < 3 for level in rights), rows, RANK), jnp.float32),
-            pltpu.VMEM((rows, RHS), jnp.float32),
-            pltpu.VMEM((RANK, width), jnp.float32),
-            pltpu.SemaphoreType.DMA((len(lefts) + len(rights), chunks)),
+            pltpu.VMEM((held, rows, RANK), jnp.float32),
+            pltpu.VMEM((height, width), jnp.float32),
+            pltpu.SemaphoreType.DMA((len(lefts) + held, chunks)),
         ],
         compiler_params=pltpu.CompilerParams(vmem_limit_bytes=STREAM_LIMIT),
-        cost_estimate=cost(6 * rows * RANK * width, rows * (len(lefts) + len(rights)) * RANK),
+        cost_estimate=cost(flops, rows * (len(lefts) * RANK + width)),
     )(core, *given, *after)
 
 
@@ -223,10 +227,15 @@
     return jnp.where(row == col, 1.0, 0.0)
 
 
-def series(start, scale, power_ref, sum_ref):
+def series(start, values, power_ref, sum_ref):
     norm = square_norm(start)
-    power_ref[...] = dot(start, start)
-    sum_ref[...] = scale * (identity() + start)
+    if values is None:
+        power_ref[...] = dot(start, start)
+        sum_ref[...] = identity() + start
+    else:
+        both = dot(start, jnp.concatenate([start, values], axis=1))
+        power_ref[...] = both[:, :RANK]
+        sum_ref[...] = values + both[:, RANK:]
 
     def proceed(state):
         count, bound = state
@@ -245,21 +254,25 @@
     return lax.while_loop(proceed, body, (jnp.int32(0), norm))[1]
 
 
+def solve_series(product, values, power_ref, sum_ref):
+    bound = series(product, values, power_ref, sum_ref)
+
+    @pl.when(jnp.logical_not(bound <= TOLERANCE))
+    def _():
+        scale = 1.0 / (1.0 + jnp.sqrt(square_norm(product)))
+        series((1.0 - scale) * identity() + scale * product, values, power_ref, sum_ref)
+        sum_ref[...] = scale * sum_ref[...]
+
+
 def invert_kernel(core_ref, own_ref, sib_ref, own_other_ref, sib_other_ref, inverse_ref, p_sib_ref, power):
     core = core_ref[0]
     p_own = symmetric(core, own_ref[:SYM, :], own_other_ref[:SYM, :])
     p_sib = symmetric(core, sib_ref[:SYM, :], sib_other_ref[:SYM, :])
     p_sib_ref[...] = p_sib
-    product = dot(p_sib, p_own)
-    bound = series(product, 1.0, power, inverse_ref)
-
-    @pl.when(jnp.logical_not(bound <= TOLERANCE))
-    def _():
-        scale = 1.0 / (1.0 + jnp.sqrt(square_norm(product)))
-        series((1.0 - scale) * identity() + scale * product, scale, power, inverse_ref)
-
-
-def call(kernel, out_shape, flops, *values, after=()):
+    solve_series(dot(p_sib, p_own), None, power, inverse_ref)
+
+
+def call(kernel, out_shape, flops, *values, after=(), scratch=()):
     many = isinstance(out_shape, (list, tuple))
     floats = sum(value.size for value in values) + sum(out.size for out in (out_shape if many else [out_shape]))
     return pl.pallas_call(
@@ -267,6 +280,7 @@
         in_specs=[SMEM] + [VMEM] * (len(values) - 1) + [ANY] * len(after),
         out_specs=[VMEM] * len(out_shape) if many else VMEM,
         out_shape=out_shape,
+        scratch_shapes=[pltpu.VMEM(shape, jnp.float32) for shape in scratch],
         compiler_params=pltpu.CompilerParams(vmem_limit_bytes=VMEM_LIMIT),
         cost_estimate=cost(flops, floats),
     )(*values, *after)
@@ -295,22 +309,22 @@
     store(out_ref.at[SYM:], value[:, HALF:])
 
 
-def last_parts(core, crossed, z, next_ref, out_ref):
+def last_parts(core, crossed, z, out_ref):
     value = dot_turned(crossed, z)
-    out_ref[:SYM, :] = next_ref[:SYM, :] - symmetric_half(core, value[:, :HALF])
-    store(out_ref.at[SYM:], unpack(next_ref.at[SYM:]) - value[:, HALF:])
-
-
-def third_kernel(core_ref, own_ref, own_other_ref, z_ref, next_ref, *refs):
-    core = core_ref[0]
-    last_parts(core, in_order(core, own_ref[:RANK, :], own_other_ref[...]), unpack(z_ref.at[RANK:]), next_ref, refs[-1])
-
-
-def middle_kernel(core_ref, inverse_ref, p_sib_ref, own_ref, sib_ref, own_other_ref, next_ref, z_ref, out_ref):
+    out_ref[:SYM, :] = symmetric_half(core, value[:, :HALF])
+    store(out_ref.at[SYM:], value[:, HALF:])
+
+
+def third_kernel(core_ref, own_ref, own_other_ref, z_ref, *refs):
+    core = core_ref[0]
+    last_parts(core, in_order(core, own_ref[:RANK, :], own_other_ref[...]), unpack(z_ref.at[RANK:]), refs[-1])
+
+
+def middle_kernel(core_ref, inverse_ref, p_sib_ref, own_ref, sib_ref, own_other_ref, z_ref, out_ref):
     core = core_ref[0]
     z = dot(inverse_ref[...], unpack(sib_ref) - dot(p_sib_ref[...], unpack(own_ref)))
     store(z_ref, z)
-    last_parts(core, in_order(core, own_ref[:RANK, :], own_other_ref[...]), z, next_ref, out_ref)
+    last_parts(core, in_order(core, own_ref[:RANK, :], own_other_ref[...]), z, out_ref)
 
 
 def rhs_in_order(core, own, other):
@@ -323,18 +337,9 @@
 
 
 def reduced_kernel(
-    core_ref, z1_ref, z1_other_ref, z0_ref, z0_other_ref, solved_ref, rhs_ref, *refs
+    core_ref, z1_ref, z1_other_ref, z0_ref, z0_other_ref, solved_ref, rhs_ref, high_ref, low_ref, out_ref
 ):
-    high_ref, low_ref, out_ref, solved, rhs, sems = refs[-6:]
-    core = core_ref[0]
-    copies = [
-        pltpu.make_async_copy(solved_ref.at[0], solved.at[0], sems.at[0]),
-        pltpu.make_async_copy(solved_ref.at[1], solved.at[1], sems.at[1]),
-        pltpu.make_async_copy(solved_ref.at[2], solved.at[2], sems.at[2]),
-        pltpu.make_async_copy(rhs_ref, rhs, sems.at[3]),
-    ]
-    for copy in copies:
-        copy.start()
+    core = core_ref[0]
     z12 = in_order(core, z1_ref[:RANK, :], z1_other_ref[:RANK, :])
     z1x = rhs_in_order(core, z1_ref[RANK:, :], z1_other_ref[RANK:, :])
     z01 = in_order(core, z0_ref[:RANK, :], z0_other_ref[:RANK, :])
@@ -343,31 +348,11 @@
     middle = jnp.concatenate([z12, z1x], axis=1)
     first = jnp.concatenate([z02, z0x], axis=1) - dot(z01, middle)
     coefs = jnp.concatenate([first, middle], axis=0)
-    for copy in copies:
-        copy.wait()
-    value = dot(jnp.concatenate([solved[0], solved[1]], axis=1), coefs)
-    high, low = split(solved[2] - value[:, :RANK])
+    value = dot(jnp.concatenate([solved_ref[0], solved_ref[1]], axis=1), coefs)
+    high, low = split(solved_ref[2] - value[:, :RANK])
     high_ref[...] = high
     low_ref[...] = low
-    out_ref[...] = rhs[...] - value[:, RANK:]
-
-
-def reduced(core, small, solved_gens, rhs, *after):
-    rows = rhs.shape[0]
-    part = jax.ShapeDtypeStruct((rows, RANK), jnp.bfloat16)
-    return pl.pallas_call(
-        reduced_kernel,
-        in_specs=[SMEM] + [VMEM] * len(small) + [HBM, HBM] + [ANY] * len(after),
-        out_specs=[VMEM] * 3,
-        out_shape=[part, part, struct(rows, RHS)],
-        scratch_shapes=[
-            pltpu.VMEM((3, rows, RANK), jnp.float32),
-            pltpu.VMEM((rows, RHS), jnp.float32),
-            pltpu.SemaphoreType.DMA((4,)),
-        ],
-        compiler_params=pltpu.CompilerParams(vmem_limit_bytes=STREAM_LIMIT),
-        cost_estimate=cost(6 * rows * 2 * RANK * (RANK + RHS), rows * 5 * RANK),
-    )(core, *small, solved_gens, rhs, *after)
+    out_ref[...] = rhs_ref[...] - value[:, RANK:]
 
 
 def keep_kernel(core_ref, value_ref, *refs):
@@ -378,14 +363,21 @@
     refs[-1][...] = first_ref[...] + second_ref[...]
 
 
+def subtract_kernel(core_ref, first_ref, second_ref, *refs):
+    refs[-1][...] = first_ref[...] - second_ref[...]
+
+
 def final_kernel(
-    core_ref, inverse_ref, p_sib_ref, own_ref, own_other_ref, sib_ref, sib_other_ref, high_ref, low_ref, rhs_ref, out_ref
+    core_ref, own_ref, own_other_ref, sib_ref, sib_other_ref, high_ref, low_ref, rhs_ref, out_ref, power, total
 ):
     core = core_ref[0]
+    p_own = symmetric(core, own_ref[:SYM, :], own_other_ref[:SYM, :])
+    p_sib = symmetric(core, sib_ref[:SYM, :], sib_other_ref[:SYM, :])
     own = rhs_in_order(core, own_ref[SYM:, :], own_other_ref[SYM:, :])
     sib = rhs_in_order(core, sib_ref[SYM:, :], sib_other_ref[SYM:, :])
-    z = dot(inverse_ref[...], sib - dot(p_sib_ref[...], own))
-    out_ref[...] = rhs_ref[...] - dot_parts((high_ref[...], low_ref[...]), split(z))
+    both = dot(p_sib, jnp.concatenate([p_own, own], axis=1))
+    solve_series(both[:, :RANK], sib - both[:, RANK:], power, total)
+    out_ref[...] = rhs_ref[...] - dot_parts((high_ref[...], low_ref[...]), split(total[...]))
 
 
 def on_device(rhs, generators, solved_gens):
@@ -411,7 +403,8 @@
     parts = [(keep, swap(send, "sub", 0)) for keep, send in zip(parts[::2], parts[1::2])]
     head = over_child(head)
     tail = over_child(parts[0][0] + parts[0][1])
-    near = over_child(call(add_kernel, struct(SYM + RANK + HALF), 0, core, *parts[1], after=(tail,)))
+    near = call(add_kernel, struct(SYM + RANK + HALF), 0, core, *parts[1], after=(tail,))
+    near = over_child(near)
     third = over_child(call(add_kernel, struct(last), 0, core, *parts[2], after=(near,)))
 
     head_sib = swap(head, "rows", span_bits)
@@ -424,11 +417,12 @@
         first_kernel, [struct(2 * RANK + HALF), struct(SYM + RANK + HALF)], FIRST_FLOPS,
         core, inverted, p_sib, head, head_sib, head_other, tail, tail_sib,
     )
-    near = near - crossed
-    third = call(third_kernel, struct(last), 2 * flops, core, tail, tail_other, z0, third, after=(near,))
-
-    near = near + swap(near, "rows", span_bits)
-    p_own, r_own = near[:SYM], near[SYM:]
+    p_own = call(subtract_kernel, struct(SYM), 0, core, near[:SYM], crossed[:SYM])
+    r_own = call(subtract_kernel, struct(RANK + HALF), 0, core, near[SYM:], crossed[SYM:], after=(p_own,))
+    third = third - call(third_kernel, struct(last), THIRD_FLOPS, core, tail, tail_other, z0, after=(r_own,))
+
+    p_own = p_own + swap(p_own, "rows", span_bits)
+    r_own = r_own + swap(r_own, "rows", span_bits)
     third = third + swap(third, "rows", span_bits)
     p_sib = swap(p_own, "rows", span_bits + 1)
     r_sib = swap(r_own, "rows", span_bits + 1)
@@ -436,21 +430,25 @@
     r_own_other = swap(r_own[:RANK], "sub", 0)
     p_sib_other = swap(p_sib, "sub", 0)
     inverted, p_sib = inverse(core, p_own, p_sib, p_own_other, p_sib_other)
-    z1, own = call(
+    z1, crossed = call(
         middle_kernel, [struct(RANK + HALF), struct(last)], 5 * flops,
-        core, inverted, p_sib, r_own, r_sib, r_own_other, third,
-    )
-
+        core, inverted, p_sib, r_own, r_sib, r_own_other,
+    )
+
+    own = third - crossed
     own = own + swap(own, "rows", span_bits + 1)
     sib = swap(own, "rows", span_bits + 2)
-    small = (z1, swap(z1, "sub", 0), z0, swap(z0, "sub", 0))
-    high, low, current = reduced(core, small, solved_gens, rhs, own)
+    z1_other = swap(call(keep_kernel, struct(RANK + HALF), 0, core, z1, after=(own,)), "sub", 0)
+    part = jax.ShapeDtypeStruct((rhs.shape[0], RANK), jnp.bfloat16)
+    high, low, current = call(
+        reduced_kernel, [part, part, struct(rhs.shape[0], RHS)], 6 * rhs.shape[0] * 2 * RANK * (RANK + RHS),
+        core, z1, z1_other, z0, swap(z0, "sub", 0), solved_gens, rhs,
+    )
     sib = call(keep_kernel, struct(last), 0, core, sib, after=(high,))
     own_other, sib_other = swap(own, "sub", 0), swap(sib, "sub", 0)
-    inverted, p_sib = inverse(core, own, sib, own_other, sib_other)
     return call(
-        final_kernel, struct(rhs.shape[0], RHS), 6 * rhs.shape[0] * RANK * RHS,
-        core, inverted, p_sib, own, own_other, sib, sib_other, high, low, current,
+        final_kernel, struct(rhs.shape[0], RHS), 6 * rhs.shape[0] * RANK * RHS + 6 * 9 * RANK**3,
+        core, own, own_other, sib, sib_other, high, low, current, scratch=((RANK, RANK), (RANK, RHS)),
     )
 
 

time: 74.2 us -> 69.8 us (0.941)
  waiting for transfers between devices: 28.5 us -> 24.2 us
  Pallas kernels: 24.6 us -> 21.3 us
  starting transfers between devices: 20.4 us -> 23.5 us
    pallas_call x1 -> x0, Pallas kernels: 5.15 us -> none  [reduced(): pl.pallas_call(reduced_kernel, in_specs=[SMEM] + [VMEM] * len(small) + [H...]
    ppermute x27 -> x28, waiting for transfers between devices: 28.5 us -> 24.2 us  [swap(): return lax.ppermute(value, axis, pairs)]
    pallas_call x8 -> x12, Pallas kernels: 4.65 us -> 8.58 us  [call(): pl.pallas_call(kernel, in_specs=[SMEM] + [VMEM] * (len(values) - 1) + [AN...]
    ppermute x27 -> x28, starting transfers between devices: 20.4 us -> 23.5 us  [swap(): return lax.ppermute(value, axis, pairs)]
    pallas_call x3 -> x2, Pallas kernels: 7.01 us -> 4.73 us  [inverse(): pl.pallas_call(invert_kernel, in_specs=[SMEM] + [VMEM] * 4, out_specs=[VM...]
  transfers between devices with their start and end apart: 27 -> 28, of which waited for: 11 -> 14; matrix products, arithmetic and copies ran while one was open for 0% -> 0% of each run, Pallas kernels for 24% -> 22%
where the time goes in v7:
time: 69.8 us; the launch traced here: 69.7 us
  waiting for transfers between devices  24.2 us (35%)
  starting transfers between devices  23.5 us (34%)
  Pallas kernels  21.3 us (31%)
    ppermute x28, waiting for transfers between devices, swap(): return lax.ppermute(value, axis, pairs)  24.2 us
    ppermute x28, starting transfers between devices, swap(): return lax.ppermute(value, axis, pairs)  23.5 us
    pallas_call x12, Pallas kernels, call(): pl.pallas_call(kernel, in_specs=[SMEM] + [VMEM] * (len(values) - 1) + [AN...  8.58 us
    pallas_call x2, Pallas kernels, products(): pl.pallas_call(functools.partial(product_kernel, groups), in_specs=[SMEM]...  8.03 us
    pallas_call x2, Pallas kernels, inverse(): pl.pallas_call(invert_kernel, in_specs=[SMEM] + [VMEM] * 4, out_specs=[VM...  4.73 us
  transfers between devices with their start and end apart: 28, of which 14 were waited for; matrix products, arithmetic and copies ran while one was open for 0% of the time, Pallas kernels for 22%

profile of v7, /device:TPU:0, one launch (start us, length us, event | category | flops | bytes accessed | tf_op | source)
XLA Modules:
  0.0 69.7 jit_solution(3054507648133946409)
XLA Ops:
  0.0 2.6 %shard_map.37 = (f32[448,128]{1,0:T(8,128)S(1)}, f32[448,128]{1,0:T(8,128)S(1)}) custom-call(s32[1]{0:T(128)} %bitcast.core_ref, f32[3,1024,256]{2,1,0:T(8,128)} %gens_ref.3, f32[3,1024,256]{2,1,0:T(8,128)} %solved_ref.5), custom_call_target="tpu_custom_call" | custom-call | flops 805306368 | bytes 3145728 | tf_op jit(solution)/shard_map/pallas_call | solution.py:204
  2.6 0.5 collective-permute-start
  3.1 1.1 %collective-permute-done = f32[448,128]{1,0:T(8,128)S(1)} collective-permute-done((f32[448,128]{1,0:T(8,128)S(1)}, f32[448,128]{1,0:T(8,128)S(1)}, u32[]{:S(2)}, u32[]{:S(2)}) %collective-permute-start) | collective-permute-done | bytes 229408 | tf_op jit(solution)/shard_map/ppermute | solution.py:31
  4.2 0.4 collective-permute-start.1
  4.7 2.7 %collective-permute-start.9 = (f32[448,128]{1,0:T(8,128)S(1)}, f32[448,128]{1,0:T(8,128)S(1)}, u32[]{:S(2)}, u32[]{:S(2)}) collective-permute-start(f32[448,128]{1,0:T(8,128)S(1)} %add.35.refs_0_), channel_id=1, source_target_pairs={{0,2},{1,3},{2,0},{3,1},{4,6},{5,7},{6,4},{7,5},{8,10},{9,11},{10,... | collective-permute-start | bytes 688136 | tf_op jit(solution)/shard_map/ppermute | solution.py:31
  7.3 0.0 collective-permute-done.1.refs_1_
  7.4 5.5 %shard_map.39 = (f32[384,128]{1,0:T(8,128)S(1)}, f32[384,128]{1,0:T(8,128)S(1)}, f32[576,128]{1,0:T(8,128)S(1)}, f32[576,128]{1,0:T(8,128)S(1)}, f32[320,128]{1,0:T(8,128)S(1)}, /*index=5*/f32[320,128]{1,0:T(8,128)S(1)}) custom-call(s32[1]{0:T(128)} %bitcast.core_ref, f32[3,1024,256]{2,1,0:T(8,128)} %gens_ref.3, f32[3,1024,256]{2,1,0:T(8,128)} %solved_ref.5, ...), custom_call_target="tpu_custom_call" | custom-call | flops 2214592512 | bytes 5767168 | tf_op jit(solution)/shard_map/pallas_call | solution.py:204
  12.8 0.1 collective-permute-start.4
  13.0 0.4 collective-permute-start.3
  13.4 0.9 %collective-permute-done.4 = f32[384,128]{1,0:T(8,128)S(1)} collective-permute-done((f32[384,128]{1,0:T(8,128)S(1)}, f32[384,128]{1,0:T(8,128)S(1)}, u32[]{:S(2)}, u32[]{:S(2)}) %collective-permute-start.4) | collective-permute-done | bytes 196640 | tf_op jit(solution)/shard_map/ppermute | solution.py:31
  14.4 1.1 %collective-permute-start.5 = (f32[384,128]{1,0:T(8,128)S(1)}, f32[384,128]{1,0:T(8,128)S(1)}, u32[]{:S(2)}, u32[]{:S(2)}) collective-permute-start(f32[384,128]{1,0:T(8,128)S(1)} %add.36), channel_id=1, source_target_pairs={{0,2},{1,3},{2,0},{3,1},{4,6},{5,7},{6,4},{7,5},{8,10},{9,11},{10,... | collective-permute-start | bytes 589832 | tf_op jit(solution)/shard_map/ppermute | solution.py:31
  15.4 0.0 collective-permute-done.9
  15.5 1.6 %collective-permute-start.10 = (f32[448,128]{1,0:T(8,128)S(1)}, f32[448,128]{1,0:T(8,128)S(1)}, u32[]{:S(2)}, u32[]{:S(2)}) collective-permute-start(f32[448,128]{1,0:T(8,128)S(1)} %add.40.own_ref.head_ref), channel_id=1, source_target_pairs={{0,4},{4,0},{8,12},{12,8},{16,20},{20,16},{24,28},{28,24},{1,5},{5... | collective-permute-start | bytes 688136 | tf_op jit(solution)/shard_map/ppermute | solution.py:31
  17.0 0.0 collective-permute-start.11
  17.0 4.3 %collective-permute-done.5 = f32[384,128]{1,0:T(8,128)S(1)} collective-permute-done((f32[384,128]{1,0:T(8,128)S(1)}, f32[384,128]{1,0:T(8,128)S(1)}, u32[]{:S(2)}, u32[]{:S(2)}) %collective-permute-start.5) | collective-permute-done | bytes 196640 | tf_op jit(solution)/shard_map/ppermute | solution.py:31
  21.4 0.0 collective-permute-done.3.second_ref
  21.5 1.1 %collective-permute-start.6 = (f32[576,128]{1,0:T(8,128)S(1)}, f32[576,128]{1,0:T(8,128)S(1)}, u32[]{:S(2)}, u32[]{:S(2)}) collective-permute-start(f32[576,128]{1,0:T(8,128)S(1)} %shard_map.40), channel_id=1, source_target_pairs={{0,2},{1,3},{2,0},{3,1},{4,6},{5,7},{6,4},{7,5},{8,10},{9,11},{10,... | collective-permute-start | bytes 884744 | tf_op jit(solution)/shard_map/ppermute | solution.py:31
  22.6 1.5 %collective-permute-start.13 = (f32[384,128]{1,0:T(8,128)S(1)}, f32[384,128]{1,0:T(8,128)S(1)}, u32[]{:S(2)}, u32[]{:S(2)}) collective-permute-start(f32[384,128]{1,0:T(8,128)S(1)} %add.37.refs_0_.tail_ref.own_ref), channel_id=1, source_target_pairs={{0,4},{4,0},{8,12},{12,8},{16,20},{20,16},{24,28},{28,24},{1,5},{5... | collective-permute-start | bytes 589832 | tf_op jit(solution)/shard_map/ppermute | solution.py:31
  24.1 0.0 collective-permute-done.10.sib_ref.head_sib_ref
  24.1 0.1 collective-permute-start.12
  24.2 0.5 collective-permute-start.2
  24.7 0.0 collective-permute-done.11.own_other_ref.head_other_ref
  24.7 0.1 collective-permute-start.8
  24.8 0.6 collective-permute-done.12.sib_other_ref
  25.4 2.3 %shard_map.42 = (f32[256,256]{1,0:T(8,128)S(1)}, f32[256,256]{1,0:T(8,128)S(1)}) custom-call(s32[1]{0:T(128)} %bitcast.core_ref, f32[448,128]{1,0:T(8,128)S(1)} %add.40.own_ref.head_ref, f32[448,128]{1,0:T(8,128)S(1)} %collective-permute-done.10.sib_ref.head_sib_ref, f32[448,128]{1,0:T(8,128)S(1)} %collective-permute-done.11.own_other_ref.head_other_ref, ...), custom_call_target="tpu_custom_call" | custom-call | flops 905969664 | bytes 1048576 | tf_op jit(solution)/shard_map/pallas_call | solution.py:290
  27.7 0.7 %collective-permute-done.13.tail_sib_ref = f32[384,128]{1,0:T(8,128)S(1)} collective-permute-done((f32[384,128]{1,0:T(8,128)S(1)}, f32[384,128]{1,0:T(8,128)S(1)}, u32[]{:S(2)}, u32[]{:S(2)}) %collective-permute-start.13) | collective-permute-done | bytes 196640 | tf_op jit(solution)/shard_map/ppermute | solution.py:31
  28.4 1.1 %shard_map.43 = (f32[640,128]{1,0:T(8,128)S(1)}, f32[576,128]{1,0:T(8,128)S(1)}) custom-call(s32[1]{0:T(128)} %bitcast.core_ref, f32[256,256]{1,0:T(8,128)S(1)} %get-tuple-element.32.inverse_ref, f32[256,256]{1,0:T(8,128)S(1)} %get-tuple-element.33.p_sib_ref, f32[448,128]{1,0:T(8,128)S(1)} %add.40.own_ref.head_ref, ...), custom_call_target="tpu_custom_call" | custom-call | flops 650000000 | bytes 2228228 | tf_op jit(solution)/shard_map/pallas_call | solution.py:278
  29.6 0.2 collective-permute-done.6
  29.8 1.6 %collective-permute-start.15 = (f32[192,128]{1,0:T(8,128)S(1)}, f32[192,128]{1,0:T(8,128)S(1)}, u32[]{:S(2)}, u32[]{:S(2)}) collective-permute-start(f32[192,128]{1,0:T(8,128)S(1)} %shard_map.44.refs_0_), channel_id=1, source_target_pairs={{0,4},{4,0},{8,12},{12,8},{16,20},{20,16},{24,28},{28,24},{1,5},{5... | collective-permute-start | bytes 294920 | tf_op jit(solution)/shard_map/ppermute | solution.py:31
  31.4 0.6 collective-permute-start.19
  32.0 0.0 collective-permute-done.2.second_ref
  32.1 1.1 %collective-permute-start.7 = (f32[320,128]{1,0:T(8,128)S(1)}, f32[320,128]{1,0:T(8,128)S(1)}, u32[]{:S(2)}, u32[]{:S(2)}) collective-permute-start(f32[320,128]{1,0:T(8,128)S(1)} %shard_map.41), channel_id=1, source_target_pairs={{0,2},{1,3},{2,0},{3,1},{4,6},{5,7},{6,4},{7,5},{8,10},{9,11},{10,... | collective-permute-start | bytes 491528 | tf_op jit(solution)/shard_map/ppermute | solution.py:31
  33.2 2.4 %collective-permute-done.15 = f32[192,128]{1,0:T(8,128)S(1)} collective-permute-done((f32[192,128]{1,0:T(8,128)S(1)}, f32[192,128]{1,0:T(8,128)S(1)}, u32[]{:S(2)}, u32[]{:S(2)}) %collective-permute-start.15) | collective-permute-done | bytes 98336 | tf_op jit(solution)/shard_map/ppermute | solution.py:31
  35.6 1.6 %collective-permute-start.16 = (f32[192,128]{1,0:T(8,128)S(1)}, f32[192,128]{1,0:T(8,128)S(1)}, u32[]{:S(2)}, u32[]{:S(2)}) collective-permute-start(f32[192,128]{1,0:T(8,128)S(1)} %add.42.own_ref), channel_id=1, source_target_pairs={{0,8},{4,12},{8,0},{12,4},{16,24},{20,28},{24,16},{28,20},{1,9},{5... | collective-permute-start | bytes 294920 | tf_op jit(solution)/shard_map/ppermute | solution.py:31
  37.3 0.0 collective-permute-done.8.own_other_ref
  37.3 0.4 shard_map.46
  37.7 0.1 collective-permute-start.17
  37.8 0.4 collective-permute-done.19
  38.2 1.6 %collective-permute-start.20 = (f32[384,128]{1,0:T(8,128)S(1)}, f32[384,128]{1,0:T(8,128)S(1)}, u32[]{:S(2)}, u32[]{:S(2)}) collective-permute-start(f32[384,128]{1,0:T(8,128)S(1)} %add.43.own_ref), channel_id=1, source_target_pairs={{0,8},{4,12},{8,0},{12,4},{16,24},{20,28},{24,16},{28,20},{1,9},{5... | collective-permute-start | bytes 589832 | tf_op jit(solution)/shard_map/ppermute | solution.py:31
  39.8 0.5 collective-permute-done.16.sib_ref
  40.3 0.0 collective-permute-start.18
  40.3 0.0 collective-permute-done.7
  40.3 0.0 copy-start
  40.4 1.3 %collective-permute-start.14 = (f32[320,128]{1,0:T(8,128)S(1)}, f32[320,128]{1,0:T(8,128)S(1)}, u32[]{:S(2)}, u32[]{:S(2)}) collective-permute-start(f32[320,128]{1,0:T(8,128)S(1)} %add_subtract_fusion.1), channel_id=1, source_target_pairs={{0,4},{4,0},{8,12},{12,8},{16,20},{20,16},{24,28},{28,24},{1,5},{5... | collective-permute-start | bytes 491528 | tf_op jit(solution)/shard_map/ppermute | solution.py:31
  41.7 0.3 collective-permute-start.21
  42.0 0.0 collective-permute-done.17.own_other_ref
  42.0 0.0 collective-permute-done.18.sib_other_ref
  42.0 2.5 %shard_map.47 = (f32[256,256]{1,0:T(8,128)S(1)}, f32[256,256]{1,0:T(8,128)S(1)}) custom-call(s32[1]{0:T(128)} %bitcast.core_ref, f32[192,128]{1,0:T(8,128)S(1)} %add.42.own_ref, f32[192,128]{1,0:T(8,128)S(1)} %collective-permute-done.16.sib_ref, f32[192,128]{1,0:T(8,128)S(1)} %collective-permute-done.17.own_other_ref, ...), custom_call_target="tpu_custom_call" | custom-call | flops 905969664 | bytes 1048576 | tf_op jit(solution)/shard_map/pallas_call | solution.py:290
  44.4 0.0 collective-permute-done.21.own_other_ref
  44.4 0.7 %collective-permute-done.20.sib_ref = f32[384,128]{1,0:T(8,128)S(1)} collective-permute-done((f32[384,128]{1,0:T(8,128)S(1)}, f32[384,128]{1,0:T(8,128)S(1)}, u32[]{:S(2)}, u32[]{:S(2)}) %collective-permute-start.20) | collective-permute-done | bytes 196640 | tf_op jit(solution)/shard_map/ppermute | solution.py:31
  45.2 1.0 %shard_map.48 = (f32[384,128]{1,0:T(8,128)S(1)}, f32[320,128]{1,0:T(8,128)S(1)}) custom-call(s32[1]{0:T(128)} %bitcast.core_ref, f32[256,256]{1,0:T(8,128)S(1)} %get-tuple-element.36.inverse_ref, f32[256,256]{1,0:T(8,128)S(1)} %get-tuple-element.37.p_sib_ref, f32[384,128]{1,0:T(8,128)S(1)} %add.43.own_ref, f32[384,128]{1,0:T(8,128)S(1)} %collective-permute-done.20.sib_ref, ...), custom_call_target="tpu_custom_call" | custom-call | flops 251658240 | bytes 1409028 | tf_op jit(solution)/shard_map/pallas_call | solution.py:278
  46.2 0.8 %collective-permute-done.14 = f32[320,128]{1,0:T(8,128)S(1)} collective-permute-done((f32[320,128]{1,0:T(8,128)S(1)}, f32[320,128]{1,0:T(8,128)S(1)}, u32[]{:S(2)}, u32[]{:S(2)}) %collective-permute-start.14) | collective-permute-done | bytes 163872 | tf_op jit(solution)/shard_map/ppermute | solution.py:31
  47.1 2.2 %collective-permute-start.22 = (f32[320,128]{1,0:T(8,128)S(1)}, f32[320,128]{1,0:T(8,128)S(1)}, u32[]{:S(2)}, u32[]{:S(2)}) collective-permute-start(f32[320,128]{1,0:T(8,128)S(1)} %add_subtract_fusion), channel_id=1, source_target_pairs={{0,8},{4,12},{8,0},{12,4},{16,24},{20,28},{24,16},{28,20},{1,9},{5... | collective-permute-start | bytes 491528 | tf_op jit(solution)/shard_map/ppermute | solution.py:31
  49.3 4.1 %collective-permute-done.22 = f32[320,128]{1,0:T(8,128)S(1)} collective-permute-done((f32[320,128]{1,0:T(8,128)S(1)}, f32[320,128]{1,0:T(8,128)S(1)}, u32[]{:S(2)}, u32[]{:S(2)}) %collective-permute-start.22) | collective-permute-done | bytes 163872 | tf_op jit(solution)/shard_map/ppermute | solution.py:31
  53.4 0.1 collective-permute-start.25
  53.5 2.6 %collective-permute-start.24 = (f32[320,128]{1,0:T(8,128)S(1)}, f32[320,128]{1,0:T(8,128)S(1)}, u32[]{:S(2)}, u32[]{:S(2)}) collective-permute-start(f32[320,128]{1,0:T(8,128)S(1)} %add.44.refs_0_.own_ref), channel_id=1, source_target_pairs={{0,16},{4,20},{8,24},{12,28},{16,0},{20,4},{24,8},{28,12},{1,17},{... | collective-permute-start | bytes 491528 | tf_op jit(solution)/shard_map/ppermute | solution.py:31
  56.1 0.2 collective-permute-start.23
  56.3 0.0 collective-permute-done.26.z0_other_ref
  56.3 0.0 collective-permute-done.25.z1_other_ref
  56.3 2.2 %shard_map.50 = (bf16[1024,256]{1,0:T(8,128)(2,1)S(1)}, bf16[1024,256]{1,0:T(8,128)(2,1)S(1)}, f32[1024,128]{1,0:T(8,128)S(1)}) custom-call(s32[1]{0:T(128)} %bitcast.core_ref, f32[384,128]{1,0:T(8,128)S(1)} %get-tuple-element.39.value_ref.z1_ref, f32[384,128]{1,0:T(8,128)S(1)} %collective-permute-done.25.z1_other_ref, ...), custom_call_target="tpu_custom_call" | custom-call | flops 1207959552 | bytes 7340036 | tf_op jit(solution)/shard_map/pallas_call | solution.py:278
  58.5 6.0 %collective-permute-done.24.value_ref = f32[320,128]{1,0:T(8,128)S(1)} collective-permute-done((f32[320,128]{1,0:T(8,128)S(1)}, f32[320,128]{1,0:T(8,128)S(1)}, u32[]{:S(2)}, u32[]{:S(2)}) %collective-permute-start.24) | collective-permute-done | bytes 163872 | tf_op jit(solution)/shard_map/ppermute | solution.py:31
  64.5 0.1 collective-permute-start.27
  64.6 1.4 %collective-permute-done.27.sib_other_ref = f32[320,128]{1,0:T(8,128)S(1)} collective-permute-done((f32[320,128]{1,0:T(8,128)S(1)}, f32[320,128]{1,0:T(8,128)S(1)}, u32[]{:S(2)}, u32[]{:S(2)}) %collective-permute-start.27) | collective-permute-done | bytes 163872 | tf_op jit(solution)/shard_map/ppermute | solution.py:31
  66.0 3.7 %shard_map.52 = f32[1024,128]{1,0:T(8,128)} custom-call(s32[1]{0:T(128)} %bitcast.core_ref, f32[320,128]{1,0:T(8,128)S(1)} %add.44.refs_0_.own_ref, f32[320,128]{1,0:T(8,128)S(1)} %collective-permute-done.23.own_other_ref, f32[320,128]{1,0:T(8,128)S(1)} %shard_map.51.sib_ref, f32[320,128]{1,0:T(8,128)S(1)} %collective-permute-done.27.sib_other_ref, ...), custom_call_target="tpu_custom_call" | custom-call | flops 1107296256 | bytes 3801092 | tf_op jit(solution)/shard_map/pallas_call | solution.py:278
  (30 shorter events, 0.4 us)
Async XLA Ops:
  0.0 7.3 %copy-start.1 = (f32[1024,128]{1,0:T(8,128)S(1)}, f32[1024,128]{1,0:T(8,128)}, u32[]{:S(2)}) copy-start(f32[1024,128]{1,0:T(8,128)} %rhs_ref.1) | copy-start | bytes 1572868
  2.6 1.6 %collective-permute-start = (f32[448,128]{1,0:T(8,128)S(1)}, f32[448,128]{1,0:T(8,128)S(1)}, u32[]{:S(2)}, u32[]{:S(2)}) collective-permute-start(f32[448,128]{1,0:T(8,128)S(1)} %get-tuple-element.24), channel_id=1, source_target_pairs={{0,1},{1,0},{2,3},{3,2},{4,5},{5,4},{6,7},{7,6},{8,9},{9,8},{10,11... | collective-permute-start | bytes 688136 | tf_op jit(solution)/shard_map/ppermute | solution.py:31
  4.2 3.1 %collective-permute-start.1 = (f32[8,128]{1,0:T(8,128)S(1)}, f32[8,128]{1,0:T(8,128)S(1)}, u32[]{:S(2)}, u32[]{:S(2)}) collective-permute-start(f32[8,128]{1,0:T(8,128)S(1)} %shard_map.38), channel_id=1, source_target_pairs={{0,1},{1,0},{2,3},{3,2},{4,5},{5,4},{6,7},{7,6},{8,9},{9,8},{10,11... | collective-permute-start | bytes 12296 | tf_op jit(solution)/shard_map/ppermute | solution.py:31
  4.7 10.8 %collective-permute-start.9 = (f32[448,128]{1,0:T(8,128)S(1)}, f32[448,128]{1,0:T(8,128)S(1)}, u32[]{:S(2)}, u32[]{:S(2)}) collective-permute-start(f32[448,128]{1,0:T(8,128)S(1)} %add.35.refs_0_), channel_id=1, source_target_pairs={{0,2},{1,3},{2,0},{3,1},{4,6},{5,7},{6,4},{7,5},{8,10},{9,11},{10,... | collective-permute-start | bytes 688136 | tf_op jit(solution)/shard_map/ppermute | solution.py:31
  12.8 1.5 %collective-permute-start.4 = (f32[384,128]{1,0:T(8,128)S(1)}, f32[384,128]{1,0:T(8,128)S(1)}, u32[]{:S(2)}, u32[]{:S(2)}) collective-permute-start(f32[384,128]{1,0:T(8,128)S(1)} %get-tuple-element.31), channel_id=1, source_target_pairs={{0,1},{1,0},{2,3},{3,2},{4,5},{5,4},{6,7},{7,6},{8,9},{9,8},{10,11... | collective-permute-start | bytes 589832 | tf_op jit(solution)/shard_map/ppermute | solution.py:31
  13.0 8.4 %collective-permute-start.3 = (f32[576,128]{1,0:T(8,128)S(1)}, f32[576,128]{1,0:T(8,128)S(1)}, u32[]{:S(2)}, u32[]{:S(2)}) collective-permute-start(f32[576,128]{1,0:T(8,128)S(1)} %get-tuple-element.29), channel_id=1, source_target_pairs={{0,1},{1,0},{2,3},{3,2},{4,5},{5,4},{6,7},{7,6},{8,9},{9,8},{10,11... | collective-permute-start | bytes 884744 | tf_op jit(solution)/shard_map/ppermute | solution.py:31
  14.4 7.0 %collective-permute-start.5 = (f32[384,128]{1,0:T(8,128)S(1)}, f32[384,128]{1,0:T(8,128)S(1)}, u32[]{:S(2)}, u32[]{:S(2)}) collective-permute-start(f32[384,128]{1,0:T(8,128)S(1)} %add.36), channel_id=1, source_target_pairs={{0,2},{1,3},{2,0},{3,1},{4,6},{5,7},{6,4},{7,5},{8,10},{9,11},{10,... | collective-permute-start | bytes 589832 | tf_op jit(solution)/shard_map/ppermute | solution.py:31
  15.5 8.6 %collective-permute-start.10 = (f32[448,128]{1,0:T(8,128)S(1)}, f32[448,128]{1,0:T(8,128)S(1)}, u32[]{:S(2)}, u32[]{:S(2)}) collective-permute-start(f32[448,128]{1,0:T(8,128)S(1)} %add.40.own_ref.head_ref), channel_id=1, source_target_pairs={{0,4},{4,0},{8,12},{12,8},{16,20},{20,16},{24,28},{28,24},{1,5},{5... | collective-permute-start | bytes 688136 | tf_op jit(solution)/shard_map/ppermute | solution.py:31
  17.0 7.6 %collective-permute-start.11 = (f32[448,128]{1,0:T(8,128)S(1)}, f32[448,128]{1,0:T(8,128)S(1)}, u32[]{:S(2)}, u32[]{:S(2)}) collective-permute-start(f32[448,128]{1,0:T(8,128)S(1)} %add.40.own_ref.head_ref), channel_id=1, source_target_pairs={{0,1},{1,0},{2,3},{3,2},{4,5},{5,4},{6,7},{7,6},{8,9},{9,8},{10,11... | collective-permute-start | bytes 688136 | tf_op jit(solution)/shard_map/ppermute | solution.py:31
  21.5 8.3 %collective-permute-start.6 = (f32[576,128]{1,0:T(8,128)S(1)}, f32[576,128]{1,0:T(8,128)S(1)}, u32[]{:S(2)}, u32[]{:S(2)}) collective-permute-start(f32[576,128]{1,0:T(8,128)S(1)} %shard_map.40), channel_id=1, source_target_pairs={{0,2},{1,3},{2,0},{3,1},{4,6},{5,7},{6,4},{7,5},{8,10},{9,11},{10,... | collective-permute-start | bytes 884744 | tf_op jit(solution)/shard_map/ppermute | solution.py:31
  22.6 5.9 %collective-permute-start.13 = (f32[384,128]{1,0:T(8,128)S(1)}, f32[384,128]{1,0:T(8,128)S(1)}, u32[]{:S(2)}, u32[]{:S(2)}) collective-permute-start(f32[384,128]{1,0:T(8,128)S(1)} %add.37.refs_0_.tail_ref.own_ref), channel_id=1, source_target_pairs={{0,4},{4,0},{8,12},{12,8},{16,20},{20,16},{24,28},{28,24},{1,5},{5... | collective-permute-start | bytes 589832 | tf_op jit(solution)/shard_map/ppermute | solution.py:31
  24.1 1.4 %collective-permute-start.12 = (f32[192,128]{1,0:T(8,128)S(1)}, f32[192,128]{1,0:T(8,128)S(1)}, u32[]{:S(2)}, u32[]{:S(2)}) collective-permute-start(f32[192,128]{1,0:T(8,128)S(1)} %slice.33), channel_id=1, source_target_pairs={{0,1},{1,0},{2,3},{3,2},{4,5},{5,4},{6,7},{7,6},{8,9},{9,8},{10,11... | collective-permute-start | bytes 294920 | tf_op jit(solution)/shard_map/ppermute | solution.py:31
  24.2 7.9 %collective-permute-start.2 = (f32[320,128]{1,0:T(8,128)S(1)}, f32[320,128]{1,0:T(8,128)S(1)}, u32[]{:S(2)}, u32[]{:S(2)}) collective-permute-start(f32[320,128]{1,0:T(8,128)S(1)} %get-tuple-element.27), channel_id=1, source_target_pairs={{0,1},{1,0},{2,3},{3,2},{4,5},{5,4},{6,7},{7,6},{8,9},{9,8},{10,11... | collective-permute-start | bytes 491528 | tf_op jit(solution)/shard_map/ppermute | solution.py:31
  24.7 12.6 %collective-permute-start.8 = (f32[256,128]{1,0:T(8,128)S(1)}, f32[256,128]{1,0:T(8,128)S(1)}, u32[]{:S(2)}, u32[]{:S(2)}) collective-permute-start(f32[256,128]{1,0:T(8,128)S(1)} %slice.32), channel_id=1, source_target_pairs={{0,1},{1,0},{2,3},{3,2},{4,5},{5,4},{6,7},{7,6},{8,9},{9,8},{10,11... | collective-permute-start | bytes 393224 | tf_op jit(solution)/shard_map/ppermute | solution.py:31
  29.8 5.8 %collective-permute-start.15 = (f32[192,128]{1,0:T(8,128)S(1)}, f32[192,128]{1,0:T(8,128)S(1)}, u32[]{:S(2)}, u32[]{:S(2)}) collective-permute-start(f32[192,128]{1,0:T(8,128)S(1)} %shard_map.44.refs_0_), channel_id=1, source_target_pairs={{0,4},{4,0},{8,12},{12,8},{16,20},{20,16},{24,28},{28,24},{1,5},{5... | collective-permute-start | bytes 294920 | tf_op jit(solution)/shard_map/ppermute | solution.py:31
  31.4 6.7 %collective-permute-start.19 = (f32[384,128]{1,0:T(8,128)S(1)}, f32[384,128]{1,0:T(8,128)S(1)}, u32[]{:S(2)}, u32[]{:S(2)}) collective-permute-start(f32[384,128]{1,0:T(8,128)S(1)} %shard_map.45.refs_0_), channel_id=1, source_target_pairs={{0,4},{4,0},{8,12},{12,8},{16,20},{20,16},{24,28},{28,24},{1,5},{5... | collective-permute-start | bytes 589832 | tf_op jit(solution)/shard_map/ppermute | solution.py:31
  32.1 8.2 %collective-permute-start.7 = (f32[320,128]{1,0:T(8,128)S(1)}, f32[320,128]{1,0:T(8,128)S(1)}, u32[]{:S(2)}, u32[]{:S(2)}) collective-permute-start(f32[320,128]{1,0:T(8,128)S(1)} %shard_map.41), channel_id=1, source_target_pairs={{0,2},{1,3},{2,0},{3,1},{4,6},{5,7},{6,4},{7,5},{8,10},{9,11},{10,... | collective-permute-start | bytes 491528 | tf_op jit(solution)/shard_map/ppermute | solution.py:31
  35.6 4.7 %collective-permute-start.16 = (f32[192,128]{1,0:T(8,128)S(1)}, f32[192,128]{1,0:T(8,128)S(1)}, u32[]{:S(2)}, u32[]{:S(2)}) collective-permute-start(f32[192,128]{1,0:T(8,128)S(1)} %add.42.own_ref), channel_id=1, source_target_pairs={{0,8},{4,12},{8,0},{12,4},{16,24},{20,28},{24,16},{28,20},{1,9},{5... | collective-permute-start | bytes 294920 | tf_op jit(solution)/shard_map/ppermute | solution.py:31
  37.7 4.3 %collective-permute-start.17 = (f32[192,128]{1,0:T(8,128)S(1)}, f32[192,128]{1,0:T(8,128)S(1)}, u32[]{:S(2)}, u32[]{:S(2)}) collective-permute-start(f32[192,128]{1,0:T(8,128)S(1)} %add.42.own_ref), channel_id=1, source_target_pairs={{0,1},{1,0},{2,3},{3,2},{4,5},{5,4},{6,7},{7,6},{8,9},{9,8},{10,11... | collective-permute-start | bytes 294920 | tf_op jit(solution)/shard_map/ppermute | solution.py:31
  38.2 7.0 %collective-permute-start.20 = (f32[384,128]{1,0:T(8,128)S(1)}, f32[384,128]{1,0:T(8,128)S(1)}, u32[]{:S(2)}, u32[]{:S(2)}) collective-permute-start(f32[384,128]{1,0:T(8,128)S(1)} %add.43.own_ref), channel_id=1, source_target_pairs={{0,8},{4,12},{8,0},{12,4},{16,24},{20,28},{24,16},{28,20},{1,9},{5... | collective-permute-start | bytes 589832 | tf_op jit(solution)/shard_map/ppermute | solution.py:31
  40.3 1.7 %collective-permute-start.18 = (f32[192,128]{1,0:T(8,128)S(1)}, f32[192,128]{1,0:T(8,128)S(1)}, u32[]{:S(2)}, u32[]{:S(2)}) collective-permute-start(f32[192,128]{1,0:T(8,128)S(1)} %collective-permute-done.16.sib_ref), channel_id=1, source_target_pairs={{0,1},{1,0},{2,3},{3,2},{4,5},{5,4},{6,7},{7,6},{8,9},{9,8},{10,11... | collective-permute-start | bytes 294920 | tf_op jit(solution)/shard_map/ppermute | solution.py:31
  40.3 16.0 %copy-start = (f32[3,1024,256]{2,1,0:T(8,128)S(1)}, f32[3,1024,256]{2,1,0:T(8,128)}, u32[]{:S(2)}) copy-start(f32[3,1024,256]{2,1,0:T(8,128)} %solved_ref.5) | copy-start | bytes 9437188
  40.4 6.7 %collective-permute-start.14 = (f32[320,128]{1,0:T(8,128)S(1)}, f32[320,128]{1,0:T(8,128)S(1)}, u32[]{:S(2)}, u32[]{:S(2)}) collective-permute-start(f32[320,128]{1,0:T(8,128)S(1)} %add_subtract_fusion.1), channel_id=1, source_target_pairs={{0,4},{4,0},{8,12},{12,8},{16,20},{20,16},{24,28},{28,24},{1,5},{5... | collective-permute-start | bytes 491528 | tf_op jit(solution)/shard_map/ppermute | solution.py:31
  41.7 2.8 %collective-permute-start.21 = (f32[256,128]{1,0:T(8,128)S(1)}, f32[256,128]{1,0:T(8,128)S(1)}, u32[]{:S(2)}, u32[]{:S(2)}) collective-permute-start(f32[256,128]{1,0:T(8,128)S(1)} %slice.36), channel_id=1, source_target_pairs={{0,1},{1,0},{2,3},{3,2},{4,5},{5,4},{6,7},{7,6},{8,9},{9,8},{10,11... | collective-permute-start | bytes 393224 | tf_op jit(solution)/shard_map/ppermute | solution.py:31
  47.1 6.3 %collective-permute-start.22 = (f32[320,128]{1,0:T(8,128)S(1)}, f32[320,128]{1,0:T(8,128)S(1)}, u32[]{:S(2)}, u32[]{:S(2)}) collective-permute-start(f32[320,128]{1,0:T(8,128)S(1)} %add_subtract_fusion), channel_id=1, source_target_pairs={{0,8},{4,12},{8,0},{12,4},{16,24},{20,28},{24,16},{28,20},{1,9},{5... | collective-permute-start | bytes 491528 | tf_op jit(solution)/shard_map/ppermute | solution.py:31
  49.3 7.0 %collective-permute-start.26 = (f32[640,128]{1,0:T(8,128)S(1)}, f32[640,128]{1,0:T(8,128)S(1)}, u32[]{:S(2)}, u32[]{:S(2)}) collective-permute-start(f32[640,128]{1,0:T(8,128)S(1)} %get-tuple-element.34.z_ref.z0_ref), channel_id=1, source_target_pairs={{0,1},{1,0},{2,3},{3,2},{4,5},{5,4},{6,7},{7,6},{8,9},{9,8},{10,11... | collective-permute-start | bytes 983048 | tf_op jit(solution)/shard_map/ppermute | solution.py:31
  53.4 2.9 %collective-permute-start.25 = (f32[384,128]{1,0:T(8,128)S(1)}, f32[384,128]{1,0:T(8,128)S(1)}, u32[]{:S(2)}, u32[]{:S(2)}) collective-permute-start(f32[384,128]{1,0:T(8,128)S(1)} %shard_map.49), channel_id=1, source_target_pairs={{0,1},{1,0},{2,3},{3,2},{4,5},{5,4},{6,7},{7,6},{8,9},{9,8},{10,11... | collective-permute-start | bytes 589832 | tf_op jit(solution)/shard_map/ppermute | solution.py:31
  53.5 11.0 %collective-permute-start.24 = (f32[320,128]{1,0:T(8,128)S(1)}, f32[320,128]{1,0:T(8,128)S(1)}, u32[]{:S(2)}, u32[]{:S(2)}) collective-permute-start(f32[320,128]{1,0:T(8,128)S(1)} %add.44.refs_0_.own_ref), channel_id=1, source_target_pairs={{0,16},{4,20},{8,24},{12,28},{16,0},{20,4},{24,8},{28,12},{1,17},{... | collective-permute-start | bytes 491528 | tf_op jit(solution)/shard_map/ppermute | solution.py:31
  56.1 8.5 %collective-permute-start.23 = (f32[320,128]{1,0:T(8,128)S(1)}, f32[320,128]{1,0:T(8,128)S(1)}, u32[]{:S(2)}, u32[]{:S(2)}) collective-permute-start(f32[320,128]{1,0:T(8,128)S(1)} %add.44.refs_0_.own_ref), channel_id=1, source_target_pairs={{0,1},{1,0},{2,3},{3,2},{4,5},{5,4},{6,7},{7,6},{8,9},{9,8},{10,11... | collective-permute-start | bytes 491528 | tf_op jit(solution)/shard_map/ppermute | solution.py:31
  64.5 1.5 %collective-permute-start.27 = (f32[320,128]{1,0:T(8,128)S(1)}, f32[320,128]{1,0:T(8,128)S(1)}, u32[]{:S(2)}, u32[]{:S(2)}) collective-permute-start(f32[320,128]{1,0:T(8,128)S(1)} %shard_map.51.sib_ref), channel_id=1, source_target_pairs={{0,1},{1,0},{2,3},{3,2},{4,5},{5,4},{6,7},{7,6},{8,9},{9,8},{10,11... | collective-permute-start | bytes 491528 | tf_op jit(solution)/shard_map/ppermute | solution.py:31

commit v8 on v7

--- a/solution.py
+++ b/solution.py
@@ -110,15 +110,15 @@
         start += unit.shape[0]
 
 
-def product_kernel(groups, core_ref, gens_ref, solved_ref, *refs):
-    gens, solved, total, sems = refs[-4:]
-    outs = refs[-4 - 2 * len(groups) : -4]
+def product_kernel(groups, chunks, core_ref, gens_ref, solved_ref, *refs):
+    gens, solved, total, sems = refs[-4:] if chunks > 1 else (None, None, refs[-1], None)
+    refs = refs[:-4] if chunks > 1 else refs[:-1]
+    outs = refs[-2 * len(groups) :]
     blocks, lefts, rights = needed(groups)
     rhs_ref = refs[0] if 3 in rights else None
-    chunks = sems.shape[1]
-    block = gens.shape[1] // chunks
+    block = gens_ref.shape[1] // chunks
     copies = []
-    for chunk in range(chunks):
+    for chunk in range(chunks if chunks > 1 else 0):
         rows = pl.ds(chunk * block, block)
         row = [(gens_ref.at[level, rows], gens.at[place, rows]) for place, level in enumerate(lefts)]
         row += [(solved_ref.at[level, rows], solved.at[place, rows]) for place, level in enumerate(rights) if level < 3]
@@ -129,12 +129,17 @@
     places = {}
     for chunk in range(chunks):
         rows = pl.ds(chunk * block, block)
-        for copy in copies[chunk]:
+        for copy in copies[chunk] if chunks > 1 else ():
             copy.wait()
         right = {}
         for place, level in enumerate(rights):
-            right[level] = split(rhs_ref[rows, :] if level == 3 else solved[place, rows, :])
-        left = [[part.T for part in split(gens[place, rows, :])] for place in range(len(lefts))]
+            if level == 3:
+                right[level] = split(rhs_ref[rows, :])
+            else:
+                right[level] = split(solved[place, rows, :] if chunks > 1 else solved_ref[level])
+        left = []
+        for place, level in enumerate(lefts):
+            left.append([part.T for part in split(gens[place, rows, :] if chunks > 1 else gens_ref[level])])
         start = 0
         for firsts, seconds in blocks:
             value = dot_parts(
@@ -189,30 +194,32 @@
     return list(blocks.items()), sorted({left for left, _ in pairs}), rights
 
 
-def products(core, generators, solved_gens, rhs, groups, *after):
+def products(core, generators, solved_gens, rhs, groups, chunks, *after):
     rows = rhs.shape[0]
-    chunks = 4
     blocks, lefts, rights = needed(groups)
     width = sum(width_of(right) for right in rights)
     height = max(len(firsts) for firsts, _ in blocks) * RANK
     flops = sum(len(firsts) * width_of(right) for firsts, seconds in blocks for right in seconds) * 6 * rows * RANK
     outs = [struct(sum(rows_of(pair) for pair in group)) for group in groups for _ in range(2)]
     held = sum(level < 3 for level in rights)
-    given, specs = [generators, solved_gens], [HBM, HBM]
+    scratch = [pltpu.VMEM((height, width), jnp.float32)]
+    if chunks > 1:
+        scratch = [
+            pltpu.VMEM((len(lefts), rows, RANK), jnp.float32),
+            pltpu.VMEM((held, rows, RANK), jnp.float32),
+            *scratch,
+            pltpu.SemaphoreType.DMA((len(lefts) + held, chunks)),
+        ]
+    given, specs = [generators, solved_gens], [HBM if chunks > 1 else VMEM] * 2
     if 3 in rights:
         given, specs = given + [rhs], specs + [VMEM]
     return pl.pallas_call(
-        functools.partial(product_kernel, groups),
+        functools.partial(product_kernel, groups, chunks),
         in_specs=[SMEM] + specs + [ANY] * len(after),
         out_specs=[VMEM] * len(outs),
         out_shape=outs,
-        scratch_shapes=[
-            pltpu.VMEM((len(lefts), rows, RANK), jnp.float32),
-            pltpu.VMEM((held, rows, RANK), jnp.float32),
-            pltpu.VMEM((height, width), jnp.float32),
-            pltpu.SemaphoreType.DMA((len(lefts) + held, chunks)),
-        ],
-        compiler_params=pltpu.CompilerParams(vmem_limit_bytes=STREAM_LIMIT),
+        scratch_shapes=scratch,
+        compiler_params=pltpu.CompilerParams(vmem_limit_bytes=STREAM_LIMIT if chunks > 1 else VMEM_LIMIT),
         cost_estimate=cost(flops, rows * (len(lefts) * RANK + width)),
     )(core, *given, *after)
 
@@ -395,11 +402,11 @@
             value = value + swap(value, "rows", bit)
         return value
 
-    keep, send = products(core, generators, solved_gens, rhs, (((0, 0), (0, 1)),))
+    keep, send = products(core, generators, solved_gens, rhs, (((0, 0), (0, 1)),), 4)
     head = keep + swap(send, "sub", 0)
     token = swap(call(keep_kernel, struct(8), 0, core, send[:8], after=(head,)), "sub", 0)
     groups = (((0, 2), (0, 3)), ((1, 1), (1, 2), (1, 3)), ((2, 2), (2, 3)))
-    parts = products(core, generators, solved_gens, rhs, groups, token)
+    parts = products(core, generators, solved_gens, rhs, groups, 1, token)
     parts = [(keep, swap(send, "sub", 0)) for keep, send in zip(parts[::2], parts[1::2])]
     head = over_child(head)
     tail = over_child(parts[0][0] + parts[0][1])

time: 69.8 us -> 67.7 us (0.970)
  Pallas kernels: 21.3 us -> 19.2 us
    pallas_call x2, Pallas kernels: 8.03 us -> 5.89 us  [products(): pl.pallas_call(functools.partial(product_kernel, groups, chunks), in_spec...]
  transfers between devices with their start and end apart: 28 -> 28, of which waited for: 14 -> 15; matrix products, arithmetic and copies ran while one was open for 0% -> 0% of each run, Pallas kernels for 22% -> 19%
where the time goes in v8:
time: 67.7 us; the launch traced here: 67.5 us
  waiting for transfers between devices  24 us (35%)
  starting transfers between devices  23.7 us (35%)
  Pallas kernels  19.2 us (28%)
    ppermute x28, waiting for transfers between devices, swap(): return lax.ppermute(value, axis, pairs)  24 us
    ppermute x28, starting transfers between devices, swap(): return lax.ppermute(value, axis, pairs)  23.7 us
    pallas_call x12, Pallas kernels, call(): pl.pallas_call(kernel, in_specs=[SMEM] + [VMEM] * (len(values) - 1) + [AN...  8.56 us
    pallas_call x2, Pallas kernels, products(): pl.pallas_call(functools.partial(product_kernel, groups, chunks), in_spec...  5.89 us
    pallas_call x2, Pallas kernels, inverse(): pl.pallas_call(invert_kernel, in_specs=[SMEM] + [VMEM] * 4, out_specs=[VM...  4.73 us
  transfers between devices with their start and end apart: 28, of which 15 were waited for; matrix products, arithmetic and copies ran while one was open for 0% of the time, Pallas kernels for 19%

profile of v8, /device:TPU:0, one launch (start us, length us, event | category | flops | bytes accessed | tf_op | source)
XLA Modules:
  0.0 67.5 jit_solution(3956425500741549898)
XLA Ops:
  0.0 2.6 %shard_map.37 = (f32[448,128]{1,0:T(8,128)S(1)}, f32[448,128]{1,0:T(8,128)S(1)}) custom-call(s32[1]{0:T(128)} %bitcast.core_ref, f32[3,1024,256]{2,1,0:T(8,128)} %gens_ref.3, f32[3,1024,256]{2,1,0:T(8,128)} %solved_ref.5), custom_call_target="tpu_custom_call" | custom-call | flops 805306368 | bytes 3145728 | tf_op jit(solution)/shard_map/pallas_call | solution.py:216
  2.7 0.5 collective-permute-start
  3.2 1.1 %collective-permute-done = f32[448,128]{1,0:T(8,128)S(1)} collective-permute-done((f32[448,128]{1,0:T(8,128)S(1)}, f32[448,128]{1,0:T(8,128)S(1)}, u32[]{:S(2)}, u32[]{:S(2)}) %collective-permute-start) | collective-permute-done | bytes 229408 | tf_op jit(solution)/shard_map/ppermute | solution.py:31
  4.3 0.4 collective-permute-start.1
  4.8 2.7 %collective-permute-start.9 = (f32[448,128]{1,0:T(8,128)S(1)}, f32[448,128]{1,0:T(8,128)S(1)}, u32[]{:S(2)}, u32[]{:S(2)}) collective-permute-start(f32[448,128]{1,0:T(8,128)S(1)} %add.35.refs_0_), channel_id=1, source_target_pairs={{0,2},{1,3},{2,0},{3,1},{4,6},{5,7},{6,4},{7,5},{8,10},{9,11},{10,... | collective-permute-start | bytes 688136 | tf_op jit(solution)/shard_map/ppermute | solution.py:31
  7.4 0.0 collective-permute-done.1.refs_1_
  7.5 3.2 %shard_map.39 = (f32[384,128]{1,0:T(8,128)S(1)}, f32[384,128]{1,0:T(8,128)S(1)}, f32[576,128]{1,0:T(8,128)S(1)}, f32[576,128]{1,0:T(8,128)S(1)}, f32[320,128]{1,0:T(8,128)S(1)}, /*index=5*/f32[320,128]{1,0:T(8,128)S(1)}) custom-call(s32[1]{0:T(128)} %bitcast.core_ref, f32[3,1024,256]{2,1,0:T(8,128)S(1)} %copy-done.1, f32[3,1024,256]{2,1,0:T(8,128)S(1)} %copy-done, ...), custom_call_target="tpu_custom_call" | custom-call | flops 2214592512 | bytes 5767168 | tf_op jit(solution)/shard_map/pallas_call | solution.py:216
  10.7 0.1 collective-permute-start.4
  10.9 0.4 collective-permute-start.3
  11.3 0.9 %collective-permute-done.4 = f32[384,128]{1,0:T(8,128)S(1)} collective-permute-done((f32[384,128]{1,0:T(8,128)S(1)}, f32[384,128]{1,0:T(8,128)S(1)}, u32[]{:S(2)}, u32[]{:S(2)}) %collective-permute-start.4) | collective-permute-done | bytes 196640 | tf_op jit(solution)/shard_map/ppermute | solution.py:31
  12.3 1.1 %collective-permute-start.5 = (f32[384,128]{1,0:T(8,128)S(1)}, f32[384,128]{1,0:T(8,128)S(1)}, u32[]{:S(2)}, u32[]{:S(2)}) collective-permute-start(f32[384,128]{1,0:T(8,128)S(1)} %add.36), channel_id=1, source_target_pairs={{0,2},{1,3},{2,0},{3,1},{4,6},{5,7},{6,4},{7,5},{8,10},{9,11},{10,... | collective-permute-start | bytes 589832 | tf_op jit(solution)/shard_map/ppermute | solution.py:31
  13.3 0.2 collective-permute-done.9
  13.6 1.8 %collective-permute-start.10 = (f32[448,128]{1,0:T(8,128)S(1)}, f32[448,128]{1,0:T(8,128)S(1)}, u32[]{:S(2)}, u32[]{:S(2)}) collective-permute-start(f32[448,128]{1,0:T(8,128)S(1)} %add.40.own_ref.head_ref), channel_id=1, source_target_pairs={{0,4},{4,0},{8,12},{12,8},{16,20},{20,16},{24,28},{28,24},{1,5},{5... | collective-permute-start | bytes 688136 | tf_op jit(solution)/shard_map/ppermute | solution.py:31
  15.4 0.0 collective-permute-start.11
  15.4 3.9 %collective-permute-done.5 = f32[384,128]{1,0:T(8,128)S(1)} collective-permute-done((f32[384,128]{1,0:T(8,128)S(1)}, f32[384,128]{1,0:T(8,128)S(1)}, u32[]{:S(2)}, u32[]{:S(2)}) %collective-permute-start.5) | collective-permute-done | bytes 196640 | tf_op jit(solution)/shard_map/ppermute | solution.py:31
  19.3 0.0 collective-permute-done.3.second_ref
  19.3 1.1 %collective-permute-start.6 = (f32[576,128]{1,0:T(8,128)S(1)}, f32[576,128]{1,0:T(8,128)S(1)}, u32[]{:S(2)}, u32[]{:S(2)}) collective-permute-start(f32[576,128]{1,0:T(8,128)S(1)} %shard_map.40), channel_id=1, source_target_pairs={{0,2},{1,3},{2,0},{3,1},{4,6},{5,7},{6,4},{7,5},{8,10},{9,11},{10,... | collective-permute-start | bytes 884744 | tf_op jit(solution)/shard_map/ppermute | solution.py:31
  20.4 1.5 %collective-permute-start.13 = (f32[384,128]{1,0:T(8,128)S(1)}, f32[384,128]{1,0:T(8,128)S(1)}, u32[]{:S(2)}, u32[]{:S(2)}) collective-permute-start(f32[384,128]{1,0:T(8,128)S(1)} %add.37.refs_0_.tail_ref.own_ref), channel_id=1, source_target_pairs={{0,4},{4,0},{8,12},{12,8},{16,20},{20,16},{24,28},{28,24},{1,5},{5... | collective-permute-start | bytes 589832 | tf_op jit(solution)/shard_map/ppermute | solution.py:31
  21.9 0.0 collective-permute-done.10.sib_ref.head_sib_ref
  22.0 0.1 collective-permute-start.12
  22.0 0.5 collective-permute-start.2
  22.6 0.0 collective-permute-done.11.own_other_ref.head_other_ref
  22.6 0.1 collective-permute-start.8
  22.7 0.6 collective-permute-done.12.sib_other_ref
  23.3 2.3 %shard_map.42 = (f32[256,256]{1,0:T(8,128)S(1)}, f32[256,256]{1,0:T(8,128)S(1)}) custom-call(s32[1]{0:T(128)} %bitcast.core_ref, f32[448,128]{1,0:T(8,128)S(1)} %add.40.own_ref.head_ref, f32[448,128]{1,0:T(8,128)S(1)} %collective-permute-done.10.sib_ref.head_sib_ref, f32[448,128]{1,0:T(8,128)S(1)} %collective-permute-done.11.own_other_ref.head_other_ref, ...), custom_call_target="tpu_custom_call" | custom-call | flops 905969664 | bytes 1048576 | tf_op jit(solution)/shard_map/pallas_call | solution.py:297
  25.6 0.7 %collective-permute-done.13.tail_sib_ref = f32[384,128]{1,0:T(8,128)S(1)} collective-permute-done((f32[384,128]{1,0:T(8,128)S(1)}, f32[384,128]{1,0:T(8,128)S(1)}, u32[]{:S(2)}, u32[]{:S(2)}) %collective-permute-start.13) | collective-permute-done | bytes 196640 | tf_op jit(solution)/shard_map/ppermute | solution.py:31
  26.3 1.1 %shard_map.43 = (f32[640,128]{1,0:T(8,128)S(1)}, f32[576,128]{1,0:T(8,128)S(1)}) custom-call(s32[1]{0:T(128)} %bitcast.core_ref, f32[256,256]{1,0:T(8,128)S(1)} %get-tuple-element.32.inverse_ref, f32[256,256]{1,0:T(8,128)S(1)} %get-tuple-element.33.p_sib_ref, f32[448,128]{1,0:T(8,128)S(1)} %add.40.own_ref.head_ref, ...), custom_call_target="tpu_custom_call" | custom-call | flops 650000000 | bytes 2228228 | tf_op jit(solution)/shard_map/pallas_call | solution.py:285
  27.5 0.2 collective-permute-done.6
  27.7 1.6 %collective-permute-start.15 = (f32[192,128]{1,0:T(8,128)S(1)}, f32[192,128]{1,0:T(8,128)S(1)}, u32[]{:S(2)}, u32[]{:S(2)}) collective-permute-start(f32[192,128]{1,0:T(8,128)S(1)} %shard_map.44.refs_0_), channel_id=1, source_target_pairs={{0,4},{4,0},{8,12},{12,8},{16,20},{20,16},{24,28},{28,24},{1,5},{5... | collective-permute-start | bytes 294920 | tf_op jit(solution)/shard_map/ppermute | solution.py:31
  29.4 0.6 collective-permute-start.19
  29.9 0.0 collective-permute-done.2.second_ref
  30.0 1.1 %collective-permute-start.7 = (f32[320,128]{1,0:T(8,128)S(1)}, f32[320,128]{1,0:T(8,128)S(1)}, u32[]{:S(2)}, u32[]{:S(2)}) collective-permute-start(f32[320,128]{1,0:T(8,128)S(1)} %shard_map.41), channel_id=1, source_target_pairs={{0,2},{1,3},{2,0},{3,1},{4,6},{5,7},{6,4},{7,5},{8,10},{9,11},{10,... | collective-permute-start | bytes 491528 | tf_op jit(solution)/shard_map/ppermute | solution.py:31
  31.1 2.4 %collective-permute-done.15 = f32[192,128]{1,0:T(8,128)S(1)} collective-permute-done((f32[192,128]{1,0:T(8,128)S(1)}, f32[192,128]{1,0:T(8,128)S(1)}, u32[]{:S(2)}, u32[]{:S(2)}) %collective-permute-start.15) | collective-permute-done | bytes 98336 | tf_op jit(solution)/shard_map/ppermute | solution.py:31
  33.5 1.6 %collective-permute-start.16 = (f32[192,128]{1,0:T(8,128)S(1)}, f32[192,128]{1,0:T(8,128)S(1)}, u32[]{:S(2)}, u32[]{:S(2)}) collective-permute-start(f32[192,128]{1,0:T(8,128)S(1)} %add.42.own_ref), channel_id=1, source_target_pairs={{0,8},{4,12},{8,0},{12,4},{16,24},{20,28},{24,16},{28,20},{1,9},{5... | collective-permute-start | bytes 294920 | tf_op jit(solution)/shard_map/ppermute | solution.py:31
  35.2 0.0 collective-permute-done.8.own_other_ref
  35.2 0.4 shard_map.46
  35.6 0.1 collective-permute-start.17
  35.7 0.3 collective-permute-done.19
  36.0 1.6 %collective-permute-start.20 = (f32[384,128]{1,0:T(8,128)S(1)}, f32[384,128]{1,0:T(8,128)S(1)}, u32[]{:S(2)}, u32[]{:S(2)}) collective-permute-start(f32[384,128]{1,0:T(8,128)S(1)} %add.43.own_ref), channel_id=1, source_target_pairs={{0,8},{4,12},{8,0},{12,4},{16,24},{20,28},{24,16},{28,20},{1,9},{5... | collective-permute-start | bytes 589832 | tf_op jit(solution)/shard_map/ppermute | solution.py:31
  37.7 0.5 collective-permute-done.16.sib_ref
  38.2 0.0 collective-permute-start.18
  38.2 0.0 collective-permute-done.7
  38.2 1.3 %collective-permute-start.14 = (f32[320,128]{1,0:T(8,128)S(1)}, f32[320,128]{1,0:T(8,128)S(1)}, u32[]{:S(2)}, u32[]{:S(2)}) collective-permute-start(f32[320,128]{1,0:T(8,128)S(1)} %add_subtract_fusion.1), channel_id=1, source_target_pairs={{0,4},{4,0},{8,12},{12,8},{16,20},{20,16},{24,28},{28,24},{1,5},{5... | collective-permute-start | bytes 491528 | tf_op jit(solution)/shard_map/ppermute | solution.py:31
  39.5 0.3 collective-permute-start.21
  39.8 0.0 collective-permute-done.17.own_other_ref
  39.8 0.0 collective-permute-done.18.sib_other_ref
  39.8 2.5 %shard_map.47 = (f32[256,256]{1,0:T(8,128)S(1)}, f32[256,256]{1,0:T(8,128)S(1)}) custom-call(s32[1]{0:T(128)} %bitcast.core_ref, f32[192,128]{1,0:T(8,128)S(1)} %add.42.own_ref, f32[192,128]{1,0:T(8,128)S(1)} %collective-permute-done.16.sib_ref, f32[192,128]{1,0:T(8,128)S(1)} %collective-permute-done.17.own_other_ref, ...), custom_call_target="tpu_custom_call" | custom-call | flops 905969664 | bytes 1048576 | tf_op jit(solution)/shard_map/pallas_call | solution.py:297
  42.3 0.0 collective-permute-done.21.own_other_ref
  42.3 0.7 %collective-permute-done.20.sib_ref = f32[384,128]{1,0:T(8,128)S(1)} collective-permute-done((f32[384,128]{1,0:T(8,128)S(1)}, f32[384,128]{1,0:T(8,128)S(1)}, u32[]{:S(2)}, u32[]{:S(2)}) %collective-permute-start.20) | collective-permute-done | bytes 196640 | tf_op jit(solution)/shard_map/ppermute | solution.py:31
  43.1 1.0 %shard_map.48 = (f32[384,128]{1,0:T(8,128)S(1)}, f32[320,128]{1,0:T(8,128)S(1)}) custom-call(s32[1]{0:T(128)} %bitcast.core_ref, f32[256,256]{1,0:T(8,128)S(1)} %get-tuple-element.36.inverse_ref, f32[256,256]{1,0:T(8,128)S(1)} %get-tuple-element.37.p_sib_ref, f32[384,128]{1,0:T(8,128)S(1)} %add.43.own_ref, f32[384,128]{1,0:T(8,128)S(1)} %collective-permute-done.20.sib_ref, ...), custom_call_target="tpu_custom_call" | custom-call | flops 251658240 | bytes 1409028 | tf_op jit(solution)/shard_map/pallas_call | solution.py:285
  44.1 0.8 %collective-permute-done.14 = f32[320,128]{1,0:T(8,128)S(1)} collective-permute-done((f32[320,128]{1,0:T(8,128)S(1)}, f32[320,128]{1,0:T(8,128)S(1)}, u32[]{:S(2)}, u32[]{:S(2)}) %collective-permute-start.14) | collective-permute-done | bytes 163872 | tf_op jit(solution)/shard_map/ppermute | solution.py:31
  45.0 2.2 %collective-permute-start.22 = (f32[320,128]{1,0:T(8,128)S(1)}, f32[320,128]{1,0:T(8,128)S(1)}, u32[]{:S(2)}, u32[]{:S(2)}) collective-permute-start(f32[320,128]{1,0:T(8,128)S(1)} %add_subtract_fusion), channel_id=1, source_target_pairs={{0,8},{4,12},{8,0},{12,4},{16,24},{20,28},{24,16},{28,20},{1,9},{5... | collective-permute-start | bytes 491528 | tf_op jit(solution)/shard_map/ppermute | solution.py:31
  47.2 0.0 collective-permute-start.26
  47.2 4.1 %collective-permute-done.22 = f32[320,128]{1,0:T(8,128)S(1)} collective-permute-done((f32[320,128]{1,0:T(8,128)S(1)}, f32[320,128]{1,0:T(8,128)S(1)}, u32[]{:S(2)}, u32[]{:S(2)}) %collective-permute-start.22) | collective-permute-done | bytes 163872 | tf_op jit(solution)/shard_map/ppermute | solution.py:31
  51.3 0.1 collective-permute-start.25
  51.4 2.6 %collective-permute-start.24 = (f32[320,128]{1,0:T(8,128)S(1)}, f32[320,128]{1,0:T(8,128)S(1)}, u32[]{:S(2)}, u32[]{:S(2)}) collective-permute-start(f32[320,128]{1,0:T(8,128)S(1)} %add.44.refs_0_.own_ref), channel_id=1, source_target_pairs={{0,16},{4,20},{8,24},{12,28},{16,0},{20,4},{24,8},{28,12},{1,17},{... | collective-permute-start | bytes 491528 | tf_op jit(solution)/shard_map/ppermute | solution.py:31
  54.0 0.2 collective-permute-start.23
  54.2 0.0 collective-permute-done.26.z0_other_ref
  54.2 0.0 collective-permute-done.25.z1_other_ref
  54.2 2.2 %shard_map.50 = (bf16[1024,256]{1,0:T(8,128)(2,1)S(1)}, bf16[1024,256]{1,0:T(8,128)(2,1)S(1)}, f32[1024,128]{1,0:T(8,128)S(1)}) custom-call(s32[1]{0:T(128)} %bitcast.core_ref, f32[384,128]{1,0:T(8,128)S(1)} %get-tuple-element.39.value_ref.z1_ref, f32[384,128]{1,0:T(8,128)S(1)} %collective-permute-done.25.z1_other_ref, ...), custom_call_target="tpu_custom_call" | custom-call | flops 1207959552 | bytes 7340036 | tf_op jit(solution)/shard_map/pallas_call | solution.py:285
  56.4 6.0 %collective-permute-done.24.value_ref = f32[320,128]{1,0:T(8,128)S(1)} collective-permute-done((f32[320,128]{1,0:T(8,128)S(1)}, f32[320,128]{1,0:T(8,128)S(1)}, u32[]{:S(2)}, u32[]{:S(2)}) %collective-permute-start.24) | collective-permute-done | bytes 163872 | tf_op jit(solution)/shard_map/ppermute | solution.py:31
  62.4 0.1 collective-permute-start.27
  62.5 1.4 %collective-permute-done.27.sib_other_ref = f32[320,128]{1,0:T(8,128)S(1)} collective-permute-done((f32[320,128]{1,0:T(8,128)S(1)}, f32[320,128]{1,0:T(8,128)S(1)}, u32[]{:S(2)}, u32[]{:S(2)}) %collective-permute-start.27) | collective-permute-done | bytes 163872 | tf_op jit(solution)/shard_map/ppermute | solution.py:31
  63.9 3.7 %shard_map.52 = f32[1024,128]{1,0:T(8,128)} custom-call(s32[1]{0:T(128)} %bitcast.core_ref, f32[320,128]{1,0:T(8,128)S(1)} %add.44.refs_0_.own_ref, f32[320,128]{1,0:T(8,128)S(1)} %collective-permute-done.23.own_other_ref, f32[320,128]{1,0:T(8,128)S(1)} %shard_map.51.sib_ref, f32[320,128]{1,0:T(8,128)S(1)} %collective-permute-done.27.sib_other_ref, ...), custom_call_target="tpu_custom_call" | custom-call | flops 1107296256 | bytes 3801092 | tf_op jit(solution)/shard_map/pallas_call | solution.py:285
  (32 shorter events, 0.5 us)
Async XLA Ops:
  0.0 7.5 %copy-start = (f32[3,1024,256]{2,1,0:T(8,128)S(1)}, f32[3,1024,256]{2,1,0:T(8,128)}, u32[]{:S(2)}) copy-start(f32[3,1024,256]{2,1,0:T(8,128)} %solved_ref.5) | copy-start | bytes 9437188
  0.0 7.5 %copy-start.1 = (f32[3,1024,256]{2,1,0:T(8,128)S(1)}, f32[3,1024,256]{2,1,0:T(8,128)}, u32[]{:S(2)}) copy-start(f32[3,1024,256]{2,1,0:T(8,128)} %gens_ref.3) | copy-start | bytes 9437188
  0.0 7.5 %copy-start.2 = (f32[1024,128]{1,0:T(8,128)S(1)}, f32[1024,128]{1,0:T(8,128)}, u32[]{:S(2)}) copy-start(f32[1024,128]{1,0:T(8,128)} %rhs_ref.1) | copy-start | bytes 1572868
  2.7 1.6 %collective-permute-start = (f32[448,128]{1,0:T(8,128)S(1)}, f32[448,128]{1,0:T(8,128)S(1)}, u32[]{:S(2)}, u32[]{:S(2)}) collective-permute-start(f32[448,128]{1,0:T(8,128)S(1)} %get-tuple-element.24), channel_id=1, source_target_pairs={{0,1},{1,0},{2,3},{3,2},{4,5},{5,4},{6,7},{7,6},{8,9},{9,8},{10,11... | collective-permute-start | bytes 688136 | tf_op jit(solution)/shard_map/ppermute | solution.py:31
  4.3 3.1 %collective-permute-start.1 = (f32[8,128]{1,0:T(8,128)S(1)}, f32[8,128]{1,0:T(8,128)S(1)}, u32[]{:S(2)}, u32[]{:S(2)}) collective-permute-start(f32[8,128]{1,0:T(8,128)S(1)} %shard_map.38), channel_id=1, source_target_pairs={{0,1},{1,0},{2,3},{3,2},{4,5},{5,4},{6,7},{7,6},{8,9},{9,8},{10,11... | collective-permute-start | bytes 12296 | tf_op jit(solution)/shard_map/ppermute | solution.py:31
  4.8 8.8 %collective-permute-start.9 = (f32[448,128]{1,0:T(8,128)S(1)}, f32[448,128]{1,0:T(8,128)S(1)}, u32[]{:S(2)}, u32[]{:S(2)}) collective-permute-start(f32[448,128]{1,0:T(8,128)S(1)} %add.35.refs_0_), channel_id=1, source_target_pairs={{0,2},{1,3},{2,0},{3,1},{4,6},{5,7},{6,4},{7,5},{8,10},{9,11},{10,... | collective-permute-start | bytes 688136 | tf_op jit(solution)/shard_map/ppermute | solution.py:31
  10.7 1.5 %collective-permute-start.4 = (f32[384,128]{1,0:T(8,128)S(1)}, f32[384,128]{1,0:T(8,128)S(1)}, u32[]{:S(2)}, u32[]{:S(2)}) collective-permute-start(f32[384,128]{1,0:T(8,128)S(1)} %get-tuple-element.31), channel_id=1, source_target_pairs={{0,1},{1,0},{2,3},{3,2},{4,5},{5,4},{6,7},{7,6},{8,9},{9,8},{10,11... | collective-permute-start | bytes 589832 | tf_op jit(solution)/shard_map/ppermute | solution.py:31
  10.9 8.4 %collective-permute-start.3 = (f32[576,128]{1,0:T(8,128)S(1)}, f32[576,128]{1,0:T(8,128)S(1)}, u32[]{:S(2)}, u32[]{:S(2)}) collective-permute-start(f32[576,128]{1,0:T(8,128)S(1)} %get-tuple-element.29), channel_id=1, source_target_pairs={{0,1},{1,0},{2,3},{3,2},{4,5},{5,4},{6,7},{7,6},{8,9},{9,8},{10,11... | collective-permute-start | bytes 884744 | tf_op jit(solution)/shard_map/ppermute | solution.py:31
  12.3 7.0 %collective-permute-start.5 = (f32[384,128]{1,0:T(8,128)S(1)}, f32[384,128]{1,0:T(8,128)S(1)}, u32[]{:S(2)}, u32[]{:S(2)}) collective-permute-start(f32[384,128]{1,0:T(8,128)S(1)} %add.36), channel_id=1, source_target_pairs={{0,2},{1,3},{2,0},{3,1},{4,6},{5,7},{6,4},{7,5},{8,10},{9,11},{10,... | collective-permute-start | bytes 589832 | tf_op jit(solution)/shard_map/ppermute | solution.py:31
  13.6 8.3 %collective-permute-start.10 = (f32[448,128]{1,0:T(8,128)S(1)}, f32[448,128]{1,0:T(8,128)S(1)}, u32[]{:S(2)}, u32[]{:S(2)}) collective-permute-start(f32[448,128]{1,0:T(8,128)S(1)} %add.40.own_ref.head_ref), channel_id=1, source_target_pairs={{0,4},{4,0},{8,12},{12,8},{16,20},{20,16},{24,28},{28,24},{1,5},{5... | collective-permute-start | bytes 688136 | tf_op jit(solution)/shard_map/ppermute | solution.py:31
  15.4 7.2 %collective-permute-start.11 = (f32[448,128]{1,0:T(8,128)S(1)}, f32[448,128]{1,0:T(8,128)S(1)}, u32[]{:S(2)}, u32[]{:S(2)}) collective-permute-start(f32[448,128]{1,0:T(8,128)S(1)} %add.40.own_ref.head_ref), channel_id=1, source_target_pairs={{0,1},{1,0},{2,3},{3,2},{4,5},{5,4},{6,7},{7,6},{8,9},{9,8},{10,11... | collective-permute-start | bytes 688136 | tf_op jit(solution)/shard_map/ppermute | solution.py:31
  19.3 8.3 %collective-permute-start.6 = (f32[576,128]{1,0:T(8,128)S(1)}, f32[576,128]{1,0:T(8,128)S(1)}, u32[]{:S(2)}, u32[]{:S(2)}) collective-permute-start(f32[576,128]{1,0:T(8,128)S(1)} %shard_map.40), channel_id=1, source_target_pairs={{0,2},{1,3},{2,0},{3,1},{4,6},{5,7},{6,4},{7,5},{8,10},{9,11},{10,... | collective-permute-start | bytes 884744 | tf_op jit(solution)/shard_map/ppermute | solution.py:31
  20.4 5.9 %collective-permute-start.13 = (f32[384,128]{1,0:T(8,128)S(1)}, f32[384,128]{1,0:T(8,128)S(1)}, u32[]{:S(2)}, u32[]{:S(2)}) collective-permute-start(f32[384,128]{1,0:T(8,128)S(1)} %add.37.refs_0_.tail_ref.own_ref), channel_id=1, source_target_pairs={{0,4},{4,0},{8,12},{12,8},{16,20},{20,16},{24,28},{28,24},{1,5},{5... | collective-permute-start | bytes 589832 | tf_op jit(solution)/shard_map/ppermute | solution.py:31
  22.0 1.4 %collective-permute-start.12 = (f32[192,128]{1,0:T(8,128)S(1)}, f32[192,128]{1,0:T(8,128)S(1)}, u32[]{:S(2)}, u32[]{:S(2)}) collective-permute-start(f32[192,128]{1,0:T(8,128)S(1)} %slice.33), channel_id=1, source_target_pairs={{0,1},{1,0},{2,3},{3,2},{4,5},{5,4},{6,7},{7,6},{8,9},{9,8},{10,11... | collective-permute-start | bytes 294920 | tf_op jit(solution)/shard_map/ppermute | solution.py:31
  22.0 7.9 %collective-permute-start.2 = (f32[320,128]{1,0:T(8,128)S(1)}, f32[320,128]{1,0:T(8,128)S(1)}, u32[]{:S(2)}, u32[]{:S(2)}) collective-permute-start(f32[320,128]{1,0:T(8,128)S(1)} %get-tuple-element.27), channel_id=1, source_target_pairs={{0,1},{1,0},{2,3},{3,2},{4,5},{5,4},{6,7},{7,6},{8,9},{9,8},{10,11... | collective-permute-start | bytes 491528 | tf_op jit(solution)/shard_map/ppermute | solution.py:31
  22.6 12.6 %collective-permute-start.8 = (f32[256,128]{1,0:T(8,128)S(1)}, f32[256,128]{1,0:T(8,128)S(1)}, u32[]{:S(2)}, u32[]{:S(2)}) collective-permute-start(f32[256,128]{1,0:T(8,128)S(1)} %slice.32), channel_id=1, source_target_pairs={{0,1},{1,0},{2,3},{3,2},{4,5},{5,4},{6,7},{7,6},{8,9},{9,8},{10,11... | collective-permute-start | bytes 393224 | tf_op jit(solution)/shard_map/ppermute | solution.py:31
  27.7 5.8 %collective-permute-start.15 = (f32[192,128]{1,0:T(8,128)S(1)}, f32[192,128]{1,0:T(8,128)S(1)}, u32[]{:S(2)}, u32[]{:S(2)}) collective-permute-start(f32[192,128]{1,0:T(8,128)S(1)} %shard_map.44.refs_0_), channel_id=1, source_target_pairs={{0,4},{4,0},{8,12},{12,8},{16,20},{20,16},{24,28},{28,24},{1,5},{5... | collective-permute-start | bytes 294920 | tf_op jit(solution)/shard_map/ppermute | solution.py:31
  29.4 6.6 %collective-permute-start.19 = (f32[384,128]{1,0:T(8,128)S(1)}, f32[384,128]{1,0:T(8,128)S(1)}, u32[]{:S(2)}, u32[]{:S(2)}) collective-permute-start(f32[384,128]{1,0:T(8,128)S(1)} %shard_map.45.refs_0_), channel_id=1, source_target_pairs={{0,4},{4,0},{8,12},{12,8},{16,20},{20,16},{24,28},{28,24},{1,5},{5... | collective-permute-start | bytes 589832 | tf_op jit(solution)/shard_map/ppermute | solution.py:31
  30.0 8.2 %collective-permute-start.7 = (f32[320,128]{1,0:T(8,128)S(1)}, f32[320,128]{1,0:T(8,128)S(1)}, u32[]{:S(2)}, u32[]{:S(2)}) collective-permute-start(f32[320,128]{1,0:T(8,128)S(1)} %shard_map.41), channel_id=1, source_target_pairs={{0,2},{1,3},{2,0},{3,1},{4,6},{5,7},{6,4},{7,5},{8,10},{9,11},{10,... | collective-permute-start | bytes 491528 | tf_op jit(solution)/shard_map/ppermute | solution.py:31
  33.5 4.7 %collective-permute-start.16 = (f32[192,128]{1,0:T(8,128)S(1)}, f32[192,128]{1,0:T(8,128)S(1)}, u32[]{:S(2)}, u32[]{:S(2)}) collective-permute-start(f32[192,128]{1,0:T(8,128)S(1)} %add.42.own_ref), channel_id=1, source_target_pairs={{0,8},{4,12},{8,0},{12,4},{16,24},{20,28},{24,16},{28,20},{1,9},{5... | collective-permute-start | bytes 294920 | tf_op jit(solution)/shard_map/ppermute | solution.py:31
  35.6 4.2 %collective-permute-start.17 = (f32[192,128]{1,0:T(8,128)S(1)}, f32[192,128]{1,0:T(8,128)S(1)}, u32[]{:S(2)}, u32[]{:S(2)}) collective-permute-start(f32[192,128]{1,0:T(8,128)S(1)} %add.42.own_ref), channel_id=1, source_target_pairs={{0,1},{1,0},{2,3},{3,2},{4,5},{5,4},{6,7},{7,6},{8,9},{9,8},{10,11... | collective-permute-start | bytes 294920 | tf_op jit(solution)/shard_map/ppermute | solution.py:31
  36.0 7.0 %collective-permute-start.20 = (f32[384,128]{1,0:T(8,128)S(1)}, f32[384,128]{1,0:T(8,128)S(1)}, u32[]{:S(2)}, u32[]{:S(2)}) collective-permute-start(f32[384,128]{1,0:T(8,128)S(1)} %add.43.own_ref), channel_id=1, source_target_pairs={{0,8},{4,12},{8,0},{12,4},{16,24},{20,28},{24,16},{28,20},{1,9},{5... | collective-permute-start | bytes 589832 | tf_op jit(solution)/shard_map/ppermute | solution.py:31
  38.2 1.6 %collective-permute-start.18 = (f32[192,128]{1,0:T(8,128)S(1)}, f32[192,128]{1,0:T(8,128)S(1)}, u32[]{:S(2)}, u32[]{:S(2)}) collective-permute-start(f32[192,128]{1,0:T(8,128)S(1)} %collective-permute-done.16.sib_ref), channel_id=1, source_target_pairs={{0,1},{1,0},{2,3},{3,2},{4,5},{5,4},{6,7},{7,6},{8,9},{9,8},{10,11... | collective-permute-start | bytes 294920 | tf_op jit(solution)/shard_map/ppermute | solution.py:31
  38.2 6.7 %collective-permute-start.14 = (f32[320,128]{1,0:T(8,128)S(1)}, f32[320,128]{1,0:T(8,128)S(1)}, u32[]{:S(2)}, u32[]{:S(2)}) collective-permute-start(f32[320,128]{1,0:T(8,128)S(1)} %add_subtract_fusion.1), channel_id=1, source_target_pairs={{0,4},{4,0},{8,12},{12,8},{16,20},{20,16},{24,28},{28,24},{1,5},{5... | collective-permute-start | bytes 491528 | tf_op jit(solution)/shard_map/ppermute | solution.py:31
  39.5 2.8 %collective-permute-start.21 = (f32[256,128]{1,0:T(8,128)S(1)}, f32[256,128]{1,0:T(8,128)S(1)}, u32[]{:S(2)}, u32[]{:S(2)}) collective-permute-start(f32[256,128]{1,0:T(8,128)S(1)} %slice.36), channel_id=1, source_target_pairs={{0,1},{1,0},{2,3},{3,2},{4,5},{5,4},{6,7},{7,6},{8,9},{9,8},{10,11... | collective-permute-start | bytes 393224 | tf_op jit(solution)/shard_map/ppermute | solution.py:31
  45.0 6.3 %collective-permute-start.22 = (f32[320,128]{1,0:T(8,128)S(1)}, f32[320,128]{1,0:T(8,128)S(1)}, u32[]{:S(2)}, u32[]{:S(2)}) collective-permute-start(f32[320,128]{1,0:T(8,128)S(1)} %add_subtract_fusion), channel_id=1, source_target_pairs={{0,8},{4,12},{8,0},{12,4},{16,24},{20,28},{24,16},{28,20},{1,9},{5... | collective-permute-start | bytes 491528 | tf_op jit(solution)/shard_map/ppermute | solution.py:31
  47.2 7.0 %collective-permute-start.26 = (f32[640,128]{1,0:T(8,128)S(1)}, f32[640,128]{1,0:T(8,128)S(1)}, u32[]{:S(2)}, u32[]{:S(2)}) collective-permute-start(f32[640,128]{1,0:T(8,128)S(1)} %get-tuple-element.34.z_ref.z0_ref), channel_id=1, source_target_pairs={{0,1},{1,0},{2,3},{3,2},{4,5},{5,4},{6,7},{7,6},{8,9},{9,8},{10,11... | collective-permute-start | bytes 983048 | tf_op jit(solution)/shard_map/ppermute | solution.py:31
  51.3 2.9 %collective-permute-start.25 = (f32[384,128]{1,0:T(8,128)S(1)}, f32[384,128]{1,0:T(8,128)S(1)}, u32[]{:S(2)}, u32[]{:S(2)}) collective-permute-start(f32[384,128]{1,0:T(8,128)S(1)} %shard_map.49), channel_id=1, source_target_pairs={{0,1},{1,0},{2,3},{3,2},{4,5},{5,4},{6,7},{7,6},{8,9},{9,8},{10,11... | collective-permute-start | bytes 589832 | tf_op jit(solution)/shard_map/ppermute | solution.py:31
  51.4 11.0 %collective-permute-start.24 = (f32[320,128]{1,0:T(8,128)S(1)}, f32[320,128]{1,0:T(8,128)S(1)}, u32[]{:S(2)}, u32[]{:S(2)}) collective-permute-start(f32[320,128]{1,0:T(8,128)S(1)} %add.44.refs_0_.own_ref), channel_id=1, source_target_pairs={{0,16},{4,20},{8,24},{12,28},{16,0},{20,4},{24,8},{28,12},{1,17},{... | collective-permute-start | bytes 491528 | tf_op jit(solution)/shard_map/ppermute | solution.py:31
  54.0 8.5 %collective-permute-start.23 = (f32[320,128]{1,0:T(8,128)S(1)}, f32[320,128]{1,0:T(8,128)S(1)}, u32[]{:S(2)}, u32[]{:S(2)}) collective-permute-start(f32[320,128]{1,0:T(8,128)S(1)} %add.44.refs_0_.own_ref), channel_id=1, source_target_pairs={{0,1},{1,0},{2,3},{3,2},{4,5},{5,4},{6,7},{7,6},{8,9},{9,8},{10,11... | collective-permute-start | bytes 491528 | tf_op jit(solution)/shard_map/ppermute | solution.py:31
  62.4 1.5 %collective-permute-start.27 = (f32[320,128]{1,0:T(8,128)S(1)}, f32[320,128]{1,0:T(8,128)S(1)}, u32[]{:S(2)}, u32[]{:S(2)}) collective-permute-start(f32[320,128]{1,0:T(8,128)S(1)} %shard_map.51.sib_ref), channel_id=1, source_target_pairs={{0,1},{1,0},{2,3},{3,2},{4,5},{5,4},{6,7},{7,6},{8,9},{9,8},{10,11... | collective-permute-start | bytes 491528 | tf_op jit(solution)/shard_map/ppermute | solution.py:31

commit v9 on v8

--- a/solution.py
+++ b/solution.py
@@ -15,6 +15,7 @@
 TOLERANCE = 1e-7
 DIVERGED = 1e4
 FIRST_FLOPS = 6.5e8
+INVERT_FLOPS = 9e8
 THIRD_FLOPS = 3e9
 VMEM_LIMIT = 40 * 2**20
 STREAM_LIMIT = 52 * 2**20
@@ -301,7 +302,7 @@
         out_shape=[struct(RANK, RANK)] * 2,
         scratch_shapes=[pltpu.VMEM((RANK, RANK), jnp.float32)],
         compiler_params=pltpu.CompilerParams(vmem_limit_bytes=VMEM_LIMIT),
-        cost_estimate=cost(6 * 9 * RANK**3, 4 * RANK * RANK),
+        cost_estimate=cost(INVERT_FLOPS, 0),
     )(core, own, sib, own_other, sib_other)
 
 
@@ -316,22 +317,34 @@
     store(out_ref.at[SYM:], value[:, HALF:])
 
 
-def last_parts(core, crossed, z, out_ref):
+def last_parts(core, crossed, z):
     value = dot_turned(crossed, z)
-    out_ref[:SYM, :] = symmetric_half(core, value[:, :HALF])
-    store(out_ref.at[SYM:], value[:, HALF:])
-
-
-def third_kernel(core_ref, own_ref, own_other_ref, z_ref, *refs):
-    core = core_ref[0]
-    last_parts(core, in_order(core, own_ref[:RANK, :], own_other_ref[...]), unpack(z_ref.at[RANK:]), refs[-1])
-
-
-def middle_kernel(core_ref, inverse_ref, p_sib_ref, own_ref, sib_ref, own_other_ref, z_ref, out_ref):
-    core = core_ref[0]
-    z = dot(inverse_ref[...], unpack(sib_ref) - dot(p_sib_ref[...], unpack(own_ref)))
+    return jnp.concatenate([symmetric_half(core, value[:, :HALF]), *pack(value[:, HALF:])], axis=0)
+
+
+def third_kernel(share, core_ref, own_ref, own_other_ref, z_ref, third_ref, *refs):
+    core = core_ref[0]
+    crossed = in_order(core, own_ref[:RANK, :], own_other_ref[...])
+    refs[-1][...] = third_ref[...] - share * last_parts(core, crossed, unpack(z_ref.at[RANK:]))
+
+
+def middle_kernel(
+    core_ref, inverse_ref, p_sib_ref, own_ref, sib_ref, own_other_ref, p_own_ref, p_own_other_ref, z_ref, z_sib_ref, out_ref,
+    crossed_ref,
+):
+    core = core_ref[0]
+    crossed_ref[...] = sib_ref[:RANK, :]
+    own = unpack(own_ref)
+    z = dot(inverse_ref[...], unpack(sib_ref) - dot(p_sib_ref[...], own))
     store(z_ref, z)
-    last_parts(core, in_order(core, own_ref[:RANK, :], own_other_ref[...]), z, out_ref)
+    store(z_sib_ref, own - dot(symmetric(core, p_own_ref[...], p_own_other_ref[...]), z))
+    out_ref[...] = last_parts(core, in_order(core, own_ref[:RANK, :], own_other_ref[...]), z)
+
+
+def cross_kernel(core_ref, sib_ref, sib_other_ref, z_sib_ref, crossed_ref, out_ref):
+    core = core_ref[0]
+    crossed = in_order(core, sib_ref[...], sib_other_ref[...])
+    out_ref[...] = crossed_ref[...] + last_parts(core, crossed, unpack(z_sib_ref))
 
 
 def rhs_in_order(core, own, other):
@@ -405,14 +418,13 @@
     keep, send = products(core, generators, solved_gens, rhs, (((0, 0), (0, 1)),), 4)
     head = keep + swap(send, "sub", 0)
     token = swap(call(keep_kernel, struct(8), 0, core, send[:8], after=(head,)), "sub", 0)
-    groups = (((0, 2), (0, 3)), ((1, 1), (1, 2), (1, 3)), ((2, 2), (2, 3)))
-    parts = products(core, generators, solved_gens, rhs, groups, 1, token)
+    rest = (((0, 2), (0, 3)), ((1, 1), (1, 2), (1, 3)), ((2, 2), (2, 3)))
+    parts = products(core, generators, solved_gens, rhs, rest, 1, token)
     parts = [(keep, swap(send, "sub", 0)) for keep, send in zip(parts[::2], parts[1::2])]
     head = over_child(head)
     tail = over_child(parts[0][0] + parts[0][1])
-    near = call(add_kernel, struct(SYM + RANK + HALF), 0, core, *parts[1], after=(tail,))
-    near = over_child(near)
-    third = over_child(call(add_kernel, struct(last), 0, core, *parts[2], after=(near,)))
+    near = over_child(call(add_kernel, struct(SYM + RANK + HALF), 0, core, *parts[1], after=(tail,)))
+    third = parts[2][0] + parts[2][1]
 
     head_sib = swap(head, "rows", span_bits)
     tail_sib = swap(tail, "rows", span_bits)
@@ -426,24 +438,30 @@
     )
     p_own = call(subtract_kernel, struct(SYM), 0, core, near[:SYM], crossed[:SYM])
     r_own = call(subtract_kernel, struct(RANK + HALF), 0, core, near[SYM:], crossed[SYM:], after=(p_own,))
-    third = third - call(third_kernel, struct(last), THIRD_FLOPS, core, tail, tail_other, z0, after=(r_own,))
+    share = 1.0 / (lax.axis_size("sub") // 2 * (groups // 8))
+    third = call(
+        functools.partial(third_kernel, share), struct(last), THIRD_FLOPS,
+        core, tail, tail_other, z0, third, after=(r_own,),
+    )
+    third = third + swap(third, "rows", span_bits + 1)
+    third = over_child(third)
+    third = third + swap(third, "rows", span_bits)
 
     p_own = p_own + swap(p_own, "rows", span_bits)
     r_own = r_own + swap(r_own, "rows", span_bits)
-    third = third + swap(third, "rows", span_bits)
     p_sib = swap(p_own, "rows", span_bits + 1)
     r_sib = swap(r_own, "rows", span_bits + 1)
     p_own_other = swap(p_own, "sub", 0)
     r_own_other = swap(r_own[:RANK], "sub", 0)
     p_sib_other = swap(p_sib, "sub", 0)
     inverted, p_sib = inverse(core, p_own, p_sib, p_own_other, p_sib_other)
-    z1, crossed = call(
-        middle_kernel, [struct(RANK + HALF), struct(last)], 5 * flops,
-        core, inverted, p_sib, r_own, r_sib, r_own_other,
-    )
+    z1, z_sib, crossed, r_sib = call(
+        middle_kernel, [struct(RANK + HALF), struct(RANK + HALF), struct(last), struct(RANK)], 6 * flops,
+        core, inverted, p_sib, r_own, r_sib, r_own_other, p_own, p_own_other,
+    )
+    crossed = call(cross_kernel, struct(last), 2 * flops, core, r_sib, swap(r_sib, "sub", 0), z_sib, crossed)
 
     own = third - crossed
-    own = own + swap(own, "rows", span_bits + 1)
     sib = swap(own, "rows", span_bits + 2)
     z1_other = swap(call(keep_kernel, struct(RANK + HALF), 0, core, z1, after=(own,)), "sub", 0)
     part = jax.ShapeDtypeStruct((rhs.shape[0], RANK), jnp.bfloat16)

time: 67.7 us -> 68.3 us (level)
    ppermute x28 -> x29, starting transfers between devices: 23.7 us -> 24 us  [swap(): return lax.ppermute(value, axis, pairs)]
    ppermute x28 -> x29, waiting for transfers between devices: 24 us -> 23.9 us  [swap(): return lax.ppermute(value, axis, pairs)]
  transfers between devices with their start and end apart: 28 -> 29, of which waited for: 15 -> 15; matrix products, arithmetic and copies ran while one was open for 0% -> 0% of each run, Pallas kernels for 19% -> 20%
where the time goes in v9:
time: 68.3 us; the launch traced here: 68.2 us
  starting transfers between devices  24 us (35%)
  waiting for transfers between devices  23.9 us (35%)
  Pallas kernels  19.7 us (29%)
    ppermute x29, starting transfers between devices, swap(): return lax.ppermute(value, axis, pairs)  24 us
    ppermute x29, waiting for transfers between devices, swap(): return lax.ppermute(value, axis, pairs)  23.9 us
    pallas_call x12, Pallas kernels, call(): pl.pallas_call(kernel, in_specs=[SMEM] + [VMEM] * (len(values) - 1) + [AN...  9.09 us
    pallas_call x2, Pallas kernels, products(): pl.pallas_call(functools.partial(product_kernel, groups, chunks), in_spec...  5.89 us
    pallas_call x2, Pallas kernels, inverse(): pl.pallas_call(invert_kernel, in_specs=[SMEM] + [VMEM] * 4, out_specs=[VM...  4.73 us
  transfers between devices with their start and end apart: 29, of which 15 were waited for; matrix products, arithmetic and copies ran while one was open for 0% of the time, Pallas kernels for 20%

profile of v9, /device:TPU:0, one launch (start us, length us, event | category | flops | bytes accessed | tf_op | source)
XLA Modules:
  0.0 68.2 jit_solution(12250606866946449810)
XLA Ops:
  0.0 2.6 %shard_map.37 = (f32[448,128]{1,0:T(8,128)S(1)}, f32[448,128]{1,0:T(8,128)S(1)}) custom-call(s32[1]{0:T(128)} %bitcast.core_ref, f32[3,1024,256]{2,1,0:T(8,128)} %gens_ref.3, f32[3,1024,256]{2,1,0:T(8,128)} %solved_ref.5), custom_call_target="tpu_custom_call" | custom-call | flops 805306368 | bytes 3145728 | tf_op jit(solution)/shard_map/pallas_call | solution.py:217
  2.7 0.5 collective-permute-start
  3.2 1.1 %collective-permute-done = f32[448,128]{1,0:T(8,128)S(1)} collective-permute-done((f32[448,128]{1,0:T(8,128)S(1)}, f32[448,128]{1,0:T(8,128)S(1)}, u32[]{:S(2)}, u32[]{:S(2)}) %collective-permute-start) | collective-permute-done | bytes 229408 | tf_op jit(solution)/shard_map/ppermute | solution.py:32
  4.3 0.4 collective-permute-start.1
  4.8 2.7 %collective-permute-start.5 = (f32[448,128]{1,0:T(8,128)S(1)}, f32[448,128]{1,0:T(8,128)S(1)}, u32[]{:S(2)}, u32[]{:S(2)}) collective-permute-start(f32[448,128]{1,0:T(8,128)S(1)} %add.38.refs_0_), channel_id=1, source_target_pairs={{0,2},{1,3},{2,0},{3,1},{4,6},{5,7},{6,4},{7,5},{8,10},{9,11},{10,... | collective-permute-start | bytes 688136 | tf_op jit(solution)/shard_map/ppermute | solution.py:32
  7.4 0.0 collective-permute-done.1.refs_1_
  7.5 3.2 %shard_map.39 = (f32[384,128]{1,0:T(8,128)S(1)}, f32[384,128]{1,0:T(8,128)S(1)}, f32[576,128]{1,0:T(8,128)S(1)}, f32[576,128]{1,0:T(8,128)S(1)}, f32[320,128]{1,0:T(8,128)S(1)}, /*index=5*/f32[320,128]{1,0:T(8,128)S(1)}) custom-call(s32[1]{0:T(128)} %bitcast.core_ref, f32[3,1024,256]{2,1,0:T(8,128)S(1)} %copy-done.1, f32[3,1024,256]{2,1,0:T(8,128)S(1)} %copy-done, ...), custom_call_target="tpu_custom_call" | custom-call | flops 2214592512 | bytes 5767168 | tf_op jit(solution)/shard_map/pallas_call | solution.py:217
  10.7 0.1 collective-permute-start.2
  10.9 0.4 collective-permute-start.11
  11.3 0.9 %collective-permute-done.2 = f32[384,128]{1,0:T(8,128)S(1)} collective-permute-done((f32[384,128]{1,0:T(8,128)S(1)}, f32[384,128]{1,0:T(8,128)S(1)}, u32[]{:S(2)}, u32[]{:S(2)}) %collective-permute-start.2) | collective-permute-done | bytes 196640 | tf_op jit(solution)/shard_map/ppermute | solution.py:32
  12.3 1.1 %collective-permute-start.3 = (f32[384,128]{1,0:T(8,128)S(1)}, f32[384,128]{1,0:T(8,128)S(1)}, u32[]{:S(2)}, u32[]{:S(2)}) collective-permute-start(f32[384,128]{1,0:T(8,128)S(1)} %add.39), channel_id=1, source_target_pairs={{0,2},{1,3},{2,0},{3,1},{4,6},{5,7},{6,4},{7,5},{8,10},{9,11},{10,... | collective-permute-start | bytes 589832 | tf_op jit(solution)/shard_map/ppermute | solution.py:32
  13.3 0.2 collective-permute-done.5
  13.6 1.8 %collective-permute-start.6 = (f32[448,128]{1,0:T(8,128)S(1)}, f32[448,128]{1,0:T(8,128)S(1)}, u32[]{:S(2)}, u32[]{:S(2)}) collective-permute-start(f32[448,128]{1,0:T(8,128)S(1)} %add.41.own_ref.head_ref), channel_id=1, source_target_pairs={{0,4},{4,0},{8,12},{12,8},{16,20},{20,16},{24,28},{28,24},{1,5},{5... | collective-permute-start | bytes 688136 | tf_op jit(solution)/shard_map/ppermute | solution.py:32
  15.4 0.0 collective-permute-start.7
  15.4 0.5 collective-permute-start.10
  15.9 3.4 %collective-permute-done.3 = f32[384,128]{1,0:T(8,128)S(1)} collective-permute-done((f32[384,128]{1,0:T(8,128)S(1)}, f32[384,128]{1,0:T(8,128)S(1)}, u32[]{:S(2)}, u32[]{:S(2)}) %collective-permute-start.3) | collective-permute-done | bytes 196640 | tf_op jit(solution)/shard_map/ppermute | solution.py:32
  19.3 0.0 collective-permute-done.11.second_ref
  19.3 1.1 %collective-permute-start.12 = (f32[576,128]{1,0:T(8,128)S(1)}, f32[576,128]{1,0:T(8,128)S(1)}, u32[]{:S(2)}, u32[]{:S(2)}) collective-permute-start(f32[576,128]{1,0:T(8,128)S(1)} %shard_map.42), channel_id=1, source_target_pairs={{0,2},{1,3},{2,0},{3,1},{4,6},{5,7},{6,4},{7,5},{8,10},{9,11},{10,... | collective-permute-start | bytes 884744 | tf_op jit(solution)/shard_map/ppermute | solution.py:32
  20.4 1.5 %collective-permute-start.9 = (f32[384,128]{1,0:T(8,128)S(1)}, f32[384,128]{1,0:T(8,128)S(1)}, u32[]{:S(2)}, u32[]{:S(2)}) collective-permute-start(f32[384,128]{1,0:T(8,128)S(1)} %add.40.tail_ref.refs_0_.own_ref), channel_id=1, source_target_pairs={{0,4},{4,0},{8,12},{12,8},{16,20},{20,16},{24,28},{28,24},{1,5},{5... | collective-permute-start | bytes 589832 | tf_op jit(solution)/shard_map/ppermute | solution.py:32
  21.9 0.0 collective-permute-done.6.sib_ref.head_sib_ref
  22.0 0.1 collective-permute-start.8
  22.0 0.0 collective-permute-done.10
  22.1 0.5 collective-permute-start.4
  22.6 0.0 collective-permute-done.7.own_other_ref.head_other_ref
  22.7 0.7 collective-permute-done.8.sib_other_ref
  23.3 2.3 %shard_map.40 = (f32[256,256]{1,0:T(8,128)S(1)}, f32[256,256]{1,0:T(8,128)S(1)}) custom-call(s32[1]{0:T(128)} %bitcast.core_ref, f32[448,128]{1,0:T(8,128)S(1)} %add.41.own_ref.head_ref, f32[448,128]{1,0:T(8,128)S(1)} %collective-permute-done.6.sib_ref.head_sib_ref, f32[448,128]{1,0:T(8,128)S(1)} %collective-permute-done.7.own_other_ref.head_other_ref, ...), custom_call_target="tpu_custom_call" | custom-call | flops 900000000 | tf_op jit(solution)/shard_map/pallas_call | solution.py:298
  25.6 0.7 %collective-permute-done.9.tail_sib_ref = f32[384,128]{1,0:T(8,128)S(1)} collective-permute-done((f32[384,128]{1,0:T(8,128)S(1)}, f32[384,128]{1,0:T(8,128)S(1)}, u32[]{:S(2)}, u32[]{:S(2)}) %collective-permute-start.9) | collective-permute-done | bytes 196640 | tf_op jit(solution)/shard_map/ppermute | solution.py:32
  26.3 1.1 %shard_map.41 = (f32[640,128]{1,0:T(8,128)S(1)}, f32[576,128]{1,0:T(8,128)S(1)}) custom-call(s32[1]{0:T(128)} %bitcast.core_ref, f32[256,256]{1,0:T(8,128)S(1)} %get-tuple-element.30.inverse_ref, f32[256,256]{1,0:T(8,128)S(1)} %get-tuple-element.31.p_sib_ref, f32[448,128]{1,0:T(8,128)S(1)} %add.41.own_ref.head_ref, ...), custom_call_target="tpu_custom_call" | custom-call | flops 650000000 | bytes 2228228 | tf_op jit(solution)/shard_map/pallas_call | solution.py:286
  27.5 0.2 collective-permute-done.12
  27.7 1.6 %collective-permute-start.16 = (f32[192,128]{1,0:T(8,128)S(1)}, f32[192,128]{1,0:T(8,128)S(1)}, u32[]{:S(2)}, u32[]{:S(2)}) collective-permute-start(f32[192,128]{1,0:T(8,128)S(1)} %shard_map.43.refs_0_), channel_id=1, source_target_pairs={{0,4},{4,0},{8,12},{12,8},{16,20},{20,16},{24,28},{28,24},{1,5},{5... | collective-permute-start | bytes 294920 | tf_op jit(solution)/shard_map/ppermute | solution.py:32
  29.3 0.6 collective-permute-start.20
  29.9 0.0 collective-permute-done.4.own_other_ref
  29.9 0.4 shard_map.45
  30.3 1.6 %collective-permute-start.13 = (f32[320,128]{1,0:T(8,128)S(1)}, f32[320,128]{1,0:T(8,128)S(1)}, u32[]{:S(2)}, u32[]{:S(2)}) collective-permute-start(f32[320,128]{1,0:T(8,128)S(1)} %shard_map.45), channel_id=1, source_target_pairs={{0,8},{4,12},{8,0},{12,4},{16,24},{20,28},{24,16},{28,20},{1,9},{5... | collective-permute-start | bytes 491528 | tf_op jit(solution)/shard_map/ppermute | solution.py:32
  32.0 1.6 %collective-permute-done.16 = f32[192,128]{1,0:T(8,128)S(1)} collective-permute-done((f32[192,128]{1,0:T(8,128)S(1)}, f32[192,128]{1,0:T(8,128)S(1)}, u32[]{:S(2)}, u32[]{:S(2)}) %collective-permute-start.16) | collective-permute-done | bytes 98336 | tf_op jit(solution)/shard_map/ppermute | solution.py:32
  33.5 1.6 %collective-permute-start.17 = (f32[192,128]{1,0:T(8,128)S(1)}, f32[192,128]{1,0:T(8,128)S(1)}, u32[]{:S(2)}, u32[]{:S(2)}) collective-permute-start(f32[192,128]{1,0:T(8,128)S(1)} %add.47.own_ref.p_own_ref), channel_id=1, source_target_pairs={{0,8},{4,12},{8,0},{12,4},{16,24},{20,28},{24,16},{28,20},{1,9},{5... | collective-permute-start | bytes 294920 | tf_op jit(solution)/shard_map/ppermute | solution.py:32
  35.2 0.9 %collective-permute-done.20 = f32[384,128]{1,0:T(8,128)S(1)} collective-permute-done((f32[384,128]{1,0:T(8,128)S(1)}, f32[384,128]{1,0:T(8,128)S(1)}, u32[]{:S(2)}, u32[]{:S(2)}) %collective-permute-start.20) | collective-permute-done | bytes 196640 | tf_op jit(solution)/shard_map/ppermute | solution.py:32
  36.1 1.6 %collective-permute-start.21 = (f32[384,128]{1,0:T(8,128)S(1)}, f32[384,128]{1,0:T(8,128)S(1)}, u32[]{:S(2)}, u32[]{:S(2)}) collective-permute-start(f32[384,128]{1,0:T(8,128)S(1)} %add.48.own_ref), channel_id=1, source_target_pairs={{0,8},{4,12},{8,0},{12,4},{16,24},{20,28},{24,16},{28,20},{1,9},{5... | collective-permute-start | bytes 589832 | tf_op jit(solution)/shard_map/ppermute | solution.py:32
  37.7 0.0 collective-permute-start.18
  37.7 1.6 %collective-permute-done.17.sib_ref = f32[192,128]{1,0:T(8,128)S(1)} collective-permute-done((f32[192,128]{1,0:T(8,128)S(1)}, f32[192,128]{1,0:T(8,128)S(1)}, u32[]{:S(2)}, u32[]{:S(2)}) %collective-permute-start.17) | collective-permute-done | bytes 98336 | tf_op jit(solution)/shard_map/ppermute | solution.py:32
  39.3 0.0 collective-permute-start.19
  39.3 1.1 %collective-permute-start.14 = (f32[320,128]{1,0:T(8,128)S(1)}, f32[320,128]{1,0:T(8,128)S(1)}, u32[]{:S(2)}, u32[]{:S(2)}) collective-permute-start(f32[320,128]{1,0:T(8,128)S(1)} %add.44), channel_id=1, source_target_pairs={{0,2},{1,3},{2,0},{3,1},{4,6},{5,7},{6,4},{7,5},{8,10},{9,11},{10,... | collective-permute-start | bytes 491528 | tf_op jit(solution)/shard_map/ppermute | solution.py:32
  40.4 0.3 collective-permute-start.22
  40.7 2.5 %shard_map.46 = (f32[256,256]{1,0:T(8,128)S(1)}, f32[256,256]{1,0:T(8,128)S(1)}) custom-call(s32[1]{0:T(128)} %bitcast.core_ref, f32[192,128]{1,0:T(8,128)S(1)} %add.47.own_ref.p_own_ref, f32[192,128]{1,0:T(8,128)S(1)} %collective-permute-done.17.sib_ref, f32[192,128]{1,0:T(8,128)S(1)} %collective-permute-done.18.own_other_ref.p_own_other_ref, ...), custom_call_target="tpu_custom_call" | custom-call | flops 900000000 | tf_op jit(solution)/shard_map/pallas_call | solution.py:298
  43.2 2.8 %collective-permute-done.14 = f32[320,128]{1,0:T(8,128)S(1)} collective-permute-done((f32[320,128]{1,0:T(8,128)S(1)}, f32[320,128]{1,0:T(8,128)S(1)}, u32[]{:S(2)}, u32[]{:S(2)}) %collective-permute-start.14) | collective-permute-done | bytes 163872 | tf_op jit(solution)/shard_map/ppermute | solution.py:32
  46.0 1.2 %collective-permute-start.15 = (f32[320,128]{1,0:T(8,128)S(1)}, f32[320,128]{1,0:T(8,128)S(1)}, u32[]{:S(2)}, u32[]{:S(2)}) collective-permute-start(f32[320,128]{1,0:T(8,128)S(1)} %add.45), channel_id=1, source_target_pairs={{0,4},{4,0},{8,12},{12,8},{16,20},{20,16},{24,28},{28,24},{1,5},{5... | collective-permute-start | bytes 491528 | tf_op jit(solution)/shard_map/ppermute | solution.py:32
  47.2 0.0 collective-permute-done.22.own_other_ref
  47.2 0.0 collective-permute-done.21.sib_ref
  47.2 1.2 %shard_map.47 = (f32[384,128]{1,0:T(8,128)S(1)}, f32[384,128]{1,0:T(8,128)S(1)}, f32[320,128]{1,0:T(8,128)S(1)}, f32[256,128]{1,0:T(8,128)S(1)}) custom-call(s32[1]{0:T(128)} %bitcast.core_ref, f32[256,256]{1,0:T(8,128)S(1)} %get-tuple-element.38.inverse_ref, f32[256,256]{1,0:T(8,128)S(1)} %get-tuple-element.39.p_sib_ref, f32[384,128]{1,0:T(8,128)S(1)} %add.48.own_ref, ...), custom_call_target="tpu_custom_call" | custom-call | flops 301989888 | bytes 1933316 | tf_op jit(solution)/shard_map/pallas_call | solution.py:286
  48.4 0.1 collective-permute-start.23
  48.5 0.5 collective-permute-start.27
  48.9 0.8 %collective-permute-done.23.sib_other_ref = f32[256,128]{1,0:T(8,128)S(1)} collective-permute-done((f32[256,128]{1,0:T(8,128)S(1)}, f32[256,128]{1,0:T(8,128)S(1)}, u32[]{:S(2)}, u32[]{:S(2)}) %collective-permute-start.23) | collective-permute-done | bytes 131104 | tf_op jit(solution)/shard_map/ppermute | solution.py:32
  49.8 0.4 shard_map.48
  50.2 1.7 %collective-permute-done.15 = f32[320,128]{1,0:T(8,128)S(1)} collective-permute-done((f32[320,128]{1,0:T(8,128)S(1)}, f32[320,128]{1,0:T(8,128)S(1)}, u32[]{:S(2)}, u32[]{:S(2)}) %collective-permute-start.15) | collective-permute-done | bytes 163872 | tf_op jit(solution)/shard_map/ppermute | solution.py:32
  52.0 0.1 collective-permute-start.26
  52.0 2.7 %collective-permute-start.25 = (f32[320,128]{1,0:T(8,128)S(1)}, f32[320,128]{1,0:T(8,128)S(1)}, u32[]{:S(2)}, u32[]{:S(2)}) collective-permute-start(f32[320,128]{1,0:T(8,128)S(1)} %add_subtract_fusion.refs_0_.own_ref), channel_id=1, source_target_pairs={{0,16},{4,20},{8,24},{12,28},{16,0},{20,4},{24,8},{28,12},{1,17},{... | collective-permute-start | bytes 491528 | tf_op jit(solution)/shard_map/ppermute | solution.py:32
  54.7 0.2 collective-permute-start.24
  54.9 0.0 collective-permute-done.27.z0_other_ref
  54.9 2.2 %shard_map.50 = (bf16[1024,256]{1,0:T(8,128)(2,1)S(1)}, bf16[1024,256]{1,0:T(8,128)(2,1)S(1)}, f32[1024,128]{1,0:T(8,128)S(1)}) custom-call(s32[1]{0:T(128)} %bitcast.core_ref, f32[384,128]{1,0:T(8,128)S(1)} %get-tuple-element.43.value_ref.z1_ref, f32[384,128]{1,0:T(8,128)S(1)} %collective-permute-done.26.z1_other_ref, ...), custom_call_target="tpu_custom_call" | custom-call | flops 1207959552 | bytes 7340036 | tf_op jit(solution)/shard_map/pallas_call | solution.py:286
  57.1 6.0 %collective-permute-done.25.value_ref = f32[320,128]{1,0:T(8,128)S(1)} collective-permute-done((f32[320,128]{1,0:T(8,128)S(1)}, f32[320,128]{1,0:T(8,128)S(1)}, u32[]{:S(2)}, u32[]{:S(2)}) %collective-permute-start.25) | collective-permute-done | bytes 163872 | tf_op jit(solution)/shard_map/ppermute | solution.py:32
  63.1 0.1 collective-permute-start.28
  63.2 0.0 collective-permute-done.24.own_other_ref
  63.2 1.4 %collective-permute-done.28.sib_other_ref = f32[320,128]{1,0:T(8,128)S(1)} collective-permute-done((f32[320,128]{1,0:T(8,128)S(1)}, f32[320,128]{1,0:T(8,128)S(1)}, u32[]{:S(2)}, u32[]{:S(2)}) %collective-permute-start.28) | collective-permute-done | bytes 163872 | tf_op jit(solution)/shard_map/ppermute | solution.py:32
  64.5 3.7 %shard_map.52 = f32[1024,128]{1,0:T(8,128)} custom-call(s32[1]{0:T(128)} %bitcast.core_ref, f32[320,128]{1,0:T(8,128)S(1)} %add_subtract_fusion.refs_0_.own_ref, f32[320,128]{1,0:T(8,128)S(1)} %collective-permute-done.24.own_other_ref, f32[320,128]{1,0:T(8,128)S(1)} %shard_map.51.sib_ref, f32[320,128]{1,0:T(8,128)S(1)} %collective-permute-done.28.sib_other_ref, ...), custom_call_target="tpu_custom_call" | custom-call | flops 1107296256 | bytes 3801092 | tf_op jit(solution)/shard_map/pallas_call | solution.py:286
  (35 shorter events, 0.5 us)
Async XLA Ops:
  0.0 7.5 %copy-start = (f32[3,1024,256]{2,1,0:T(8,128)S(1)}, f32[3,1024,256]{2,1,0:T(8,128)}, u32[]{:S(2)}) copy-start(f32[3,1024,256]{2,1,0:T(8,128)} %solved_ref.5) | copy-start | bytes 9437188
  0.0 7.5 %copy-start.1 = (f32[3,1024,256]{2,1,0:T(8,128)S(1)}, f32[3,1024,256]{2,1,0:T(8,128)}, u32[]{:S(2)}) copy-start(f32[3,1024,256]{2,1,0:T(8,128)} %gens_ref.3) | copy-start | bytes 9437188
  0.0 7.5 %copy-start.2 = (f32[1024,128]{1,0:T(8,128)S(1)}, f32[1024,128]{1,0:T(8,128)}, u32[]{:S(2)}) copy-start(f32[1024,128]{1,0:T(8,128)} %rhs_ref.1) | copy-start | bytes 1572868
  2.7 1.6 %collective-permute-start = (f32[448,128]{1,0:T(8,128)S(1)}, f32[448,128]{1,0:T(8,128)S(1)}, u32[]{:S(2)}, u32[]{:S(2)}) collective-permute-start(f32[448,128]{1,0:T(8,128)S(1)} %get-tuple-element.26), channel_id=1, source_target_pairs={{0,1},{1,0},{2,3},{3,2},{4,5},{5,4},{6,7},{7,6},{8,9},{9,8},{10,11... | collective-permute-start | bytes 688136 | tf_op jit(solution)/shard_map/ppermute | solution.py:32
  4.3 3.1 %collective-permute-start.1 = (f32[8,128]{1,0:T(8,128)S(1)}, f32[8,128]{1,0:T(8,128)S(1)}, u32[]{:S(2)}, u32[]{:S(2)}) collective-permute-start(f32[8,128]{1,0:T(8,128)S(1)} %shard_map.38), channel_id=1, source_target_pairs={{0,1},{1,0},{2,3},{3,2},{4,5},{5,4},{6,7},{7,6},{8,9},{9,8},{10,11... | collective-permute-start | bytes 12296 | tf_op jit(solution)/shard_map/ppermute | solution.py:32
  4.8 8.8 %collective-permute-start.5 = (f32[448,128]{1,0:T(8,128)S(1)}, f32[448,128]{1,0:T(8,128)S(1)}, u32[]{:S(2)}, u32[]{:S(2)}) collective-permute-start(f32[448,128]{1,0:T(8,128)S(1)} %add.38.refs_0_), channel_id=1, source_target_pairs={{0,2},{1,3},{2,0},{3,1},{4,6},{5,7},{6,4},{7,5},{8,10},{9,11},{10,... | collective-permute-start | bytes 688136 | tf_op jit(solution)/shard_map/ppermute | solution.py:32
  10.7 1.5 %collective-permute-start.2 = (f32[384,128]{1,0:T(8,128)S(1)}, f32[384,128]{1,0:T(8,128)S(1)}, u32[]{:S(2)}, u32[]{:S(2)}) collective-permute-start(f32[384,128]{1,0:T(8,128)S(1)} %get-tuple-element.29), channel_id=1, source_target_pairs={{0,1},{1,0},{2,3},{3,2},{4,5},{5,4},{6,7},{7,6},{8,9},{9,8},{10,11... | collective-permute-start | bytes 589832 | tf_op jit(solution)/shard_map/ppermute | solution.py:32
  10.9 8.4 %collective-permute-start.11 = (f32[576,128]{1,0:T(8,128)S(1)}, f32[576,128]{1,0:T(8,128)S(1)}, u32[]{:S(2)}, u32[]{:S(2)}) collective-permute-start(f32[576,128]{1,0:T(8,128)S(1)} %get-tuple-element.36), channel_id=1, source_target_pairs={{0,1},{1,0},{2,3},{3,2},{4,5},{5,4},{6,7},{7,6},{8,9},{9,8},{10,11... | collective-permute-start | bytes 884744 | tf_op jit(solution)/shard_map/ppermute | solution.py:32
  12.3 7.0 %collective-permute-start.3 = (f32[384,128]{1,0:T(8,128)S(1)}, f32[384,128]{1,0:T(8,128)S(1)}, u32[]{:S(2)}, u32[]{:S(2)}) collective-permute-start(f32[384,128]{1,0:T(8,128)S(1)} %add.39), channel_id=1, source_target_pairs={{0,2},{1,3},{2,0},{3,1},{4,6},{5,7},{6,4},{7,5},{8,10},{9,11},{10,... | collective-permute-start | bytes 589832 | tf_op jit(solution)/shard_map/ppermute | solution.py:32
  13.6 8.3 %collective-permute-start.6 = (f32[448,128]{1,0:T(8,128)S(1)}, f32[448,128]{1,0:T(8,128)S(1)}, u32[]{:S(2)}, u32[]{:S(2)}) collective-permute-start(f32[448,128]{1,0:T(8,128)S(1)} %add.41.own_ref.head_ref), channel_id=1, source_target_pairs={{0,4},{4,0},{8,12},{12,8},{16,20},{20,16},{24,28},{28,24},{1,5},{5... | collective-permute-start | bytes 688136 | tf_op jit(solution)/shard_map/ppermute | solution.py:32
  15.4 7.3 %collective-permute-start.7 = (f32[448,128]{1,0:T(8,128)S(1)}, f32[448,128]{1,0:T(8,128)S(1)}, u32[]{:S(2)}, u32[]{:S(2)}) collective-permute-start(f32[448,128]{1,0:T(8,128)S(1)} %add.41.own_ref.head_ref), channel_id=1, source_target_pairs={{0,1},{1,0},{2,3},{3,2},{4,5},{5,4},{6,7},{7,6},{8,9},{9,8},{10,11... | collective-permute-start | bytes 688136 | tf_op jit(solution)/shard_map/ppermute | solution.py:32
  15.4 6.6 %collective-permute-start.10 = (f32[320,128]{1,0:T(8,128)S(1)}, f32[320,128]{1,0:T(8,128)S(1)}, u32[]{:S(2)}, u32[]{:S(2)}) collective-permute-start(f32[320,128]{1,0:T(8,128)S(1)} %get-tuple-element.34), channel_id=1, source_target_pairs={{0,1},{1,0},{2,3},{3,2},{4,5},{5,4},{6,7},{7,6},{8,9},{9,8},{10,11... | collective-permute-start | bytes 491528 | tf_op jit(solution)/shard_map/ppermute | solution.py:32
  19.3 8.3 %collective-permute-start.12 = (f32[576,128]{1,0:T(8,128)S(1)}, f32[576,128]{1,0:T(8,128)S(1)}, u32[]{:S(2)}, u32[]{:S(2)}) collective-permute-start(f32[576,128]{1,0:T(8,128)S(1)} %shard_map.42), channel_id=1, source_target_pairs={{0,2},{1,3},{2,0},{3,1},{4,6},{5,7},{6,4},{7,5},{8,10},{9,11},{10,... | collective-permute-start | bytes 884744 | tf_op jit(solution)/shard_map/ppermute | solution.py:32
  20.4 5.9 %collective-permute-start.9 = (f32[384,128]{1,0:T(8,128)S(1)}, f32[384,128]{1,0:T(8,128)S(1)}, u32[]{:S(2)}, u32[]{:S(2)}) collective-permute-start(f32[384,128]{1,0:T(8,128)S(1)} %add.40.tail_ref.refs_0_.own_ref), channel_id=1, source_target_pairs={{0,4},{4,0},{8,12},{12,8},{16,20},{20,16},{24,28},{28,24},{1,5},{5... | collective-permute-start | bytes 589832 | tf_op jit(solution)/shard_map/ppermute | solution.py:32
  22.0 1.4 %collective-permute-start.8 = (f32[192,128]{1,0:T(8,128)S(1)}, f32[192,128]{1,0:T(8,128)S(1)}, u32[]{:S(2)}, u32[]{:S(2)}) collective-permute-start(f32[192,128]{1,0:T(8,128)S(1)} %slice.33), channel_id=1, source_target_pairs={{0,1},{1,0},{2,3},{3,2},{4,5},{5,4},{6,7},{7,6},{8,9},{9,8},{10,11... | collective-permute-start | bytes 294920 | tf_op jit(solution)/shard_map/ppermute | solution.py:32
  22.1 7.8 %collective-permute-start.4 = (f32[256,128]{1,0:T(8,128)S(1)}, f32[256,128]{1,0:T(8,128)S(1)}, u32[]{:S(2)}, u32[]{:S(2)}) collective-permute-start(f32[256,128]{1,0:T(8,128)S(1)} %slice.32), channel_id=1, source_target_pairs={{0,1},{1,0},{2,3},{3,2},{4,5},{5,4},{6,7},{7,6},{8,9},{9,8},{10,11... | collective-permute-start | bytes 393224 | tf_op jit(solution)/shard_map/ppermute | solution.py:32
  27.7 5.8 %collective-permute-start.16 = (f32[192,128]{1,0:T(8,128)S(1)}, f32[192,128]{1,0:T(8,128)S(1)}, u32[]{:S(2)}, u32[]{:S(2)}) collective-permute-start(f32[192,128]{1,0:T(8,128)S(1)} %shard_map.43.refs_0_), channel_id=1, source_target_pairs={{0,4},{4,0},{8,12},{12,8},{16,20},{20,16},{24,28},{28,24},{1,5},{5... | collective-permute-start | bytes 294920 | tf_op jit(solution)/shard_map/ppermute | solution.py:32
  29.3 6.7 %collective-permute-start.20 = (f32[384,128]{1,0:T(8,128)S(1)}, f32[384,128]{1,0:T(8,128)S(1)}, u32[]{:S(2)}, u32[]{:S(2)}) collective-permute-start(f32[384,128]{1,0:T(8,128)S(1)} %shard_map.44.refs_0_), channel_id=1, source_target_pairs={{0,4},{4,0},{8,12},{12,8},{16,20},{20,16},{24,28},{28,24},{1,5},{5... | collective-permute-start | bytes 589832 | tf_op jit(solution)/shard_map/ppermute | solution.py:32
  30.3 8.9 %collective-permute-start.13 = (f32[320,128]{1,0:T(8,128)S(1)}, f32[320,128]{1,0:T(8,128)S(1)}, u32[]{:S(2)}, u32[]{:S(2)}) collective-permute-start(f32[320,128]{1,0:T(8,128)S(1)} %shard_map.45), channel_id=1, source_target_pairs={{0,8},{4,12},{8,0},{12,4},{16,24},{20,28},{24,16},{28,20},{1,9},{5... | collective-permute-start | bytes 491528 | tf_op jit(solution)/shard_map/ppermute | solution.py:32
  33.5 5.7 %collective-permute-start.17 = (f32[192,128]{1,0:T(8,128)S(1)}, f32[192,128]{1,0:T(8,128)S(1)}, u32[]{:S(2)}, u32[]{:S(2)}) collective-permute-start(f32[192,128]{1,0:T(8,128)S(1)} %add.47.own_ref.p_own_ref), channel_id=1, source_target_pairs={{0,8},{4,12},{8,0},{12,4},{16,24},{20,28},{24,16},{28,20},{1,9},{5... | collective-permute-start | bytes 294920 | tf_op jit(solution)/shard_map/ppermute | solution.py:32
  36.1 11.1 %collective-permute-start.21 = (f32[384,128]{1,0:T(8,128)S(1)}, f32[384,128]{1,0:T(8,128)S(1)}, u32[]{:S(2)}, u32[]{:S(2)}) collective-permute-start(f32[384,128]{1,0:T(8,128)S(1)} %add.48.own_ref), channel_id=1, source_target_pairs={{0,8},{4,12},{8,0},{12,4},{16,24},{20,28},{24,16},{28,20},{1,9},{5... | collective-permute-start | bytes 589832 | tf_op jit(solution)/shard_map/ppermute | solution.py:32
  37.7 3.0 %collective-permute-start.18 = (f32[192,128]{1,0:T(8,128)S(1)}, f32[192,128]{1,0:T(8,128)S(1)}, u32[]{:S(2)}, u32[]{:S(2)}) collective-permute-start(f32[192,128]{1,0:T(8,128)S(1)} %add.47.own_ref.p_own_ref), channel_id=1, source_target_pairs={{0,1},{1,0},{2,3},{3,2},{4,5},{5,4},{6,7},{7,6},{8,9},{9,8},{10,11... | collective-permute-start | bytes 294920 | tf_op jit(solution)/shard_map/ppermute | solution.py:32
  39.3 1.5 %collective-permute-start.19 = (f32[192,128]{1,0:T(8,128)S(1)}, f32[192,128]{1,0:T(8,128)S(1)}, u32[]{:S(2)}, u32[]{:S(2)}) collective-permute-start(f32[192,128]{1,0:T(8,128)S(1)} %collective-permute-done.17.sib_ref), channel_id=1, source_target_pairs={{0,1},{1,0},{2,3},{3,2},{4,5},{5,4},{6,7},{7,6},{8,9},{9,8},{10,11... | collective-permute-start | bytes 294920 | tf_op jit(solution)/shard_map/ppermute | solution.py:32
  39.3 6.7 %collective-permute-start.14 = (f32[320,128]{1,0:T(8,128)S(1)}, f32[320,128]{1,0:T(8,128)S(1)}, u32[]{:S(2)}, u32[]{:S(2)}) collective-permute-start(f32[320,128]{1,0:T(8,128)S(1)} %add.44), channel_id=1, source_target_pairs={{0,2},{1,3},{2,0},{3,1},{4,6},{5,7},{6,4},{7,5},{8,10},{9,11},{10,... | collective-permute-start | bytes 491528 | tf_op jit(solution)/shard_map/ppermute | solution.py:32
  40.4 6.7 %collective-permute-start.22 = (f32[256,128]{1,0:T(8,128)S(1)}, f32[256,128]{1,0:T(8,128)S(1)}, u32[]{:S(2)}, u32[]{:S(2)}) collective-permute-start(f32[256,128]{1,0:T(8,128)S(1)} %slice.36), channel_id=1, source_target_pairs={{0,1},{1,0},{2,3},{3,2},{4,5},{5,4},{6,7},{7,6},{8,9},{9,8},{10,11... | collective-permute-start | bytes 393224 | tf_op jit(solution)/shard_map/ppermute | solution.py:32
  46.0 5.9 %collective-permute-start.15 = (f32[320,128]{1,0:T(8,128)S(1)}, f32[320,128]{1,0:T(8,128)S(1)}, u32[]{:S(2)}, u32[]{:S(2)}) collective-permute-start(f32[320,128]{1,0:T(8,128)S(1)} %add.45), channel_id=1, source_target_pairs={{0,4},{4,0},{8,12},{12,8},{16,20},{20,16},{24,28},{28,24},{1,5},{5... | collective-permute-start | bytes 491528 | tf_op jit(solution)/shard_map/ppermute | solution.py:32
  48.4 1.4 %collective-permute-start.23 = (f32[256,128]{1,0:T(8,128)S(1)}, f32[256,128]{1,0:T(8,128)S(1)}, u32[]{:S(2)}, u32[]{:S(2)}) collective-permute-start(f32[256,128]{1,0:T(8,128)S(1)} %get-tuple-element.40.sib_ref), channel_id=1, source_target_pairs={{0,1},{1,0},{2,3},{3,2},{4,5},{5,4},{6,7},{7,6},{8,9},{9,8},{10,11... | collective-permute-start | bytes 393224 | tf_op jit(solution)/shard_map/ppermute | solution.py:32
  48.5 6.4 %collective-permute-start.27 = (f32[640,128]{1,0:T(8,128)S(1)}, f32[640,128]{1,0:T(8,128)S(1)}, u32[]{:S(2)}, u32[]{:S(2)}) collective-permute-start(f32[640,128]{1,0:T(8,128)S(1)} %get-tuple-element.32.z_ref.z0_ref), channel_id=1, source_target_pairs={{0,1},{1,0},{2,3},{3,2},{4,5},{5,4},{6,7},{7,6},{8,9},{9,8},{10,11... | collective-permute-start | bytes 983048 | tf_op jit(solution)/shard_map/ppermute | solution.py:32
  52.0 2.9 %collective-permute-start.26 = (f32[384,128]{1,0:T(8,128)S(1)}, f32[384,128]{1,0:T(8,128)S(1)}, u32[]{:S(2)}, u32[]{:S(2)}) collective-permute-start(f32[384,128]{1,0:T(8,128)S(1)} %shard_map.49), channel_id=1, source_target_pairs={{0,1},{1,0},{2,3},{3,2},{4,5},{5,4},{6,7},{7,6},{8,9},{9,8},{10,11... | collective-permute-start | bytes 589832 | tf_op jit(solution)/shard_map/ppermute | solution.py:32
  52.0 11.0 %collective-permute-start.25 = (f32[320,128]{1,0:T(8,128)S(1)}, f32[320,128]{1,0:T(8,128)S(1)}, u32[]{:S(2)}, u32[]{:S(2)}) collective-permute-start(f32[320,128]{1,0:T(8,128)S(1)} %add_subtract_fusion.refs_0_.own_ref), channel_id=1, source_target_pairs={{0,16},{4,20},{8,24},{12,28},{16,0},{20,4},{24,8},{28,12},{1,17},{... | collective-permute-start | bytes 491528 | tf_op jit(solution)/shard_map/ppermute | solution.py:32
  54.7 8.5 %collective-permute-start.24 = (f32[320,128]{1,0:T(8,128)S(1)}, f32[320,128]{1,0:T(8,128)S(1)}, u32[]{:S(2)}, u32[]{:S(2)}) collective-permute-start(f32[320,128]{1,0:T(8,128)S(1)} %add_subtract_fusion.refs_0_.own_ref), channel_id=1, source_target_pairs={{0,1},{1,0},{2,3},{3,2},{4,5},{5,4},{6,7},{7,6},{8,9},{9,8},{10,11... | collective-permute-start | bytes 491528 | tf_op jit(solution)/shard_map/ppermute | solution.py:32
  63.1 1.5 %collective-permute-start.28 = (f32[320,128]{1,0:T(8,128)S(1)}, f32[320,128]{1,0:T(8,128)S(1)}, u32[]{:S(2)}, u32[]{:S(2)}) collective-permute-start(f32[320,128]{1,0:T(8,128)S(1)} %shard_map.51.sib_ref), channel_id=1, source_target_pairs={{0,1},{1,0},{2,3},{3,2},{4,5},{5,4},{6,7},{7,6},{8,9},{9,8},{10,11... | collective-permute-start | bytes 491528 | tf_op jit(solution)/shard_map/ppermute | solution.py:32

commit v10 on v9

--- a/solution.py
+++ b/solution.py
@@ -16,7 +16,10 @@
 DIVERGED = 1e4
 FIRST_FLOPS = 6.5e8
 INVERT_FLOPS = 9e8
-THIRD_FLOPS = 3e9
+INVERT_SECOND = 9e8
+MIDDLE_FLOPS = 0
+CROSS_FLOPS = 0
+THIRD_FLOPS = 1e9
 VMEM_LIMIT = 40 * 2**20
 STREAM_LIMIT = 52 * 2**20
 
@@ -294,7 +297,7 @@
     )(*values, *after)
 
 
-def inverse(core, own, sib, own_other, sib_other):
+def inverse(flops, core, own, sib, own_other, sib_other):
     return pl.pallas_call(
         invert_kernel,
         in_specs=[SMEM] + [VMEM] * 4,
@@ -302,7 +305,7 @@
         out_shape=[struct(RANK, RANK)] * 2,
         scratch_shapes=[pltpu.VMEM((RANK, RANK), jnp.float32)],
         compiler_params=pltpu.CompilerParams(vmem_limit_bytes=VMEM_LIMIT),
-        cost_estimate=cost(INVERT_FLOPS, 0),
+        cost_estimate=cost(flops, 0),
     )(core, own, sib, own_other, sib_other)
 
 
@@ -322,10 +325,10 @@
     return jnp.concatenate([symmetric_half(core, value[:, :HALF]), *pack(value[:, HALF:])], axis=0)
 
 
-def third_kernel(share, core_ref, own_ref, own_other_ref, z_ref, third_ref, *refs):
+def third_kernel(core_ref, own_ref, own_other_ref, z_ref, *refs):
     core = core_ref[0]
     crossed = in_order(core, own_ref[:RANK, :], own_other_ref[...])
-    refs[-1][...] = third_ref[...] - share * last_parts(core, crossed, unpack(z_ref.at[RANK:]))
+    refs[-1][...] = last_parts(core, crossed, unpack(z_ref.at[RANK:]))
 
 
 def middle_kernel(
@@ -425,26 +428,24 @@
     tail = over_child(parts[0][0] + parts[0][1])
     near = over_child(call(add_kernel, struct(SYM + RANK + HALF), 0, core, *parts[1], after=(tail,)))
     third = parts[2][0] + parts[2][1]
+    third = over_child(
+        call(add_kernel, struct(last), 0, core, third, swap(third, "rows", span_bits + 1), after=(near,))
+    )
 
     head_sib = swap(head, "rows", span_bits)
     tail_sib = swap(tail, "rows", span_bits)
     head_other = swap(head, "sub", 0)
     tail_other = swap(tail[:RANK], "sub", 0)
     p_sib_other = swap(head_sib[:SYM], "sub", 0)
-    inverted, p_sib = inverse(core, head, head_sib, head_other, p_sib_other)
+    inverted, p_sib = inverse(INVERT_FLOPS, core, head, head_sib, head_other, p_sib_other)
     z0, crossed = call(
         first_kernel, [struct(2 * RANK + HALF), struct(SYM + RANK + HALF)], FIRST_FLOPS,
         core, inverted, p_sib, head, head_sib, head_other, tail, tail_sib,
     )
     p_own = call(subtract_kernel, struct(SYM), 0, core, near[:SYM], crossed[:SYM])
     r_own = call(subtract_kernel, struct(RANK + HALF), 0, core, near[SYM:], crossed[SYM:], after=(p_own,))
-    share = 1.0 / (lax.axis_size("sub") // 2 * (groups // 8))
-    third = call(
-        functools.partial(third_kernel, share), struct(last), THIRD_FLOPS,
-        core, tail, tail_other, z0, third, after=(r_own,),
-    )
-    third = third + swap(third, "rows", span_bits + 1)
-    third = over_child(third)
+    crossed = call(third_kernel, struct(last), THIRD_FLOPS, core, tail, tail_other, z0, after=(r_own,))
+    third = third - (crossed + swap(crossed, "rows", span_bits + 1))
     third = third + swap(third, "rows", span_bits)
 
     p_own = p_own + swap(p_own, "rows", span_bits)
@@ -454,12 +455,12 @@
     p_own_other = swap(p_own, "sub", 0)
     r_own_other = swap(r_own[:RANK], "sub", 0)
     p_sib_other = swap(p_sib, "sub", 0)
-    inverted, p_sib = inverse(core, p_own, p_sib, p_own_other, p_sib_other)
+    inverted, p_sib = inverse(INVERT_SECOND, core, p_own, p_sib, p_own_other, p_sib_other)
     z1, z_sib, crossed, r_sib = call(
-        middle_kernel, [struct(RANK + HALF), struct(RANK + HALF), struct(last), struct(RANK)], 6 * flops,
+        middle_kernel, [struct(RANK + HALF), struct(RANK + HALF), struct(last), struct(RANK)], MIDDLE_FLOPS,
         core, inverted, p_sib, r_own, r_sib, r_own_other, p_own, p_own_other,
     )
-    crossed = call(cross_kernel, struct(last), 2 * flops, core, r_sib, swap(r_sib, "sub", 0), z_sib, crossed)
+    crossed = call(cross_kernel, struct(last), CROSS_FLOPS, core, r_sib, swap(r_sib, "sub", 0), z_sib, crossed)
 
     own = third - crossed
     sib = swap(own, "rows", span_bits + 2)

time: 68.3 us -> 64.1 us (0.939)
  waiting for transfers between devices: 23.9 us -> 18.7 us
  starting transfers between devices: 24 us -> 25 us
    ppermute x29 -> x30, waiting for transfers between devices: 23.9 us -> 18.7 us  [swap(): return lax.ppermute(value, axis, pairs)]
    ppermute x29 -> x30, starting transfers between devices: 24 us -> 25 us  [swap(): return lax.ppermute(value, axis, pairs)]
    pallas_call x12 -> x13, Pallas kernels: 9.09 us -> 9.1 us  [call(): pl.pallas_call(kernel, in_specs=[SMEM] + [VMEM] * (len(values) - 1) + [AN...]
  transfers between devices with their start and end apart: 29 -> 30, of which waited for: 15 -> 14; matrix products, arithmetic and copies ran while one was open for 0% -> 0% of each run, Pallas kernels for 20% -> 21%
where the time goes in v10:
time: 64.1 us; the launch traced here: 64 us
  starting transfers between devices  25 us (39%)
  Pallas kernels  19.7 us (31%)
  waiting for transfers between devices  18.7 us (29%)
    ppermute x30, starting transfers between devices, swap(): return lax.ppermute(value, axis, pairs)  25 us
    ppermute x30, waiting for transfers between devices, swap(): return lax.ppermute(value, axis, pairs)  18.7 us
    pallas_call x13, Pallas kernels, call(): pl.pallas_call(kernel, in_specs=[SMEM] + [VMEM] * (len(values) - 1) + [AN...  9.1 us
    pallas_call x2, Pallas kernels, products(): pl.pallas_call(functools.partial(product_kernel, groups, chunks), in_spec...  5.89 us
    pallas_call x2, Pallas kernels, inverse(): pl.pallas_call(invert_kernel, in_specs=[SMEM] + [VMEM] * 4, out_specs=[VM...  4.73 us
  transfers between devices with their start and end apart: 30, of which 14 were waited for; matrix products, arithmetic and copies ran while one was open for 0% of the time, Pallas kernels for 21%

profile of v10, /device:TPU:0, one launch (start us, length us, event | category | flops | bytes accessed | tf_op | source)
XLA Modules:
  0.0 64.0 jit_solution(17571130610658310142)
XLA Ops:
  0.0 2.6 %shard_map.37 = (f32[448,128]{1,0:T(8,128)S(1)}, f32[448,128]{1,0:T(8,128)S(1)}) custom-call(s32[1]{0:T(128)} %bitcast.core_ref, f32[3,1024,256]{2,1,0:T(8,128)} %gens_ref.3, f32[3,1024,256]{2,1,0:T(8,128)} %solved_ref.5), custom_call_target="tpu_custom_call" | custom-call | flops 805306368 | bytes 3145728 | tf_op jit(solution)/shard_map/pallas_call | solution.py:220
  2.7 0.5 collective-permute-start
  3.2 1.1 %collective-permute-done = f32[448,128]{1,0:T(8,128)S(1)} collective-permute-done((f32[448,128]{1,0:T(8,128)S(1)}, f32[448,128]{1,0:T(8,128)S(1)}, u32[]{:S(2)}, u32[]{:S(2)}) %collective-permute-start) | collective-permute-done | bytes 229408 | tf_op jit(solution)/shard_map/ppermute | solution.py:35
  4.3 0.4 collective-permute-start.1
  4.8 2.7 %collective-permute-start.10 = (f32[448,128]{1,0:T(8,128)S(1)}, f32[448,128]{1,0:T(8,128)S(1)}, u32[]{:S(2)}, u32[]{:S(2)}) collective-permute-start(f32[448,128]{1,0:T(8,128)S(1)} %add.38.refs_0_), channel_id=1, source_target_pairs={{0,2},{1,3},{2,0},{3,1},{4,6},{5,7},{6,4},{7,5},{8,10},{9,11},{10,... | collective-permute-start | bytes 688136 | tf_op jit(solution)/shard_map/ppermute | solution.py:35
  7.4 0.0 collective-permute-done.1.refs_1_
  7.5 3.2 %shard_map.39 = (f32[384,128]{1,0:T(8,128)S(1)}, f32[384,128]{1,0:T(8,128)S(1)}, f32[576,128]{1,0:T(8,128)S(1)}, f32[576,128]{1,0:T(8,128)S(1)}, f32[320,128]{1,0:T(8,128)S(1)}, /*index=5*/f32[320,128]{1,0:T(8,128)S(1)}) custom-call(s32[1]{0:T(128)} %bitcast.core_ref, f32[3,1024,256]{2,1,0:T(8,128)S(1)} %copy-done.1, f32[3,1024,256]{2,1,0:T(8,128)S(1)} %copy-done, ...), custom_call_target="tpu_custom_call" | custom-call | flops 2214592512 | bytes 5767168 | tf_op jit(solution)/shard_map/pallas_call | solution.py:220
  10.7 0.1 collective-permute-start.5
  10.9 0.4 collective-permute-start.4
  11.3 0.9 %collective-permute-done.5 = f32[384,128]{1,0:T(8,128)S(1)} collective-permute-done((f32[384,128]{1,0:T(8,128)S(1)}, f32[384,128]{1,0:T(8,128)S(1)}, u32[]{:S(2)}, u32[]{:S(2)}) %collective-permute-start.5) | collective-permute-done | bytes 196640 | tf_op jit(solution)/shard_map/ppermute | solution.py:35
  12.3 1.1 %collective-permute-start.6 = (f32[384,128]{1,0:T(8,128)S(1)}, f32[384,128]{1,0:T(8,128)S(1)}, u32[]{:S(2)}, u32[]{:S(2)}) collective-permute-start(f32[384,128]{1,0:T(8,128)S(1)} %add.40), channel_id=1, source_target_pairs={{0,2},{1,3},{2,0},{3,1},{4,6},{5,7},{6,4},{7,5},{8,10},{9,11},{10,... | collective-permute-start | bytes 589832 | tf_op jit(solution)/shard_map/ppermute | solution.py:35
  13.3 0.2 collective-permute-done.10
  13.6 1.8 %collective-permute-start.11 = (f32[448,128]{1,0:T(8,128)S(1)}, f32[448,128]{1,0:T(8,128)S(1)}, u32[]{:S(2)}, u32[]{:S(2)}) collective-permute-start(f32[448,128]{1,0:T(8,128)S(1)} %add.44.own_ref.head_ref), channel_id=1, source_target_pairs={{0,4},{4,0},{8,12},{12,8},{16,20},{20,16},{24,28},{28,24},{1,5},{5... | collective-permute-start | bytes 688136 | tf_op jit(solution)/shard_map/ppermute | solution.py:35
  15.4 0.0 collective-permute-start.12
  15.4 0.5 collective-permute-start.2
  15.9 3.4 %collective-permute-done.6 = f32[384,128]{1,0:T(8,128)S(1)} collective-permute-done((f32[384,128]{1,0:T(8,128)S(1)}, f32[384,128]{1,0:T(8,128)S(1)}, u32[]{:S(2)}, u32[]{:S(2)}) %collective-permute-start.6) | collective-permute-done | bytes 196640 | tf_op jit(solution)/shard_map/ppermute | solution.py:35
  19.3 0.0 collective-permute-done.4.second_ref
  19.3 1.1 %collective-permute-start.7 = (f32[576,128]{1,0:T(8,128)S(1)}, f32[576,128]{1,0:T(8,128)S(1)}, u32[]{:S(2)}, u32[]{:S(2)}) collective-permute-start(f32[576,128]{1,0:T(8,128)S(1)} %shard_map.40), channel_id=1, source_target_pairs={{0,2},{1,3},{2,0},{3,1},{4,6},{5,7},{6,4},{7,5},{8,10},{9,11},{10,... | collective-permute-start | bytes 884744 | tf_op jit(solution)/shard_map/ppermute | solution.py:35
  20.4 1.5 %collective-permute-start.14 = (f32[384,128]{1,0:T(8,128)S(1)}, f32[384,128]{1,0:T(8,128)S(1)}, u32[]{:S(2)}, u32[]{:S(2)}) collective-permute-start(f32[384,128]{1,0:T(8,128)S(1)} %add.41.refs_0_.tail_ref.own_ref), channel_id=1, source_target_pairs={{0,4},{4,0},{8,12},{12,8},{16,20},{20,16},{24,28},{28,24},{1,5},{5... | collective-permute-start | bytes 589832 | tf_op jit(solution)/shard_map/ppermute | solution.py:35
  21.9 0.0 collective-permute-done.11.sib_ref.head_sib_ref
  22.0 0.1 collective-permute-start.13
  22.0 0.0 collective-permute-done.2
  22.1 1.6 %collective-permute-start.3 = (f32[320,128]{1,0:T(8,128)S(1)}, f32[320,128]{1,0:T(8,128)S(1)}, u32[]{:S(2)}, u32[]{:S(2)}) collective-permute-start(f32[320,128]{1,0:T(8,128)S(1)} %add.39.first_ref), channel_id=1, source_target_pairs={{0,8},{4,12},{8,0},{12,4},{16,24},{20,28},{24,16},{28,20},{1,9},{5... | collective-permute-start | bytes 491528 | tf_op jit(solution)/shard_map/ppermute | solution.py:35
  23.7 0.3 collective-permute-start.9
  24.0 2.3 %shard_map.42 = (f32[256,256]{1,0:T(8,128)S(1)}, f32[256,256]{1,0:T(8,128)S(1)}) custom-call(s32[1]{0:T(128)} %bitcast.core_ref, f32[448,128]{1,0:T(8,128)S(1)} %add.44.own_ref.head_ref, f32[448,128]{1,0:T(8,128)S(1)} %collective-permute-done.11.sib_ref.head_sib_ref, f32[448,128]{1,0:T(8,128)S(1)} %collective-permute-done.12.own_other_ref.head_other_ref, ...), custom_call_target="tpu_custom_call" | custom-call | flops 900000000 | tf_op jit(solution)/shard_map/pallas_call | solution.py:301
  26.3 0.0 collective-permute-done.14.tail_sib_ref
  26.3 1.1 %shard_map.43 = (f32[640,128]{1,0:T(8,128)S(1)}, f32[576,128]{1,0:T(8,128)S(1)}) custom-call(s32[1]{0:T(128)} %bitcast.core_ref, f32[256,256]{1,0:T(8,128)S(1)} %get-tuple-element.34.inverse_ref, f32[256,256]{1,0:T(8,128)S(1)} %get-tuple-element.35.p_sib_ref, f32[448,128]{1,0:T(8,128)S(1)} %add.44.own_ref.head_ref, ...), custom_call_target="tpu_custom_call" | custom-call | flops 650000000 | bytes 2228228 | tf_op jit(solution)/shard_map/pallas_call | solution.py:289
  27.5 0.2 collective-permute-done.7
  27.7 1.0 %collective-permute-done.3.second_ref = f32[320,128]{1,0:T(8,128)S(1)} collective-permute-done((f32[320,128]{1,0:T(8,128)S(1)}, f32[320,128]{1,0:T(8,128)S(1)}, u32[]{:S(2)}, u32[]{:S(2)}) %collective-permute-start.3) | collective-permute-done | bytes 163872 | tf_op jit(solution)/shard_map/ppermute | solution.py:35
  28.8 1.1 %collective-permute-start.8 = (f32[320,128]{1,0:T(8,128)S(1)}, f32[320,128]{1,0:T(8,128)S(1)}, u32[]{:S(2)}, u32[]{:S(2)}) collective-permute-start(f32[320,128]{1,0:T(8,128)S(1)} %shard_map.41), channel_id=1, source_target_pairs={{0,2},{1,3},{2,0},{3,1},{4,6},{5,7},{6,4},{7,5},{8,10},{9,11},{10,... | collective-permute-start | bytes 491528 | tf_op jit(solution)/shard_map/ppermute | solution.py:35
  29.8 1.1 %collective-permute-start.17 = (f32[192,128]{1,0:T(8,128)S(1)}, f32[192,128]{1,0:T(8,128)S(1)}, u32[]{:S(2)}, u32[]{:S(2)}) collective-permute-start(f32[192,128]{1,0:T(8,128)S(1)} %shard_map.44.refs_0_), channel_id=1, source_target_pairs={{0,4},{4,0},{8,12},{12,8},{16,20},{20,16},{24,28},{28,24},{1,5},{5... | collective-permute-start | bytes 294920 | tf_op jit(solution)/shard_map/ppermute | solution.py:35
  31.0 1.1 %collective-permute-start.21 = (f32[384,128]{1,0:T(8,128)S(1)}, f32[384,128]{1,0:T(8,128)S(1)}, u32[]{:S(2)}, u32[]{:S(2)}) collective-permute-start(f32[384,128]{1,0:T(8,128)S(1)} %shard_map.45.refs_0_), channel_id=1, source_target_pairs={{0,4},{4,0},{8,12},{12,8},{16,20},{20,16},{24,28},{28,24},{1,5},{5... | collective-permute-start | bytes 589832 | tf_op jit(solution)/shard_map/ppermute | solution.py:35
  32.0 0.4 shard_map.46
  32.4 1.6 %collective-permute-start.15 = (f32[320,128]{1,0:T(8,128)S(1)}, f32[320,128]{1,0:T(8,128)S(1)}, u32[]{:S(2)}, u32[]{:S(2)}) collective-permute-start(f32[320,128]{1,0:T(8,128)S(1)} %shard_map.46), channel_id=1, source_target_pairs={{0,8},{4,12},{8,0},{12,4},{16,24},{20,28},{24,16},{28,20},{1,9},{5... | collective-permute-start | bytes 491528 | tf_op jit(solution)/shard_map/ppermute | solution.py:35
  34.1 1.6 %collective-permute-done.17 = f32[192,128]{1,0:T(8,128)S(1)} collective-permute-done((f32[192,128]{1,0:T(8,128)S(1)}, f32[192,128]{1,0:T(8,128)S(1)}, u32[]{:S(2)}, u32[]{:S(2)}) %collective-permute-start.17) | collective-permute-done | bytes 98336 | tf_op jit(solution)/shard_map/ppermute | solution.py:35
  35.6 1.6 %collective-permute-start.18 = (f32[192,128]{1,0:T(8,128)S(1)}, f32[192,128]{1,0:T(8,128)S(1)}, u32[]{:S(2)}, u32[]{:S(2)}) collective-permute-start(f32[192,128]{1,0:T(8,128)S(1)} %add.47.own_ref.p_own_ref), channel_id=1, source_target_pairs={{0,8},{4,12},{8,0},{12,4},{16,24},{20,28},{24,16},{28,20},{1,9},{5... | collective-permute-start | bytes 294920 | tf_op jit(solution)/shard_map/ppermute | solution.py:35
  37.3 0.0 collective-permute-start.19
  37.3 1.0 %collective-permute-done.21 = f32[384,128]{1,0:T(8,128)S(1)} collective-permute-done((f32[384,128]{1,0:T(8,128)S(1)}, f32[384,128]{1,0:T(8,128)S(1)}, u32[]{:S(2)}, u32[]{:S(2)}) %collective-permute-start.21) | collective-permute-done | bytes 196640 | tf_op jit(solution)/shard_map/ppermute | solution.py:35
  38.3 1.6 %collective-permute-start.22 = (f32[384,128]{1,0:T(8,128)S(1)}, f32[384,128]{1,0:T(8,128)S(1)}, u32[]{:S(2)}, u32[]{:S(2)}) collective-permute-start(f32[384,128]{1,0:T(8,128)S(1)} %add.48.own_ref), channel_id=1, source_target_pairs={{0,8},{4,12},{8,0},{12,4},{16,24},{20,28},{24,16},{28,20},{1,9},{5... | collective-permute-start | bytes 589832 | tf_op jit(solution)/shard_map/ppermute | solution.py:35
  39.9 0.0 collective-permute-start.23
  39.9 0.4 collective-permute-done.18.sib_ref
  40.3 0.1 collective-permute-start.20
  40.5 1.1 %collective-permute-start.16 = (f32[320,128]{1,0:T(8,128)S(1)}, f32[320,128]{1,0:T(8,128)S(1)}, u32[]{:S(2)}, u32[]{:S(2)}) collective-permute-start(f32[320,128]{1,0:T(8,128)S(1)} %add_subtract_fusion.1), channel_id=1, source_target_pairs={{0,4},{4,0},{8,12},{12,8},{16,20},{20,16},{24,28},{28,24},{1,5},{5... | collective-permute-start | bytes 491528 | tf_op jit(solution)/shard_map/ppermute | solution.py:35
  41.6 0.0 collective-permute-done.19.own_other_ref.p_own_other_ref
  41.6 0.1 collective-permute-done.20.sib_other_ref
  41.6 2.5 %shard_map.47 = (f32[256,256]{1,0:T(8,128)S(1)}, f32[256,256]{1,0:T(8,128)S(1)}) custom-call(s32[1]{0:T(128)} %bitcast.core_ref, f32[192,128]{1,0:T(8,128)S(1)} %add.47.own_ref.p_own_ref, f32[192,128]{1,0:T(8,128)S(1)} %collective-permute-done.18.sib_ref, f32[192,128]{1,0:T(8,128)S(1)} %collective-permute-done.19.own_other_ref.p_own_other_ref, ...), custom_call_target="tpu_custom_call" | custom-call | flops 900000000 | tf_op jit(solution)/shard_map/pallas_call | solution.py:301
  44.1 0.6 collective-permute-done.22.sib_ref
  44.7 1.2 %shard_map.48 = (f32[384,128]{1,0:T(8,128)S(1)}, f32[384,128]{1,0:T(8,128)S(1)}, f32[320,128]{1,0:T(8,128)S(1)}, f32[256,128]{1,0:T(8,128)S(1)}) custom-call(s32[1]{0:T(128)} %bitcast.core_ref, f32[256,256]{1,0:T(8,128)S(1)} %get-tuple-element.38.inverse_ref, f32[256,256]{1,0:T(8,128)S(1)} %get-tuple-element.39.p_sib_ref, f32[384,128]{1,0:T(8,128)S(1)} %add.48.own_ref, ...), custom_call_target="tpu_custom_call" | custom-call | bytes 1933316 | tf_op jit(solution)/shard_map/pallas_call | solution.py:289
  45.9 0.1 collective-permute-start.24
  46.0 0.5 collective-permute-start.28
  46.5 0.8 %collective-permute-done.24.sib_other_ref = f32[256,128]{1,0:T(8,128)S(1)} collective-permute-done((f32[256,128]{1,0:T(8,128)S(1)}, f32[256,128]{1,0:T(8,128)S(1)}, u32[]{:S(2)}, u32[]{:S(2)}) %collective-permute-start.24) | collective-permute-done | bytes 131104 | tf_op jit(solution)/shard_map/ppermute | solution.py:35
  47.3 0.4 shard_map.49
  47.7 0.0 collective-permute-done.16
  47.8 0.2 collective-permute-start.27
  48.0 2.6 %collective-permute-start.26 = (f32[320,128]{1,0:T(8,128)S(1)}, f32[320,128]{1,0:T(8,128)S(1)}, u32[]{:S(2)}, u32[]{:S(2)}) collective-permute-start(f32[320,128]{1,0:T(8,128)S(1)} %add_subtract_fusion.refs_0_.own_ref), channel_id=1, source_target_pairs={{0,16},{4,20},{8,24},{12,28},{16,0},{20,4},{24,8},{28,12},{1,17},{... | collective-permute-start | bytes 491528 | tf_op jit(solution)/shard_map/ppermute | solution.py:35
  50.6 0.1 collective-permute-start.25
  50.7 0.0 collective-permute-done.28.z0_other_ref
  50.7 0.0 collective-permute-done.27.z1_other_ref
  50.7 2.2 %shard_map.51 = (bf16[1024,256]{1,0:T(8,128)(2,1)S(1)}, bf16[1024,256]{1,0:T(8,128)(2,1)S(1)}, f32[1024,128]{1,0:T(8,128)S(1)}) custom-call(s32[1]{0:T(128)} %bitcast.core_ref, f32[384,128]{1,0:T(8,128)S(1)} %get-tuple-element.43.value_ref.z1_ref, f32[384,128]{1,0:T(8,128)S(1)} %collective-permute-done.27.z1_other_ref, ...), custom_call_target="tpu_custom_call" | custom-call | flops 1207959552 | bytes 7340036 | tf_op jit(solution)/shard_map/pallas_call | solution.py:289
  52.9 6.0 %collective-permute-done.26.value_ref = f32[320,128]{1,0:T(8,128)S(1)} collective-permute-done((f32[320,128]{1,0:T(8,128)S(1)}, f32[320,128]{1,0:T(8,128)S(1)}, u32[]{:S(2)}, u32[]{:S(2)}) %collective-permute-start.26) | collective-permute-done | bytes 163872 | tf_op jit(solution)/shard_map/ppermute | solution.py:35
  58.9 0.1 collective-permute-start.29
  59.0 0.0 collective-permute-done.25.own_other_ref
  59.0 1.4 %collective-permute-done.29.sib_other_ref = f32[320,128]{1,0:T(8,128)S(1)} collective-permute-done((f32[320,128]{1,0:T(8,128)S(1)}, f32[320,128]{1,0:T(8,128)S(1)}, u32[]{:S(2)}, u32[]{:S(2)}) %collective-permute-start.29) | collective-permute-done | bytes 163872 | tf_op jit(solution)/shard_map/ppermute | solution.py:35
  60.3 3.7 %shard_map.53 = f32[1024,128]{1,0:T(8,128)} custom-call(s32[1]{0:T(128)} %bitcast.core_ref, f32[320,128]{1,0:T(8,128)S(1)} %add_subtract_fusion.refs_0_.own_ref, f32[320,128]{1,0:T(8,128)S(1)} %collective-permute-done.25.own_other_ref, f32[320,128]{1,0:T(8,128)S(1)} %shard_map.52.sib_ref, f32[320,128]{1,0:T(8,128)S(1)} %collective-permute-done.29.sib_other_ref, ...), custom_call_target="tpu_custom_call" | custom-call | flops 1107296256 | bytes 3801092 | tf_op jit(solution)/shard_map/pallas_call | solution.py:289
  (37 shorter events, 0.5 us)
Async XLA Ops:
  0.0 7.5 %copy-start = (f32[3,1024,256]{2,1,0:T(8,128)S(1)}, f32[3,1024,256]{2,1,0:T(8,128)}, u32[]{:S(2)}) copy-start(f32[3,1024,256]{2,1,0:T(8,128)} %solved_ref.5) | copy-start | bytes 9437188
  0.0 7.5 %copy-start.1 = (f32[3,1024,256]{2,1,0:T(8,128)S(1)}, f32[3,1024,256]{2,1,0:T(8,128)}, u32[]{:S(2)}) copy-start(f32[3,1024,256]{2,1,0:T(8,128)} %gens_ref.3) | copy-start | bytes 9437188
  0.0 7.5 %copy-start.2 = (f32[1024,128]{1,0:T(8,128)S(1)}, f32[1024,128]{1,0:T(8,128)}, u32[]{:S(2)}) copy-start(f32[1024,128]{1,0:T(8,128)} %rhs_ref.1) | copy-start | bytes 1572868
  2.7 1.6 %collective-permute-start = (f32[448,128]{1,0:T(8,128)S(1)}, f32[448,128]{1,0:T(8,128)S(1)}, u32[]{:S(2)}, u32[]{:S(2)}) collective-permute-start(f32[448,128]{1,0:T(8,128)S(1)} %get-tuple-element.26), channel_id=1, source_target_pairs={{0,1},{1,0},{2,3},{3,2},{4,5},{5,4},{6,7},{7,6},{8,9},{9,8},{10,11... | collective-permute-start | bytes 688136 | tf_op jit(solution)/shard_map/ppermute | solution.py:35
  4.3 3.1 %collective-permute-start.1 = (f32[8,128]{1,0:T(8,128)S(1)}, f32[8,128]{1,0:T(8,128)S(1)}, u32[]{:S(2)}, u32[]{:S(2)}) collective-permute-start(f32[8,128]{1,0:T(8,128)S(1)} %shard_map.38), channel_id=1, source_target_pairs={{0,1},{1,0},{2,3},{3,2},{4,5},{5,4},{6,7},{7,6},{8,9},{9,8},{10,11... | collective-permute-start | bytes 12296 | tf_op jit(solution)/shard_map/ppermute | solution.py:35
  4.8 8.8 %collective-permute-start.10 = (f32[448,128]{1,0:T(8,128)S(1)}, f32[448,128]{1,0:T(8,128)S(1)}, u32[]{:S(2)}, u32[]{:S(2)}) collective-permute-start(f32[448,128]{1,0:T(8,128)S(1)} %add.38.refs_0_), channel_id=1, source_target_pairs={{0,2},{1,3},{2,0},{3,1},{4,6},{5,7},{6,4},{7,5},{8,10},{9,11},{10,... | collective-permute-start | bytes 688136 | tf_op jit(solution)/shard_map/ppermute | solution.py:35
  10.7 1.5 %collective-permute-start.5 = (f32[384,128]{1,0:T(8,128)S(1)}, f32[384,128]{1,0:T(8,128)S(1)}, u32[]{:S(2)}, u32[]{:S(2)}) collective-permute-start(f32[384,128]{1,0:T(8,128)S(1)} %get-tuple-element.33), channel_id=1, source_target_pairs={{0,1},{1,0},{2,3},{3,2},{4,5},{5,4},{6,7},{7,6},{8,9},{9,8},{10,11... | collective-permute-start | bytes 589832 | tf_op jit(solution)/shard_map/ppermute | solution.py:35
  10.9 8.4 %collective-permute-start.4 = (f32[576,128]{1,0:T(8,128)S(1)}, f32[576,128]{1,0:T(8,128)S(1)}, u32[]{:S(2)}, u32[]{:S(2)}) collective-permute-start(f32[576,128]{1,0:T(8,128)S(1)} %get-tuple-element.31), channel_id=1, source_target_pairs={{0,1},{1,0},{2,3},{3,2},{4,5},{5,4},{6,7},{7,6},{8,9},{9,8},{10,11... | collective-permute-start | bytes 884744 | tf_op jit(solution)/shard_map/ppermute | solution.py:35
  12.3 7.0 %collective-permute-start.6 = (f32[384,128]{1,0:T(8,128)S(1)}, f32[384,128]{1,0:T(8,128)S(1)}, u32[]{:S(2)}, u32[]{:S(2)}) collective-permute-start(f32[384,128]{1,0:T(8,128)S(1)} %add.40), channel_id=1, source_target_pairs={{0,2},{1,3},{2,0},{3,1},{4,6},{5,7},{6,4},{7,5},{8,10},{9,11},{10,... | collective-permute-start | bytes 589832 | tf_op jit(solution)/shard_map/ppermute | solution.py:35
  13.6 8.3 %collective-permute-start.11 = (f32[448,128]{1,0:T(8,128)S(1)}, f32[448,128]{1,0:T(8,128)S(1)}, u32[]{:S(2)}, u32[]{:S(2)}) collective-permute-start(f32[448,128]{1,0:T(8,128)S(1)} %add.44.own_ref.head_ref), channel_id=1, source_target_pairs={{0,4},{4,0},{8,12},{12,8},{16,20},{20,16},{24,28},{28,24},{1,5},{5... | collective-permute-start | bytes 688136 | tf_op jit(solution)/shard_map/ppermute | solution.py:35
  15.4 8.3 %collective-permute-start.12 = (f32[448,128]{1,0:T(8,128)S(1)}, f32[448,128]{1,0:T(8,128)S(1)}, u32[]{:S(2)}, u32[]{:S(2)}) collective-permute-start(f32[448,128]{1,0:T(8,128)S(1)} %add.44.own_ref.head_ref), channel_id=1, source_target_pairs={{0,1},{1,0},{2,3},{3,2},{4,5},{5,4},{6,7},{7,6},{8,9},{9,8},{10,11... | collective-permute-start | bytes 688136 | tf_op jit(solution)/shard_map/ppermute | solution.py:35
  15.4 6.6 %collective-permute-start.2 = (f32[320,128]{1,0:T(8,128)S(1)}, f32[320,128]{1,0:T(8,128)S(1)}, u32[]{:S(2)}, u32[]{:S(2)}) collective-permute-start(f32[320,128]{1,0:T(8,128)S(1)} %get-tuple-element.29), channel_id=1, source_target_pairs={{0,1},{1,0},{2,3},{3,2},{4,5},{5,4},{6,7},{7,6},{8,9},{9,8},{10,11... | collective-permute-start | bytes 491528 | tf_op jit(solution)/shard_map/ppermute | solution.py:35
  19.3 8.3 %collective-permute-start.7 = (f32[576,128]{1,0:T(8,128)S(1)}, f32[576,128]{1,0:T(8,128)S(1)}, u32[]{:S(2)}, u32[]{:S(2)}) collective-permute-start(f32[576,128]{1,0:T(8,128)S(1)} %shard_map.40), channel_id=1, source_target_pairs={{0,2},{1,3},{2,0},{3,1},{4,6},{5,7},{6,4},{7,5},{8,10},{9,11},{10,... | collective-permute-start | bytes 884744 | tf_op jit(solution)/shard_map/ppermute | solution.py:35
  20.4 5.9 %collective-permute-start.14 = (f32[384,128]{1,0:T(8,128)S(1)}, f32[384,128]{1,0:T(8,128)S(1)}, u32[]{:S(2)}, u32[]{:S(2)}) collective-permute-start(f32[384,128]{1,0:T(8,128)S(1)} %add.41.refs_0_.tail_ref.own_ref), channel_id=1, source_target_pairs={{0,4},{4,0},{8,12},{12,8},{16,20},{20,16},{24,28},{28,24},{1,5},{5... | collective-permute-start | bytes 589832 | tf_op jit(solution)/shard_map/ppermute | solution.py:35
  22.0 2.0 %collective-permute-start.13 = (f32[192,128]{1,0:T(8,128)S(1)}, f32[192,128]{1,0:T(8,128)S(1)}, u32[]{:S(2)}, u32[]{:S(2)}) collective-permute-start(f32[192,128]{1,0:T(8,128)S(1)} %slice.33), channel_id=1, source_target_pairs={{0,1},{1,0},{2,3},{3,2},{4,5},{5,4},{6,7},{7,6},{8,9},{9,8},{10,11... | collective-permute-start | bytes 294920 | tf_op jit(solution)/shard_map/ppermute | solution.py:35
  22.1 6.7 %collective-permute-start.3 = (f32[320,128]{1,0:T(8,128)S(1)}, f32[320,128]{1,0:T(8,128)S(1)}, u32[]{:S(2)}, u32[]{:S(2)}) collective-permute-start(f32[320,128]{1,0:T(8,128)S(1)} %add.39.first_ref), channel_id=1, source_target_pairs={{0,8},{4,12},{8,0},{12,4},{16,24},{20,28},{24,16},{28,20},{1,9},{5... | collective-permute-start | bytes 491528 | tf_op jit(solution)/shard_map/ppermute | solution.py:35
  23.7 8.3 %collective-permute-start.9 = (f32[256,128]{1,0:T(8,128)S(1)}, f32[256,128]{1,0:T(8,128)S(1)}, u32[]{:S(2)}, u32[]{:S(2)}) collective-permute-start(f32[256,128]{1,0:T(8,128)S(1)} %slice.32), channel_id=1, source_target_pairs={{0,1},{1,0},{2,3},{3,2},{4,5},{5,4},{6,7},{7,6},{8,9},{9,8},{10,11... | collective-permute-start | bytes 393224 | tf_op jit(solution)/shard_map/ppermute | solution.py:35
  28.8 11.2 %collective-permute-start.8 = (f32[320,128]{1,0:T(8,128)S(1)}, f32[320,128]{1,0:T(8,128)S(1)}, u32[]{:S(2)}, u32[]{:S(2)}) collective-permute-start(f32[320,128]{1,0:T(8,128)S(1)} %shard_map.41), channel_id=1, source_target_pairs={{0,2},{1,3},{2,0},{3,1},{4,6},{5,7},{6,4},{7,5},{8,10},{9,11},{10,... | collective-permute-start | bytes 491528 | tf_op jit(solution)/shard_map/ppermute | solution.py:35
  29.8 5.8 %collective-permute-start.17 = (f32[192,128]{1,0:T(8,128)S(1)}, f32[192,128]{1,0:T(8,128)S(1)}, u32[]{:S(2)}, u32[]{:S(2)}) collective-permute-start(f32[192,128]{1,0:T(8,128)S(1)} %shard_map.44.refs_0_), channel_id=1, source_target_pairs={{0,4},{4,0},{8,12},{12,8},{16,20},{20,16},{24,28},{28,24},{1,5},{5... | collective-permute-start | bytes 294920 | tf_op jit(solution)/shard_map/ppermute | solution.py:35
  31.0 7.3 %collective-permute-start.21 = (f32[384,128]{1,0:T(8,128)S(1)}, f32[384,128]{1,0:T(8,128)S(1)}, u32[]{:S(2)}, u32[]{:S(2)}) collective-permute-start(f32[384,128]{1,0:T(8,128)S(1)} %shard_map.45.refs_0_), channel_id=1, source_target_pairs={{0,4},{4,0},{8,12},{12,8},{16,20},{20,16},{24,28},{28,24},{1,5},{5... | collective-permute-start | bytes 589832 | tf_op jit(solution)/shard_map/ppermute | solution.py:35
  32.4 8.0 %collective-permute-start.15 = (f32[320,128]{1,0:T(8,128)S(1)}, f32[320,128]{1,0:T(8,128)S(1)}, u32[]{:S(2)}, u32[]{:S(2)}) collective-permute-start(f32[320,128]{1,0:T(8,128)S(1)} %shard_map.46), channel_id=1, source_target_pairs={{0,8},{4,12},{8,0},{12,4},{16,24},{20,28},{24,16},{28,20},{1,9},{5... | collective-permute-start | bytes 491528 | tf_op jit(solution)/shard_map/ppermute | solution.py:35
  35.6 4.7 %collective-permute-start.18 = (f32[192,128]{1,0:T(8,128)S(1)}, f32[192,128]{1,0:T(8,128)S(1)}, u32[]{:S(2)}, u32[]{:S(2)}) collective-permute-start(f32[192,128]{1,0:T(8,128)S(1)} %add.47.own_ref.p_own_ref), channel_id=1, source_target_pairs={{0,8},{4,12},{8,0},{12,4},{16,24},{20,28},{24,16},{28,20},{1,9},{5... | collective-permute-start | bytes 294920 | tf_op jit(solution)/shard_map/ppermute | solution.py:35
  37.3 4.3 %collective-permute-start.19 = (f32[192,128]{1,0:T(8,128)S(1)}, f32[192,128]{1,0:T(8,128)S(1)}, u32[]{:S(2)}, u32[]{:S(2)}) collective-permute-start(f32[192,128]{1,0:T(8,128)S(1)} %add.47.own_ref.p_own_ref), channel_id=1, source_target_pairs={{0,1},{1,0},{2,3},{3,2},{4,5},{5,4},{6,7},{7,6},{8,9},{9,8},{10,11... | collective-permute-start | bytes 294920 | tf_op jit(solution)/shard_map/ppermute | solution.py:35
  38.3 6.4 %collective-permute-start.22 = (f32[384,128]{1,0:T(8,128)S(1)}, f32[384,128]{1,0:T(8,128)S(1)}, u32[]{:S(2)}, u32[]{:S(2)}) collective-permute-start(f32[384,128]{1,0:T(8,128)S(1)} %add.48.own_ref), channel_id=1, source_target_pairs={{0,8},{4,12},{8,0},{12,4},{16,24},{20,28},{24,16},{28,20},{1,9},{5... | collective-permute-start | bytes 589832 | tf_op jit(solution)/shard_map/ppermute | solution.py:35
  39.9 4.2 %collective-permute-start.23 = (f32[256,128]{1,0:T(8,128)S(1)}, f32[256,128]{1,0:T(8,128)S(1)}, u32[]{:S(2)}, u32[]{:S(2)}) collective-permute-start(f32[256,128]{1,0:T(8,128)S(1)} %slice.36), channel_id=1, source_target_pairs={{0,1},{1,0},{2,3},{3,2},{4,5},{5,4},{6,7},{7,6},{8,9},{9,8},{10,11... | collective-permute-start | bytes 393224 | tf_op jit(solution)/shard_map/ppermute | solution.py:35
  40.3 1.3 %collective-permute-start.20 = (f32[192,128]{1,0:T(8,128)S(1)}, f32[192,128]{1,0:T(8,128)S(1)}, u32[]{:S(2)}, u32[]{:S(2)}) collective-permute-start(f32[192,128]{1,0:T(8,128)S(1)} %collective-permute-done.18.sib_ref), channel_id=1, source_target_pairs={{0,1},{1,0},{2,3},{3,2},{4,5},{5,4},{6,7},{7,6},{8,9},{9,8},{10,11... | collective-permute-start | bytes 294920 | tf_op jit(solution)/shard_map/ppermute | solution.py:35
  40.5 7.2 %collective-permute-start.16 = (f32[320,128]{1,0:T(8,128)S(1)}, f32[320,128]{1,0:T(8,128)S(1)}, u32[]{:S(2)}, u32[]{:S(2)}) collective-permute-start(f32[320,128]{1,0:T(8,128)S(1)} %add_subtract_fusion.1), channel_id=1, source_target_pairs={{0,4},{4,0},{8,12},{12,8},{16,20},{20,16},{24,28},{28,24},{1,5},{5... | collective-permute-start | bytes 491528 | tf_op jit(solution)/shard_map/ppermute | solution.py:35
  45.9 1.4 %collective-permute-start.24 = (f32[256,128]{1,0:T(8,128)S(1)}, f32[256,128]{1,0:T(8,128)S(1)}, u32[]{:S(2)}, u32[]{:S(2)}) collective-permute-start(f32[256,128]{1,0:T(8,128)S(1)} %get-tuple-element.40.sib_ref), channel_id=1, source_target_pairs={{0,1},{1,0},{2,3},{3,2},{4,5},{5,4},{6,7},{7,6},{8,9},{9,8},{10,11... | collective-permute-start | bytes 393224 | tf_op jit(solution)/shard_map/ppermute | solution.py:35
  46.0 4.7 %collective-permute-start.28 = (f32[640,128]{1,0:T(8,128)S(1)}, f32[640,128]{1,0:T(8,128)S(1)}, u32[]{:S(2)}, u32[]{:S(2)}) collective-permute-start(f32[640,128]{1,0:T(8,128)S(1)} %get-tuple-element.36.z_ref.z0_ref), channel_id=1, source_target_pairs={{0,1},{1,0},{2,3},{3,2},{4,5},{5,4},{6,7},{7,6},{8,9},{9,8},{10,11... | collective-permute-start | bytes 983048 | tf_op jit(solution)/shard_map/ppermute | solution.py:35
  47.8 2.9 %collective-permute-start.27 = (f32[384,128]{1,0:T(8,128)S(1)}, f32[384,128]{1,0:T(8,128)S(1)}, u32[]{:S(2)}, u32[]{:S(2)}) collective-permute-start(f32[384,128]{1,0:T(8,128)S(1)} %shard_map.50), channel_id=1, source_target_pairs={{0,1},{1,0},{2,3},{3,2},{4,5},{5,4},{6,7},{7,6},{8,9},{9,8},{10,11... | collective-permute-start | bytes 589832 | tf_op jit(solution)/shard_map/ppermute | solution.py:35
  48.0 10.9 %collective-permute-start.26 = (f32[320,128]{1,0:T(8,128)S(1)}, f32[320,128]{1,0:T(8,128)S(1)}, u32[]{:S(2)}, u32[]{:S(2)}) collective-permute-start(f32[320,128]{1,0:T(8,128)S(1)} %add_subtract_fusion.refs_0_.own_ref), channel_id=1, source_target_pairs={{0,16},{4,20},{8,24},{12,28},{16,0},{20,4},{24,8},{28,12},{1,17},{... | collective-permute-start | bytes 491528 | tf_op jit(solution)/shard_map/ppermute | solution.py:35
  50.6 8.4 %collective-permute-start.25 = (f32[320,128]{1,0:T(8,128)S(1)}, f32[320,128]{1,0:T(8,128)S(1)}, u32[]{:S(2)}, u32[]{:S(2)}) collective-permute-start(f32[320,128]{1,0:T(8,128)S(1)} %add_subtract_fusion.refs_0_.own_ref), channel_id=1, source_target_pairs={{0,1},{1,0},{2,3},{3,2},{4,5},{5,4},{6,7},{7,6},{8,9},{9,8},{10,11... | collective-permute-start | bytes 491528 | tf_op jit(solution)/shard_map/ppermute | solution.py:35
  58.9 1.5 %collective-permute-start.29 = (f32[320,128]{1,0:T(8,128)S(1)}, f32[320,128]{1,0:T(8,128)S(1)}, u32[]{:S(2)}, u32[]{:S(2)}) collective-permute-start(f32[320,128]{1,0:T(8,128)S(1)} %shard_map.52.sib_ref), channel_id=1, source_target_pairs={{0,1},{1,0},{2,3},{3,2},{4,5},{5,4},{6,7},{7,6},{8,9},{9,8},{10,11... | collective-permute-start | bytes 491528 | tf_op jit(solution)/shard_map/ppermute | solution.py:35

commit v11 on v10

--- a/solution.py
+++ b/solution.py
@@ -418,19 +418,17 @@
             value = value + swap(value, "rows", bit)
         return value
 
-    keep, send = products(core, generators, solved_gens, rhs, (((0, 0), (0, 1)),), 4)
+    keep, send = products(core, generators, solved_gens, rhs, (((0, 0), (0, 1)),), 2)
     head = keep + swap(send, "sub", 0)
     token = swap(call(keep_kernel, struct(8), 0, core, send[:8], after=(head,)), "sub", 0)
-    rest = (((0, 2), (0, 3)), ((1, 1), (1, 2), (1, 3)), ((2, 2), (2, 3)))
-    parts = products(core, generators, solved_gens, rhs, rest, 1, token)
+    parts = products(core, generators, solved_gens, rhs, (((0, 2), (0, 3)),), 1, token)
+    rest = (((1, 1), (1, 2), (1, 3)), ((2, 2), (2, 3)))
+    parts += products(core, generators, solved_gens, rhs, rest, 1, parts[1])
     parts = [(keep, swap(send, "sub", 0)) for keep, send in zip(parts[::2], parts[1::2])]
     head = over_child(head)
     tail = over_child(parts[0][0] + parts[0][1])
     near = over_child(call(add_kernel, struct(SYM + RANK + HALF), 0, core, *parts[1], after=(tail,)))
     third = parts[2][0] + parts[2][1]
-    third = over_child(
-        call(add_kernel, struct(last), 0, core, third, swap(third, "rows", span_bits + 1), after=(near,))
-    )
 
     head_sib = swap(head, "rows", span_bits)
     tail_sib = swap(tail, "rows", span_bits)
@@ -444,6 +442,9 @@
     )
     p_own = call(subtract_kernel, struct(SYM), 0, core, near[:SYM], crossed[:SYM])
     r_own = call(subtract_kernel, struct(RANK + HALF), 0, core, near[SYM:], crossed[SYM:], after=(p_own,))
+    third = over_child(
+        call(add_kernel, struct(last), 0, core, third, swap(third, "rows", span_bits + 1), after=(r_own,))
+    )
     crossed = call(third_kernel, struct(last), THIRD_FLOPS, core, tail, tail_other, z0, after=(r_own,))
     third = third - (crossed + swap(crossed, "rows", span_bits + 1))
     third = third + swap(third, "rows", span_bits)

time: 64.1 us -> 62.9 us (0.981)
  waiting for transfers between devices: 18.7 us -> 16.4 us
  starting transfers between devices: 25 us -> 25.7 us
    ppermute x30, waiting for transfers between devices: 18.7 us -> 16.4 us  [swap(): return lax.ppermute(value, axis, pairs)]
    ppermute x30, starting transfers between devices: 25 us -> 25.7 us  [swap(): return lax.ppermute(value, axis, pairs)]
    pallas_call x2 -> x3, Pallas kernels: 5.89 us -> 6.24 us  [products(): pl.pallas_call(functools.partial(product_kernel, groups, chunks), in_spec...]
  transfers between devices with their start and end apart: 30 -> 30, of which waited for: 14 -> 9; matrix products, arithmetic and copies ran while one was open for 0% -> 0% of each run, Pallas kernels for 21% -> 22%
where the time goes in v11:
time: 62.9 us; the launch traced here: 62.8 us
  starting transfers between devices  25.7 us (41%)
  Pallas kernels  20.1 us (32%)
  waiting for transfers between devices  16.4 us (26%)
    ppermute x30, starting transfers between devices, swap(): return lax.ppermute(value, axis, pairs)  25.7 us
    ppermute x30, waiting for transfers between devices, swap(): return lax.ppermute(value, axis, pairs)  16.4 us
    pallas_call x13, Pallas kernels, call(): pl.pallas_call(kernel, in_specs=[SMEM] + [VMEM] * (len(values) - 1) + [AN...  9.12 us
    pallas_call x3, Pallas kernels, products(): pl.pallas_call(functools.partial(product_kernel, groups, chunks), in_spec...  6.24 us
    pallas_call x2, Pallas kernels, inverse(): pl.pallas_call(invert_kernel, in_specs=[SMEM] + [VMEM] * 4, out_specs=[VM...  4.73 us
  transfers between devices with their start and end apart: 30, of which 9 were waited for; matrix products, arithmetic and copies ran while one was open for 0% of the time, Pallas kernels for 22%

profile of v11, /device:TPU:0, one launch (start us, length us, event | category | flops | bytes accessed | tf_op | source)
XLA Modules:
  0.0 62.8 jit_solution(3466010105202537065)
XLA Ops:
  0.0 2.7 %shard_map.37 = (f32[448,128]{1,0:T(8,128)S(1)}, f32[448,128]{1,0:T(8,128)S(1)}) custom-call(s32[1]{0:T(128)} %bitcast.core_ref, f32[3,1024,256]{2,1,0:T(8,128)} %gens_ref.5, f32[3,1024,256]{2,1,0:T(8,128)} %solved_ref.7), custom_call_target="tpu_custom_call" | custom-call | flops 805306368 | bytes 3145728 | tf_op jit(solution)/shard_map/pallas_call | solution.py:220
  2.7 0.5 collective-permute-start
  3.2 1.1 %collective-permute-done = f32[448,128]{1,0:T(8,128)S(1)} collective-permute-done((f32[448,128]{1,0:T(8,128)S(1)}, f32[448,128]{1,0:T(8,128)S(1)}, u32[]{:S(2)}, u32[]{:S(2)}) %collective-permute-start) | collective-permute-done | bytes 229408 | tf_op jit(solution)/shard_map/ppermute | solution.py:35
  4.4 0.4 collective-permute-start.1
  4.8 2.7 %collective-permute-start.8 = (f32[448,128]{1,0:T(8,128)S(1)}, f32[448,128]{1,0:T(8,128)S(1)}, u32[]{:S(2)}, u32[]{:S(2)}) collective-permute-start(f32[448,128]{1,0:T(8,128)S(1)} %add.38.refs_0_), channel_id=1, source_target_pairs={{0,2},{1,3},{2,0},{3,1},{4,6},{5,7},{6,4},{7,5},{8,10},{9,11},{10,... | collective-permute-start | bytes 688136 | tf_op jit(solution)/shard_map/ppermute | solution.py:35
  7.5 0.0 collective-permute-done.1.refs_1_
  7.5 1.2 %shard_map.39 = (f32[384,128]{1,0:T(8,128)S(1)}, f32[384,128]{1,0:T(8,128)S(1)}) custom-call(s32[1]{0:T(128)} %bitcast.core_ref, f32[3,1024,256]{2,1,0:T(8,128)S(1)} %copy-done.1, f32[3,1024,256]{2,1,0:T(8,128)S(1)} %copy-done, f32[1024,128]{1,0:T(8,128)S(1)} %copy-done.2, f32[8,128]{1,0:T(8,128)S(1)} %collective-permute-done.1.refs_1_), custom_call_target="tpu_custom_call" | custom-call | flops 603979776 | bytes 2621440 | tf_op jit(solution)/shard_map/pallas_call | solution.py:220
  8.7 0.1 collective-permute-start.5
  8.8 2.4 %shard_map.40 = (f32[576,128]{1,0:T(8,128)S(1)}, f32[576,128]{1,0:T(8,128)S(1)}, f32[320,128]{1,0:T(8,128)S(1)}, f32[320,128]{1,0:T(8,128)S(1)}) custom-call(s32[1]{0:T(128)} %bitcast.core_ref, f32[3,1024,256]{2,1,0:T(8,128)S(1)} %copy-done.1, f32[3,1024,256]{2,1,0:T(8,128)S(1)} %copy-done, f32[1024,128]{1,0:T(8,128)S(1)} %copy-done.2, ...), custom_call_target="tpu_custom_call" | custom-call | flops 1610612736 | bytes 4718592 | tf_op jit(solution)/shard_map/pallas_call | solution.py:220
  11.2 0.5 collective-permute-start.4
  11.7 0.0 collective-permute-done.5
  11.7 1.1 %collective-permute-start.6 = (f32[384,128]{1,0:T(8,128)S(1)}, f32[384,128]{1,0:T(8,128)S(1)}, u32[]{:S(2)}, u32[]{:S(2)}) collective-permute-start(f32[384,128]{1,0:T(8,128)S(1)} %add.40), channel_id=1, source_target_pairs={{0,2},{1,3},{2,0},{3,1},{4,6},{5,7},{6,4},{7,5},{8,10},{9,11},{10,... | collective-permute-start | bytes 589832 | tf_op jit(solution)/shard_map/ppermute | solution.py:35
  12.8 0.8 %collective-permute-done.8 = f32[448,128]{1,0:T(8,128)S(1)} collective-permute-done((f32[448,128]{1,0:T(8,128)S(1)}, f32[448,128]{1,0:T(8,128)S(1)}, u32[]{:S(2)}, u32[]{:S(2)}) %collective-permute-start.8) | collective-permute-done | bytes 229408 | tf_op jit(solution)/shard_map/ppermute | solution.py:35
  13.6 1.8 %collective-permute-start.9 = (f32[448,128]{1,0:T(8,128)S(1)}, f32[448,128]{1,0:T(8,128)S(1)}, u32[]{:S(2)}, u32[]{:S(2)}) collective-permute-start(f32[448,128]{1,0:T(8,128)S(1)} %add.43.own_ref.head_ref), channel_id=1, source_target_pairs={{0,4},{4,0},{8,12},{12,8},{16,20},{20,16},{24,28},{28,24},{1,5},{5... | collective-permute-start | bytes 688136 | tf_op jit(solution)/shard_map/ppermute | solution.py:35
  15.4 0.0 collective-permute-start.10
  15.4 0.5 collective-permute-start.2
  15.9 2.8 %collective-permute-done.6 = f32[384,128]{1,0:T(8,128)S(1)} collective-permute-done((f32[384,128]{1,0:T(8,128)S(1)}, f32[384,128]{1,0:T(8,128)S(1)}, u32[]{:S(2)}, u32[]{:S(2)}) %collective-permute-start.6) | collective-permute-done | bytes 196640 | tf_op jit(solution)/shard_map/ppermute | solution.py:35
  18.7 0.0 collective-permute-done.4.second_ref
  18.8 1.2 %collective-permute-start.7 = (f32[576,128]{1,0:T(8,128)S(1)}, f32[576,128]{1,0:T(8,128)S(1)}, u32[]{:S(2)}, u32[]{:S(2)}) collective-permute-start(f32[576,128]{1,0:T(8,128)S(1)} %shard_map.41), channel_id=1, source_target_pairs={{0,2},{1,3},{2,0},{3,1},{4,6},{5,7},{6,4},{7,5},{8,10},{9,11},{10,... | collective-permute-start | bytes 884744 | tf_op jit(solution)/shard_map/ppermute | solution.py:35
  19.9 1.5 %collective-permute-start.12 = (f32[384,128]{1,0:T(8,128)S(1)}, f32[384,128]{1,0:T(8,128)S(1)}, u32[]{:S(2)}, u32[]{:S(2)}) collective-permute-start(f32[384,128]{1,0:T(8,128)S(1)} %add.41.refs_0_.tail_ref.own_ref), channel_id=1, source_target_pairs={{0,4},{4,0},{8,12},{12,8},{16,20},{20,16},{24,28},{28,24},{1,5},{5... | collective-permute-start | bytes 589832 | tf_op jit(solution)/shard_map/ppermute | solution.py:35
  21.4 0.0 collective-permute-done.9.sib_ref.head_sib_ref
  21.4 0.1 collective-permute-start.11
  21.5 0.0 collective-permute-done.2
  21.6 1.6 %collective-permute-start.3 = (f32[320,128]{1,0:T(8,128)S(1)}, f32[320,128]{1,0:T(8,128)S(1)}, u32[]{:S(2)}, u32[]{:S(2)}) collective-permute-start(f32[320,128]{1,0:T(8,128)S(1)} %add.39.first_ref), channel_id=1, source_target_pairs={{0,8},{4,12},{8,0},{12,4},{16,24},{20,28},{24,16},{28,20},{1,9},{5... | collective-permute-start | bytes 491528 | tf_op jit(solution)/shard_map/ppermute | solution.py:35
  23.2 0.0 collective-permute-done.10.own_other_ref.head_other_ref
  23.2 0.3 collective-permute-start.14
  23.5 0.0 collective-permute-done.11.sib_other_ref
  23.5 2.3 %shard_map.42 = (f32[256,256]{1,0:T(8,128)S(1)}, f32[256,256]{1,0:T(8,128)S(1)}) custom-call(s32[1]{0:T(128)} %bitcast.core_ref, f32[448,128]{1,0:T(8,128)S(1)} %add.43.own_ref.head_ref, f32[448,128]{1,0:T(8,128)S(1)} %collective-permute-done.9.sib_ref.head_sib_ref, f32[448,128]{1,0:T(8,128)S(1)} %collective-permute-done.10.own_other_ref.head_other_ref, ...), custom_call_target="tpu_custom_call" | custom-call | flops 900000000 | tf_op jit(solution)/shard_map/pallas_call | solution.py:301
  25.8 0.0 collective-permute-done.12.tail_sib_ref
  25.8 1.1 %shard_map.43 = (f32[640,128]{1,0:T(8,128)S(1)}, f32[576,128]{1,0:T(8,128)S(1)}) custom-call(s32[1]{0:T(128)} %bitcast.core_ref, f32[256,256]{1,0:T(8,128)S(1)} %get-tuple-element.34.inverse_ref, f32[256,256]{1,0:T(8,128)S(1)} %get-tuple-element.35.p_sib_ref, f32[448,128]{1,0:T(8,128)S(1)} %add.43.own_ref.head_ref, ...), custom_call_target="tpu_custom_call" | custom-call | flops 650000000 | bytes 2228228 | tf_op jit(solution)/shard_map/pallas_call | solution.py:289
  27.0 0.0 collective-permute-done.7
  27.1 1.6 %collective-permute-start.17 = (f32[192,128]{1,0:T(8,128)S(1)}, f32[192,128]{1,0:T(8,128)S(1)}, u32[]{:S(2)}, u32[]{:S(2)}) collective-permute-start(f32[192,128]{1,0:T(8,128)S(1)} %shard_map.44.refs_0_), channel_id=1, source_target_pairs={{0,4},{4,0},{8,12},{12,8},{16,20},{20,16},{24,28},{28,24},{1,5},{5... | collective-permute-start | bytes 294920 | tf_op jit(solution)/shard_map/ppermute | solution.py:35
  28.7 0.6 collective-permute-start.21
  29.3 0.0 collective-permute-done.3.second_ref
  29.3 1.3 %collective-permute-start.13 = (f32[320,128]{1,0:T(8,128)S(1)}, f32[320,128]{1,0:T(8,128)S(1)}, u32[]{:S(2)}, u32[]{:S(2)}) collective-permute-start(f32[320,128]{1,0:T(8,128)S(1)} %shard_map.46), channel_id=1, source_target_pairs={{0,2},{1,3},{2,0},{3,1},{4,6},{5,7},{6,4},{7,5},{8,10},{9,11},{10,... | collective-permute-start | bytes 491528 | tf_op jit(solution)/shard_map/ppermute | solution.py:35
  30.6 0.4 shard_map.47
  31.0 1.6 %collective-permute-start.15 = (f32[320,128]{1,0:T(8,128)S(1)}, f32[320,128]{1,0:T(8,128)S(1)}, u32[]{:S(2)}, u32[]{:S(2)}) collective-permute-start(f32[320,128]{1,0:T(8,128)S(1)} %shard_map.47), channel_id=1, source_target_pairs={{0,8},{4,12},{8,0},{12,4},{16,24},{20,28},{24,16},{28,20},{1,9},{5... | collective-permute-start | bytes 491528 | tf_op jit(solution)/shard_map/ppermute | solution.py:35
  32.6 0.2 collective-permute-done.17
  32.8 1.8 %collective-permute-start.18 = (f32[192,128]{1,0:T(8,128)S(1)}, f32[192,128]{1,0:T(8,128)S(1)}, u32[]{:S(2)}, u32[]{:S(2)}) collective-permute-start(f32[192,128]{1,0:T(8,128)S(1)} %add.47.own_ref.p_own_ref), channel_id=1, source_target_pairs={{0,8},{4,12},{8,0},{12,4},{16,24},{20,28},{24,16},{28,20},{1,9},{5... | collective-permute-start | bytes 294920 | tf_op jit(solution)/shard_map/ppermute | solution.py:35
  34.6 1.8 %collective-permute-done.21 = f32[384,128]{1,0:T(8,128)S(1)} collective-permute-done((f32[384,128]{1,0:T(8,128)S(1)}, f32[384,128]{1,0:T(8,128)S(1)}, u32[]{:S(2)}, u32[]{:S(2)}) %collective-permute-start.21) | collective-permute-done | bytes 196640 | tf_op jit(solution)/shard_map/ppermute | solution.py:35
  36.4 0.8 %collective-permute-start.22 = (f32[384,128]{1,0:T(8,128)S(1)}, f32[384,128]{1,0:T(8,128)S(1)}, u32[]{:S(2)}, u32[]{:S(2)}) collective-permute-start(f32[384,128]{1,0:T(8,128)S(1)} %add.48.own_ref), channel_id=1, source_target_pairs={{0,8},{4,12},{8,0},{12,4},{16,24},{20,28},{24,16},{28,20},{1,9},{5... | collective-permute-start | bytes 589832 | tf_op jit(solution)/shard_map/ppermute | solution.py:35
  37.2 0.0 collective-permute-done.13
  37.2 1.4 %collective-permute-done.18.sib_ref = f32[192,128]{1,0:T(8,128)S(1)} collective-permute-done((f32[192,128]{1,0:T(8,128)S(1)}, f32[192,128]{1,0:T(8,128)S(1)}, u32[]{:S(2)}, u32[]{:S(2)}) %collective-permute-start.18) | collective-permute-done | bytes 98336 | tf_op jit(solution)/shard_map/ppermute | solution.py:35
  38.6 0.0 collective-permute-done.15
  38.6 2.3 %collective-permute-start.16 = (f32[320,128]{1,0:T(8,128)S(1)}, f32[320,128]{1,0:T(8,128)S(1)}, u32[]{:S(2)}, u32[]{:S(2)}) collective-permute-start(f32[320,128]{1,0:T(8,128)S(1)} %add_subtract_fusion.1), channel_id=1, source_target_pairs={{0,4},{4,0},{8,12},{12,8},{16,20},{20,16},{24,28},{28,24},{1,5},{5... | collective-permute-start | bytes 491528 | tf_op jit(solution)/shard_map/ppermute | solution.py:35
  41.0 0.0 collective-permute-done.19.own_other_ref.p_own_other_ref
  41.0 2.5 %shard_map.48 = (f32[256,256]{1,0:T(8,128)S(1)}, f32[256,256]{1,0:T(8,128)S(1)}) custom-call(s32[1]{0:T(128)} %bitcast.core_ref, f32[192,128]{1,0:T(8,128)S(1)} %add.47.own_ref.p_own_ref, f32[192,128]{1,0:T(8,128)S(1)} %collective-permute-done.18.sib_ref, f32[192,128]{1,0:T(8,128)S(1)} %collective-permute-done.19.own_other_ref.p_own_other_ref, ...), custom_call_target="tpu_custom_call" | custom-call | flops 900000000 | tf_op jit(solution)/shard_map/pallas_call | solution.py:301
  43.5 0.0 collective-permute-done.23.own_other_ref
  43.5 0.0 collective-permute-done.22.sib_ref
  43.5 1.2 %shard_map.49 = (f32[384,128]{1,0:T(8,128)S(1)}, f32[384,128]{1,0:T(8,128)S(1)}, f32[320,128]{1,0:T(8,128)S(1)}, f32[256,128]{1,0:T(8,128)S(1)}) custom-call(s32[1]{0:T(128)} %bitcast.core_ref, f32[256,256]{1,0:T(8,128)S(1)} %get-tuple-element.38.inverse_ref, f32[256,256]{1,0:T(8,128)S(1)} %get-tuple-element.39.p_sib_ref, f32[384,128]{1,0:T(8,128)S(1)} %add.48.own_ref, ...), custom_call_target="tpu_custom_call" | custom-call | bytes 1933316 | tf_op jit(solution)/shard_map/pallas_call | solution.py:289
  44.7 0.3 collective-permute-start.24
  45.0 0.3 collective-permute-start.28
  45.2 0.8 %collective-permute-done.24.sib_other_ref = f32[256,128]{1,0:T(8,128)S(1)} collective-permute-done((f32[256,128]{1,0:T(8,128)S(1)}, f32[256,128]{1,0:T(8,128)S(1)}, u32[]{:S(2)}, u32[]{:S(2)}) %collective-permute-start.24) | collective-permute-done | bytes 131104 | tf_op jit(solution)/shard_map/ppermute | solution.py:35
  46.1 0.4 shard_map.50
  46.6 0.3 collective-permute-start.27
  46.8 2.6 %collective-permute-start.26 = (f32[320,128]{1,0:T(8,128)S(1)}, f32[320,128]{1,0:T(8,128)S(1)}, u32[]{:S(2)}, u32[]{:S(2)}) collective-permute-start(f32[320,128]{1,0:T(8,128)S(1)} %add_subtract_fusion.refs_0_.own_ref), channel_id=1, source_target_pairs={{0,16},{4,20},{8,24},{12,28},{16,0},{20,4},{24,8},{28,12},{1,17},{... | collective-permute-start | bytes 491528 | tf_op jit(solution)/shard_map/ppermute | solution.py:35
  49.4 0.0 collective-permute-start.25
  49.4 0.0 collective-permute-done.28.z0_other_ref
  49.4 0.0 collective-permute-done.27.z1_other_ref
  49.4 2.2 %shard_map.52 = (bf16[1024,256]{1,0:T(8,128)(2,1)S(1)}, bf16[1024,256]{1,0:T(8,128)(2,1)S(1)}, f32[1024,128]{1,0:T(8,128)S(1)}) custom-call(s32[1]{0:T(128)} %bitcast.core_ref, f32[384,128]{1,0:T(8,128)S(1)} %get-tuple-element.43.value_ref.z1_ref, f32[384,128]{1,0:T(8,128)S(1)} %collective-permute-done.27.z1_other_ref, ...), custom_call_target="tpu_custom_call" | custom-call | flops 1207959552 | bytes 7340036 | tf_op jit(solution)/shard_map/pallas_call | solution.py:289
  51.6 6.0 %collective-permute-done.26.value_ref = f32[320,128]{1,0:T(8,128)S(1)} collective-permute-done((f32[320,128]{1,0:T(8,128)S(1)}, f32[320,128]{1,0:T(8,128)S(1)}, u32[]{:S(2)}, u32[]{:S(2)}) %collective-permute-start.26) | collective-permute-done | bytes 163872 | tf_op jit(solution)/shard_map/ppermute | solution.py:35
  57.7 0.1 collective-permute-start.29
  57.7 1.4 %collective-permute-done.29.sib_other_ref = f32[320,128]{1,0:T(8,128)S(1)} collective-permute-done((f32[320,128]{1,0:T(8,128)S(1)}, f32[320,128]{1,0:T(8,128)S(1)}, u32[]{:S(2)}, u32[]{:S(2)}) %collective-permute-start.29) | collective-permute-done | bytes 163872 | tf_op jit(solution)/shard_map/ppermute | solution.py:35
  59.1 3.7 %shard_map.54 = f32[1024,128]{1,0:T(8,128)} custom-call(s32[1]{0:T(128)} %bitcast.core_ref, f32[320,128]{1,0:T(8,128)S(1)} %add_subtract_fusion.refs_0_.own_ref, f32[320,128]{1,0:T(8,128)S(1)} %collective-permute-done.25.own_other_ref, f32[320,128]{1,0:T(8,128)S(1)} %shard_map.53.sib_ref, f32[320,128]{1,0:T(8,128)S(1)} %collective-permute-done.29.sib_other_ref, ...), custom_call_target="tpu_custom_call" | custom-call | flops 1107296256 | bytes 3801092 | tf_op jit(solution)/shard_map/pallas_call | solution.py:289
  (38 shorter events, 0.5 us)
Async XLA Ops:
  0.0 7.5 %copy-start = (f32[3,1024,256]{2,1,0:T(8,128)S(1)}, f32[3,1024,256]{2,1,0:T(8,128)}, u32[]{:S(2)}) copy-start(f32[3,1024,256]{2,1,0:T(8,128)} %solved_ref.7) | copy-start | bytes 9437188
  0.0 7.5 %copy-start.1 = (f32[3,1024,256]{2,1,0:T(8,128)S(1)}, f32[3,1024,256]{2,1,0:T(8,128)}, u32[]{:S(2)}) copy-start(f32[3,1024,256]{2,1,0:T(8,128)} %gens_ref.5) | copy-start | bytes 9437188
  0.0 7.5 %copy-start.2 = (f32[1024,128]{1,0:T(8,128)S(1)}, f32[1024,128]{1,0:T(8,128)}, u32[]{:S(2)}) copy-start(f32[1024,128]{1,0:T(8,128)} %rhs_ref.1) | copy-start | bytes 1572868
  2.7 1.6 %collective-permute-start = (f32[448,128]{1,0:T(8,128)S(1)}, f32[448,128]{1,0:T(8,128)S(1)}, u32[]{:S(2)}, u32[]{:S(2)}) collective-permute-start(f32[448,128]{1,0:T(8,128)S(1)} %get-tuple-element.26), channel_id=1, source_target_pairs={{0,1},{1,0},{2,3},{3,2},{4,5},{5,4},{6,7},{7,6},{8,9},{9,8},{10,11... | collective-permute-start | bytes 688136 | tf_op jit(solution)/shard_map/ppermute | solution.py:35
  4.4 3.1 %collective-permute-start.1 = (f32[8,128]{1,0:T(8,128)S(1)}, f32[8,128]{1,0:T(8,128)S(1)}, u32[]{:S(2)}, u32[]{:S(2)}) collective-permute-start(f32[8,128]{1,0:T(8,128)S(1)} %shard_map.38), channel_id=1, source_target_pairs={{0,1},{1,0},{2,3},{3,2},{4,5},{5,4},{6,7},{7,6},{8,9},{9,8},{10,11... | collective-permute-start | bytes 12296 | tf_op jit(solution)/shard_map/ppermute | solution.py:35
  4.8 8.8 %collective-permute-start.8 = (f32[448,128]{1,0:T(8,128)S(1)}, f32[448,128]{1,0:T(8,128)S(1)}, u32[]{:S(2)}, u32[]{:S(2)}) collective-permute-start(f32[448,128]{1,0:T(8,128)S(1)} %add.38.refs_0_), channel_id=1, source_target_pairs={{0,2},{1,3},{2,0},{3,1},{4,6},{5,7},{6,4},{7,5},{8,10},{9,11},{10,... | collective-permute-start | bytes 688136 | tf_op jit(solution)/shard_map/ppermute | solution.py:35
  8.7 3.0 %collective-permute-start.5 = (f32[384,128]{1,0:T(8,128)S(1)}, f32[384,128]{1,0:T(8,128)S(1)}, u32[]{:S(2)}, u32[]{:S(2)}) collective-permute-start(f32[384,128]{1,0:T(8,128)S(1)} %get-tuple-element.28.refs_1_), channel_id=1, source_target_pairs={{0,1},{1,0},{2,3},{3,2},{4,5},{5,4},{6,7},{7,6},{8,9},{9,8},{10,11... | collective-permute-start | bytes 589832 | tf_op jit(solution)/shard_map/ppermute | solution.py:35
  11.2 7.5 %collective-permute-start.4 = (f32[576,128]{1,0:T(8,128)S(1)}, f32[576,128]{1,0:T(8,128)S(1)}, u32[]{:S(2)}, u32[]{:S(2)}) collective-permute-start(f32[576,128]{1,0:T(8,128)S(1)} %get-tuple-element.32), channel_id=1, source_target_pairs={{0,1},{1,0},{2,3},{3,2},{4,5},{5,4},{6,7},{7,6},{8,9},{9,8},{10,11... | collective-permute-start | bytes 884744 | tf_op jit(solution)/shard_map/ppermute | solution.py:35
  11.7 7.0 %collective-permute-start.6 = (f32[384,128]{1,0:T(8,128)S(1)}, f32[384,128]{1,0:T(8,128)S(1)}, u32[]{:S(2)}, u32[]{:S(2)}) collective-permute-start(f32[384,128]{1,0:T(8,128)S(1)} %add.40), channel_id=1, source_target_pairs={{0,2},{1,3},{2,0},{3,1},{4,6},{5,7},{6,4},{7,5},{8,10},{9,11},{10,... | collective-permute-start | bytes 589832 | tf_op jit(solution)/shard_map/ppermute | solution.py:35
  13.6 7.8 %collective-permute-start.9 = (f32[448,128]{1,0:T(8,128)S(1)}, f32[448,128]{1,0:T(8,128)S(1)}, u32[]{:S(2)}, u32[]{:S(2)}) collective-permute-start(f32[448,128]{1,0:T(8,128)S(1)} %add.43.own_ref.head_ref), channel_id=1, source_target_pairs={{0,4},{4,0},{8,12},{12,8},{16,20},{20,16},{24,28},{28,24},{1,5},{5... | collective-permute-start | bytes 688136 | tf_op jit(solution)/shard_map/ppermute | solution.py:35
  15.4 7.8 %collective-permute-start.10 = (f32[448,128]{1,0:T(8,128)S(1)}, f32[448,128]{1,0:T(8,128)S(1)}, u32[]{:S(2)}, u32[]{:S(2)}) collective-permute-start(f32[448,128]{1,0:T(8,128)S(1)} %add.43.own_ref.head_ref), channel_id=1, source_target_pairs={{0,1},{1,0},{2,3},{3,2},{4,5},{5,4},{6,7},{7,6},{8,9},{9,8},{10,11... | collective-permute-start | bytes 688136 | tf_op jit(solution)/shard_map/ppermute | solution.py:35
  15.4 6.1 %collective-permute-start.2 = (f32[320,128]{1,0:T(8,128)S(1)}, f32[320,128]{1,0:T(8,128)S(1)}, u32[]{:S(2)}, u32[]{:S(2)}) collective-permute-start(f32[320,128]{1,0:T(8,128)S(1)} %get-tuple-element.30), channel_id=1, source_target_pairs={{0,1},{1,0},{2,3},{3,2},{4,5},{5,4},{6,7},{7,6},{8,9},{9,8},{10,11... | collective-permute-start | bytes 491528 | tf_op jit(solution)/shard_map/ppermute | solution.py:35
  18.8 8.2 %collective-permute-start.7 = (f32[576,128]{1,0:T(8,128)S(1)}, f32[576,128]{1,0:T(8,128)S(1)}, u32[]{:S(2)}, u32[]{:S(2)}) collective-permute-start(f32[576,128]{1,0:T(8,128)S(1)} %shard_map.41), channel_id=1, source_target_pairs={{0,2},{1,3},{2,0},{3,1},{4,6},{5,7},{6,4},{7,5},{8,10},{9,11},{10,... | collective-permute-start | bytes 884744 | tf_op jit(solution)/shard_map/ppermute | solution.py:35
  19.9 5.9 %collective-permute-start.12 = (f32[384,128]{1,0:T(8,128)S(1)}, f32[384,128]{1,0:T(8,128)S(1)}, u32[]{:S(2)}, u32[]{:S(2)}) collective-permute-start(f32[384,128]{1,0:T(8,128)S(1)} %add.41.refs_0_.tail_ref.own_ref), channel_id=1, source_target_pairs={{0,4},{4,0},{8,12},{12,8},{16,20},{20,16},{24,28},{28,24},{1,5},{5... | collective-permute-start | bytes 589832 | tf_op jit(solution)/shard_map/ppermute | solution.py:35
  21.4 2.0 %collective-permute-start.11 = (f32[192,128]{1,0:T(8,128)S(1)}, f32[192,128]{1,0:T(8,128)S(1)}, u32[]{:S(2)}, u32[]{:S(2)}) collective-permute-start(f32[192,128]{1,0:T(8,128)S(1)} %slice.33), channel_id=1, source_target_pairs={{0,1},{1,0},{2,3},{3,2},{4,5},{5,4},{6,7},{7,6},{8,9},{9,8},{10,11... | collective-permute-start | bytes 294920 | tf_op jit(solution)/shard_map/ppermute | solution.py:35
  21.6 7.7 %collective-permute-start.3 = (f32[320,128]{1,0:T(8,128)S(1)}, f32[320,128]{1,0:T(8,128)S(1)}, u32[]{:S(2)}, u32[]{:S(2)}) collective-permute-start(f32[320,128]{1,0:T(8,128)S(1)} %add.39.first_ref), channel_id=1, source_target_pairs={{0,8},{4,12},{8,0},{12,4},{16,24},{20,28},{24,16},{28,20},{1,9},{5... | collective-permute-start | bytes 491528 | tf_op jit(solution)/shard_map/ppermute | solution.py:35
  23.2 7.3 %collective-permute-start.14 = (f32[256,128]{1,0:T(8,128)S(1)}, f32[256,128]{1,0:T(8,128)S(1)}, u32[]{:S(2)}, u32[]{:S(2)}) collective-permute-start(f32[256,128]{1,0:T(8,128)S(1)} %slice.35), channel_id=1, source_target_pairs={{0,1},{1,0},{2,3},{3,2},{4,5},{5,4},{6,7},{7,6},{8,9},{9,8},{10,11... | collective-permute-start | bytes 393224 | tf_op jit(solution)/shard_map/ppermute | solution.py:35
  27.1 5.7 %collective-permute-start.17 = (f32[192,128]{1,0:T(8,128)S(1)}, f32[192,128]{1,0:T(8,128)S(1)}, u32[]{:S(2)}, u32[]{:S(2)}) collective-permute-start(f32[192,128]{1,0:T(8,128)S(1)} %shard_map.44.refs_0_), channel_id=1, source_target_pairs={{0,4},{4,0},{8,12},{12,8},{16,20},{20,16},{24,28},{28,24},{1,5},{5... | collective-permute-start | bytes 294920 | tf_op jit(solution)/shard_map/ppermute | solution.py:35
  28.7 7.7 %collective-permute-start.21 = (f32[384,128]{1,0:T(8,128)S(1)}, f32[384,128]{1,0:T(8,128)S(1)}, u32[]{:S(2)}, u32[]{:S(2)}) collective-permute-start(f32[384,128]{1,0:T(8,128)S(1)} %shard_map.45.refs_0_), channel_id=1, source_target_pairs={{0,4},{4,0},{8,12},{12,8},{16,20},{20,16},{24,28},{28,24},{1,5},{5... | collective-permute-start | bytes 589832 | tf_op jit(solution)/shard_map/ppermute | solution.py:35
  29.3 7.9 %collective-permute-start.13 = (f32[320,128]{1,0:T(8,128)S(1)}, f32[320,128]{1,0:T(8,128)S(1)}, u32[]{:S(2)}, u32[]{:S(2)}) collective-permute-start(f32[320,128]{1,0:T(8,128)S(1)} %shard_map.46), channel_id=1, source_target_pairs={{0,2},{1,3},{2,0},{3,1},{4,6},{5,7},{6,4},{7,5},{8,10},{9,11},{10,... | collective-permute-start | bytes 491528 | tf_op jit(solution)/shard_map/ppermute | solution.py:35
  31.0 7.6 %collective-permute-start.15 = (f32[320,128]{1,0:T(8,128)S(1)}, f32[320,128]{1,0:T(8,128)S(1)}, u32[]{:S(2)}, u32[]{:S(2)}) collective-permute-start(f32[320,128]{1,0:T(8,128)S(1)} %shard_map.47), channel_id=1, source_target_pairs={{0,8},{4,12},{8,0},{12,4},{16,24},{20,28},{24,16},{28,20},{1,9},{5... | collective-permute-start | bytes 491528 | tf_op jit(solution)/shard_map/ppermute | solution.py:35
  32.8 5.8 %collective-permute-start.18 = (f32[192,128]{1,0:T(8,128)S(1)}, f32[192,128]{1,0:T(8,128)S(1)}, u32[]{:S(2)}, u32[]{:S(2)}) collective-permute-start(f32[192,128]{1,0:T(8,128)S(1)} %add.47.own_ref.p_own_ref), channel_id=1, source_target_pairs={{0,8},{4,12},{8,0},{12,4},{16,24},{20,28},{24,16},{28,20},{1,9},{5... | collective-permute-start | bytes 294920 | tf_op jit(solution)/shard_map/ppermute | solution.py:35
  34.5 6.4 %collective-permute-start.19 = (f32[192,128]{1,0:T(8,128)S(1)}, f32[192,128]{1,0:T(8,128)S(1)}, u32[]{:S(2)}, u32[]{:S(2)}) collective-permute-start(f32[192,128]{1,0:T(8,128)S(1)} %add.47.own_ref.p_own_ref), channel_id=1, source_target_pairs={{0,1},{1,0},{2,3},{3,2},{4,5},{5,4},{6,7},{7,6},{8,9},{9,8},{10,11... | collective-permute-start | bytes 294920 | tf_op jit(solution)/shard_map/ppermute | solution.py:35
  36.4 7.1 %collective-permute-start.22 = (f32[384,128]{1,0:T(8,128)S(1)}, f32[384,128]{1,0:T(8,128)S(1)}, u32[]{:S(2)}, u32[]{:S(2)}) collective-permute-start(f32[384,128]{1,0:T(8,128)S(1)} %add.48.own_ref), channel_id=1, source_target_pairs={{0,8},{4,12},{8,0},{12,4},{16,24},{20,28},{24,16},{28,20},{1,9},{5... | collective-permute-start | bytes 589832 | tf_op jit(solution)/shard_map/ppermute | solution.py:35
  37.2 6.3 %collective-permute-start.23 = (f32[256,128]{1,0:T(8,128)S(1)}, f32[256,128]{1,0:T(8,128)S(1)}, u32[]{:S(2)}, u32[]{:S(2)}) collective-permute-start(f32[256,128]{1,0:T(8,128)S(1)} %slice.36), channel_id=1, source_target_pairs={{0,1},{1,0},{2,3},{3,2},{4,5},{5,4},{6,7},{7,6},{8,9},{9,8},{10,11... | collective-permute-start | bytes 393224 | tf_op jit(solution)/shard_map/ppermute | solution.py:35
  38.6 2.4 %collective-permute-start.20 = (f32[192,128]{1,0:T(8,128)S(1)}, f32[192,128]{1,0:T(8,128)S(1)}, u32[]{:S(2)}, u32[]{:S(2)}) collective-permute-start(f32[192,128]{1,0:T(8,128)S(1)} %collective-permute-done.18.sib_ref), channel_id=1, source_target_pairs={{0,1},{1,0},{2,3},{3,2},{4,5},{5,4},{6,7},{7,6},{8,9},{9,8},{10,11... | collective-permute-start | bytes 294920 | tf_op jit(solution)/shard_map/ppermute | solution.py:35
  38.6 7.8 %collective-permute-start.16 = (f32[320,128]{1,0:T(8,128)S(1)}, f32[320,128]{1,0:T(8,128)S(1)}, u32[]{:S(2)}, u32[]{:S(2)}) collective-permute-start(f32[320,128]{1,0:T(8,128)S(1)} %add_subtract_fusion.1), channel_id=1, source_target_pairs={{0,4},{4,0},{8,12},{12,8},{16,20},{20,16},{24,28},{28,24},{1,5},{5... | collective-permute-start | bytes 491528 | tf_op jit(solution)/shard_map/ppermute | solution.py:35
  44.7 1.4 %collective-permute-start.24 = (f32[256,128]{1,0:T(8,128)S(1)}, f32[256,128]{1,0:T(8,128)S(1)}, u32[]{:S(2)}, u32[]{:S(2)}) collective-permute-start(f32[256,128]{1,0:T(8,128)S(1)} %get-tuple-element.40.sib_ref), channel_id=1, source_target_pairs={{0,1},{1,0},{2,3},{3,2},{4,5},{5,4},{6,7},{7,6},{8,9},{9,8},{10,11... | collective-permute-start | bytes 393224 | tf_op jit(solution)/shard_map/ppermute | solution.py:35
  45.0 4.5 %collective-permute-start.28 = (f32[640,128]{1,0:T(8,128)S(1)}, f32[640,128]{1,0:T(8,128)S(1)}, u32[]{:S(2)}, u32[]{:S(2)}) collective-permute-start(f32[640,128]{1,0:T(8,128)S(1)} %get-tuple-element.37.z_ref.z0_ref), channel_id=1, source_target_pairs={{0,1},{1,0},{2,3},{3,2},{4,5},{5,4},{6,7},{7,6},{8,9},{9,8},{10,11... | collective-permute-start | bytes 983048 | tf_op jit(solution)/shard_map/ppermute | solution.py:35
  46.6 2.9 %collective-permute-start.27 = (f32[384,128]{1,0:T(8,128)S(1)}, f32[384,128]{1,0:T(8,128)S(1)}, u32[]{:S(2)}, u32[]{:S(2)}) collective-permute-start(f32[384,128]{1,0:T(8,128)S(1)} %shard_map.51), channel_id=1, source_target_pairs={{0,1},{1,0},{2,3},{3,2},{4,5},{5,4},{6,7},{7,6},{8,9},{9,8},{10,11... | collective-permute-start | bytes 589832 | tf_op jit(solution)/shard_map/ppermute | solution.py:35
  46.8 10.8 %collective-permute-start.26 = (f32[320,128]{1,0:T(8,128)S(1)}, f32[320,128]{1,0:T(8,128)S(1)}, u32[]{:S(2)}, u32[]{:S(2)}) collective-permute-start(f32[320,128]{1,0:T(8,128)S(1)} %add_subtract_fusion.refs_0_.own_ref), channel_id=1, source_target_pairs={{0,16},{4,20},{8,24},{12,28},{16,0},{20,4},{24,8},{28,12},{1,17},{... | collective-permute-start | bytes 491528 | tf_op jit(solution)/shard_map/ppermute | solution.py:35
  49.4 8.3 %collective-permute-start.25 = (f32[320,128]{1,0:T(8,128)S(1)}, f32[320,128]{1,0:T(8,128)S(1)}, u32[]{:S(2)}, u32[]{:S(2)}) collective-permute-start(f32[320,128]{1,0:T(8,128)S(1)} %add_subtract_fusion.refs_0_.own_ref), channel_id=1, source_target_pairs={{0,1},{1,0},{2,3},{3,2},{4,5},{5,4},{6,7},{7,6},{8,9},{9,8},{10,11... | collective-permute-start | bytes 491528 | tf_op jit(solution)/shard_map/ppermute | solution.py:35
  57.7 1.5 %collective-permute-start.29 = (f32[320,128]{1,0:T(8,128)S(1)}, f32[320,128]{1,0:T(8,128)S(1)}, u32[]{:S(2)}, u32[]{:S(2)}) collective-permute-start(f32[320,128]{1,0:T(8,128)S(1)} %shard_map.53.sib_ref), channel_id=1, source_target_pairs={{0,1},{1,0},{2,3},{3,2},{4,5},{5,4},{6,7},{7,6},{8,9},{9,8},{10,11... | collective-permute-start | bytes 491528 | tf_op jit(solution)/shard_map/ppermute | solution.py:35

commit v12 on v11

--- a/solution.py
+++ b/solution.py
@@ -238,15 +238,20 @@
     return jnp.where(row == col, 1.0, 0.0)
 
 
+def doubled(power, values):
+    both = dot(power, jnp.concatenate([power, values], axis=1))
+    return both[:, :RANK], values + both[:, RANK:]
+
+
 def series(start, values, power_ref, sum_ref):
-    norm = square_norm(start)
     if values is None:
-        power_ref[...] = dot(start, start)
-        sum_ref[...] = identity() + start
+        power, values = dot(start, start), identity() + start
     else:
-        both = dot(start, jnp.concatenate([start, values], axis=1))
-        power_ref[...] = both[:, :RANK]
-        sum_ref[...] = values + both[:, RANK:]
+        power, values = doubled(start, values)
+    for _ in range(2):
+        power, values = doubled(power, values)
+    norm = square_norm(power)
+    power_ref[...], sum_ref[...] = doubled(power, values)
 
     def proceed(state):
         count, bound = state
@@ -254,12 +259,8 @@
 
     def body(state):
         count, _ = state
-        power = power_ref[...]
-        bound = square_norm(power)
-        values = sum_ref[...]
-        both = dot(power, jnp.concatenate([power, values], axis=1))
-        power_ref[...] = both[:, :RANK]
-        sum_ref[...] = values + both[:, RANK:]
+        bound = square_norm(power_ref[...])
+        power_ref[...], sum_ref[...] = doubled(power_ref[...], sum_ref[...])
         return count + 1, bound
 
     return lax.while_loop(proceed, body, (jnp.int32(0), norm))[1]
@@ -332,11 +333,9 @@
 
 
 def middle_kernel(
-    core_ref, inverse_ref, p_sib_ref, own_ref, sib_ref, own_other_ref, p_own_ref, p_own_other_ref, z_ref, z_sib_ref, out_ref,
-    crossed_ref,
+    core_ref, inverse_ref, p_sib_ref, own_ref, sib_ref, own_other_ref, p_own_ref, p_own_other_ref, z_ref, z_sib_ref, out_ref
 ):
     core = core_ref[0]
-    crossed_ref[...] = sib_ref[:RANK, :]
     own = unpack(own_ref)
     z = dot(inverse_ref[...], unpack(sib_ref) - dot(p_sib_ref[...], own))
     store(z_ref, z)
@@ -457,11 +456,12 @@
     r_own_other = swap(r_own[:RANK], "sub", 0)
     p_sib_other = swap(p_sib, "sub", 0)
     inverted, p_sib = inverse(INVERT_SECOND, core, p_own, p_sib, p_own_other, p_sib_other)
-    z1, z_sib, crossed, r_sib = call(
-        middle_kernel, [struct(RANK + HALF), struct(RANK + HALF), struct(last), struct(RANK)], MIDDLE_FLOPS,
+    cross_sib = call(keep_kernel, struct(RANK), 0, core, r_sib[:RANK], after=(inverted,))
+    z1, z_sib, crossed = call(
+        middle_kernel, [struct(RANK + HALF), struct(RANK + HALF), struct(last)], MIDDLE_FLOPS,
         core, inverted, p_sib, r_own, r_sib, r_own_other, p_own, p_own_other,
     )
-    crossed = call(cross_kernel, struct(last), CROSS_FLOPS, core, r_sib, swap(r_sib, "sub", 0), z_sib, crossed)
+    crossed = call(cross_kernel, struct(last), CROSS_FLOPS, core, cross_sib, swap(cross_sib, "sub", 0), z_sib, crossed)
 
     own = third - crossed
     sib = swap(own, "rows", span_bits + 2)

time: 62.9 us -> 61.9 us (0.984)
    pallas_call x13 -> x14, Pallas kernels: 9.12 us -> 9.04 us  [call(): pl.pallas_call(kernel, in_specs=[SMEM] + [VMEM] * (len(values) - 1) + [AN...]
  transfers between devices with their start and end apart: 30 -> 30, of which waited for: 9 -> 9; matrix products, arithmetic and copies ran while one was open for 0% -> 1% of each run, Pallas kernels for 22% -> 22%
where the time goes in v12:
time: 61.9 us; the launch traced here: 61.8 us
  starting transfers between devices  25.7 us (42%)
  Pallas kernels  19.7 us (32%)
  waiting for transfers between devices  15.8 us (26%)
    ppermute x30, starting transfers between devices, swap(): return lax.ppermute(value, axis, pairs)  25.7 us
    ppermute x30, waiting for transfers between devices, swap(): return lax.ppermute(value, axis, pairs)  15.8 us
    pallas_call x14, Pallas kernels, call(): pl.pallas_call(kernel, in_specs=[SMEM] + [VMEM] * (len(values) - 1) + [AN...  9.04 us
    pallas_call x3, Pallas kernels, products(): pl.pallas_call(functools.partial(product_kernel, groups, chunks), in_spec...  6.24 us
    pallas_call x2, Pallas kernels, inverse(): pl.pallas_call(invert_kernel, in_specs=[SMEM] + [VMEM] * 4, out_specs=[VM...  4.39 us
  transfers between devices with their start and end apart: 30, of which 9 were waited for; matrix products, arithmetic and copies ran while one was open for 1% of the time, Pallas kernels for 22%

profile of v12, /device:TPU:0, one launch (start us, length us, event | category | flops | bytes accessed | tf_op | source)
XLA Modules:
  0.0 61.8 jit_solution(15548831239703171612)
XLA Ops:
  0.0 2.7 %shard_map.37 = (f32[448,128]{1,0:T(8,128)S(1)}, f32[448,128]{1,0:T(8,128)S(1)}) custom-call(s32[1]{0:T(128)} %bitcast.core_ref, f32[3,1024,256]{2,1,0:T(8,128)} %gens_ref.5, f32[3,1024,256]{2,1,0:T(8,128)} %solved_ref.7), custom_call_target="tpu_custom_call" | custom-call | flops 805306368 | bytes 3145728 | tf_op jit(solution)/shard_map/pallas_call | solution.py:220
  2.7 0.5 collective-permute-start
  3.2 1.1 %collective-permute-done = f32[448,128]{1,0:T(8,128)S(1)} collective-permute-done((f32[448,128]{1,0:T(8,128)S(1)}, f32[448,128]{1,0:T(8,128)S(1)}, u32[]{:S(2)}, u32[]{:S(2)}) %collective-permute-start) | collective-permute-done | bytes 229408 | tf_op jit(solution)/shard_map/ppermute | solution.py:35
  4.4 0.4 collective-permute-start.1
  4.8 2.7 %collective-permute-start.8 = (f32[448,128]{1,0:T(8,128)S(1)}, f32[448,128]{1,0:T(8,128)S(1)}, u32[]{:S(2)}, u32[]{:S(2)}) collective-permute-start(f32[448,128]{1,0:T(8,128)S(1)} %add.38.refs_0_), channel_id=1, source_target_pairs={{0,2},{1,3},{2,0},{3,1},{4,6},{5,7},{6,4},{7,5},{8,10},{9,11},{10,... | collective-permute-start | bytes 688136 | tf_op jit(solution)/shard_map/ppermute | solution.py:35
  7.5 0.0 collective-permute-done.1.refs_1_
  7.5 1.2 %shard_map.39 = (f32[384,128]{1,0:T(8,128)S(1)}, f32[384,128]{1,0:T(8,128)S(1)}) custom-call(s32[1]{0:T(128)} %bitcast.core_ref, f32[3,1024,256]{2,1,0:T(8,128)S(1)} %copy-done.1, f32[3,1024,256]{2,1,0:T(8,128)S(1)} %copy-done, f32[1024,128]{1,0:T(8,128)S(1)} %copy-done.2, f32[8,128]{1,0:T(8,128)S(1)} %collective-permute-done.1.refs_1_), custom_call_target="tpu_custom_call" | custom-call | flops 603979776 | bytes 2621440 | tf_op jit(solution)/shard_map/pallas_call | solution.py:220
  8.7 0.1 collective-permute-start.5
  8.8 2.4 %shard_map.40 = (f32[576,128]{1,0:T(8,128)S(1)}, f32[576,128]{1,0:T(8,128)S(1)}, f32[320,128]{1,0:T(8,128)S(1)}, f32[320,128]{1,0:T(8,128)S(1)}) custom-call(s32[1]{0:T(128)} %bitcast.core_ref, f32[3,1024,256]{2,1,0:T(8,128)S(1)} %copy-done.1, f32[3,1024,256]{2,1,0:T(8,128)S(1)} %copy-done, f32[1024,128]{1,0:T(8,128)S(1)} %copy-done.2, ...), custom_call_target="tpu_custom_call" | custom-call | flops 1610612736 | bytes 4718592 | tf_op jit(solution)/shard_map/pallas_call | solution.py:220
  11.2 0.5 collective-permute-start.4
  11.7 0.0 collective-permute-done.5
  11.7 1.1 %collective-permute-start.6 = (f32[384,128]{1,0:T(8,128)S(1)}, f32[384,128]{1,0:T(8,128)S(1)}, u32[]{:S(2)}, u32[]{:S(2)}) collective-permute-start(f32[384,128]{1,0:T(8,128)S(1)} %add.40), channel_id=1, source_target_pairs={{0,2},{1,3},{2,0},{3,1},{4,6},{5,7},{6,4},{7,5},{8,10},{9,11},{10,... | collective-permute-start | bytes 589832 | tf_op jit(solution)/shard_map/ppermute | solution.py:35
  12.8 0.8 %collective-permute-done.8 = f32[448,128]{1,0:T(8,128)S(1)} collective-permute-done((f32[448,128]{1,0:T(8,128)S(1)}, f32[448,128]{1,0:T(8,128)S(1)}, u32[]{:S(2)}, u32[]{:S(2)}) %collective-permute-start.8) | collective-permute-done | bytes 229408 | tf_op jit(solution)/shard_map/ppermute | solution.py:35
  13.6 1.8 %collective-permute-start.9 = (f32[448,128]{1,0:T(8,128)S(1)}, f32[448,128]{1,0:T(8,128)S(1)}, u32[]{:S(2)}, u32[]{:S(2)}) collective-permute-start(f32[448,128]{1,0:T(8,128)S(1)} %add.43.own_ref.head_ref), channel_id=1, source_target_pairs={{0,4},{4,0},{8,12},{12,8},{16,20},{20,16},{24,28},{28,24},{1,5},{5... | collective-permute-start | bytes 688136 | tf_op jit(solution)/shard_map/ppermute | solution.py:35
  15.4 0.0 collective-permute-start.10
  15.4 0.5 collective-permute-start.2
  15.9 2.8 %collective-permute-done.6 = f32[384,128]{1,0:T(8,128)S(1)} collective-permute-done((f32[384,128]{1,0:T(8,128)S(1)}, f32[384,128]{1,0:T(8,128)S(1)}, u32[]{:S(2)}, u32[]{:S(2)}) %collective-permute-start.6) | collective-permute-done | bytes 196640 | tf_op jit(solution)/shard_map/ppermute | solution.py:35
  18.7 0.0 collective-permute-done.4.second_ref
  18.8 1.2 %collective-permute-start.7 = (f32[576,128]{1,0:T(8,128)S(1)}, f32[576,128]{1,0:T(8,128)S(1)}, u32[]{:S(2)}, u32[]{:S(2)}) collective-permute-start(f32[576,128]{1,0:T(8,128)S(1)} %shard_map.41), channel_id=1, source_target_pairs={{0,2},{1,3},{2,0},{3,1},{4,6},{5,7},{6,4},{7,5},{8,10},{9,11},{10,... | collective-permute-start | bytes 884744 | tf_op jit(solution)/shard_map/ppermute | solution.py:35
  19.9 1.5 %collective-permute-start.12 = (f32[384,128]{1,0:T(8,128)S(1)}, f32[384,128]{1,0:T(8,128)S(1)}, u32[]{:S(2)}, u32[]{:S(2)}) collective-permute-start(f32[384,128]{1,0:T(8,128)S(1)} %add.41.refs_0_.tail_ref.own_ref), channel_id=1, source_target_pairs={{0,4},{4,0},{8,12},{12,8},{16,20},{20,16},{24,28},{28,24},{1,5},{5... | collective-permute-start | bytes 589832 | tf_op jit(solution)/shard_map/ppermute | solution.py:35
  21.4 0.0 collective-permute-done.9.sib_ref.head_sib_ref
  21.4 0.1 collective-permute-start.11
  21.5 0.0 collective-permute-done.2
  21.6 1.6 %collective-permute-start.3 = (f32[320,128]{1,0:T(8,128)S(1)}, f32[320,128]{1,0:T(8,128)S(1)}, u32[]{:S(2)}, u32[]{:S(2)}) collective-permute-start(f32[320,128]{1,0:T(8,128)S(1)} %add.39.first_ref), channel_id=1, source_target_pairs={{0,8},{4,12},{8,0},{12,4},{16,24},{20,28},{24,16},{28,20},{1,9},{5... | collective-permute-start | bytes 491528 | tf_op jit(solution)/shard_map/ppermute | solution.py:35
  23.2 0.0 collective-permute-done.10.own_other_ref.head_other_ref
  23.2 0.3 collective-permute-start.14
  23.5 0.0 collective-permute-done.11.sib_other_ref
  23.5 2.1 %shard_map.42 = (f32[256,256]{1,0:T(8,128)S(1)}, f32[256,256]{1,0:T(8,128)S(1)}) custom-call(s32[1]{0:T(128)} %bitcast.core_ref, f32[448,128]{1,0:T(8,128)S(1)} %add.43.own_ref.head_ref, f32[448,128]{1,0:T(8,128)S(1)} %collective-permute-done.9.sib_ref.head_sib_ref, f32[448,128]{1,0:T(8,128)S(1)} %collective-permute-done.10.own_other_ref.head_other_ref, ...), custom_call_target="tpu_custom_call" | custom-call | flops 900000000 | tf_op jit(solution)/shard_map/pallas_call | solution.py:302
  25.6 0.2 collective-permute-done.12.tail_sib_ref
  25.8 1.1 %shard_map.43 = (f32[640,128]{1,0:T(8,128)S(1)}, f32[576,128]{1,0:T(8,128)S(1)}) custom-call(s32[1]{0:T(128)} %bitcast.core_ref, f32[256,256]{1,0:T(8,128)S(1)} %get-tuple-element.33.inverse_ref, f32[256,256]{1,0:T(8,128)S(1)} %get-tuple-element.34.p_sib_ref, f32[448,128]{1,0:T(8,128)S(1)} %add.43.own_ref.head_ref, ...), custom_call_target="tpu_custom_call" | custom-call | flops 650000000 | bytes 2228228 | tf_op jit(solution)/shard_map/pallas_call | solution.py:290
  27.0 0.0 collective-permute-done.7
  27.1 1.6 %collective-permute-start.19 = (f32[192,128]{1,0:T(8,128)S(1)}, f32[192,128]{1,0:T(8,128)S(1)}, u32[]{:S(2)}, u32[]{:S(2)}) collective-permute-start(f32[192,128]{1,0:T(8,128)S(1)} %shard_map.44.refs_0_), channel_id=1, source_target_pairs={{0,4},{4,0},{8,12},{12,8},{16,20},{20,16},{24,28},{28,24},{1,5},{5... | collective-permute-start | bytes 294920 | tf_op jit(solution)/shard_map/ppermute | solution.py:35
  28.7 0.6 collective-permute-start.17
  29.3 0.0 collective-permute-done.3.second_ref
  29.3 1.3 %collective-permute-start.13 = (f32[320,128]{1,0:T(8,128)S(1)}, f32[320,128]{1,0:T(8,128)S(1)}, u32[]{:S(2)}, u32[]{:S(2)}) collective-permute-start(f32[320,128]{1,0:T(8,128)S(1)} %shard_map.46), channel_id=1, source_target_pairs={{0,2},{1,3},{2,0},{3,1},{4,6},{5,7},{6,4},{7,5},{8,10},{9,11},{10,... | collective-permute-start | bytes 491528 | tf_op jit(solution)/shard_map/ppermute | solution.py:35
  30.6 0.0 collective-permute-done.14.own_other_ref
  30.6 0.4 shard_map.47
  31.0 1.6 %collective-permute-start.15 = (f32[320,128]{1,0:T(8,128)S(1)}, f32[320,128]{1,0:T(8,128)S(1)}, u32[]{:S(2)}, u32[]{:S(2)}) collective-permute-start(f32[320,128]{1,0:T(8,128)S(1)} %shard_map.47), channel_id=1, source_target_pairs={{0,8},{4,12},{8,0},{12,4},{16,24},{20,28},{24,16},{28,20},{1,9},{5... | collective-permute-start | bytes 491528 | tf_op jit(solution)/shard_map/ppermute | solution.py:35
  32.6 0.2 collective-permute-done.19
  32.8 1.7 %collective-permute-start.20 = (f32[192,128]{1,0:T(8,128)S(1)}, f32[192,128]{1,0:T(8,128)S(1)}, u32[]{:S(2)}, u32[]{:S(2)}) collective-permute-start(f32[192,128]{1,0:T(8,128)S(1)} %add.48.own_ref.p_own_ref), channel_id=1, source_target_pairs={{0,8},{4,12},{8,0},{12,4},{16,24},{20,28},{24,16},{28,20},{1,9},{5... | collective-permute-start | bytes 294920 | tf_op jit(solution)/shard_map/ppermute | solution.py:35
  34.5 0.0 collective-permute-start.21
  34.6 1.6 %collective-permute-done.17 = f32[384,128]{1,0:T(8,128)S(1)} collective-permute-done((f32[384,128]{1,0:T(8,128)S(1)}, f32[384,128]{1,0:T(8,128)S(1)}, u32[]{:S(2)}, u32[]{:S(2)}) %collective-permute-start.17) | collective-permute-done | bytes 196640 | tf_op jit(solution)/shard_map/ppermute | solution.py:35
  36.2 0.8 %collective-permute-start.18 = (f32[384,128]{1,0:T(8,128)S(1)}, f32[384,128]{1,0:T(8,128)S(1)}, u32[]{:S(2)}, u32[]{:S(2)}) collective-permute-start(f32[384,128]{1,0:T(8,128)S(1)} %add.47.own_ref), channel_id=1, source_target_pairs={{0,8},{4,12},{8,0},{12,4},{16,24},{20,28},{24,16},{28,20},{1,9},{5... | collective-permute-start | bytes 589832 | tf_op jit(solution)/shard_map/ppermute | solution.py:35
  37.0 1.7 %collective-permute-done.20.sib_ref = f32[192,128]{1,0:T(8,128)S(1)} collective-permute-done((f32[192,128]{1,0:T(8,128)S(1)}, f32[192,128]{1,0:T(8,128)S(1)}, u32[]{:S(2)}, u32[]{:S(2)}) %collective-permute-start.20) | collective-permute-done | bytes 98336 | tf_op jit(solution)/shard_map/ppermute | solution.py:35
  38.8 2.0 %collective-permute-start.16 = (f32[320,128]{1,0:T(8,128)S(1)}, f32[320,128]{1,0:T(8,128)S(1)}, u32[]{:S(2)}, u32[]{:S(2)}) collective-permute-start(f32[320,128]{1,0:T(8,128)S(1)} %add_subtract_fusion.1), channel_id=1, source_target_pairs={{0,4},{4,0},{8,12},{12,8},{16,20},{20,16},{24,28},{28,24},{1,5},{5... | collective-permute-start | bytes 491528 | tf_op jit(solution)/shard_map/ppermute | solution.py:35
  40.8 0.3 collective-permute-start.24
  41.0 2.3 %shard_map.48 = (f32[256,256]{1,0:T(8,128)S(1)}, f32[256,256]{1,0:T(8,128)S(1)}) custom-call(s32[1]{0:T(128)} %bitcast.core_ref, f32[192,128]{1,0:T(8,128)S(1)} %add.48.own_ref.p_own_ref, f32[192,128]{1,0:T(8,128)S(1)} %collective-permute-done.20.sib_ref, f32[192,128]{1,0:T(8,128)S(1)} %collective-permute-done.21.own_other_ref.p_own_other_ref, ...), custom_call_target="tpu_custom_call" | custom-call | flops 900000000 | tf_op jit(solution)/shard_map/pallas_call | solution.py:302
  43.3 0.0 collective-permute-done.18.sib_ref
  43.4 0.4 collective-permute-start.23
  43.7 0.2 collective-permute-start.28
  44.0 1.2 %shard_map.50 = (f32[384,128]{1,0:T(8,128)S(1)}, f32[384,128]{1,0:T(8,128)S(1)}, f32[320,128]{1,0:T(8,128)S(1)}) custom-call(s32[1]{0:T(128)} %bitcast.core_ref, f32[256,256]{1,0:T(8,128)S(1)} %get-tuple-element.37.refs_0_.inverse_ref, f32[256,256]{1,0:T(8,128)S(1)} %get-tuple-element.38.p_sib_ref, f32[384,128]{1,0:T(8,128)S(1)} %add.47.own_ref, ...), custom_call_target="tpu_custom_call" | custom-call | bytes 1802244 | tf_op jit(solution)/shard_map/pallas_call | solution.py:290
  45.1 0.0 collective-permute-done.23.sib_other_ref
  45.2 0.4 shard_map.51
  45.6 0.0 collective-permute-done.16
  45.7 0.3 collective-permute-start.27
  46.0 2.6 %collective-permute-start.26 = (f32[320,128]{1,0:T(8,128)S(1)}, f32[320,128]{1,0:T(8,128)S(1)}, u32[]{:S(2)}, u32[]{:S(2)}) collective-permute-start(f32[320,128]{1,0:T(8,128)S(1)} %add_subtract_fusion.refs_0_.own_ref), channel_id=1, source_target_pairs={{0,16},{4,20},{8,24},{12,28},{16,0},{20,4},{24,8},{28,12},{1,17},{... | collective-permute-start | bytes 491528 | tf_op jit(solution)/shard_map/ppermute | solution.py:35
  48.6 0.0 collective-permute-start.25
  48.6 0.0 collective-permute-done.28.z0_other_ref
  48.6 0.0 collective-permute-done.27.z1_other_ref
  48.6 2.2 %shard_map.53 = (bf16[1024,256]{1,0:T(8,128)(2,1)S(1)}, bf16[1024,256]{1,0:T(8,128)(2,1)S(1)}, f32[1024,128]{1,0:T(8,128)S(1)}) custom-call(s32[1]{0:T(128)} %bitcast.core_ref, f32[384,128]{1,0:T(8,128)S(1)} %get-tuple-element.41.value_ref.z1_ref, f32[384,128]{1,0:T(8,128)S(1)} %collective-permute-done.27.z1_other_ref, ...), custom_call_target="tpu_custom_call" | custom-call | flops 1207959552 | bytes 7340036 | tf_op jit(solution)/shard_map/pallas_call | solution.py:290
  50.8 5.9 %collective-permute-done.26.value_ref = f32[320,128]{1,0:T(8,128)S(1)} collective-permute-done((f32[320,128]{1,0:T(8,128)S(1)}, f32[320,128]{1,0:T(8,128)S(1)}, u32[]{:S(2)}, u32[]{:S(2)}) %collective-permute-start.26) | collective-permute-done | bytes 163872 | tf_op jit(solution)/shard_map/ppermute | solution.py:35
  56.8 0.1 collective-permute-start.29
  56.9 1.4 %collective-permute-done.29.sib_other_ref = f32[320,128]{1,0:T(8,128)S(1)} collective-permute-done((f32[320,128]{1,0:T(8,128)S(1)}, f32[320,128]{1,0:T(8,128)S(1)}, u32[]{:S(2)}, u32[]{:S(2)}) %collective-permute-start.29) | collective-permute-done | bytes 163872 | tf_op jit(solution)/shard_map/ppermute | solution.py:35
  58.2 3.6 %shard_map.55 = f32[1024,128]{1,0:T(8,128)} custom-call(s32[1]{0:T(128)} %bitcast.core_ref, f32[320,128]{1,0:T(8,128)S(1)} %add_subtract_fusion.refs_0_.own_ref, f32[320,128]{1,0:T(8,128)S(1)} %collective-permute-done.25.own_other_ref, f32[320,128]{1,0:T(8,128)S(1)} %shard_map.54.sib_ref, f32[320,128]{1,0:T(8,128)S(1)} %collective-permute-done.29.sib_other_ref, ...), custom_call_target="tpu_custom_call" | custom-call | flops 1107296256 | bytes 3801092 | tf_op jit(solution)/shard_map/pallas_call | solution.py:290
  (40 shorter events, 0.5 us)
Async XLA Ops:
  0.0 7.5 %copy-start = (f32[3,1024,256]{2,1,0:T(8,128)S(1)}, f32[3,1024,256]{2,1,0:T(8,128)}, u32[]{:S(2)}) copy-start(f32[3,1024,256]{2,1,0:T(8,128)} %solved_ref.7) | copy-start | bytes 9437188
  0.0 7.5 %copy-start.1 = (f32[3,1024,256]{2,1,0:T(8,128)S(1)}, f32[3,1024,256]{2,1,0:T(8,128)}, u32[]{:S(2)}) copy-start(f32[3,1024,256]{2,1,0:T(8,128)} %gens_ref.5) | copy-start | bytes 9437188
  0.0 7.5 %copy-start.2 = (f32[1024,128]{1,0:T(8,128)S(1)}, f32[1024,128]{1,0:T(8,128)}, u32[]{:S(2)}) copy-start(f32[1024,128]{1,0:T(8,128)} %rhs_ref.1) | copy-start | bytes 1572868
  2.7 1.6 %collective-permute-start = (f32[448,128]{1,0:T(8,128)S(1)}, f32[448,128]{1,0:T(8,128)S(1)}, u32[]{:S(2)}, u32[]{:S(2)}) collective-permute-start(f32[448,128]{1,0:T(8,128)S(1)} %get-tuple-element.25), channel_id=1, source_target_pairs={{0,1},{1,0},{2,3},{3,2},{4,5},{5,4},{6,7},{7,6},{8,9},{9,8},{10,11... | collective-permute-start | bytes 688136 | tf_op jit(solution)/shard_map/ppermute | solution.py:35
  4.4 3.1 %collective-permute-start.1 = (f32[8,128]{1,0:T(8,128)S(1)}, f32[8,128]{1,0:T(8,128)S(1)}, u32[]{:S(2)}, u32[]{:S(2)}) collective-permute-start(f32[8,128]{1,0:T(8,128)S(1)} %shard_map.38), channel_id=1, source_target_pairs={{0,1},{1,0},{2,3},{3,2},{4,5},{5,4},{6,7},{7,6},{8,9},{9,8},{10,11... | collective-permute-start | bytes 12296 | tf_op jit(solution)/shard_map/ppermute | solution.py:35
  4.8 8.8 %collective-permute-start.8 = (f32[448,128]{1,0:T(8,128)S(1)}, f32[448,128]{1,0:T(8,128)S(1)}, u32[]{:S(2)}, u32[]{:S(2)}) collective-permute-start(f32[448,128]{1,0:T(8,128)S(1)} %add.38.refs_0_), channel_id=1, source_target_pairs={{0,2},{1,3},{2,0},{3,1},{4,6},{5,7},{6,4},{7,5},{8,10},{9,11},{10,... | collective-permute-start | bytes 688136 | tf_op jit(solution)/shard_map/ppermute | solution.py:35
  8.7 3.0 %collective-permute-start.5 = (f32[384,128]{1,0:T(8,128)S(1)}, f32[384,128]{1,0:T(8,128)S(1)}, u32[]{:S(2)}, u32[]{:S(2)}) collective-permute-start(f32[384,128]{1,0:T(8,128)S(1)} %get-tuple-element.27.refs_1_), channel_id=1, source_target_pairs={{0,1},{1,0},{2,3},{3,2},{4,5},{5,4},{6,7},{7,6},{8,9},{9,8},{10,11... | collective-permute-start | bytes 589832 | tf_op jit(solution)/shard_map/ppermute | solution.py:35
  11.2 7.5 %collective-permute-start.4 = (f32[576,128]{1,0:T(8,128)S(1)}, f32[576,128]{1,0:T(8,128)S(1)}, u32[]{:S(2)}, u32[]{:S(2)}) collective-permute-start(f32[576,128]{1,0:T(8,128)S(1)} %get-tuple-element.31), channel_id=1, source_target_pairs={{0,1},{1,0},{2,3},{3,2},{4,5},{5,4},{6,7},{7,6},{8,9},{9,8},{10,11... | collective-permute-start | bytes 884744 | tf_op jit(solution)/shard_map/ppermute | solution.py:35
  11.7 7.0 %collective-permute-start.6 = (f32[384,128]{1,0:T(8,128)S(1)}, f32[384,128]{1,0:T(8,128)S(1)}, u32[]{:S(2)}, u32[]{:S(2)}) collective-permute-start(f32[384,128]{1,0:T(8,128)S(1)} %add.40), channel_id=1, source_target_pairs={{0,2},{1,3},{2,0},{3,1},{4,6},{5,7},{6,4},{7,5},{8,10},{9,11},{10,... | collective-permute-start | bytes 589832 | tf_op jit(solution)/shard_map/ppermute | solution.py:35
  13.6 7.8 %collective-permute-start.9 = (f32[448,128]{1,0:T(8,128)S(1)}, f32[448,128]{1,0:T(8,128)S(1)}, u32[]{:S(2)}, u32[]{:S(2)}) collective-permute-start(f32[448,128]{1,0:T(8,128)S(1)} %add.43.own_ref.head_ref), channel_id=1, source_target_pairs={{0,4},{4,0},{8,12},{12,8},{16,20},{20,16},{24,28},{28,24},{1,5},{5... | collective-permute-start | bytes 688136 | tf_op jit(solution)/shard_map/ppermute | solution.py:35
  15.4 7.8 %collective-permute-start.10 = (f32[448,128]{1,0:T(8,128)S(1)}, f32[448,128]{1,0:T(8,128)S(1)}, u32[]{:S(2)}, u32[]{:S(2)}) collective-permute-start(f32[448,128]{1,0:T(8,128)S(1)} %add.43.own_ref.head_ref), channel_id=1, source_target_pairs={{0,1},{1,0},{2,3},{3,2},{4,5},{5,4},{6,7},{7,6},{8,9},{9,8},{10,11... | collective-permute-start | bytes 688136 | tf_op jit(solution)/shard_map/ppermute | solution.py:35
  15.4 6.1 %collective-permute-start.2 = (f32[320,128]{1,0:T(8,128)S(1)}, f32[320,128]{1,0:T(8,128)S(1)}, u32[]{:S(2)}, u32[]{:S(2)}) collective-permute-start(f32[320,128]{1,0:T(8,128)S(1)} %get-tuple-element.29), channel_id=1, source_target_pairs={{0,1},{1,0},{2,3},{3,2},{4,5},{5,4},{6,7},{7,6},{8,9},{9,8},{10,11... | collective-permute-start | bytes 491528 | tf_op jit(solution)/shard_map/ppermute | solution.py:35
  18.8 8.2 %collective-permute-start.7 = (f32[576,128]{1,0:T(8,128)S(1)}, f32[576,128]{1,0:T(8,128)S(1)}, u32[]{:S(2)}, u32[]{:S(2)}) collective-permute-start(f32[576,128]{1,0:T(8,128)S(1)} %shard_map.41), channel_id=1, source_target_pairs={{0,2},{1,3},{2,0},{3,1},{4,6},{5,7},{6,4},{7,5},{8,10},{9,11},{10,... | collective-permute-start | bytes 884744 | tf_op jit(solution)/shard_map/ppermute | solution.py:35
  19.9 5.9 %collective-permute-start.12 = (f32[384,128]{1,0:T(8,128)S(1)}, f32[384,128]{1,0:T(8,128)S(1)}, u32[]{:S(2)}, u32[]{:S(2)}) collective-permute-start(f32[384,128]{1,0:T(8,128)S(1)} %add.41.refs_0_.tail_ref.own_ref), channel_id=1, source_target_pairs={{0,4},{4,0},{8,12},{12,8},{16,20},{20,16},{24,28},{28,24},{1,5},{5... | collective-permute-start | bytes 589832 | tf_op jit(solution)/shard_map/ppermute | solution.py:35
  21.4 2.0 %collective-permute-start.11 = (f32[192,128]{1,0:T(8,128)S(1)}, f32[192,128]{1,0:T(8,128)S(1)}, u32[]{:S(2)}, u32[]{:S(2)}) collective-permute-start(f32[192,128]{1,0:T(8,128)S(1)} %slice.37), channel_id=1, source_target_pairs={{0,1},{1,0},{2,3},{3,2},{4,5},{5,4},{6,7},{7,6},{8,9},{9,8},{10,11... | collective-permute-start | bytes 294920 | tf_op jit(solution)/shard_map/ppermute | solution.py:35
  21.6 7.7 %collective-permute-start.3 = (f32[320,128]{1,0:T(8,128)S(1)}, f32[320,128]{1,0:T(8,128)S(1)}, u32[]{:S(2)}, u32[]{:S(2)}) collective-permute-start(f32[320,128]{1,0:T(8,128)S(1)} %add.39.first_ref), channel_id=1, source_target_pairs={{0,8},{4,12},{8,0},{12,4},{16,24},{20,28},{24,16},{28,20},{1,9},{5... | collective-permute-start | bytes 491528 | tf_op jit(solution)/shard_map/ppermute | solution.py:35
  23.2 7.3 %collective-permute-start.14 = (f32[256,128]{1,0:T(8,128)S(1)}, f32[256,128]{1,0:T(8,128)S(1)}, u32[]{:S(2)}, u32[]{:S(2)}) collective-permute-start(f32[256,128]{1,0:T(8,128)S(1)} %slice.39), channel_id=1, source_target_pairs={{0,1},{1,0},{2,3},{3,2},{4,5},{5,4},{6,7},{7,6},{8,9},{9,8},{10,11... | collective-permute-start | bytes 393224 | tf_op jit(solution)/shard_map/ppermute | solution.py:35
  27.1 5.7 %collective-permute-start.19 = (f32[192,128]{1,0:T(8,128)S(1)}, f32[192,128]{1,0:T(8,128)S(1)}, u32[]{:S(2)}, u32[]{:S(2)}) collective-permute-start(f32[192,128]{1,0:T(8,128)S(1)} %shard_map.44.refs_0_), channel_id=1, source_target_pairs={{0,4},{4,0},{8,12},{12,8},{16,20},{20,16},{24,28},{28,24},{1,5},{5... | collective-permute-start | bytes 294920 | tf_op jit(solution)/shard_map/ppermute | solution.py:35
  28.7 7.5 %collective-permute-start.17 = (f32[384,128]{1,0:T(8,128)S(1)}, f32[384,128]{1,0:T(8,128)S(1)}, u32[]{:S(2)}, u32[]{:S(2)}) collective-permute-start(f32[384,128]{1,0:T(8,128)S(1)} %shard_map.45.refs_0_), channel_id=1, source_target_pairs={{0,4},{4,0},{8,12},{12,8},{16,20},{20,16},{24,28},{28,24},{1,5},{5... | collective-permute-start | bytes 589832 | tf_op jit(solution)/shard_map/ppermute | solution.py:35
  29.3 9.4 %collective-permute-start.13 = (f32[320,128]{1,0:T(8,128)S(1)}, f32[320,128]{1,0:T(8,128)S(1)}, u32[]{:S(2)}, u32[]{:S(2)}) collective-permute-start(f32[320,128]{1,0:T(8,128)S(1)} %shard_map.46), channel_id=1, source_target_pairs={{0,2},{1,3},{2,0},{3,1},{4,6},{5,7},{6,4},{7,5},{8,10},{9,11},{10,... | collective-permute-start | bytes 491528 | tf_op jit(solution)/shard_map/ppermute | solution.py:35
  31.0 7.8 %collective-permute-start.15 = (f32[320,128]{1,0:T(8,128)S(1)}, f32[320,128]{1,0:T(8,128)S(1)}, u32[]{:S(2)}, u32[]{:S(2)}) collective-permute-start(f32[320,128]{1,0:T(8,128)S(1)} %shard_map.47), channel_id=1, source_target_pairs={{0,8},{4,12},{8,0},{12,4},{16,24},{20,28},{24,16},{28,20},{1,9},{5... | collective-permute-start | bytes 491528 | tf_op jit(solution)/shard_map/ppermute | solution.py:35
  32.8 5.9 %collective-permute-start.20 = (f32[192,128]{1,0:T(8,128)S(1)}, f32[192,128]{1,0:T(8,128)S(1)}, u32[]{:S(2)}, u32[]{:S(2)}) collective-permute-start(f32[192,128]{1,0:T(8,128)S(1)} %add.48.own_ref.p_own_ref), channel_id=1, source_target_pairs={{0,8},{4,12},{8,0},{12,4},{16,24},{20,28},{24,16},{28,20},{1,9},{5... | collective-permute-start | bytes 294920 | tf_op jit(solution)/shard_map/ppermute | solution.py:35
  34.5 6.5 %collective-permute-start.21 = (f32[192,128]{1,0:T(8,128)S(1)}, f32[192,128]{1,0:T(8,128)S(1)}, u32[]{:S(2)}, u32[]{:S(2)}) collective-permute-start(f32[192,128]{1,0:T(8,128)S(1)} %add.48.own_ref.p_own_ref), channel_id=1, source_target_pairs={{0,1},{1,0},{2,3},{3,2},{4,5},{5,4},{6,7},{7,6},{8,9},{9,8},{10,11... | collective-permute-start | bytes 294920 | tf_op jit(solution)/shard_map/ppermute | solution.py:35
  36.2 7.1 %collective-permute-start.18 = (f32[384,128]{1,0:T(8,128)S(1)}, f32[384,128]{1,0:T(8,128)S(1)}, u32[]{:S(2)}, u32[]{:S(2)}) collective-permute-start(f32[384,128]{1,0:T(8,128)S(1)} %add.47.own_ref), channel_id=1, source_target_pairs={{0,8},{4,12},{8,0},{12,4},{16,24},{20,28},{24,16},{28,20},{1,9},{5... | collective-permute-start | bytes 589832 | tf_op jit(solution)/shard_map/ppermute | solution.py:35
  38.7 2.3 %collective-permute-start.22 = (f32[192,128]{1,0:T(8,128)S(1)}, f32[192,128]{1,0:T(8,128)S(1)}, u32[]{:S(2)}, u32[]{:S(2)}) collective-permute-start(f32[192,128]{1,0:T(8,128)S(1)} %collective-permute-done.20.sib_ref), channel_id=1, source_target_pairs={{0,1},{1,0},{2,3},{3,2},{4,5},{5,4},{6,7},{7,6},{8,9},{9,8},{10,11... | collective-permute-start | bytes 294920 | tf_op jit(solution)/shard_map/ppermute | solution.py:35
  38.8 6.8 %collective-permute-start.16 = (f32[320,128]{1,0:T(8,128)S(1)}, f32[320,128]{1,0:T(8,128)S(1)}, u32[]{:S(2)}, u32[]{:S(2)}) collective-permute-start(f32[320,128]{1,0:T(8,128)S(1)} %add_subtract_fusion.1), channel_id=1, source_target_pairs={{0,4},{4,0},{8,12},{12,8},{16,20},{20,16},{24,28},{28,24},{1,5},{5... | collective-permute-start | bytes 491528 | tf_op jit(solution)/shard_map/ppermute | solution.py:35
  40.8 3.2 %collective-permute-start.24 = (f32[256,128]{1,0:T(8,128)S(1)}, f32[256,128]{1,0:T(8,128)S(1)}, u32[]{:S(2)}, u32[]{:S(2)}) collective-permute-start(f32[256,128]{1,0:T(8,128)S(1)} %slice.41), channel_id=1, source_target_pairs={{0,1},{1,0},{2,3},{3,2},{4,5},{5,4},{6,7},{7,6},{8,9},{9,8},{10,11... | collective-permute-start | bytes 393224 | tf_op jit(solution)/shard_map/ppermute | solution.py:35
  43.4 1.8 %collective-permute-start.23 = (f32[256,128]{1,0:T(8,128)S(1)}, f32[256,128]{1,0:T(8,128)S(1)}, u32[]{:S(2)}, u32[]{:S(2)}) collective-permute-start(f32[256,128]{1,0:T(8,128)S(1)} %shard_map.49.sib_ref), channel_id=1, source_target_pairs={{0,1},{1,0},{2,3},{3,2},{4,5},{5,4},{6,7},{7,6},{8,9},{9,8},{10,11... | collective-permute-start | bytes 393224 | tf_op jit(solution)/shard_map/ppermute | solution.py:35
  43.7 4.9 %collective-permute-start.28 = (f32[640,128]{1,0:T(8,128)S(1)}, f32[640,128]{1,0:T(8,128)S(1)}, u32[]{:S(2)}, u32[]{:S(2)}) collective-permute-start(f32[640,128]{1,0:T(8,128)S(1)} %get-tuple-element.36.z_ref.z0_ref), channel_id=1, source_target_pairs={{0,1},{1,0},{2,3},{3,2},{4,5},{5,4},{6,7},{7,6},{8,9},{9,8},{10,11... | collective-permute-start | bytes 983048 | tf_op jit(solution)/shard_map/ppermute | solution.py:35
  45.7 3.0 %collective-permute-start.27 = (f32[384,128]{1,0:T(8,128)S(1)}, f32[384,128]{1,0:T(8,128)S(1)}, u32[]{:S(2)}, u32[]{:S(2)}) collective-permute-start(f32[384,128]{1,0:T(8,128)S(1)} %shard_map.52), channel_id=1, source_target_pairs={{0,1},{1,0},{2,3},{3,2},{4,5},{5,4},{6,7},{7,6},{8,9},{9,8},{10,11... | collective-permute-start | bytes 589832 | tf_op jit(solution)/shard_map/ppermute | solution.py:35
  46.0 10.8 %collective-permute-start.26 = (f32[320,128]{1,0:T(8,128)S(1)}, f32[320,128]{1,0:T(8,128)S(1)}, u32[]{:S(2)}, u32[]{:S(2)}) collective-permute-start(f32[320,128]{1,0:T(8,128)S(1)} %add_subtract_fusion.refs_0_.own_ref), channel_id=1, source_target_pairs={{0,16},{4,20},{8,24},{12,28},{16,0},{20,4},{24,8},{28,12},{1,17},{... | collective-permute-start | bytes 491528 | tf_op jit(solution)/shard_map/ppermute | solution.py:35
  48.6 8.2 %collective-permute-start.25 = (f32[320,128]{1,0:T(8,128)S(1)}, f32[320,128]{1,0:T(8,128)S(1)}, u32[]{:S(2)}, u32[]{:S(2)}) collective-permute-start(f32[320,128]{1,0:T(8,128)S(1)} %add_subtract_fusion.refs_0_.own_ref), channel_id=1, source_target_pairs={{0,1},{1,0},{2,3},{3,2},{4,5},{5,4},{6,7},{7,6},{8,9},{9,8},{10,11... | collective-permute-start | bytes 491528 | tf_op jit(solution)/shard_map/ppermute | solution.py:35
  56.8 1.5 %collective-permute-start.29 = (f32[320,128]{1,0:T(8,128)S(1)}, f32[320,128]{1,0:T(8,128)S(1)}, u32[]{:S(2)}, u32[]{:S(2)}) collective-permute-start(f32[320,128]{1,0:T(8,128)S(1)} %shard_map.54.sib_ref), channel_id=1, source_target_pairs={{0,1},{1,0},{2,3},{3,2},{4,5},{5,4},{6,7},{7,6},{8,9},{9,8},{10,11... | collective-permute-start | bytes 491528 | tf_op jit(solution)/shard_map/ppermute | solution.py:35

commit v13 on v12

--- a/solution.py
+++ b/solution.py
@@ -284,6 +284,20 @@
     solve_series(dot(p_sib, p_own), None, power, inverse_ref)
 
 
+def invert_second_kernel(
+    core_ref, own_ref, sib_ref, own_other_ref, sib_other_ref, r_own_ref, r_own_other_ref,
+    inverse_ref, product_ref, turned_ref, power,
+):
+    core = core_ref[0]
+    p_own = symmetric(core, own_ref[...], own_other_ref[...])
+    p_sib = symmetric(core, sib_ref[...], sib_other_ref[...])
+    both = dot(p_sib, jnp.concatenate([p_own, unpack(r_own_ref)], axis=1))
+    product_ref[...] = both[:, RANK:]
+    turned_ref[:RANK, :] = p_own
+    turned_ref[RANK:, :] = in_order(core, r_own_ref[:RANK, :], r_own_other_ref[...]).T
+    solve_series(both[:, :RANK], None, power, inverse_ref)
+
+
 def call(kernel, out_shape, flops, *values, after=(), scratch=()):
     many = isinstance(out_shape, (list, tuple))
     floats = sum(value.size for value in values) + sum(out.size for out in (out_shape if many else [out_shape]))
@@ -322,7 +336,10 @@
 
 
 def last_parts(core, crossed, z):
-    value = dot_turned(crossed, z)
+    return lost_parts(core, dot_turned(crossed, z))
+
+
+def lost_parts(core, value):
     return jnp.concatenate([symmetric_half(core, value[:, :HALF]), *pack(value[:, HALF:])], axis=0)
 
 
@@ -332,15 +349,13 @@
     refs[-1][...] = last_parts(core, crossed, unpack(z_ref.at[RANK:]))
 
 
-def middle_kernel(
-    core_ref, inverse_ref, p_sib_ref, own_ref, sib_ref, own_other_ref, p_own_ref, p_own_other_ref, z_ref, z_sib_ref, out_ref
-):
-    core = core_ref[0]
-    own = unpack(own_ref)
-    z = dot(inverse_ref[...], unpack(sib_ref) - dot(p_sib_ref[...], own))
+def middle_kernel(core_ref, inverse_ref, product_ref, turned_ref, own_ref, sib_ref, z_ref, z_sib_ref, out_ref):
+    core = core_ref[0]
+    z = dot(inverse_ref[...], unpack(sib_ref) - product_ref[...])
     store(z_ref, z)
-    store(z_sib_ref, own - dot(symmetric(core, p_own_ref[...], p_own_other_ref[...]), z))
-    out_ref[...] = last_parts(core, in_order(core, own_ref[:RANK, :], own_other_ref[...]), z)
+    value = dot(turned_ref[...], z)
+    store(z_sib_ref, unpack(own_ref) - value[:RANK])
+    out_ref[...] = lost_parts(core, value[RANK:])
 
 
 def cross_kernel(core_ref, sib_ref, sib_other_ref, z_sib_ref, crossed_ref, out_ref):
@@ -390,7 +405,7 @@
 
 
 def final_kernel(
-    core_ref, own_ref, own_other_ref, sib_ref, sib_other_ref, high_ref, low_ref, rhs_ref, out_ref, power, total
+    core_ref, own_ref, own_other_ref, sib_ref, sib_other_ref, high_ref, low_ref, rhs_ref, out_ref, power, total, out, sems
 ):
     core = core_ref[0]
     p_own = symmetric(core, own_ref[:SYM, :], own_other_ref[:SYM, :])
@@ -399,7 +414,17 @@
     sib = rhs_in_order(core, sib_ref[SYM:, :], sib_other_ref[SYM:, :])
     both = dot(p_sib, jnp.concatenate([p_own, own], axis=1))
     solve_series(both[:, :RANK], sib - both[:, RANK:], power, total)
-    out_ref[...] = rhs_ref[...] - dot_parts((high_ref[...], low_ref[...]), split(total[...]))
+    z = split(total[...])
+    blocks = sems.shape[0]
+    block = out.shape[0] // blocks
+    copies = []
+    for index in range(blocks):
+        rows = pl.ds(index * block, block)
+        out[rows, :] = rhs_ref[rows, :] - dot_parts((high_ref[rows, :], low_ref[rows, :]), z)
+        copies.append(pltpu.make_async_copy(out.at[rows], out_ref.at[rows], sems.at[index]))
+        copies[-1].start()
+    for copy in copies:
+        copy.wait()
 
 
 def on_device(rhs, generators, solved_gens):
@@ -455,11 +480,15 @@
     p_own_other = swap(p_own, "sub", 0)
     r_own_other = swap(r_own[:RANK], "sub", 0)
     p_sib_other = swap(p_sib, "sub", 0)
-    inverted, p_sib = inverse(INVERT_SECOND, core, p_own, p_sib, p_own_other, p_sib_other)
+    width = HALF + QUARTER
+    inverted, product, turned = call(
+        invert_second_kernel, [struct(RANK, RANK), struct(RANK, width), struct(2 * RANK, RANK)], INVERT_SECOND,
+        core, p_own, p_sib, p_own_other, p_sib_other, r_own, r_own_other, scratch=((RANK, RANK),),
+    )
     cross_sib = call(keep_kernel, struct(RANK), 0, core, r_sib[:RANK], after=(inverted,))
     z1, z_sib, crossed = call(
         middle_kernel, [struct(RANK + HALF), struct(RANK + HALF), struct(last)], MIDDLE_FLOPS,
-        core, inverted, p_sib, r_own, r_sib, r_own_other, p_own, p_own_other,
+        core, inverted, product, turned, r_own, r_sib,
     )
     crossed = call(cross_kernel, struct(last), CROSS_FLOPS, core, cross_sib, swap(cross_sib, "sub", 0), z_sib, crossed)
 
@@ -473,10 +502,22 @@
     )
     sib = call(keep_kernel, struct(last), 0, core, sib, after=(high,))
     own_other, sib_other = swap(own, "sub", 0), swap(sib, "sub", 0)
-    return call(
-        final_kernel, struct(rhs.shape[0], RHS), 6 * rhs.shape[0] * RANK * RHS + 6 * 9 * RANK**3,
-        core, own, own_other, sib, sib_other, high, low, current, scratch=((RANK, RANK), (RANK, RHS)),
-    )
+    rows = rhs.shape[0]
+    small = (own, own_other, sib, sib_other, high, low, current)
+    return pl.pallas_call(
+        final_kernel,
+        in_specs=[SMEM] + [VMEM] * len(small),
+        out_specs=HBM,
+        out_shape=struct(rows, RHS),
+        scratch_shapes=[
+            pltpu.VMEM((RANK, RANK), jnp.float32),
+            pltpu.VMEM((RANK, RHS), jnp.float32),
+            pltpu.VMEM((rows, RHS), jnp.float32),
+            pltpu.SemaphoreType.DMA((2,)),
+        ],
+        compiler_params=pltpu.CompilerParams(vmem_limit_bytes=VMEM_LIMIT),
+        cost_estimate=cost(6 * rows * RANK * RHS + 6 * 9 * RANK**3, 3 * rows * RANK),
+    )(core, *small)
 
 
 def solution(mesh):

time: 61.9 us -> 62.1 us (level)
    pallas_call x0 -> x1, Pallas kernels: none -> 3.57 us  [on_device(): pl.pallas_call(final_kernel, in_specs=[SMEM] + [VMEM] * len(small), out_s...]
    pallas_call x2 -> x1, Pallas kernels: 4.39 us -> 2.11 us  [inverse(): pl.pallas_call(invert_kernel, in_specs=[SMEM] + [VMEM] * 4, out_specs=[VM...]
    pallas_call x14, Pallas kernels: 9.04 us -> 7.44 us  [call(): pl.pallas_call(kernel, in_specs=[SMEM] + [VMEM] * (len(values) - 1) + [AN...]
    ppermute x30, waiting for transfers between devices: 15.8 us -> 16.4 us  [swap(): return lax.ppermute(value, axis, pairs)]
  transfers between devices with their start and end apart: 30 -> 30, of which waited for: 9 -> 10; matrix products, arithmetic and copies ran while one was open for 1% -> 1% of each run, Pallas kernels for 22% -> 21%
where the time goes in v13:
time: 62.1 us; the launch traced here: 61.9 us
  starting transfers between devices  25.3 us (41%)
  Pallas kernels  19.4 us (31%)
  waiting for transfers between devices  16.4 us (26%)
    ppermute x30, starting transfers between devices, swap(): return lax.ppermute(value, axis, pairs)  25.3 us
    ppermute x30, waiting for transfers between devices, swap(): return lax.ppermute(value, axis, pairs)  16.4 us
    pallas_call x14, Pallas kernels, call(): pl.pallas_call(kernel, in_specs=[SMEM] + [VMEM] * (len(values) - 1) + [AN...  7.44 us
    pallas_call x3, Pallas kernels, products(): pl.pallas_call(functools.partial(product_kernel, groups, chunks), in_spec...  6.24 us
    pallas_call x1, Pallas kernels, on_device(): pl.pallas_call(final_kernel, in_specs=[SMEM] + [VMEM] * len(small), out_s...  3.57 us
    pallas_call x1, Pallas kernels, inverse(): pl.pallas_call(invert_kernel, in_specs=[SMEM] + [VMEM] * 4, out_specs=[VM...  2.11 us
  transfers between devices with their start and end apart: 30, of which 10 were waited for; matrix products, arithmetic and copies ran while one was open for 1% of the time, Pallas kernels for 21%

profile of v13, /device:TPU:0, one launch (start us, length us, event | category | flops | bytes accessed | tf_op | source)
XLA Modules:
  0.0 61.9 jit_solution(4032949651796305780)
XLA Ops:
  0.0 2.7 %shard_map.37 = (f32[448,128]{1,0:T(8,128)S(1)}, f32[448,128]{1,0:T(8,128)S(1)}) custom-call(s32[1]{0:T(128)} %bitcast.core_ref, f32[3,1024,256]{2,1,0:T(8,128)} %gens_ref.5, f32[3,1024,256]{2,1,0:T(8,128)} %solved_ref.7), custom_call_target="tpu_custom_call" | custom-call | flops 805306368 | bytes 3145728 | tf_op jit(solution)/shard_map/pallas_call | solution.py:220
  2.7 0.5 collective-permute-start
  3.2 1.1 %collective-permute-done = f32[448,128]{1,0:T(8,128)S(1)} collective-permute-done((f32[448,128]{1,0:T(8,128)S(1)}, f32[448,128]{1,0:T(8,128)S(1)}, u32[]{:S(2)}, u32[]{:S(2)}) %collective-permute-start) | collective-permute-done | bytes 229408 | tf_op jit(solution)/shard_map/ppermute | solution.py:35
  4.4 0.4 collective-permute-start.1
  4.8 2.7 %collective-permute-start.8 = (f32[448,128]{1,0:T(8,128)S(1)}, f32[448,128]{1,0:T(8,128)S(1)}, u32[]{:S(2)}, u32[]{:S(2)}) collective-permute-start(f32[448,128]{1,0:T(8,128)S(1)} %add.38.refs_0_), channel_id=1, source_target_pairs={{0,2},{1,3},{2,0},{3,1},{4,6},{5,7},{6,4},{7,5},{8,10},{9,11},{10,... | collective-permute-start | bytes 688136 | tf_op jit(solution)/shard_map/ppermute | solution.py:35
  7.5 0.0 collective-permute-done.1.refs_1_
  7.5 1.2 %shard_map.39 = (f32[384,128]{1,0:T(8,128)S(1)}, f32[384,128]{1,0:T(8,128)S(1)}) custom-call(s32[1]{0:T(128)} %bitcast.core_ref, f32[3,1024,256]{2,1,0:T(8,128)S(1)} %copy-done.1, f32[3,1024,256]{2,1,0:T(8,128)S(1)} %copy-done, f32[1024,128]{1,0:T(8,128)S(1)} %copy-done.2, f32[8,128]{1,0:T(8,128)S(1)} %collective-permute-done.1.refs_1_), custom_call_target="tpu_custom_call" | custom-call | flops 603979776 | bytes 2621440 | tf_op jit(solution)/shard_map/pallas_call | solution.py:220
  8.7 0.1 collective-permute-start.5
  8.8 2.4 %shard_map.40 = (f32[576,128]{1,0:T(8,128)S(1)}, f32[576,128]{1,0:T(8,128)S(1)}, f32[320,128]{1,0:T(8,128)S(1)}, f32[320,128]{1,0:T(8,128)S(1)}) custom-call(s32[1]{0:T(128)} %bitcast.core_ref, f32[3,1024,256]{2,1,0:T(8,128)S(1)} %copy-done.1, f32[3,1024,256]{2,1,0:T(8,128)S(1)} %copy-done, f32[1024,128]{1,0:T(8,128)S(1)} %copy-done.2, ...), custom_call_target="tpu_custom_call" | custom-call | flops 1610612736 | bytes 4718592 | tf_op jit(solution)/shard_map/pallas_call | solution.py:220
  11.2 0.5 collective-permute-start.4
  11.7 0.0 collective-permute-done.5
  11.7 1.1 %collective-permute-start.6 = (f32[384,128]{1,0:T(8,128)S(1)}, f32[384,128]{1,0:T(8,128)S(1)}, u32[]{:S(2)}, u32[]{:S(2)}) collective-permute-start(f32[384,128]{1,0:T(8,128)S(1)} %add.40), channel_id=1, source_target_pairs={{0,2},{1,3},{2,0},{3,1},{4,6},{5,7},{6,4},{7,5},{8,10},{9,11},{10,... | collective-permute-start | bytes 589832 | tf_op jit(solution)/shard_map/ppermute | solution.py:35
  12.8 0.8 %collective-permute-done.8 = f32[448,128]{1,0:T(8,128)S(1)} collective-permute-done((f32[448,128]{1,0:T(8,128)S(1)}, f32[448,128]{1,0:T(8,128)S(1)}, u32[]{:S(2)}, u32[]{:S(2)}) %collective-permute-start.8) | collective-permute-done | bytes 229408 | tf_op jit(solution)/shard_map/ppermute | solution.py:35
  13.6 1.8 %collective-permute-start.9 = (f32[448,128]{1,0:T(8,128)S(1)}, f32[448,128]{1,0:T(8,128)S(1)}, u32[]{:S(2)}, u32[]{:S(2)}) collective-permute-start(f32[448,128]{1,0:T(8,128)S(1)} %add.43.own_ref.head_ref), channel_id=1, source_target_pairs={{0,4},{4,0},{8,12},{12,8},{16,20},{20,16},{24,28},{28,24},{1,5},{5... | collective-permute-start | bytes 688136 | tf_op jit(solution)/shard_map/ppermute | solution.py:35
  15.4 0.0 collective-permute-start.10
  15.4 0.5 collective-permute-start.2
  15.9 2.8 %collective-permute-done.6 = f32[384,128]{1,0:T(8,128)S(1)} collective-permute-done((f32[384,128]{1,0:T(8,128)S(1)}, f32[384,128]{1,0:T(8,128)S(1)}, u32[]{:S(2)}, u32[]{:S(2)}) %collective-permute-start.6) | collective-permute-done | bytes 196640 | tf_op jit(solution)/shard_map/ppermute | solution.py:35
  18.7 0.0 collective-permute-done.4.second_ref
  18.8 1.2 %collective-permute-start.7 = (f32[576,128]{1,0:T(8,128)S(1)}, f32[576,128]{1,0:T(8,128)S(1)}, u32[]{:S(2)}, u32[]{:S(2)}) collective-permute-start(f32[576,128]{1,0:T(8,128)S(1)} %shard_map.41), channel_id=1, source_target_pairs={{0,2},{1,3},{2,0},{3,1},{4,6},{5,7},{6,4},{7,5},{8,10},{9,11},{10,... | collective-permute-start | bytes 884744 | tf_op jit(solution)/shard_map/ppermute | solution.py:35
  19.9 1.5 %collective-permute-start.12 = (f32[384,128]{1,0:T(8,128)S(1)}, f32[384,128]{1,0:T(8,128)S(1)}, u32[]{:S(2)}, u32[]{:S(2)}) collective-permute-start(f32[384,128]{1,0:T(8,128)S(1)} %add.41.refs_0_.tail_ref.own_ref), channel_id=1, source_target_pairs={{0,4},{4,0},{8,12},{12,8},{16,20},{20,16},{24,28},{28,24},{1,5},{5... | collective-permute-start | bytes 589832 | tf_op jit(solution)/shard_map/ppermute | solution.py:35
  21.4 0.0 collective-permute-done.9.sib_ref.head_sib_ref
  21.4 0.1 collective-permute-start.11
  21.5 0.0 collective-permute-done.2
  21.6 1.6 %collective-permute-start.3 = (f32[320,128]{1,0:T(8,128)S(1)}, f32[320,128]{1,0:T(8,128)S(1)}, u32[]{:S(2)}, u32[]{:S(2)}) collective-permute-start(f32[320,128]{1,0:T(8,128)S(1)} %add.39.first_ref), channel_id=1, source_target_pairs={{0,8},{4,12},{8,0},{12,4},{16,24},{20,28},{24,16},{28,20},{1,9},{5... | collective-permute-start | bytes 491528 | tf_op jit(solution)/shard_map/ppermute | solution.py:35
  23.2 0.0 collective-permute-done.10.own_other_ref.head_other_ref
  23.2 0.3 collective-permute-start.14
  23.5 0.0 collective-permute-done.11.sib_other_ref
  23.5 2.1 %shard_map.42 = (f32[256,256]{1,0:T(8,128)S(1)}, f32[256,256]{1,0:T(8,128)S(1)}) custom-call(s32[1]{0:T(128)} %bitcast.core_ref, f32[448,128]{1,0:T(8,128)S(1)} %add.43.own_ref.head_ref, f32[448,128]{1,0:T(8,128)S(1)} %collective-permute-done.9.sib_ref.head_sib_ref, f32[448,128]{1,0:T(8,128)S(1)} %collective-permute-done.10.own_other_ref.head_other_ref, ...), custom_call_target="tpu_custom_call" | custom-call | flops 900000000 | tf_op jit(solution)/shard_map/pallas_call | solution.py:316
  25.6 0.2 collective-permute-done.12.tail_sib_ref
  25.8 1.1 %shard_map.43 = (f32[640,128]{1,0:T(8,128)S(1)}, f32[576,128]{1,0:T(8,128)S(1)}) custom-call(s32[1]{0:T(128)} %bitcast.core_ref, f32[256,256]{1,0:T(8,128)S(1)} %get-tuple-element.34.inverse_ref, f32[256,256]{1,0:T(8,128)S(1)} %get-tuple-element.35.p_sib_ref, f32[448,128]{1,0:T(8,128)S(1)} %add.43.own_ref.head_ref, ...), custom_call_target="tpu_custom_call" | custom-call | flops 650000000 | bytes 2228228 | tf_op jit(solution)/shard_map/pallas_call | solution.py:304
  27.0 0.0 collective-permute-done.7
  27.1 1.6 %collective-permute-start.19 = (f32[192,128]{1,0:T(8,128)S(1)}, f32[192,128]{1,0:T(8,128)S(1)}, u32[]{:S(2)}, u32[]{:S(2)}) collective-permute-start(f32[192,128]{1,0:T(8,128)S(1)} %shard_map.44.refs_0_), channel_id=1, source_target_pairs={{0,4},{4,0},{8,12},{12,8},{16,20},{20,16},{24,28},{28,24},{1,5},{5... | collective-permute-start | bytes 294920 | tf_op jit(solution)/shard_map/ppermute | solution.py:35
  28.7 0.6 collective-permute-start.17
  29.3 0.0 collective-permute-done.3.second_ref
  29.3 1.3 %collective-permute-start.13 = (f32[320,128]{1,0:T(8,128)S(1)}, f32[320,128]{1,0:T(8,128)S(1)}, u32[]{:S(2)}, u32[]{:S(2)}) collective-permute-start(f32[320,128]{1,0:T(8,128)S(1)} %shard_map.46), channel_id=1, source_target_pairs={{0,2},{1,3},{2,0},{3,1},{4,6},{5,7},{6,4},{7,5},{8,10},{9,11},{10,... | collective-permute-start | bytes 491528 | tf_op jit(solution)/shard_map/ppermute | solution.py:35
  30.6 0.0 collective-permute-done.14.own_other_ref
  30.6 0.4 shard_map.47
  31.0 1.6 %collective-permute-start.15 = (f32[320,128]{1,0:T(8,128)S(1)}, f32[320,128]{1,0:T(8,128)S(1)}, u32[]{:S(2)}, u32[]{:S(2)}) collective-permute-start(f32[320,128]{1,0:T(8,128)S(1)} %shard_map.47), channel_id=1, source_target_pairs={{0,8},{4,12},{8,0},{12,4},{16,24},{20,28},{24,16},{28,20},{1,9},{5... | collective-permute-start | bytes 491528 | tf_op jit(solution)/shard_map/ppermute | solution.py:35
  32.6 0.2 collective-permute-done.19
  32.8 1.7 %collective-permute-start.20 = (f32[192,128]{1,0:T(8,128)S(1)}, f32[192,128]{1,0:T(8,128)S(1)}, u32[]{:S(2)}, u32[]{:S(2)}) collective-permute-start(f32[192,128]{1,0:T(8,128)S(1)} %add.48.own_ref), channel_id=1, source_target_pairs={{0,8},{4,12},{8,0},{12,4},{16,24},{20,28},{24,16},{28,20},{1,9},{5... | collective-permute-start | bytes 294920 | tf_op jit(solution)/shard_map/ppermute | solution.py:35
  34.5 0.0 collective-permute-start.21
  34.6 1.6 %collective-permute-done.17 = f32[384,128]{1,0:T(8,128)S(1)} collective-permute-done((f32[384,128]{1,0:T(8,128)S(1)}, f32[384,128]{1,0:T(8,128)S(1)}, u32[]{:S(2)}, u32[]{:S(2)}) %collective-permute-start.17) | collective-permute-done | bytes 196640 | tf_op jit(solution)/shard_map/ppermute | solution.py:35
  36.2 0.8 %collective-permute-start.18 = (f32[384,128]{1,0:T(8,128)S(1)}, f32[384,128]{1,0:T(8,128)S(1)}, u32[]{:S(2)}, u32[]{:S(2)}) collective-permute-start(f32[384,128]{1,0:T(8,128)S(1)} %add.47.r_own_ref.own_ref), channel_id=1, source_target_pairs={{0,8},{4,12},{8,0},{12,4},{16,24},{20,28},{24,16},{28,20},{1,9},{5... | collective-permute-start | bytes 589832 | tf_op jit(solution)/shard_map/ppermute | solution.py:35
  37.0 0.0 collective-permute-done.13
  37.0 0.0 collective-permute-start.23
  37.0 1.7 %collective-permute-done.20.sib_ref = f32[192,128]{1,0:T(8,128)S(1)} collective-permute-done((f32[192,128]{1,0:T(8,128)S(1)}, f32[192,128]{1,0:T(8,128)S(1)}, u32[]{:S(2)}, u32[]{:S(2)}) %collective-permute-start.20) | collective-permute-done | bytes 98336 | tf_op jit(solution)/shard_map/ppermute | solution.py:35
  38.7 0.0 collective-permute-start.22
  38.7 0.0 collective-permute-done.15
  38.7 2.0 %collective-permute-start.16 = (f32[320,128]{1,0:T(8,128)S(1)}, f32[320,128]{1,0:T(8,128)S(1)}, u32[]{:S(2)}, u32[]{:S(2)}) collective-permute-start(f32[320,128]{1,0:T(8,128)S(1)} %add_subtract_fusion.1), channel_id=1, source_target_pairs={{0,4},{4,0},{8,12},{12,8},{16,20},{20,16},{24,28},{28,24},{1,5},{5... | collective-permute-start | bytes 491528 | tf_op jit(solution)/shard_map/ppermute | solution.py:35
  40.7 0.0 collective-permute-done.23.r_own_other_ref
  40.7 2.2 %shard_map.48 = (f32[256,256]{1,0:T(8,128)S(1)}, f32[256,192]{1,0:T(8,128)S(1)}, f32[512,256]{1,0:T(8,128)S(1)}) custom-call(s32[1]{0:T(128)} %bitcast.core_ref, f32[192,128]{1,0:T(8,128)S(1)} %add.48.own_ref, f32[192,128]{1,0:T(8,128)S(1)} %collective-permute-done.20.sib_ref, f32[192,128]{1,0:T(8,128)S(1)} %collective-permute-done.21.own_other_ref, ...), custom_call_target="tpu_custom_call" | custom-call | flops 900000000 | bytes 1703940 | tf_op jit(solution)/shard_map/pallas_call | solution.py:304
  43.0 0.3 collective-permute-start.24
  43.3 0.3 collective-permute-start.28
  43.6 0.9 %shard_map.50 = (f32[384,128]{1,0:T(8,128)S(1)}, f32[384,128]{1,0:T(8,128)S(1)}, f32[320,128]{1,0:T(8,128)S(1)}) custom-call(s32[1]{0:T(128)} %bitcast.core_ref, f32[256,256]{1,0:T(8,128)S(1)} %get-tuple-element.38.refs_0_.inverse_ref, f32[256,192]{1,0:T(8,128)S(1)} %get-tuple-element.39.product_ref, f32[512,256]{1,0:T(8,128)S(1)} %get-tuple-element.40.turned_ref, ...), custom_call_target="tpu_custom_call" | custom-call | bytes 1933316 | tf_op jit(solution)/shard_map/pallas_call | solution.py:304
  44.5 0.4 shard_map.51
  44.9 0.6 %collective-permute-done.16 = f32[320,128]{1,0:T(8,128)S(1)} collective-permute-done((f32[320,128]{1,0:T(8,128)S(1)}, f32[320,128]{1,0:T(8,128)S(1)}, u32[]{:S(2)}, u32[]{:S(2)}) %collective-permute-start.16) | collective-permute-done | bytes 163872 | tf_op jit(solution)/shard_map/ppermute | solution.py:35
  45.6 0.1 collective-permute-start.27
  45.7 2.7 %collective-permute-start.26 = (f32[320,128]{1,0:T(8,128)S(1)}, f32[320,128]{1,0:T(8,128)S(1)}, u32[]{:S(2)}, u32[]{:S(2)}) collective-permute-start(f32[320,128]{1,0:T(8,128)S(1)} %add_subtract_fusion.refs_0_.own_ref), channel_id=1, source_target_pairs={{0,16},{4,20},{8,24},{12,28},{16,0},{20,4},{24,8},{28,12},{1,17},{... | collective-permute-start | bytes 491528 | tf_op jit(solution)/shard_map/ppermute | solution.py:35
  48.4 0.2 collective-permute-start.25
  48.6 2.2 %shard_map.53 = (bf16[1024,256]{1,0:T(8,128)(2,1)S(1)}, bf16[1024,256]{1,0:T(8,128)(2,1)S(1)}, f32[1024,128]{1,0:T(8,128)S(1)}) custom-call(s32[1]{0:T(128)} %bitcast.core_ref, f32[384,128]{1,0:T(8,128)S(1)} %get-tuple-element.43.value_ref.z1_ref, f32[384,128]{1,0:T(8,128)S(1)} %collective-permute-done.27.z1_other_ref, ...), custom_call_target="tpu_custom_call" | custom-call | flops 1207959552 | bytes 7340036 | tf_op jit(solution)/shard_map/pallas_call | solution.py:304
  50.8 6.0 %collective-permute-done.26.value_ref = f32[320,128]{1,0:T(8,128)S(1)} collective-permute-done((f32[320,128]{1,0:T(8,128)S(1)}, f32[320,128]{1,0:T(8,128)S(1)}, u32[]{:S(2)}, u32[]{:S(2)}) %collective-permute-start.26) | collective-permute-done | bytes 163872 | tf_op jit(solution)/shard_map/ppermute | solution.py:35
  56.8 0.1 collective-permute-start.29
  56.8 1.4 %collective-permute-done.29.sib_other_ref = f32[320,128]{1,0:T(8,128)S(1)} collective-permute-done((f32[320,128]{1,0:T(8,128)S(1)}, f32[320,128]{1,0:T(8,128)S(1)}, u32[]{:S(2)}, u32[]{:S(2)}) %collective-permute-start.29) | collective-permute-done | bytes 163872 | tf_op jit(solution)/shard_map/ppermute | solution.py:35
  58.2 3.6 %shard_map.55 = f32[1024,128]{1,0:T(8,128)} custom-call(s32[1]{0:T(128)} %bitcast.core_ref, f32[320,128]{1,0:T(8,128)S(1)} %add_subtract_fusion.refs_0_.own_ref, f32[320,128]{1,0:T(8,128)S(1)} %collective-permute-done.25.own_other_ref, f32[320,128]{1,0:T(8,128)S(1)} %shard_map.54.sib_ref, f32[320,128]{1,0:T(8,128)S(1)} %collective-permute-done.29.sib_other_ref, ...), custom_call_target="tpu_custom_call" | custom-call | flops 1107296256 | bytes 3145728 | tf_op jit(solution)/shard_map/pallas_call | solution.py:507
  (40 shorter events, 0.5 us)
Async XLA Ops:
  0.0 7.5 %copy-start = (f32[3,1024,256]{2,1,0:T(8,128)S(1)}, f32[3,1024,256]{2,1,0:T(8,128)}, u32[]{:S(2)}) copy-start(f32[3,1024,256]{2,1,0:T(8,128)} %solved_ref.7) | copy-start | bytes 9437188
  0.0 7.5 %copy-start.1 = (f32[3,1024,256]{2,1,0:T(8,128)S(1)}, f32[3,1024,256]{2,1,0:T(8,128)}, u32[]{:S(2)}) copy-start(f32[3,1024,256]{2,1,0:T(8,128)} %gens_ref.5) | copy-start | bytes 9437188
  0.0 7.5 %copy-start.2 = (f32[1024,128]{1,0:T(8,128)S(1)}, f32[1024,128]{1,0:T(8,128)}, u32[]{:S(2)}) copy-start(f32[1024,128]{1,0:T(8,128)} %rhs_ref.1) | copy-start | bytes 1572868
  2.7 1.6 %collective-permute-start = (f32[448,128]{1,0:T(8,128)S(1)}, f32[448,128]{1,0:T(8,128)S(1)}, u32[]{:S(2)}, u32[]{:S(2)}) collective-permute-start(f32[448,128]{1,0:T(8,128)S(1)} %get-tuple-element.26), channel_id=1, source_target_pairs={{0,1},{1,0},{2,3},{3,2},{4,5},{5,4},{6,7},{7,6},{8,9},{9,8},{10,11... | collective-permute-start | bytes 688136 | tf_op jit(solution)/shard_map/ppermute | solution.py:35
  4.4 3.1 %collective-permute-start.1 = (f32[8,128]{1,0:T(8,128)S(1)}, f32[8,128]{1,0:T(8,128)S(1)}, u32[]{:S(2)}, u32[]{:S(2)}) collective-permute-start(f32[8,128]{1,0:T(8,128)S(1)} %shard_map.38), channel_id=1, source_target_pairs={{0,1},{1,0},{2,3},{3,2},{4,5},{5,4},{6,7},{7,6},{8,9},{9,8},{10,11... | collective-permute-start | bytes 12296 | tf_op jit(solution)/shard_map/ppermute | solution.py:35
  4.8 8.8 %collective-permute-start.8 = (f32[448,128]{1,0:T(8,128)S(1)}, f32[448,128]{1,0:T(8,128)S(1)}, u32[]{:S(2)}, u32[]{:S(2)}) collective-permute-start(f32[448,128]{1,0:T(8,128)S(1)} %add.38.refs_0_), channel_id=1, source_target_pairs={{0,2},{1,3},{2,0},{3,1},{4,6},{5,7},{6,4},{7,5},{8,10},{9,11},{10,... | collective-permute-start | bytes 688136 | tf_op jit(solution)/shard_map/ppermute | solution.py:35
  8.7 3.0 %collective-permute-start.5 = (f32[384,128]{1,0:T(8,128)S(1)}, f32[384,128]{1,0:T(8,128)S(1)}, u32[]{:S(2)}, u32[]{:S(2)}) collective-permute-start(f32[384,128]{1,0:T(8,128)S(1)} %get-tuple-element.28.refs_1_), channel_id=1, source_target_pairs={{0,1},{1,0},{2,3},{3,2},{4,5},{5,4},{6,7},{7,6},{8,9},{9,8},{10,11... | collective-permute-start | bytes 589832 | tf_op jit(solution)/shard_map/ppermute | solution.py:35
  11.2 7.5 %collective-permute-start.4 = (f32[576,128]{1,0:T(8,128)S(1)}, f32[576,128]{1,0:T(8,128)S(1)}, u32[]{:S(2)}, u32[]{:S(2)}) collective-permute-start(f32[576,128]{1,0:T(8,128)S(1)} %get-tuple-element.32), channel_id=1, source_target_pairs={{0,1},{1,0},{2,3},{3,2},{4,5},{5,4},{6,7},{7,6},{8,9},{9,8},{10,11... | collective-permute-start | bytes 884744 | tf_op jit(solution)/shard_map/ppermute | solution.py:35
  11.7 7.0 %collective-permute-start.6 = (f32[384,128]{1,0:T(8,128)S(1)}, f32[384,128]{1,0:T(8,128)S(1)}, u32[]{:S(2)}, u32[]{:S(2)}) collective-permute-start(f32[384,128]{1,0:T(8,128)S(1)} %add.40), channel_id=1, source_target_pairs={{0,2},{1,3},{2,0},{3,1},{4,6},{5,7},{6,4},{7,5},{8,10},{9,11},{10,... | collective-permute-start | bytes 589832 | tf_op jit(solution)/shard_map/ppermute | solution.py:35
  13.6 7.8 %collective-permute-start.9 = (f32[448,128]{1,0:T(8,128)S(1)}, f32[448,128]{1,0:T(8,128)S(1)}, u32[]{:S(2)}, u32[]{:S(2)}) collective-permute-start(f32[448,128]{1,0:T(8,128)S(1)} %add.43.own_ref.head_ref), channel_id=1, source_target_pairs={{0,4},{4,0},{8,12},{12,8},{16,20},{20,16},{24,28},{28,24},{1,5},{5... | collective-permute-start | bytes 688136 | tf_op jit(solution)/shard_map/ppermute | solution.py:35
  15.4 7.8 %collective-permute-start.10 = (f32[448,128]{1,0:T(8,128)S(1)}, f32[448,128]{1,0:T(8,128)S(1)}, u32[]{:S(2)}, u32[]{:S(2)}) collective-permute-start(f32[448,128]{1,0:T(8,128)S(1)} %add.43.own_ref.head_ref), channel_id=1, source_target_pairs={{0,1},{1,0},{2,3},{3,2},{4,5},{5,4},{6,7},{7,6},{8,9},{9,8},{10,11... | collective-permute-start | bytes 688136 | tf_op jit(solution)/shard_map/ppermute | solution.py:35
  15.4 6.1 %collective-permute-start.2 = (f32[320,128]{1,0:T(8,128)S(1)}, f32[320,128]{1,0:T(8,128)S(1)}, u32[]{:S(2)}, u32[]{:S(2)}) collective-permute-start(f32[320,128]{1,0:T(8,128)S(1)} %get-tuple-element.30), channel_id=1, source_target_pairs={{0,1},{1,0},{2,3},{3,2},{4,5},{5,4},{6,7},{7,6},{8,9},{9,8},{10,11... | collective-permute-start | bytes 491528 | tf_op jit(solution)/shard_map/ppermute | solution.py:35
  18.8 8.2 %collective-permute-start.7 = (f32[576,128]{1,0:T(8,128)S(1)}, f32[576,128]{1,0:T(8,128)S(1)}, u32[]{:S(2)}, u32[]{:S(2)}) collective-permute-start(f32[576,128]{1,0:T(8,128)S(1)} %shard_map.41), channel_id=1, source_target_pairs={{0,2},{1,3},{2,0},{3,1},{4,6},{5,7},{6,4},{7,5},{8,10},{9,11},{10,... | collective-permute-start | bytes 884744 | tf_op jit(solution)/shard_map/ppermute | solution.py:35
  19.9 5.9 %collective-permute-start.12 = (f32[384,128]{1,0:T(8,128)S(1)}, f32[384,128]{1,0:T(8,128)S(1)}, u32[]{:S(2)}, u32[]{:S(2)}) collective-permute-start(f32[384,128]{1,0:T(8,128)S(1)} %add.41.refs_0_.tail_ref.own_ref), channel_id=1, source_target_pairs={{0,4},{4,0},{8,12},{12,8},{16,20},{20,16},{24,28},{28,24},{1,5},{5... | collective-permute-start | bytes 589832 | tf_op jit(solution)/shard_map/ppermute | solution.py:35
  21.4 2.0 %collective-permute-start.11 = (f32[192,128]{1,0:T(8,128)S(1)}, f32[192,128]{1,0:T(8,128)S(1)}, u32[]{:S(2)}, u32[]{:S(2)}) collective-permute-start(f32[192,128]{1,0:T(8,128)S(1)} %slice.37), channel_id=1, source_target_pairs={{0,1},{1,0},{2,3},{3,2},{4,5},{5,4},{6,7},{7,6},{8,9},{9,8},{10,11... | collective-permute-start | bytes 294920 | tf_op jit(solution)/shard_map/ppermute | solution.py:35
  21.6 7.7 %collective-permute-start.3 = (f32[320,128]{1,0:T(8,128)S(1)}, f32[320,128]{1,0:T(8,128)S(1)}, u32[]{:S(2)}, u32[]{:S(2)}) collective-permute-start(f32[320,128]{1,0:T(8,128)S(1)} %add.39.first_ref), channel_id=1, source_target_pairs={{0,8},{4,12},{8,0},{12,4},{16,24},{20,28},{24,16},{28,20},{1,9},{5... | collective-permute-start | bytes 491528 | tf_op jit(solution)/shard_map/ppermute | solution.py:35
  23.2 7.3 %collective-permute-start.14 = (f32[256,128]{1,0:T(8,128)S(1)}, f32[256,128]{1,0:T(8,128)S(1)}, u32[]{:S(2)}, u32[]{:S(2)}) collective-permute-start(f32[256,128]{1,0:T(8,128)S(1)} %slice.39), channel_id=1, source_target_pairs={{0,1},{1,0},{2,3},{3,2},{4,5},{5,4},{6,7},{7,6},{8,9},{9,8},{10,11... | collective-permute-start | bytes 393224 | tf_op jit(solution)/shard_map/ppermute | solution.py:35
  27.1 5.7 %collective-permute-start.19 = (f32[192,128]{1,0:T(8,128)S(1)}, f32[192,128]{1,0:T(8,128)S(1)}, u32[]{:S(2)}, u32[]{:S(2)}) collective-permute-start(f32[192,128]{1,0:T(8,128)S(1)} %shard_map.44.refs_0_), channel_id=1, source_target_pairs={{0,4},{4,0},{8,12},{12,8},{16,20},{20,16},{24,28},{28,24},{1,5},{5... | collective-permute-start | bytes 294920 | tf_op jit(solution)/shard_map/ppermute | solution.py:35
  28.7 7.5 %collective-permute-start.17 = (f32[384,128]{1,0:T(8,128)S(1)}, f32[384,128]{1,0:T(8,128)S(1)}, u32[]{:S(2)}, u32[]{:S(2)}) collective-permute-start(f32[384,128]{1,0:T(8,128)S(1)} %shard_map.45.refs_0_), channel_id=1, source_target_pairs={{0,4},{4,0},{8,12},{12,8},{16,20},{20,16},{24,28},{28,24},{1,5},{5... | collective-permute-start | bytes 589832 | tf_op jit(solution)/shard_map/ppermute | solution.py:35
  29.3 7.7 %collective-permute-start.13 = (f32[320,128]{1,0:T(8,128)S(1)}, f32[320,128]{1,0:T(8,128)S(1)}, u32[]{:S(2)}, u32[]{:S(2)}) collective-permute-start(f32[320,128]{1,0:T(8,128)S(1)} %shard_map.46), channel_id=1, source_target_pairs={{0,2},{1,3},{2,0},{3,1},{4,6},{5,7},{6,4},{7,5},{8,10},{9,11},{10,... | collective-permute-start | bytes 491528 | tf_op jit(solution)/shard_map/ppermute | solution.py:35
  31.0 7.7 %collective-permute-start.15 = (f32[320,128]{1,0:T(8,128)S(1)}, f32[320,128]{1,0:T(8,128)S(1)}, u32[]{:S(2)}, u32[]{:S(2)}) collective-permute-start(f32[320,128]{1,0:T(8,128)S(1)} %shard_map.47), channel_id=1, source_target_pairs={{0,8},{4,12},{8,0},{12,4},{16,24},{20,28},{24,16},{28,20},{1,9},{5... | collective-permute-start | bytes 491528 | tf_op jit(solution)/shard_map/ppermute | solution.py:35
  32.8 5.9 %collective-permute-start.20 = (f32[192,128]{1,0:T(8,128)S(1)}, f32[192,128]{1,0:T(8,128)S(1)}, u32[]{:S(2)}, u32[]{:S(2)}) collective-permute-start(f32[192,128]{1,0:T(8,128)S(1)} %add.48.own_ref), channel_id=1, source_target_pairs={{0,8},{4,12},{8,0},{12,4},{16,24},{20,28},{24,16},{28,20},{1,9},{5... | collective-permute-start | bytes 294920 | tf_op jit(solution)/shard_map/ppermute | solution.py:35
  34.5 6.2 %collective-permute-start.21 = (f32[192,128]{1,0:T(8,128)S(1)}, f32[192,128]{1,0:T(8,128)S(1)}, u32[]{:S(2)}, u32[]{:S(2)}) collective-permute-start(f32[192,128]{1,0:T(8,128)S(1)} %add.48.own_ref), channel_id=1, source_target_pairs={{0,1},{1,0},{2,3},{3,2},{4,5},{5,4},{6,7},{7,6},{8,9},{9,8},{10,11... | collective-permute-start | bytes 294920 | tf_op jit(solution)/shard_map/ppermute | solution.py:35
  36.2 6.7 %collective-permute-start.18 = (f32[384,128]{1,0:T(8,128)S(1)}, f32[384,128]{1,0:T(8,128)S(1)}, u32[]{:S(2)}, u32[]{:S(2)}) collective-permute-start(f32[384,128]{1,0:T(8,128)S(1)} %add.47.r_own_ref.own_ref), channel_id=1, source_target_pairs={{0,8},{4,12},{8,0},{12,4},{16,24},{20,28},{24,16},{28,20},{1,9},{5... | collective-permute-start | bytes 589832 | tf_op jit(solution)/shard_map/ppermute | solution.py:35
  37.0 3.7 %collective-permute-start.23 = (f32[256,128]{1,0:T(8,128)S(1)}, f32[256,128]{1,0:T(8,128)S(1)}, u32[]{:S(2)}, u32[]{:S(2)}) collective-permute-start(f32[256,128]{1,0:T(8,128)S(1)} %slice.41), channel_id=1, source_target_pairs={{0,1},{1,0},{2,3},{3,2},{4,5},{5,4},{6,7},{7,6},{8,9},{9,8},{10,11... | collective-permute-start | bytes 393224 | tf_op jit(solution)/shard_map/ppermute | solution.py:35
  38.7 2.0 %collective-permute-start.22 = (f32[192,128]{1,0:T(8,128)S(1)}, f32[192,128]{1,0:T(8,128)S(1)}, u32[]{:S(2)}, u32[]{:S(2)}) collective-permute-start(f32[192,128]{1,0:T(8,128)S(1)} %collective-permute-done.20.sib_ref), channel_id=1, source_target_pairs={{0,1},{1,0},{2,3},{3,2},{4,5},{5,4},{6,7},{7,6},{8,9},{9,8},{10,11... | collective-permute-start | bytes 294920 | tf_op jit(solution)/shard_map/ppermute | solution.py:35
  38.7 6.8 %collective-permute-start.16 = (f32[320,128]{1,0:T(8,128)S(1)}, f32[320,128]{1,0:T(8,128)S(1)}, u32[]{:S(2)}, u32[]{:S(2)}) collective-permute-start(f32[320,128]{1,0:T(8,128)S(1)} %add_subtract_fusion.1), channel_id=1, source_target_pairs={{0,4},{4,0},{8,12},{12,8},{16,20},{20,16},{24,28},{28,24},{1,5},{5... | collective-permute-start | bytes 491528 | tf_op jit(solution)/shard_map/ppermute | solution.py:35
  43.0 1.5 %collective-permute-start.24 = (f32[256,128]{1,0:T(8,128)S(1)}, f32[256,128]{1,0:T(8,128)S(1)}, u32[]{:S(2)}, u32[]{:S(2)}) collective-permute-start(f32[256,128]{1,0:T(8,128)S(1)} %shard_map.49.sib_ref), channel_id=1, source_target_pairs={{0,1},{1,0},{2,3},{3,2},{4,5},{5,4},{6,7},{7,6},{8,9},{9,8},{10,11... | collective-permute-start | bytes 393224 | tf_op jit(solution)/shard_map/ppermute | solution.py:35
  43.3 5.3 %collective-permute-start.28 = (f32[640,128]{1,0:T(8,128)S(1)}, f32[640,128]{1,0:T(8,128)S(1)}, u32[]{:S(2)}, u32[]{:S(2)}) collective-permute-start(f32[640,128]{1,0:T(8,128)S(1)} %get-tuple-element.37.z_ref.z0_ref), channel_id=1, source_target_pairs={{0,1},{1,0},{2,3},{3,2},{4,5},{5,4},{6,7},{7,6},{8,9},{9,8},{10,11... | collective-permute-start | bytes 983048 | tf_op jit(solution)/shard_map/ppermute | solution.py:35
  45.6 2.9 %collective-permute-start.27 = (f32[384,128]{1,0:T(8,128)S(1)}, f32[384,128]{1,0:T(8,128)S(1)}, u32[]{:S(2)}, u32[]{:S(2)}) collective-permute-start(f32[384,128]{1,0:T(8,128)S(1)} %shard_map.52), channel_id=1, source_target_pairs={{0,1},{1,0},{2,3},{3,2},{4,5},{5,4},{6,7},{7,6},{8,9},{9,8},{10,11... | collective-permute-start | bytes 589832 | tf_op jit(solution)/shard_map/ppermute | solution.py:35
  45.7 11.0 %collective-permute-start.26 = (f32[320,128]{1,0:T(8,128)S(1)}, f32[320,128]{1,0:T(8,128)S(1)}, u32[]{:S(2)}, u32[]{:S(2)}) collective-permute-start(f32[320,128]{1,0:T(8,128)S(1)} %add_subtract_fusion.refs_0_.own_ref), channel_id=1, source_target_pairs={{0,16},{4,20},{8,24},{12,28},{16,0},{20,4},{24,8},{28,12},{1,17},{... | collective-permute-start | bytes 491528 | tf_op jit(solution)/shard_map/ppermute | solution.py:35
  48.4 8.4 %collective-permute-start.25 = (f32[320,128]{1,0:T(8,128)S(1)}, f32[320,128]{1,0:T(8,128)S(1)}, u32[]{:S(2)}, u32[]{:S(2)}) collective-permute-start(f32[320,128]{1,0:T(8,128)S(1)} %add_subtract_fusion.refs_0_.own_ref), channel_id=1, source_target_pairs={{0,1},{1,0},{2,3},{3,2},{4,5},{5,4},{6,7},{7,6},{8,9},{9,8},{10,11... | collective-permute-start | bytes 491528 | tf_op jit(solution)/shard_map/ppermute | solution.py:35
  56.8 1.5 %collective-permute-start.29 = (f32[320,128]{1,0:T(8,128)S(1)}, f32[320,128]{1,0:T(8,128)S(1)}, u32[]{:S(2)}, u32[]{:S(2)}) collective-permute-start(f32[320,128]{1,0:T(8,128)S(1)} %shard_map.54.sib_ref), channel_id=1, source_target_pairs={{0,1},{1,0},{2,3},{3,2},{4,5},{5,4},{6,7},{7,6},{8,9},{9,8},{10,11... | collective-permute-start | bytes 491528 | tf_op jit(solution)/shard_map/ppermute | solution.py:35

commit v14 on v13

--- a/solution.py
+++ b/solution.py
@@ -239,7 +239,9 @@
 
 
 def doubled(power, values):
-    both = dot(power, jnp.concatenate([power, values], axis=1))
+    power = split(power)
+    right = [jnp.concatenate(parts, axis=1) for parts in zip(power, split(values))]
+    both = dot_parts(power, right)
     return both[:, :RANK], values + both[:, RANK:]
 
 
@@ -251,7 +253,8 @@
     for _ in range(2):
         power, values = doubled(power, values)
     norm = square_norm(power)
-    power_ref[...], sum_ref[...] = doubled(power, values)
+    power_ref[...] = power
+    sum_ref[...] = values + dot(power, values)
 
     def proceed(state):
         count, bound = state
@@ -259,9 +262,10 @@
 
     def body(state):
         count, _ = state
-        bound = square_norm(power_ref[...])
-        power_ref[...], sum_ref[...] = doubled(power_ref[...], sum_ref[...])
-        return count + 1, bound
+        power = dot(power_ref[...], power_ref[...])
+        power_ref[...] = power
+        sum_ref[...] = sum_ref[...] + dot(power, sum_ref[...])
+        return count + 1, square_norm(power)
 
     return lax.while_loop(proceed, body, (jnp.int32(0), norm))[1]
 
@@ -442,7 +446,7 @@
             value = value + swap(value, "rows", bit)
         return value
 
-    keep, send = products(core, generators, solved_gens, rhs, (((0, 0), (0, 1)),), 2)
+    keep, send = products(core, generators, solved_gens, rhs, (((0, 0), (0, 1)),), 8)
     head = keep + swap(send, "sub", 0)
     token = swap(call(keep_kernel, struct(8), 0, core, send[:8], after=(head,)), "sub", 0)
     parts = products(core, generators, solved_gens, rhs, (((0, 2), (0, 3)),), 1, token)

time: 62.1 us -> 62.9 us (1.013)
  Pallas kernels: 19.4 us -> 20.4 us
  transfers between devices with their start and end apart: 30 -> 30, of which waited for: 10 -> 10; matrix products, arithmetic and copies ran while one was open for 1% -> 0% of each run, Pallas kernels for 21% -> 21%
where the time goes in v14:
time: 62.9 us; the launch traced here: 62.8 us
  starting transfers between devices  25.6 us (41%)
  Pallas kernels  20.4 us (32%)
  waiting for transfers between devices  16 us (25%)
    ppermute x30, starting transfers between devices, swap(): return lax.ppermute(value, axis, pairs)  25.6 us
    ppermute x30, waiting for transfers between devices, swap(): return lax.ppermute(value, axis, pairs)  16 us
    pallas_call x14, Pallas kernels, call(): pl.pallas_call(kernel, in_specs=[SMEM] + [VMEM] * (len(values) - 1) + [AN...  7.68 us
    pallas_call x3, Pallas kernels, products(): pl.pallas_call(functools.partial(product_kernel, groups, chunks), in_spec...  6.76 us
    pallas_call x1, Pallas kernels, on_device(): pl.pallas_call(final_kernel, in_specs=[SMEM] + [VMEM] * len(small), out_s...  3.73 us
    pallas_call x1, Pallas kernels, inverse(): pl.pallas_call(invert_kernel, in_specs=[SMEM] + [VMEM] * 4, out_specs=[VM...  2.2 us
  transfers between devices with their start and end apart: 30, of which 10 were waited for; matrix products, arithmetic and copies ran while one was open for 0% of the time, Pallas kernels for 21%

profile of v14, /device:TPU:0, one launch (start us, length us, event | category | flops | bytes accessed | tf_op | source)
XLA Modules:
  0.0 62.8 jit_solution(9736590298623425529)
XLA Ops:
  0.0 3.2 %shard_map.37 = (f32[448,128]{1,0:T(8,128)S(1)}, f32[448,128]{1,0:T(8,128)S(1)}) custom-call(s32[1]{0:T(128)} %bitcast.core_ref, f32[3,1024,256]{2,1,0:T(8,128)} %gens_ref.5, f32[3,1024,256]{2,1,0:T(8,128)} %solved_ref.7), custom_call_target="tpu_custom_call" | custom-call | flops 805306368 | bytes 3145728 | tf_op jit(solution)/shard_map/pallas_call | solution.py:220
  3.2 0.5 collective-permute-start
  3.7 1.1 %collective-permute-done = f32[448,128]{1,0:T(8,128)S(1)} collective-permute-done((f32[448,128]{1,0:T(8,128)S(1)}, f32[448,128]{1,0:T(8,128)S(1)}, u32[]{:S(2)}, u32[]{:S(2)}) %collective-permute-start) | collective-permute-done | bytes 229408 | tf_op jit(solution)/shard_map/ppermute | solution.py:35
  4.9 0.4 collective-permute-start.1
  5.3 2.7 %collective-permute-start.8 = (f32[448,128]{1,0:T(8,128)S(1)}, f32[448,128]{1,0:T(8,128)S(1)}, u32[]{:S(2)}, u32[]{:S(2)}) collective-permute-start(f32[448,128]{1,0:T(8,128)S(1)} %add.38.refs_0_), channel_id=1, source_target_pairs={{0,2},{1,3},{2,0},{3,1},{4,6},{5,7},{6,4},{7,5},{8,10},{9,11},{10,... | collective-permute-start | bytes 688136 | tf_op jit(solution)/shard_map/ppermute | solution.py:35
  8.0 0.0 collective-permute-done.1.refs_1_
  8.0 1.2 %shard_map.39 = (f32[384,128]{1,0:T(8,128)S(1)}, f32[384,128]{1,0:T(8,128)S(1)}) custom-call(s32[1]{0:T(128)} %bitcast.core_ref, f32[3,1024,256]{2,1,0:T(8,128)S(1)} %copy-done.1, f32[3,1024,256]{2,1,0:T(8,128)S(1)} %copy-done, f32[1024,128]{1,0:T(8,128)S(1)} %copy-done.2, f32[8,128]{1,0:T(8,128)S(1)} %collective-permute-done.1.refs_1_), custom_call_target="tpu_custom_call" | custom-call | flops 603979776 | bytes 2621440 | tf_op jit(solution)/shard_map/pallas_call | solution.py:220
  9.2 0.1 collective-permute-start.5
  9.3 2.4 %shard_map.40 = (f32[576,128]{1,0:T(8,128)S(1)}, f32[576,128]{1,0:T(8,128)S(1)}, f32[320,128]{1,0:T(8,128)S(1)}, f32[320,128]{1,0:T(8,128)S(1)}) custom-call(s32[1]{0:T(128)} %bitcast.core_ref, f32[3,1024,256]{2,1,0:T(8,128)S(1)} %copy-done.1, f32[3,1024,256]{2,1,0:T(8,128)S(1)} %copy-done, f32[1024,128]{1,0:T(8,128)S(1)} %copy-done.2, ...), custom_call_target="tpu_custom_call" | custom-call | flops 1610612736 | bytes 4718592 | tf_op jit(solution)/shard_map/pallas_call | solution.py:220
  11.7 0.5 collective-permute-start.4
  12.2 0.0 collective-permute-done.5
  12.3 1.1 %collective-permute-start.6 = (f32[384,128]{1,0:T(8,128)S(1)}, f32[384,128]{1,0:T(8,128)S(1)}, u32[]{:S(2)}, u32[]{:S(2)}) collective-permute-start(f32[384,128]{1,0:T(8,128)S(1)} %add.40), channel_id=1, source_target_pairs={{0,2},{1,3},{2,0},{3,1},{4,6},{5,7},{6,4},{7,5},{8,10},{9,11},{10,... | collective-permute-start | bytes 589832 | tf_op jit(solution)/shard_map/ppermute | solution.py:35
  13.3 0.8 %collective-permute-done.8 = f32[448,128]{1,0:T(8,128)S(1)} collective-permute-done((f32[448,128]{1,0:T(8,128)S(1)}, f32[448,128]{1,0:T(8,128)S(1)}, u32[]{:S(2)}, u32[]{:S(2)}) %collective-permute-start.8) | collective-permute-done | bytes 229408 | tf_op jit(solution)/shard_map/ppermute | solution.py:35
  14.2 1.8 %collective-permute-start.9 = (f32[448,128]{1,0:T(8,128)S(1)}, f32[448,128]{1,0:T(8,128)S(1)}, u32[]{:S(2)}, u32[]{:S(2)}) collective-permute-start(f32[448,128]{1,0:T(8,128)S(1)} %add.43.own_ref.head_ref), channel_id=1, source_target_pairs={{0,4},{4,0},{8,12},{12,8},{16,20},{20,16},{24,28},{28,24},{1,5},{5... | collective-permute-start | bytes 688136 | tf_op jit(solution)/shard_map/ppermute | solution.py:35
  15.9 0.0 collective-permute-start.10
  15.9 0.5 collective-permute-start.2
  16.5 2.8 %collective-permute-done.6 = f32[384,128]{1,0:T(8,128)S(1)} collective-permute-done((f32[384,128]{1,0:T(8,128)S(1)}, f32[384,128]{1,0:T(8,128)S(1)}, u32[]{:S(2)}, u32[]{:S(2)}) %collective-permute-start.6) | collective-permute-done | bytes 196640 | tf_op jit(solution)/shard_map/ppermute | solution.py:35
  19.2 0.0 collective-permute-done.4.second_ref
  19.3 1.2 %collective-permute-start.7 = (f32[576,128]{1,0:T(8,128)S(1)}, f32[576,128]{1,0:T(8,128)S(1)}, u32[]{:S(2)}, u32[]{:S(2)}) collective-permute-start(f32[576,128]{1,0:T(8,128)S(1)} %shard_map.41), channel_id=1, source_target_pairs={{0,2},{1,3},{2,0},{3,1},{4,6},{5,7},{6,4},{7,5},{8,10},{9,11},{10,... | collective-permute-start | bytes 884744 | tf_op jit(solution)/shard_map/ppermute | solution.py:35
  20.5 1.5 %collective-permute-start.12 = (f32[384,128]{1,0:T(8,128)S(1)}, f32[384,128]{1,0:T(8,128)S(1)}, u32[]{:S(2)}, u32[]{:S(2)}) collective-permute-start(f32[384,128]{1,0:T(8,128)S(1)} %add.41.refs_0_.tail_ref.own_ref), channel_id=1, source_target_pairs={{0,4},{4,0},{8,12},{12,8},{16,20},{20,16},{24,28},{28,24},{1,5},{5... | collective-permute-start | bytes 589832 | tf_op jit(solution)/shard_map/ppermute | solution.py:35
  21.9 0.0 collective-permute-done.9.sib_ref.head_sib_ref
  22.0 0.1 collective-permute-start.11
  22.0 0.0 collective-permute-done.2
  22.1 1.6 %collective-permute-start.3 = (f32[320,128]{1,0:T(8,128)S(1)}, f32[320,128]{1,0:T(8,128)S(1)}, u32[]{:S(2)}, u32[]{:S(2)}) collective-permute-start(f32[320,128]{1,0:T(8,128)S(1)} %add.39.first_ref), channel_id=1, source_target_pairs={{0,8},{4,12},{8,0},{12,4},{16,24},{20,28},{24,16},{28,20},{1,9},{5... | collective-permute-start | bytes 491528 | tf_op jit(solution)/shard_map/ppermute | solution.py:35
  23.7 0.0 collective-permute-done.10.own_other_ref.head_other_ref
  23.7 0.3 collective-permute-start.14
  24.0 0.0 collective-permute-done.11.sib_other_ref
  24.0 2.2 %shard_map.42 = (f32[256,256]{1,0:T(8,128)S(1)}, f32[256,256]{1,0:T(8,128)S(1)}) custom-call(s32[1]{0:T(128)} %bitcast.core_ref, f32[448,128]{1,0:T(8,128)S(1)} %add.43.own_ref.head_ref, f32[448,128]{1,0:T(8,128)S(1)} %collective-permute-done.9.sib_ref.head_sib_ref, f32[448,128]{1,0:T(8,128)S(1)} %collective-permute-done.10.own_other_ref.head_other_ref, ...), custom_call_target="tpu_custom_call" | custom-call | flops 900000000 | tf_op jit(solution)/shard_map/pallas_call | solution.py:320
  26.2 0.1 collective-permute-done.12.tail_sib_ref
  26.3 1.1 %shard_map.43 = (f32[640,128]{1,0:T(8,128)S(1)}, f32[576,128]{1,0:T(8,128)S(1)}) custom-call(s32[1]{0:T(128)} %bitcast.core_ref, f32[256,256]{1,0:T(8,128)S(1)} %get-tuple-element.34.inverse_ref, f32[256,256]{1,0:T(8,128)S(1)} %get-tuple-element.35.p_sib_ref, f32[448,128]{1,0:T(8,128)S(1)} %add.43.own_ref.head_ref, ...), custom_call_target="tpu_custom_call" | custom-call | flops 650000000 | bytes 2228228 | tf_op jit(solution)/shard_map/pallas_call | solution.py:308
  27.5 0.0 collective-permute-done.7
  27.6 1.6 %collective-permute-start.19 = (f32[192,128]{1,0:T(8,128)S(1)}, f32[192,128]{1,0:T(8,128)S(1)}, u32[]{:S(2)}, u32[]{:S(2)}) collective-permute-start(f32[192,128]{1,0:T(8,128)S(1)} %shard_map.44.refs_0_), channel_id=1, source_target_pairs={{0,4},{4,0},{8,12},{12,8},{16,20},{20,16},{24,28},{28,24},{1,5},{5... | collective-permute-start | bytes 294920 | tf_op jit(solution)/shard_map/ppermute | solution.py:35
  29.2 0.6 collective-permute-start.17
  29.8 0.0 collective-permute-done.3.second_ref
  29.8 1.2 %collective-permute-start.13 = (f32[320,128]{1,0:T(8,128)S(1)}, f32[320,128]{1,0:T(8,128)S(1)}, u32[]{:S(2)}, u32[]{:S(2)}) collective-permute-start(f32[320,128]{1,0:T(8,128)S(1)} %shard_map.46), channel_id=1, source_target_pairs={{0,2},{1,3},{2,0},{3,1},{4,6},{5,7},{6,4},{7,5},{8,10},{9,11},{10,... | collective-permute-start | bytes 491528 | tf_op jit(solution)/shard_map/ppermute | solution.py:35
  31.1 0.0 collective-permute-done.14.own_other_ref
  31.1 0.4 shard_map.47
  31.5 1.6 %collective-permute-start.15 = (f32[320,128]{1,0:T(8,128)S(1)}, f32[320,128]{1,0:T(8,128)S(1)}, u32[]{:S(2)}, u32[]{:S(2)}) collective-permute-start(f32[320,128]{1,0:T(8,128)S(1)} %shard_map.47), channel_id=1, source_target_pairs={{0,8},{4,12},{8,0},{12,4},{16,24},{20,28},{24,16},{28,20},{1,9},{5... | collective-permute-start | bytes 491528 | tf_op jit(solution)/shard_map/ppermute | solution.py:35
  33.1 0.2 collective-permute-done.19
  33.3 1.7 %collective-permute-start.20 = (f32[192,128]{1,0:T(8,128)S(1)}, f32[192,128]{1,0:T(8,128)S(1)}, u32[]{:S(2)}, u32[]{:S(2)}) collective-permute-start(f32[192,128]{1,0:T(8,128)S(1)} %add.48.own_ref), channel_id=1, source_target_pairs={{0,8},{4,12},{8,0},{12,4},{16,24},{20,28},{24,16},{28,20},{1,9},{5... | collective-permute-start | bytes 294920 | tf_op jit(solution)/shard_map/ppermute | solution.py:35
  35.1 0.0 collective-permute-start.21
  35.1 1.7 %collective-permute-done.17 = f32[384,128]{1,0:T(8,128)S(1)} collective-permute-done((f32[384,128]{1,0:T(8,128)S(1)}, f32[384,128]{1,0:T(8,128)S(1)}, u32[]{:S(2)}, u32[]{:S(2)}) %collective-permute-start.17) | collective-permute-done | bytes 196640 | tf_op jit(solution)/shard_map/ppermute | solution.py:35
  36.9 0.8 %collective-permute-start.18 = (f32[384,128]{1,0:T(8,128)S(1)}, f32[384,128]{1,0:T(8,128)S(1)}, u32[]{:S(2)}, u32[]{:S(2)}) collective-permute-start(f32[384,128]{1,0:T(8,128)S(1)} %add.47.r_own_ref.own_ref), channel_id=1, source_target_pairs={{0,8},{4,12},{8,0},{12,4},{16,24},{20,28},{24,16},{28,20},{1,9},{5... | collective-permute-start | bytes 589832 | tf_op jit(solution)/shard_map/ppermute | solution.py:35
  37.7 1.5 %collective-permute-done.20.sib_ref = f32[192,128]{1,0:T(8,128)S(1)} collective-permute-done((f32[192,128]{1,0:T(8,128)S(1)}, f32[192,128]{1,0:T(8,128)S(1)}, u32[]{:S(2)}, u32[]{:S(2)}) %collective-permute-start.20) | collective-permute-done | bytes 98336 | tf_op jit(solution)/shard_map/ppermute | solution.py:35
  39.1 0.0 collective-permute-start.22
  39.2 0.0 collective-permute-done.15
  39.2 2.2 %collective-permute-start.16 = (f32[320,128]{1,0:T(8,128)S(1)}, f32[320,128]{1,0:T(8,128)S(1)}, u32[]{:S(2)}, u32[]{:S(2)}) collective-permute-start(f32[320,128]{1,0:T(8,128)S(1)} %add_subtract_fusion.1), channel_id=1, source_target_pairs={{0,4},{4,0},{8,12},{12,8},{16,20},{20,16},{24,28},{28,24},{1,5},{5... | collective-permute-start | bytes 491528 | tf_op jit(solution)/shard_map/ppermute | solution.py:35
  41.4 0.0 collective-permute-done.21.own_other_ref
  41.4 0.0 collective-permute-done.22.sib_other_ref
  41.4 0.0 collective-permute-done.23.r_own_other_ref
  41.4 2.5 %shard_map.48 = (f32[256,256]{1,0:T(8,128)S(1)}, f32[256,192]{1,0:T(8,128)S(1)}, f32[512,256]{1,0:T(8,128)S(1)}) custom-call(s32[1]{0:T(128)} %bitcast.core_ref, f32[192,128]{1,0:T(8,128)S(1)} %add.48.own_ref, f32[192,128]{1,0:T(8,128)S(1)} %collective-permute-done.20.sib_ref, f32[192,128]{1,0:T(8,128)S(1)} %collective-permute-done.21.own_other_ref, ...), custom_call_target="tpu_custom_call" | custom-call | flops 900000000 | bytes 1703940 | tf_op jit(solution)/shard_map/pallas_call | solution.py:308
  43.9 0.3 collective-permute-start.24
  44.2 0.3 collective-permute-start.28
  44.5 0.9 %shard_map.50 = (f32[384,128]{1,0:T(8,128)S(1)}, f32[384,128]{1,0:T(8,128)S(1)}, f32[320,128]{1,0:T(8,128)S(1)}) custom-call(s32[1]{0:T(128)} %bitcast.core_ref, f32[256,256]{1,0:T(8,128)S(1)} %get-tuple-element.38.refs_0_.inverse_ref, f32[256,192]{1,0:T(8,128)S(1)} %get-tuple-element.39.product_ref, f32[512,256]{1,0:T(8,128)S(1)} %get-tuple-element.40.turned_ref, ...), custom_call_target="tpu_custom_call" | custom-call | bytes 1933316 | tf_op jit(solution)/shard_map/pallas_call | solution.py:308
  45.4 0.4 shard_map.51
  45.8 0.4 collective-permute-done.16
  46.3 0.1 collective-permute-start.27
  46.4 2.7 %collective-permute-start.26 = (f32[320,128]{1,0:T(8,128)S(1)}, f32[320,128]{1,0:T(8,128)S(1)}, u32[]{:S(2)}, u32[]{:S(2)}) collective-permute-start(f32[320,128]{1,0:T(8,128)S(1)} %add_subtract_fusion.refs_0_.own_ref), channel_id=1, source_target_pairs={{0,16},{4,20},{8,24},{12,28},{16,0},{20,4},{24,8},{28,12},{1,17},{... | collective-permute-start | bytes 491528 | tf_op jit(solution)/shard_map/ppermute | solution.py:35
  49.0 0.2 collective-permute-start.25
  49.2 2.2 %shard_map.53 = (bf16[1024,256]{1,0:T(8,128)(2,1)S(1)}, bf16[1024,256]{1,0:T(8,128)(2,1)S(1)}, f32[1024,128]{1,0:T(8,128)S(1)}) custom-call(s32[1]{0:T(128)} %bitcast.core_ref, f32[384,128]{1,0:T(8,128)S(1)} %get-tuple-element.43.value_ref.z1_ref, f32[384,128]{1,0:T(8,128)S(1)} %collective-permute-done.27.z1_other_ref, ...), custom_call_target="tpu_custom_call" | custom-call | flops 1207959552 | bytes 7340036 | tf_op jit(solution)/shard_map/pallas_call | solution.py:308
  51.4 6.0 %collective-permute-done.26.value_ref = f32[320,128]{1,0:T(8,128)S(1)} collective-permute-done((f32[320,128]{1,0:T(8,128)S(1)}, f32[320,128]{1,0:T(8,128)S(1)}, u32[]{:S(2)}, u32[]{:S(2)}) %collective-permute-start.26) | collective-permute-done | bytes 163872 | tf_op jit(solution)/shard_map/ppermute | solution.py:35
  57.4 0.1 collective-permute-start.29
  57.5 1.4 %collective-permute-done.29.sib_other_ref = f32[320,128]{1,0:T(8,128)S(1)} collective-permute-done((f32[320,128]{1,0:T(8,128)S(1)}, f32[320,128]{1,0:T(8,128)S(1)}, u32[]{:S(2)}, u32[]{:S(2)}) %collective-permute-start.29) | collective-permute-done | bytes 163872 | tf_op jit(solution)/shard_map/ppermute | solution.py:35
  58.9 3.7 %shard_map.55 = f32[1024,128]{1,0:T(8,128)} custom-call(s32[1]{0:T(128)} %bitcast.core_ref, f32[320,128]{1,0:T(8,128)S(1)} %add_subtract_fusion.refs_0_.own_ref, f32[320,128]{1,0:T(8,128)S(1)} %collective-permute-done.25.own_other_ref, f32[320,128]{1,0:T(8,128)S(1)} %shard_map.54.sib_ref, f32[320,128]{1,0:T(8,128)S(1)} %collective-permute-done.29.sib_other_ref, ...), custom_call_target="tpu_custom_call" | custom-call | flops 1107296256 | bytes 3145728 | tf_op jit(solution)/shard_map/pallas_call | solution.py:511
  (40 shorter events, 0.5 us)
Async XLA Ops:
  0.0 8.0 %copy-start = (f32[3,1024,256]{2,1,0:T(8,128)S(1)}, f32[3,1024,256]{2,1,0:T(8,128)}, u32[]{:S(2)}) copy-start(f32[3,1024,256]{2,1,0:T(8,128)} %solved_ref.7) | copy-start | bytes 9437188
  0.0 8.0 %copy-start.1 = (f32[3,1024,256]{2,1,0:T(8,128)S(1)}, f32[3,1024,256]{2,1,0:T(8,128)}, u32[]{:S(2)}) copy-start(f32[3,1024,256]{2,1,0:T(8,128)} %gens_ref.5) | copy-start | bytes 9437188
  0.0 8.0 %copy-start.2 = (f32[1024,128]{1,0:T(8,128)S(1)}, f32[1024,128]{1,0:T(8,128)}, u32[]{:S(2)}) copy-start(f32[1024,128]{1,0:T(8,128)} %rhs_ref.1) | copy-start | bytes 1572868
  3.2 1.6 %collective-permute-start = (f32[448,128]{1,0:T(8,128)S(1)}, f32[448,128]{1,0:T(8,128)S(1)}, u32[]{:S(2)}, u32[]{:S(2)}) collective-permute-start(f32[448,128]{1,0:T(8,128)S(1)} %get-tuple-element.26), channel_id=1, source_target_pairs={{0,1},{1,0},{2,3},{3,2},{4,5},{5,4},{6,7},{7,6},{8,9},{9,8},{10,11... | collective-permute-start | bytes 688136 | tf_op jit(solution)/shard_map/ppermute | solution.py:35
  4.9 3.1 %collective-permute-start.1 = (f32[8,128]{1,0:T(8,128)S(1)}, f32[8,128]{1,0:T(8,128)S(1)}, u32[]{:S(2)}, u32[]{:S(2)}) collective-permute-start(f32[8,128]{1,0:T(8,128)S(1)} %shard_map.38), channel_id=1, source_target_pairs={{0,1},{1,0},{2,3},{3,2},{4,5},{5,4},{6,7},{7,6},{8,9},{9,8},{10,11... | collective-permute-start | bytes 12296 | tf_op jit(solution)/shard_map/ppermute | solution.py:35
  5.3 8.8 %collective-permute-start.8 = (f32[448,128]{1,0:T(8,128)S(1)}, f32[448,128]{1,0:T(8,128)S(1)}, u32[]{:S(2)}, u32[]{:S(2)}) collective-permute-start(f32[448,128]{1,0:T(8,128)S(1)} %add.38.refs_0_), channel_id=1, source_target_pairs={{0,2},{1,3},{2,0},{3,1},{4,6},{5,7},{6,4},{7,5},{8,10},{9,11},{10,... | collective-permute-start | bytes 688136 | tf_op jit(solution)/shard_map/ppermute | solution.py:35
  9.2 3.0 %collective-permute-start.5 = (f32[384,128]{1,0:T(8,128)S(1)}, f32[384,128]{1,0:T(8,128)S(1)}, u32[]{:S(2)}, u32[]{:S(2)}) collective-permute-start(f32[384,128]{1,0:T(8,128)S(1)} %get-tuple-element.28.refs_1_), channel_id=1, source_target_pairs={{0,1},{1,0},{2,3},{3,2},{4,5},{5,4},{6,7},{7,6},{8,9},{9,8},{10,11... | collective-permute-start | bytes 589832 | tf_op jit(solution)/shard_map/ppermute | solution.py:35
  11.7 7.5 %collective-permute-start.4 = (f32[576,128]{1,0:T(8,128)S(1)}, f32[576,128]{1,0:T(8,128)S(1)}, u32[]{:S(2)}, u32[]{:S(2)}) collective-permute-start(f32[576,128]{1,0:T(8,128)S(1)} %get-tuple-element.32), channel_id=1, source_target_pairs={{0,1},{1,0},{2,3},{3,2},{4,5},{5,4},{6,7},{7,6},{8,9},{9,8},{10,11... | collective-permute-start | bytes 884744 | tf_op jit(solution)/shard_map/ppermute | solution.py:35
  12.3 6.9 %collective-permute-start.6 = (f32[384,128]{1,0:T(8,128)S(1)}, f32[384,128]{1,0:T(8,128)S(1)}, u32[]{:S(2)}, u32[]{:S(2)}) collective-permute-start(f32[384,128]{1,0:T(8,128)S(1)} %add.40), channel_id=1, source_target_pairs={{0,2},{1,3},{2,0},{3,1},{4,6},{5,7},{6,4},{7,5},{8,10},{9,11},{10,... | collective-permute-start | bytes 589832 | tf_op jit(solution)/shard_map/ppermute | solution.py:35
  14.2 7.8 %collective-permute-start.9 = (f32[448,128]{1,0:T(8,128)S(1)}, f32[448,128]{1,0:T(8,128)S(1)}, u32[]{:S(2)}, u32[]{:S(2)}) collective-permute-start(f32[448,128]{1,0:T(8,128)S(1)} %add.43.own_ref.head_ref), channel_id=1, source_target_pairs={{0,4},{4,0},{8,12},{12,8},{16,20},{20,16},{24,28},{28,24},{1,5},{5... | collective-permute-start | bytes 688136 | tf_op jit(solution)/shard_map/ppermute | solution.py:35
  15.9 7.8 %collective-permute-start.10 = (f32[448,128]{1,0:T(8,128)S(1)}, f32[448,128]{1,0:T(8,128)S(1)}, u32[]{:S(2)}, u32[]{:S(2)}) collective-permute-start(f32[448,128]{1,0:T(8,128)S(1)} %add.43.own_ref.head_ref), channel_id=1, source_target_pairs={{0,1},{1,0},{2,3},{3,2},{4,5},{5,4},{6,7},{7,6},{8,9},{9,8},{10,11... | collective-permute-start | bytes 688136 | tf_op jit(solution)/shard_map/ppermute | solution.py:35
  15.9 6.1 %collective-permute-start.2 = (f32[320,128]{1,0:T(8,128)S(1)}, f32[320,128]{1,0:T(8,128)S(1)}, u32[]{:S(2)}, u32[]{:S(2)}) collective-permute-start(f32[320,128]{1,0:T(8,128)S(1)} %get-tuple-element.30), channel_id=1, source_target_pairs={{0,1},{1,0},{2,3},{3,2},{4,5},{5,4},{6,7},{7,6},{8,9},{9,8},{10,11... | collective-permute-start | bytes 491528 | tf_op jit(solution)/shard_map/ppermute | solution.py:35
  19.3 8.2 %collective-permute-start.7 = (f32[576,128]{1,0:T(8,128)S(1)}, f32[576,128]{1,0:T(8,128)S(1)}, u32[]{:S(2)}, u32[]{:S(2)}) collective-permute-start(f32[576,128]{1,0:T(8,128)S(1)} %shard_map.41), channel_id=1, source_target_pairs={{0,2},{1,3},{2,0},{3,1},{4,6},{5,7},{6,4},{7,5},{8,10},{9,11},{10,... | collective-permute-start | bytes 884744 | tf_op jit(solution)/shard_map/ppermute | solution.py:35
  20.5 5.9 %collective-permute-start.12 = (f32[384,128]{1,0:T(8,128)S(1)}, f32[384,128]{1,0:T(8,128)S(1)}, u32[]{:S(2)}, u32[]{:S(2)}) collective-permute-start(f32[384,128]{1,0:T(8,128)S(1)} %add.41.refs_0_.tail_ref.own_ref), channel_id=1, source_target_pairs={{0,4},{4,0},{8,12},{12,8},{16,20},{20,16},{24,28},{28,24},{1,5},{5... | collective-permute-start | bytes 589832 | tf_op jit(solution)/shard_map/ppermute | solution.py:35
  22.0 2.1 %collective-permute-start.11 = (f32[192,128]{1,0:T(8,128)S(1)}, f32[192,128]{1,0:T(8,128)S(1)}, u32[]{:S(2)}, u32[]{:S(2)}) collective-permute-start(f32[192,128]{1,0:T(8,128)S(1)} %slice.37), channel_id=1, source_target_pairs={{0,1},{1,0},{2,3},{3,2},{4,5},{5,4},{6,7},{7,6},{8,9},{9,8},{10,11... | collective-permute-start | bytes 294920 | tf_op jit(solution)/shard_map/ppermute | solution.py:35
  22.1 7.7 %collective-permute-start.3 = (f32[320,128]{1,0:T(8,128)S(1)}, f32[320,128]{1,0:T(8,128)S(1)}, u32[]{:S(2)}, u32[]{:S(2)}) collective-permute-start(f32[320,128]{1,0:T(8,128)S(1)} %add.39.first_ref), channel_id=1, source_target_pairs={{0,8},{4,12},{8,0},{12,4},{16,24},{20,28},{24,16},{28,20},{1,9},{5... | collective-permute-start | bytes 491528 | tf_op jit(solution)/shard_map/ppermute | solution.py:35
  23.7 7.3 %collective-permute-start.14 = (f32[256,128]{1,0:T(8,128)S(1)}, f32[256,128]{1,0:T(8,128)S(1)}, u32[]{:S(2)}, u32[]{:S(2)}) collective-permute-start(f32[256,128]{1,0:T(8,128)S(1)} %slice.39), channel_id=1, source_target_pairs={{0,1},{1,0},{2,3},{3,2},{4,5},{5,4},{6,7},{7,6},{8,9},{9,8},{10,11... | collective-permute-start | bytes 393224 | tf_op jit(solution)/shard_map/ppermute | solution.py:35
  27.6 5.7 %collective-permute-start.19 = (f32[192,128]{1,0:T(8,128)S(1)}, f32[192,128]{1,0:T(8,128)S(1)}, u32[]{:S(2)}, u32[]{:S(2)}) collective-permute-start(f32[192,128]{1,0:T(8,128)S(1)} %shard_map.44.refs_0_), channel_id=1, source_target_pairs={{0,4},{4,0},{8,12},{12,8},{16,20},{20,16},{24,28},{28,24},{1,5},{5... | collective-permute-start | bytes 294920 | tf_op jit(solution)/shard_map/ppermute | solution.py:35
  29.2 7.6 %collective-permute-start.17 = (f32[384,128]{1,0:T(8,128)S(1)}, f32[384,128]{1,0:T(8,128)S(1)}, u32[]{:S(2)}, u32[]{:S(2)}) collective-permute-start(f32[384,128]{1,0:T(8,128)S(1)} %shard_map.45.refs_0_), channel_id=1, source_target_pairs={{0,4},{4,0},{8,12},{12,8},{16,20},{20,16},{24,28},{28,24},{1,5},{5... | collective-permute-start | bytes 589832 | tf_op jit(solution)/shard_map/ppermute | solution.py:35
  29.8 7.8 %collective-permute-start.13 = (f32[320,128]{1,0:T(8,128)S(1)}, f32[320,128]{1,0:T(8,128)S(1)}, u32[]{:S(2)}, u32[]{:S(2)}) collective-permute-start(f32[320,128]{1,0:T(8,128)S(1)} %shard_map.46), channel_id=1, source_target_pairs={{0,2},{1,3},{2,0},{3,1},{4,6},{5,7},{6,4},{7,5},{8,10},{9,11},{10,... | collective-permute-start | bytes 491528 | tf_op jit(solution)/shard_map/ppermute | solution.py:35
  31.5 7.7 %collective-permute-start.15 = (f32[320,128]{1,0:T(8,128)S(1)}, f32[320,128]{1,0:T(8,128)S(1)}, u32[]{:S(2)}, u32[]{:S(2)}) collective-permute-start(f32[320,128]{1,0:T(8,128)S(1)} %shard_map.47), channel_id=1, source_target_pairs={{0,8},{4,12},{8,0},{12,4},{16,24},{20,28},{24,16},{28,20},{1,9},{5... | collective-permute-start | bytes 491528 | tf_op jit(solution)/shard_map/ppermute | solution.py:35
  33.3 5.8 %collective-permute-start.20 = (f32[192,128]{1,0:T(8,128)S(1)}, f32[192,128]{1,0:T(8,128)S(1)}, u32[]{:S(2)}, u32[]{:S(2)}) collective-permute-start(f32[192,128]{1,0:T(8,128)S(1)} %add.48.own_ref), channel_id=1, source_target_pairs={{0,8},{4,12},{8,0},{12,4},{16,24},{20,28},{24,16},{28,20},{1,9},{5... | collective-permute-start | bytes 294920 | tf_op jit(solution)/shard_map/ppermute | solution.py:35
  35.1 6.3 %collective-permute-start.21 = (f32[192,128]{1,0:T(8,128)S(1)}, f32[192,128]{1,0:T(8,128)S(1)}, u32[]{:S(2)}, u32[]{:S(2)}) collective-permute-start(f32[192,128]{1,0:T(8,128)S(1)} %add.48.own_ref), channel_id=1, source_target_pairs={{0,1},{1,0},{2,3},{3,2},{4,5},{5,4},{6,7},{7,6},{8,9},{9,8},{10,11... | collective-permute-start | bytes 294920 | tf_op jit(solution)/shard_map/ppermute | solution.py:35
  36.9 7.0 %collective-permute-start.18 = (f32[384,128]{1,0:T(8,128)S(1)}, f32[384,128]{1,0:T(8,128)S(1)}, u32[]{:S(2)}, u32[]{:S(2)}) collective-permute-start(f32[384,128]{1,0:T(8,128)S(1)} %add.47.r_own_ref.own_ref), channel_id=1, source_target_pairs={{0,8},{4,12},{8,0},{12,4},{16,24},{20,28},{24,16},{28,20},{1,9},{5... | collective-permute-start | bytes 589832 | tf_op jit(solution)/shard_map/ppermute | solution.py:35
  37.7 3.7 %collective-permute-start.23 = (f32[256,128]{1,0:T(8,128)S(1)}, f32[256,128]{1,0:T(8,128)S(1)}, u32[]{:S(2)}, u32[]{:S(2)}) collective-permute-start(f32[256,128]{1,0:T(8,128)S(1)} %slice.41), channel_id=1, source_target_pairs={{0,1},{1,0},{2,3},{3,2},{4,5},{5,4},{6,7},{7,6},{8,9},{9,8},{10,11... | collective-permute-start | bytes 393224 | tf_op jit(solution)/shard_map/ppermute | solution.py:35
  39.1 2.2 %collective-permute-start.22 = (f32[192,128]{1,0:T(8,128)S(1)}, f32[192,128]{1,0:T(8,128)S(1)}, u32[]{:S(2)}, u32[]{:S(2)}) collective-permute-start(f32[192,128]{1,0:T(8,128)S(1)} %collective-permute-done.20.sib_ref), channel_id=1, source_target_pairs={{0,1},{1,0},{2,3},{3,2},{4,5},{5,4},{6,7},{7,6},{8,9},{9,8},{10,11... | collective-permute-start | bytes 294920 | tf_op jit(solution)/shard_map/ppermute | solution.py:35
  39.2 7.0 %collective-permute-start.16 = (f32[320,128]{1,0:T(8,128)S(1)}, f32[320,128]{1,0:T(8,128)S(1)}, u32[]{:S(2)}, u32[]{:S(2)}) collective-permute-start(f32[320,128]{1,0:T(8,128)S(1)} %add_subtract_fusion.1), channel_id=1, source_target_pairs={{0,4},{4,0},{8,12},{12,8},{16,20},{20,16},{24,28},{28,24},{1,5},{5... | collective-permute-start | bytes 491528 | tf_op jit(solution)/shard_map/ppermute | solution.py:35
  43.9 1.5 %collective-permute-start.24 = (f32[256,128]{1,0:T(8,128)S(1)}, f32[256,128]{1,0:T(8,128)S(1)}, u32[]{:S(2)}, u32[]{:S(2)}) collective-permute-start(f32[256,128]{1,0:T(8,128)S(1)} %shard_map.49.sib_ref), channel_id=1, source_target_pairs={{0,1},{1,0},{2,3},{3,2},{4,5},{5,4},{6,7},{7,6},{8,9},{9,8},{10,11... | collective-permute-start | bytes 393224 | tf_op jit(solution)/shard_map/ppermute | solution.py:35
  44.2 5.0 %collective-permute-start.28 = (f32[640,128]{1,0:T(8,128)S(1)}, f32[640,128]{1,0:T(8,128)S(1)}, u32[]{:S(2)}, u32[]{:S(2)}) collective-permute-start(f32[640,128]{1,0:T(8,128)S(1)} %get-tuple-element.37.z_ref.z0_ref), channel_id=1, source_target_pairs={{0,1},{1,0},{2,3},{3,2},{4,5},{5,4},{6,7},{7,6},{8,9},{9,8},{10,11... | collective-permute-start | bytes 983048 | tf_op jit(solution)/shard_map/ppermute | solution.py:35
  46.3 2.9 %collective-permute-start.27 = (f32[384,128]{1,0:T(8,128)S(1)}, f32[384,128]{1,0:T(8,128)S(1)}, u32[]{:S(2)}, u32[]{:S(2)}) collective-permute-start(f32[384,128]{1,0:T(8,128)S(1)} %shard_map.52), channel_id=1, source_target_pairs={{0,1},{1,0},{2,3},{3,2},{4,5},{5,4},{6,7},{7,6},{8,9},{9,8},{10,11... | collective-permute-start | bytes 589832 | tf_op jit(solution)/shard_map/ppermute | solution.py:35
  46.4 11.0 %collective-permute-start.26 = (f32[320,128]{1,0:T(8,128)S(1)}, f32[320,128]{1,0:T(8,128)S(1)}, u32[]{:S(2)}, u32[]{:S(2)}) collective-permute-start(f32[320,128]{1,0:T(8,128)S(1)} %add_subtract_fusion.refs_0_.own_ref), channel_id=1, source_target_pairs={{0,16},{4,20},{8,24},{12,28},{16,0},{20,4},{24,8},{28,12},{1,17},{... | collective-permute-start | bytes 491528 | tf_op jit(solution)/shard_map/ppermute | solution.py:35
  49.0 8.4 %collective-permute-start.25 = (f32[320,128]{1,0:T(8,128)S(1)}, f32[320,128]{1,0:T(8,128)S(1)}, u32[]{:S(2)}, u32[]{:S(2)}) collective-permute-start(f32[320,128]{1,0:T(8,128)S(1)} %add_subtract_fusion.refs_0_.own_ref), channel_id=1, source_target_pairs={{0,1},{1,0},{2,3},{3,2},{4,5},{5,4},{6,7},{7,6},{8,9},{9,8},{10,11... | collective-permute-start | bytes 491528 | tf_op jit(solution)/shard_map/ppermute | solution.py:35
  57.4 1.5 %collective-permute-start.29 = (f32[320,128]{1,0:T(8,128)S(1)}, f32[320,128]{1,0:T(8,128)S(1)}, u32[]{:S(2)}, u32[]{:S(2)}) collective-permute-start(f32[320,128]{1,0:T(8,128)S(1)} %shard_map.54.sib_ref), channel_id=1, source_target_pairs={{0,1},{1,0},{2,3},{3,2},{4,5},{5,4},{6,7},{7,6},{8,9},{9,8},{10,11... | collective-permute-start | bytes 491528 | tf_op jit(solution)/shard_map/ppermute | solution.py:35

commit v15 on v14

--- a/solution.py
+++ b/solution.py
@@ -280,12 +280,13 @@
         sum_ref[...] = scale * sum_ref[...]
 
 
-def invert_kernel(core_ref, own_ref, sib_ref, own_other_ref, sib_other_ref, inverse_ref, p_sib_ref, power):
+def invert_kernel(core_ref, own_ref, sib_ref, own_other_ref, sib_other_ref, tail_ref, inverse_ref, product_ref, power):
     core = core_ref[0]
     p_own = symmetric(core, own_ref[:SYM, :], own_other_ref[:SYM, :])
-    p_sib = symmetric(core, sib_ref[:SYM, :], sib_other_ref[:SYM, :])
-    p_sib_ref[...] = p_sib
-    solve_series(dot(p_sib, p_own), None, power, inverse_ref)
+    p_sib = symmetric(core, sib_ref[:SYM, :], sib_other_ref[...])
+    both = dot(p_sib, jnp.concatenate([p_own, own_ref[SYM:, :], unpack(tail_ref)], axis=1))
+    product_ref[...] = both[:, RANK:]
+    solve_series(both[:, :RANK], None, power, inverse_ref)
 
 
 def invert_second_kernel(
@@ -316,23 +317,10 @@
     )(*values, *after)
 
 
-def inverse(flops, core, own, sib, own_other, sib_other):
-    return pl.pallas_call(
-        invert_kernel,
-        in_specs=[SMEM] + [VMEM] * 4,
-        out_specs=[VMEM] * 2,
-        out_shape=[struct(RANK, RANK)] * 2,
-        scratch_shapes=[pltpu.VMEM((RANK, RANK), jnp.float32)],
-        compiler_params=pltpu.CompilerParams(vmem_limit_bytes=VMEM_LIMIT),
-        cost_estimate=cost(flops, 0),
-    )(core, own, sib, own_other, sib_other)
-
-
-def first_kernel(core_ref, inverse_ref, p_sib_ref, head_ref, head_sib_ref, head_other_ref, tail_ref, tail_sib_ref, z_ref, out_ref):
-    core = core_ref[0]
-    own = jnp.concatenate([head_ref[SYM:, :], unpack(tail_ref)], axis=1)
+def first_kernel(core_ref, inverse_ref, product_ref, head_ref, head_sib_ref, head_other_ref, tail_sib_ref, z_ref, out_ref):
+    core = core_ref[0]
     sib = jnp.concatenate([head_sib_ref[SYM:, :], unpack(tail_sib_ref)], axis=1)
-    z = dot(inverse_ref[...], sib - dot(p_sib_ref[...], own))
+    z = dot(inverse_ref[...], sib - product_ref[...])
     store(z_ref, z)
     value = dot_turned(in_order(core, head_ref[SYM:, :], head_other_ref[SYM:, :]), z)
     out_ref[:SYM, :] = symmetric_half(core, value[:, :HALF])
@@ -446,7 +434,7 @@
             value = value + swap(value, "rows", bit)
         return value
 
-    keep, send = products(core, generators, solved_gens, rhs, (((0, 0), (0, 1)),), 8)
+    keep, send = products(core, generators, solved_gens, rhs, (((0, 0), (0, 1)),), 4)
     head = keep + swap(send, "sub", 0)
     token = swap(call(keep_kernel, struct(8), 0, core, send[:8], after=(head,)), "sub", 0)
     parts = products(core, generators, solved_gens, rhs, (((0, 2), (0, 3)),), 1, token)
@@ -463,10 +451,13 @@
     head_other = swap(head, "sub", 0)
     tail_other = swap(tail[:RANK], "sub", 0)
     p_sib_other = swap(head_sib[:SYM], "sub", 0)
-    inverted, p_sib = inverse(INVERT_FLOPS, core, head, head_sib, head_other, p_sib_other)
+    inverted, product = call(
+        invert_kernel, [struct(RANK, RANK), struct(RANK, 2 * HALF + QUARTER)], INVERT_FLOPS,
+        core, head, head_sib, head_other, p_sib_other, tail, scratch=((RANK, RANK),),
+    )
     z0, crossed = call(
         first_kernel, [struct(2 * RANK + HALF), struct(SYM + RANK + HALF)], FIRST_FLOPS,
-        core, inverted, p_sib, head, head_sib, head_other, tail, tail_sib,
+        core, inverted, product, head, head_sib, head_other, tail_sib,
     )
     p_own = call(subtract_kernel, struct(SYM), 0, core, near[:SYM], crossed[:SYM])
     r_own = call(subtract_kernel, struct(RANK + HALF), 0, core, near[SYM:], crossed[SYM:], after=(p_own,))

time: 62.9 us -> 62.1 us (0.987)
  Pallas kernels: 20.4 us -> 19.6 us
    pallas_call x1 -> x0, Pallas kernels: 2.2 us -> none  [inverse(): pl.pallas_call(invert_kernel, in_specs=[SMEM] + [VMEM] * 4, out_specs=[VM...]
    pallas_call x14 -> x15, Pallas kernels: 7.68 us -> 9.65 us  [call(): pl.pallas_call(kernel, in_specs=[SMEM] + [VMEM] * (len(values) - 1) + [AN...]
  transfers between devices with their start and end apart: 30 -> 30, of which waited for: 10 -> 10; matrix products, arithmetic and copies ran while one was open for 0% -> 1% of each run, Pallas kernels for 21% -> 21%
where the time goes in v15:
time: 62.1 us; the launch traced here: 61.9 us
  starting transfers between devices  25.3 us (41%)
  Pallas kernels  19.6 us (32%)
  waiting for transfers between devices  16.3 us (26%)
    ppermute x30, starting transfers between devices, swap(): return lax.ppermute(value, axis, pairs)  25.3 us
    ppermute x30, waiting for transfers between devices, swap(): return lax.ppermute(value, axis, pairs)  16.3 us
    pallas_call x15, Pallas kernels, call(): pl.pallas_call(kernel, in_specs=[SMEM] + [VMEM] * (len(values) - 1) + [AN...  9.65 us
    pallas_call x3, Pallas kernels, products(): pl.pallas_call(functools.partial(product_kernel, groups, chunks), in_spec...  6.21 us
    pallas_call x1, Pallas kernels, on_device(): pl.pallas_call(final_kernel, in_specs=[SMEM] + [VMEM] * len(small), out_s...  3.74 us
  transfers between devices with their start and end apart: 30, of which 10 were waited for; matrix products, arithmetic and copies ran while one was open for 1% of the time, Pallas kernels for 21%

profile of v15, /device:TPU:0, one launch (start us, length us, event | category | flops | bytes accessed | tf_op | source)
XLA Modules:
  0.0 61.9 jit_solution(16197221576439413349)
XLA Ops:
  0.0 2.6 %shard_map.37 = (f32[448,128]{1,0:T(8,128)S(1)}, f32[448,128]{1,0:T(8,128)S(1)}) custom-call(s32[1]{0:T(128)} %bitcast.core_ref, f32[3,1024,256]{2,1,0:T(8,128)} %gens_ref.5, f32[3,1024,256]{2,1,0:T(8,128)} %solved_ref.7), custom_call_target="tpu_custom_call" | custom-call | flops 805306368 | bytes 3145728 | tf_op jit(solution)/shard_map/pallas_call | solution.py:220
  2.7 0.5 collective-permute-start
  3.2 1.1 %collective-permute-done = f32[448,128]{1,0:T(8,128)S(1)} collective-permute-done((f32[448,128]{1,0:T(8,128)S(1)}, f32[448,128]{1,0:T(8,128)S(1)}, u32[]{:S(2)}, u32[]{:S(2)}) %collective-permute-start) | collective-permute-done | bytes 229408 | tf_op jit(solution)/shard_map/ppermute | solution.py:35
  4.3 0.4 collective-permute-start.1
  4.8 2.7 %collective-permute-start.8 = (f32[448,128]{1,0:T(8,128)S(1)}, f32[448,128]{1,0:T(8,128)S(1)}, u32[]{:S(2)}, u32[]{:S(2)}) collective-permute-start(f32[448,128]{1,0:T(8,128)S(1)} %add.38.refs_0_), channel_id=1, source_target_pairs={{0,2},{1,3},{2,0},{3,1},{4,6},{5,7},{6,4},{7,5},{8,10},{9,11},{10,... | collective-permute-start | bytes 688136 | tf_op jit(solution)/shard_map/ppermute | solution.py:35
  7.4 0.0 collective-permute-done.1.refs_1_
  7.5 1.2 %shard_map.39 = (f32[384,128]{1,0:T(8,128)S(1)}, f32[384,128]{1,0:T(8,128)S(1)}) custom-call(s32[1]{0:T(128)} %bitcast.core_ref, f32[3,1024,256]{2,1,0:T(8,128)S(1)} %copy-done.1, f32[3,1024,256]{2,1,0:T(8,128)S(1)} %copy-done, f32[1024,128]{1,0:T(8,128)S(1)} %copy-done.2, f32[8,128]{1,0:T(8,128)S(1)} %collective-permute-done.1.refs_1_), custom_call_target="tpu_custom_call" | custom-call | flops 603979776 | bytes 2621440 | tf_op jit(solution)/shard_map/pallas_call | solution.py:220
  8.6 0.1 collective-permute-start.5
  8.8 2.4 %shard_map.40 = (f32[576,128]{1,0:T(8,128)S(1)}, f32[576,128]{1,0:T(8,128)S(1)}, f32[320,128]{1,0:T(8,128)S(1)}, f32[320,128]{1,0:T(8,128)S(1)}) custom-call(s32[1]{0:T(128)} %bitcast.core_ref, f32[3,1024,256]{2,1,0:T(8,128)S(1)} %copy-done.1, f32[3,1024,256]{2,1,0:T(8,128)S(1)} %copy-done, f32[1024,128]{1,0:T(8,128)S(1)} %copy-done.2, ...), custom_call_target="tpu_custom_call" | custom-call | flops 1610612736 | bytes 4718592 | tf_op jit(solution)/shard_map/pallas_call | solution.py:220
  11.2 0.5 collective-permute-start.4
  11.7 0.0 collective-permute-done.5
  11.7 1.1 %collective-permute-start.6 = (f32[384,128]{1,0:T(8,128)S(1)}, f32[384,128]{1,0:T(8,128)S(1)}, u32[]{:S(2)}, u32[]{:S(2)}) collective-permute-start(f32[384,128]{1,0:T(8,128)S(1)} %add.40), channel_id=1, source_target_pairs={{0,2},{1,3},{2,0},{3,1},{4,6},{5,7},{6,4},{7,5},{8,10},{9,11},{10,... | collective-permute-start | bytes 589832 | tf_op jit(solution)/shard_map/ppermute | solution.py:35
  12.8 0.8 %collective-permute-done.8 = f32[448,128]{1,0:T(8,128)S(1)} collective-permute-done((f32[448,128]{1,0:T(8,128)S(1)}, f32[448,128]{1,0:T(8,128)S(1)}, u32[]{:S(2)}, u32[]{:S(2)}) %collective-permute-start.8) | collective-permute-done | bytes 229408 | tf_op jit(solution)/shard_map/ppermute | solution.py:35
  13.6 1.8 %collective-permute-start.9 = (f32[448,128]{1,0:T(8,128)S(1)}, f32[448,128]{1,0:T(8,128)S(1)}, u32[]{:S(2)}, u32[]{:S(2)}) collective-permute-start(f32[448,128]{1,0:T(8,128)S(1)} %add.43.own_ref.head_ref), channel_id=1, source_target_pairs={{0,4},{4,0},{8,12},{12,8},{16,20},{20,16},{24,28},{28,24},{1,5},{5... | collective-permute-start | bytes 688136 | tf_op jit(solution)/shard_map/ppermute | solution.py:35
  15.4 0.0 collective-permute-start.10
  15.4 0.5 collective-permute-start.2
  15.9 2.8 %collective-permute-done.6 = f32[384,128]{1,0:T(8,128)S(1)} collective-permute-done((f32[384,128]{1,0:T(8,128)S(1)}, f32[384,128]{1,0:T(8,128)S(1)}, u32[]{:S(2)}, u32[]{:S(2)}) %collective-permute-start.6) | collective-permute-done | bytes 196640 | tf_op jit(solution)/shard_map/ppermute | solution.py:35
  18.7 0.0 collective-permute-done.4.second_ref
  18.7 1.2 %collective-permute-start.7 = (f32[576,128]{1,0:T(8,128)S(1)}, f32[576,128]{1,0:T(8,128)S(1)}, u32[]{:S(2)}, u32[]{:S(2)}) collective-permute-start(f32[576,128]{1,0:T(8,128)S(1)} %shard_map.41), channel_id=1, source_target_pairs={{0,2},{1,3},{2,0},{3,1},{4,6},{5,7},{6,4},{7,5},{8,10},{9,11},{10,... | collective-permute-start | bytes 884744 | tf_op jit(solution)/shard_map/ppermute | solution.py:35
  19.9 1.5 %collective-permute-start.12 = (f32[384,128]{1,0:T(8,128)S(1)}, f32[384,128]{1,0:T(8,128)S(1)}, u32[]{:S(2)}, u32[]{:S(2)}) collective-permute-start(f32[384,128]{1,0:T(8,128)S(1)} %add.41.refs_0_.tail_ref.own_ref), channel_id=1, source_target_pairs={{0,4},{4,0},{8,12},{12,8},{16,20},{20,16},{24,28},{28,24},{1,5},{5... | collective-permute-start | bytes 589832 | tf_op jit(solution)/shard_map/ppermute | solution.py:35
  21.4 0.0 collective-permute-done.9.sib_ref.head_sib_ref
  21.4 0.1 collective-permute-start.11
  21.5 0.0 collective-permute-done.2
  21.5 1.6 %collective-permute-start.3 = (f32[320,128]{1,0:T(8,128)S(1)}, f32[320,128]{1,0:T(8,128)S(1)}, u32[]{:S(2)}, u32[]{:S(2)}) collective-permute-start(f32[320,128]{1,0:T(8,128)S(1)} %add.39.first_ref), channel_id=1, source_target_pairs={{0,8},{4,12},{8,0},{12,4},{16,24},{20,28},{24,16},{28,20},{1,9},{5... | collective-permute-start | bytes 491528 | tf_op jit(solution)/shard_map/ppermute | solution.py:35
  23.2 0.0 collective-permute-done.10.own_other_ref.head_other_ref
  23.2 0.3 collective-permute-start.14
  23.5 0.0 collective-permute-done.11.sib_other_ref
  23.5 2.3 %shard_map.42 = (f32[256,256]{1,0:T(8,128)S(1)}, f32[256,320]{1,0:T(8,128)S(1)}) custom-call(s32[1]{0:T(128)} %bitcast.core_ref, f32[448,128]{1,0:T(8,128)S(1)} %add.43.own_ref.head_ref, f32[448,128]{1,0:T(8,128)S(1)} %collective-permute-done.9.sib_ref.head_sib_ref, f32[448,128]{1,0:T(8,128)S(1)} %collective-permute-done.10.own_other_ref.head_other_ref, ...), custom_call_target="tpu_custom_call" | custom-call | flops 900000000 | bytes 1572868 | tf_op jit(solution)/shard_map/pallas_call | solution.py:309
  25.8 0.8 %shard_map.43 = (f32[640,128]{1,0:T(8,128)S(1)}, f32[576,128]{1,0:T(8,128)S(1)}) custom-call(s32[1]{0:T(128)} %bitcast.core_ref, f32[256,256]{1,0:T(8,128)S(1)} %get-tuple-element.34.inverse_ref, f32[256,320]{1,0:T(8,128)S(1)} %get-tuple-element.35.product_ref, f32[448,128]{1,0:T(8,128)S(1)} %add.43.own_ref.head_ref, ...), custom_call_target="tpu_custom_call" | custom-call | flops 650000000 | bytes 2097156 | tf_op jit(solution)/shard_map/pallas_call | solution.py:309
  26.6 0.3 collective-permute-done.7
  27.1 1.6 %collective-permute-start.19 = (f32[192,128]{1,0:T(8,128)S(1)}, f32[192,128]{1,0:T(8,128)S(1)}, u32[]{:S(2)}, u32[]{:S(2)}) collective-permute-start(f32[192,128]{1,0:T(8,128)S(1)} %shard_map.44.refs_0_), channel_id=1, source_target_pairs={{0,4},{4,0},{8,12},{12,8},{16,20},{20,16},{24,28},{28,24},{1,5},{5... | collective-permute-start | bytes 294920 | tf_op jit(solution)/shard_map/ppermute | solution.py:35
  28.7 0.6 collective-permute-start.17
  29.2 0.0 collective-permute-done.3.second_ref
  29.3 1.2 %collective-permute-start.13 = (f32[320,128]{1,0:T(8,128)S(1)}, f32[320,128]{1,0:T(8,128)S(1)}, u32[]{:S(2)}, u32[]{:S(2)}) collective-permute-start(f32[320,128]{1,0:T(8,128)S(1)} %shard_map.46), channel_id=1, source_target_pairs={{0,2},{1,3},{2,0},{3,1},{4,6},{5,7},{6,4},{7,5},{8,10},{9,11},{10,... | collective-permute-start | bytes 491528 | tf_op jit(solution)/shard_map/ppermute | solution.py:35
  30.5 0.4 shard_map.47
  30.9 1.6 %collective-permute-start.15 = (f32[320,128]{1,0:T(8,128)S(1)}, f32[320,128]{1,0:T(8,128)S(1)}, u32[]{:S(2)}, u32[]{:S(2)}) collective-permute-start(f32[320,128]{1,0:T(8,128)S(1)} %shard_map.47), channel_id=1, source_target_pairs={{0,8},{4,12},{8,0},{12,4},{16,24},{20,28},{24,16},{28,20},{1,9},{5... | collective-permute-start | bytes 491528 | tf_op jit(solution)/shard_map/ppermute | solution.py:35
  32.6 0.2 collective-permute-done.19
  32.8 1.7 %collective-permute-start.20 = (f32[192,128]{1,0:T(8,128)S(1)}, f32[192,128]{1,0:T(8,128)S(1)}, u32[]{:S(2)}, u32[]{:S(2)}) collective-permute-start(f32[192,128]{1,0:T(8,128)S(1)} %add.48.own_ref), channel_id=1, source_target_pairs={{0,8},{4,12},{8,0},{12,4},{16,24},{20,28},{24,16},{28,20},{1,9},{5... | collective-permute-start | bytes 294920 | tf_op jit(solution)/shard_map/ppermute | solution.py:35
  34.5 0.0 collective-permute-start.21
  34.5 1.5 %collective-permute-done.17 = f32[384,128]{1,0:T(8,128)S(1)} collective-permute-done((f32[384,128]{1,0:T(8,128)S(1)}, f32[384,128]{1,0:T(8,128)S(1)}, u32[]{:S(2)}, u32[]{:S(2)}) %collective-permute-start.17) | collective-permute-done | bytes 196640 | tf_op jit(solution)/shard_map/ppermute | solution.py:35
  36.1 0.8 %collective-permute-start.18 = (f32[384,128]{1,0:T(8,128)S(1)}, f32[384,128]{1,0:T(8,128)S(1)}, u32[]{:S(2)}, u32[]{:S(2)}) collective-permute-start(f32[384,128]{1,0:T(8,128)S(1)} %add.47.r_own_ref.own_ref), channel_id=1, source_target_pairs={{0,8},{4,12},{8,0},{12,4},{16,24},{20,28},{24,16},{28,20},{1,9},{5... | collective-permute-start | bytes 589832 | tf_op jit(solution)/shard_map/ppermute | solution.py:35
  36.9 0.0 collective-permute-done.13
  36.9 0.0 collective-permute-start.23
  36.9 1.8 %collective-permute-done.20.sib_ref = f32[192,128]{1,0:T(8,128)S(1)} collective-permute-done((f32[192,128]{1,0:T(8,128)S(1)}, f32[192,128]{1,0:T(8,128)S(1)}, u32[]{:S(2)}, u32[]{:S(2)}) %collective-permute-start.20) | collective-permute-done | bytes 98336 | tf_op jit(solution)/shard_map/ppermute | solution.py:35
  38.6 0.0 collective-permute-start.22
  38.7 1.9 %collective-permute-start.16 = (f32[320,128]{1,0:T(8,128)S(1)}, f32[320,128]{1,0:T(8,128)S(1)}, u32[]{:S(2)}, u32[]{:S(2)}) collective-permute-start(f32[320,128]{1,0:T(8,128)S(1)} %add_subtract_fusion.1), channel_id=1, source_target_pairs={{0,4},{4,0},{8,12},{12,8},{16,20},{20,16},{24,28},{28,24},{1,5},{5... | collective-permute-start | bytes 491528 | tf_op jit(solution)/shard_map/ppermute | solution.py:35
  40.5 0.0 collective-permute-done.21.own_other_ref
  40.6 2.5 %shard_map.48 = (f32[256,256]{1,0:T(8,128)S(1)}, f32[256,192]{1,0:T(8,128)S(1)}, f32[512,256]{1,0:T(8,128)S(1)}) custom-call(s32[1]{0:T(128)} %bitcast.core_ref, f32[192,128]{1,0:T(8,128)S(1)} %add.48.own_ref, f32[192,128]{1,0:T(8,128)S(1)} %collective-permute-done.20.sib_ref, f32[192,128]{1,0:T(8,128)S(1)} %collective-permute-done.21.own_other_ref, ...), custom_call_target="tpu_custom_call" | custom-call | flops 900000000 | bytes 1703940 | tf_op jit(solution)/shard_map/pallas_call | solution.py:309
  43.0 0.0 collective-permute-done.18.sib_ref
  43.1 0.3 collective-permute-start.24
  43.4 0.3 collective-permute-start.28
  43.7 0.9 %shard_map.50 = (f32[384,128]{1,0:T(8,128)S(1)}, f32[384,128]{1,0:T(8,128)S(1)}, f32[320,128]{1,0:T(8,128)S(1)}) custom-call(s32[1]{0:T(128)} %bitcast.core_ref, f32[256,256]{1,0:T(8,128)S(1)} %get-tuple-element.38.refs_0_.inverse_ref, f32[256,192]{1,0:T(8,128)S(1)} %get-tuple-element.39.product_ref, f32[512,256]{1,0:T(8,128)S(1)} %get-tuple-element.40.turned_ref, ...), custom_call_target="tpu_custom_call" | custom-call | bytes 1933316 | tf_op jit(solution)/shard_map/pallas_call | solution.py:309
  44.6 0.0 collective-permute-done.24.sib_other_ref
  44.6 0.4 shard_map.51
  45.0 0.4 collective-permute-done.16
  45.5 0.1 collective-permute-start.27
  45.6 2.7 %collective-permute-start.26 = (f32[320,128]{1,0:T(8,128)S(1)}, f32[320,128]{1,0:T(8,128)S(1)}, u32[]{:S(2)}, u32[]{:S(2)}) collective-permute-start(f32[320,128]{1,0:T(8,128)S(1)} %add_subtract_fusion.refs_0_.own_ref), channel_id=1, source_target_pairs={{0,16},{4,20},{8,24},{12,28},{16,0},{20,4},{24,8},{28,12},{1,17},{... | collective-permute-start | bytes 491528 | tf_op jit(solution)/shard_map/ppermute | solution.py:35
  48.2 0.2 collective-permute-start.25
  48.4 2.2 %shard_map.53 = (bf16[1024,256]{1,0:T(8,128)(2,1)S(1)}, bf16[1024,256]{1,0:T(8,128)(2,1)S(1)}, f32[1024,128]{1,0:T(8,128)S(1)}) custom-call(s32[1]{0:T(128)} %bitcast.core_ref, f32[384,128]{1,0:T(8,128)S(1)} %get-tuple-element.43.value_ref.z1_ref, f32[384,128]{1,0:T(8,128)S(1)} %collective-permute-done.27.z1_other_ref, ...), custom_call_target="tpu_custom_call" | custom-call | flops 1207959552 | bytes 7340036 | tf_op jit(solution)/shard_map/pallas_call | solution.py:309
  50.6 6.0 %collective-permute-done.26.value_ref = f32[320,128]{1,0:T(8,128)S(1)} collective-permute-done((f32[320,128]{1,0:T(8,128)S(1)}, f32[320,128]{1,0:T(8,128)S(1)}, u32[]{:S(2)}, u32[]{:S(2)}) %collective-permute-start.26) | collective-permute-done | bytes 163872 | tf_op jit(solution)/shard_map/ppermute | solution.py:35
  56.6 0.1 collective-permute-start.29
  56.7 0.0 collective-permute-done.25.own_other_ref
  56.7 1.4 %collective-permute-done.29.sib_other_ref = f32[320,128]{1,0:T(8,128)S(1)} collective-permute-done((f32[320,128]{1,0:T(8,128)S(1)}, f32[320,128]{1,0:T(8,128)S(1)}, u32[]{:S(2)}, u32[]{:S(2)}) %collective-permute-start.29) | collective-permute-done | bytes 163872 | tf_op jit(solution)/shard_map/ppermute | solution.py:35
  58.1 3.7 %shard_map.55 = f32[1024,128]{1,0:T(8,128)} custom-call(s32[1]{0:T(128)} %bitcast.core_ref, f32[320,128]{1,0:T(8,128)S(1)} %add_subtract_fusion.refs_0_.own_ref, f32[320,128]{1,0:T(8,128)S(1)} %collective-permute-done.25.own_other_ref, f32[320,128]{1,0:T(8,128)S(1)} %shard_map.54.sib_ref, f32[320,128]{1,0:T(8,128)S(1)} %collective-permute-done.29.sib_other_ref, ...), custom_call_target="tpu_custom_call" | custom-call | flops 1107296256 | bytes 3145728 | tf_op jit(solution)/shard_map/pallas_call | solution.py:502
  (40 shorter events, 0.5 us)
Async XLA Ops:
  0.0 7.5 %copy-start = (f32[3,1024,256]{2,1,0:T(8,128)S(1)}, f32[3,1024,256]{2,1,0:T(8,128)}, u32[]{:S(2)}) copy-start(f32[3,1024,256]{2,1,0:T(8,128)} %solved_ref.7) | copy-start | bytes 9437188
  0.0 7.5 %copy-start.1 = (f32[3,1024,256]{2,1,0:T(8,128)S(1)}, f32[3,1024,256]{2,1,0:T(8,128)}, u32[]{:S(2)}) copy-start(f32[3,1024,256]{2,1,0:T(8,128)} %gens_ref.5) | copy-start | bytes 9437188
  0.0 7.5 %copy-start.2 = (f32[1024,128]{1,0:T(8,128)S(1)}, f32[1024,128]{1,0:T(8,128)}, u32[]{:S(2)}) copy-start(f32[1024,128]{1,0:T(8,128)} %rhs_ref.1) | copy-start | bytes 1572868
  2.7 1.6 %collective-permute-start = (f32[448,128]{1,0:T(8,128)S(1)}, f32[448,128]{1,0:T(8,128)S(1)}, u32[]{:S(2)}, u32[]{:S(2)}) collective-permute-start(f32[448,128]{1,0:T(8,128)S(1)} %get-tuple-element.26), channel_id=1, source_target_pairs={{0,1},{1,0},{2,3},{3,2},{4,5},{5,4},{6,7},{7,6},{8,9},{9,8},{10,11... | collective-permute-start | bytes 688136 | tf_op jit(solution)/shard_map/ppermute | solution.py:35
  4.3 3.1 %collective-permute-start.1 = (f32[8,128]{1,0:T(8,128)S(1)}, f32[8,128]{1,0:T(8,128)S(1)}, u32[]{:S(2)}, u32[]{:S(2)}) collective-permute-start(f32[8,128]{1,0:T(8,128)S(1)} %shard_map.38), channel_id=1, source_target_pairs={{0,1},{1,0},{2,3},{3,2},{4,5},{5,4},{6,7},{7,6},{8,9},{9,8},{10,11... | collective-permute-start | bytes 12296 | tf_op jit(solution)/shard_map/ppermute | solution.py:35
  4.8 8.8 %collective-permute-start.8 = (f32[448,128]{1,0:T(8,128)S(1)}, f32[448,128]{1,0:T(8,128)S(1)}, u32[]{:S(2)}, u32[]{:S(2)}) collective-permute-start(f32[448,128]{1,0:T(8,128)S(1)} %add.38.refs_0_), channel_id=1, source_target_pairs={{0,2},{1,3},{2,0},{3,1},{4,6},{5,7},{6,4},{7,5},{8,10},{9,11},{10,... | collective-permute-start | bytes 688136 | tf_op jit(solution)/shard_map/ppermute | solution.py:35
  8.6 3.1 %collective-permute-start.5 = (f32[384,128]{1,0:T(8,128)S(1)}, f32[384,128]{1,0:T(8,128)S(1)}, u32[]{:S(2)}, u32[]{:S(2)}) collective-permute-start(f32[384,128]{1,0:T(8,128)S(1)} %get-tuple-element.28.refs_1_), channel_id=1, source_target_pairs={{0,1},{1,0},{2,3},{3,2},{4,5},{5,4},{6,7},{7,6},{8,9},{9,8},{10,11... | collective-permute-start | bytes 589832 | tf_op jit(solution)/shard_map/ppermute | solution.py:35
  11.2 7.5 %collective-permute-start.4 = (f32[576,128]{1,0:T(8,128)S(1)}, f32[576,128]{1,0:T(8,128)S(1)}, u32[]{:S(2)}, u32[]{:S(2)}) collective-permute-start(f32[576,128]{1,0:T(8,128)S(1)} %get-tuple-element.32), channel_id=1, source_target_pairs={{0,1},{1,0},{2,3},{3,2},{4,5},{5,4},{6,7},{7,6},{8,9},{9,8},{10,11... | collective-permute-start | bytes 884744 | tf_op jit(solution)/shard_map/ppermute | solution.py:35
  11.7 7.0 %collective-permute-start.6 = (f32[384,128]{1,0:T(8,128)S(1)}, f32[384,128]{1,0:T(8,128)S(1)}, u32[]{:S(2)}, u32[]{:S(2)}) collective-permute-start(f32[384,128]{1,0:T(8,128)S(1)} %add.40), channel_id=1, source_target_pairs={{0,2},{1,3},{2,0},{3,1},{4,6},{5,7},{6,4},{7,5},{8,10},{9,11},{10,... | collective-permute-start | bytes 589832 | tf_op jit(solution)/shard_map/ppermute | solution.py:35
  13.6 7.8 %collective-permute-start.9 = (f32[448,128]{1,0:T(8,128)S(1)}, f32[448,128]{1,0:T(8,128)S(1)}, u32[]{:S(2)}, u32[]{:S(2)}) collective-permute-start(f32[448,128]{1,0:T(8,128)S(1)} %add.43.own_ref.head_ref), channel_id=1, source_target_pairs={{0,4},{4,0},{8,12},{12,8},{16,20},{20,16},{24,28},{28,24},{1,5},{5... | collective-permute-start | bytes 688136 | tf_op jit(solution)/shard_map/ppermute | solution.py:35
  15.4 7.8 %collective-permute-start.10 = (f32[448,128]{1,0:T(8,128)S(1)}, f32[448,128]{1,0:T(8,128)S(1)}, u32[]{:S(2)}, u32[]{:S(2)}) collective-permute-start(f32[448,128]{1,0:T(8,128)S(1)} %add.43.own_ref.head_ref), channel_id=1, source_target_pairs={{0,1},{1,0},{2,3},{3,2},{4,5},{5,4},{6,7},{7,6},{8,9},{9,8},{10,11... | collective-permute-start | bytes 688136 | tf_op jit(solution)/shard_map/ppermute | solution.py:35
  15.4 6.1 %collective-permute-start.2 = (f32[320,128]{1,0:T(8,128)S(1)}, f32[320,128]{1,0:T(8,128)S(1)}, u32[]{:S(2)}, u32[]{:S(2)}) collective-permute-start(f32[320,128]{1,0:T(8,128)S(1)} %get-tuple-element.30), channel_id=1, source_target_pairs={{0,1},{1,0},{2,3},{3,2},{4,5},{5,4},{6,7},{7,6},{8,9},{9,8},{10,11... | collective-permute-start | bytes 491528 | tf_op jit(solution)/shard_map/ppermute | solution.py:35
  18.7 8.2 %collective-permute-start.7 = (f32[576,128]{1,0:T(8,128)S(1)}, f32[576,128]{1,0:T(8,128)S(1)}, u32[]{:S(2)}, u32[]{:S(2)}) collective-permute-start(f32[576,128]{1,0:T(8,128)S(1)} %shard_map.41), channel_id=1, source_target_pairs={{0,2},{1,3},{2,0},{3,1},{4,6},{5,7},{6,4},{7,5},{8,10},{9,11},{10,... | collective-permute-start | bytes 884744 | tf_op jit(solution)/shard_map/ppermute | solution.py:35
  19.9 5.9 %collective-permute-start.12 = (f32[384,128]{1,0:T(8,128)S(1)}, f32[384,128]{1,0:T(8,128)S(1)}, u32[]{:S(2)}, u32[]{:S(2)}) collective-permute-start(f32[384,128]{1,0:T(8,128)S(1)} %add.41.refs_0_.tail_ref.own_ref), channel_id=1, source_target_pairs={{0,4},{4,0},{8,12},{12,8},{16,20},{20,16},{24,28},{28,24},{1,5},{5... | collective-permute-start | bytes 589832 | tf_op jit(solution)/shard_map/ppermute | solution.py:35
  21.4 2.0 %collective-permute-start.11 = (f32[192,128]{1,0:T(8,128)S(1)}, f32[192,128]{1,0:T(8,128)S(1)}, u32[]{:S(2)}, u32[]{:S(2)}) collective-permute-start(f32[192,128]{1,0:T(8,128)S(1)} %slice.37), channel_id=1, source_target_pairs={{0,1},{1,0},{2,3},{3,2},{4,5},{5,4},{6,7},{7,6},{8,9},{9,8},{10,11... | collective-permute-start | bytes 294920 | tf_op jit(solution)/shard_map/ppermute | solution.py:35
  21.5 7.7 %collective-permute-start.3 = (f32[320,128]{1,0:T(8,128)S(1)}, f32[320,128]{1,0:T(8,128)S(1)}, u32[]{:S(2)}, u32[]{:S(2)}) collective-permute-start(f32[320,128]{1,0:T(8,128)S(1)} %add.39.first_ref), channel_id=1, source_target_pairs={{0,8},{4,12},{8,0},{12,4},{16,24},{20,28},{24,16},{28,20},{1,9},{5... | collective-permute-start | bytes 491528 | tf_op jit(solution)/shard_map/ppermute | solution.py:35
  23.2 7.3 %collective-permute-start.14 = (f32[256,128]{1,0:T(8,128)S(1)}, f32[256,128]{1,0:T(8,128)S(1)}, u32[]{:S(2)}, u32[]{:S(2)}) collective-permute-start(f32[256,128]{1,0:T(8,128)S(1)} %slice.39), channel_id=1, source_target_pairs={{0,1},{1,0},{2,3},{3,2},{4,5},{5,4},{6,7},{7,6},{8,9},{9,8},{10,11... | collective-permute-start | bytes 393224 | tf_op jit(solution)/shard_map/ppermute | solution.py:35
  27.1 5.7 %collective-permute-start.19 = (f32[192,128]{1,0:T(8,128)S(1)}, f32[192,128]{1,0:T(8,128)S(1)}, u32[]{:S(2)}, u32[]{:S(2)}) collective-permute-start(f32[192,128]{1,0:T(8,128)S(1)} %shard_map.44.refs_0_), channel_id=1, source_target_pairs={{0,4},{4,0},{8,12},{12,8},{16,20},{20,16},{24,28},{28,24},{1,5},{5... | collective-permute-start | bytes 294920 | tf_op jit(solution)/shard_map/ppermute | solution.py:35
  28.7 7.4 %collective-permute-start.17 = (f32[384,128]{1,0:T(8,128)S(1)}, f32[384,128]{1,0:T(8,128)S(1)}, u32[]{:S(2)}, u32[]{:S(2)}) collective-permute-start(f32[384,128]{1,0:T(8,128)S(1)} %shard_map.45.refs_0_), channel_id=1, source_target_pairs={{0,4},{4,0},{8,12},{12,8},{16,20},{20,16},{24,28},{28,24},{1,5},{5... | collective-permute-start | bytes 589832 | tf_op jit(solution)/shard_map/ppermute | solution.py:35
  29.3 7.6 %collective-permute-start.13 = (f32[320,128]{1,0:T(8,128)S(1)}, f32[320,128]{1,0:T(8,128)S(1)}, u32[]{:S(2)}, u32[]{:S(2)}) collective-permute-start(f32[320,128]{1,0:T(8,128)S(1)} %shard_map.46), channel_id=1, source_target_pairs={{0,2},{1,3},{2,0},{3,1},{4,6},{5,7},{6,4},{7,5},{8,10},{9,11},{10,... | collective-permute-start | bytes 491528 | tf_op jit(solution)/shard_map/ppermute | solution.py:35
  30.9 7.7 %collective-permute-start.15 = (f32[320,128]{1,0:T(8,128)S(1)}, f32[320,128]{1,0:T(8,128)S(1)}, u32[]{:S(2)}, u32[]{:S(2)}) collective-permute-start(f32[320,128]{1,0:T(8,128)S(1)} %shard_map.47), channel_id=1, source_target_pairs={{0,8},{4,12},{8,0},{12,4},{16,24},{20,28},{24,16},{28,20},{1,9},{5... | collective-permute-start | bytes 491528 | tf_op jit(solution)/shard_map/ppermute | solution.py:35
  32.8 5.8 %collective-permute-start.20 = (f32[192,128]{1,0:T(8,128)S(1)}, f32[192,128]{1,0:T(8,128)S(1)}, u32[]{:S(2)}, u32[]{:S(2)}) collective-permute-start(f32[192,128]{1,0:T(8,128)S(1)} %add.48.own_ref), channel_id=1, source_target_pairs={{0,8},{4,12},{8,0},{12,4},{16,24},{20,28},{24,16},{28,20},{1,9},{5... | collective-permute-start | bytes 294920 | tf_op jit(solution)/shard_map/ppermute | solution.py:35
  34.5 6.0 %collective-permute-start.21 = (f32[192,128]{1,0:T(8,128)S(1)}, f32[192,128]{1,0:T(8,128)S(1)}, u32[]{:S(2)}, u32[]{:S(2)}) collective-permute-start(f32[192,128]{1,0:T(8,128)S(1)} %add.48.own_ref), channel_id=1, source_target_pairs={{0,1},{1,0},{2,3},{3,2},{4,5},{5,4},{6,7},{7,6},{8,9},{9,8},{10,11... | collective-permute-start | bytes 294920 | tf_op jit(solution)/shard_map/ppermute | solution.py:35
  36.1 7.0 %collective-permute-start.18 = (f32[384,128]{1,0:T(8,128)S(1)}, f32[384,128]{1,0:T(8,128)S(1)}, u32[]{:S(2)}, u32[]{:S(2)}) collective-permute-start(f32[384,128]{1,0:T(8,128)S(1)} %add.47.r_own_ref.own_ref), channel_id=1, source_target_pairs={{0,8},{4,12},{8,0},{12,4},{16,24},{20,28},{24,16},{28,20},{1,9},{5... | collective-permute-start | bytes 589832 | tf_op jit(solution)/shard_map/ppermute | solution.py:35
  36.9 3.7 %collective-permute-start.23 = (f32[256,128]{1,0:T(8,128)S(1)}, f32[256,128]{1,0:T(8,128)S(1)}, u32[]{:S(2)}, u32[]{:S(2)}) collective-permute-start(f32[256,128]{1,0:T(8,128)S(1)} %slice.41), channel_id=1, source_target_pairs={{0,1},{1,0},{2,3},{3,2},{4,5},{5,4},{6,7},{7,6},{8,9},{9,8},{10,11... | collective-permute-start | bytes 393224 | tf_op jit(solution)/shard_map/ppermute | solution.py:35
  38.6 1.9 %collective-permute-start.22 = (f32[192,128]{1,0:T(8,128)S(1)}, f32[192,128]{1,0:T(8,128)S(1)}, u32[]{:S(2)}, u32[]{:S(2)}) collective-permute-start(f32[192,128]{1,0:T(8,128)S(1)} %collective-permute-done.20.sib_ref), channel_id=1, source_target_pairs={{0,1},{1,0},{2,3},{3,2},{4,5},{5,4},{6,7},{7,6},{8,9},{9,8},{10,11... | collective-permute-start | bytes 294920 | tf_op jit(solution)/shard_map/ppermute | solution.py:35
  38.7 6.8 %collective-permute-start.16 = (f32[320,128]{1,0:T(8,128)S(1)}, f32[320,128]{1,0:T(8,128)S(1)}, u32[]{:S(2)}, u32[]{:S(2)}) collective-permute-start(f32[320,128]{1,0:T(8,128)S(1)} %add_subtract_fusion.1), channel_id=1, source_target_pairs={{0,4},{4,0},{8,12},{12,8},{16,20},{20,16},{24,28},{28,24},{1,5},{5... | collective-permute-start | bytes 491528 | tf_op jit(solution)/shard_map/ppermute | solution.py:35
  43.1 1.5 %collective-permute-start.24 = (f32[256,128]{1,0:T(8,128)S(1)}, f32[256,128]{1,0:T(8,128)S(1)}, u32[]{:S(2)}, u32[]{:S(2)}) collective-permute-start(f32[256,128]{1,0:T(8,128)S(1)} %shard_map.49.sib_ref), channel_id=1, source_target_pairs={{0,1},{1,0},{2,3},{3,2},{4,5},{5,4},{6,7},{7,6},{8,9},{9,8},{10,11... | collective-permute-start | bytes 393224 | tf_op jit(solution)/shard_map/ppermute | solution.py:35
  43.4 5.0 %collective-permute-start.28 = (f32[640,128]{1,0:T(8,128)S(1)}, f32[640,128]{1,0:T(8,128)S(1)}, u32[]{:S(2)}, u32[]{:S(2)}) collective-permute-start(f32[640,128]{1,0:T(8,128)S(1)} %get-tuple-element.37.z_ref.z0_ref), channel_id=1, source_target_pairs={{0,1},{1,0},{2,3},{3,2},{4,5},{5,4},{6,7},{7,6},{8,9},{9,8},{10,11... | collective-permute-start | bytes 983048 | tf_op jit(solution)/shard_map/ppermute | solution.py:35
  45.5 2.9 %collective-permute-start.27 = (f32[384,128]{1,0:T(8,128)S(1)}, f32[384,128]{1,0:T(8,128)S(1)}, u32[]{:S(2)}, u32[]{:S(2)}) collective-permute-start(f32[384,128]{1,0:T(8,128)S(1)} %shard_map.52), channel_id=1, source_target_pairs={{0,1},{1,0},{2,3},{3,2},{4,5},{5,4},{6,7},{7,6},{8,9},{9,8},{10,11... | collective-permute-start | bytes 589832 | tf_op jit(solution)/shard_map/ppermute | solution.py:35
  45.6 11.0 %collective-permute-start.26 = (f32[320,128]{1,0:T(8,128)S(1)}, f32[320,128]{1,0:T(8,128)S(1)}, u32[]{:S(2)}, u32[]{:S(2)}) collective-permute-start(f32[320,128]{1,0:T(8,128)S(1)} %add_subtract_fusion.refs_0_.own_ref), channel_id=1, source_target_pairs={{0,16},{4,20},{8,24},{12,28},{16,0},{20,4},{24,8},{28,12},{1,17},{... | collective-permute-start | bytes 491528 | tf_op jit(solution)/shard_map/ppermute | solution.py:35
  48.2 8.5 %collective-permute-start.25 = (f32[320,128]{1,0:T(8,128)S(1)}, f32[320,128]{1,0:T(8,128)S(1)}, u32[]{:S(2)}, u32[]{:S(2)}) collective-permute-start(f32[320,128]{1,0:T(8,128)S(1)} %add_subtract_fusion.refs_0_.own_ref), channel_id=1, source_target_pairs={{0,1},{1,0},{2,3},{3,2},{4,5},{5,4},{6,7},{7,6},{8,9},{9,8},{10,11... | collective-permute-start | bytes 491528 | tf_op jit(solution)/shard_map/ppermute | solution.py:35
  56.6 1.5 %collective-permute-start.29 = (f32[320,128]{1,0:T(8,128)S(1)}, f32[320,128]{1,0:T(8,128)S(1)}, u32[]{:S(2)}, u32[]{:S(2)}) collective-permute-start(f32[320,128]{1,0:T(8,128)S(1)} %shard_map.54.sib_ref), channel_id=1, source_target_pairs={{0,1},{1,0},{2,3},{3,2},{4,5},{5,4},{6,7},{7,6},{8,9},{9,8},{10,11... | collective-permute-start | bytes 491528 | tf_op jit(solution)/shard_map/ppermute | solution.py:35

commit v16 on v15

--- a/solution.py
+++ b/solution.py
@@ -15,7 +15,7 @@
 TOLERANCE = 1e-7
 DIVERGED = 1e4
 FIRST_FLOPS = 6.5e8
-INVERT_FLOPS = 9e8
+INVERT_FLOPS = 5e8
 INVERT_SECOND = 9e8
 MIDDLE_FLOPS = 0
 CROSS_FLOPS = 0
@@ -443,8 +443,8 @@
     parts = [(keep, swap(send, "sub", 0)) for keep, send in zip(parts[::2], parts[1::2])]
     head = over_child(head)
     tail = over_child(parts[0][0] + parts[0][1])
-    near = over_child(call(add_kernel, struct(SYM + RANK + HALF), 0, core, *parts[1], after=(tail,)))
     third = parts[2][0] + parts[2][1]
+    near = over_child(call(add_kernel, struct(SYM + RANK + HALF), 0, core, *parts[1], after=(third,)))
 
     head_sib = swap(head, "rows", span_bits)
     tail_sib = swap(tail, "rows", span_bits)

time: 62.1 us -> 62.3 us (level)
  transfers between devices with their start and end apart: 30 -> 30, of which waited for: 10 -> 10; matrix products, arithmetic and copies ran while one was open for 1% -> 0% of each run, Pallas kernels for 21% -> 21%
where the time goes in v16:
time: 62.3 us; the launch traced here: 62.2 us
  starting transfers between devices  25.3 us (41%)
  Pallas kernels  19.6 us (31%)
  waiting for transfers between devices  16.5 us (26%)
    ppermute x30, starting transfers between devices, swap(): return lax.ppermute(value, axis, pairs)  25.3 us
    ppermute x30, waiting for transfers between devices, swap(): return lax.ppermute(value, axis, pairs)  16.5 us
    pallas_call x15, Pallas kernels, call(): pl.pallas_call(kernel, in_specs=[SMEM] + [VMEM] * (len(values) - 1) + [AN...  9.64 us
    pallas_call x3, Pallas kernels, products(): pl.pallas_call(functools.partial(product_kernel, groups, chunks), in_spec...  6.21 us
    pallas_call x1, Pallas kernels, on_device(): pl.pallas_call(final_kernel, in_specs=[SMEM] + [VMEM] * len(small), out_s...  3.73 us
  transfers between devices with their start and end apart: 30, of which 10 were waited for; matrix products, arithmetic and copies ran while one was open for 0% of the time, Pallas kernels for 21%

profile of v16, /device:TPU:0, one launch (start us, length us, event | category | flops | bytes accessed | tf_op | source)
XLA Modules:
  0.0 62.2 jit_solution(5248554397541541321)
XLA Ops:
  0.0 2.6 %shard_map.37 = (f32[448,128]{1,0:T(8,128)S(1)}, f32[448,128]{1,0:T(8,128)S(1)}) custom-call(s32[1]{0:T(128)} %bitcast.core_ref, f32[3,1024,256]{2,1,0:T(8,128)} %gens_ref.5, f32[3,1024,256]{2,1,0:T(8,128)} %solved_ref.7), custom_call_target="tpu_custom_call" | custom-call | flops 805306368 | bytes 3145728 | tf_op jit(solution)/shard_map/pallas_call | solution.py:220
  2.7 0.5 collective-permute-start
  3.2 1.1 %collective-permute-done = f32[448,128]{1,0:T(8,128)S(1)} collective-permute-done((f32[448,128]{1,0:T(8,128)S(1)}, f32[448,128]{1,0:T(8,128)S(1)}, u32[]{:S(2)}, u32[]{:S(2)}) %collective-permute-start) | collective-permute-done | bytes 229408 | tf_op jit(solution)/shard_map/ppermute | solution.py:35
  4.3 0.4 collective-permute-start.1
  4.8 2.7 %collective-permute-start.6 = (f32[448,128]{1,0:T(8,128)S(1)}, f32[448,128]{1,0:T(8,128)S(1)}, u32[]{:S(2)}, u32[]{:S(2)}) collective-permute-start(f32[448,128]{1,0:T(8,128)S(1)} %add.38.refs_0_), channel_id=1, source_target_pairs={{0,2},{1,3},{2,0},{3,1},{4,6},{5,7},{6,4},{7,5},{8,10},{9,11},{10,... | collective-permute-start | bytes 688136 | tf_op jit(solution)/shard_map/ppermute | solution.py:35
  7.4 0.0 collective-permute-done.1.refs_1_
  7.5 1.2 %shard_map.39 = (f32[384,128]{1,0:T(8,128)S(1)}, f32[384,128]{1,0:T(8,128)S(1)}) custom-call(s32[1]{0:T(128)} %bitcast.core_ref, f32[3,1024,256]{2,1,0:T(8,128)S(1)} %copy-done.1, f32[3,1024,256]{2,1,0:T(8,128)S(1)} %copy-done, f32[1024,128]{1,0:T(8,128)S(1)} %copy-done.2, f32[8,128]{1,0:T(8,128)S(1)} %collective-permute-done.1.refs_1_), custom_call_target="tpu_custom_call" | custom-call | flops 603979776 | bytes 2621440 | tf_op jit(solution)/shard_map/pallas_call | solution.py:220
  8.6 0.1 collective-permute-start.10
  8.8 2.4 %shard_map.40 = (f32[576,128]{1,0:T(8,128)S(1)}, f32[576,128]{1,0:T(8,128)S(1)}, f32[320,128]{1,0:T(8,128)S(1)}, f32[320,128]{1,0:T(8,128)S(1)}) custom-call(s32[1]{0:T(128)} %bitcast.core_ref, f32[3,1024,256]{2,1,0:T(8,128)S(1)} %copy-done.1, f32[3,1024,256]{2,1,0:T(8,128)S(1)} %copy-done, f32[1024,128]{1,0:T(8,128)S(1)} %copy-done.2, ...), custom_call_target="tpu_custom_call" | custom-call | flops 1610612736 | bytes 4718592 | tf_op jit(solution)/shard_map/pallas_call | solution.py:220
  11.2 0.5 collective-permute-start.4
  11.7 0.1 collective-permute-start.2
  11.8 0.0 collective-permute-done.10
  11.8 1.2 %collective-permute-start.11 = (f32[384,128]{1,0:T(8,128)S(1)}, f32[384,128]{1,0:T(8,128)S(1)}, u32[]{:S(2)}, u32[]{:S(2)}) collective-permute-start(f32[384,128]{1,0:T(8,128)S(1)} %add.42), channel_id=1, source_target_pairs={{0,2},{1,3},{2,0},{3,1},{4,6},{5,7},{6,4},{7,5},{8,10},{9,11},{10,... | collective-permute-start | bytes 589832 | tf_op jit(solution)/shard_map/ppermute | solution.py:35
  12.9 0.6 %collective-permute-done.6 = f32[448,128]{1,0:T(8,128)S(1)} collective-permute-done((f32[448,128]{1,0:T(8,128)S(1)}, f32[448,128]{1,0:T(8,128)S(1)}, u32[]{:S(2)}, u32[]{:S(2)}) %collective-permute-start.6) | collective-permute-done | bytes 229408 | tf_op jit(solution)/shard_map/ppermute | solution.py:35
  13.6 1.8 %collective-permute-start.7 = (f32[448,128]{1,0:T(8,128)S(1)}, f32[448,128]{1,0:T(8,128)S(1)}, u32[]{:S(2)}, u32[]{:S(2)}) collective-permute-start(f32[448,128]{1,0:T(8,128)S(1)} %add.41.own_ref.head_ref), channel_id=1, source_target_pairs={{0,4},{4,0},{8,12},{12,8},{16,20},{20,16},{24,28},{28,24},{1,5},{5... | collective-permute-start | bytes 688136 | tf_op jit(solution)/shard_map/ppermute | solution.py:35
  15.4 0.0 collective-permute-start.8
  15.4 0.0 collective-permute-done.2
  15.4 0.0 collective-permute-done.4.second_ref
  15.5 1.6 %collective-permute-start.5 = (f32[576,128]{1,0:T(8,128)S(1)}, f32[576,128]{1,0:T(8,128)S(1)}, u32[]{:S(2)}, u32[]{:S(2)}) collective-permute-start(f32[576,128]{1,0:T(8,128)S(1)} %shard_map.41), channel_id=1, source_target_pairs={{0,2},{1,3},{2,0},{3,1},{4,6},{5,7},{6,4},{7,5},{8,10},{9,11},{10,... | collective-permute-start | bytes 884744 | tf_op jit(solution)/shard_map/ppermute | solution.py:35
  17.1 2.5 %collective-permute-done.11 = f32[384,128]{1,0:T(8,128)S(1)} collective-permute-done((f32[384,128]{1,0:T(8,128)S(1)}, f32[384,128]{1,0:T(8,128)S(1)}, u32[]{:S(2)}, u32[]{:S(2)}) %collective-permute-start.11) | collective-permute-done | bytes 196640 | tf_op jit(solution)/shard_map/ppermute | solution.py:35
  19.6 1.6 %collective-permute-start.12 = (f32[384,128]{1,0:T(8,128)S(1)}, f32[384,128]{1,0:T(8,128)S(1)}, u32[]{:S(2)}, u32[]{:S(2)}) collective-permute-start(f32[384,128]{1,0:T(8,128)S(1)} %add.43.tail_ref.own_ref), channel_id=1, source_target_pairs={{0,4},{4,0},{8,12},{12,8},{16,20},{20,16},{24,28},{28,24},{1,5},{5... | collective-permute-start | bytes 589832 | tf_op jit(solution)/shard_map/ppermute | solution.py:35
  21.2 0.1 collective-permute-start.9
  21.3 1.6 %collective-permute-start.3 = (f32[320,128]{1,0:T(8,128)S(1)}, f32[320,128]{1,0:T(8,128)S(1)}, u32[]{:S(2)}, u32[]{:S(2)}) collective-permute-start(f32[320,128]{1,0:T(8,128)S(1)} %add.39.refs_0_.first_ref), channel_id=1, source_target_pairs={{0,8},{4,12},{8,0},{12,4},{16,24},{20,28},{24,16},{28,20},{1,9},{5... | collective-permute-start | bytes 491528 | tf_op jit(solution)/shard_map/ppermute | solution.py:35
  22.9 0.0 collective-permute-done.8.own_other_ref.head_other_ref
  22.9 0.2 collective-permute-start.14
  23.1 0.0 collective-permute-done.9.sib_other_ref
  23.1 2.3 %shard_map.42 = (f32[256,256]{1,0:T(8,128)S(1)}, f32[256,320]{1,0:T(8,128)S(1)}) custom-call(s32[1]{0:T(128)} %bitcast.core_ref, f32[448,128]{1,0:T(8,128)S(1)} %add.41.own_ref.head_ref, f32[448,128]{1,0:T(8,128)S(1)} %collective-permute-done.7.sib_ref.head_sib_ref, f32[448,128]{1,0:T(8,128)S(1)} %collective-permute-done.8.own_other_ref.head_other_ref, ...), custom_call_target="tpu_custom_call" | custom-call | flops 500000000 | bytes 1572868 | tf_op jit(solution)/shard_map/pallas_call | solution.py:309
  25.4 0.2 collective-permute-done.12.tail_sib_ref
  25.7 0.8 %shard_map.43 = (f32[640,128]{1,0:T(8,128)S(1)}, f32[576,128]{1,0:T(8,128)S(1)}) custom-call(s32[1]{0:T(128)} %bitcast.core_ref, f32[256,256]{1,0:T(8,128)S(1)} %get-tuple-element.34.inverse_ref, f32[256,320]{1,0:T(8,128)S(1)} %get-tuple-element.35.product_ref, f32[448,128]{1,0:T(8,128)S(1)} %add.41.own_ref.head_ref, ...), custom_call_target="tpu_custom_call" | custom-call | flops 650000000 | bytes 2097156 | tf_op jit(solution)/shard_map/pallas_call | solution.py:309
  26.5 0.0 collective-permute-done.5
  26.6 1.6 %collective-permute-start.19 = (f32[192,128]{1,0:T(8,128)S(1)}, f32[192,128]{1,0:T(8,128)S(1)}, u32[]{:S(2)}, u32[]{:S(2)}) collective-permute-start(f32[192,128]{1,0:T(8,128)S(1)} %shard_map.44.refs_0_), channel_id=1, source_target_pairs={{0,4},{4,0},{8,12},{12,8},{16,20},{20,16},{24,28},{28,24},{1,5},{5... | collective-permute-start | bytes 294920 | tf_op jit(solution)/shard_map/ppermute | solution.py:35
  28.2 0.6 collective-permute-start.17
  28.8 0.0 collective-permute-done.3.second_ref
  28.8 1.2 %collective-permute-start.13 = (f32[320,128]{1,0:T(8,128)S(1)}, f32[320,128]{1,0:T(8,128)S(1)}, u32[]{:S(2)}, u32[]{:S(2)}) collective-permute-start(f32[320,128]{1,0:T(8,128)S(1)} %shard_map.46), channel_id=1, source_target_pairs={{0,2},{1,3},{2,0},{3,1},{4,6},{5,7},{6,4},{7,5},{8,10},{9,11},{10,... | collective-permute-start | bytes 491528 | tf_op jit(solution)/shard_map/ppermute | solution.py:35
  30.1 0.0 collective-permute-done.14.own_other_ref
  30.1 0.4 shard_map.47
  30.5 1.5 %collective-permute-start.15 = (f32[320,128]{1,0:T(8,128)S(1)}, f32[320,128]{1,0:T(8,128)S(1)}, u32[]{:S(2)}, u32[]{:S(2)}) collective-permute-start(f32[320,128]{1,0:T(8,128)S(1)} %shard_map.47), channel_id=1, source_target_pairs={{0,8},{4,12},{8,0},{12,4},{16,24},{20,28},{24,16},{28,20},{1,9},{5... | collective-permute-start | bytes 491528 | tf_op jit(solution)/shard_map/ppermute | solution.py:35
  32.0 0.4 collective-permute-done.19
  32.4 1.6 %collective-permute-start.20 = (f32[192,128]{1,0:T(8,128)S(1)}, f32[192,128]{1,0:T(8,128)S(1)}, u32[]{:S(2)}, u32[]{:S(2)}) collective-permute-start(f32[192,128]{1,0:T(8,128)S(1)} %add.48.own_ref), channel_id=1, source_target_pairs={{0,8},{4,12},{8,0},{12,4},{16,24},{20,28},{24,16},{28,20},{1,9},{5... | collective-permute-start | bytes 294920 | tf_op jit(solution)/shard_map/ppermute | solution.py:35
  34.0 0.0 collective-permute-start.21
  34.0 1.8 %collective-permute-done.17 = f32[384,128]{1,0:T(8,128)S(1)} collective-permute-done((f32[384,128]{1,0:T(8,128)S(1)}, f32[384,128]{1,0:T(8,128)S(1)}, u32[]{:S(2)}, u32[]{:S(2)}) %collective-permute-start.17) | collective-permute-done | bytes 196640 | tf_op jit(solution)/shard_map/ppermute | solution.py:35
  35.8 0.9 %collective-permute-start.18 = (f32[384,128]{1,0:T(8,128)S(1)}, f32[384,128]{1,0:T(8,128)S(1)}, u32[]{:S(2)}, u32[]{:S(2)}) collective-permute-start(f32[384,128]{1,0:T(8,128)S(1)} %add.47.r_own_ref.own_ref), channel_id=1, source_target_pairs={{0,8},{4,12},{8,0},{12,4},{16,24},{20,28},{24,16},{28,20},{1,9},{5... | collective-permute-start | bytes 589832 | tf_op jit(solution)/shard_map/ppermute | solution.py:35
  36.7 2.0 %collective-permute-done.20.sib_ref = f32[192,128]{1,0:T(8,128)S(1)} collective-permute-done((f32[192,128]{1,0:T(8,128)S(1)}, f32[192,128]{1,0:T(8,128)S(1)}, u32[]{:S(2)}, u32[]{:S(2)}) %collective-permute-start.20) | collective-permute-done | bytes 98336 | tf_op jit(solution)/shard_map/ppermute | solution.py:35
  38.7 0.0 collective-permute-done.15
  38.8 2.0 %collective-permute-start.16 = (f32[320,128]{1,0:T(8,128)S(1)}, f32[320,128]{1,0:T(8,128)S(1)}, u32[]{:S(2)}, u32[]{:S(2)}) collective-permute-start(f32[320,128]{1,0:T(8,128)S(1)} %add_subtract_fusion.1), channel_id=1, source_target_pairs={{0,4},{4,0},{8,12},{12,8},{16,20},{20,16},{24,28},{28,24},{1,5},{5... | collective-permute-start | bytes 491528 | tf_op jit(solution)/shard_map/ppermute | solution.py:35
  40.8 0.0 collective-permute-done.21.own_other_ref
  40.8 2.5 %shard_map.48 = (f32[256,256]{1,0:T(8,128)S(1)}, f32[256,192]{1,0:T(8,128)S(1)}, f32[512,256]{1,0:T(8,128)S(1)}) custom-call(s32[1]{0:T(128)} %bitcast.core_ref, f32[192,128]{1,0:T(8,128)S(1)} %add.48.own_ref, f32[192,128]{1,0:T(8,128)S(1)} %collective-permute-done.20.sib_ref, f32[192,128]{1,0:T(8,128)S(1)} %collective-permute-done.21.own_other_ref, ...), custom_call_target="tpu_custom_call" | custom-call | flops 900000000 | bytes 1703940 | tf_op jit(solution)/shard_map/pallas_call | solution.py:309
  43.3 0.3 collective-permute-start.24
  43.6 0.3 collective-permute-start.28
  43.9 0.9 %shard_map.50 = (f32[384,128]{1,0:T(8,128)S(1)}, f32[384,128]{1,0:T(8,128)S(1)}, f32[320,128]{1,0:T(8,128)S(1)}) custom-call(s32[1]{0:T(128)} %bitcast.core_ref, f32[256,256]{1,0:T(8,128)S(1)} %get-tuple-element.38.refs_0_.inverse_ref, f32[256,192]{1,0:T(8,128)S(1)} %get-tuple-element.39.product_ref, f32[512,256]{1,0:T(8,128)S(1)} %get-tuple-element.40.turned_ref, ...), custom_call_target="tpu_custom_call" | custom-call | bytes 1933316 | tf_op jit(solution)/shard_map/pallas_call | solution.py:309
  44.8 0.0 collective-permute-done.24.sib_other_ref
  44.8 0.4 shard_map.51
  45.2 0.4 collective-permute-done.16
  45.7 0.1 collective-permute-start.27
  45.8 2.7 %collective-permute-start.26 = (f32[320,128]{1,0:T(8,128)S(1)}, f32[320,128]{1,0:T(8,128)S(1)}, u32[]{:S(2)}, u32[]{:S(2)}) collective-permute-start(f32[320,128]{1,0:T(8,128)S(1)} %add_subtract_fusion.refs_0_.own_ref), channel_id=1, source_target_pairs={{0,16},{4,20},{8,24},{12,28},{16,0},{20,4},{24,8},{28,12},{1,17},{... | collective-permute-start | bytes 491528 | tf_op jit(solution)/shard_map/ppermute | solution.py:35
  48.4 0.2 collective-permute-start.25
  48.6 0.0 collective-permute-done.28.z0_other_ref
  48.6 0.0 collective-permute-done.27.z1_other_ref
  48.6 2.2 %shard_map.53 = (bf16[1024,256]{1,0:T(8,128)(2,1)S(1)}, bf16[1024,256]{1,0:T(8,128)(2,1)S(1)}, f32[1024,128]{1,0:T(8,128)S(1)}) custom-call(s32[1]{0:T(128)} %bitcast.core_ref, f32[384,128]{1,0:T(8,128)S(1)} %get-tuple-element.43.value_ref.z1_ref, f32[384,128]{1,0:T(8,128)S(1)} %collective-permute-done.27.z1_other_ref, ...), custom_call_target="tpu_custom_call" | custom-call | flops 1207959552 | bytes 7340036 | tf_op jit(solution)/shard_map/pallas_call | solution.py:309
  50.8 6.0 %collective-permute-done.26.value_ref = f32[320,128]{1,0:T(8,128)S(1)} collective-permute-done((f32[320,128]{1,0:T(8,128)S(1)}, f32[320,128]{1,0:T(8,128)S(1)}, u32[]{:S(2)}, u32[]{:S(2)}) %collective-permute-start.26) | collective-permute-done | bytes 163872 | tf_op jit(solution)/shard_map/ppermute | solution.py:35
  56.8 0.1 collective-permute-start.29
  56.9 0.0 collective-permute-done.25.own_other_ref
  56.9 1.4 %collective-permute-done.29.sib_other_ref = f32[320,128]{1,0:T(8,128)S(1)} collective-permute-done((f32[320,128]{1,0:T(8,128)S(1)}, f32[320,128]{1,0:T(8,128)S(1)}, u32[]{:S(2)}, u32[]{:S(2)}) %collective-permute-start.29) | collective-permute-done | bytes 163872 | tf_op jit(solution)/shard_map/ppermute | solution.py:35
  58.3 3.7 %shard_map.55 = f32[1024,128]{1,0:T(8,128)} custom-call(s32[1]{0:T(128)} %bitcast.core_ref, f32[320,128]{1,0:T(8,128)S(1)} %add_subtract_fusion.refs_0_.own_ref, f32[320,128]{1,0:T(8,128)S(1)} %collective-permute-done.25.own_other_ref, f32[320,128]{1,0:T(8,128)S(1)} %shard_map.54.sib_ref, f32[320,128]{1,0:T(8,128)S(1)} %collective-permute-done.29.sib_other_ref, ...), custom_call_target="tpu_custom_call" | custom-call | flops 1107296256 | bytes 3145728 | tf_op jit(solution)/shard_map/pallas_call | solution.py:502
  (40 shorter events, 0.5 us)
Async XLA Ops:
  0.0 7.5 %copy-start = (f32[3,1024,256]{2,1,0:T(8,128)S(1)}, f32[3,1024,256]{2,1,0:T(8,128)}, u32[]{:S(2)}) copy-start(f32[3,1024,256]{2,1,0:T(8,128)} %solved_ref.7) | copy-start | bytes 9437188
  0.0 7.5 %copy-start.1 = (f32[3,1024,256]{2,1,0:T(8,128)S(1)}, f32[3,1024,256]{2,1,0:T(8,128)}, u32[]{:S(2)}) copy-start(f32[3,1024,256]{2,1,0:T(8,128)} %gens_ref.5) | copy-start | bytes 9437188
  0.0 7.5 %copy-start.2 = (f32[1024,128]{1,0:T(8,128)S(1)}, f32[1024,128]{1,0:T(8,128)}, u32[]{:S(2)}) copy-start(f32[1024,128]{1,0:T(8,128)} %rhs_ref.1) | copy-start | bytes 1572868
  2.7 1.6 %collective-permute-start = (f32[448,128]{1,0:T(8,128)S(1)}, f32[448,128]{1,0:T(8,128)S(1)}, u32[]{:S(2)}, u32[]{:S(2)}) collective-permute-start(f32[448,128]{1,0:T(8,128)S(1)} %get-tuple-element.26), channel_id=1, source_target_pairs={{0,1},{1,0},{2,3},{3,2},{4,5},{5,4},{6,7},{7,6},{8,9},{9,8},{10,11... | collective-permute-start | bytes 688136 | tf_op jit(solution)/shard_map/ppermute | solution.py:35
  4.3 3.1 %collective-permute-start.1 = (f32[8,128]{1,0:T(8,128)S(1)}, f32[8,128]{1,0:T(8,128)S(1)}, u32[]{:S(2)}, u32[]{:S(2)}) collective-permute-start(f32[8,128]{1,0:T(8,128)S(1)} %shard_map.38), channel_id=1, source_target_pairs={{0,1},{1,0},{2,3},{3,2},{4,5},{5,4},{6,7},{7,6},{8,9},{9,8},{10,11... | collective-permute-start | bytes 12296 | tf_op jit(solution)/shard_map/ppermute | solution.py:35
  4.8 8.8 %collective-permute-start.6 = (f32[448,128]{1,0:T(8,128)S(1)}, f32[448,128]{1,0:T(8,128)S(1)}, u32[]{:S(2)}, u32[]{:S(2)}) collective-permute-start(f32[448,128]{1,0:T(8,128)S(1)} %add.38.refs_0_), channel_id=1, source_target_pairs={{0,2},{1,3},{2,0},{3,1},{4,6},{5,7},{6,4},{7,5},{8,10},{9,11},{10,... | collective-permute-start | bytes 688136 | tf_op jit(solution)/shard_map/ppermute | solution.py:35
  8.6 3.1 %collective-permute-start.10 = (f32[384,128]{1,0:T(8,128)S(1)}, f32[384,128]{1,0:T(8,128)S(1)}, u32[]{:S(2)}, u32[]{:S(2)}) collective-permute-start(f32[384,128]{1,0:T(8,128)S(1)} %get-tuple-element.28.refs_1_), channel_id=1, source_target_pairs={{0,1},{1,0},{2,3},{3,2},{4,5},{5,4},{6,7},{7,6},{8,9},{9,8},{10,11... | collective-permute-start | bytes 589832 | tf_op jit(solution)/shard_map/ppermute | solution.py:35
  11.2 4.2 %collective-permute-start.4 = (f32[576,128]{1,0:T(8,128)S(1)}, f32[576,128]{1,0:T(8,128)S(1)}, u32[]{:S(2)}, u32[]{:S(2)}) collective-permute-start(f32[576,128]{1,0:T(8,128)S(1)} %get-tuple-element.32), channel_id=1, source_target_pairs={{0,1},{1,0},{2,3},{3,2},{4,5},{5,4},{6,7},{7,6},{8,9},{9,8},{10,11... | collective-permute-start | bytes 884744 | tf_op jit(solution)/shard_map/ppermute | solution.py:35
  11.7 3.7 %collective-permute-start.2 = (f32[320,128]{1,0:T(8,128)S(1)}, f32[320,128]{1,0:T(8,128)S(1)}, u32[]{:S(2)}, u32[]{:S(2)}) collective-permute-start(f32[320,128]{1,0:T(8,128)S(1)} %get-tuple-element.30), channel_id=1, source_target_pairs={{0,1},{1,0},{2,3},{3,2},{4,5},{5,4},{6,7},{7,6},{8,9},{9,8},{10,11... | collective-permute-start | bytes 491528 | tf_op jit(solution)/shard_map/ppermute | solution.py:35
  11.8 7.8 %collective-permute-start.11 = (f32[384,128]{1,0:T(8,128)S(1)}, f32[384,128]{1,0:T(8,128)S(1)}, u32[]{:S(2)}, u32[]{:S(2)}) collective-permute-start(f32[384,128]{1,0:T(8,128)S(1)} %add.42), channel_id=1, source_target_pairs={{0,2},{1,3},{2,0},{3,1},{4,6},{5,7},{6,4},{7,5},{8,10},{9,11},{10,... | collective-permute-start | bytes 589832 | tf_op jit(solution)/shard_map/ppermute | solution.py:35
  13.6 7.6 %collective-permute-start.7 = (f32[448,128]{1,0:T(8,128)S(1)}, f32[448,128]{1,0:T(8,128)S(1)}, u32[]{:S(2)}, u32[]{:S(2)}) collective-permute-start(f32[448,128]{1,0:T(8,128)S(1)} %add.41.own_ref.head_ref), channel_id=1, source_target_pairs={{0,4},{4,0},{8,12},{12,8},{16,20},{20,16},{24,28},{28,24},{1,5},{5... | collective-permute-start | bytes 688136 | tf_op jit(solution)/shard_map/ppermute | solution.py:35
  15.4 7.5 %collective-permute-start.8 = (f32[448,128]{1,0:T(8,128)S(1)}, f32[448,128]{1,0:T(8,128)S(1)}, u32[]{:S(2)}, u32[]{:S(2)}) collective-permute-start(f32[448,128]{1,0:T(8,128)S(1)} %add.41.own_ref.head_ref), channel_id=1, source_target_pairs={{0,1},{1,0},{2,3},{3,2},{4,5},{5,4},{6,7},{7,6},{8,9},{9,8},{10,11... | collective-permute-start | bytes 688136 | tf_op jit(solution)/shard_map/ppermute | solution.py:35
  15.5 11.1 %collective-permute-start.5 = (f32[576,128]{1,0:T(8,128)S(1)}, f32[576,128]{1,0:T(8,128)S(1)}, u32[]{:S(2)}, u32[]{:S(2)}) collective-permute-start(f32[576,128]{1,0:T(8,128)S(1)} %shard_map.41), channel_id=1, source_target_pairs={{0,2},{1,3},{2,0},{3,1},{4,6},{5,7},{6,4},{7,5},{8,10},{9,11},{10,... | collective-permute-start | bytes 884744 | tf_op jit(solution)/shard_map/ppermute | solution.py:35
  19.6 6.1 %collective-permute-start.12 = (f32[384,128]{1,0:T(8,128)S(1)}, f32[384,128]{1,0:T(8,128)S(1)}, u32[]{:S(2)}, u32[]{:S(2)}) collective-permute-start(f32[384,128]{1,0:T(8,128)S(1)} %add.43.tail_ref.own_ref), channel_id=1, source_target_pairs={{0,4},{4,0},{8,12},{12,8},{16,20},{20,16},{24,28},{28,24},{1,5},{5... | collective-permute-start | bytes 589832 | tf_op jit(solution)/shard_map/ppermute | solution.py:35
  21.2 2.0 %collective-permute-start.9 = (f32[192,128]{1,0:T(8,128)S(1)}, f32[192,128]{1,0:T(8,128)S(1)}, u32[]{:S(2)}, u32[]{:S(2)}) collective-permute-start(f32[192,128]{1,0:T(8,128)S(1)} %slice.37), channel_id=1, source_target_pairs={{0,1},{1,0},{2,3},{3,2},{4,5},{5,4},{6,7},{7,6},{8,9},{9,8},{10,11... | collective-permute-start | bytes 294920 | tf_op jit(solution)/shard_map/ppermute | solution.py:35
  21.3 7.6 %collective-permute-start.3 = (f32[320,128]{1,0:T(8,128)S(1)}, f32[320,128]{1,0:T(8,128)S(1)}, u32[]{:S(2)}, u32[]{:S(2)}) collective-permute-start(f32[320,128]{1,0:T(8,128)S(1)} %add.39.refs_0_.first_ref), channel_id=1, source_target_pairs={{0,8},{4,12},{8,0},{12,4},{16,24},{20,28},{24,16},{28,20},{1,9},{5... | collective-permute-start | bytes 491528 | tf_op jit(solution)/shard_map/ppermute | solution.py:35
  22.9 7.2 %collective-permute-start.14 = (f32[256,128]{1,0:T(8,128)S(1)}, f32[256,128]{1,0:T(8,128)S(1)}, u32[]{:S(2)}, u32[]{:S(2)}) collective-permute-start(f32[256,128]{1,0:T(8,128)S(1)} %slice.39), channel_id=1, source_target_pairs={{0,1},{1,0},{2,3},{3,2},{4,5},{5,4},{6,7},{7,6},{8,9},{9,8},{10,11... | collective-permute-start | bytes 393224 | tf_op jit(solution)/shard_map/ppermute | solution.py:35
  26.6 5.7 %collective-permute-start.19 = (f32[192,128]{1,0:T(8,128)S(1)}, f32[192,128]{1,0:T(8,128)S(1)}, u32[]{:S(2)}, u32[]{:S(2)}) collective-permute-start(f32[192,128]{1,0:T(8,128)S(1)} %shard_map.44.refs_0_), channel_id=1, source_target_pairs={{0,4},{4,0},{8,12},{12,8},{16,20},{20,16},{24,28},{28,24},{1,5},{5... | collective-permute-start | bytes 294920 | tf_op jit(solution)/shard_map/ppermute | solution.py:35
  28.2 7.5 %collective-permute-start.17 = (f32[384,128]{1,0:T(8,128)S(1)}, f32[384,128]{1,0:T(8,128)S(1)}, u32[]{:S(2)}, u32[]{:S(2)}) collective-permute-start(f32[384,128]{1,0:T(8,128)S(1)} %shard_map.45.refs_0_), channel_id=1, source_target_pairs={{0,4},{4,0},{8,12},{12,8},{16,20},{20,16},{24,28},{28,24},{1,5},{5... | collective-permute-start | bytes 589832 | tf_op jit(solution)/shard_map/ppermute | solution.py:35
  28.8 7.8 %collective-permute-start.13 = (f32[320,128]{1,0:T(8,128)S(1)}, f32[320,128]{1,0:T(8,128)S(1)}, u32[]{:S(2)}, u32[]{:S(2)}) collective-permute-start(f32[320,128]{1,0:T(8,128)S(1)} %shard_map.46), channel_id=1, source_target_pairs={{0,2},{1,3},{2,0},{3,1},{4,6},{5,7},{6,4},{7,5},{8,10},{9,11},{10,... | collective-permute-start | bytes 491528 | tf_op jit(solution)/shard_map/ppermute | solution.py:35
  30.5 8.2 %collective-permute-start.15 = (f32[320,128]{1,0:T(8,128)S(1)}, f32[320,128]{1,0:T(8,128)S(1)}, u32[]{:S(2)}, u32[]{:S(2)}) collective-permute-start(f32[320,128]{1,0:T(8,128)S(1)} %shard_map.47), channel_id=1, source_target_pairs={{0,8},{4,12},{8,0},{12,4},{16,24},{20,28},{24,16},{28,20},{1,9},{5... | collective-permute-start | bytes 491528 | tf_op jit(solution)/shard_map/ppermute | solution.py:35
  32.4 6.4 %collective-permute-start.20 = (f32[192,128]{1,0:T(8,128)S(1)}, f32[192,128]{1,0:T(8,128)S(1)}, u32[]{:S(2)}, u32[]{:S(2)}) collective-permute-start(f32[192,128]{1,0:T(8,128)S(1)} %add.48.own_ref), channel_id=1, source_target_pairs={{0,8},{4,12},{8,0},{12,4},{16,24},{20,28},{24,16},{28,20},{1,9},{5... | collective-permute-start | bytes 294920 | tf_op jit(solution)/shard_map/ppermute | solution.py:35
  34.0 6.8 %collective-permute-start.21 = (f32[192,128]{1,0:T(8,128)S(1)}, f32[192,128]{1,0:T(8,128)S(1)}, u32[]{:S(2)}, u32[]{:S(2)}) collective-permute-start(f32[192,128]{1,0:T(8,128)S(1)} %add.48.own_ref), channel_id=1, source_target_pairs={{0,1},{1,0},{2,3},{3,2},{4,5},{5,4},{6,7},{7,6},{8,9},{9,8},{10,11... | collective-permute-start | bytes 294920 | tf_op jit(solution)/shard_map/ppermute | solution.py:35
  35.8 7.5 %collective-permute-start.18 = (f32[384,128]{1,0:T(8,128)S(1)}, f32[384,128]{1,0:T(8,128)S(1)}, u32[]{:S(2)}, u32[]{:S(2)}) collective-permute-start(f32[384,128]{1,0:T(8,128)S(1)} %add.47.r_own_ref.own_ref), channel_id=1, source_target_pairs={{0,8},{4,12},{8,0},{12,4},{16,24},{20,28},{24,16},{28,20},{1,9},{5... | collective-permute-start | bytes 589832 | tf_op jit(solution)/shard_map/ppermute | solution.py:35
  36.7 4.1 %collective-permute-start.23 = (f32[256,128]{1,0:T(8,128)S(1)}, f32[256,128]{1,0:T(8,128)S(1)}, u32[]{:S(2)}, u32[]{:S(2)}) collective-permute-start(f32[256,128]{1,0:T(8,128)S(1)} %slice.41), channel_id=1, source_target_pairs={{0,1},{1,0},{2,3},{3,2},{4,5},{5,4},{6,7},{7,6},{8,9},{9,8},{10,11... | collective-permute-start | bytes 393224 | tf_op jit(solution)/shard_map/ppermute | solution.py:35
  38.7 2.0 %collective-permute-start.22 = (f32[192,128]{1,0:T(8,128)S(1)}, f32[192,128]{1,0:T(8,128)S(1)}, u32[]{:S(2)}, u32[]{:S(2)}) collective-permute-start(f32[192,128]{1,0:T(8,128)S(1)} %collective-permute-done.20.sib_ref), channel_id=1, source_target_pairs={{0,1},{1,0},{2,3},{3,2},{4,5},{5,4},{6,7},{7,6},{8,9},{9,8},{10,11... | collective-permute-start | bytes 294920 | tf_op jit(solution)/shard_map/ppermute | solution.py:35
  38.8 6.8 %collective-permute-start.16 = (f32[320,128]{1,0:T(8,128)S(1)}, f32[320,128]{1,0:T(8,128)S(1)}, u32[]{:S(2)}, u32[]{:S(2)}) collective-permute-start(f32[320,128]{1,0:T(8,128)S(1)} %add_subtract_fusion.1), channel_id=1, source_target_pairs={{0,4},{4,0},{8,12},{12,8},{16,20},{20,16},{24,28},{28,24},{1,5},{5... | collective-permute-start | bytes 491528 | tf_op jit(solution)/shard_map/ppermute | solution.py:35
  43.3 1.5 %collective-permute-start.24 = (f32[256,128]{1,0:T(8,128)S(1)}, f32[256,128]{1,0:T(8,128)S(1)}, u32[]{:S(2)}, u32[]{:S(2)}) collective-permute-start(f32[256,128]{1,0:T(8,128)S(1)} %shard_map.49.sib_ref), channel_id=1, source_target_pairs={{0,1},{1,0},{2,3},{3,2},{4,5},{5,4},{6,7},{7,6},{8,9},{9,8},{10,11... | collective-permute-start | bytes 393224 | tf_op jit(solution)/shard_map/ppermute | solution.py:35
  43.6 5.0 %collective-permute-start.28 = (f32[640,128]{1,0:T(8,128)S(1)}, f32[640,128]{1,0:T(8,128)S(1)}, u32[]{:S(2)}, u32[]{:S(2)}) collective-permute-start(f32[640,128]{1,0:T(8,128)S(1)} %get-tuple-element.37.z_ref.z0_ref), channel_id=1, source_target_pairs={{0,1},{1,0},{2,3},{3,2},{4,5},{5,4},{6,7},{7,6},{8,9},{9,8},{10,11... | collective-permute-start | bytes 983048 | tf_op jit(solution)/shard_map/ppermute | solution.py:35
  45.7 2.9 %collective-permute-start.27 = (f32[384,128]{1,0:T(8,128)S(1)}, f32[384,128]{1,0:T(8,128)S(1)}, u32[]{:S(2)}, u32[]{:S(2)}) collective-permute-start(f32[384,128]{1,0:T(8,128)S(1)} %shard_map.52), channel_id=1, source_target_pairs={{0,1},{1,0},{2,3},{3,2},{4,5},{5,4},{6,7},{7,6},{8,9},{9,8},{10,11... | collective-permute-start | bytes 589832 | tf_op jit(solution)/shard_map/ppermute | solution.py:35
  45.8 11.0 %collective-permute-start.26 = (f32[320,128]{1,0:T(8,128)S(1)}, f32[320,128]{1,0:T(8,128)S(1)}, u32[]{:S(2)}, u32[]{:S(2)}) collective-permute-start(f32[320,128]{1,0:T(8,128)S(1)} %add_subtract_fusion.refs_0_.own_ref), channel_id=1, source_target_pairs={{0,16},{4,20},{8,24},{12,28},{16,0},{20,4},{24,8},{28,12},{1,17},{... | collective-permute-start | bytes 491528 | tf_op jit(solution)/shard_map/ppermute | solution.py:35
  48.4 8.5 %collective-permute-start.25 = (f32[320,128]{1,0:T(8,128)S(1)}, f32[320,128]{1,0:T(8,128)S(1)}, u32[]{:S(2)}, u32[]{:S(2)}) collective-permute-start(f32[320,128]{1,0:T(8,128)S(1)} %add_subtract_fusion.refs_0_.own_ref), channel_id=1, source_target_pairs={{0,1},{1,0},{2,3},{3,2},{4,5},{5,4},{6,7},{7,6},{8,9},{9,8},{10,11... | collective-permute-start | bytes 491528 | tf_op jit(solution)/shard_map/ppermute | solution.py:35
  56.8 1.5 %collective-permute-start.29 = (f32[320,128]{1,0:T(8,128)S(1)}, f32[320,128]{1,0:T(8,128)S(1)}, u32[]{:S(2)}, u32[]{:S(2)}) collective-permute-start(f32[320,128]{1,0:T(8,128)S(1)} %shard_map.54.sib_ref), channel_id=1, source_target_pairs={{0,1},{1,0},{2,3},{3,2},{4,5},{5,4},{6,7},{7,6},{8,9},{9,8},{10,11... | collective-permute-start | bytes 491528 | tf_op jit(solution)/shard_map/ppermute | solution.py:35

commit v17 on v16

--- a/solution.py
+++ b/solution.py
@@ -14,7 +14,7 @@
 SYM = HALF + QUARTER
 TOLERANCE = 1e-7
 DIVERGED = 1e4
-FIRST_FLOPS = 6.5e8
+FIRST_FLOPS = 8e8
 INVERT_FLOPS = 5e8
 INVERT_SECOND = 9e8
 MIDDLE_FLOPS = 0
@@ -444,7 +444,8 @@
     head = over_child(head)
     tail = over_child(parts[0][0] + parts[0][1])
     third = parts[2][0] + parts[2][1]
-    near = over_child(call(add_kernel, struct(SYM + RANK + HALF), 0, core, *parts[1], after=(third,)))
+    token = swap(call(keep_kernel, struct(8), 0, core, third[:8]), "sub", 0)
+    near = over_child(call(add_kernel, struct(SYM + RANK + HALF), 0, core, *parts[1], after=(token,)))
 
     head_sib = swap(head, "rows", span_bits)
     tail_sib = swap(tail, "rows", span_bits)

time: 62.3 us -> 63.2 us (1.014)
    ppermute x30 -> x31, starting transfers between devices: 25.3 us -> 25.8 us  [swap(): return lax.ppermute(value, axis, pairs)]
    ppermute x30 -> x31, waiting for transfers between devices: 16.5 us -> 16.8 us  [swap(): return lax.ppermute(value, axis, pairs)]
    pallas_call x15 -> x16, Pallas kernels: 9.64 us -> 9.64 us  [call(): pl.pallas_call(kernel, in_specs=[SMEM] + [VMEM] * (len(values) - 1) + [AN...]
  transfers between devices with their start and end apart: 30 -> 31, of which waited for: 10 -> 11; matrix products, arithmetic and copies ran while one was open for 0% -> 0% of each run, Pallas kernels for 21% -> 21%
where the time goes in v17:
time: 63.2 us; the launch traced here: 63 us
  starting transfers between devices  25.8 us (41%)
  Pallas kernels  19.6 us (31%)
  waiting for transfers between devices  16.8 us (27%)
    ppermute x31, starting transfers between devices, swap(): return lax.ppermute(value, axis, pairs)  25.8 us
    ppermute x31, waiting for transfers between devices, swap(): return lax.ppermute(value, axis, pairs)  16.8 us
    pallas_call x16, Pallas kernels, call(): pl.pallas_call(kernel, in_specs=[SMEM] + [VMEM] * (len(values) - 1) + [AN...  9.64 us
    pallas_call x3, Pallas kernels, products(): pl.pallas_call(functools.partial(product_kernel, groups, chunks), in_spec...  6.21 us
    pallas_call x1, Pallas kernels, on_device(): pl.pallas_call(final_kernel, in_specs=[SMEM] + [VMEM] * len(small), out_s...  3.73 us
  transfers between devices with their start and end apart: 31, of which 11 were waited for; matrix products, arithmetic and copies ran while one was open for 0% of the time, Pallas kernels for 21%

profile of v17, /device:TPU:0, one launch (start us, length us, event | category | flops | bytes accessed | tf_op | source)
XLA Modules:
  0.0 63.0 jit_solution(12624079725764528986)
XLA Ops:
  0.0 2.6 %shard_map.37 = (f32[448,128]{1,0:T(8,128)S(1)}, f32[448,128]{1,0:T(8,128)S(1)}) custom-call(s32[1]{0:T(128)} %bitcast.core_ref, f32[3,1024,256]{2,1,0:T(8,128)} %gens_ref.5, f32[3,1024,256]{2,1,0:T(8,128)} %solved_ref.7), custom_call_target="tpu_custom_call" | custom-call | flops 805306368 | bytes 3145728 | tf_op jit(solution)/shard_map/pallas_call | solution.py:220
  2.7 0.5 collective-permute-start
  3.2 1.1 %collective-permute-done = f32[448,128]{1,0:T(8,128)S(1)} collective-permute-done((f32[448,128]{1,0:T(8,128)S(1)}, f32[448,128]{1,0:T(8,128)S(1)}, u32[]{:S(2)}, u32[]{:S(2)}) %collective-permute-start) | collective-permute-done | bytes 229408 | tf_op jit(solution)/shard_map/ppermute | solution.py:35
  4.3 0.4 collective-permute-start.1
  4.8 2.7 %collective-permute-start.7 = (f32[448,128]{1,0:T(8,128)S(1)}, f32[448,128]{1,0:T(8,128)S(1)}, u32[]{:S(2)}, u32[]{:S(2)}) collective-permute-start(f32[448,128]{1,0:T(8,128)S(1)} %add.38.refs_0_), channel_id=1, source_target_pairs={{0,2},{1,3},{2,0},{3,1},{4,6},{5,7},{6,4},{7,5},{8,10},{9,11},{10,... | collective-permute-start | bytes 688136 | tf_op jit(solution)/shard_map/ppermute | solution.py:35
  7.4 0.0 collective-permute-done.1.refs_1_
  7.5 1.2 %shard_map.39 = (f32[384,128]{1,0:T(8,128)S(1)}, f32[384,128]{1,0:T(8,128)S(1)}) custom-call(s32[1]{0:T(128)} %bitcast.core_ref, f32[3,1024,256]{2,1,0:T(8,128)S(1)} %copy-done.1, f32[3,1024,256]{2,1,0:T(8,128)S(1)} %copy-done, f32[1024,128]{1,0:T(8,128)S(1)} %copy-done.2, f32[8,128]{1,0:T(8,128)S(1)} %collective-permute-done.1.refs_1_), custom_call_target="tpu_custom_call" | custom-call | flops 603979776 | bytes 2621440 | tf_op jit(solution)/shard_map/pallas_call | solution.py:220
  8.6 0.1 collective-permute-start.11
  8.8 2.4 %shard_map.40 = (f32[576,128]{1,0:T(8,128)S(1)}, f32[576,128]{1,0:T(8,128)S(1)}, f32[320,128]{1,0:T(8,128)S(1)}, f32[320,128]{1,0:T(8,128)S(1)}) custom-call(s32[1]{0:T(128)} %bitcast.core_ref, f32[3,1024,256]{2,1,0:T(8,128)S(1)} %copy-done.1, f32[3,1024,256]{2,1,0:T(8,128)S(1)} %copy-done, f32[1024,128]{1,0:T(8,128)S(1)} %copy-done.2, ...), custom_call_target="tpu_custom_call" | custom-call | flops 1610612736 | bytes 4718592 | tf_op jit(solution)/shard_map/pallas_call | solution.py:220
  11.2 0.5 collective-permute-start.4
  11.7 0.0 collective-permute-done.11
  11.7 1.1 %collective-permute-start.12 = (f32[384,128]{1,0:T(8,128)S(1)}, f32[384,128]{1,0:T(8,128)S(1)}, u32[]{:S(2)}, u32[]{:S(2)}) collective-permute-start(f32[384,128]{1,0:T(8,128)S(1)} %add.42), channel_id=1, source_target_pairs={{0,2},{1,3},{2,0},{3,1},{4,6},{5,7},{6,4},{7,5},{8,10},{9,11},{10,... | collective-permute-start | bytes 589832 | tf_op jit(solution)/shard_map/ppermute | solution.py:35
  12.8 0.0 collective-permute-start.2
  12.8 0.8 %collective-permute-done.7 = f32[448,128]{1,0:T(8,128)S(1)} collective-permute-done((f32[448,128]{1,0:T(8,128)S(1)}, f32[448,128]{1,0:T(8,128)S(1)}, u32[]{:S(2)}, u32[]{:S(2)}) %collective-permute-start.7) | collective-permute-done | bytes 229408 | tf_op jit(solution)/shard_map/ppermute | solution.py:35
  13.6 1.8 %collective-permute-start.8 = (f32[448,128]{1,0:T(8,128)S(1)}, f32[448,128]{1,0:T(8,128)S(1)}, u32[]{:S(2)}, u32[]{:S(2)}) collective-permute-start(f32[448,128]{1,0:T(8,128)S(1)} %add.41.own_ref.head_ref), channel_id=1, source_target_pairs={{0,4},{4,0},{8,12},{12,8},{16,20},{20,16},{24,28},{28,24},{1,5},{5... | collective-permute-start | bytes 688136 | tf_op jit(solution)/shard_map/ppermute | solution.py:35
  15.4 0.0 collective-permute-start.9
  15.4 0.6 collective-permute-start.5
  16.0 0.9 %collective-permute-done.5.refs_0_ = f32[8,128]{1,0:T(8,128)S(1)} collective-permute-done((f32[8,128]{1,0:T(8,128)S(1)}, f32[8,128]{1,0:T(8,128)S(1)}, u32[]{:S(2)}, u32[]{:S(2)}) %collective-permute-start.5) | collective-permute-done | bytes 4128 | tf_op jit(solution)/shard_map/ppermute | solution.py:35
  16.9 1.6 %collective-permute-start.6 = (f32[576,128]{1,0:T(8,128)S(1)}, f32[576,128]{1,0:T(8,128)S(1)}, u32[]{:S(2)}, u32[]{:S(2)}) collective-permute-start(f32[576,128]{1,0:T(8,128)S(1)} %shard_map.42), channel_id=1, source_target_pairs={{0,2},{1,3},{2,0},{3,1},{4,6},{5,7},{6,4},{7,5},{8,10},{9,11},{10,... | collective-permute-start | bytes 884744 | tf_op jit(solution)/shard_map/ppermute | solution.py:35
  18.5 0.2 collective-permute-done.12
  18.7 1.6 %collective-permute-start.13 = (f32[384,128]{1,0:T(8,128)S(1)}, f32[384,128]{1,0:T(8,128)S(1)}, u32[]{:S(2)}, u32[]{:S(2)}) collective-permute-start(f32[384,128]{1,0:T(8,128)S(1)} %add.43.tail_ref.own_ref), channel_id=1, source_target_pairs={{0,4},{4,0},{8,12},{12,8},{16,20},{20,16},{24,28},{28,24},{1,5},{5... | collective-permute-start | bytes 589832 | tf_op jit(solution)/shard_map/ppermute | solution.py:35
  20.3 0.7 %collective-permute-done.8.sib_ref.head_sib_ref = f32[448,128]{1,0:T(8,128)S(1)} collective-permute-done((f32[448,128]{1,0:T(8,128)S(1)}, f32[448,128]{1,0:T(8,128)S(1)}, u32[]{:S(2)}, u32[]{:S(2)}) %collective-permute-start.8) | collective-permute-done | bytes 229408 | tf_op jit(solution)/shard_map/ppermute | solution.py:35
  21.0 0.1 collective-permute-start.10
  21.1 1.6 %collective-permute-start.3 = (f32[320,128]{1,0:T(8,128)S(1)}, f32[320,128]{1,0:T(8,128)S(1)}, u32[]{:S(2)}, u32[]{:S(2)}) collective-permute-start(f32[320,128]{1,0:T(8,128)S(1)} %add.39.first_ref), channel_id=1, source_target_pairs={{0,8},{4,12},{8,0},{12,4},{16,24},{20,28},{24,16},{28,20},{1,9},{5... | collective-permute-start | bytes 491528 | tf_op jit(solution)/shard_map/ppermute | solution.py:35
  22.7 0.0 collective-permute-done.9.own_other_ref.head_other_ref
  22.7 0.2 collective-permute-start.15
  22.9 0.0 collective-permute-done.10.sib_other_ref
  22.9 2.3 %shard_map.43 = (f32[256,256]{1,0:T(8,128)S(1)}, f32[256,320]{1,0:T(8,128)S(1)}) custom-call(s32[1]{0:T(128)} %bitcast.core_ref, f32[448,128]{1,0:T(8,128)S(1)} %add.41.own_ref.head_ref, f32[448,128]{1,0:T(8,128)S(1)} %collective-permute-done.8.sib_ref.head_sib_ref, f32[448,128]{1,0:T(8,128)S(1)} %collective-permute-done.9.own_other_ref.head_other_ref, ...), custom_call_target="tpu_custom_call" | custom-call | flops 500000000 | bytes 1572868 | tf_op jit(solution)/shard_map/pallas_call | solution.py:309
  25.2 0.2 collective-permute-done.13.tail_sib_ref
  25.4 0.8 %shard_map.44 = (f32[640,128]{1,0:T(8,128)S(1)}, f32[576,128]{1,0:T(8,128)S(1)}) custom-call(s32[1]{0:T(128)} %bitcast.core_ref, f32[256,256]{1,0:T(8,128)S(1)} %get-tuple-element.34.inverse_ref, f32[256,320]{1,0:T(8,128)S(1)} %get-tuple-element.35.product_ref, f32[448,128]{1,0:T(8,128)S(1)} %add.41.own_ref.head_ref, ...), custom_call_target="tpu_custom_call" | custom-call | flops 800000000 | bytes 2097156 | tf_op jit(solution)/shard_map/pallas_call | solution.py:309
  26.3 0.0 collective-permute-done.6
  26.4 1.7 %collective-permute-start.20 = (f32[192,128]{1,0:T(8,128)S(1)}, f32[192,128]{1,0:T(8,128)S(1)}, u32[]{:S(2)}, u32[]{:S(2)}) collective-permute-start(f32[192,128]{1,0:T(8,128)S(1)} %shard_map.45.refs_0_), channel_id=1, source_target_pairs={{0,4},{4,0},{8,12},{12,8},{16,20},{20,16},{24,28},{28,24},{1,5},{5... | collective-permute-start | bytes 294920 | tf_op jit(solution)/shard_map/ppermute | solution.py:35
  28.1 0.5 collective-permute-start.18
  28.6 0.0 collective-permute-done.3.second_ref
  28.6 2.0 %collective-permute-start.14 = (f32[320,128]{1,0:T(8,128)S(1)}, f32[320,128]{1,0:T(8,128)S(1)}, u32[]{:S(2)}, u32[]{:S(2)}) collective-permute-start(f32[320,128]{1,0:T(8,128)S(1)} %shard_map.47), channel_id=1, source_target_pairs={{0,2},{1,3},{2,0},{3,1},{4,6},{5,7},{6,4},{7,5},{8,10},{9,11},{10,... | collective-permute-start | bytes 491528 | tf_op jit(solution)/shard_map/ppermute | solution.py:35
  30.6 0.0 collective-permute-done.15.own_other_ref
  30.6 0.4 shard_map.48
  31.1 1.1 %collective-permute-start.16 = (f32[320,128]{1,0:T(8,128)S(1)}, f32[320,128]{1,0:T(8,128)S(1)}, u32[]{:S(2)}, u32[]{:S(2)}) collective-permute-start(f32[320,128]{1,0:T(8,128)S(1)} %shard_map.48), channel_id=1, source_target_pairs={{0,8},{4,12},{8,0},{12,4},{16,24},{20,28},{24,16},{28,20},{1,9},{5... | collective-permute-start | bytes 491528 | tf_op jit(solution)/shard_map/ppermute | solution.py:35
  32.1 0.0 collective-permute-done.20
  32.1 1.6 %collective-permute-start.21 = (f32[192,128]{1,0:T(8,128)S(1)}, f32[192,128]{1,0:T(8,128)S(1)}, u32[]{:S(2)}, u32[]{:S(2)}) collective-permute-start(f32[192,128]{1,0:T(8,128)S(1)} %add.48.own_ref), channel_id=1, source_target_pairs={{0,8},{4,12},{8,0},{12,4},{16,24},{20,28},{24,16},{28,20},{1,9},{5... | collective-permute-start | bytes 294920 | tf_op jit(solution)/shard_map/ppermute | solution.py:35
  33.8 1.8 %collective-permute-done.18 = f32[384,128]{1,0:T(8,128)S(1)} collective-permute-done((f32[384,128]{1,0:T(8,128)S(1)}, f32[384,128]{1,0:T(8,128)S(1)}, u32[]{:S(2)}, u32[]{:S(2)}) %collective-permute-start.18) | collective-permute-done | bytes 196640 | tf_op jit(solution)/shard_map/ppermute | solution.py:35
  35.6 1.3 %collective-permute-start.19 = (f32[384,128]{1,0:T(8,128)S(1)}, f32[384,128]{1,0:T(8,128)S(1)}, u32[]{:S(2)}, u32[]{:S(2)}) collective-permute-start(f32[384,128]{1,0:T(8,128)S(1)} %add.47.r_own_ref.own_ref), channel_id=1, source_target_pairs={{0,8},{4,12},{8,0},{12,4},{16,24},{20,28},{24,16},{28,20},{1,9},{5... | collective-permute-start | bytes 589832 | tf_op jit(solution)/shard_map/ppermute | solution.py:35
  37.0 2.8 %collective-permute-done.21.sib_ref = f32[192,128]{1,0:T(8,128)S(1)} collective-permute-done((f32[192,128]{1,0:T(8,128)S(1)}, f32[192,128]{1,0:T(8,128)S(1)}, u32[]{:S(2)}, u32[]{:S(2)}) %collective-permute-start.21) | collective-permute-done | bytes 98336 | tf_op jit(solution)/shard_map/ppermute | solution.py:35
  39.8 0.0 collective-permute-start.23
  39.8 0.0 collective-permute-done.16
  39.8 1.3 %collective-permute-start.17 = (f32[320,128]{1,0:T(8,128)S(1)}, f32[320,128]{1,0:T(8,128)S(1)}, u32[]{:S(2)}, u32[]{:S(2)}) collective-permute-start(f32[320,128]{1,0:T(8,128)S(1)} %add_subtract_fusion.1), channel_id=1, source_target_pairs={{0,4},{4,0},{8,12},{12,8},{16,20},{20,16},{24,28},{28,24},{1,5},{5... | collective-permute-start | bytes 491528 | tf_op jit(solution)/shard_map/ppermute | solution.py:35
  41.1 0.0 collective-permute-done.23.sib_other_ref
  41.1 0.0 collective-permute-done.24.r_own_other_ref
  41.1 2.5 %shard_map.49 = (f32[256,256]{1,0:T(8,128)S(1)}, f32[256,192]{1,0:T(8,128)S(1)}, f32[512,256]{1,0:T(8,128)S(1)}) custom-call(s32[1]{0:T(128)} %bitcast.core_ref, f32[192,128]{1,0:T(8,128)S(1)} %add.48.own_ref, f32[192,128]{1,0:T(8,128)S(1)} %collective-permute-done.21.sib_ref, f32[192,128]{1,0:T(8,128)S(1)} %collective-permute-done.22.own_other_ref, ...), custom_call_target="tpu_custom_call" | custom-call | flops 900000000 | bytes 1703940 | tf_op jit(solution)/shard_map/pallas_call | solution.py:309
  43.6 0.0 collective-permute-done.19.sib_ref
  43.7 0.3 collective-permute-start.25
  44.0 0.3 collective-permute-start.29
  44.2 0.9 %shard_map.51 = (f32[384,128]{1,0:T(8,128)S(1)}, f32[384,128]{1,0:T(8,128)S(1)}, f32[320,128]{1,0:T(8,128)S(1)}) custom-call(s32[1]{0:T(128)} %bitcast.core_ref, f32[256,256]{1,0:T(8,128)S(1)} %get-tuple-element.38.refs_0_.inverse_ref, f32[256,192]{1,0:T(8,128)S(1)} %get-tuple-element.39.product_ref, f32[512,256]{1,0:T(8,128)S(1)} %get-tuple-element.40.turned_ref, ...), custom_call_target="tpu_custom_call" | custom-call | bytes 1933316 | tf_op jit(solution)/shard_map/pallas_call | solution.py:309
  45.2 0.4 shard_map.52
  45.6 0.9 %collective-permute-done.17 = f32[320,128]{1,0:T(8,128)S(1)} collective-permute-done((f32[320,128]{1,0:T(8,128)S(1)}, f32[320,128]{1,0:T(8,128)S(1)}, u32[]{:S(2)}, u32[]{:S(2)}) %collective-permute-start.17) | collective-permute-done | bytes 163872 | tf_op jit(solution)/shard_map/ppermute | solution.py:35
  46.6 0.1 collective-permute-start.28
  46.6 2.7 %collective-permute-start.27 = (f32[320,128]{1,0:T(8,128)S(1)}, f32[320,128]{1,0:T(8,128)S(1)}, u32[]{:S(2)}, u32[]{:S(2)}) collective-permute-start(f32[320,128]{1,0:T(8,128)S(1)} %add_subtract_fusion.refs_0_.own_ref), channel_id=1, source_target_pairs={{0,16},{4,20},{8,24},{12,28},{16,0},{20,4},{24,8},{28,12},{1,17},{... | collective-permute-start | bytes 491528 | tf_op jit(solution)/shard_map/ppermute | solution.py:35
  49.3 0.2 collective-permute-start.26
  49.5 2.2 %shard_map.54 = (bf16[1024,256]{1,0:T(8,128)(2,1)S(1)}, bf16[1024,256]{1,0:T(8,128)(2,1)S(1)}, f32[1024,128]{1,0:T(8,128)S(1)}) custom-call(s32[1]{0:T(128)} %bitcast.core_ref, f32[384,128]{1,0:T(8,128)S(1)} %get-tuple-element.43.value_ref.z1_ref, f32[384,128]{1,0:T(8,128)S(1)} %collective-permute-done.28.z1_other_ref, ...), custom_call_target="tpu_custom_call" | custom-call | flops 1207959552 | bytes 7340036 | tf_op jit(solution)/shard_map/pallas_call | solution.py:309
  51.7 6.0 %collective-permute-done.27.value_ref = f32[320,128]{1,0:T(8,128)S(1)} collective-permute-done((f32[320,128]{1,0:T(8,128)S(1)}, f32[320,128]{1,0:T(8,128)S(1)}, u32[]{:S(2)}, u32[]{:S(2)}) %collective-permute-start.27) | collective-permute-done | bytes 163872 | tf_op jit(solution)/shard_map/ppermute | solution.py:35
  57.7 0.1 collective-permute-start.30
  57.8 0.0 collective-permute-done.26.own_other_ref
  57.8 1.4 %collective-permute-done.30.sib_other_ref = f32[320,128]{1,0:T(8,128)S(1)} collective-permute-done((f32[320,128]{1,0:T(8,128)S(1)}, f32[320,128]{1,0:T(8,128)S(1)}, u32[]{:S(2)}, u32[]{:S(2)}) %collective-permute-start.30) | collective-permute-done | bytes 163872 | tf_op jit(solution)/shard_map/ppermute | solution.py:35
  59.1 3.7 %shard_map.56 = f32[1024,128]{1,0:T(8,128)} custom-call(s32[1]{0:T(128)} %bitcast.core_ref, f32[320,128]{1,0:T(8,128)S(1)} %add_subtract_fusion.refs_0_.own_ref, f32[320,128]{1,0:T(8,128)S(1)} %collective-permute-done.26.own_other_ref, f32[320,128]{1,0:T(8,128)S(1)} %shard_map.55.sib_ref, f32[320,128]{1,0:T(8,128)S(1)} %collective-permute-done.30.sib_other_ref, ...), custom_call_target="tpu_custom_call" | custom-call | flops 1107296256 | bytes 3145728 | tf_op jit(solution)/shard_map/pallas_call | solution.py:503
  (44 shorter events, 0.5 us)
Async XLA Ops:
  0.0 7.5 %copy-start = (f32[3,1024,256]{2,1,0:T(8,128)S(1)}, f32[3,1024,256]{2,1,0:T(8,128)}, u32[]{:S(2)}) copy-start(f32[3,1024,256]{2,1,0:T(8,128)} %solved_ref.7) | copy-start | bytes 9437188
  0.0 7.5 %copy-start.1 = (f32[3,1024,256]{2,1,0:T(8,128)S(1)}, f32[3,1024,256]{2,1,0:T(8,128)}, u32[]{:S(2)}) copy-start(f32[3,1024,256]{2,1,0:T(8,128)} %gens_ref.5) | copy-start | bytes 9437188
  0.0 7.5 %copy-start.2 = (f32[1024,128]{1,0:T(8,128)S(1)}, f32[1024,128]{1,0:T(8,128)}, u32[]{:S(2)}) copy-start(f32[1024,128]{1,0:T(8,128)} %rhs_ref.1) | copy-start | bytes 1572868
  2.7 1.6 %collective-permute-start = (f32[448,128]{1,0:T(8,128)S(1)}, f32[448,128]{1,0:T(8,128)S(1)}, u32[]{:S(2)}, u32[]{:S(2)}) collective-permute-start(f32[448,128]{1,0:T(8,128)S(1)} %get-tuple-element.26), channel_id=1, source_target_pairs={{0,1},{1,0},{2,3},{3,2},{4,5},{5,4},{6,7},{7,6},{8,9},{9,8},{10,11... | collective-permute-start | bytes 688136 | tf_op jit(solution)/shard_map/ppermute | solution.py:35
  4.3 3.1 %collective-permute-start.1 = (f32[8,128]{1,0:T(8,128)S(1)}, f32[8,128]{1,0:T(8,128)S(1)}, u32[]{:S(2)}, u32[]{:S(2)}) collective-permute-start(f32[8,128]{1,0:T(8,128)S(1)} %shard_map.38), channel_id=1, source_target_pairs={{0,1},{1,0},{2,3},{3,2},{4,5},{5,4},{6,7},{7,6},{8,9},{9,8},{10,11... | collective-permute-start | bytes 12296 | tf_op jit(solution)/shard_map/ppermute | solution.py:35
  4.8 8.8 %collective-permute-start.7 = (f32[448,128]{1,0:T(8,128)S(1)}, f32[448,128]{1,0:T(8,128)S(1)}, u32[]{:S(2)}, u32[]{:S(2)}) collective-permute-start(f32[448,128]{1,0:T(8,128)S(1)} %add.38.refs_0_), channel_id=1, source_target_pairs={{0,2},{1,3},{2,0},{3,1},{4,6},{5,7},{6,4},{7,5},{8,10},{9,11},{10,... | collective-permute-start | bytes 688136 | tf_op jit(solution)/shard_map/ppermute | solution.py:35
  8.6 3.1 %collective-permute-start.11 = (f32[384,128]{1,0:T(8,128)S(1)}, f32[384,128]{1,0:T(8,128)S(1)}, u32[]{:S(2)}, u32[]{:S(2)}) collective-permute-start(f32[384,128]{1,0:T(8,128)S(1)} %get-tuple-element.28.refs_1_), channel_id=1, source_target_pairs={{0,1},{1,0},{2,3},{3,2},{4,5},{5,4},{6,7},{7,6},{8,9},{9,8},{10,11... | collective-permute-start | bytes 589832 | tf_op jit(solution)/shard_map/ppermute | solution.py:35
  11.2 5.7 %collective-permute-start.4 = (f32[576,128]{1,0:T(8,128)S(1)}, f32[576,128]{1,0:T(8,128)S(1)}, u32[]{:S(2)}, u32[]{:S(2)}) collective-permute-start(f32[576,128]{1,0:T(8,128)S(1)} %get-tuple-element.32), channel_id=1, source_target_pairs={{0,1},{1,0},{2,3},{3,2},{4,5},{5,4},{6,7},{7,6},{8,9},{9,8},{10,11... | collective-permute-start | bytes 884744 | tf_op jit(solution)/shard_map/ppermute | solution.py:35
  11.7 7.0 %collective-permute-start.12 = (f32[384,128]{1,0:T(8,128)S(1)}, f32[384,128]{1,0:T(8,128)S(1)}, u32[]{:S(2)}, u32[]{:S(2)}) collective-permute-start(f32[384,128]{1,0:T(8,128)S(1)} %add.42), channel_id=1, source_target_pairs={{0,2},{1,3},{2,0},{3,1},{4,6},{5,7},{6,4},{7,5},{8,10},{9,11},{10,... | collective-permute-start | bytes 589832 | tf_op jit(solution)/shard_map/ppermute | solution.py:35
  12.8 2.6 %collective-permute-start.2 = (f32[320,128]{1,0:T(8,128)S(1)}, f32[320,128]{1,0:T(8,128)S(1)}, u32[]{:S(2)}, u32[]{:S(2)}) collective-permute-start(f32[320,128]{1,0:T(8,128)S(1)} %get-tuple-element.30), channel_id=1, source_target_pairs={{0,1},{1,0},{2,3},{3,2},{4,5},{5,4},{6,7},{7,6},{8,9},{9,8},{10,11... | collective-permute-start | bytes 491528 | tf_op jit(solution)/shard_map/ppermute | solution.py:35
  13.6 7.4 %collective-permute-start.8 = (f32[448,128]{1,0:T(8,128)S(1)}, f32[448,128]{1,0:T(8,128)S(1)}, u32[]{:S(2)}, u32[]{:S(2)}) collective-permute-start(f32[448,128]{1,0:T(8,128)S(1)} %add.41.own_ref.head_ref), channel_id=1, source_target_pairs={{0,4},{4,0},{8,12},{12,8},{16,20},{20,16},{24,28},{28,24},{1,5},{5... | collective-permute-start | bytes 688136 | tf_op jit(solution)/shard_map/ppermute | solution.py:35
  15.4 7.3 %collective-permute-start.9 = (f32[448,128]{1,0:T(8,128)S(1)}, f32[448,128]{1,0:T(8,128)S(1)}, u32[]{:S(2)}, u32[]{:S(2)}) collective-permute-start(f32[448,128]{1,0:T(8,128)S(1)} %add.41.own_ref.head_ref), channel_id=1, source_target_pairs={{0,1},{1,0},{2,3},{3,2},{4,5},{5,4},{6,7},{7,6},{8,9},{9,8},{10,11... | collective-permute-start | bytes 688136 | tf_op jit(solution)/shard_map/ppermute | solution.py:35
  15.4 1.4 %collective-permute-start.5 = (f32[8,128]{1,0:T(8,128)S(1)}, f32[8,128]{1,0:T(8,128)S(1)}, u32[]{:S(2)}, u32[]{:S(2)}) collective-permute-start(f32[8,128]{1,0:T(8,128)S(1)} %shard_map.41), channel_id=1, source_target_pairs={{0,1},{1,0},{2,3},{3,2},{4,5},{5,4},{6,7},{7,6},{8,9},{9,8},{10,11... | collective-permute-start | bytes 12296 | tf_op jit(solution)/shard_map/ppermute | solution.py:35
  16.9 9.4 %collective-permute-start.6 = (f32[576,128]{1,0:T(8,128)S(1)}, f32[576,128]{1,0:T(8,128)S(1)}, u32[]{:S(2)}, u32[]{:S(2)}) collective-permute-start(f32[576,128]{1,0:T(8,128)S(1)} %shard_map.42), channel_id=1, source_target_pairs={{0,2},{1,3},{2,0},{3,1},{4,6},{5,7},{6,4},{7,5},{8,10},{9,11},{10,... | collective-permute-start | bytes 884744 | tf_op jit(solution)/shard_map/ppermute | solution.py:35
  18.7 6.7 %collective-permute-start.13 = (f32[384,128]{1,0:T(8,128)S(1)}, f32[384,128]{1,0:T(8,128)S(1)}, u32[]{:S(2)}, u32[]{:S(2)}) collective-permute-start(f32[384,128]{1,0:T(8,128)S(1)} %add.43.tail_ref.own_ref), channel_id=1, source_target_pairs={{0,4},{4,0},{8,12},{12,8},{16,20},{20,16},{24,28},{28,24},{1,5},{5... | collective-permute-start | bytes 589832 | tf_op jit(solution)/shard_map/ppermute | solution.py:35
  21.0 2.0 %collective-permute-start.10 = (f32[192,128]{1,0:T(8,128)S(1)}, f32[192,128]{1,0:T(8,128)S(1)}, u32[]{:S(2)}, u32[]{:S(2)}) collective-permute-start(f32[192,128]{1,0:T(8,128)S(1)} %slice.42), channel_id=1, source_target_pairs={{0,1},{1,0},{2,3},{3,2},{4,5},{5,4},{6,7},{7,6},{8,9},{9,8},{10,11... | collective-permute-start | bytes 294920 | tf_op jit(solution)/shard_map/ppermute | solution.py:35
  21.1 7.5 %collective-permute-start.3 = (f32[320,128]{1,0:T(8,128)S(1)}, f32[320,128]{1,0:T(8,128)S(1)}, u32[]{:S(2)}, u32[]{:S(2)}) collective-permute-start(f32[320,128]{1,0:T(8,128)S(1)} %add.39.first_ref), channel_id=1, source_target_pairs={{0,8},{4,12},{8,0},{12,4},{16,24},{20,28},{24,16},{28,20},{1,9},{5... | collective-permute-start | bytes 491528 | tf_op jit(solution)/shard_map/ppermute | solution.py:35
  22.7 7.9 %collective-permute-start.15 = (f32[256,128]{1,0:T(8,128)S(1)}, f32[256,128]{1,0:T(8,128)S(1)}, u32[]{:S(2)}, u32[]{:S(2)}) collective-permute-start(f32[256,128]{1,0:T(8,128)S(1)} %slice.44), channel_id=1, source_target_pairs={{0,1},{1,0},{2,3},{3,2},{4,5},{5,4},{6,7},{7,6},{8,9},{9,8},{10,11... | collective-permute-start | bytes 393224 | tf_op jit(solution)/shard_map/ppermute | solution.py:35
  26.4 5.7 %collective-permute-start.20 = (f32[192,128]{1,0:T(8,128)S(1)}, f32[192,128]{1,0:T(8,128)S(1)}, u32[]{:S(2)}, u32[]{:S(2)}) collective-permute-start(f32[192,128]{1,0:T(8,128)S(1)} %shard_map.45.refs_0_), channel_id=1, source_target_pairs={{0,4},{4,0},{8,12},{12,8},{16,20},{20,16},{24,28},{28,24},{1,5},{5... | collective-permute-start | bytes 294920 | tf_op jit(solution)/shard_map/ppermute | solution.py:35
  28.1 7.5 %collective-permute-start.18 = (f32[384,128]{1,0:T(8,128)S(1)}, f32[384,128]{1,0:T(8,128)S(1)}, u32[]{:S(2)}, u32[]{:S(2)}) collective-permute-start(f32[384,128]{1,0:T(8,128)S(1)} %shard_map.46.refs_0_), channel_id=1, source_target_pairs={{0,4},{4,0},{8,12},{12,8},{16,20},{20,16},{24,28},{28,24},{1,5},{5... | collective-permute-start | bytes 589832 | tf_op jit(solution)/shard_map/ppermute | solution.py:35
  28.6 8.4 %collective-permute-start.14 = (f32[320,128]{1,0:T(8,128)S(1)}, f32[320,128]{1,0:T(8,128)S(1)}, u32[]{:S(2)}, u32[]{:S(2)}) collective-permute-start(f32[320,128]{1,0:T(8,128)S(1)} %shard_map.47), channel_id=1, source_target_pairs={{0,2},{1,3},{2,0},{3,1},{4,6},{5,7},{6,4},{7,5},{8,10},{9,11},{10,... | collective-permute-start | bytes 491528 | tf_op jit(solution)/shard_map/ppermute | solution.py:35
  31.1 8.7 %collective-permute-start.16 = (f32[320,128]{1,0:T(8,128)S(1)}, f32[320,128]{1,0:T(8,128)S(1)}, u32[]{:S(2)}, u32[]{:S(2)}) collective-permute-start(f32[320,128]{1,0:T(8,128)S(1)} %shard_map.48), channel_id=1, source_target_pairs={{0,8},{4,12},{8,0},{12,4},{16,24},{20,28},{24,16},{28,20},{1,9},{5... | collective-permute-start | bytes 491528 | tf_op jit(solution)/shard_map/ppermute | solution.py:35
  32.1 7.6 %collective-permute-start.21 = (f32[192,128]{1,0:T(8,128)S(1)}, f32[192,128]{1,0:T(8,128)S(1)}, u32[]{:S(2)}, u32[]{:S(2)}) collective-permute-start(f32[192,128]{1,0:T(8,128)S(1)} %add.48.own_ref), channel_id=1, source_target_pairs={{0,8},{4,12},{8,0},{12,4},{16,24},{20,28},{24,16},{28,20},{1,9},{5... | collective-permute-start | bytes 294920 | tf_op jit(solution)/shard_map/ppermute | solution.py:35
  33.8 7.3 %collective-permute-start.22 = (f32[192,128]{1,0:T(8,128)S(1)}, f32[192,128]{1,0:T(8,128)S(1)}, u32[]{:S(2)}, u32[]{:S(2)}) collective-permute-start(f32[192,128]{1,0:T(8,128)S(1)} %add.48.own_ref), channel_id=1, source_target_pairs={{0,1},{1,0},{2,3},{3,2},{4,5},{5,4},{6,7},{7,6},{8,9},{9,8},{10,11... | collective-permute-start | bytes 294920 | tf_op jit(solution)/shard_map/ppermute | solution.py:35
  35.6 8.0 %collective-permute-start.19 = (f32[384,128]{1,0:T(8,128)S(1)}, f32[384,128]{1,0:T(8,128)S(1)}, u32[]{:S(2)}, u32[]{:S(2)}) collective-permute-start(f32[384,128]{1,0:T(8,128)S(1)} %add.47.r_own_ref.own_ref), channel_id=1, source_target_pairs={{0,8},{4,12},{8,0},{12,4},{16,24},{20,28},{24,16},{28,20},{1,9},{5... | collective-permute-start | bytes 589832 | tf_op jit(solution)/shard_map/ppermute | solution.py:35
  37.0 4.2 %collective-permute-start.24 = (f32[256,128]{1,0:T(8,128)S(1)}, f32[256,128]{1,0:T(8,128)S(1)}, u32[]{:S(2)}, u32[]{:S(2)}) collective-permute-start(f32[256,128]{1,0:T(8,128)S(1)} %slice.46), channel_id=1, source_target_pairs={{0,1},{1,0},{2,3},{3,2},{4,5},{5,4},{6,7},{7,6},{8,9},{9,8},{10,11... | collective-permute-start | bytes 393224 | tf_op jit(solution)/shard_map/ppermute | solution.py:35
  39.8 1.3 %collective-permute-start.23 = (f32[192,128]{1,0:T(8,128)S(1)}, f32[192,128]{1,0:T(8,128)S(1)}, u32[]{:S(2)}, u32[]{:S(2)}) collective-permute-start(f32[192,128]{1,0:T(8,128)S(1)} %collective-permute-done.21.sib_ref), channel_id=1, source_target_pairs={{0,1},{1,0},{2,3},{3,2},{4,5},{5,4},{6,7},{7,6},{8,9},{9,8},{10,11... | collective-permute-start | bytes 294920 | tf_op jit(solution)/shard_map/ppermute | solution.py:35
  39.8 6.7 %collective-permute-start.17 = (f32[320,128]{1,0:T(8,128)S(1)}, f32[320,128]{1,0:T(8,128)S(1)}, u32[]{:S(2)}, u32[]{:S(2)}) collective-permute-start(f32[320,128]{1,0:T(8,128)S(1)} %add_subtract_fusion.1), channel_id=1, source_target_pairs={{0,4},{4,0},{8,12},{12,8},{16,20},{20,16},{24,28},{28,24},{1,5},{5... | collective-permute-start | bytes 491528 | tf_op jit(solution)/shard_map/ppermute | solution.py:35
  43.7 1.5 %collective-permute-start.25 = (f32[256,128]{1,0:T(8,128)S(1)}, f32[256,128]{1,0:T(8,128)S(1)}, u32[]{:S(2)}, u32[]{:S(2)}) collective-permute-start(f32[256,128]{1,0:T(8,128)S(1)} %shard_map.50.sib_ref), channel_id=1, source_target_pairs={{0,1},{1,0},{2,3},{3,2},{4,5},{5,4},{6,7},{7,6},{8,9},{9,8},{10,11... | collective-permute-start | bytes 393224 | tf_op jit(solution)/shard_map/ppermute | solution.py:35
  44.0 5.5 %collective-permute-start.29 = (f32[640,128]{1,0:T(8,128)S(1)}, f32[640,128]{1,0:T(8,128)S(1)}, u32[]{:S(2)}, u32[]{:S(2)}) collective-permute-start(f32[640,128]{1,0:T(8,128)S(1)} %get-tuple-element.37.z_ref.z0_ref), channel_id=1, source_target_pairs={{0,1},{1,0},{2,3},{3,2},{4,5},{5,4},{6,7},{7,6},{8,9},{9,8},{10,11... | collective-permute-start | bytes 983048 | tf_op jit(solution)/shard_map/ppermute | solution.py:35
  46.6 2.9 %collective-permute-start.28 = (f32[384,128]{1,0:T(8,128)S(1)}, f32[384,128]{1,0:T(8,128)S(1)}, u32[]{:S(2)}, u32[]{:S(2)}) collective-permute-start(f32[384,128]{1,0:T(8,128)S(1)} %shard_map.53), channel_id=1, source_target_pairs={{0,1},{1,0},{2,3},{3,2},{4,5},{5,4},{6,7},{7,6},{8,9},{9,8},{10,11... | collective-permute-start | bytes 589832 | tf_op jit(solution)/shard_map/ppermute | solution.py:35
  46.6 11.0 %collective-permute-start.27 = (f32[320,128]{1,0:T(8,128)S(1)}, f32[320,128]{1,0:T(8,128)S(1)}, u32[]{:S(2)}, u32[]{:S(2)}) collective-permute-start(f32[320,128]{1,0:T(8,128)S(1)} %add_subtract_fusion.refs_0_.own_ref), channel_id=1, source_target_pairs={{0,16},{4,20},{8,24},{12,28},{16,0},{20,4},{24,8},{28,12},{1,17},{... | collective-permute-start | bytes 491528 | tf_op jit(solution)/shard_map/ppermute | solution.py:35
  49.3 8.5 %collective-permute-start.26 = (f32[320,128]{1,0:T(8,128)S(1)}, f32[320,128]{1,0:T(8,128)S(1)}, u32[]{:S(2)}, u32[]{:S(2)}) collective-permute-start(f32[320,128]{1,0:T(8,128)S(1)} %add_subtract_fusion.refs_0_.own_ref), channel_id=1, source_target_pairs={{0,1},{1,0},{2,3},{3,2},{4,5},{5,4},{6,7},{7,6},{8,9},{9,8},{10,11... | collective-permute-start | bytes 491528 | tf_op jit(solution)/shard_map/ppermute | solution.py:35
  57.7 1.5 %collective-permute-start.30 = (f32[320,128]{1,0:T(8,128)S(1)}, f32[320,128]{1,0:T(8,128)S(1)}, u32[]{:S(2)}, u32[]{:S(2)}) collective-permute-start(f32[320,128]{1,0:T(8,128)S(1)} %shard_map.55.sib_ref), channel_id=1, source_target_pairs={{0,1},{1,0},{2,3},{3,2},{4,5},{5,4},{6,7},{7,6},{8,9},{9,8},{10,11... | collective-permute-start | bytes 491528 | tf_op jit(solution)/shard_map/ppermute | solution.py:35

commit v18 on v15

--- a/solution.py
+++ b/solution.py
@@ -388,6 +388,12 @@
     refs[-1][...] = value_ref[...]
 
 
+def join_kernel(core_ref, first_ref, second_ref, *refs):
+    rows = first_ref.shape[0]
+    refs[-1][:rows, :] = first_ref[...]
+    refs[-1][rows:, :] = second_ref[...]
+
+
 def add_kernel(core_ref, first_ref, second_ref, *refs):
     refs[-1][...] = first_ref[...] + second_ref[...]
 
@@ -489,11 +495,12 @@
 
     own = third - crossed
     sib = swap(own, "rows", span_bits + 2)
-    z1_other = swap(call(keep_kernel, struct(RANK + HALF), 0, core, z1, after=(own,)), "sub", 0)
+    solved = swap(call(join_kernel, struct(3 * RANK + 2 * HALF), 0, core, z1, z0, after=(own,)), "sub", 0)
+    z1_other, z0_other = solved[: RANK + HALF], solved[RANK + HALF :]
     part = jax.ShapeDtypeStruct((rhs.shape[0], RANK), jnp.bfloat16)
     high, low, current = call(
         reduced_kernel, [part, part, struct(rhs.shape[0], RHS)], 6 * rhs.shape[0] * 2 * RANK * (RANK + RHS),
-        core, z1, z1_other, z0, swap(z0, "sub", 0), solved_gens, rhs,
+        core, z1, z1_other, z0, z0_other, solved_gens, rhs,
     )
     sib = call(keep_kernel, struct(last), 0, core, sib, after=(high,))
     own_other, sib_other = swap(own, "sub", 0), swap(sib, "sub", 0)

time: 62.1 us -> 62.1 us (level)
    ppermute x30 -> x29, starting transfers between devices: 25.3 us -> 25 us  [swap(): return lax.ppermute(value, axis, pairs)]
    ppermute x30 -> x29, waiting for transfers between devices: 16.3 us -> 16.5 us  [swap(): return lax.ppermute(value, axis, pairs)]
  transfers between devices with their start and end apart: 30 -> 29, of which waited for: 10 -> 11; matrix products, arithmetic and copies ran while one was open for 1% -> 1% of each run, Pallas kernels for 21% -> 21%
where the time goes in v18:
time: 62.1 us; the launch traced here: 62 us
  starting transfers between devices  25 us (40%)
  Pallas kernels  19.6 us (32%)
  waiting for transfers between devices  16.5 us (27%)
    ppermute x29, starting transfers between devices, swap(): return lax.ppermute(value, axis, pairs)  25 us
    ppermute x29, waiting for transfers between devices, swap(): return lax.ppermute(value, axis, pairs)  16.5 us
    pallas_call x15, Pallas kernels, call(): pl.pallas_call(kernel, in_specs=[SMEM] + [VMEM] * (len(values) - 1) + [AN...  9.67 us
    pallas_call x3, Pallas kernels, products(): pl.pallas_call(functools.partial(product_kernel, groups, chunks), in_spec...  6.21 us
    pallas_call x1, Pallas kernels, on_device(): pl.pallas_call(final_kernel, in_specs=[SMEM] + [VMEM] * len(small), out_s...  3.73 us
  transfers between devices with their start and end apart: 29, of which 11 were waited for; matrix products, arithmetic and copies ran while one was open for 1% of the time, Pallas kernels for 21%

profile of v18, /device:TPU:0, one launch (start us, length us, event | category | flops | bytes accessed | tf_op | source)
XLA Modules:
  0.0 62.0 jit_solution(10808116171771114963)
XLA Ops:
  0.0 2.6 %shard_map.37 = (f32[448,128]{1,0:T(8,128)S(1)}, f32[448,128]{1,0:T(8,128)S(1)}) custom-call(s32[1]{0:T(128)} %bitcast.core_ref, f32[3,1024,256]{2,1,0:T(8,128)} %gens_ref.5, f32[3,1024,256]{2,1,0:T(8,128)} %solved_ref.7), custom_call_target="tpu_custom_call" | custom-call | flops 805306368 | bytes 3145728 | tf_op jit(solution)/shard_map/pallas_call | solution.py:220
  2.7 0.5 collective-permute-start
  3.2 1.1 %collective-permute-done = f32[448,128]{1,0:T(8,128)S(1)} collective-permute-done((f32[448,128]{1,0:T(8,128)S(1)}, f32[448,128]{1,0:T(8,128)S(1)}, u32[]{:S(2)}, u32[]{:S(2)}) %collective-permute-start) | collective-permute-done | bytes 229408 | tf_op jit(solution)/shard_map/ppermute | solution.py:35
  4.3 0.4 collective-permute-start.1
  4.8 2.7 %collective-permute-start.8 = (f32[448,128]{1,0:T(8,128)S(1)}, f32[448,128]{1,0:T(8,128)S(1)}, u32[]{:S(2)}, u32[]{:S(2)}) collective-permute-start(f32[448,128]{1,0:T(8,128)S(1)} %add.38.refs_0_), channel_id=1, source_target_pairs={{0,2},{1,3},{2,0},{3,1},{4,6},{5,7},{6,4},{7,5},{8,10},{9,11},{10,... | collective-permute-start | bytes 688136 | tf_op jit(solution)/shard_map/ppermute | solution.py:35
  7.4 0.0 collective-permute-done.1.refs_1_
  7.5 1.2 %shard_map.39 = (f32[384,128]{1,0:T(8,128)S(1)}, f32[384,128]{1,0:T(8,128)S(1)}) custom-call(s32[1]{0:T(128)} %bitcast.core_ref, f32[3,1024,256]{2,1,0:T(8,128)S(1)} %copy-done.1, f32[3,1024,256]{2,1,0:T(8,128)S(1)} %copy-done, f32[1024,128]{1,0:T(8,128)S(1)} %copy-done.2, f32[8,128]{1,0:T(8,128)S(1)} %collective-permute-done.1.refs_1_), custom_call_target="tpu_custom_call" | custom-call | flops 603979776 | bytes 2621440 | tf_op jit(solution)/shard_map/pallas_call | solution.py:220
  8.6 0.1 collective-permute-start.5
  8.8 2.4 %shard_map.40 = (f32[576,128]{1,0:T(8,128)S(1)}, f32[576,128]{1,0:T(8,128)S(1)}, f32[320,128]{1,0:T(8,128)S(1)}, f32[320,128]{1,0:T(8,128)S(1)}) custom-call(s32[1]{0:T(128)} %bitcast.core_ref, f32[3,1024,256]{2,1,0:T(8,128)S(1)} %copy-done.1, f32[3,1024,256]{2,1,0:T(8,128)S(1)} %copy-done, f32[1024,128]{1,0:T(8,128)S(1)} %copy-done.2, ...), custom_call_target="tpu_custom_call" | custom-call | flops 1610612736 | bytes 4718592 | tf_op jit(solution)/shard_map/pallas_call | solution.py:220
  11.2 0.5 collective-permute-start.4
  11.7 0.0 collective-permute-done.5
  11.7 1.1 %collective-permute-start.6 = (f32[384,128]{1,0:T(8,128)S(1)}, f32[384,128]{1,0:T(8,128)S(1)}, u32[]{:S(2)}, u32[]{:S(2)}) collective-permute-start(f32[384,128]{1,0:T(8,128)S(1)} %add.40), channel_id=1, source_target_pairs={{0,2},{1,3},{2,0},{3,1},{4,6},{5,7},{6,4},{7,5},{8,10},{9,11},{10,... | collective-permute-start | bytes 589832 | tf_op jit(solution)/shard_map/ppermute | solution.py:35
  12.8 0.8 %collective-permute-done.8 = f32[448,128]{1,0:T(8,128)S(1)} collective-permute-done((f32[448,128]{1,0:T(8,128)S(1)}, f32[448,128]{1,0:T(8,128)S(1)}, u32[]{:S(2)}, u32[]{:S(2)}) %collective-permute-start.8) | collective-permute-done | bytes 229408 | tf_op jit(solution)/shard_map/ppermute | solution.py:35
  13.6 1.8 %collective-permute-start.9 = (f32[448,128]{1,0:T(8,128)S(1)}, f32[448,128]{1,0:T(8,128)S(1)}, u32[]{:S(2)}, u32[]{:S(2)}) collective-permute-start(f32[448,128]{1,0:T(8,128)S(1)} %add.43.own_ref.head_ref), channel_id=1, source_target_pairs={{0,4},{4,0},{8,12},{12,8},{16,20},{20,16},{24,28},{28,24},{1,5},{5... | collective-permute-start | bytes 688136 | tf_op jit(solution)/shard_map/ppermute | solution.py:35
  15.4 0.0 collective-permute-start.10
  15.4 0.5 collective-permute-start.2
  15.9 2.8 %collective-permute-done.6 = f32[384,128]{1,0:T(8,128)S(1)} collective-permute-done((f32[384,128]{1,0:T(8,128)S(1)}, f32[384,128]{1,0:T(8,128)S(1)}, u32[]{:S(2)}, u32[]{:S(2)}) %collective-permute-start.6) | collective-permute-done | bytes 196640 | tf_op jit(solution)/shard_map/ppermute | solution.py:35
  18.7 0.0 collective-permute-done.4.second_ref
  18.7 1.2 %collective-permute-start.7 = (f32[576,128]{1,0:T(8,128)S(1)}, f32[576,128]{1,0:T(8,128)S(1)}, u32[]{:S(2)}, u32[]{:S(2)}) collective-permute-start(f32[576,128]{1,0:T(8,128)S(1)} %shard_map.41), channel_id=1, source_target_pairs={{0,2},{1,3},{2,0},{3,1},{4,6},{5,7},{6,4},{7,5},{8,10},{9,11},{10,... | collective-permute-start | bytes 884744 | tf_op jit(solution)/shard_map/ppermute | solution.py:35
  19.9 1.5 %collective-permute-start.12 = (f32[384,128]{1,0:T(8,128)S(1)}, f32[384,128]{1,0:T(8,128)S(1)}, u32[]{:S(2)}, u32[]{:S(2)}) collective-permute-start(f32[384,128]{1,0:T(8,128)S(1)} %add.41.refs_0_.tail_ref.own_ref), channel_id=1, source_target_pairs={{0,4},{4,0},{8,12},{12,8},{16,20},{20,16},{24,28},{28,24},{1,5},{5... | collective-permute-start | bytes 589832 | tf_op jit(solution)/shard_map/ppermute | solution.py:35
  21.4 0.0 collective-permute-done.9.sib_ref.head_sib_ref
  21.4 0.1 collective-permute-start.11
  21.5 0.0 collective-permute-done.2
  21.5 1.6 %collective-permute-start.3 = (f32[320,128]{1,0:T(8,128)S(1)}, f32[320,128]{1,0:T(8,128)S(1)}, u32[]{:S(2)}, u32[]{:S(2)}) collective-permute-start(f32[320,128]{1,0:T(8,128)S(1)} %add.39.first_ref), channel_id=1, source_target_pairs={{0,8},{4,12},{8,0},{12,4},{16,24},{20,28},{24,16},{28,20},{1,9},{5... | collective-permute-start | bytes 491528 | tf_op jit(solution)/shard_map/ppermute | solution.py:35
  23.2 0.0 collective-permute-done.10.own_other_ref.head_other_ref
  23.2 0.3 collective-permute-start.14
  23.5 0.0 collective-permute-done.11.sib_other_ref
  23.5 2.3 %shard_map.42 = (f32[256,256]{1,0:T(8,128)S(1)}, f32[256,320]{1,0:T(8,128)S(1)}) custom-call(s32[1]{0:T(128)} %bitcast.core_ref, f32[448,128]{1,0:T(8,128)S(1)} %add.43.own_ref.head_ref, f32[448,128]{1,0:T(8,128)S(1)} %collective-permute-done.9.sib_ref.head_sib_ref, f32[448,128]{1,0:T(8,128)S(1)} %collective-permute-done.10.own_other_ref.head_other_ref, ...), custom_call_target="tpu_custom_call" | custom-call | flops 900000000 | bytes 1572868 | tf_op jit(solution)/shard_map/pallas_call | solution.py:309
  25.8 0.0 collective-permute-done.12.tail_sib_ref
  25.8 0.8 %shard_map.43 = (f32[640,128]{1,0:T(8,128)S(1)}, f32[576,128]{1,0:T(8,128)S(1)}) custom-call(s32[1]{0:T(128)} %bitcast.core_ref, f32[256,256]{1,0:T(8,128)S(1)} %get-tuple-element.34.inverse_ref, f32[256,320]{1,0:T(8,128)S(1)} %get-tuple-element.35.product_ref, f32[448,128]{1,0:T(8,128)S(1)} %add.43.own_ref.head_ref, ...), custom_call_target="tpu_custom_call" | custom-call | flops 650000000 | bytes 2097156 | tf_op jit(solution)/shard_map/pallas_call | solution.py:309
  26.6 0.3 collective-permute-done.7
  27.1 1.6 %collective-permute-start.19 = (f32[192,128]{1,0:T(8,128)S(1)}, f32[192,128]{1,0:T(8,128)S(1)}, u32[]{:S(2)}, u32[]{:S(2)}) collective-permute-start(f32[192,128]{1,0:T(8,128)S(1)} %shard_map.44.refs_0_), channel_id=1, source_target_pairs={{0,4},{4,0},{8,12},{12,8},{16,20},{20,16},{24,28},{28,24},{1,5},{5... | collective-permute-start | bytes 294920 | tf_op jit(solution)/shard_map/ppermute | solution.py:35
  28.7 0.6 collective-permute-start.17
  29.2 0.0 collective-permute-done.3.second_ref
  29.3 1.2 %collective-permute-start.13 = (f32[320,128]{1,0:T(8,128)S(1)}, f32[320,128]{1,0:T(8,128)S(1)}, u32[]{:S(2)}, u32[]{:S(2)}) collective-permute-start(f32[320,128]{1,0:T(8,128)S(1)} %shard_map.46), channel_id=1, source_target_pairs={{0,2},{1,3},{2,0},{3,1},{4,6},{5,7},{6,4},{7,5},{8,10},{9,11},{10,... | collective-permute-start | bytes 491528 | tf_op jit(solution)/shard_map/ppermute | solution.py:35
  30.5 0.0 collective-permute-done.14.own_other_ref
  30.5 0.4 shard_map.47
  30.9 1.6 %collective-permute-start.15 = (f32[320,128]{1,0:T(8,128)S(1)}, f32[320,128]{1,0:T(8,128)S(1)}, u32[]{:S(2)}, u32[]{:S(2)}) collective-permute-start(f32[320,128]{1,0:T(8,128)S(1)} %shard_map.47), channel_id=1, source_target_pairs={{0,8},{4,12},{8,0},{12,4},{16,24},{20,28},{24,16},{28,20},{1,9},{5... | collective-permute-start | bytes 491528 | tf_op jit(solution)/shard_map/ppermute | solution.py:35
  32.6 0.2 collective-permute-done.19
  32.8 1.7 %collective-permute-start.20 = (f32[192,128]{1,0:T(8,128)S(1)}, f32[192,128]{1,0:T(8,128)S(1)}, u32[]{:S(2)}, u32[]{:S(2)}) collective-permute-start(f32[192,128]{1,0:T(8,128)S(1)} %add.48.own_ref), channel_id=1, source_target_pairs={{0,8},{4,12},{8,0},{12,4},{16,24},{20,28},{24,16},{28,20},{1,9},{5... | collective-permute-start | bytes 294920 | tf_op jit(solution)/shard_map/ppermute | solution.py:35
  34.5 0.0 collective-permute-start.21
  34.5 1.5 %collective-permute-done.17 = f32[384,128]{1,0:T(8,128)S(1)} collective-permute-done((f32[384,128]{1,0:T(8,128)S(1)}, f32[384,128]{1,0:T(8,128)S(1)}, u32[]{:S(2)}, u32[]{:S(2)}) %collective-permute-start.17) | collective-permute-done | bytes 196640 | tf_op jit(solution)/shard_map/ppermute | solution.py:35
  36.1 0.8 %collective-permute-start.18 = (f32[384,128]{1,0:T(8,128)S(1)}, f32[384,128]{1,0:T(8,128)S(1)}, u32[]{:S(2)}, u32[]{:S(2)}) collective-permute-start(f32[384,128]{1,0:T(8,128)S(1)} %add.47.r_own_ref.own_ref), channel_id=1, source_target_pairs={{0,8},{4,12},{8,0},{12,4},{16,24},{20,28},{24,16},{28,20},{1,9},{5... | collective-permute-start | bytes 589832 | tf_op jit(solution)/shard_map/ppermute | solution.py:35
  36.9 0.0 collective-permute-done.13
  36.9 1.7 %collective-permute-done.20.sib_ref = f32[192,128]{1,0:T(8,128)S(1)} collective-permute-done((f32[192,128]{1,0:T(8,128)S(1)}, f32[192,128]{1,0:T(8,128)S(1)}, u32[]{:S(2)}, u32[]{:S(2)}) %collective-permute-start.20) | collective-permute-done | bytes 98336 | tf_op jit(solution)/shard_map/ppermute | solution.py:35
  38.6 0.0 collective-permute-start.22
  38.6 0.0 collective-permute-done.15
  38.6 1.9 %collective-permute-start.16 = (f32[320,128]{1,0:T(8,128)S(1)}, f32[320,128]{1,0:T(8,128)S(1)}, u32[]{:S(2)}, u32[]{:S(2)}) collective-permute-start(f32[320,128]{1,0:T(8,128)S(1)} %add_subtract_fusion.1), channel_id=1, source_target_pairs={{0,4},{4,0},{8,12},{12,8},{16,20},{20,16},{24,28},{28,24},{1,5},{5... | collective-permute-start | bytes 491528 | tf_op jit(solution)/shard_map/ppermute | solution.py:35
  40.5 2.5 %shard_map.48 = (f32[256,256]{1,0:T(8,128)S(1)}, f32[256,192]{1,0:T(8,128)S(1)}, f32[512,256]{1,0:T(8,128)S(1)}) custom-call(s32[1]{0:T(128)} %bitcast.core_ref, f32[192,128]{1,0:T(8,128)S(1)} %add.48.own_ref, f32[192,128]{1,0:T(8,128)S(1)} %collective-permute-done.20.sib_ref, f32[192,128]{1,0:T(8,128)S(1)} %collective-permute-done.21.own_other_ref, ...), custom_call_target="tpu_custom_call" | custom-call | flops 900000000 | bytes 1703940 | tf_op jit(solution)/shard_map/pallas_call | solution.py:309
  43.0 0.0 collective-permute-done.18.sib_ref
  43.1 0.3 collective-permute-start.24
  43.4 0.9 %shard_map.50 = (f32[384,128]{1,0:T(8,128)S(1)}, f32[384,128]{1,0:T(8,128)S(1)}, f32[320,128]{1,0:T(8,128)S(1)}) custom-call(s32[1]{0:T(128)} %bitcast.core_ref, f32[256,256]{1,0:T(8,128)S(1)} %get-tuple-element.38.refs_0_.inverse_ref, f32[256,192]{1,0:T(8,128)S(1)} %get-tuple-element.39.product_ref, f32[512,256]{1,0:T(8,128)S(1)} %get-tuple-element.40.turned_ref, ...), custom_call_target="tpu_custom_call" | custom-call | bytes 1933316 | tf_op jit(solution)/shard_map/pallas_call | solution.py:309
  44.3 0.2 collective-permute-done.24.sib_other_ref
  44.5 0.4 shard_map.51
  44.9 0.5 collective-permute-done.16
  45.5 0.1 collective-permute-start.27
  45.6 2.7 %collective-permute-start.26 = (f32[320,128]{1,0:T(8,128)S(1)}, f32[320,128]{1,0:T(8,128)S(1)}, u32[]{:S(2)}, u32[]{:S(2)}) collective-permute-start(f32[320,128]{1,0:T(8,128)S(1)} %add_subtract_fusion.refs_0_.own_ref), channel_id=1, source_target_pairs={{0,16},{4,20},{8,24},{12,28},{16,0},{20,4},{24,8},{28,12},{1,17},{... | collective-permute-start | bytes 491528 | tf_op jit(solution)/shard_map/ppermute | solution.py:35
  48.2 0.2 collective-permute-start.25
  48.4 2.2 %shard_map.53 = (bf16[1024,256]{1,0:T(8,128)(2,1)S(1)}, bf16[1024,256]{1,0:T(8,128)(2,1)S(1)}, f32[1024,128]{1,0:T(8,128)S(1)}) custom-call(s32[1]{0:T(128)} %bitcast.core_ref, f32[384,128]{1,0:T(8,128)S(1)} %get-tuple-element.43.first_ref.z1_ref, f32[384,128]{1,0:T(8,128)S(1)} %slice.50.z1_other_ref, ...), custom_call_target="tpu_custom_call" | custom-call | flops 1207959552 | bytes 7340036 | tf_op jit(solution)/shard_map/pallas_call | solution.py:309
  50.6 5.9 %collective-permute-done.26.value_ref = f32[320,128]{1,0:T(8,128)S(1)} collective-permute-done((f32[320,128]{1,0:T(8,128)S(1)}, f32[320,128]{1,0:T(8,128)S(1)}, u32[]{:S(2)}, u32[]{:S(2)}) %collective-permute-start.26) | collective-permute-done | bytes 163872 | tf_op jit(solution)/shard_map/ppermute | solution.py:35
  56.6 0.1 collective-permute-start.28
  56.7 0.0 collective-permute-done.25.own_other_ref
  56.7 1.4 %collective-permute-done.28.sib_other_ref = f32[320,128]{1,0:T(8,128)S(1)} collective-permute-done((f32[320,128]{1,0:T(8,128)S(1)}, f32[320,128]{1,0:T(8,128)S(1)}, u32[]{:S(2)}, u32[]{:S(2)}) %collective-permute-start.28) | collective-permute-done | bytes 163872 | tf_op jit(solution)/shard_map/ppermute | solution.py:35
  58.1 3.7 %shard_map.55 = f32[1024,128]{1,0:T(8,128)} custom-call(s32[1]{0:T(128)} %bitcast.core_ref, f32[320,128]{1,0:T(8,128)S(1)} %add_subtract_fusion.refs_0_.own_ref, f32[320,128]{1,0:T(8,128)S(1)} %collective-permute-done.25.own_other_ref, f32[320,128]{1,0:T(8,128)S(1)} %shard_map.54.sib_ref, f32[320,128]{1,0:T(8,128)S(1)} %collective-permute-done.28.sib_other_ref, ...), custom_call_target="tpu_custom_call" | custom-call | flops 1107296256 | bytes 3145728 | tf_op jit(solution)/shard_map/pallas_call | solution.py:509
  (40 shorter events, 0.5 us)
Async XLA Ops:
  0.0 7.5 %copy-start = (f32[3,1024,256]{2,1,0:T(8,128)S(1)}, f32[3,1024,256]{2,1,0:T(8,128)}, u32[]{:S(2)}) copy-start(f32[3,1024,256]{2,1,0:T(8,128)} %solved_ref.7) | copy-start | bytes 9437188
  0.0 7.5 %copy-start.1 = (f32[3,1024,256]{2,1,0:T(8,128)S(1)}, f32[3,1024,256]{2,1,0:T(8,128)}, u32[]{:S(2)}) copy-start(f32[3,1024,256]{2,1,0:T(8,128)} %gens_ref.5) | copy-start | bytes 9437188
  0.0 7.5 %copy-start.2 = (f32[1024,128]{1,0:T(8,128)S(1)}, f32[1024,128]{1,0:T(8,128)}, u32[]{:S(2)}) copy-start(f32[1024,128]{1,0:T(8,128)} %rhs_ref.1) | copy-start | bytes 1572868
  2.7 1.6 %collective-permute-start = (f32[448,128]{1,0:T(8,128)S(1)}, f32[448,128]{1,0:T(8,128)S(1)}, u32[]{:S(2)}, u32[]{:S(2)}) collective-permute-start(f32[448,128]{1,0:T(8,128)S(1)} %get-tuple-element.26), channel_id=1, source_target_pairs={{0,1},{1,0},{2,3},{3,2},{4,5},{5,4},{6,7},{7,6},{8,9},{9,8},{10,11... | collective-permute-start | bytes 688136 | tf_op jit(solution)/shard_map/ppermute | solution.py:35
  4.3 3.1 %collective-permute-start.1 = (f32[8,128]{1,0:T(8,128)S(1)}, f32[8,128]{1,0:T(8,128)S(1)}, u32[]{:S(2)}, u32[]{:S(2)}) collective-permute-start(f32[8,128]{1,0:T(8,128)S(1)} %shard_map.38), channel_id=1, source_target_pairs={{0,1},{1,0},{2,3},{3,2},{4,5},{5,4},{6,7},{7,6},{8,9},{9,8},{10,11... | collective-permute-start | bytes 12296 | tf_op jit(solution)/shard_map/ppermute | solution.py:35
  4.8 8.8 %collective-permute-start.8 = (f32[448,128]{1,0:T(8,128)S(1)}, f32[448,128]{1,0:T(8,128)S(1)}, u32[]{:S(2)}, u32[]{:S(2)}) collective-permute-start(f32[448,128]{1,0:T(8,128)S(1)} %add.38.refs_0_), channel_id=1, source_target_pairs={{0,2},{1,3},{2,0},{3,1},{4,6},{5,7},{6,4},{7,5},{8,10},{9,11},{10,... | collective-permute-start | bytes 688136 | tf_op jit(solution)/shard_map/ppermute | solution.py:35
  8.6 3.1 %collective-permute-start.5 = (f32[384,128]{1,0:T(8,128)S(1)}, f32[384,128]{1,0:T(8,128)S(1)}, u32[]{:S(2)}, u32[]{:S(2)}) collective-permute-start(f32[384,128]{1,0:T(8,128)S(1)} %get-tuple-element.28.refs_1_), channel_id=1, source_target_pairs={{0,1},{1,0},{2,3},{3,2},{4,5},{5,4},{6,7},{7,6},{8,9},{9,8},{10,11... | collective-permute-start | bytes 589832 | tf_op jit(solution)/shard_map/ppermute | solution.py:35
  11.2 7.5 %collective-permute-start.4 = (f32[576,128]{1,0:T(8,128)S(1)}, f32[576,128]{1,0:T(8,128)S(1)}, u32[]{:S(2)}, u32[]{:S(2)}) collective-permute-start(f32[576,128]{1,0:T(8,128)S(1)} %get-tuple-element.32), channel_id=1, source_target_pairs={{0,1},{1,0},{2,3},{3,2},{4,5},{5,4},{6,7},{7,6},{8,9},{9,8},{10,11... | collective-permute-start | bytes 884744 | tf_op jit(solution)/shard_map/ppermute | solution.py:35
  11.7 7.0 %collective-permute-start.6 = (f32[384,128]{1,0:T(8,128)S(1)}, f32[384,128]{1,0:T(8,128)S(1)}, u32[]{:S(2)}, u32[]{:S(2)}) collective-permute-start(f32[384,128]{1,0:T(8,128)S(1)} %add.40), channel_id=1, source_target_pairs={{0,2},{1,3},{2,0},{3,1},{4,6},{5,7},{6,4},{7,5},{8,10},{9,11},{10,... | collective-permute-start | bytes 589832 | tf_op jit(solution)/shard_map/ppermute | solution.py:35
  13.6 7.8 %collective-permute-start.9 = (f32[448,128]{1,0:T(8,128)S(1)}, f32[448,128]{1,0:T(8,128)S(1)}, u32[]{:S(2)}, u32[]{:S(2)}) collective-permute-start(f32[448,128]{1,0:T(8,128)S(1)} %add.43.own_ref.head_ref), channel_id=1, source_target_pairs={{0,4},{4,0},{8,12},{12,8},{16,20},{20,16},{24,28},{28,24},{1,5},{5... | collective-permute-start | bytes 688136 | tf_op jit(solution)/shard_map/ppermute | solution.py:35
  15.4 7.8 %collective-permute-start.10 = (f32[448,128]{1,0:T(8,128)S(1)}, f32[448,128]{1,0:T(8,128)S(1)}, u32[]{:S(2)}, u32[]{:S(2)}) collective-permute-start(f32[448,128]{1,0:T(8,128)S(1)} %add.43.own_ref.head_ref), channel_id=1, source_target_pairs={{0,1},{1,0},{2,3},{3,2},{4,5},{5,4},{6,7},{7,6},{8,9},{9,8},{10,11... | collective-permute-start | bytes 688136 | tf_op jit(solution)/shard_map/ppermute | solution.py:35
  15.4 6.1 %collective-permute-start.2 = (f32[320,128]{1,0:T(8,128)S(1)}, f32[320,128]{1,0:T(8,128)S(1)}, u32[]{:S(2)}, u32[]{:S(2)}) collective-permute-start(f32[320,128]{1,0:T(8,128)S(1)} %get-tuple-element.30), channel_id=1, source_target_pairs={{0,1},{1,0},{2,3},{3,2},{4,5},{5,4},{6,7},{7,6},{8,9},{9,8},{10,11... | collective-permute-start | bytes 491528 | tf_op jit(solution)/shard_map/ppermute | solution.py:35
  18.7 8.2 %collective-permute-start.7 = (f32[576,128]{1,0:T(8,128)S(1)}, f32[576,128]{1,0:T(8,128)S(1)}, u32[]{:S(2)}, u32[]{:S(2)}) collective-permute-start(f32[576,128]{1,0:T(8,128)S(1)} %shard_map.41), channel_id=1, source_target_pairs={{0,2},{1,3},{2,0},{3,1},{4,6},{5,7},{6,4},{7,5},{8,10},{9,11},{10,... | collective-permute-start | bytes 884744 | tf_op jit(solution)/shard_map/ppermute | solution.py:35
  19.9 5.9 %collective-permute-start.12 = (f32[384,128]{1,0:T(8,128)S(1)}, f32[384,128]{1,0:T(8,128)S(1)}, u32[]{:S(2)}, u32[]{:S(2)}) collective-permute-start(f32[384,128]{1,0:T(8,128)S(1)} %add.41.refs_0_.tail_ref.own_ref), channel_id=1, source_target_pairs={{0,4},{4,0},{8,12},{12,8},{16,20},{20,16},{24,28},{28,24},{1,5},{5... | collective-permute-start | bytes 589832 | tf_op jit(solution)/shard_map/ppermute | solution.py:35
  21.4 2.0 %collective-permute-start.11 = (f32[192,128]{1,0:T(8,128)S(1)}, f32[192,128]{1,0:T(8,128)S(1)}, u32[]{:S(2)}, u32[]{:S(2)}) collective-permute-start(f32[192,128]{1,0:T(8,128)S(1)} %slice.45), channel_id=1, source_target_pairs={{0,1},{1,0},{2,3},{3,2},{4,5},{5,4},{6,7},{7,6},{8,9},{9,8},{10,11... | collective-permute-start | bytes 294920 | tf_op jit(solution)/shard_map/ppermute | solution.py:35
  21.5 7.7 %collective-permute-start.3 = (f32[320,128]{1,0:T(8,128)S(1)}, f32[320,128]{1,0:T(8,128)S(1)}, u32[]{:S(2)}, u32[]{:S(2)}) collective-permute-start(f32[320,128]{1,0:T(8,128)S(1)} %add.39.first_ref), channel_id=1, source_target_pairs={{0,8},{4,12},{8,0},{12,4},{16,24},{20,28},{24,16},{28,20},{1,9},{5... | collective-permute-start | bytes 491528 | tf_op jit(solution)/shard_map/ppermute | solution.py:35
  23.2 7.3 %collective-permute-start.14 = (f32[256,128]{1,0:T(8,128)S(1)}, f32[256,128]{1,0:T(8,128)S(1)}, u32[]{:S(2)}, u32[]{:S(2)}) collective-permute-start(f32[256,128]{1,0:T(8,128)S(1)} %slice.47), channel_id=1, source_target_pairs={{0,1},{1,0},{2,3},{3,2},{4,5},{5,4},{6,7},{7,6},{8,9},{9,8},{10,11... | collective-permute-start | bytes 393224 | tf_op jit(solution)/shard_map/ppermute | solution.py:35
  27.1 5.7 %collective-permute-start.19 = (f32[192,128]{1,0:T(8,128)S(1)}, f32[192,128]{1,0:T(8,128)S(1)}, u32[]{:S(2)}, u32[]{:S(2)}) collective-permute-start(f32[192,128]{1,0:T(8,128)S(1)} %shard_map.44.refs_0_), channel_id=1, source_target_pairs={{0,4},{4,0},{8,12},{12,8},{16,20},{20,16},{24,28},{28,24},{1,5},{5... | collective-permute-start | bytes 294920 | tf_op jit(solution)/shard_map/ppermute | solution.py:35
  28.7 7.4 %collective-permute-start.17 = (f32[384,128]{1,0:T(8,128)S(1)}, f32[384,128]{1,0:T(8,128)S(1)}, u32[]{:S(2)}, u32[]{:S(2)}) collective-permute-start(f32[384,128]{1,0:T(8,128)S(1)} %shard_map.45.refs_0_), channel_id=1, source_target_pairs={{0,4},{4,0},{8,12},{12,8},{16,20},{20,16},{24,28},{28,24},{1,5},{5... | collective-permute-start | bytes 589832 | tf_op jit(solution)/shard_map/ppermute | solution.py:35
  29.3 7.6 %collective-permute-start.13 = (f32[320,128]{1,0:T(8,128)S(1)}, f32[320,128]{1,0:T(8,128)S(1)}, u32[]{:S(2)}, u32[]{:S(2)}) collective-permute-start(f32[320,128]{1,0:T(8,128)S(1)} %shard_map.46), channel_id=1, source_target_pairs={{0,2},{1,3},{2,0},{3,1},{4,6},{5,7},{6,4},{7,5},{8,10},{9,11},{10,... | collective-permute-start | bytes 491528 | tf_op jit(solution)/shard_map/ppermute | solution.py:35
  30.9 7.7 %collective-permute-start.15 = (f32[320,128]{1,0:T(8,128)S(1)}, f32[320,128]{1,0:T(8,128)S(1)}, u32[]{:S(2)}, u32[]{:S(2)}) collective-permute-start(f32[320,128]{1,0:T(8,128)S(1)} %shard_map.47), channel_id=1, source_target_pairs={{0,8},{4,12},{8,0},{12,4},{16,24},{20,28},{24,16},{28,20},{1,9},{5... | collective-permute-start | bytes 491528 | tf_op jit(solution)/shard_map/ppermute | solution.py:35
  32.8 5.8 %collective-permute-start.20 = (f32[192,128]{1,0:T(8,128)S(1)}, f32[192,128]{1,0:T(8,128)S(1)}, u32[]{:S(2)}, u32[]{:S(2)}) collective-permute-start(f32[192,128]{1,0:T(8,128)S(1)} %add.48.own_ref), channel_id=1, source_target_pairs={{0,8},{4,12},{8,0},{12,4},{16,24},{20,28},{24,16},{28,20},{1,9},{5... | collective-permute-start | bytes 294920 | tf_op jit(solution)/shard_map/ppermute | solution.py:35
  34.5 6.0 %collective-permute-start.21 = (f32[192,128]{1,0:T(8,128)S(1)}, f32[192,128]{1,0:T(8,128)S(1)}, u32[]{:S(2)}, u32[]{:S(2)}) collective-permute-start(f32[192,128]{1,0:T(8,128)S(1)} %add.48.own_ref), channel_id=1, source_target_pairs={{0,1},{1,0},{2,3},{3,2},{4,5},{5,4},{6,7},{7,6},{8,9},{9,8},{10,11... | collective-permute-start | bytes 294920 | tf_op jit(solution)/shard_map/ppermute | solution.py:35
  36.1 7.0 %collective-permute-start.18 = (f32[384,128]{1,0:T(8,128)S(1)}, f32[384,128]{1,0:T(8,128)S(1)}, u32[]{:S(2)}, u32[]{:S(2)}) collective-permute-start(f32[384,128]{1,0:T(8,128)S(1)} %add.47.r_own_ref.own_ref), channel_id=1, source_target_pairs={{0,8},{4,12},{8,0},{12,4},{16,24},{20,28},{24,16},{28,20},{1,9},{5... | collective-permute-start | bytes 589832 | tf_op jit(solution)/shard_map/ppermute | solution.py:35
  36.9 3.7 %collective-permute-start.23 = (f32[256,128]{1,0:T(8,128)S(1)}, f32[256,128]{1,0:T(8,128)S(1)}, u32[]{:S(2)}, u32[]{:S(2)}) collective-permute-start(f32[256,128]{1,0:T(8,128)S(1)} %slice.49), channel_id=1, source_target_pairs={{0,1},{1,0},{2,3},{3,2},{4,5},{5,4},{6,7},{7,6},{8,9},{9,8},{10,11... | collective-permute-start | bytes 393224 | tf_op jit(solution)/shard_map/ppermute | solution.py:35
  38.6 2.0 %collective-permute-start.22 = (f32[192,128]{1,0:T(8,128)S(1)}, f32[192,128]{1,0:T(8,128)S(1)}, u32[]{:S(2)}, u32[]{:S(2)}) collective-permute-start(f32[192,128]{1,0:T(8,128)S(1)} %collective-permute-done.20.sib_ref), channel_id=1, source_target_pairs={{0,1},{1,0},{2,3},{3,2},{4,5},{5,4},{6,7},{7,6},{8,9},{9,8},{10,11... | collective-permute-start | bytes 294920 | tf_op jit(solution)/shard_map/ppermute | solution.py:35
  38.6 6.8 %collective-permute-start.16 = (f32[320,128]{1,0:T(8,128)S(1)}, f32[320,128]{1,0:T(8,128)S(1)}, u32[]{:S(2)}, u32[]{:S(2)}) collective-permute-start(f32[320,128]{1,0:T(8,128)S(1)} %add_subtract_fusion.1), channel_id=1, source_target_pairs={{0,4},{4,0},{8,12},{12,8},{16,20},{20,16},{24,28},{28,24},{1,5},{5... | collective-permute-start | bytes 491528 | tf_op jit(solution)/shard_map/ppermute | solution.py:35
  43.1 1.4 %collective-permute-start.24 = (f32[256,128]{1,0:T(8,128)S(1)}, f32[256,128]{1,0:T(8,128)S(1)}, u32[]{:S(2)}, u32[]{:S(2)}) collective-permute-start(f32[256,128]{1,0:T(8,128)S(1)} %shard_map.49.sib_ref), channel_id=1, source_target_pairs={{0,1},{1,0},{2,3},{3,2},{4,5},{5,4},{6,7},{7,6},{8,9},{9,8},{10,11... | collective-permute-start | bytes 393224 | tf_op jit(solution)/shard_map/ppermute | solution.py:35
  45.5 2.9 %collective-permute-start.27 = (f32[1024,128]{1,0:T(8,128)S(1)}, f32[1024,128]{1,0:T(8,128)S(1)}, u32[]{:S(2)}, u32[]{:S(2)}) collective-permute-start(f32[1024,128]{1,0:T(8,128)S(1)} %shard_map.52), channel_id=1, source_target_pairs={{0,1},{1,0},{2,3},{3,2},{4,5},{5,4},{6,7},{7,6},{8,9},{9,8},{10,11... | collective-permute-start | bytes 1572872 | tf_op jit(solution)/shard_map/ppermute | solution.py:35
  45.6 11.0 %collective-permute-start.26 = (f32[320,128]{1,0:T(8,128)S(1)}, f32[320,128]{1,0:T(8,128)S(1)}, u32[]{:S(2)}, u32[]{:S(2)}) collective-permute-start(f32[320,128]{1,0:T(8,128)S(1)} %add_subtract_fusion.refs_0_.own_ref), channel_id=1, source_target_pairs={{0,16},{4,20},{8,24},{12,28},{16,0},{20,4},{24,8},{28,12},{1,17},{... | collective-permute-start | bytes 491528 | tf_op jit(solution)/shard_map/ppermute | solution.py:35
  48.2 8.5 %collective-permute-start.25 = (f32[320,128]{1,0:T(8,128)S(1)}, f32[320,128]{1,0:T(8,128)S(1)}, u32[]{:S(2)}, u32[]{:S(2)}) collective-permute-start(f32[320,128]{1,0:T(8,128)S(1)} %add_subtract_fusion.refs_0_.own_ref), channel_id=1, source_target_pairs={{0,1},{1,0},{2,3},{3,2},{4,5},{5,4},{6,7},{7,6},{8,9},{9,8},{10,11... | collective-permute-start | bytes 491528 | tf_op jit(solution)/shard_map/ppermute | solution.py:35
  56.6 1.5 %collective-permute-start.28 = (f32[320,128]{1,0:T(8,128)S(1)}, f32[320,128]{1,0:T(8,128)S(1)}, u32[]{:S(2)}, u32[]{:S(2)}) collective-permute-start(f32[320,128]{1,0:T(8,128)S(1)} %shard_map.54.sib_ref), channel_id=1, source_target_pairs={{0,1},{1,0},{2,3},{3,2},{4,5},{5,4},{6,7},{7,6},{8,9},{9,8},{10,11... | collective-permute-start | bytes 491528 | tf_op jit(solution)/shard_map/ppermute | solution.py:35

commit v19 on v18

--- a/solution.py
+++ b/solution.py
@@ -317,7 +317,8 @@
     )(*values, *after)
 
 
-def first_kernel(core_ref, inverse_ref, product_ref, head_ref, head_sib_ref, head_other_ref, tail_sib_ref, z_ref, out_ref):
+def first_kernel(core_ref, inverse_ref, product_ref, head_ref, head_sib_ref, head_other_ref, tail_ref, tail_other_ref, tail_sib_ref, *refs):
+    z_ref, out_ref, last_ref = refs
     core = core_ref[0]
     sib = jnp.concatenate([head_sib_ref[SYM:, :], unpack(tail_sib_ref)], axis=1)
     z = dot(inverse_ref[...], sib - product_ref[...])
@@ -325,6 +326,7 @@
     value = dot_turned(in_order(core, head_ref[SYM:, :], head_other_ref[SYM:, :]), z)
     out_ref[:SYM, :] = symmetric_half(core, value[:, :HALF])
     store(out_ref.at[SYM:], value[:, HALF:])
+    last_ref[...] = last_parts(core, in_order(core, tail_ref[:RANK, :], tail_other_ref[...]), z[:, HALF:])
 
 
 def last_parts(core, crossed, z):
@@ -333,12 +335,6 @@
 
 def lost_parts(core, value):
     return jnp.concatenate([symmetric_half(core, value[:, :HALF]), *pack(value[:, HALF:])], axis=0)
-
-
-def third_kernel(core_ref, own_ref, own_other_ref, z_ref, *refs):
-    core = core_ref[0]
-    crossed = in_order(core, own_ref[:RANK, :], own_other_ref[...])
-    refs[-1][...] = last_parts(core, crossed, unpack(z_ref.at[RANK:]))
 
 
 def middle_kernel(core_ref, inverse_ref, product_ref, turned_ref, own_ref, sib_ref, z_ref, z_sib_ref, out_ref):
@@ -461,16 +457,16 @@
         invert_kernel, [struct(RANK, RANK), struct(RANK, 2 * HALF + QUARTER)], INVERT_FLOPS,
         core, head, head_sib, head_other, p_sib_other, tail, scratch=((RANK, RANK),),
     )
-    z0, crossed = call(
-        first_kernel, [struct(2 * RANK + HALF), struct(SYM + RANK + HALF)], FIRST_FLOPS,
-        core, inverted, product, head, head_sib, head_other, tail_sib,
+    z0, crossed, lost = call(
+        first_kernel, [struct(2 * RANK + HALF), struct(SYM + RANK + HALF), struct(last)], FIRST_FLOPS,
+        core, inverted, product, head, head_sib, head_other, tail, tail_other, tail_sib,
     )
     p_own = call(subtract_kernel, struct(SYM), 0, core, near[:SYM], crossed[:SYM])
     r_own = call(subtract_kernel, struct(RANK + HALF), 0, core, near[SYM:], crossed[SYM:], after=(p_own,))
     third = over_child(
         call(add_kernel, struct(last), 0, core, third, swap(third, "rows", span_bits + 1), after=(r_own,))
     )
-    crossed = call(third_kernel, struct(last), THIRD_FLOPS, core, tail, tail_other, z0, after=(r_own,))
+    crossed = call(keep_kernel, struct(last), THIRD_FLOPS, core, lost, after=(r_own,))
     third = third - (crossed + swap(crossed, "rows", span_bits + 1))
     third = third + swap(third, "rows", span_bits)
 

time: 62.1 us -> 61.2 us (0.986)
  no operation moved by 1% of the time
where the time goes in v19:
time: 61.2 us; the launch traced here: 61 us
  starting transfers between devices  24.8 us (41%)
  Pallas kernels  19.4 us (32%)
  waiting for transfers between devices  16 us (26%)
    ppermute x29, starting transfers between devices, swap(): return lax.ppermute(value, axis, pairs)  24.8 us
    ppermute x29, waiting for transfers between devices, swap(): return lax.ppermute(value, axis, pairs)  16 us
    pallas_call x15, Pallas kernels, call(): pl.pallas_call(kernel, in_specs=[SMEM] + [VMEM] * (len(values) - 1) + [AN...  9.45 us
    pallas_call x3, Pallas kernels, products(): pl.pallas_call(functools.partial(product_kernel, groups, chunks), in_spec...  6.21 us
    pallas_call x1, Pallas kernels, on_device(): pl.pallas_call(final_kernel, in_specs=[SMEM] + [VMEM] * len(small), out_s...  3.73 us
  transfers between devices with their start and end apart: 29, of which 11 were waited for; matrix products, arithmetic and copies ran while one was open for 1% of the time, Pallas kernels for 21%

profile of v19, /device:TPU:0, one launch (start us, length us, event | category | flops | bytes accessed | tf_op | source)
XLA Modules:
  0.0 61.0 jit_solution(15350080667663545603)
XLA Ops:
  0.0 2.6 %shard_map.37 = (f32[448,128]{1,0:T(8,128)S(1)}, f32[448,128]{1,0:T(8,128)S(1)}) custom-call(s32[1]{0:T(128)} %bitcast.core_ref, f32[3,1024,256]{2,1,0:T(8,128)} %gens_ref.5, f32[3,1024,256]{2,1,0:T(8,128)} %solved_ref.7), custom_call_target="tpu_custom_call" | custom-call | flops 805306368 | bytes 3145728 | tf_op jit(solution)/shard_map/pallas_call | solution.py:220
  2.7 0.5 collective-permute-start
  3.2 1.1 %collective-permute-done = f32[448,128]{1,0:T(8,128)S(1)} collective-permute-done((f32[448,128]{1,0:T(8,128)S(1)}, f32[448,128]{1,0:T(8,128)S(1)}, u32[]{:S(2)}, u32[]{:S(2)}) %collective-permute-start) | collective-permute-done | bytes 229408 | tf_op jit(solution)/shard_map/ppermute | solution.py:35
  4.3 0.4 collective-permute-start.1
  4.8 2.7 %collective-permute-start.8 = (f32[448,128]{1,0:T(8,128)S(1)}, f32[448,128]{1,0:T(8,128)S(1)}, u32[]{:S(2)}, u32[]{:S(2)}) collective-permute-start(f32[448,128]{1,0:T(8,128)S(1)} %add.38.refs_0_), channel_id=1, source_target_pairs={{0,2},{1,3},{2,0},{3,1},{4,6},{5,7},{6,4},{7,5},{8,10},{9,11},{10,... | collective-permute-start | bytes 688136 | tf_op jit(solution)/shard_map/ppermute | solution.py:35
  7.4 0.0 collective-permute-done.1.refs_1_
  7.5 1.2 %shard_map.39 = (f32[384,128]{1,0:T(8,128)S(1)}, f32[384,128]{1,0:T(8,128)S(1)}) custom-call(s32[1]{0:T(128)} %bitcast.core_ref, f32[3,1024,256]{2,1,0:T(8,128)S(1)} %copy-done.1, f32[3,1024,256]{2,1,0:T(8,128)S(1)} %copy-done, f32[1024,128]{1,0:T(8,128)S(1)} %copy-done.2, f32[8,128]{1,0:T(8,128)S(1)} %collective-permute-done.1.refs_1_), custom_call_target="tpu_custom_call" | custom-call | flops 603979776 | bytes 2621440 | tf_op jit(solution)/shard_map/pallas_call | solution.py:220
  8.6 0.1 collective-permute-start.5
  8.8 2.4 %shard_map.40 = (f32[576,128]{1,0:T(8,128)S(1)}, f32[576,128]{1,0:T(8,128)S(1)}, f32[320,128]{1,0:T(8,128)S(1)}, f32[320,128]{1,0:T(8,128)S(1)}) custom-call(s32[1]{0:T(128)} %bitcast.core_ref, f32[3,1024,256]{2,1,0:T(8,128)S(1)} %copy-done.1, f32[3,1024,256]{2,1,0:T(8,128)S(1)} %copy-done, f32[1024,128]{1,0:T(8,128)S(1)} %copy-done.2, ...), custom_call_target="tpu_custom_call" | custom-call | flops 1610612736 | bytes 4718592 | tf_op jit(solution)/shard_map/pallas_call | solution.py:220
  11.2 0.5 collective-permute-start.4
  11.7 0.0 collective-permute-done.5
  11.7 1.1 %collective-permute-start.6 = (f32[384,128]{1,0:T(8,128)S(1)}, f32[384,128]{1,0:T(8,128)S(1)}, u32[]{:S(2)}, u32[]{:S(2)}) collective-permute-start(f32[384,128]{1,0:T(8,128)S(1)} %add.40), channel_id=1, source_target_pairs={{0,2},{1,3},{2,0},{3,1},{4,6},{5,7},{6,4},{7,5},{8,10},{9,11},{10,... | collective-permute-start | bytes 589832 | tf_op jit(solution)/shard_map/ppermute | solution.py:35
  12.8 0.8 %collective-permute-done.8 = f32[448,128]{1,0:T(8,128)S(1)} collective-permute-done((f32[448,128]{1,0:T(8,128)S(1)}, f32[448,128]{1,0:T(8,128)S(1)}, u32[]{:S(2)}, u32[]{:S(2)}) %collective-permute-start.8) | collective-permute-done | bytes 229408 | tf_op jit(solution)/shard_map/ppermute | solution.py:35
  13.6 1.8 %collective-permute-start.9 = (f32[448,128]{1,0:T(8,128)S(1)}, f32[448,128]{1,0:T(8,128)S(1)}, u32[]{:S(2)}, u32[]{:S(2)}) collective-permute-start(f32[448,128]{1,0:T(8,128)S(1)} %add.43.own_ref.head_ref), channel_id=1, source_target_pairs={{0,4},{4,0},{8,12},{12,8},{16,20},{20,16},{24,28},{28,24},{1,5},{5... | collective-permute-start | bytes 688136 | tf_op jit(solution)/shard_map/ppermute | solution.py:35
  15.4 0.0 collective-permute-start.10
  15.4 0.5 collective-permute-start.2
  15.9 2.8 %collective-permute-done.6 = f32[384,128]{1,0:T(8,128)S(1)} collective-permute-done((f32[384,128]{1,0:T(8,128)S(1)}, f32[384,128]{1,0:T(8,128)S(1)}, u32[]{:S(2)}, u32[]{:S(2)}) %collective-permute-start.6) | collective-permute-done | bytes 196640 | tf_op jit(solution)/shard_map/ppermute | solution.py:35
  18.7 0.0 collective-permute-done.4.second_ref
  18.7 1.2 %collective-permute-start.7 = (f32[576,128]{1,0:T(8,128)S(1)}, f32[576,128]{1,0:T(8,128)S(1)}, u32[]{:S(2)}, u32[]{:S(2)}) collective-permute-start(f32[576,128]{1,0:T(8,128)S(1)} %shard_map.41), channel_id=1, source_target_pairs={{0,2},{1,3},{2,0},{3,1},{4,6},{5,7},{6,4},{7,5},{8,10},{9,11},{10,... | collective-permute-start | bytes 884744 | tf_op jit(solution)/shard_map/ppermute | solution.py:35
  19.9 1.5 %collective-permute-start.13 = (f32[384,128]{1,0:T(8,128)S(1)}, f32[384,128]{1,0:T(8,128)S(1)}, u32[]{:S(2)}, u32[]{:S(2)}) collective-permute-start(f32[384,128]{1,0:T(8,128)S(1)} %add.41.refs_0_.tail_ref), channel_id=1, source_target_pairs={{0,4},{4,0},{8,12},{12,8},{16,20},{20,16},{24,28},{28,24},{1,5},{5... | collective-permute-start | bytes 589832 | tf_op jit(solution)/shard_map/ppermute | solution.py:35
  21.4 0.0 collective-permute-done.9.sib_ref.head_sib_ref
  21.4 0.1 collective-permute-start.11
  21.5 0.0 collective-permute-done.2
  21.5 0.6 collective-permute-start.12
  22.1 0.0 collective-permute-done.10.own_other_ref.head_other_ref
  22.1 1.6 %collective-permute-start.3 = (f32[320,128]{1,0:T(8,128)S(1)}, f32[320,128]{1,0:T(8,128)S(1)}, u32[]{:S(2)}, u32[]{:S(2)}) collective-permute-start(f32[320,128]{1,0:T(8,128)S(1)} %add.39.first_ref), channel_id=1, source_target_pairs={{0,8},{4,12},{8,0},{12,4},{16,24},{20,28},{24,16},{28,20},{1,9},{5... | collective-permute-start | bytes 491528 | tf_op jit(solution)/shard_map/ppermute | solution.py:35
  23.7 0.0 collective-permute-done.11.sib_other_ref
  23.8 2.3 %shard_map.42 = (f32[256,256]{1,0:T(8,128)S(1)}, f32[256,320]{1,0:T(8,128)S(1)}) custom-call(s32[1]{0:T(128)} %bitcast.core_ref, f32[448,128]{1,0:T(8,128)S(1)} %add.43.own_ref.head_ref, f32[448,128]{1,0:T(8,128)S(1)} %collective-permute-done.9.sib_ref.head_sib_ref, f32[448,128]{1,0:T(8,128)S(1)} %collective-permute-done.10.own_other_ref.head_other_ref, ...), custom_call_target="tpu_custom_call" | custom-call | flops 900000000 | bytes 1572868 | tf_op jit(solution)/shard_map/pallas_call | solution.py:309
  26.0 0.0 collective-permute-done.12.tail_other_ref
  26.1 0.0 collective-permute-done.13.tail_sib_ref
  26.1 1.0 %shard_map.43 = (f32[640,128]{1,0:T(8,128)S(1)}, f32[576,128]{1,0:T(8,128)S(1)}, f32[320,128]{1,0:T(8,128)S(1)}) custom-call(s32[1]{0:T(128)} %bitcast.core_ref, f32[256,256]{1,0:T(8,128)S(1)} %get-tuple-element.35.inverse_ref, f32[256,320]{1,0:T(8,128)S(1)} %get-tuple-element.36.product_ref, f32[448,128]{1,0:T(8,128)S(1)} %add.43.own_ref.head_ref, ...), custom_call_target="tpu_custom_call" | custom-call | flops 650000000 | bytes 2588676 | tf_op jit(solution)/shard_map/pallas_call | solution.py:309
  27.1 0.0 collective-permute-done.7
  27.2 1.4 %collective-permute-start.19 = (f32[192,128]{1,0:T(8,128)S(1)}, f32[192,128]{1,0:T(8,128)S(1)}, u32[]{:S(2)}, u32[]{:S(2)}) collective-permute-start(f32[192,128]{1,0:T(8,128)S(1)} %shard_map.44.refs_0_), channel_id=1, source_target_pairs={{0,4},{4,0},{8,12},{12,8},{16,20},{20,16},{24,28},{28,24},{1,5},{5... | collective-permute-start | bytes 294920 | tf_op jit(solution)/shard_map/ppermute | solution.py:35
  28.7 0.7 %collective-permute-start.17 = (f32[384,128]{1,0:T(8,128)S(1)}, f32[384,128]{1,0:T(8,128)S(1)}, u32[]{:S(2)}, u32[]{:S(2)}) collective-permute-start(f32[384,128]{1,0:T(8,128)S(1)} %shard_map.45.refs_0_), channel_id=1, source_target_pairs={{0,4},{4,0},{8,12},{12,8},{16,20},{20,16},{24,28},{28,24},{1,5},{5... | collective-permute-start | bytes 589832 | tf_op jit(solution)/shard_map/ppermute | solution.py:35
  29.4 0.0 collective-permute-done.3.second_ref
  29.4 1.2 %collective-permute-start.14 = (f32[320,128]{1,0:T(8,128)S(1)}, f32[320,128]{1,0:T(8,128)S(1)}, u32[]{:S(2)}, u32[]{:S(2)}) collective-permute-start(f32[320,128]{1,0:T(8,128)S(1)} %shard_map.46), channel_id=1, source_target_pairs={{0,2},{1,3},{2,0},{3,1},{4,6},{5,7},{6,4},{7,5},{8,10},{9,11},{10,... | collective-permute-start | bytes 491528 | tf_op jit(solution)/shard_map/ppermute | solution.py:35
  30.6 1.6 %collective-permute-start.15 = (f32[320,128]{1,0:T(8,128)S(1)}, f32[320,128]{1,0:T(8,128)S(1)}, u32[]{:S(2)}, u32[]{:S(2)}) collective-permute-start(f32[320,128]{1,0:T(8,128)S(1)} %shard_map.47), channel_id=1, source_target_pairs={{0,8},{4,12},{8,0},{12,4},{16,24},{20,28},{24,16},{28,20},{1,9},{5... | collective-permute-start | bytes 491528 | tf_op jit(solution)/shard_map/ppermute | solution.py:35
  32.2 0.8 %collective-permute-done.19 = f32[192,128]{1,0:T(8,128)S(1)} collective-permute-done((f32[192,128]{1,0:T(8,128)S(1)}, f32[192,128]{1,0:T(8,128)S(1)}, u32[]{:S(2)}, u32[]{:S(2)}) %collective-permute-start.19) | collective-permute-done | bytes 98336 | tf_op jit(solution)/shard_map/ppermute | solution.py:35
  33.0 1.5 %collective-permute-start.20 = (f32[192,128]{1,0:T(8,128)S(1)}, f32[192,128]{1,0:T(8,128)S(1)}, u32[]{:S(2)}, u32[]{:S(2)}) collective-permute-start(f32[192,128]{1,0:T(8,128)S(1)} %add.48.own_ref), channel_id=1, source_target_pairs={{0,8},{4,12},{8,0},{12,4},{16,24},{20,28},{24,16},{28,20},{1,9},{5... | collective-permute-start | bytes 294920 | tf_op jit(solution)/shard_map/ppermute | solution.py:35
  34.5 0.0 collective-permute-start.21
  34.5 1.4 %collective-permute-done.17 = f32[384,128]{1,0:T(8,128)S(1)} collective-permute-done((f32[384,128]{1,0:T(8,128)S(1)}, f32[384,128]{1,0:T(8,128)S(1)}, u32[]{:S(2)}, u32[]{:S(2)}) %collective-permute-start.17) | collective-permute-done | bytes 196640 | tf_op jit(solution)/shard_map/ppermute | solution.py:35
  36.0 1.1 %collective-permute-start.18 = (f32[384,128]{1,0:T(8,128)S(1)}, f32[384,128]{1,0:T(8,128)S(1)}, u32[]{:S(2)}, u32[]{:S(2)}) collective-permute-start(f32[384,128]{1,0:T(8,128)S(1)} %add.47.r_own_ref.own_ref), channel_id=1, source_target_pairs={{0,8},{4,12},{8,0},{12,4},{16,24},{20,28},{24,16},{28,20},{1,9},{5... | collective-permute-start | bytes 589832 | tf_op jit(solution)/shard_map/ppermute | solution.py:35
  37.1 0.0 collective-permute-start.23
  37.1 0.7 %collective-permute-done.20.sib_ref = f32[192,128]{1,0:T(8,128)S(1)} collective-permute-done((f32[192,128]{1,0:T(8,128)S(1)}, f32[192,128]{1,0:T(8,128)S(1)}, u32[]{:S(2)}, u32[]{:S(2)}) %collective-permute-start.20) | collective-permute-done | bytes 98336 | tf_op jit(solution)/shard_map/ppermute | solution.py:35
  37.8 0.0 collective-permute-start.22
  37.8 0.0 collective-permute-done.15
  37.8 1.6 %collective-permute-start.16 = (f32[320,128]{1,0:T(8,128)S(1)}, f32[320,128]{1,0:T(8,128)S(1)}, u32[]{:S(2)}, u32[]{:S(2)}) collective-permute-start(f32[320,128]{1,0:T(8,128)S(1)} %add_subtract_fusion.1), channel_id=1, source_target_pairs={{0,4},{4,0},{8,12},{12,8},{16,20},{20,16},{24,28},{28,24},{1,5},{5... | collective-permute-start | bytes 491528 | tf_op jit(solution)/shard_map/ppermute | solution.py:35
  39.4 0.0 collective-permute-done.21.own_other_ref
  39.4 2.5 %shard_map.48 = (f32[256,256]{1,0:T(8,128)S(1)}, f32[256,192]{1,0:T(8,128)S(1)}, f32[512,256]{1,0:T(8,128)S(1)}) custom-call(s32[1]{0:T(128)} %bitcast.core_ref, f32[192,128]{1,0:T(8,128)S(1)} %add.48.own_ref, f32[192,128]{1,0:T(8,128)S(1)} %collective-permute-done.20.sib_ref, f32[192,128]{1,0:T(8,128)S(1)} %collective-permute-done.21.own_other_ref, ...), custom_call_target="tpu_custom_call" | custom-call | flops 900000000 | bytes 1703940 | tf_op jit(solution)/shard_map/pallas_call | solution.py:309
  41.9 0.1 collective-permute-done.18.sib_ref
  42.0 0.2 collective-permute-start.24
  42.2 0.9 %shard_map.50 = (f32[384,128]{1,0:T(8,128)S(1)}, f32[384,128]{1,0:T(8,128)S(1)}, f32[320,128]{1,0:T(8,128)S(1)}) custom-call(s32[1]{0:T(128)} %bitcast.core_ref, f32[256,256]{1,0:T(8,128)S(1)} %get-tuple-element.39.refs_0_.inverse_ref, f32[256,192]{1,0:T(8,128)S(1)} %get-tuple-element.40.product_ref, f32[512,256]{1,0:T(8,128)S(1)} %get-tuple-element.41.turned_ref, ...), custom_call_target="tpu_custom_call" | custom-call | bytes 1933316 | tf_op jit(solution)/shard_map/pallas_call | solution.py:309
  43.2 0.3 collective-permute-done.24.sib_other_ref
  43.4 0.4 shard_map.51
  43.9 0.6 %collective-permute-done.16 = f32[320,128]{1,0:T(8,128)S(1)} collective-permute-done((f32[320,128]{1,0:T(8,128)S(1)}, f32[320,128]{1,0:T(8,128)S(1)}, u32[]{:S(2)}, u32[]{:S(2)}) %collective-permute-start.16) | collective-permute-done | bytes 163872 | tf_op jit(solution)/shard_map/ppermute | solution.py:35
  44.6 0.1 collective-permute-start.27
  44.7 2.7 %collective-permute-start.26 = (f32[320,128]{1,0:T(8,128)S(1)}, f32[320,128]{1,0:T(8,128)S(1)}, u32[]{:S(2)}, u32[]{:S(2)}) collective-permute-start(f32[320,128]{1,0:T(8,128)S(1)} %add_subtract_fusion.refs_0_.own_ref), channel_id=1, source_target_pairs={{0,16},{4,20},{8,24},{12,28},{16,0},{20,4},{24,8},{28,12},{1,17},{... | collective-permute-start | bytes 491528 | tf_op jit(solution)/shard_map/ppermute | solution.py:35
  47.3 0.2 collective-permute-start.25
  47.5 2.2 %shard_map.53 = (bf16[1024,256]{1,0:T(8,128)(2,1)S(1)}, bf16[1024,256]{1,0:T(8,128)(2,1)S(1)}, f32[1024,128]{1,0:T(8,128)S(1)}) custom-call(s32[1]{0:T(128)} %bitcast.core_ref, f32[384,128]{1,0:T(8,128)S(1)} %get-tuple-element.44.first_ref.z1_ref, f32[384,128]{1,0:T(8,128)S(1)} %slice.50.z1_other_ref, f32[640,128]{1,0:T(8,128)S(1)} %get-tuple-element.45.second_ref.z0_ref, ...), custom_call_target="tpu_custom_call" | custom-call | flops 1207959552 | bytes 7340036 | tf_op jit(solution)/shard_map/pallas_call | solution.py:309
  49.7 5.9 %collective-permute-done.26.value_ref = f32[320,128]{1,0:T(8,128)S(1)} collective-permute-done((f32[320,128]{1,0:T(8,128)S(1)}, f32[320,128]{1,0:T(8,128)S(1)}, u32[]{:S(2)}, u32[]{:S(2)}) %collective-permute-start.26) | collective-permute-done | bytes 163872 | tf_op jit(solution)/shard_map/ppermute | solution.py:35
  55.7 0.1 collective-permute-start.28
  55.8 0.0 collective-permute-done.25.own_other_ref
  55.8 1.4 %collective-permute-done.28.sib_other_ref = f32[320,128]{1,0:T(8,128)S(1)} collective-permute-done((f32[320,128]{1,0:T(8,128)S(1)}, f32[320,128]{1,0:T(8,128)S(1)}, u32[]{:S(2)}, u32[]{:S(2)}) %collective-permute-start.28) | collective-permute-done | bytes 163872 | tf_op jit(solution)/shard_map/ppermute | solution.py:35
  57.2 3.7 %shard_map.55 = f32[1024,128]{1,0:T(8,128)} custom-call(s32[1]{0:T(128)} %bitcast.core_ref, f32[320,128]{1,0:T(8,128)S(1)} %add_subtract_fusion.refs_0_.own_ref, f32[320,128]{1,0:T(8,128)S(1)} %collective-permute-done.25.own_other_ref, f32[320,128]{1,0:T(8,128)S(1)} %shard_map.54.sib_ref, f32[320,128]{1,0:T(8,128)S(1)} %collective-permute-done.28.sib_other_ref, ...), custom_call_target="tpu_custom_call" | custom-call | flops 1107296256 | bytes 3145728 | tf_op jit(solution)/shard_map/pallas_call | solution.py:505
  (40 shorter events, 0.6 us)
Async XLA Ops:
  0.0 7.5 %copy-start = (f32[3,1024,256]{2,1,0:T(8,128)S(1)}, f32[3,1024,256]{2,1,0:T(8,128)}, u32[]{:S(2)}) copy-start(f32[3,1024,256]{2,1,0:T(8,128)} %solved_ref.7) | copy-start | bytes 9437188
  0.0 7.5 %copy-start.1 = (f32[3,1024,256]{2,1,0:T(8,128)S(1)}, f32[3,1024,256]{2,1,0:T(8,128)}, u32[]{:S(2)}) copy-start(f32[3,1024,256]{2,1,0:T(8,128)} %gens_ref.5) | copy-start | bytes 9437188
  0.0 7.5 %copy-start.2 = (f32[1024,128]{1,0:T(8,128)S(1)}, f32[1024,128]{1,0:T(8,128)}, u32[]{:S(2)}) copy-start(f32[1024,128]{1,0:T(8,128)} %rhs_ref.1) | copy-start | bytes 1572868
  2.7 1.6 %collective-permute-start = (f32[448,128]{1,0:T(8,128)S(1)}, f32[448,128]{1,0:T(8,128)S(1)}, u32[]{:S(2)}, u32[]{:S(2)}) collective-permute-start(f32[448,128]{1,0:T(8,128)S(1)} %get-tuple-element.27), channel_id=1, source_target_pairs={{0,1},{1,0},{2,3},{3,2},{4,5},{5,4},{6,7},{7,6},{8,9},{9,8},{10,11... | collective-permute-start | bytes 688136 | tf_op jit(solution)/shard_map/ppermute | solution.py:35
  4.3 3.1 %collective-permute-start.1 = (f32[8,128]{1,0:T(8,128)S(1)}, f32[8,128]{1,0:T(8,128)S(1)}, u32[]{:S(2)}, u32[]{:S(2)}) collective-permute-start(f32[8,128]{1,0:T(8,128)S(1)} %shard_map.38), channel_id=1, source_target_pairs={{0,1},{1,0},{2,3},{3,2},{4,5},{5,4},{6,7},{7,6},{8,9},{9,8},{10,11... | collective-permute-start | bytes 12296 | tf_op jit(solution)/shard_map/ppermute | solution.py:35
  4.8 8.8 %collective-permute-start.8 = (f32[448,128]{1,0:T(8,128)S(1)}, f32[448,128]{1,0:T(8,128)S(1)}, u32[]{:S(2)}, u32[]{:S(2)}) collective-permute-start(f32[448,128]{1,0:T(8,128)S(1)} %add.38.refs_0_), channel_id=1, source_target_pairs={{0,2},{1,3},{2,0},{3,1},{4,6},{5,7},{6,4},{7,5},{8,10},{9,11},{10,... | collective-permute-start | bytes 688136 | tf_op jit(solution)/shard_map/ppermute | solution.py:35
  8.6 3.1 %collective-permute-start.5 = (f32[384,128]{1,0:T(8,128)S(1)}, f32[384,128]{1,0:T(8,128)S(1)}, u32[]{:S(2)}, u32[]{:S(2)}) collective-permute-start(f32[384,128]{1,0:T(8,128)S(1)} %get-tuple-element.29.refs_1_), channel_id=1, source_target_pairs={{0,1},{1,0},{2,3},{3,2},{4,5},{5,4},{6,7},{7,6},{8,9},{9,8},{10,11... | collective-permute-start | bytes 589832 | tf_op jit(solution)/shard_map/ppermute | solution.py:35
  11.2 7.5 %collective-permute-start.4 = (f32[576,128]{1,0:T(8,128)S(1)}, f32[576,128]{1,0:T(8,128)S(1)}, u32[]{:S(2)}, u32[]{:S(2)}) collective-permute-start(f32[576,128]{1,0:T(8,128)S(1)} %get-tuple-element.33), channel_id=1, source_target_pairs={{0,1},{1,0},{2,3},{3,2},{4,5},{5,4},{6,7},{7,6},{8,9},{9,8},{10,11... | collective-permute-start | bytes 884744 | tf_op jit(solution)/shard_map/ppermute | solution.py:35
  11.7 7.0 %collective-permute-start.6 = (f32[384,128]{1,0:T(8,128)S(1)}, f32[384,128]{1,0:T(8,128)S(1)}, u32[]{:S(2)}, u32[]{:S(2)}) collective-permute-start(f32[384,128]{1,0:T(8,128)S(1)} %add.40), channel_id=1, source_target_pairs={{0,2},{1,3},{2,0},{3,1},{4,6},{5,7},{6,4},{7,5},{8,10},{9,11},{10,... | collective-permute-start | bytes 589832 | tf_op jit(solution)/shard_map/ppermute | solution.py:35
  13.6 7.8 %collective-permute-start.9 = (f32[448,128]{1,0:T(8,128)S(1)}, f32[448,128]{1,0:T(8,128)S(1)}, u32[]{:S(2)}, u32[]{:S(2)}) collective-permute-start(f32[448,128]{1,0:T(8,128)S(1)} %add.43.own_ref.head_ref), channel_id=1, source_target_pairs={{0,4},{4,0},{8,12},{12,8},{16,20},{20,16},{24,28},{28,24},{1,5},{5... | collective-permute-start | bytes 688136 | tf_op jit(solution)/shard_map/ppermute | solution.py:35
  15.4 6.7 %collective-permute-start.10 = (f32[448,128]{1,0:T(8,128)S(1)}, f32[448,128]{1,0:T(8,128)S(1)}, u32[]{:S(2)}, u32[]{:S(2)}) collective-permute-start(f32[448,128]{1,0:T(8,128)S(1)} %add.43.own_ref.head_ref), channel_id=1, source_target_pairs={{0,1},{1,0},{2,3},{3,2},{4,5},{5,4},{6,7},{7,6},{8,9},{9,8},{10,11... | collective-permute-start | bytes 688136 | tf_op jit(solution)/shard_map/ppermute | solution.py:35
  15.4 6.1 %collective-permute-start.2 = (f32[320,128]{1,0:T(8,128)S(1)}, f32[320,128]{1,0:T(8,128)S(1)}, u32[]{:S(2)}, u32[]{:S(2)}) collective-permute-start(f32[320,128]{1,0:T(8,128)S(1)} %get-tuple-element.31), channel_id=1, source_target_pairs={{0,1},{1,0},{2,3},{3,2},{4,5},{5,4},{6,7},{7,6},{8,9},{9,8},{10,11... | collective-permute-start | bytes 491528 | tf_op jit(solution)/shard_map/ppermute | solution.py:35
  18.7 8.4 %collective-permute-start.7 = (f32[576,128]{1,0:T(8,128)S(1)}, f32[576,128]{1,0:T(8,128)S(1)}, u32[]{:S(2)}, u32[]{:S(2)}) collective-permute-start(f32[576,128]{1,0:T(8,128)S(1)} %shard_map.41), channel_id=1, source_target_pairs={{0,2},{1,3},{2,0},{3,1},{4,6},{5,7},{6,4},{7,5},{8,10},{9,11},{10,... | collective-permute-start | bytes 884744 | tf_op jit(solution)/shard_map/ppermute | solution.py:35
  19.9 6.2 %collective-permute-start.13 = (f32[384,128]{1,0:T(8,128)S(1)}, f32[384,128]{1,0:T(8,128)S(1)}, u32[]{:S(2)}, u32[]{:S(2)}) collective-permute-start(f32[384,128]{1,0:T(8,128)S(1)} %add.41.refs_0_.tail_ref), channel_id=1, source_target_pairs={{0,4},{4,0},{8,12},{12,8},{16,20},{20,16},{24,28},{28,24},{1,5},{5... | collective-permute-start | bytes 589832 | tf_op jit(solution)/shard_map/ppermute | solution.py:35
  21.4 2.3 %collective-permute-start.11 = (f32[192,128]{1,0:T(8,128)S(1)}, f32[192,128]{1,0:T(8,128)S(1)}, u32[]{:S(2)}, u32[]{:S(2)}) collective-permute-start(f32[192,128]{1,0:T(8,128)S(1)} %slice.45), channel_id=1, source_target_pairs={{0,1},{1,0},{2,3},{3,2},{4,5},{5,4},{6,7},{7,6},{8,9},{9,8},{10,11... | collective-permute-start | bytes 294920 | tf_op jit(solution)/shard_map/ppermute | solution.py:35
  21.5 4.5 %collective-permute-start.12 = (f32[256,128]{1,0:T(8,128)S(1)}, f32[256,128]{1,0:T(8,128)S(1)}, u32[]{:S(2)}, u32[]{:S(2)}) collective-permute-start(f32[256,128]{1,0:T(8,128)S(1)} %slice.46), channel_id=1, source_target_pairs={{0,1},{1,0},{2,3},{3,2},{4,5},{5,4},{6,7},{7,6},{8,9},{9,8},{10,11... | collective-permute-start | bytes 393224 | tf_op jit(solution)/shard_map/ppermute | solution.py:35
  22.1 7.3 %collective-permute-start.3 = (f32[320,128]{1,0:T(8,128)S(1)}, f32[320,128]{1,0:T(8,128)S(1)}, u32[]{:S(2)}, u32[]{:S(2)}) collective-permute-start(f32[320,128]{1,0:T(8,128)S(1)} %add.39.first_ref), channel_id=1, source_target_pairs={{0,8},{4,12},{8,0},{12,4},{16,24},{20,28},{24,16},{28,20},{1,9},{5... | collective-permute-start | bytes 491528 | tf_op jit(solution)/shard_map/ppermute | solution.py:35
  27.2 5.8 %collective-permute-start.19 = (f32[192,128]{1,0:T(8,128)S(1)}, f32[192,128]{1,0:T(8,128)S(1)}, u32[]{:S(2)}, u32[]{:S(2)}) collective-permute-start(f32[192,128]{1,0:T(8,128)S(1)} %shard_map.44.refs_0_), channel_id=1, source_target_pairs={{0,4},{4,0},{8,12},{12,8},{16,20},{20,16},{24,28},{28,24},{1,5},{5... | collective-permute-start | bytes 294920 | tf_op jit(solution)/shard_map/ppermute | solution.py:35
  28.7 7.3 %collective-permute-start.17 = (f32[384,128]{1,0:T(8,128)S(1)}, f32[384,128]{1,0:T(8,128)S(1)}, u32[]{:S(2)}, u32[]{:S(2)}) collective-permute-start(f32[384,128]{1,0:T(8,128)S(1)} %shard_map.45.refs_0_), channel_id=1, source_target_pairs={{0,4},{4,0},{8,12},{12,8},{16,20},{20,16},{24,28},{28,24},{1,5},{5... | collective-permute-start | bytes 589832 | tf_op jit(solution)/shard_map/ppermute | solution.py:35
  29.4 7.6 %collective-permute-start.14 = (f32[320,128]{1,0:T(8,128)S(1)}, f32[320,128]{1,0:T(8,128)S(1)}, u32[]{:S(2)}, u32[]{:S(2)}) collective-permute-start(f32[320,128]{1,0:T(8,128)S(1)} %shard_map.46), channel_id=1, source_target_pairs={{0,2},{1,3},{2,0},{3,1},{4,6},{5,7},{6,4},{7,5},{8,10},{9,11},{10,... | collective-permute-start | bytes 491528 | tf_op jit(solution)/shard_map/ppermute | solution.py:35
  30.6 7.2 %collective-permute-start.15 = (f32[320,128]{1,0:T(8,128)S(1)}, f32[320,128]{1,0:T(8,128)S(1)}, u32[]{:S(2)}, u32[]{:S(2)}) collective-permute-start(f32[320,128]{1,0:T(8,128)S(1)} %shard_map.47), channel_id=1, source_target_pairs={{0,8},{4,12},{8,0},{12,4},{16,24},{20,28},{24,16},{28,20},{1,9},{5... | collective-permute-start | bytes 491528 | tf_op jit(solution)/shard_map/ppermute | solution.py:35
  33.0 4.8 %collective-permute-start.20 = (f32[192,128]{1,0:T(8,128)S(1)}, f32[192,128]{1,0:T(8,128)S(1)}, u32[]{:S(2)}, u32[]{:S(2)}) collective-permute-start(f32[192,128]{1,0:T(8,128)S(1)} %add.48.own_ref), channel_id=1, source_target_pairs={{0,8},{4,12},{8,0},{12,4},{16,24},{20,28},{24,16},{28,20},{1,9},{5... | collective-permute-start | bytes 294920 | tf_op jit(solution)/shard_map/ppermute | solution.py:35
  34.5 4.9 %collective-permute-start.21 = (f32[192,128]{1,0:T(8,128)S(1)}, f32[192,128]{1,0:T(8,128)S(1)}, u32[]{:S(2)}, u32[]{:S(2)}) collective-permute-start(f32[192,128]{1,0:T(8,128)S(1)} %add.48.own_ref), channel_id=1, source_target_pairs={{0,1},{1,0},{2,3},{3,2},{4,5},{5,4},{6,7},{7,6},{8,9},{9,8},{10,11... | collective-permute-start | bytes 294920 | tf_op jit(solution)/shard_map/ppermute | solution.py:35
  36.0 6.0 %collective-permute-start.18 = (f32[384,128]{1,0:T(8,128)S(1)}, f32[384,128]{1,0:T(8,128)S(1)}, u32[]{:S(2)}, u32[]{:S(2)}) collective-permute-start(f32[384,128]{1,0:T(8,128)S(1)} %add.47.r_own_ref.own_ref), channel_id=1, source_target_pairs={{0,8},{4,12},{8,0},{12,4},{16,24},{20,28},{24,16},{28,20},{1,9},{5... | collective-permute-start | bytes 589832 | tf_op jit(solution)/shard_map/ppermute | solution.py:35
  37.1 2.3 %collective-permute-start.23 = (f32[256,128]{1,0:T(8,128)S(1)}, f32[256,128]{1,0:T(8,128)S(1)}, u32[]{:S(2)}, u32[]{:S(2)}) collective-permute-start(f32[256,128]{1,0:T(8,128)S(1)} %slice.49), channel_id=1, source_target_pairs={{0,1},{1,0},{2,3},{3,2},{4,5},{5,4},{6,7},{7,6},{8,9},{9,8},{10,11... | collective-permute-start | bytes 393224 | tf_op jit(solution)/shard_map/ppermute | solution.py:35
  37.8 1.6 %collective-permute-start.22 = (f32[192,128]{1,0:T(8,128)S(1)}, f32[192,128]{1,0:T(8,128)S(1)}, u32[]{:S(2)}, u32[]{:S(2)}) collective-permute-start(f32[192,128]{1,0:T(8,128)S(1)} %collective-permute-done.20.sib_ref), channel_id=1, source_target_pairs={{0,1},{1,0},{2,3},{3,2},{4,5},{5,4},{6,7},{7,6},{8,9},{9,8},{10,11... | collective-permute-start | bytes 294920 | tf_op jit(solution)/shard_map/ppermute | solution.py:35
  37.8 6.7 %collective-permute-start.16 = (f32[320,128]{1,0:T(8,128)S(1)}, f32[320,128]{1,0:T(8,128)S(1)}, u32[]{:S(2)}, u32[]{:S(2)}) collective-permute-start(f32[320,128]{1,0:T(8,128)S(1)} %add_subtract_fusion.1), channel_id=1, source_target_pairs={{0,4},{4,0},{8,12},{12,8},{16,20},{20,16},{24,28},{28,24},{1,5},{5... | collective-permute-start | bytes 491528 | tf_op jit(solution)/shard_map/ppermute | solution.py:35
  42.0 1.4 %collective-permute-start.24 = (f32[256,128]{1,0:T(8,128)S(1)}, f32[256,128]{1,0:T(8,128)S(1)}, u32[]{:S(2)}, u32[]{:S(2)}) collective-permute-start(f32[256,128]{1,0:T(8,128)S(1)} %shard_map.49.sib_ref), channel_id=1, source_target_pairs={{0,1},{1,0},{2,3},{3,2},{4,5},{5,4},{6,7},{7,6},{8,9},{9,8},{10,11... | collective-permute-start | bytes 393224 | tf_op jit(solution)/shard_map/ppermute | solution.py:35
  44.6 2.9 %collective-permute-start.27 = (f32[1024,128]{1,0:T(8,128)S(1)}, f32[1024,128]{1,0:T(8,128)S(1)}, u32[]{:S(2)}, u32[]{:S(2)}) collective-permute-start(f32[1024,128]{1,0:T(8,128)S(1)} %shard_map.52), channel_id=1, source_target_pairs={{0,1},{1,0},{2,3},{3,2},{4,5},{5,4},{6,7},{7,6},{8,9},{9,8},{10,11... | collective-permute-start | bytes 1572872 | tf_op jit(solution)/shard_map/ppermute | solution.py:35
  44.7 11.0 %collective-permute-start.26 = (f32[320,128]{1,0:T(8,128)S(1)}, f32[320,128]{1,0:T(8,128)S(1)}, u32[]{:S(2)}, u32[]{:S(2)}) collective-permute-start(f32[320,128]{1,0:T(8,128)S(1)} %add_subtract_fusion.refs_0_.own_ref), channel_id=1, source_target_pairs={{0,16},{4,20},{8,24},{12,28},{16,0},{20,4},{24,8},{28,12},{1,17},{... | collective-permute-start | bytes 491528 | tf_op jit(solution)/shard_map/ppermute | solution.py:35
  47.3 8.5 %collective-permute-start.25 = (f32[320,128]{1,0:T(8,128)S(1)}, f32[320,128]{1,0:T(8,128)S(1)}, u32[]{:S(2)}, u32[]{:S(2)}) collective-permute-start(f32[320,128]{1,0:T(8,128)S(1)} %add_subtract_fusion.refs_0_.own_ref), channel_id=1, source_target_pairs={{0,1},{1,0},{2,3},{3,2},{4,5},{5,4},{6,7},{7,6},{8,9},{9,8},{10,11... | collective-permute-start | bytes 491528 | tf_op jit(solution)/shard_map/ppermute | solution.py:35
  55.7 1.5 %collective-permute-start.28 = (f32[320,128]{1,0:T(8,128)S(1)}, f32[320,128]{1,0:T(8,128)S(1)}, u32[]{:S(2)}, u32[]{:S(2)}) collective-permute-start(f32[320,128]{1,0:T(8,128)S(1)} %shard_map.54.sib_ref), channel_id=1, source_target_pairs={{0,1},{1,0},{2,3},{3,2},{4,5},{5,4},{6,7},{7,6},{8,9},{9,8},{10,11... | collective-permute-start | bytes 491528 | tf_op jit(solution)/shard_map/ppermute | solution.py:35

commit v20 on v19

--- a/solution.py
+++ b/solution.py
@@ -15,7 +15,7 @@
 TOLERANCE = 1e-7
 DIVERGED = 1e4
 FIRST_FLOPS = 6.5e8
-INVERT_FLOPS = 9e8
+INVERT_FLOPS = 5e8
 INVERT_SECOND = 9e8
 MIDDLE_FLOPS = 0
 CROSS_FLOPS = 0
@@ -445,8 +445,8 @@
     parts = [(keep, swap(send, "sub", 0)) for keep, send in zip(parts[::2], parts[1::2])]
     head = over_child(head)
     tail = over_child(parts[0][0] + parts[0][1])
-    near = over_child(call(add_kernel, struct(SYM + RANK + HALF), 0, core, *parts[1], after=(tail,)))
     third = parts[2][0] + parts[2][1]
+    near = over_child(call(add_kernel, struct(SYM + RANK + HALF), 0, core, *parts[1], after=(third,)))
 
     head_sib = swap(head, "rows", span_bits)
     tail_sib = swap(tail, "rows", span_bits)

time: 61.2 us -> 61.5 us (level)
  transfers between devices with their start and end apart: 29 -> 29, of which waited for: 11 -> 10; matrix products, arithmetic and copies ran while one was open for 1% -> 1% of each run, Pallas kernels for 21% -> 21%
where the time goes in v20:
time: 61.5 us; the launch traced here: 61.4 us
  starting transfers between devices  24.9 us (40%)
  Pallas kernels  19.4 us (32%)
  waiting for transfers between devices  16.2 us (26%)
    ppermute x29, starting transfers between devices, swap(): return lax.ppermute(value, axis, pairs)  24.9 us
    ppermute x29, waiting for transfers between devices, swap(): return lax.ppermute(value, axis, pairs)  16.2 us
    pallas_call x15, Pallas kernels, call(): pl.pallas_call(kernel, in_specs=[SMEM] + [VMEM] * (len(values) - 1) + [AN...  9.45 us
    pallas_call x3, Pallas kernels, products(): pl.pallas_call(functools.partial(product_kernel, groups, chunks), in_spec...  6.21 us
    pallas_call x1, Pallas kernels, on_device(): pl.pallas_call(final_kernel, in_specs=[SMEM] + [VMEM] * len(small), out_s...  3.73 us
  transfers between devices with their start and end apart: 29, of which 10 were waited for; matrix products, arithmetic and copies ran while one was open for 1% of the time, Pallas kernels for 21%

profile of v20, /device:TPU:0, one launch (start us, length us, event | category | flops | bytes accessed | tf_op | source)
XLA Modules:
  0.0 61.4 jit_solution(6860798719330644016)
XLA Ops:
  0.0 2.6 %shard_map.37 = (f32[448,128]{1,0:T(8,128)S(1)}, f32[448,128]{1,0:T(8,128)S(1)}) custom-call(s32[1]{0:T(128)} %bitcast.core_ref, f32[3,1024,256]{2,1,0:T(8,128)} %gens_ref.5, f32[3,1024,256]{2,1,0:T(8,128)} %solved_ref.7), custom_call_target="tpu_custom_call" | custom-call | flops 805306368 | bytes 3145728 | tf_op jit(solution)/shard_map/pallas_call | solution.py:220
  2.7 0.5 collective-permute-start
  3.2 1.1 %collective-permute-done = f32[448,128]{1,0:T(8,128)S(1)} collective-permute-done((f32[448,128]{1,0:T(8,128)S(1)}, f32[448,128]{1,0:T(8,128)S(1)}, u32[]{:S(2)}, u32[]{:S(2)}) %collective-permute-start) | collective-permute-done | bytes 229408 | tf_op jit(solution)/shard_map/ppermute | solution.py:35
  4.3 0.4 collective-permute-start.1
  4.8 2.7 %collective-permute-start.6 = (f32[448,128]{1,0:T(8,128)S(1)}, f32[448,128]{1,0:T(8,128)S(1)}, u32[]{:S(2)}, u32[]{:S(2)}) collective-permute-start(f32[448,128]{1,0:T(8,128)S(1)} %add.38.refs_0_), channel_id=1, source_target_pairs={{0,2},{1,3},{2,0},{3,1},{4,6},{5,7},{6,4},{7,5},{8,10},{9,11},{10,... | collective-permute-start | bytes 688136 | tf_op jit(solution)/shard_map/ppermute | solution.py:35
  7.4 0.0 collective-permute-done.1.refs_1_
  7.5 1.2 %shard_map.39 = (f32[384,128]{1,0:T(8,128)S(1)}, f32[384,128]{1,0:T(8,128)S(1)}) custom-call(s32[1]{0:T(128)} %bitcast.core_ref, f32[3,1024,256]{2,1,0:T(8,128)S(1)} %copy-done.1, f32[3,1024,256]{2,1,0:T(8,128)S(1)} %copy-done, f32[1024,128]{1,0:T(8,128)S(1)} %copy-done.2, f32[8,128]{1,0:T(8,128)S(1)} %collective-permute-done.1.refs_1_), custom_call_target="tpu_custom_call" | custom-call | flops 603979776 | bytes 2621440 | tf_op jit(solution)/shard_map/pallas_call | solution.py:220
  8.6 0.1 collective-permute-start.10
  8.8 2.4 %shard_map.40 = (f32[576,128]{1,0:T(8,128)S(1)}, f32[576,128]{1,0:T(8,128)S(1)}, f32[320,128]{1,0:T(8,128)S(1)}, f32[320,128]{1,0:T(8,128)S(1)}) custom-call(s32[1]{0:T(128)} %bitcast.core_ref, f32[3,1024,256]{2,1,0:T(8,128)S(1)} %copy-done.1, f32[3,1024,256]{2,1,0:T(8,128)S(1)} %copy-done, f32[1024,128]{1,0:T(8,128)S(1)} %copy-done.2, ...), custom_call_target="tpu_custom_call" | custom-call | flops 1610612736 | bytes 4718592 | tf_op jit(solution)/shard_map/pallas_call | solution.py:220
  11.2 0.5 collective-permute-start.4
  11.7 0.1 collective-permute-start.2
  11.8 0.0 collective-permute-done.10
  11.8 1.2 %collective-permute-start.11 = (f32[384,128]{1,0:T(8,128)S(1)}, f32[384,128]{1,0:T(8,128)S(1)}, u32[]{:S(2)}, u32[]{:S(2)}) collective-permute-start(f32[384,128]{1,0:T(8,128)S(1)} %add.42), channel_id=1, source_target_pairs={{0,2},{1,3},{2,0},{3,1},{4,6},{5,7},{6,4},{7,5},{8,10},{9,11},{10,... | collective-permute-start | bytes 589832 | tf_op jit(solution)/shard_map/ppermute | solution.py:35
  12.9 0.6 %collective-permute-done.6 = f32[448,128]{1,0:T(8,128)S(1)} collective-permute-done((f32[448,128]{1,0:T(8,128)S(1)}, f32[448,128]{1,0:T(8,128)S(1)}, u32[]{:S(2)}, u32[]{:S(2)}) %collective-permute-start.6) | collective-permute-done | bytes 229408 | tf_op jit(solution)/shard_map/ppermute | solution.py:35
  13.6 1.8 %collective-permute-start.7 = (f32[448,128]{1,0:T(8,128)S(1)}, f32[448,128]{1,0:T(8,128)S(1)}, u32[]{:S(2)}, u32[]{:S(2)}) collective-permute-start(f32[448,128]{1,0:T(8,128)S(1)} %add.41.own_ref.head_ref), channel_id=1, source_target_pairs={{0,4},{4,0},{8,12},{12,8},{16,20},{20,16},{24,28},{28,24},{1,5},{5... | collective-permute-start | bytes 688136 | tf_op jit(solution)/shard_map/ppermute | solution.py:35
  15.4 0.0 collective-permute-start.8
  15.4 0.0 collective-permute-done.2
  15.4 0.0 collective-permute-done.4.second_ref
  15.5 1.6 %collective-permute-start.5 = (f32[576,128]{1,0:T(8,128)S(1)}, f32[576,128]{1,0:T(8,128)S(1)}, u32[]{:S(2)}, u32[]{:S(2)}) collective-permute-start(f32[576,128]{1,0:T(8,128)S(1)} %shard_map.41), channel_id=1, source_target_pairs={{0,2},{1,3},{2,0},{3,1},{4,6},{5,7},{6,4},{7,5},{8,10},{9,11},{10,... | collective-permute-start | bytes 884744 | tf_op jit(solution)/shard_map/ppermute | solution.py:35
  17.1 2.5 %collective-permute-done.11 = f32[384,128]{1,0:T(8,128)S(1)} collective-permute-done((f32[384,128]{1,0:T(8,128)S(1)}, f32[384,128]{1,0:T(8,128)S(1)}, u32[]{:S(2)}, u32[]{:S(2)}) %collective-permute-start.11) | collective-permute-done | bytes 196640 | tf_op jit(solution)/shard_map/ppermute | solution.py:35
  19.6 1.6 %collective-permute-start.13 = (f32[384,128]{1,0:T(8,128)S(1)}, f32[384,128]{1,0:T(8,128)S(1)}, u32[]{:S(2)}, u32[]{:S(2)}) collective-permute-start(f32[384,128]{1,0:T(8,128)S(1)} %add.43.tail_ref), channel_id=1, source_target_pairs={{0,4},{4,0},{8,12},{12,8},{16,20},{20,16},{24,28},{28,24},{1,5},{5... | collective-permute-start | bytes 589832 | tf_op jit(solution)/shard_map/ppermute | solution.py:35
  21.2 0.0 collective-permute-done.7.sib_ref.head_sib_ref
  21.2 0.1 collective-permute-start.9
  21.3 0.6 collective-permute-start.12
  21.8 0.0 collective-permute-done.8.own_other_ref.head_other_ref
  21.8 1.6 %collective-permute-start.3 = (f32[320,128]{1,0:T(8,128)S(1)}, f32[320,128]{1,0:T(8,128)S(1)}, u32[]{:S(2)}, u32[]{:S(2)}) collective-permute-start(f32[320,128]{1,0:T(8,128)S(1)} %add.39.refs_0_.first_ref), channel_id=1, source_target_pairs={{0,8},{4,12},{8,0},{12,4},{16,24},{20,28},{24,16},{28,20},{1,9},{5... | collective-permute-start | bytes 491528 | tf_op jit(solution)/shard_map/ppermute | solution.py:35
  23.4 0.0 collective-permute-done.9.sib_other_ref
  23.4 2.3 %shard_map.42 = (f32[256,256]{1,0:T(8,128)S(1)}, f32[256,320]{1,0:T(8,128)S(1)}) custom-call(s32[1]{0:T(128)} %bitcast.core_ref, f32[448,128]{1,0:T(8,128)S(1)} %add.41.own_ref.head_ref, f32[448,128]{1,0:T(8,128)S(1)} %collective-permute-done.7.sib_ref.head_sib_ref, f32[448,128]{1,0:T(8,128)S(1)} %collective-permute-done.8.own_other_ref.head_other_ref, ...), custom_call_target="tpu_custom_call" | custom-call | flops 500000000 | bytes 1572868 | tf_op jit(solution)/shard_map/pallas_call | solution.py:309
  25.7 0.0 collective-permute-done.12.tail_other_ref
  25.7 0.0 collective-permute-done.13.tail_sib_ref
  25.7 1.0 %shard_map.43 = (f32[640,128]{1,0:T(8,128)S(1)}, f32[576,128]{1,0:T(8,128)S(1)}, f32[320,128]{1,0:T(8,128)S(1)}) custom-call(s32[1]{0:T(128)} %bitcast.core_ref, f32[256,256]{1,0:T(8,128)S(1)} %get-tuple-element.35.inverse_ref, f32[256,320]{1,0:T(8,128)S(1)} %get-tuple-element.36.product_ref, f32[448,128]{1,0:T(8,128)S(1)} %add.41.own_ref.head_ref, ...), custom_call_target="tpu_custom_call" | custom-call | flops 650000000 | bytes 2588676 | tf_op jit(solution)/shard_map/pallas_call | solution.py:309
  26.8 0.0 collective-permute-done.5
  26.9 1.5 %collective-permute-start.19 = (f32[192,128]{1,0:T(8,128)S(1)}, f32[192,128]{1,0:T(8,128)S(1)}, u32[]{:S(2)}, u32[]{:S(2)}) collective-permute-start(f32[192,128]{1,0:T(8,128)S(1)} %shard_map.44.refs_0_), channel_id=1, source_target_pairs={{0,4},{4,0},{8,12},{12,8},{16,20},{20,16},{24,28},{28,24},{1,5},{5... | collective-permute-start | bytes 294920 | tf_op jit(solution)/shard_map/ppermute | solution.py:35
  28.4 0.6 %collective-permute-start.17 = (f32[384,128]{1,0:T(8,128)S(1)}, f32[384,128]{1,0:T(8,128)S(1)}, u32[]{:S(2)}, u32[]{:S(2)}) collective-permute-start(f32[384,128]{1,0:T(8,128)S(1)} %shard_map.45.refs_0_), channel_id=1, source_target_pairs={{0,4},{4,0},{8,12},{12,8},{16,20},{20,16},{24,28},{28,24},{1,5},{5... | collective-permute-start | bytes 589832 | tf_op jit(solution)/shard_map/ppermute | solution.py:35
  29.1 1.5 %collective-permute-start.14 = (f32[320,128]{1,0:T(8,128)S(1)}, f32[320,128]{1,0:T(8,128)S(1)}, u32[]{:S(2)}, u32[]{:S(2)}) collective-permute-start(f32[320,128]{1,0:T(8,128)S(1)} %shard_map.46), channel_id=1, source_target_pairs={{0,2},{1,3},{2,0},{3,1},{4,6},{5,7},{6,4},{7,5},{8,10},{9,11},{10,... | collective-permute-start | bytes 491528 | tf_op jit(solution)/shard_map/ppermute | solution.py:35
  30.6 1.2 %collective-permute-start.15 = (f32[320,128]{1,0:T(8,128)S(1)}, f32[320,128]{1,0:T(8,128)S(1)}, u32[]{:S(2)}, u32[]{:S(2)}) collective-permute-start(f32[320,128]{1,0:T(8,128)S(1)} %shard_map.47), channel_id=1, source_target_pairs={{0,8},{4,12},{8,0},{12,4},{16,24},{20,28},{24,16},{28,20},{1,9},{5... | collective-permute-start | bytes 491528 | tf_op jit(solution)/shard_map/ppermute | solution.py:35
  31.8 0.8 %collective-permute-done.19 = f32[192,128]{1,0:T(8,128)S(1)} collective-permute-done((f32[192,128]{1,0:T(8,128)S(1)}, f32[192,128]{1,0:T(8,128)S(1)}, u32[]{:S(2)}, u32[]{:S(2)}) %collective-permute-start.19) | collective-permute-done | bytes 98336 | tf_op jit(solution)/shard_map/ppermute | solution.py:35
  32.6 1.5 %collective-permute-start.20 = (f32[192,128]{1,0:T(8,128)S(1)}, f32[192,128]{1,0:T(8,128)S(1)}, u32[]{:S(2)}, u32[]{:S(2)}) collective-permute-start(f32[192,128]{1,0:T(8,128)S(1)} %add.48.own_ref), channel_id=1, source_target_pairs={{0,8},{4,12},{8,0},{12,4},{16,24},{20,28},{24,16},{28,20},{1,9},{5... | collective-permute-start | bytes 294920 | tf_op jit(solution)/shard_map/ppermute | solution.py:35
  34.1 0.0 collective-permute-start.21
  34.1 1.6 %collective-permute-done.17 = f32[384,128]{1,0:T(8,128)S(1)} collective-permute-done((f32[384,128]{1,0:T(8,128)S(1)}, f32[384,128]{1,0:T(8,128)S(1)}, u32[]{:S(2)}, u32[]{:S(2)}) %collective-permute-start.17) | collective-permute-done | bytes 196640 | tf_op jit(solution)/shard_map/ppermute | solution.py:35
  35.8 1.1 %collective-permute-start.18 = (f32[384,128]{1,0:T(8,128)S(1)}, f32[384,128]{1,0:T(8,128)S(1)}, u32[]{:S(2)}, u32[]{:S(2)}) collective-permute-start(f32[384,128]{1,0:T(8,128)S(1)} %add.47.r_own_ref.own_ref), channel_id=1, source_target_pairs={{0,8},{4,12},{8,0},{12,4},{16,24},{20,28},{24,16},{28,20},{1,9},{5... | collective-permute-start | bytes 589832 | tf_op jit(solution)/shard_map/ppermute | solution.py:35
  36.9 0.0 collective-permute-done.14
  36.9 0.0 collective-permute-start.23
  36.9 1.2 %collective-permute-done.20.sib_ref = f32[192,128]{1,0:T(8,128)S(1)} collective-permute-done((f32[192,128]{1,0:T(8,128)S(1)}, f32[192,128]{1,0:T(8,128)S(1)}, u32[]{:S(2)}, u32[]{:S(2)}) %collective-permute-start.20) | collective-permute-done | bytes 98336 | tf_op jit(solution)/shard_map/ppermute | solution.py:35
  38.1 0.0 collective-permute-start.22
  38.1 0.0 collective-permute-done.15
  38.2 1.5 %collective-permute-start.16 = (f32[320,128]{1,0:T(8,128)S(1)}, f32[320,128]{1,0:T(8,128)S(1)}, u32[]{:S(2)}, u32[]{:S(2)}) collective-permute-start(f32[320,128]{1,0:T(8,128)S(1)} %add_subtract_fusion.1), channel_id=1, source_target_pairs={{0,4},{4,0},{8,12},{12,8},{16,20},{20,16},{24,28},{28,24},{1,5},{5... | collective-permute-start | bytes 491528 | tf_op jit(solution)/shard_map/ppermute | solution.py:35
  39.6 2.5 %shard_map.48 = (f32[256,256]{1,0:T(8,128)S(1)}, f32[256,192]{1,0:T(8,128)S(1)}, f32[512,256]{1,0:T(8,128)S(1)}) custom-call(s32[1]{0:T(128)} %bitcast.core_ref, f32[192,128]{1,0:T(8,128)S(1)} %add.48.own_ref, f32[192,128]{1,0:T(8,128)S(1)} %collective-permute-done.20.sib_ref, f32[192,128]{1,0:T(8,128)S(1)} %collective-permute-done.21.own_other_ref, ...), custom_call_target="tpu_custom_call" | custom-call | flops 900000000 | bytes 1703940 | tf_op jit(solution)/shard_map/pallas_call | solution.py:309
  42.1 0.0 collective-permute-done.18.sib_ref
  42.2 0.3 collective-permute-start.24
  42.5 0.9 %shard_map.50 = (f32[384,128]{1,0:T(8,128)S(1)}, f32[384,128]{1,0:T(8,128)S(1)}, f32[320,128]{1,0:T(8,128)S(1)}) custom-call(s32[1]{0:T(128)} %bitcast.core_ref, f32[256,256]{1,0:T(8,128)S(1)} %get-tuple-element.39.refs_0_.inverse_ref, f32[256,192]{1,0:T(8,128)S(1)} %get-tuple-element.40.product_ref, f32[512,256]{1,0:T(8,128)S(1)} %get-tuple-element.41.turned_ref, ...), custom_call_target="tpu_custom_call" | custom-call | bytes 1933316 | tf_op jit(solution)/shard_map/pallas_call | solution.py:309
  43.4 0.2 collective-permute-done.24.sib_other_ref
  43.6 0.4 shard_map.51
  44.0 0.8 %collective-permute-done.16 = f32[320,128]{1,0:T(8,128)S(1)} collective-permute-done((f32[320,128]{1,0:T(8,128)S(1)}, f32[320,128]{1,0:T(8,128)S(1)}, u32[]{:S(2)}, u32[]{:S(2)}) %collective-permute-start.16) | collective-permute-done | bytes 163872 | tf_op jit(solution)/shard_map/ppermute | solution.py:35
  44.9 0.1 collective-permute-start.27
  45.0 2.7 %collective-permute-start.26 = (f32[320,128]{1,0:T(8,128)S(1)}, f32[320,128]{1,0:T(8,128)S(1)}, u32[]{:S(2)}, u32[]{:S(2)}) collective-permute-start(f32[320,128]{1,0:T(8,128)S(1)} %add_subtract_fusion.refs_0_.own_ref), channel_id=1, source_target_pairs={{0,16},{4,20},{8,24},{12,28},{16,0},{20,4},{24,8},{28,12},{1,17},{... | collective-permute-start | bytes 491528 | tf_op jit(solution)/shard_map/ppermute | solution.py:35
  47.7 0.2 collective-permute-start.25
  47.8 0.0 collective-permute-done.27
  47.9 2.2 %shard_map.53 = (bf16[1024,256]{1,0:T(8,128)(2,1)S(1)}, bf16[1024,256]{1,0:T(8,128)(2,1)S(1)}, f32[1024,128]{1,0:T(8,128)S(1)}) custom-call(s32[1]{0:T(128)} %bitcast.core_ref, f32[384,128]{1,0:T(8,128)S(1)} %get-tuple-element.44.first_ref.z1_ref, f32[384,128]{1,0:T(8,128)S(1)} %slice.50.z1_other_ref, f32[640,128]{1,0:T(8,128)S(1)} %get-tuple-element.45.second_ref.z0_ref, ...), custom_call_target="tpu_custom_call" | custom-call | flops 1207959552 | bytes 7340036 | tf_op jit(solution)/shard_map/pallas_call | solution.py:309
  50.1 5.9 %collective-permute-done.26.value_ref = f32[320,128]{1,0:T(8,128)S(1)} collective-permute-done((f32[320,128]{1,0:T(8,128)S(1)}, f32[320,128]{1,0:T(8,128)S(1)}, u32[]{:S(2)}, u32[]{:S(2)}) %collective-permute-start.26) | collective-permute-done | bytes 163872 | tf_op jit(solution)/shard_map/ppermute | solution.py:35
  56.0 0.1 collective-permute-start.28
  56.1 0.0 collective-permute-done.25.own_other_ref
  56.1 1.4 %collective-permute-done.28.sib_other_ref = f32[320,128]{1,0:T(8,128)S(1)} collective-permute-done((f32[320,128]{1,0:T(8,128)S(1)}, f32[320,128]{1,0:T(8,128)S(1)}, u32[]{:S(2)}, u32[]{:S(2)}) %collective-permute-start.28) | collective-permute-done | bytes 163872 | tf_op jit(solution)/shard_map/ppermute | solution.py:35
  57.5 3.7 %shard_map.55 = f32[1024,128]{1,0:T(8,128)} custom-call(s32[1]{0:T(128)} %bitcast.core_ref, f32[320,128]{1,0:T(8,128)S(1)} %add_subtract_fusion.refs_0_.own_ref, f32[320,128]{1,0:T(8,128)S(1)} %collective-permute-done.25.own_other_ref, f32[320,128]{1,0:T(8,128)S(1)} %shard_map.54.sib_ref, f32[320,128]{1,0:T(8,128)S(1)} %collective-permute-done.28.sib_other_ref, ...), custom_call_target="tpu_custom_call" | custom-call | flops 1107296256 | bytes 3145728 | tf_op jit(solution)/shard_map/pallas_call | solution.py:505
  (40 shorter events, 0.6 us)
Async XLA Ops:
  0.0 7.5 %copy-start = (f32[3,1024,256]{2,1,0:T(8,128)S(1)}, f32[3,1024,256]{2,1,0:T(8,128)}, u32[]{:S(2)}) copy-start(f32[3,1024,256]{2,1,0:T(8,128)} %solved_ref.7) | copy-start | bytes 9437188
  0.0 7.5 %copy-start.1 = (f32[3,1024,256]{2,1,0:T(8,128)S(1)}, f32[3,1024,256]{2,1,0:T(8,128)}, u32[]{:S(2)}) copy-start(f32[3,1024,256]{2,1,0:T(8,128)} %gens_ref.5) | copy-start | bytes 9437188
  0.0 7.5 %copy-start.2 = (f32[1024,128]{1,0:T(8,128)S(1)}, f32[1024,128]{1,0:T(8,128)}, u32[]{:S(2)}) copy-start(f32[1024,128]{1,0:T(8,128)} %rhs_ref.1) | copy-start | bytes 1572868
  2.7 1.6 %collective-permute-start = (f32[448,128]{1,0:T(8,128)S(1)}, f32[448,128]{1,0:T(8,128)S(1)}, u32[]{:S(2)}, u32[]{:S(2)}) collective-permute-start(f32[448,128]{1,0:T(8,128)S(1)} %get-tuple-element.27), channel_id=1, source_target_pairs={{0,1},{1,0},{2,3},{3,2},{4,5},{5,4},{6,7},{7,6},{8,9},{9,8},{10,11... | collective-permute-start | bytes 688136 | tf_op jit(solution)/shard_map/ppermute | solution.py:35
  4.3 3.1 %collective-permute-start.1 = (f32[8,128]{1,0:T(8,128)S(1)}, f32[8,128]{1,0:T(8,128)S(1)}, u32[]{:S(2)}, u32[]{:S(2)}) collective-permute-start(f32[8,128]{1,0:T(8,128)S(1)} %shard_map.38), channel_id=1, source_target_pairs={{0,1},{1,0},{2,3},{3,2},{4,5},{5,4},{6,7},{7,6},{8,9},{9,8},{10,11... | collective-permute-start | bytes 12296 | tf_op jit(solution)/shard_map/ppermute | solution.py:35
  4.8 8.8 %collective-permute-start.6 = (f32[448,128]{1,0:T(8,128)S(1)}, f32[448,128]{1,0:T(8,128)S(1)}, u32[]{:S(2)}, u32[]{:S(2)}) collective-permute-start(f32[448,128]{1,0:T(8,128)S(1)} %add.38.refs_0_), channel_id=1, source_target_pairs={{0,2},{1,3},{2,0},{3,1},{4,6},{5,7},{6,4},{7,5},{8,10},{9,11},{10,... | collective-permute-start | bytes 688136 | tf_op jit(solution)/shard_map/ppermute | solution.py:35
  8.6 3.1 %collective-permute-start.10 = (f32[384,128]{1,0:T(8,128)S(1)}, f32[384,128]{1,0:T(8,128)S(1)}, u32[]{:S(2)}, u32[]{:S(2)}) collective-permute-start(f32[384,128]{1,0:T(8,128)S(1)} %get-tuple-element.29.refs_1_), channel_id=1, source_target_pairs={{0,1},{1,0},{2,3},{3,2},{4,5},{5,4},{6,7},{7,6},{8,9},{9,8},{10,11... | collective-permute-start | bytes 589832 | tf_op jit(solution)/shard_map/ppermute | solution.py:35
  11.2 4.2 %collective-permute-start.4 = (f32[576,128]{1,0:T(8,128)S(1)}, f32[576,128]{1,0:T(8,128)S(1)}, u32[]{:S(2)}, u32[]{:S(2)}) collective-permute-start(f32[576,128]{1,0:T(8,128)S(1)} %get-tuple-element.33), channel_id=1, source_target_pairs={{0,1},{1,0},{2,3},{3,2},{4,5},{5,4},{6,7},{7,6},{8,9},{9,8},{10,11... | collective-permute-start | bytes 884744 | tf_op jit(solution)/shard_map/ppermute | solution.py:35
  11.7 3.7 %collective-permute-start.2 = (f32[320,128]{1,0:T(8,128)S(1)}, f32[320,128]{1,0:T(8,128)S(1)}, u32[]{:S(2)}, u32[]{:S(2)}) collective-permute-start(f32[320,128]{1,0:T(8,128)S(1)} %get-tuple-element.31), channel_id=1, source_target_pairs={{0,1},{1,0},{2,3},{3,2},{4,5},{5,4},{6,7},{7,6},{8,9},{9,8},{10,11... | collective-permute-start | bytes 491528 | tf_op jit(solution)/shard_map/ppermute | solution.py:35
  11.8 7.8 %collective-permute-start.11 = (f32[384,128]{1,0:T(8,128)S(1)}, f32[384,128]{1,0:T(8,128)S(1)}, u32[]{:S(2)}, u32[]{:S(2)}) collective-permute-start(f32[384,128]{1,0:T(8,128)S(1)} %add.42), channel_id=1, source_target_pairs={{0,2},{1,3},{2,0},{3,1},{4,6},{5,7},{6,4},{7,5},{8,10},{9,11},{10,... | collective-permute-start | bytes 589832 | tf_op jit(solution)/shard_map/ppermute | solution.py:35
  13.6 7.6 %collective-permute-start.7 = (f32[448,128]{1,0:T(8,128)S(1)}, f32[448,128]{1,0:T(8,128)S(1)}, u32[]{:S(2)}, u32[]{:S(2)}) collective-permute-start(f32[448,128]{1,0:T(8,128)S(1)} %add.41.own_ref.head_ref), channel_id=1, source_target_pairs={{0,4},{4,0},{8,12},{12,8},{16,20},{20,16},{24,28},{28,24},{1,5},{5... | collective-permute-start | bytes 688136 | tf_op jit(solution)/shard_map/ppermute | solution.py:35
  15.4 6.4 %collective-permute-start.8 = (f32[448,128]{1,0:T(8,128)S(1)}, f32[448,128]{1,0:T(8,128)S(1)}, u32[]{:S(2)}, u32[]{:S(2)}) collective-permute-start(f32[448,128]{1,0:T(8,128)S(1)} %add.41.own_ref.head_ref), channel_id=1, source_target_pairs={{0,1},{1,0},{2,3},{3,2},{4,5},{5,4},{6,7},{7,6},{8,9},{9,8},{10,11... | collective-permute-start | bytes 688136 | tf_op jit(solution)/shard_map/ppermute | solution.py:35
  15.5 11.3 %collective-permute-start.5 = (f32[576,128]{1,0:T(8,128)S(1)}, f32[576,128]{1,0:T(8,128)S(1)}, u32[]{:S(2)}, u32[]{:S(2)}) collective-permute-start(f32[576,128]{1,0:T(8,128)S(1)} %shard_map.41), channel_id=1, source_target_pairs={{0,2},{1,3},{2,0},{3,1},{4,6},{5,7},{6,4},{7,5},{8,10},{9,11},{10,... | collective-permute-start | bytes 884744 | tf_op jit(solution)/shard_map/ppermute | solution.py:35
  19.6 6.1 %collective-permute-start.13 = (f32[384,128]{1,0:T(8,128)S(1)}, f32[384,128]{1,0:T(8,128)S(1)}, u32[]{:S(2)}, u32[]{:S(2)}) collective-permute-start(f32[384,128]{1,0:T(8,128)S(1)} %add.43.tail_ref), channel_id=1, source_target_pairs={{0,4},{4,0},{8,12},{12,8},{16,20},{20,16},{24,28},{28,24},{1,5},{5... | collective-permute-start | bytes 589832 | tf_op jit(solution)/shard_map/ppermute | solution.py:35
  21.2 2.2 %collective-permute-start.9 = (f32[192,128]{1,0:T(8,128)S(1)}, f32[192,128]{1,0:T(8,128)S(1)}, u32[]{:S(2)}, u32[]{:S(2)}) collective-permute-start(f32[192,128]{1,0:T(8,128)S(1)} %slice.45), channel_id=1, source_target_pairs={{0,1},{1,0},{2,3},{3,2},{4,5},{5,4},{6,7},{7,6},{8,9},{9,8},{10,11... | collective-permute-start | bytes 294920 | tf_op jit(solution)/shard_map/ppermute | solution.py:35
  21.3 4.4 %collective-permute-start.12 = (f32[256,128]{1,0:T(8,128)S(1)}, f32[256,128]{1,0:T(8,128)S(1)}, u32[]{:S(2)}, u32[]{:S(2)}) collective-permute-start(f32[256,128]{1,0:T(8,128)S(1)} %slice.46), channel_id=1, source_target_pairs={{0,1},{1,0},{2,3},{3,2},{4,5},{5,4},{6,7},{7,6},{8,9},{9,8},{10,11... | collective-permute-start | bytes 393224 | tf_op jit(solution)/shard_map/ppermute | solution.py:35
  21.8 7.2 %collective-permute-start.3 = (f32[320,128]{1,0:T(8,128)S(1)}, f32[320,128]{1,0:T(8,128)S(1)}, u32[]{:S(2)}, u32[]{:S(2)}) collective-permute-start(f32[320,128]{1,0:T(8,128)S(1)} %add.39.refs_0_.first_ref), channel_id=1, source_target_pairs={{0,8},{4,12},{8,0},{12,4},{16,24},{20,28},{24,16},{28,20},{1,9},{5... | collective-permute-start | bytes 491528 | tf_op jit(solution)/shard_map/ppermute | solution.py:35
  26.9 5.7 %collective-permute-start.19 = (f32[192,128]{1,0:T(8,128)S(1)}, f32[192,128]{1,0:T(8,128)S(1)}, u32[]{:S(2)}, u32[]{:S(2)}) collective-permute-start(f32[192,128]{1,0:T(8,128)S(1)} %shard_map.44.refs_0_), channel_id=1, source_target_pairs={{0,4},{4,0},{8,12},{12,8},{16,20},{20,16},{24,28},{28,24},{1,5},{5... | collective-permute-start | bytes 294920 | tf_op jit(solution)/shard_map/ppermute | solution.py:35
  28.4 7.3 %collective-permute-start.17 = (f32[384,128]{1,0:T(8,128)S(1)}, f32[384,128]{1,0:T(8,128)S(1)}, u32[]{:S(2)}, u32[]{:S(2)}) collective-permute-start(f32[384,128]{1,0:T(8,128)S(1)} %shard_map.45.refs_0_), channel_id=1, source_target_pairs={{0,4},{4,0},{8,12},{12,8},{16,20},{20,16},{24,28},{28,24},{1,5},{5... | collective-permute-start | bytes 589832 | tf_op jit(solution)/shard_map/ppermute | solution.py:35
  29.1 7.8 %collective-permute-start.14 = (f32[320,128]{1,0:T(8,128)S(1)}, f32[320,128]{1,0:T(8,128)S(1)}, u32[]{:S(2)}, u32[]{:S(2)}) collective-permute-start(f32[320,128]{1,0:T(8,128)S(1)} %shard_map.46), channel_id=1, source_target_pairs={{0,2},{1,3},{2,0},{3,1},{4,6},{5,7},{6,4},{7,5},{8,10},{9,11},{10,... | collective-permute-start | bytes 491528 | tf_op jit(solution)/shard_map/ppermute | solution.py:35
  30.6 7.6 %collective-permute-start.15 = (f32[320,128]{1,0:T(8,128)S(1)}, f32[320,128]{1,0:T(8,128)S(1)}, u32[]{:S(2)}, u32[]{:S(2)}) collective-permute-start(f32[320,128]{1,0:T(8,128)S(1)} %shard_map.47), channel_id=1, source_target_pairs={{0,8},{4,12},{8,0},{12,4},{16,24},{20,28},{24,16},{28,20},{1,9},{5... | collective-permute-start | bytes 491528 | tf_op jit(solution)/shard_map/ppermute | solution.py:35
  32.6 5.5 %collective-permute-start.20 = (f32[192,128]{1,0:T(8,128)S(1)}, f32[192,128]{1,0:T(8,128)S(1)}, u32[]{:S(2)}, u32[]{:S(2)}) collective-permute-start(f32[192,128]{1,0:T(8,128)S(1)} %add.48.own_ref), channel_id=1, source_target_pairs={{0,8},{4,12},{8,0},{12,4},{16,24},{20,28},{24,16},{28,20},{1,9},{5... | collective-permute-start | bytes 294920 | tf_op jit(solution)/shard_map/ppermute | solution.py:35
  34.1 5.5 %collective-permute-start.21 = (f32[192,128]{1,0:T(8,128)S(1)}, f32[192,128]{1,0:T(8,128)S(1)}, u32[]{:S(2)}, u32[]{:S(2)}) collective-permute-start(f32[192,128]{1,0:T(8,128)S(1)} %add.48.own_ref), channel_id=1, source_target_pairs={{0,1},{1,0},{2,3},{3,2},{4,5},{5,4},{6,7},{7,6},{8,9},{9,8},{10,11... | collective-permute-start | bytes 294920 | tf_op jit(solution)/shard_map/ppermute | solution.py:35
  35.8 6.4 %collective-permute-start.18 = (f32[384,128]{1,0:T(8,128)S(1)}, f32[384,128]{1,0:T(8,128)S(1)}, u32[]{:S(2)}, u32[]{:S(2)}) collective-permute-start(f32[384,128]{1,0:T(8,128)S(1)} %add.47.r_own_ref.own_ref), channel_id=1, source_target_pairs={{0,8},{4,12},{8,0},{12,4},{16,24},{20,28},{24,16},{28,20},{1,9},{5... | collective-permute-start | bytes 589832 | tf_op jit(solution)/shard_map/ppermute | solution.py:35
  36.9 2.8 %collective-permute-start.23 = (f32[256,128]{1,0:T(8,128)S(1)}, f32[256,128]{1,0:T(8,128)S(1)}, u32[]{:S(2)}, u32[]{:S(2)}) collective-permute-start(f32[256,128]{1,0:T(8,128)S(1)} %slice.49), channel_id=1, source_target_pairs={{0,1},{1,0},{2,3},{3,2},{4,5},{5,4},{6,7},{7,6},{8,9},{9,8},{10,11... | collective-permute-start | bytes 393224 | tf_op jit(solution)/shard_map/ppermute | solution.py:35
  38.1 1.5 %collective-permute-start.22 = (f32[192,128]{1,0:T(8,128)S(1)}, f32[192,128]{1,0:T(8,128)S(1)}, u32[]{:S(2)}, u32[]{:S(2)}) collective-permute-start(f32[192,128]{1,0:T(8,128)S(1)} %collective-permute-done.20.sib_ref), channel_id=1, source_target_pairs={{0,1},{1,0},{2,3},{3,2},{4,5},{5,4},{6,7},{7,6},{8,9},{9,8},{10,11... | collective-permute-start | bytes 294920 | tf_op jit(solution)/shard_map/ppermute | solution.py:35
  38.2 6.7 %collective-permute-start.16 = (f32[320,128]{1,0:T(8,128)S(1)}, f32[320,128]{1,0:T(8,128)S(1)}, u32[]{:S(2)}, u32[]{:S(2)}) collective-permute-start(f32[320,128]{1,0:T(8,128)S(1)} %add_subtract_fusion.1), channel_id=1, source_target_pairs={{0,4},{4,0},{8,12},{12,8},{16,20},{20,16},{24,28},{28,24},{1,5},{5... | collective-permute-start | bytes 491528 | tf_op jit(solution)/shard_map/ppermute | solution.py:35
  42.2 1.4 %collective-permute-start.24 = (f32[256,128]{1,0:T(8,128)S(1)}, f32[256,128]{1,0:T(8,128)S(1)}, u32[]{:S(2)}, u32[]{:S(2)}) collective-permute-start(f32[256,128]{1,0:T(8,128)S(1)} %shard_map.49.sib_ref), channel_id=1, source_target_pairs={{0,1},{1,0},{2,3},{3,2},{4,5},{5,4},{6,7},{7,6},{8,9},{9,8},{10,11... | collective-permute-start | bytes 393224 | tf_op jit(solution)/shard_map/ppermute | solution.py:35
  44.9 2.9 %collective-permute-start.27 = (f32[1024,128]{1,0:T(8,128)S(1)}, f32[1024,128]{1,0:T(8,128)S(1)}, u32[]{:S(2)}, u32[]{:S(2)}) collective-permute-start(f32[1024,128]{1,0:T(8,128)S(1)} %shard_map.52), channel_id=1, source_target_pairs={{0,1},{1,0},{2,3},{3,2},{4,5},{5,4},{6,7},{7,6},{8,9},{9,8},{10,11... | collective-permute-start | bytes 1572872 | tf_op jit(solution)/shard_map/ppermute | solution.py:35
  45.0 11.0 %collective-permute-start.26 = (f32[320,128]{1,0:T(8,128)S(1)}, f32[320,128]{1,0:T(8,128)S(1)}, u32[]{:S(2)}, u32[]{:S(2)}) collective-permute-start(f32[320,128]{1,0:T(8,128)S(1)} %add_subtract_fusion.refs_0_.own_ref), channel_id=1, source_target_pairs={{0,16},{4,20},{8,24},{12,28},{16,0},{20,4},{24,8},{28,12},{1,17},{... | collective-permute-start | bytes 491528 | tf_op jit(solution)/shard_map/ppermute | solution.py:35
  47.7 8.5 %collective-permute-start.25 = (f32[320,128]{1,0:T(8,128)S(1)}, f32[320,128]{1,0:T(8,128)S(1)}, u32[]{:S(2)}, u32[]{:S(2)}) collective-permute-start(f32[320,128]{1,0:T(8,128)S(1)} %add_subtract_fusion.refs_0_.own_ref), channel_id=1, source_target_pairs={{0,1},{1,0},{2,3},{3,2},{4,5},{5,4},{6,7},{7,6},{8,9},{9,8},{10,11... | collective-permute-start | bytes 491528 | tf_op jit(solution)/shard_map/ppermute | solution.py:35
  56.0 1.5 %collective-permute-start.28 = (f32[320,128]{1,0:T(8,128)S(1)}, f32[320,128]{1,0:T(8,128)S(1)}, u32[]{:S(2)}, u32[]{:S(2)}) collective-permute-start(f32[320,128]{1,0:T(8,128)S(1)} %shard_map.54.sib_ref), channel_id=1, source_target_pairs={{0,1},{1,0},{2,3},{3,2},{4,5},{5,4},{6,7},{7,6},{8,9},{9,8},{10,11... | collective-permute-start | bytes 491528 | tf_op jit(solution)/shard_map/ppermute | solution.py:35
